TPU v7x, 32 devices: a whole 2x2x4 slice. The times are simulated.
32 devices in a mesh: section: 2 (over y), expert: 16 (over z, x, core).
Axes of the slice: x: 2, y: 2, z: 4, core: 2. Of those that a mesh axis runs over, the one named last changes fastest.
Arguments:
- front_input: bfloat16 [2, 2048, 3584], P('section', 'expert'), may hold values from -6 to 6
- queries: bfloat16 [2, 2048, 3584], P('section', 'expert'), may hold values from -400 to 400
- keys_values: bfloat16 [2, 2048, 448], P('section', 'expert'), may hold values from -6 to 6
- selected_blocks: int32 [2, 32, 2, 4], P('section', 'expert'), may hold values from 0 to 31, as said below
- front_route: int32 [2, 2048, 1], P('section', 'expert'), may hold values from 0 to 3; in each aligned block of 128 rows (0 to 127, 128 to 255, ..., all dimensions but the last counted through in order) at most 36 rows name the same one
- front_gate: float32 [2, 2048, 1], P('section', 'expert'), may hold values from 0.3 to 1
- back_middle: bfloat16 [2, 2048, 3584], P('section', 'expert'), may hold values from -6 to 6
- back_grad: bfloat16 [2, 2048, 3584], P('section', 'expert'), may hold values from -6 to 6
- back_route: int32 [2, 2048, 1], P('section', 'expert'), may hold values from 0 to 3; in each aligned block of 128 rows (0 to 127, 128 to 255, ..., all dimensions but the last counted through in order) at most 36 rows name the same one
- back_gate: float32 [2, 2048, 1], P('section', 'expert'), may hold values from 0.3 to 1
- norm_gain: float32 [2, 3584], P('section'), may hold values from 0.1 to 1.9
- gate_slice: bfloat16 [2, 16, 3584, 256], P('section', 'expert'), may hold values from -0.09375 to 0.09375
- up_slice: bfloat16 [2, 16, 3584, 256], P('section', 'expert'), may hold values from -0.09375 to 0.09375
- down_slice: bfloat16 [2, 16, 256, 3584], P('section', 'expert'), may hold values from -0.1875 to 0.1875
Outputs:
- front_output: bfloat16 [2, 2048, 3584], P('section', 'expert')
- back_output: bfloat16 [2, 2048, 3584], P('section', 'expert')
Inputs may be any that keep to these rules, and one draw needn't show every extreme that they name: `selected_blocks`: each list holds 4 different block numbers, among them the query block's own; the others are at most the larger of the query block's number and 3. `front_route`: in the tokens of one device at one section, no expert is named more than 36 times. `back_route`: in the tokens of one device at one section, no expert is named more than 36 times.
All inputs are finite; a program needn't handle non-finite values.
Results may differ from a plain program's by a relative error of at most 0.0057.
Values may be sent and summed in bfloat16 or wider, within the bound.
No kernel may reach another device: no remote copies, remote signals or barrier semaphores. Data moves between devices by JAX's collectives and lax.ppermute only.
A program may use at most 192 MiB of HBM per device.

v0:
```python
import jax
import jax.numpy as jnp
from jax import lax
from jax.sharding import PartitionSpec as P

GROUP = 4
HEADS = 32
HEAD_DIM = 112
KV_HEADS = 2
BLK = 64


epsilon = 1e-06
negative_large = -1e30


def passed_along(array, axis, by):
    length = lax.axis_size(axis)
    return lax.ppermute(array, axis, [(i, (i + by) % length) for i in range(length)])


def rms_scale(rows):
    return lax.rsqrt(jnp.mean(rows * rows, axis=-1, keepdims=True) + epsilon)


def attend_local(query_rows, kv_rows, chosen_blocks):
    gathered = lax.all_gather(kv_rows, "expert", axis=0, tiled=True)
    block_count = gathered.shape[0] // BLK
    blocks_view = gathered.reshape(block_count, BLK, 2, KV_HEADS, HEAD_DIM)
    groups = HEADS // KV_HEADS
    query_blocks = query_rows.reshape(-1, BLK, KV_HEADS, groups, HEAD_DIM)
    local_blocks = query_blocks.shape[0]
    first_block = lax.axis_index("expert") * local_blocks
    head_index = jnp.arange(KV_HEADS, dtype=jnp.int32)[:, None]
    offsets = jnp.arange(BLK, dtype=jnp.int32)

    def one_block(query_block, chosen, block_index):
        key_sel = blocks_view[chosen, :, 0, head_index].reshape(KV_HEADS, -1, HEAD_DIM)
        value_sel = blocks_view[chosen, :, 1, head_index].reshape(KV_HEADS, -1, HEAD_DIM)
        scores = jnp.einsum(
            "qhgd,hkd->hgqk", query_block, key_sel, preferred_element_type=jnp.float32
        ) * HEAD_DIM ** (-0.5)
        key_pos = (chosen[:, :, None] * BLK + offsets[None, None, :]).reshape(KV_HEADS, -1)
        query_pos = block_index * BLK + offsets
        allowed = key_pos[:, None, None, :] <= query_pos[None, None, :, None]
        scores = jnp.where(allowed, scores, negative_large)
        row_max = jnp.max(scores, axis=-1, keepdims=True)
        exp_scores = jnp.exp(scores - row_max)
        row_total = jnp.sum(exp_scores, axis=-1, keepdims=True)
        attention_weights = (exp_scores / row_total).astype(jnp.bfloat16)
        mixed_out = jnp.einsum(
            "hgqk,hkd->qhgd", attention_weights, value_sel, preferred_element_type=jnp.float32
        )
        return mixed_out.reshape(BLK, HEADS * HEAD_DIM)

    attended = jax.vmap(one_block)(
        query_blocks, chosen_blocks, first_block + jnp.arange(local_blocks, dtype=jnp.int32)
    )
    return attended.reshape(query_rows.shape[0], HEADS * HEAD_DIM)


def place_rows(route, experts, capacity):
    flat_route = route.reshape(-1)
    onehot = (flat_route[:, None] == jnp.arange(experts, dtype=jnp.int32)[None, :]).astype(
        jnp.int32
    )
    before = jnp.cumsum(onehot, axis=0) - onehot
    return flat_route * capacity + jnp.sum(before * onehot, axis=1)


def pack_rows(rows, destination, experts, capacity):
    feature_width = rows.shape[1]
    buffer = jnp.zeros((experts * capacity, feature_width), rows.dtype).at[destination].set(rows)
    return jnp.repeat(buffer.reshape(experts, capacity, feature_width), GROUP, axis=0)


def unpack_rows(returned, destination, experts, capacity):
    feature_width = returned.shape[2]
    grid = returned.reshape(experts, GROUP, capacity, feature_width)
    picked = grid[destination // capacity, :, destination % capacity]
    return jnp.sum(picked.astype(jnp.float32), axis=1)


def slice_forward(rows, w_gate, w_up, w_down):
    gate_val = jnp.dot(rows, w_gate, preferred_element_type=jnp.float32)
    up_val = jnp.dot(rows, w_up, preferred_element_type=jnp.float32)
    hidden = (jax.nn.silu(gate_val) * up_val).astype(jnp.bfloat16)
    return jnp.dot(hidden, w_down, preferred_element_type=jnp.float32).astype(jnp.bfloat16)


def slice_backward(rows, grads, w_gate, w_up, w_down):
    contract_last = (((1,), (1,)), ((), ()))
    gate_val = jnp.dot(rows, w_gate, preferred_element_type=jnp.float32)
    up_val = jnp.dot(rows, w_up, preferred_element_type=jnp.float32)
    sigmoid_val = jax.nn.sigmoid(gate_val)
    act_val = gate_val * sigmoid_val
    slope_val = sigmoid_val * (1.0 + gate_val * (1.0 - sigmoid_val))
    down_back = lax.dot_general(grads, w_down, contract_last, preferred_element_type=jnp.float32)
    gate_grad = (down_back * up_val * slope_val).astype(jnp.bfloat16)
    up_grad = (down_back * act_val).astype(jnp.bfloat16)
    both_grad = jnp.concatenate([gate_grad, up_grad], axis=1)
    both_weight = jnp.concatenate([w_gate, w_up], axis=1)
    total_val = lax.dot_general(
        both_grad, both_weight, contract_last, preferred_element_type=jnp.float32
    )
    return total_val.astype(jnp.bfloat16)


def shards(
    front_input,
    queries,
    keys_values,
    selected_blocks,
    front_route,
    front_gate,
    back_middle,
    back_grad,
    back_route,
    back_gate,
    norm_gain,
    gate_slice,
    up_slice,
    down_slice,
):
    feature_width = front_input.shape[2]
    tokens_here = front_input.shape[1]
    routes_per = front_route.shape[2]
    experts = lax.axis_size("expert") // GROUP
    average = tokens_here * routes_per // experts
    capacity = average + max(1, average // 8)
    w_gate = gate_slice[0, 0]
    w_up = up_slice[0, 0]
    w_down = down_slice[0, 0]
    gain_row = norm_gain[0]
    attention_out = attend_local(queries[0], keys_values[0], selected_blocks[0])
    middle = (front_input[0].astype(jnp.float32) + attention_out).astype(jnp.bfloat16)
    middle = lax.optimization_barrier(middle).astype(jnp.float32)
    normed = (middle * rms_scale(middle) * gain_row).astype(jnp.bfloat16)
    front_rows = jnp.repeat(normed, routes_per, axis=0)
    back_mid = back_middle[0].astype(jnp.float32)
    back_scale = rms_scale(back_mid)
    back_normed = (back_mid * back_scale * gain_row).astype(jnp.bfloat16)
    grad_rows = jnp.repeat(back_grad[0].astype(jnp.float32), routes_per, axis=0)
    scaled = (back_gate[0] * grad_rows).astype(jnp.bfloat16)
    back_rows = jnp.repeat(back_normed, routes_per, axis=0)
    front_dest = place_rows(front_route[0], experts, capacity)
    back_dest = place_rows(back_route[0], experts, capacity)
    front_send = pack_rows(front_rows, front_dest, experts, capacity)
    back_send_rows = pack_rows(back_rows, back_dest, experts, capacity)
    back_send_grads = pack_rows(scaled, back_dest, experts, capacity)
    received = lax.all_to_all(front_send, "expert", split_axis=0, concat_axis=0, tiled=True)
    partial_value = slice_forward(received.reshape(-1, feature_width), w_gate, w_up, w_down)
    front_return = lax.all_to_all(
        partial_value.reshape(received.shape), "expert", split_axis=0, concat_axis=0, tiled=True
    )
    received = (
        lax.all_to_all(back_send_rows, "expert", split_axis=0, concat_axis=0, tiled=True),
        lax.all_to_all(back_send_grads, "expert", split_axis=0, concat_axis=0, tiled=True),
    )
    received_rows = received[0]
    partial_value = slice_backward(
        received_rows.reshape(-1, feature_width),
        received[1].reshape(-1, feature_width),
        w_gate,
        w_up,
        w_down,
    )
    back_return = lax.all_to_all(
        partial_value.reshape(received_rows.shape),
        "expert",
        split_axis=0,
        concat_axis=0,
        tiled=True,
    )
    expert_out = unpack_rows(front_return, front_dest, experts, capacity)
    expert_grad = unpack_rows(back_return, back_dest, experts, capacity)
    weighted = expert_out * front_gate[0]
    contrib = jnp.sum(weighted.reshape(tokens_here, routes_per, feature_width), axis=1)
    front_result = (middle + contrib).astype(jnp.bfloat16)
    normed_grad = jnp.sum(expert_grad.reshape(tokens_here, routes_per, feature_width), axis=1)
    amount = gain_row * normed_grad
    cube = back_scale * back_scale * back_scale
    back_result = (
        back_grad[0].astype(jnp.float32)
        + back_scale * amount
        - back_mid * cube * jnp.mean(back_mid * amount, axis=-1, keepdims=True)
    )
    back_result = back_result.astype(jnp.bfloat16)
    front_output = passed_along(front_result, "section", 1)
    back_output = passed_along(back_result, "section", -1)
    return (front_output[None], back_output[None])


def solution(mesh):
    placed = (
        P("section", "expert", None),
        P("section", "expert", None),
        P("section", "expert", None),
        P("section", "expert", None, None),
        P("section", "expert", None),
        P("section", "expert", None),
        P("section", "expert", None),
        P("section", "expert", None),
        P("section", "expert", None),
        P("section", "expert", None),
        P("section", None),
        P("section", "expert", None, None),
        P("section", "expert", None, None),
        P("section", "expert", None, None),
    )
    return jax.shard_map(
        shards,
        mesh=mesh,
        in_specs=placed,
        out_specs=(P("section", "expert", None), P("section", "expert", None)),
        check_vma=False,
    )
```

profile of v0, /device:TPU:10, one launch (start us, length us, event | category | flops | bytes accessed | tf_op | source)
XLA Modules:
  0.0 644.4 jit_solution(12824755303156659399)
XLA Ops:
  7.2 0.9 fusion.56
  8.2 0.8 select_reduce_fusion
  9.1 0.7 fusion.73
  9.7 1.4 fusion.16
  11.2 0.8 reduce
  12.0 3.7 scatter_custom_fusion.2
  15.7 2.2 reshape.390
  17.8 3.7 broadcast_in_dim.33
  21.5 6.4 all-to-all-start.3
  27.9 2.9 scatter_custom_fusion.1
  30.9 2.2 reshape.387
  33.0 95.6 %all-to-all-done.3 = bf16[16,36,3584]{2,1,0:T(8,128)(2,1)} async-done(((bf16[16,36,3584]{2,1,0:T(8,128)(2,1)}), bf16[16,36,3584]{2,1,0:T(8,128)(2,1)}, u32[]{:S(2)}, u32[]{:S(2)}) %all-to-all-start.3) | async-done | bytes 4128800 | tf_op jit(solution)/shard_map/all_to_all | solution.py:157
  128.7 3.8 broadcast_in_dim.32
  132.4 5.2 all-to-all-start.2
  137.6 0.5 all-gather.3.cloned.1.call-start
  138.5 2.5 reshape_squeeze.2
  142.0 89.4 %all-gather.3.cloned.1.call-done = bf16[1,2048,448]{1,2,0:T(8,128)(2,1)} async-done(((bf16[1,128,448]{1,2,0:T(8,128)(2,1)}), bf16[1,2048,448]{1,2,0:T(8,128)(2,1)}) %all-gather.3.cloned.1.call-update) | async-done | bytes 1835024 | tf_op jit(solution)/shard_map/all_gather | solution.py:27
  231.4 6.5 %reshape.452 = bf16[32,64,2,2,112]{1,0,4,3,2:T(8,128)(2,1)} reshape(bf16[1,2048,448]{1,2,0:T(8,128)(2,1)} %all-gather.3.cloned.1.call-done) | data formatting | bytes 3670016 | tf_op jit(solution)/shard_map/reshape | solution.py:29
  237.9 5.1 copy.25
  243.0 2.2 gather_fusion.1
  245.3 2.2 gather_fusion
  247.5 1.9 fusion.29
  249.4 1.9 fusion.86
  251.4 1.5 fusion.25
  252.8 2.5 copy.30
  255.4 3.5 reshape.381
  258.9 1.9 fusion.21
  261.0 3.0 scatter_custom_fusion
  264.0 2.1 reshape.382
  266.2 3.6 broadcast_in_dim.30
  269.8 7.7 %all-to-all-start = ((bf16[16,36,3584]{2,1,0:T(8,128)(2,1)}), bf16[16,36,3584]{2,1,0:T(8,128)(2,1)}, u32[]{:S(2)}, u32[]{:S(2)}) async-start(bf16[16,36,3584]{2,1,0:T(8,128)(2,1)} %bitcast.127), calls=%async_computation | async-start | bytes 9175040 | tf_op jit(solution)/shard_map/all_to_all | solution.py:151
  277.5 6.9 %reshape.392 = bf16[576,3584]{1,0:T(8,128)(2,1)} reshape(bf16[16,36,3584]{2,1,0:T(8,128)(2,1)} %all-to-all-done.3) | data formatting | bytes 8257536 | tf_op jit(solution)/shard_map/reshape | solution.py:162
  284.5 6.9 %reshape.389 = bf16[576,3584]{1,0:T(8,128)(2,1)} reshape(bf16[16,36,3584]{2,1,0:T(8,128)(2,1)} %all-to-all-done.2) | data formatting | bytes 8257536 | tf_op jit(solution)/shard_map/reshape | solution.py:163
  291.4 4.1 fusion.79
  295.6 1.3 multiply_convert_fusion
  296.8 0.9 copy-done.2
  297.7 0.6 copy-done.12
  298.3 1.3 fusion.27
  299.8 4.3 convolution_convert_fusion
  304.1 6.9 %reshape.393 = bf16[16,36,3584]{2,1,0:T(8,128)(2,1)} reshape(bf16[576,3584]{1,0:T(8,128)(2,1)} %convolution_convert_fusion) | data formatting | bytes 8257536 | tf_op jit(solution)/shard_map/reshape | solution.py:169
  310.9 67.2 %all-to-all-done = bf16[16,36,3584]{2,1,0:T(8,128)(2,1)} async-done(((bf16[16,36,3584]{2,1,0:T(8,128)(2,1)}), bf16[16,36,3584]{2,1,0:T(8,128)(2,1)}, u32[]{:S(2)}, u32[]{:S(2)}) %all-to-all-start) | async-done | bytes 4128800 | tf_op jit(solution)/shard_map/all_to_all | solution.py:151
  378.1 5.0 all-to-all-start.4
  383.1 7.0 %reshape.384 = bf16[576,3584]{1,0:T(8,128)(2,1)} reshape(bf16[16,36,3584]{2,1,0:T(8,128)(2,1)} %all-to-all-done) | data formatting | bytes 8257536 | tf_op jit(solution)/shard_map/reshape | solution.py:152
  390.1 4.0 fusion.81
  394.1 9.2 %convolution_convert_fusion.1 = bf16[576,3584]{1,0:T(8,128)(2,1)} fusion(bf16[1,1,256,3584]{3,2,1,0:T(8,128)(2,1)S(1)} %copy-done, bf16[576,3584]{1,0:T(8,128)(2,1)} %reshape.384, f32[576,256]{1,0:T(8,128)S(1)} %fusion.81, bf16[1,1,3584,256]{3,2,1,0:T(8,128)(2,1)} %param.26), kind=kOutput, calls=%fused_computation.11 | convolution fusion | flops 2116878336 | bytes 12517376 | tf_op jit(solution)/shard_map/dot_general | solution.py:88
  403.2 6.9 %reshape.385 = bf16[16,36,3584]{2,1,0:T(8,128)(2,1)} reshape(bf16[576,3584]{1,0:T(8,128)(2,1)} %convolution_convert_fusion.1) | data formatting | bytes 8257536 | tf_op jit(solution)/shard_map/reshape | solution.py:154
  410.2 73.7 %all-to-all-done.4 = bf16[16,36,3584]{2,1,0:T(8,128)(2,1)} async-done(((bf16[16,36,3584]{2,1,0:T(8,128)(2,1)}), bf16[16,36,3584]{2,1,0:T(8,128)(2,1)}, u32[]{:S(2)}, u32[]{:S(2)}) %all-to-all-start.4) | async-done | bytes 4128800 | tf_op jit(solution)/shard_map/all_to_all | solution.py:168
  483.9 5.2 all-to-all-start.1
  489.1 6.3 copy.34
  495.5 7.5 %gather_fusion.3 = bf16[128,4,3584]{2,1,0:T(4,128)(2,1)} fusion(bf16[4,4,36,3584]{3,1,2,0:T(4,128)(2,1)} %copy.34, s32[128]{0:T(128)S(1)} %get-tuple-element.4), kind=kCustom, calls=%fused_computation.3 | custom fusion | bytes 7341056 | tf_op jit(solution)/shard_map/gather | solution.py:80
  503.0 7.3 %convert_reduce_fusion = f32[128,3584]{1,0:T(8,128)S(1)} fusion(bf16[128,4,3584]{2,1,0:T(4,128)(2,1)} %gather_fusion.3), kind=kLoop, calls=%fused_computation.8 | loop fusion | flops 3211264 | bytes 5505024 | tf_op jit(solution)/shard_map/reduce_sum | solution.py:81
  510.4 0.3 fusion.20
  510.7 0.8 copy-done.5
  511.5 1.7 fusion.11
  513.3 1.5 collective-permute-start.1
  514.8 74.9 %all-to-all-done.1 = bf16[16,36,3584]{2,1,0:T(8,128)(2,1)} async-done(((bf16[16,36,3584]{2,1,0:T(8,128)(2,1)}), bf16[16,36,3584]{2,1,0:T(8,128)(2,1)}, u32[]{:S(2)}, u32[]{:S(2)}) %all-to-all-start.1) | async-done | bytes 4128800 | tf_op jit(solution)/shard_map/all_to_all | solution.py:153
  589.7 6.6 %copy.32 = bf16[4,4,36,3584]{3,1,2,0:T(4,128)(2,1)} copy(bf16[4,4,36,3584]{3,2,1,0:T(8,128)(2,1)} %bitcast.17) | data formatting | bytes 8257536 | tf_op jit(solution)/shard_map/reshape | solution.py:79
  596.3 7.6 %gather_fusion.2 = bf16[128,4,3584]{2,1,0:T(4,128)(2,1)} fusion(bf16[4,4,36,3584]{3,1,2,0:T(4,128)(2,1)} %copy.32, s32[128]{0:T(128)S(1)} %get-tuple-element.6), kind=kCustom, calls=%fused_computation.2 | custom fusion | bytes 7341056 | tf_op jit(solution)/shard_map/gather | solution.py:80
  603.8 7.3 %convert_reduce_fusion.1 = f32[128,3584]{1,0:T(8,128)S(1)} fusion(bf16[128,4,3584]{2,1,0:T(4,128)(2,1)} %gather_fusion.2), kind=kLoop, calls=%fused_computation.9 | loop fusion | flops 3211264 | bytes 5505024 | tf_op jit(solution)/shard_map/reduce_sum | solution.py:81
  611.1 0.3 fusion.15
  611.4 1.6 collective-permute-start
  613.0 21.1 %collective-permute-done = bf16[128,3584]{1,0:T(8,128)(2,1)S(1)} collective-permute-done((bf16[128,3584]{1,0:T(8,128)(2,1)S(1)}, bf16[128,3584]{1,0:T(8,128)(2,1)S(1)}, u32[]{:S(2)}, u32[]{:S(2)}) %collective-permute-start) | collective-permute-done | bytes 917536 | tf_op jit(solution)/shard_map/ppermute | solution.py:19
  634.0 0.9 copy.51
  635.0 2.2 copy.52
  (47 shorter events, 2.0 us)
Async XLA Ops:
  7.2 288.4 %copy-start = (bf16[1,1,256,3584]{3,2,1,0:T(8,128)(2,1)S(1)}, bf16[1,1,256,3584]{3,2,1,0:T(8,128)(2,1)}, u32[]{:S(2)}) copy-start(bf16[1,1,256,3584]{3,2,1,0:T(8,128)(2,1)} %param.27) | copy-start | bytes 5505028
  21.5 6.4 copy-start.4
  21.5 6.4 copy-start.9
  21.5 107.1 %all-to-all-start.3 = ((bf16[16,36,3584]{2,1,0:T(8,128)(2,1)}), bf16[16,36,3584]{2,1,0:T(8,128)(2,1)}, u32[]{:S(2)}, u32[]{:S(2)}) async-start(bf16[16,36,3584]{2,1,0:T(8,128)(2,1)} %bitcast.128), calls=%async_computation.3 | async-start | bytes 9175040 | tf_op jit(solution)/shard_map/all_to_all | solution.py:157
  132.4 5.9 copy-start.7
  132.4 6.1 copy-start.6
  132.4 133.7 %all-to-all-start.2 = ((bf16[16,36,3584]{2,1,0:T(8,128)(2,1)}), bf16[16,36,3584]{2,1,0:T(8,128)(2,1)}, u32[]{:S(2)}, u32[]{:S(2)}) async-start(bf16[16,36,3584]{2,1,0:T(8,128)(2,1)} %bitcast.126), calls=%async_computation.2 | async-start | bytes 9175040 | tf_op jit(solution)/shard_map/all_to_all | solution.py:158
  137.6 3.7 copy-start.8
  137.6 93.7 %all-gather.3.cloned.1.call-start = ((), (), s32[]{:S(2)}) async-start(), calls=%async_computation.5 | async-start | bytes 1949696 | tf_op jit(solution)/shard_map/all_gather | solution.py:27
  269.8 108.3 %all-to-all-start = ((bf16[16,36,3584]{2,1,0:T(8,128)(2,1)}), bf16[16,36,3584]{2,1,0:T(8,128)(2,1)}, u32[]{:S(2)}, u32[]{:S(2)}) async-start(bf16[16,36,3584]{2,1,0:T(8,128)(2,1)} %bitcast.127), calls=%async_computation | async-start | bytes 9175040 | tf_op jit(solution)/shard_map/all_to_all | solution.py:151
  291.4 4.1 copy-start.3
  295.5 2.2 copy-start.2
  295.5 2.7 copy-start.12
  298.3 1.5 copy-start.11
  378.1 105.8 %all-to-all-start.4 = ((bf16[16,36,3584]{2,1,0:T(8,128)(2,1)}), bf16[16,36,3584]{2,1,0:T(8,128)(2,1)}, u32[]{:S(2)}, u32[]{:S(2)}) async-start(bf16[16,36,3584]{2,1,0:T(8,128)(2,1)} %reshape.393), calls=%async_computation.4 | async-start | bytes 9175040 | tf_op jit(solution)/shard_map/all_to_all | solution.py:168
  483.9 105.8 %all-to-all-start.1 = ((bf16[16,36,3584]{2,1,0:T(8,128)(2,1)}), bf16[16,36,3584]{2,1,0:T(8,128)(2,1)}, u32[]{:S(2)}, u32[]{:S(2)}) async-start(bf16[16,36,3584]{2,1,0:T(8,128)(2,1)} %reshape.385), calls=%async_computation.1 | async-start | bytes 9175040 | tf_op jit(solution)/shard_map/all_to_all | solution.py:153
  503.0 7.3 %copy-start.1 = (bf16[1,128,3584]{2,1,0:T(8,128)(2,1)S(1)}, bf16[1,128,3584]{2,1,0:T(8,128)(2,1)}, u32[]{:S(2)}) copy-start(bf16[1,128,3584]{2,1,0:T(8,128)(2,1)} %param.20) | copy-start | bytes 2752516
  510.3 1.2 copy-start.5
  513.3 99.7 %collective-permute-start.1 = (bf16[128,3584]{1,0:T(8,128)(2,1)}, bf16[128,3584]{1,0:T(8,128)(2,1)}, u32[]{:S(2)}, u32[]{:S(2)}) collective-permute-start(bf16[128,3584]{1,0:T(8,128)(2,1)} %fusion.11), channel_id=1, source_target_pairs={{0,16},{16,0},{1,17},{17,1},{2,18},{18,2},{3,19},{19,3},{4,20},{20... | collective-permute-start | bytes 2752520 | tf_op jit(solution)/shard_map/ppermute | solution.py:19
  603.8 7.3 %copy-start.10 = (f32[1,128,1]{1,2,0:T(1,128)S(1)}, f32[1,128,1]{1,2,0:T(1,128)}, u32[]{:S(2)}) copy-start(f32[1,128,1]{1,2,0:T(1,128)} %param.19) | copy-start | bytes 1540
  611.4 22.6 %collective-permute-start = (bf16[128,3584]{1,0:T(8,128)(2,1)S(1)}, bf16[128,3584]{1,0:T(8,128)(2,1)S(1)}, u32[]{:S(2)}, u32[]{:S(2)}) collective-permute-start(bf16[128,3584]{1,0:T(8,128)(2,1)S(1)} %fusion.15), channel_id=1, source_target_pairs={{0,16},{16,0},{1,17},{17,1},{2,18},{18,2},{3,19},{19,3},{4,20},{20... | collective-permute-start | bytes 2752520 | tf_op jit(solution)/shard_map/ppermute | solution.py:19
Sparse Core Ops, SparseCore 0:
  140.6 90.6 all-gather.2
where the time goes:
time: 651 us; the launch traced here: 644 us
  waiting for transfers between devices  422 us (65%)
  local copies, waits for them, and re-layouts  111 us (17%)
  other arithmetic  36.1 us (6%)
  starting transfers between devices  33.1 us (5%)
  matrix products  27.4 us (4%)
  between operations  14.7 us (2%)
    all_to_all x1, waiting for transfers between devices, shards(): lax.all_to_all(back_send_rows, 'expert', split_axis=0, concat_axis=0, til...  95.6 us
    all_gather x1, waiting for transfers between devices, attend_local(): gathered = lax.all_gather(kv_rows, 'expert', axis=0, tiled=True)  89.4 us
    all_to_all x1, waiting for transfers between devices, shards(): lax.all_to_all(partial_value.reshape(received.shape), 'expert', split_axi...  74.9 us
    all_to_all x1, waiting for transfers between devices, shards(): lax.all_to_all(partial_value.reshape(received_rows.shape), 'expert', spli...  73.7 us
    all_to_all x1, waiting for transfers between devices, shards(): lax.all_to_all(front_send, 'expert', split_axis=0, concat_axis=0, tiled=T...  67.2 us
    ppermute x2, waiting for transfers between devices, passed_along(): lax.ppermute(array, axis, [(i, (i + by) % length) for i in range(length)])  21.1 us
    gather x2, local copies, waits for them, and re-layouts, unpack_rows(): picked = grid[destination // capacity, :, destination % capacity]  15.1 us
    reduce_sum x2, other arithmetic, unpack_rows(): return jnp.sum(picked.astype(jnp.float32), axis=1)  14.6 us
  transfers between devices with their start and end apart: 8, of which 6 were waited for; matrix products, arithmetic and copies ran while one was open for 23% of the time, Pallas kernels for 0%

commit v1 on v0

v1 whole, which is shorter than its diff:
```python
import jax
import jax.numpy as jnp
from jax import lax
from jax.sharding import PartitionSpec as P

GROUP = 4
HEADS = 32
HEAD_DIM = 112
KV_HEADS = 2
BLK = 64


epsilon = 1e-06
negative_large = -1e30


def passed_along(array, axis, by):
    length = lax.axis_size(axis)
    return lax.ppermute(array, axis, [(i, (i + by) % length) for i in range(length)])


def rms_scale(rows):
    return lax.rsqrt(jnp.mean(rows * rows, axis=-1, keepdims=True) + epsilon)


def swapped(array, bit):
    return lax.ppermute(array, "expert", [(i, i ^ bit) for i in range(lax.axis_size("expert"))])


def across_experts(array):
    experts = lax.axis_size("expert") // GROUP
    groups = [[e * GROUP + j for e in range(experts)] for j in range(GROUP)]
    return lax.all_to_all(
        array, "expert", split_axis=0, concat_axis=0, axis_index_groups=groups, tiled=True
    )


def gather_blocks(kv_rows):
    length = lax.axis_size("expert")
    experts = length // GROUP
    column = [kv_rows]
    for back in range(1, experts):
        pairs = [(i, i + back * GROUP) for i in range(length - back * GROUP)]
        column.append(lax.ppermute(kv_rows, "expert", pairs))
    column = jnp.concatenate(column, axis=0)
    chip = jnp.concatenate([column, swapped(column, 2)], axis=0)
    return jnp.concatenate([chip, swapped(chip, 1)], axis=0)


def attend_local(query_rows, kv_rows, chosen_blocks):
    gathered = gather_blocks(kv_rows)
    experts = lax.axis_size("expert") // GROUP
    per_device = kv_rows.shape[0] // BLK
    me = lax.axis_index("expert")
    blocks_view = gathered.reshape(-1, BLK, kv_rows.shape[1])
    groups = HEADS // KV_HEADS
    query_blocks = query_rows.reshape(-1, BLK, KV_HEADS, groups, HEAD_DIM)
    local_blocks = query_blocks.shape[0]
    first_block = me * local_blocks
    offsets = jnp.arange(BLK, dtype=jnp.int32)
    owner = chosen_blocks // per_device
    place = (owner % GROUP) ^ (me % GROUP)
    place = (place % 2) * 2 + place // 2
    index = (place * experts + me // GROUP - owner // GROUP) * per_device
    index = jnp.clip(index + chosen_blocks % per_device, 0, blocks_view.shape[0] - 1)

    def one_block(query_block, chosen, place_of, block_index):
        picked = blocks_view[place_of].reshape(KV_HEADS, -1, 2, KV_HEADS, HEAD_DIM)
        key_sel = jnp.stack([picked[h, :, 0, h] for h in range(KV_HEADS)])
        value_sel = jnp.stack([picked[h, :, 1, h] for h in range(KV_HEADS)])
        scores = jnp.einsum(
            "qhgd,hkd->hgqk", query_block, key_sel, preferred_element_type=jnp.float32
        ) * HEAD_DIM ** (-0.5)
        key_pos = (chosen[:, :, None] * BLK + offsets[None, None, :]).reshape(KV_HEADS, -1)
        query_pos = block_index * BLK + offsets
        allowed = key_pos[:, None, None, :] <= query_pos[None, None, :, None]
        scores = jnp.where(allowed, scores, negative_large)
        row_max = jnp.max(scores, axis=-1, keepdims=True)
        exp_scores = jnp.exp(scores - row_max)
        row_total = jnp.sum(exp_scores, axis=-1, keepdims=True)
        attention_weights = (exp_scores / row_total).astype(jnp.bfloat16)
        mixed_out = jnp.einsum(
            "hgqk,hkd->qhgd", attention_weights, value_sel, preferred_element_type=jnp.float32
        )
        return mixed_out.reshape(BLK, HEADS * HEAD_DIM)

    attended = jax.vmap(one_block)(
        query_blocks,
        chosen_blocks,
        index,
        first_block + jnp.arange(local_blocks, dtype=jnp.int32),
    )
    return attended.reshape(query_rows.shape[0], HEADS * HEAD_DIM)


def place_rows(route, experts, capacity):
    flat_route = route.reshape(-1)
    onehot = (flat_route[:, None] == jnp.arange(experts, dtype=jnp.int32)[None, :]).astype(
        jnp.int32
    )
    before = jnp.cumsum(onehot, axis=0) - onehot
    first = flat_route * (2 * capacity) + jnp.sum(before * onehot, axis=1)
    return jnp.concatenate([first, first + capacity])


def selection(places, count):
    return (jnp.arange(count, dtype=jnp.int32)[:, None] == places[None, :]).astype(jnp.bfloat16)


def moved(matrix, rows):
    return jnp.dot(matrix, rows, preferred_element_type=jnp.float32)


def halves_down(rows):
    return jnp.concatenate(jnp.split(rows, 2, axis=1), axis=0)


def halves_across(rows):
    return jnp.concatenate(jnp.split(rows, 2, axis=0), axis=1)


def gather_group(rows):
    other_chip = swapped(rows, 2)
    return [rows, other_chip, swapped(rows, 1), swapped(other_chip, 1)]


def sum_group(pieces):
    own = pieces[0].astype(jnp.float32) + swapped(pieces[2], 1).astype(jnp.float32)
    other = pieces[1].astype(jnp.float32) + swapped(pieces[3], 1).astype(jnp.float32)
    return own + swapped(other.astype(jnp.bfloat16), 2).astype(jnp.float32)


def slice_forward(rows, w_gate, w_up, w_down):
    gate_val = jnp.dot(rows, w_gate, preferred_element_type=jnp.float32)
    up_val = jnp.dot(rows, w_up, preferred_element_type=jnp.float32)
    hidden = (jax.nn.silu(gate_val) * up_val).astype(jnp.bfloat16)
    return jnp.dot(hidden, w_down, preferred_element_type=jnp.float32).astype(jnp.bfloat16)


def slice_backward(rows, grads, w_gate, w_up, w_down):
    contract_last = (((1,), (1,)), ((), ()))
    gate_val = jnp.dot(rows, w_gate, preferred_element_type=jnp.float32)
    up_val = jnp.dot(rows, w_up, preferred_element_type=jnp.float32)
    sigmoid_val = jax.nn.sigmoid(gate_val)
    act_val = gate_val * sigmoid_val
    slope_val = sigmoid_val * (1.0 + gate_val * (1.0 - sigmoid_val))
    down_back = lax.dot_general(grads, w_down, contract_last, preferred_element_type=jnp.float32)
    gate_grad = (down_back * up_val * slope_val).astype(jnp.bfloat16)
    up_grad = (down_back * act_val).astype(jnp.bfloat16)
    total_val = lax.dot_general(
        gate_grad, w_gate, contract_last, preferred_element_type=jnp.float32
    ) + lax.dot_general(up_grad, w_up, contract_last, preferred_element_type=jnp.float32)
    return total_val.astype(jnp.bfloat16)


def shards(
    front_input,
    queries,
    keys_values,
    selected_blocks,
    front_route,
    front_gate,
    back_middle,
    back_grad,
    back_route,
    back_gate,
    norm_gain,
    gate_slice,
    up_slice,
    down_slice,
):
    tokens_here = front_input.shape[1]
    experts = lax.axis_size("expert") // GROUP
    average = tokens_here // experts
    capacity = average + max(1, average // 8)
    slots = experts * capacity
    w_gate = gate_slice[0, 0]
    w_up = up_slice[0, 0]
    w_down = down_slice[0, 0]
    gain_row = norm_gain[0]

    order = jnp.arange(2 * slots, dtype=jnp.int32).reshape(2, experts, capacity)
    order = order.transpose(1, 0, 2).reshape(-1)
    apart = selection(order, 2 * slots)
    together = apart.T

    back_mid = back_middle[0].astype(jnp.float32)
    back_scale = rms_scale(back_mid)
    back_normed = (back_mid * back_scale * gain_row).astype(jnp.bfloat16)
    scaled = (back_gate[0] * back_grad[0].astype(jnp.float32)).astype(jnp.bfloat16)
    back_pick = selection(place_rows(back_route[0], experts, capacity), 2 * slots)
    back_send = moved(back_pick, jnp.concatenate([back_normed, scaled], axis=0))
    received = across_experts(back_send.astype(jnp.bfloat16))
    received = moved(apart, received).astype(jnp.bfloat16)
    pieces = [
        slice_backward(piece[:slots], piece[slots:], w_gate, w_up, w_down)
        for piece in gather_group(received)
    ]
    back_total = sum_group(pieces).astype(jnp.bfloat16)
    back_return = across_experts(moved(together, halves_down(back_total)).astype(jnp.bfloat16))

    attention_out = attend_local(queries[0], keys_values[0], selected_blocks[0])
    middle = (front_input[0].astype(jnp.float32) + attention_out).astype(jnp.bfloat16)
    middle = lax.optimization_barrier(middle).astype(jnp.float32)
    normed = (middle * rms_scale(middle) * gain_row).astype(jnp.bfloat16)
    front_pick = selection(place_rows(front_route[0], experts, capacity), 2 * slots)
    front_send = moved(front_pick, halves_down(normed)).astype(jnp.bfloat16)
    received = across_experts(front_send)
    received = halves_across(moved(apart, received).astype(jnp.bfloat16))
    pieces = [slice_forward(piece, w_gate, w_up, w_down) for piece in gather_group(received)]
    front_total = sum_group(pieces).astype(jnp.bfloat16)
    front_return = across_experts(moved(together, halves_down(front_total)).astype(jnp.bfloat16))

    normed_grad = halves_across(moved(back_pick.T, back_return))
    amount = gain_row * normed_grad
    cube = back_scale * back_scale * back_scale
    back_result = (
        back_grad[0].astype(jnp.float32)
        + back_scale * amount
        - back_mid * cube * jnp.mean(back_mid * amount, axis=-1, keepdims=True)
    )
    back_result = back_result.astype(jnp.bfloat16)
    back_output = passed_along(back_result, "section", -1)

    contrib = front_gate[0] * halves_across(moved(front_pick.T, front_return))
    front_result = (middle + contrib).astype(jnp.bfloat16)
    front_output = passed_along(front_result, "section", 1)
    return (front_output[None], back_output[None])


def solution(mesh):
    placed = (
        P("section", "expert", None),
        P("section", "expert", None),
        P("section", "expert", None),
        P("section", "expert", None, None),
        P("section", "expert", None),
        P("section", "expert", None),
        P("section", "expert", None),
        P("section", "expert", None),
        P("section", "expert", None),
        P("section", "expert", None),
        P("section", None),
        P("section", "expert", None, None),
        P("section", "expert", None, None),
        P("section", "expert", None, None),
    )
    return jax.shard_map(
        shards,
        mesh=mesh,
        in_specs=placed,
        out_specs=(P("section", "expert", None), P("section", "expert", None)),
        check_vma=False,
    )
```

time: 651 us -> 405 us (0.62)
  the two profiles are of different devices: /device:TPU:10 before, /device:TPU:0 now
where the time goes in v1:
time: 405 us; the launch traced here: 404 us
  waiting for transfers between devices  167 us (41%)
  matrix products  89.3 us (22%)
  starting transfers between devices  52.8 us (13%)
  local copies, waits for them, and re-layouts  40.5 us (10%)
  blocking collectives  27.3 us (7%)
  other arithmetic  25.1 us (6%)
    ppermute x14, waiting for transfers between devices, swapped(): lax.ppermute(array, 'expert', [(i, i ^ bit) for i in range(lax.axis_size(...  77.9 us
    all_to_all x3, waiting for transfers between devices, across_experts(): lax.all_to_all(array, 'expert', split_axis=0, concat_axis=0, axis_index_g...  41.3 us
    all_to_all x3, starting transfers between devices, across_experts(): lax.all_to_all(array, 'expert', split_axis=0, concat_axis=0, axis_index_g...  30.5 us
    ppermute x3, waiting for transfers between devices, gather_blocks(): column.append(lax.ppermute(kv_rows, 'expert', pairs))  28.3 us
    all_to_all x1, blocking collectives, across_experts(): lax.all_to_all(array, 'expert', split_axis=0, concat_axis=0, axis_index_g...  27.3 us
    ppermute x2, waiting for transfers between devices, passed_along(): lax.ppermute(array, axis, [(i, (i + by) % length) for i in range(length)])  19.8 us
    dot_general x4, matrix products, slice_backward(): lax.dot_general(gate_grad, w_gate, contract_last, preferred_element_type=...  18.8 us
    dot_general x4, matrix products, slice_forward(): jnp.dot(hidden, w_down, preferred_element_type=jnp.float32)  18.6 us
  transfers between devices with their start and end apart: 22, of which 12 were waited for; matrix products, arithmetic and copies ran while one was open for 28% of the time, Pallas kernels for 0%

profile of v1, /device:TPU:0, one launch (start us, length us, event | category | flops | bytes accessed | tf_op | source)
XLA Modules:
  0.0 403.6 jit_solution(9290464654591491357)
XLA Ops:
  0.7 1.6 fusion.21
  6.0 1.6 fusion.14
  7.6 2.1 convolution_convert_fusion.1
  9.7 6.5 %all-to-all-start.2 = ((bf16[4,72,3584]{2,1,0:T(8,128)(2,1)}), bf16[4,72,3584]{2,1,0:T(8,128)(2,1)}, u32[]{:S(2)}, u32[]{:S(2)}) async-start(bf16[4,72,3584]{2,1,0:T(8,128)(2,1)} %bitcast.216), calls=%async_computation.2 | async-start | bytes 4128768 | tf_op jit(solution)/shard_map/all_to_all | solution.py:33
  16.3 3.9 collective-permute-start
  20.2 4.3 %collective-permute-start.1 = (bf16[128,448]{1,0:T(8,128)(2,1)S(1)}, bf16[128,448]{1,0:T(8,128)(2,1)S(1)}, u32[]{:S(2)}, u32[]{:S(2)}) collective-permute-start(bf16[128,448]{1,0:T(8,128)(2,1)S(1)} %bitcast.218), channel_id=1, source_target_pairs={{0,8},{1,9},{2,10},{3,11},{4,12},{5,13},{6,14},{7,15},{16,24},{17,... | collective-permute-start | bytes 344072 | tf_op jit(solution)/shard_map/ppermute | solution.py:44
  29.7 23.8 %collective-permute-done = bf16[128,448]{1,0:T(8,128)(2,1)S(1)} collective-permute-done((bf16[128,448]{1,0:T(8,128)(2,1)S(1)}, bf16[128,448]{1,0:T(8,128)(2,1)S(1)}, u32[]{:S(2)}, u32[]{:S(2)}) %collective-permute-start) | collective-permute-done | bytes 114720 | tf_op jit(solution)/shard_map/ppermute | solution.py:44
  53.5 2.9 collective-permute-done.1
  56.4 1.6 collective-permute-done.2
  60.4 3.4 all-to-all-done.2
  63.8 4.2 %convolution_convert_fusion = bf16[288,3584]{1,0:T(8,128)(2,1)} fusion(bf16[288,3584]{1,0:T(8,128)(2,1)} %bitcast.32, s32[288]{0:T(512)} %reshape.451), kind=kOutput, calls=%fused_computation.2 | convolution fusion | flops 595657728 | bytes 4129920 | tf_op jit(solution)/shard_map/dot_general | solution.py:111
  77.4 3.2 reshape_squeeze.9
  85.2 2.2 gather_fusion
  88.9 3.0 fusion.258
  93.0 1.7 copy.39
  96.2 20.0 %collective-permute-done.14 = bf16[288,3584]{1,0:T(8,128)(2,1)} collective-permute-done((bf16[288,3584]{1,0:T(8,128)(2,1)}, bf16[288,3584]{1,0:T(8,128)(2,1)}, u32[]{:S(2)}, u32[]{:S(2)}) %collective-permute-start.14) | collective-permute-done | bytes 2064416 | tf_op jit(solution)/shard_map/ppermute | solution.py:27
  116.2 1.6 fusion.143
  117.9 3.3 fusion.263
  121.2 1.9 fusion.36
  123.2 2.1 fusion.34
  125.3 1.7 fusion.76
  127.0 4.7 %fusion.74 = f32[144,3584]{1,0:T(8,128)} fusion(bf16[1,1,3584,256]{3,2,1,0:T(8,128)(2,1)} %param.25, f32[144,256]{1,0:T(8,128)S(1)} %fusion.34, bf16[1,1,3584,256]{3,2,1,0:T(8,128)(2,1)S(1)} %copy-done, bf16[288,3584]{1,0:T(8,128)(2,1)} %collective-permute-done.12, f32[144,256]{1,0:T(8,128)S(1)} %fusion.76), kind=kOutput, calls=%fused_computation.104 | convolution fusion | flops 528850944 | bytes 7061504 | tf_op jit(solution)/shard_map/dot_general | solution.py:150
  131.6 2.7 fusion.30
  134.3 1.7 fusion.68
  136.0 4.7 %fusion.66 = f32[144,3584]{1,0:T(8,128)} fusion(bf16[1,1,3584,256]{3,2,1,0:T(8,128)(2,1)} %param.25, f32[144,256]{1,0:T(8,128)S(1)} %fusion.30, bf16[1,1,3584,256]{3,2,1,0:T(8,128)(2,1)S(1)} %copy-done, bf16[288,3584]{1,0:T(8,128)(2,1)} %collective-permute-done.15, f32[144,256]{1,0:T(8,128)S(1)} %fusion.68), kind=kOutput, calls=%fused_computation.96 | convolution fusion | flops 528850944 | bytes 7061504 | tf_op jit(solution)/shard_map/dot_general | solution.py:150
  140.7 3.5 fusion.6
  144.7 1.7 fusion.3
  146.4 2.1 fusion.32
  148.5 1.7 fusion.72
  150.2 4.7 %fusion.70 = f32[144,3584]{1,0:T(8,128)} fusion(bf16[1,1,3584,256]{3,2,1,0:T(8,128)(2,1)} %param.25, f32[144,256]{1,0:T(8,128)S(1)} %fusion.32, bf16[1,1,3584,256]{3,2,1,0:T(8,128)(2,1)S(1)} %copy-done, bf16[288,3584]{1,0:T(8,128)(2,1)} %collective-permute-done.14, f32[144,256]{1,0:T(8,128)S(1)} %fusion.72), kind=kOutput, calls=%fused_computation.100 | convolution fusion | flops 528850944 | bytes 7061504 | tf_op jit(solution)/shard_map/dot_general | solution.py:150
  154.9 3.8 add_convert_fusion.1
  160.2 1.7 fusion.80
  161.9 4.8 %fusion.78 = f32[144,3584]{1,0:T(8,128)} fusion(bf16[1,1,3584,256]{3,2,1,0:T(8,128)(2,1)} %param.25, f32[144,256]{1,0:T(8,128)S(1)} %fusion.36, bf16[1,1,3584,256]{3,2,1,0:T(8,128)(2,1)S(1)} %copy-done, bf16[288,3584]{1,0:T(8,128)(2,1)} %convolution_convert_fusion, f32[144,256]{1,0:T(8,128)S(1)} %fusion.80), kind=kOutput, calls=%fused_computation.108 | convolution fusion | flops 528850944 | bytes 7061504 | tf_op jit(solution)/shard_map/dot_general | solution.py:150
  166.6 2.5 fusion.2
  169.2 15.0 %collective-permute-done.17 = bf16[144,3584]{1,0:T(8,128)(2,1)} collective-permute-done((bf16[144,3584]{1,0:T(8,128)(2,1)}, bf16[144,3584]{1,0:T(8,128)(2,1)}, u32[]{:S(2)}, u32[]{:S(2)}) %collective-permute-start.17) | collective-permute-done | bytes 1032224 | tf_op jit(solution)/shard_map/ppermute | solution.py:27
  186.4 1.7 convolution_convert_fusion.7
  188.1 19.8 %all-to-all-start.3 = ((bf16[4,72,1792]{2,1,0:T(8,128)(2,1)}), bf16[4,72,1792]{2,1,0:T(8,128)(2,1)}, u32[]{:S(2)}, u32[]{:S(2)}) async-start(bf16[4,72,1792]{2,1,0:T(8,128)(2,1)} %bitcast.33), calls=%async_computation.3 | async-start | bytes 2064384 | tf_op jit(solution)/shard_map/all_to_all | solution.py:33
  207.9 2.7 fusion.90
  210.7 2.5 copy.34
  213.2 3.5 reshape.444
  216.7 1.9 fusion.29
  218.9 14.3 %all-to-all-done.3 = bf16[4,72,1792]{2,1,0:T(8,128)(2,1)} async-done(((bf16[4,72,1792]{2,1,0:T(8,128)(2,1)}), bf16[4,72,1792]{2,1,0:T(8,128)(2,1)}, u32[]{:S(2)}, u32[]{:S(2)}) %all-to-all-start.3) | async-done | bytes 1032224 | tf_op jit(solution)/shard_map/all_to_all | solution.py:33
  233.2 1.9 fusion.170
  236.7 1.9 fusion.16
  239.1 27.3 %all_to_all.48 = bf16[4,72,1792]{2,1,0:T(8,128)(2,1)S(1)} all-to-all(bf16[4,72,1792]{2,1,0:T(8,128)(2,1)S(1)} %bitcast.222), channel_id=1, replica_groups={{0,4,8,12},{1,5,9,13},{2,6,10,14},{3,7,11,15},{16,20,24,28},{17,21,25,2..., dimensions={0} | all-to-all | bytes 2064384 | tf_op jit(solution)/shard_map/all_to_all | solution.py:33
  270.6 22.2 %collective-permute-done.7 = bf16[144,3584]{1,0:T(8,128)(2,1)S(1)} collective-permute-done((bf16[144,3584]{1,0:T(8,128)(2,1)}, bf16[144,3584]{1,0:T(8,128)(2,1)S(1)}, u32[]{:S(2)}, u32[]{:S(2)}) %collective-permute-start.7) | collective-permute-done | bytes 1032224 | tf_op jit(solution)/shard_map/ppermute | solution.py:27
  294.3 3.6 collective-permute-done.8
  299.3 4.7 %convolution_convert_fusion.2 = bf16[144,3584]{1,0:T(8,128)(2,1)} fusion(bf16[1,1,256,3584]{3,2,1,0:T(8,128)(2,1)} %param.27, f32[144,256]{1,0:T(8,128)S(1)} %fusion.56, bf16[144,3584]{1,0:T(8,128)(2,1)} %copy-done.13, bf16[1,1,3584,256]{3,2,1,0:T(8,128)(2,1)} %param.25), kind=kOutput, calls=%fused_computation.14 | convolution fusion | flops 529219584 | bytes 5881856 | tf_op jit(solution)/shard_map/dot_general | solution.py:137
  304.1 1.7 fusion.60
  305.8 4.6 %convolution_convert_fusion.4 = bf16[144,3584]{1,0:T(8,128)(2,1)} fusion(bf16[1,1,256,3584]{3,2,1,0:T(8,128)(2,1)} %param.27, f32[144,256]{1,0:T(8,128)S(1)} %fusion.60, bf16[144,3584]{1,0:T(8,128)(2,1)} %collective-permute-done.5, bf16[1,1,3584,256]{3,2,1,0:T(8,128)(2,1)} %param.25), kind=kOutput, calls=%fused_computation.17 | convolution fusion | flops 529219584 | bytes 5881856 | tf_op jit(solution)/shard_map/dot_general | solution.py:137
  310.8 1.7 fusion.58
  312.5 4.9 %add_convert_fusion.3 = bf16[144,3584]{1,0:T(8,128)(2,1)} fusion(bf16[144,3584]{1,0:T(8,128)(2,1)} %collective-permute-done.9, bf16[1,1,256,3584]{3,2,1,0:T(8,128)(2,1)} %param.27, f32[144,256]{1,0:T(8,128)S(1)} %fusion.58, bf16[144,3584]{1,0:T(8,128)(2,1)} %copy-done.12, bf16[1,1,3584,256]{3,2,1,0:T(8,128)(2,1)} %param.25), kind=kOutput, calls=%fused_computation.44 | convolution fusion | flops 531283968 | bytes 6914048 | tf_op jit(solution)/shard_map/dot_general | solution.py:137
  318.9 2.1 fusion.88
  321.0 4.3 %fusion.8 = f32[144,3584]{1,0:T(8,128)} fusion(bf16[1,1,256,3584]{3,2,1,0:T(8,128)(2,1)} %param.27, bf16[1,1,3584,256]{3,2,1,0:T(8,128)(2,1)S(1)} %copy-done, f32[144,256]{1,0:T(8,128)S(1)} %fusion.88, bf16[144,1792]{1,0:T(8,128)(2,1)} %copy-done.10, bf16[144,1792]{1,0:T(8,128)(2,1)S(1)} %get-tuple-element.18), kind=kOutput, calls=%fused_computation.19 | convolution fusion | flops 531800064 | bytes 6914048 | tf_op jit(solution)/shard_map/dot_general | solution.py:137
  325.3 17.2 %collective-permute-done.10 = bf16[144,3584]{1,0:T(8,128)(2,1)} collective-permute-done((bf16[144,3584]{1,0:T(8,128)(2,1)}, bf16[144,3584]{1,0:T(8,128)(2,1)}, u32[]{:S(2)}, u32[]{:S(2)}) %collective-permute-start.10) | collective-permute-done | bytes 1032224 | tf_op jit(solution)/shard_map/ppermute | solution.py:27
  342.6 2.5 add_convert_fusion.2
  345.1 1.7 convolution_convert_fusion.8
  346.8 4.2 %all-to-all-start.1 = ((bf16[4,72,1792]{2,1,0:T(8,128)(2,1)}), bf16[4,72,1792]{2,1,0:T(8,128)(2,1)}, u32[]{:S(2)}, u32[]{:S(2)}) async-start(bf16[4,72,1792]{2,1,0:T(8,128)(2,1)} %bitcast.221), calls=%async_computation.1 | async-start | bytes 2064384 | tf_op jit(solution)/shard_map/all_to_all | solution.py:33
  351.1 1.6 collective-permute-start.18
  352.7 23.6 %all-to-all-done.1 = bf16[4,72,1792]{2,1,0:T(8,128)(2,1)} async-done(((bf16[4,72,1792]{2,1,0:T(8,128)(2,1)}), bf16[4,72,1792]{2,1,0:T(8,128)(2,1)}, u32[]{:S(2)}, u32[]{:S(2)}) %all-to-all-start.1) | async-done | bytes 1032224 | tf_op jit(solution)/shard_map/all_to_all | solution.py:33
  376.3 1.9 fusion.171
  379.2 1.6 collective-permute-start.11
  380.8 19.8 %collective-permute-done.11 = bf16[128,3584]{1,0:T(8,128)(2,1)S(1)} collective-permute-done((bf16[128,3584]{1,0:T(8,128)(2,1)S(1)}, bf16[128,3584]{1,0:T(8,128)(2,1)S(1)}, u32[]{:S(2)}, u32[]{:S(2)}) %collective-permute-start.11) | collective-permute-done | bytes 917536 | tf_op jit(solution)/shard_map/ppermute | solution.py:19
  401.4 2.2 copy.55
  (154 shorter events, 46.9 us)
Async XLA Ops:
  0.6 126.3 %copy-start = (bf16[1,1,3584,256]{3,2,1,0:T(8,128)(2,1)S(1)}, bf16[1,1,3584,256]{3,2,1,0:T(8,128)(2,1)}, u32[]{:S(2)}) copy-start(bf16[1,1,3584,256]{3,2,1,0:T(8,128)(2,1)} %param.26) | copy-start | bytes 5505028
  0.6 5.3 %copy-start.7 = (bf16[1,128,3584]{2,1,0:T(8,128)(2,1)S(1)}, bf16[1,128,3584]{2,1,0:T(8,128)(2,1)}, u32[]{:S(2)}) copy-start(bf16[1,128,3584]{2,1,0:T(8,128)(2,1)} %param.20) | copy-start | bytes 2752516
  2.8 4.9 %copy-start.29 = (f32[128]{0:T(128)}, f32[128]{0:T(128)S(1)}, u32[]{:S(2)}) copy-start(f32[128]{0:T(128)S(1)} %get-tuple-element.35) | copy-start | bytes 1540
  5.9 1.7 copy-start.27
  9.7 6.5 %copy-start.18 = (bf16[1,128,448]{1,2,0:T(8,128)(2,1)S(1)}, bf16[1,128,448]{1,2,0:T(8,128)(2,1)}, u32[]{:S(2)}) copy-start(bf16[1,128,448]{1,2,0:T(8,128)(2,1)} %param.16) | copy-start | bytes 344068
  9.7 16.1 %copy-start.24 = (s32[1,2,2,4]{3,2,1,0:T(2,128)S(1)}, s32[1,2,2,4]{3,2,1,0:T(2,128)}, u32[]{:S(2)}) copy-start(s32[1,2,2,4]{3,2,1,0:T(2,128)} %param.17) | copy-start | bytes 196
  9.7 17.4 %copy-start.25 = (s32[1,128,1]{1,2,0:T(1,128)S(1)}, s32[1,128,1]{1,2,0:T(1,128)}, u32[]{:S(2)}) copy-start(s32[1,128,1]{1,2,0:T(1,128)} %param.18) | copy-start | bytes 1540
  9.7 54.0 %all-to-all-start.2 = ((bf16[4,72,3584]{2,1,0:T(8,128)(2,1)}), bf16[4,72,3584]{2,1,0:T(8,128)(2,1)}, u32[]{:S(2)}, u32[]{:S(2)}) async-start(bf16[4,72,3584]{2,1,0:T(8,128)(2,1)} %bitcast.216), calls=%async_computation.2 | async-start | bytes 4128768 | tf_op jit(solution)/shard_map/all_to_all | solution.py:33
  16.3 37.2 %collective-permute-start = (bf16[128,448]{1,0:T(8,128)(2,1)S(1)}, bf16[128,448]{1,0:T(8,128)(2,1)S(1)}, u32[]{:S(2)}, u32[]{:S(2)}) collective-permute-start(bf16[128,448]{1,0:T(8,128)(2,1)S(1)} %bitcast.217), channel_id=1, source_target_pairs={{0,4},{1,5},{2,6},{3,7},{4,8},{5,9},{6,10},{7,11},{8,12},{9,13},{1... | collective-permute-start | bytes 344072 | tf_op jit(solution)/shard_map/ppermute | solution.py:44
  20.2 36.1 %collective-permute-start.1 = (bf16[128,448]{1,0:T(8,128)(2,1)S(1)}, bf16[128,448]{1,0:T(8,128)(2,1)S(1)}, u32[]{:S(2)}, u32[]{:S(2)}) collective-permute-start(bf16[128,448]{1,0:T(8,128)(2,1)S(1)} %bitcast.218), channel_id=1, source_target_pairs={{0,8},{1,9},{2,10},{3,11},{4,12},{5,13},{6,14},{7,15},{16,24},{17,... | collective-permute-start | bytes 344072 | tf_op jit(solution)/shard_map/ppermute | solution.py:44
  24.5 33.5 %collective-permute-start.2 = (bf16[128,448]{1,0:T(8,128)(2,1)S(1)}, bf16[128,448]{1,0:T(8,128)(2,1)S(1)}, u32[]{:S(2)}, u32[]{:S(2)}) collective-permute-start(bf16[128,448]{1,0:T(8,128)(2,1)S(1)} %bitcast.219), channel_id=1, source_target_pairs={{0,12},{1,13},{2,14},{3,15},{16,28},{17,29},{18,30},{19,31}} | collective-permute-start | bytes 344072 | tf_op jit(solution)/shard_map/ppermute | solution.py:44
  53.5 4.5 %copy-start.16 = (bf16[128,448]{1,0:T(8,128)(2,1)}, bf16[128,448]{1,0:T(8,128)(2,1)S(1)}, u32[]{:S(2)}) copy-start(bf16[128,448]{1,0:T(8,128)(2,1)S(1)} %collective-permute-done) | copy-start | bytes 344068
  56.4 1.7 copy-start.15
  58.9 16.4 %collective-permute-start.3 = (bf16[512,448]{1,0:T(8,128)(2,1)}, bf16[512,448]{1,0:T(8,128)(2,1)S(1)}, u32[]{:S(2)}, u32[]{:S(2)}) collective-permute-start(bf16[512,448]{1,0:T(8,128)(2,1)} %pad_maximum_fusion.1), channel_id=1, source_target_pairs={{0,2},{1,3},{2,0},{3,1},{4,6},{5,7},{6,4},{7,5},{8,10},{9,11},{10,... | collective-permute-start | bytes 1376264 | tf_op jit(solution)/shard_map/ppermute | solution.py:27
  63.8 5.7 %copy-start.35 = (s32[2]{0:T(128)S(1)}, s32[2]{0:T(128)}, u32[]{:S(2)}) copy-start(s32[2]{0:T(128)} %add_multiply_fusion) | copy-start | bytes 28
  67.9 48.3 %collective-permute-start.14 = (bf16[288,3584]{1,0:T(8,128)(2,1)}, bf16[288,3584]{1,0:T(8,128)(2,1)}, u32[]{:S(2)}, u32[]{:S(2)}) collective-permute-start(bf16[288,3584]{1,0:T(8,128)(2,1)} %convolution_convert_fusion), channel_id=1, source_target_pairs={{0,2},{1,3},{2,0},{3,1},{4,6},{5,7},{6,4},{7,5},{8,10},{9,11},{10,... | collective-permute-start | bytes 6193160 | tf_op jit(solution)/shard_map/ppermute | solution.py:27
  75.2 2.2 copy-start.31
  76.1 4.5 %copy-start.23 = (s32[2,2,4]{2,1,0:T(2,128)S(1)}, s32[2,2,4]{2,1,0:T(2,128)}, u32[]{:S(2)}) copy-start(s32[2,2,4]{2,1,0:T(2,128)} %multiply_bitcast_fusion) | copy-start | bytes 196
  76.1 4.8 %copy-start.17 = (s32[128,4]{1,0:T(8,128)S(1)}, s32[128,4]{1,0:T(8,128)}, u32[]{:S(2)}) copy-start(s32[128,4]{1,0:T(8,128)} %fusion.230) | copy-start | bytes 6148
  76.2 5.0 %copy-start.26 = (s32[1,128,1]{1,2,0:T(1,128)S(1)}, s32[1,128,1]{1,2,0:T(1,128)}, u32[]{:S(2)}) copy-start(s32[1,128,1]{1,2,0:T(1,128)} %param.18) | copy-start | bytes 1540
  76.2 5.7 %copy-start.32 = (s32[2,64]{1,0:T(2,128)S(1)}, s32[2,64]{1,0:T(2,128)}, u32[]{:S(2)}) copy-start(s32[2,64]{1,0:T(2,128)} %iota_add_fusion) | copy-start | bytes 1540
  77.4 5.2 %collective-permute-start.4 = (bf16[1024,448]{0,1:T(8,128)(2,1)}, bf16[1024,448]{0,1:T(8,128)(2,1)}, u32[]{:S(2)}, u32[]{:S(2)}) collective-permute-start(bf16[1024,448]{0,1:T(8,128)(2,1)} %copy.27), channel_id=1, source_target_pairs={{0,1},{1,0},{2,3},{3,2},{4,5},{5,4},{6,7},{7,6},{8,9},{9,8},{10,11... | collective-permute-start | bytes 2752520 | tf_op jit(solution)/shard_map/ppermute | solution.py:27
  81.3 41.9 %collective-permute-start.12 = (bf16[288,3584]{1,0:T(8,128)(2,1)}, bf16[288,3584]{1,0:T(8,128)(2,1)}, u32[]{:S(2)}, u32[]{:S(2)}) collective-permute-start(bf16[288,3584]{1,0:T(8,128)(2,1)} %convolution_convert_fusion), channel_id=1, source_target_pairs={{0,1},{1,0},{2,3},{3,2},{4,5},{5,4},{6,7},{7,6},{8,9},{9,8},{10,11... | collective-permute-start | bytes 6193160 | tf_op jit(solution)/shard_map/ppermute | solution.py:27
  88.9 27.3 %copy-start.11 = (bf16[2,64,2,16,112]{4,3,2,1,0:T(8,128)(2,1)S(1)}, bf16[2,64,2,16,112]{4,3,2,1,0:T(8,128)(2,1)}, u32[]{:S(2)}) copy-start(bf16[2,64,2,16,112]{4,3,2,1,0:T(8,128)(2,1)} %reshape_squeeze.9) | copy-start | bytes 2752516
  116.2 15.4 %collective-permute-start.15 = (bf16[288,3584]{1,0:T(8,128)(2,1)}, bf16[288,3584]{1,0:T(8,128)(2,1)}, u32[]{:S(2)}, u32[]{:S(2)}) collective-permute-start(bf16[288,3584]{1,0:T(8,128)(2,1)} %collective-permute-done.14), channel_id=1, source_target_pairs={{0,1},{1,0},{2,3},{3,2},{4,5},{5,4},{6,7},{7,6},{8,9},{9,8},{10,11... | collective-permute-start | bytes 6193160 | tf_op jit(solution)/shard_map/ppermute | solution.py:27
  116.2 1.6 copy-start.21
  117.9 3.4 copy-start.5
  123.2 2.1 copy-start.1
  131.6 2.7 copy-start.2
  140.7 4.0 copy-start.9
  144.2 2.3 copy-start.6
  144.2 10.7 %collective-permute-start.16 = (bf16[144,3584]{1,0:T(8,128)(2,1)}, bf16[144,3584]{1,0:T(8,128)(2,1)}, u32[]{:S(2)}, u32[]{:S(2)}) collective-permute-start(bf16[144,3584]{1,0:T(8,128)(2,1)} %fusion.6), channel_id=1, source_target_pairs={{0,1},{1,0},{2,3},{3,2},{4,5},{5,4},{6,7},{7,6},{8,9},{9,8},{10,11... | collective-permute-start | bytes 3096584 | tf_op jit(solution)/shard_map/ppermute | solution.py:27
  146.4 2.1 copy-start.3
  146.4 22.7 %collective-permute-start.13 = (bf16[144,3584]{1,0:T(8,128)(2,1)}, bf16[144,3584]{1,0:T(8,128)(2,1)S(1)}, u32[]{:S(2)}, u32[]{:S(2)}) collective-permute-start(bf16[144,3584]{1,0:T(8,128)(2,1)} %fusion.3), channel_id=1, source_target_pairs={{0,1},{1,0},{2,3},{3,2},{4,5},{5,4},{6,7},{7,6},{8,9},{9,8},{10,11... | collective-permute-start | bytes 3096584 | tf_op jit(solution)/shard_map/ppermute | solution.py:27
  154.9 5.3 %copy-start.4 = (bf16[1,1,3584,256]{3,2,1,0:T(8,128)(2,1)S(1)}, bf16[1,1,3584,256]{3,2,1,0:T(8,128)(2,1)}, u32[]{:S(2)}) copy-start(bf16[1,1,3584,256]{3,2,1,0:T(8,128)(2,1)} %param.25) | copy-start | bytes 5505028
  158.7 25.5 %collective-permute-start.17 = (bf16[144,3584]{1,0:T(8,128)(2,1)}, bf16[144,3584]{1,0:T(8,128)(2,1)}, u32[]{:S(2)}, u32[]{:S(2)}) collective-permute-start(bf16[144,3584]{1,0:T(8,128)(2,1)} %add_convert_fusion.1), channel_id=1, source_target_pairs={{0,2},{1,3},{2,0},{3,1},{4,6},{5,7},{6,4},{7,5},{8,10},{9,11},{10,... | collective-permute-start | bytes 3096584 | tf_op jit(solution)/shard_map/ppermute | solution.py:27
  185.7 0.7 copy-start.22
  188.1 19.8 %copy-start.19 = (bf16[2,1,256,1,1,112]{2,5,0,4,3,1:T(8,128)(2,1)S(1)}, bf16[2,1,256,1,1,112]{2,5,0,4,3,1:T(8,128)(2,1)}, u32[]{:S(2)}) copy-start(bf16[2,1,256,1,1,112]{2,5,0,4,3,1:T(8,128)(2,1)} %copy.38) | copy-start | bytes 344068
  188.1 19.8 %copy-start.20 = (bf16[2,1,256,1,1,112]{2,5,0,4,3,1:T(8,128)(2,1)S(1)}, bf16[2,1,256,1,1,112]{2,5,0,4,3,1:T(8,128)(2,1)}, u32[]{:S(2)}) copy-start(bf16[2,1,256,1,1,112]{2,5,0,4,3,1:T(8,128)(2,1)} %copy.37) | copy-start | bytes 344068
  188.1 45.1 %all-to-all-start.3 = ((bf16[4,72,1792]{2,1,0:T(8,128)(2,1)}), bf16[4,72,1792]{2,1,0:T(8,128)(2,1)}, u32[]{:S(2)}, u32[]{:S(2)}) async-start(bf16[4,72,1792]{2,1,0:T(8,128)(2,1)} %bitcast.33), calls=%async_computation.3 | async-start | bytes 2064384 | tf_op jit(solution)/shard_map/all_to_all | solution.py:33
  216.7 16.5 %copy-start.28 = (s32[256]{0:T(256)S(1)}, s32[256]{0:T(256)}, u32[]{:S(2)}) copy-start(s32[256]{0:T(256)} %copy-done.27) | copy-start | bytes 3076
  235.1 1.2 copy-start.8
  235.3 1.4 copy-start.14
  235.3 1.4 copy-start.30
  235.3 1.4 copy-start.33
  267.2 0.8 copy-start.10
  269.1 23.7 %collective-permute-start.7 = (bf16[144,3584]{1,0:T(8,128)(2,1)}, bf16[144,3584]{1,0:T(8,128)(2,1)S(1)}, u32[]{:S(2)}, u32[]{:S(2)}) collective-permute-start(bf16[144,3584]{1,0:T(8,128)(2,1)} %pad_maximum_fusion), channel_id=1, source_target_pairs={{0,2},{1,3},{2,0},{3,1},{4,6},{5,7},{6,4},{7,5},{8,10},{9,11},{10,... | collective-permute-start | bytes 3096584 | tf_op jit(solution)/shard_map/ppermute | solution.py:27
  292.8 1.0 copy-start.12
  293.8 4.1 %collective-permute-start.8 = (bf16[144,3584]{1,0:T(8,128)(2,1)S(1)}, bf16[144,3584]{1,0:T(8,128)(2,1)S(1)}, u32[]{:S(2)}, u32[]{:S(2)}) collective-permute-start(bf16[144,3584]{1,0:T(8,128)(2,1)S(1)} %collective-permute-done.7), channel_id=1, source_target_pairs={{0,1},{1,0},{2,3},{3,2},{4,5},{5,4},{6,7},{7,6},{8,9},{9,8},{10,11... | collective-permute-start | bytes 3096584 | tf_op jit(solution)/shard_map/ppermute | solution.py:27
  293.8 10.3 %collective-permute-start.5 = (bf16[144,3584]{1,0:T(8,128)(2,1)}, bf16[144,3584]{1,0:T(8,128)(2,1)}, u32[]{:S(2)}, u32[]{:S(2)}) collective-permute-start(bf16[144,3584]{1,0:T(8,128)(2,1)} %pad_maximum_fusion), channel_id=1, source_target_pairs={{0,1},{1,0},{2,3},{3,2},{4,5},{5,4},{6,7},{7,6},{8,9},{9,8},{10,11... | collective-permute-start | bytes 3096584 | tf_op jit(solution)/shard_map/ppermute | solution.py:27
  297.9 1.0 copy-start.13
  304.0 8.5 %collective-permute-start.9 = (bf16[144,3584]{1,0:T(8,128)(2,1)}, bf16[144,3584]{1,0:T(8,128)(2,1)}, u32[]{:S(2)}, u32[]{:S(2)}) collective-permute-start(bf16[144,3584]{1,0:T(8,128)(2,1)} %convolution_convert_fusion.2), channel_id=1, source_target_pairs={{0,1},{1,0},{2,3},{3,2},{4,5},{5,4},{6,7},{7,6},{8,9},{9,8},{10,11... | collective-permute-start | bytes 3096584 | tf_op jit(solution)/shard_map/ppermute | solution.py:27
  310.4 14.9 %collective-permute-start.6 = (bf16[144,3584]{1,0:T(8,128)(2,1)}, bf16[144,3584]{1,0:T(8,128)(2,1)}, u32[]{:S(2)}, u32[]{:S(2)}) collective-permute-start(bf16[144,3584]{1,0:T(8,128)(2,1)} %convolution_convert_fusion.4), channel_id=1, source_target_pairs={{0,1},{1,0},{2,3},{3,2},{4,5},{5,4},{6,7},{7,6},{8,9},{9,8},{10,11... | collective-permute-start | bytes 3096584 | tf_op jit(solution)/shard_map/ppermute | solution.py:27
  317.4 25.2 %collective-permute-start.10 = (bf16[144,3584]{1,0:T(8,128)(2,1)}, bf16[144,3584]{1,0:T(8,128)(2,1)}, u32[]{:S(2)}, u32[]{:S(2)}) collective-permute-start(bf16[144,3584]{1,0:T(8,128)(2,1)} %add_convert_fusion.3), channel_id=1, source_target_pairs={{0,2},{1,3},{2,0},{3,1},{4,6},{5,7},{6,4},{7,5},{8,10},{9,11},{10,... | collective-permute-start | bytes 3096584 | tf_op jit(solution)/shard_map/ppermute | solution.py:27
  346.8 29.4 %all-to-all-start.1 = ((bf16[4,72,1792]{2,1,0:T(8,128)(2,1)}), bf16[4,72,1792]{2,1,0:T(8,128)(2,1)}, u32[]{:S(2)}, u32[]{:S(2)}) async-start(bf16[4,72,1792]{2,1,0:T(8,128)(2,1)} %bitcast.221), calls=%async_computation.1 | async-start | bytes 2064384 | tf_op jit(solution)/shard_map/all_to_all | solution.py:33
  351.1 29.7 %collective-permute-start.18 = (bf16[128,3584]{1,0:T(8,128)(2,1)}, bf16[128,3584]{1,0:T(8,128)(2,1)}, u32[]{:S(2)}, u32[]{:S(2)}) collective-permute-start(bf16[128,3584]{1,0:T(8,128)(2,1)} %get-tuple-element.32), channel_id=1, source_target_pairs={{0,16},{16,0},{1,17},{17,1},{2,18},{18,2},{3,19},{19,3},{4,20},{20... | collective-permute-start | bytes 2752520 | tf_op jit(solution)/shard_map/ppermute | solution.py:19
  378.2 0.7 copy-start.34
  379.2 21.4 %collective-permute-start.11 = (bf16[128,3584]{1,0:T(8,128)(2,1)S(1)}, bf16[128,3584]{1,0:T(8,128)(2,1)S(1)}, u32[]{:S(2)}, u32[]{:S(2)}) collective-permute-start(bf16[128,3584]{1,0:T(8,128)(2,1)S(1)} %fusion.20), channel_id=1, source_target_pairs={{0,16},{16,0},{1,17},{17,1},{2,18},{18,2},{3,19},{19,3},{4,20},{20... | collective-permute-start | bytes 2752520 | tf_op jit(solution)/shard_map/ppermute | solution.py:19

commit v2 on v0

v2 whole, which is shorter than its diff:
```python
import functools

import jax
import jax.numpy as jnp
from jax import lax
from jax.experimental import pallas as pl
from jax.experimental.pallas import tpu as pltpu
from jax.sharding import PartitionSpec as P

GROUP = 4
HEADS = 32
HEAD_DIM = 112
KV_HEADS = 2
BLK = 64
SEL = 4
PARTS = 4
LANES = 128
VMEM_BYTES = 56 * 1024 * 1024

epsilon = 1e-06
negative_large = -1e30
bf16 = jnp.bfloat16
f32 = jnp.float32


def passed_along(array, axis, by):
    length = lax.axis_size(axis)
    return lax.ppermute(array, axis, [(i, (i + by) % length) for i in range(length)])


def swapped(array, bit):
    return lax.ppermute(array, "expert", [(i, i ^ bit) for i in range(lax.axis_size("expert"))])


def turned(array, by):
    length = lax.axis_size("expert")
    return lax.ppermute(
        array, "expert", [(i, (i + by * GROUP) % length) for i in range(length)]
    )


def call(body, outs, args, scratch=(), flops=0, smem=0):
    specs = [
        pl.BlockSpec(memory_space=pltpu.SMEM if i < smem else pltpu.VMEM)
        for i in range(len(args))
    ]
    many = isinstance(outs, list)
    shapes = outs if many else [outs]
    moved_bytes = sum(a.size * a.dtype.itemsize for a in list(args) + shapes)
    result = pl.pallas_call(
        body,
        out_shape=shapes,
        in_specs=specs,
        out_specs=[pl.BlockSpec(memory_space=pltpu.VMEM) for _ in shapes],
        scratch_shapes=list(scratch),
        compiler_params=pltpu.CompilerParams(vmem_limit_bytes=VMEM_BYTES),
        cost_estimate=pl.CostEstimate(
            flops=int(flops), bytes_accessed=int(moved_bytes), transcendentals=0
        ),
    )(*args)
    return result if many else result[0]


def dot(a, b):
    return jnp.dot(a, b, preferred_element_type=f32)


def dot_last(a, b):
    return lax.dot_general(a, b, (((1,), (1,)), ((), ())), preferred_element_type=f32)


def rms_scale(rows):
    return lax.rsqrt(jnp.mean(rows * rows, axis=-1, keepdims=True) + epsilon)


def iota(shape, dim):
    return lax.broadcasted_iota(jnp.int32, shape, dim)


def stacked(rows):
    width = rows.shape[1] // PARTS
    return jnp.concatenate([rows[:, p * width : (p + 1) * width] for p in range(PARTS)], axis=0)


def place_across(route_row, experts, capacity):
    tokens = route_row.shape[1]
    names = iota((max(8, experts), tokens), 0)
    onehot = jnp.where(names == route_row, 1.0, 0.0)
    earlier = jnp.where(iota((tokens, tokens), 0) < iota((tokens, tokens), 1), 1.0, 0.0)
    before = dot(onehot.astype(bf16), earlier.astype(bf16))
    place = onehot * (before + (names * (PARTS * capacity)).astype(f32))
    return jnp.sum(place, axis=0, keepdims=True).astype(jnp.int32)


def place_down(route_column, experts, capacity):
    tokens = route_column.shape[0]
    names = iota((tokens, LANES), 1)
    onehot = jnp.where(names == route_column, 1.0, 0.0)
    earlier = jnp.where(iota((tokens, tokens), 1) < iota((tokens, tokens), 0), 1.0, 0.0)
    before = dot(earlier.astype(bf16), onehot.astype(bf16))
    place = onehot * (before + (names * (PARTS * capacity)).astype(f32))
    return jnp.sum(place, axis=1, keepdims=True).astype(jnp.int32)


def pack_into(rows, place, out_refs, capacity):
    tokens = rows.shape[0]
    height = PARTS * capacity
    total = height * len(out_refs)
    places = jnp.concatenate([place + p * capacity for p in range(PARTS)], axis=1)
    pick = jnp.where(iota((total, PARTS * tokens), 0) == places, 1.0, 0.0).astype(bf16)
    packed = dot(pick, stacked(rows)).astype(bf16)
    for e, ref in enumerate(out_refs):
        ref[...] = packed[e * height : (e + 1) * height]


def back_pack_body(experts, capacity, route_ref, gate_ref, gain_ref, middle_ref, grad_ref, *outs):
    place = place_across(route_ref[...], experts, capacity)
    middle = middle_ref[...].astype(f32)
    normed = (middle * rms_scale(middle) * gain_ref[...]).astype(bf16)
    pack_into(normed, place, outs[:experts], capacity)
    scaled = (gate_ref[...] * grad_ref[...].astype(f32)).astype(bf16)
    pack_into(scaled, place, outs[experts:], capacity)


def join_body(capacity, *refs):
    chunks, out = refs[:-1], refs[-1]
    sources = len(chunks)
    height = PARTS * capacity
    rows = jnp.concatenate([ref[...] for ref in chunks], axis=0)
    slots = sources * capacity
    width = rows.shape[1]
    index = iota((slots, 1), 0)
    source = index * 0
    for s in range(1, sources):
        source = source + jnp.where(index >= s * capacity, 1, 0)
    first = index + source * (height - capacity)
    columns = iota((slots, rows.shape[0]), 1)
    for p in range(PARTS):
        pick = jnp.where(columns == first + p * capacity, 1.0, 0.0).astype(bf16)
        out[:, p * width : (p + 1) * width] = dot(pick, rows).astype(bf16)


def split_body(capacity, own_ref, core_ref, chip_ref, *outs):
    total = own_ref[...].astype(f32) + core_ref[...].astype(f32) + chip_ref[...].astype(f32)
    rows = stacked(total.astype(bf16))
    height = PARTS * capacity
    slots = own_ref.shape[0]
    count = height * len(outs)
    index = iota((count, 1), 0)
    group = index * 0
    source = index * 0
    for g in range(1, count // capacity):
        group = group + jnp.where(index >= g * capacity, 1, 0)
    for s in range(1, len(outs)):
        source = source + jnp.where(index >= s * height, 1, 0)
    part = group - source * PARTS
    place = part * slots + source * capacity + index - group * capacity
    pick = jnp.where(iota((count, PARTS * slots), 1) == place, 1.0, 0.0).astype(bf16)
    packed = dot(pick, rows).astype(bf16)
    for s, ref in enumerate(outs):
        ref[...] = packed[s * height : (s + 1) * height]


def unpacked(route_column, chunk_refs, experts, capacity):
    tokens = route_column.shape[0]
    place = place_down(route_column, experts, capacity)
    rows = jnp.concatenate([ref[...] for ref in chunk_refs], axis=0)
    columns = iota((tokens, rows.shape[0]), 1)
    parts = []
    for p in range(PARTS):
        pick = jnp.where(columns == place + p * capacity, 1.0, 0.0).astype(bf16)
        parts.append(dot(pick, rows))
    return jnp.concatenate(parts, axis=1)


def front_finish_body(experts, capacity, route_ref, gate_ref, middle_ref, *refs):
    chunks, out = refs[:-1], refs[-1]
    contrib = gate_ref[...] * unpacked(route_ref[...], chunks, experts, capacity)
    out[...] = (middle_ref[...].astype(f32) + contrib).astype(bf16)


def back_finish_body(experts, capacity, route_ref, gain_ref, middle_ref, grad_ref, *refs):
    chunks, out = refs[:-1], refs[-1]
    amount = gain_ref[...] * unpacked(route_ref[...], chunks, experts, capacity)
    middle = middle_ref[...].astype(f32)
    scale = rms_scale(middle)
    cube = scale * scale * scale
    mean = jnp.mean(middle * amount, axis=-1, keepdims=True)
    out[...] = (grad_ref[...].astype(f32) + scale * amount - middle * cube * mean).astype(bf16)


def forward_body(first_ref, second_ref, gate_ref, up_ref, down_ref, first_out, second_out):
    half = first_ref.shape[0]
    rows = jnp.concatenate([first_ref[...], second_ref[...]], axis=0)
    gate_val = dot(rows, gate_ref[...])
    up_val = dot(rows, up_ref[...])
    hidden = (gate_val / (1.0 + jnp.exp(-gate_val)) * up_val).astype(bf16)
    width = down_ref.shape[1]
    step = 4 * LANES
    for n in range(0, width, step):
        value = dot(hidden, down_ref[:, n : n + step]).astype(bf16)
        first_out[:, n : n + step] = value[:half]
        second_out[:, n : n + step] = value[half:]


def backward_body(
    first_ref, second_ref, first_grad, second_grad, gate_ref, up_ref, down_ref, first_out, second_out
):
    half = first_ref.shape[0]
    rows = jnp.concatenate([first_ref[...], second_ref[...]], axis=0)
    gate_val = dot(rows, gate_ref[...])
    up_val = dot(rows, up_ref[...])
    grads = jnp.concatenate([first_grad[...], second_grad[...]], axis=0)
    down_back = dot_last(grads, down_ref[...])
    sigmoid_val = 1.0 / (1.0 + jnp.exp(-gate_val))
    slope_val = sigmoid_val * (1.0 + gate_val * (1.0 - sigmoid_val))
    gate_grad = (down_back * up_val * slope_val).astype(bf16)
    up_grad = (down_back * gate_val * sigmoid_val).astype(bf16)
    width = down_ref.shape[1]
    step = 4 * LANES
    for n in range(0, width, step):
        value = dot_last(gate_grad, gate_ref[n : n + step])
        value = (value + dot_last(up_grad, up_ref[n : n + step])).astype(bf16)
        first_out[:, n : n + step] = value[:half]
        second_out[:, n : n + step] = value[half:]


def attend_body(
    experts,
    capacity,
    chosen_ref,
    index_ref,
    base_ref,
    route_ref,
    gain_ref,
    input_ref,
    query_ref,
    kv0,
    kv1,
    kv2,
    kv3,
    middle_ref,
    *refs,
):
    outs, (kv_all, kv_now, stack, attended) = refs[:experts], refs[experts:]
    tokens, width = query_ref.shape
    rows_each = kv0.shape[0]
    for place, ref in enumerate((kv0, kv1, kv2, kv3)):
        kv_all[place * rows_each : (place + 1) * rows_each, : ref.shape[1]] = ref[...]
    attended[...] = jnp.zeros_like(attended)
    heads_each = HEADS // KV_HEADS
    period = 8
    window = 2 * LANES
    keys = SEL * BLK
    lane = iota((keys, LANES), 1)
    batch = 4
    scale = HEAD_DIM**-0.5

    def one_block(block, _):
        top = pl.multiple_of(block * BLK, BLK)
        position = (base_ref[0] + block) * BLK + (iota((batch * BLK, keys), 0) & (BLK - 1))
        for head in range(KV_HEADS):
            key_pos = iota((1, keys), 1)
            shift = key_pos * 0
            for s in range(SEL):
                at = (block * KV_HEADS + head) * SEL + s
                start = pl.multiple_of(index_ref[at] * BLK, BLK)
                kv_now[s * BLK : (s + 1) * BLK, :] = kv_all[pl.ds(start, BLK), :].astype(f32)
                inside = (key_pos >= s * BLK) & (key_pos < (s + 1) * BLK)
                shift = jnp.where(inside, (chosen_ref[at] - s) * BLK, shift)
            allowed = key_pos + shift <= position
            sides = []
            for side in range(2):
                lead = (side * KV_HEADS + head) * HEAD_DIM
                tile = min(lead // LANES, 2)
                piece = kv_now[:, tile * LANES : tile * LANES + window]
                offset = lead - tile * LANES
                if offset:
                    piece = pltpu.roll(piece, window - offset, 1)
                sides.append(jnp.where(lane < HEAD_DIM, piece[:, :LANES], 0.0).astype(bf16))
            key_rows, value_rows = sides
            spots = []
            for j in range(heads_each):
                c = j % period
                tile = min(c * HEAD_DIM // LANES, period - 3)
                offset = c * HEAD_DIM - tile * LANES
                tile = tile + (j // period) * (period - 1) + head * heads_each * HEAD_DIM // LANES
                spots.append((tile * LANES, offset))
            for j, (lead, offset) in enumerate(spots):
                piece = query_ref[pl.ds(top, BLK), lead : lead + window].astype(f32)
                if offset:
                    piece = pltpu.roll(piece, window - offset, 1)
                stack[j * BLK : (j + 1) * BLK, :] = piece[:, :LANES].astype(bf16)
            for b in range(0, heads_each, batch):
                scores = dot_last(stack[b * BLK : (b + batch) * BLK, :], key_rows) * scale
                scores = jnp.where(allowed, scores, negative_large)
                exp_scores = jnp.exp(scores - jnp.max(scores, axis=-1, keepdims=True))
                total = jnp.sum(exp_scores, axis=-1, keepdims=True)
                mixed = dot((exp_scores / total).astype(bf16), value_rows)
                for i in range(batch):
                    lead, offset = spots[b + i]
                    piece = mixed[i * BLK : (i + 1) * BLK]
                    piece = jnp.concatenate([piece, jnp.zeros_like(piece)], axis=1)
                    if offset:
                        piece = pltpu.roll(piece, offset, 1)
                    spot = (pl.ds(top, BLK), slice(lead, lead + window))
                    attended[spot] = attended[spot] + piece
        return 0

    lax.fori_loop(0, tokens // BLK, one_block, 0)
    middle = (input_ref[...].astype(f32) + attended[...]).astype(bf16)
    middle_ref[...] = middle
    middle = middle.astype(f32)
    normed = (middle * rms_scale(middle) * gain_ref[...]).astype(bf16)
    pack_into(normed, place_across(route_ref[...], experts, capacity), outs, capacity)


def after(arrays, others):
    count = len(arrays)
    return list(lax.optimization_barrier(tuple(arrays) + tuple(others))[:count])


def shape_of(rows, columns, kind=bf16):
    return jax.ShapeDtypeStruct((rows, columns), kind)


def shards(
    front_input,
    queries,
    keys_values,
    selected_blocks,
    front_route,
    front_gate,
    back_middle,
    back_grad,
    back_route,
    back_gate,
    norm_gain,
    gate_slice,
    up_slice,
    down_slice,
):
    tokens, width = front_input.shape[1:]
    length = lax.axis_size("expert")
    experts = length // GROUP
    average = tokens // experts
    capacity = average + max(1, average // 8)
    slots = experts * capacity
    hidden_width = gate_slice.shape[3]
    weights = (gate_slice[0, 0], up_slice[0, 0], down_slice[0, 0])
    me = lax.axis_index("expert")
    group = me // GROUP
    chunk = shape_of(PARTS * capacity, width // PARTS)
    piece = shape_of(slots, width)
    whole = shape_of(tokens, width)

    column = [keys_values[0]]
    for back in range(1, experts):
        pairs = [(i, i + back * GROUP) for i in range(length - back * GROUP)]
        column.append(lax.ppermute(keys_values[0], "expert", pairs))
    column = jnp.concatenate(column, axis=0)
    other_chip = swapped(column, 2)
    kv = [column, other_chip, swapped(column, 1), swapped(other_chip, 1)]

    front_from = lax.rem(front_route[0] - group + experts, experts)
    back_from = lax.rem(back_route[0] - group + experts, experts)
    front_row, back_row = front_from.reshape(1, tokens), back_from.reshape(1, tokens)

    pack_flops = 4 * slots * PARTS * tokens * width
    packed = call(
        functools.partial(back_pack_body, experts, capacity),
        [chunk] * (2 * experts),
        (back_row, back_gate[0], norm_gain, back_middle[0], back_grad[0]),
        flops=2 * pack_flops,
    )
    packed = after(packed, [column])

    def joined(chunks):
        chunks = [chunks[0]] + [turned(chunks[k], k) for k in range(1, experts)]
        return call(functools.partial(join_body, capacity), piece, chunks, flops=pack_flops)

    def pieces_of(rows):
        other = swapped(rows, 2)
        return [rows, swapped(rows, 1), other, swapped(other, 1)]

    def returned(near, far):
        chip = far[0].astype(f32) + swapped(far[1], 1).astype(f32)
        parts = (near[0], swapped(near[1], 1), swapped(chip.astype(bf16), 2))
        chunks = call(
            functools.partial(split_body, capacity), [chunk] * experts, parts, flops=pack_flops
        )
        return [chunks[0]] + [turned(chunks[k], -k) for k in range(1, experts)]

    back_rows = joined(packed[:experts])
    grad_chunks = after(packed[experts:], [back_rows])
    back_pieces = pieces_of(back_rows)
    back_grads = joined(grad_chunks)
    grad_pieces = pieces_of(back_grads)

    per_device = tokens // BLK
    chosen = selected_blocks[0].reshape(-1)
    owner = chosen // per_device
    place = (owner % GROUP) ^ (me % GROUP)
    place = (place % 2) * 2 + place // 2
    index = (place * experts + group - owner // GROUP) * per_device + chosen % per_device
    index = jnp.clip(index, 0, length * per_device - 1)
    base = (me * per_device).astype(jnp.int32).reshape(1)
    result = call(
        functools.partial(attend_body, experts, capacity),
        [whole] + [chunk] * experts,
        (chosen, index, base, front_row, norm_gain, front_input[0], queries[0], *kv),
        scratch=[
            pltpu.VMEM((length * tokens, 4 * LANES), bf16),
            pltpu.VMEM((SEL * BLK, 4 * LANES), f32),
            pltpu.VMEM((HEADS // KV_HEADS * BLK, LANES), bf16),
            pltpu.VMEM((tokens, width), f32),
        ],
        flops=pack_flops + 4 * tokens * HEADS * SEL * BLK * LANES,
        smem=3,
    )
    middle, front_chunks = result[0], result[1:]
    front_rows = joined(front_chunks)
    front_pieces = pieces_of(front_rows)

    work = 2 * 2 * slots * width * hidden_width

    def backward(first, second):
        return call(
            backward_body,
            [piece, piece],
            (*back_pieces[first:second], *grad_pieces[first:second], *weights),
            flops=5 * work,
        )

    def forward(first, second):
        return call(
            forward_body,
            [piece, piece],
            (*front_pieces[first:second], *weights),
            flops=3 * work,
        )

    back_far = backward(2, 4)
    back_near = backward(0, 2)
    back_return = returned(back_near, back_far)
    back_result = call(
        functools.partial(back_finish_body, experts, capacity),
        whole,
        (back_from, norm_gain, back_middle[0], back_grad[0], *back_return),
        flops=pack_flops,
    )
    back_output = passed_along(back_result, "section", -1)

    front_far = forward(2, 4)
    front_near = forward(0, 2)
    front_return = returned(front_near, front_far)
    front_result = call(
        functools.partial(front_finish_body, experts, capacity),
        whole,
        (front_from, front_gate[0], middle, *front_return),
        flops=pack_flops,
    )
    front_output = passed_along(front_result, "section", 1)
    return (front_output[None], back_output[None])


def solution(mesh):
    placed = (
        P("section", "expert", None),
        P("section", "expert", None),
        P("section", "expert", None),
        P("section", "expert", None, None),
        P("section", "expert", None),
        P("section", "expert", None),
        P("section", "expert", None),
        P("section", "expert", None),
        P("section", "expert", None),
        P("section", "expert", None),
        P("section", None),
        P("section", "expert", None, None),
        P("section", "expert", None, None),
        P("section", "expert", None, None),
    )
    return jax.shard_map(
        shards,
        mesh=mesh,
        in_specs=placed,
        out_specs=(P("section", "expert", None), P("section", "expert", None)),
        check_vma=False,
    )
```

time: 651 us -> 285 us (0.44)
  the two profiles are of different devices: /device:TPU:10 before, /device:TPU:0 now
where the time goes in v2:
time: 285 us
  waiting for transfers between devices  135 us (47%)
  Pallas kernels  71.1 us (25%)
  starting transfers between devices  60.3 us (21%)
  local copies, waits for them, and re-layouts  12.8 us (4%)
  other arithmetic  4.22 us (1%)
    pallas_call x13, Pallas kernels, call(): pl.pallas_call(body, out_shape=shapes, in_specs=specs, out_specs=[pl.Bloc...  71.1 us
    ppermute x15, waiting for transfers between devices, turned(): lax.ppermute(array, 'expert', [(i, (i + by * GROUP) % length) for i in ra...  60.1 us
    ppermute x18, waiting for transfers between devices, swapped(): lax.ppermute(array, 'expert', [(i, i ^ bit) for i in range(lax.axis_size(...  56 us
    ppermute x15, starting transfers between devices, turned(): lax.ppermute(array, 'expert', [(i, (i + by * GROUP) % length) for i in ra...  36.4 us
    ppermute x2, waiting for transfers between devices, passed_along(): lax.ppermute(array, axis, [(i, (i + by) % length) for i in range(length)])  19.3 us
    ppermute x3, starting transfers between devices, shards(): column.append(lax.ppermute(keys_values[0], 'expert', pairs))  10.7 us
    unnamed x75, local copies, waits for them, and re-layouts  10.4 us
    ppermute x18, starting transfers between devices, swapped(): lax.ppermute(array, 'expert', [(i, i ^ bit) for i in range(lax.axis_size(...  10.2 us
  transfers between devices with their start and end apart: 38, of which 14 were waited for; matrix products, arithmetic and copies ran while one was open for 2% of the time, Pallas kernels for 25%

profile of v2, /device:TPU:0, one launch (start us, length us, event | category | flops | bytes accessed | tf_op | source)
XLA Modules:
  0.0 284.7 jit_solution(10949667557405691910)
XLA Ops:
  0.6 1.0 copy.19
  1.6 4.9 %collective-permute-start = (bf16[128,448]{1,0:T(8,128)(2,1)S(1)}, bf16[128,448]{1,0:T(8,128)(2,1)S(1)}, u32[]{:S(2)}, u32[]{:S(2)}) collective-permute-start(bf16[128,448]{1,0:T(8,128)(2,1)S(1)} %bitcast.35), channel_id=1, source_target_pairs={{0,4},{1,5},{2,6},{3,7},{4,8},{5,9},{6,10},{7,11},{8,12},{9,13},{1... | collective-permute-start | bytes 344072 | tf_op jit(solution)/shard_map/ppermute | solution.py:360
  6.6 4.5 %collective-permute-start.1 = (bf16[128,448]{1,0:T(8,128)(2,1)S(1)}, bf16[128,448]{1,0:T(8,128)(2,1)S(1)}, u32[]{:S(2)}, u32[]{:S(2)}) collective-permute-start(bf16[128,448]{1,0:T(8,128)(2,1)S(1)} %bitcast.36), channel_id=1, source_target_pairs={{0,8},{1,9},{2,10},{3,11},{4,12},{5,13},{6,14},{7,15},{16,24},{17,... | collective-permute-start | bytes 344072 | tf_op jit(solution)/shard_map/ppermute | solution.py:360
  11.1 1.3 collective-permute-start.2
  12.4 1.4 copy.24.gate_ref
  13.8 1.2 compare_select_fusion.route_ref
  15.0 4.1 %shard_map.155 = (bf16[144,896]{1,0:T(8,128)(2,1)}, bf16[144,896]{1,0:T(8,128)(2,1)}, bf16[144,896]{1,0:T(8,128)(2,1)}, bf16[144,896]{1,0:T(8,128)(2,1)}, bf16[1...) custom-call(s32[1,128]{1,0:T(1,128)} %compare_select_fusion.route_ref, ...), custom_call_target="tpu_custom_call" | custom-call | flops 2113929216 | bytes 3914752 | tf_op jit(solution)/shard_map/pallas_call | solution.py:50
  19.5 3.4 %collective-permute-start.20 = (bf16[144,896]{1,0:T(8,128)(2,1)}, bf16[144,896]{1,0:T(8,128)(2,1)S(1)}, u32[]{:S(2)}, u32[]{:S(2)}) collective-permute-start(bf16[144,896]{1,0:T(8,128)(2,1)} %get-tuple-element.66), channel_id=1, source_target_pairs={{0,8},{1,9},{2,10},{3,11},{4,12},{5,13},{6,14},{7,15},{8,0},{9,1},... | collective-permute-start | bytes 774152 | tf_op jit(solution)/shard_map/ppermute | solution.py:37
  23.1 1.5 collective-permute-start.3
  24.6 5.9 %collective-permute-done.19.refs_1_ = bf16[144,896]{1,0:T(8,128)(2,1)S(1)} collective-permute-done((bf16[144,896]{1,0:T(8,128)(2,1)}, bf16[144,896]{1,0:T(8,128)(2,1)S(1)}, u32[]{:S(2)}, u32[]{:S(2)}) %collective-permute-start.19) | collective-permute-done | bytes 258080 | tf_op jit(solution)/shard_map/ppermute | solution.py:37
  30.5 9.3 %collective-permute-done.20.refs_2_ = bf16[144,896]{1,0:T(8,128)(2,1)S(1)} collective-permute-done((bf16[144,896]{1,0:T(8,128)(2,1)}, bf16[144,896]{1,0:T(8,128)(2,1)S(1)}, u32[]{:S(2)}, u32[]{:S(2)}) %collective-permute-start.20) | collective-permute-done | bytes 258080 | tf_op jit(solution)/shard_map/ppermute | solution.py:37
  39.9 0.7 copy-done.27
  40.6 0.7 copy-done.30
  41.3 3.4 %shard_map.156.first_ref = bf16[144,3584]{1,0:T(8,128)(2,1)} custom-call(bf16[144,896]{1,0:T(8,128)(2,1)} %get-tuple-element.64.refs_0_, bf16[144,896]{1,0:T(8,128)(2,1)} %copy-done.25, bf16[144,896]{1,0:T(8,128)(2,1)} %copy-done.27, bf16[144,896]{1,0:T(8,128)(2,1)} %copy-done.30), custom_call_target="tpu_custom_call" | custom-call | flops 1056964608 | bytes 2064384 | tf_op jit(solution)/shard_map/pallas_call | solution.py:50
  44.7 5.3 %collective-permute-start.23 = (bf16[144,896]{1,0:T(8,128)(2,1)S(1)}, bf16[144,896]{1,0:T(8,128)(2,1)S(1)}, u32[]{:S(2)}, u32[]{:S(2)}) collective-permute-start(bf16[144,896]{1,0:T(8,128)(2,1)S(1)} %copy-done.18), channel_id=1, source_target_pairs={{0,4},{1,5},{2,6},{3,7},{4,8},{5,9},{6,10},{7,11},{8,12},{9,13},{1... | collective-permute-start | bytes 774152 | tf_op jit(solution)/shard_map/ppermute | solution.py:37
  50.0 2.4 collective-permute-start.25
  52.4 1.5 collective-permute-start.28
  53.9 2.7 collective-permute-done.23.refs_1_
  56.6 9.0 %collective-permute-done.24.refs_2_ = bf16[144,896]{1,0:T(8,128)(2,1)S(1)} collective-permute-done((bf16[144,896]{1,0:T(8,128)(2,1)S(1)}, bf16[144,896]{1,0:T(8,128)(2,1)S(1)}, u32[]{:S(2)}, u32[]{:S(2)}) %collective-permute-start.24) | collective-permute-done | bytes 258080 | tf_op jit(solution)/shard_map/ppermute | solution.py:37
  65.6 1.1 collective-permute-done.25.refs_3_
  66.7 0.7 copy-done.31
  67.4 3.4 %shard_map.157.first_grad = bf16[144,3584]{1,0:T(8,128)(2,1)} custom-call(bf16[144,896]{1,0:T(8,128)(2,1)} %get-tuple-element.72.refs_0_, bf16[144,896]{1,0:T(8,128)(2,1)} %copy-done.26, bf16[144,896]{1,0:T(8,128)(2,1)} %copy-done.28, bf16[144,896]{1,0:T(8,128)(2,1)} %copy-done.31), custom_call_target="tpu_custom_call" | custom-call | flops 1056964608 | bytes 2064384 | tf_op jit(solution)/shard_map/pallas_call | solution.py:50
  70.8 1.5 collective-permute-start.30
  72.9 0.6 compare_select_fusion.2.route_ref
  73.5 0.6 fusion.8.index_ref
  74.3 0.7 collective-permute-done.5.kv3
  75.1 9.9 %shard_map.149 = (bf16[128,3584]{1,0:T(8,128)(2,1)}, bf16[144,896]{1,0:T(8,128)(2,1)}, bf16[144,896]{1,0:T(8,128)(2,1)}, bf16[144,896]{1,0:T(8,128)(2,1)}, bf16[144,896]{1,0:T(8,128)(2,1)}) custom-call(s32[16]{0:T(128)} %copy-done.7, s32[16]{0:T(128)} %fusion.8.index_ref, s32[1]{0:T(128)} %bitcast.2.base_ref, s32[1,128]{1,0:T(1,128)} %compare_select_fusion.2.route_ref, ...), custom_call_target="tpu_custom_call" | custom-call | flops 1593835520 | bytes 5634692 | tf_op jit(solution)/shard_map/pallas_call | solution.py:50
  85.0 6.5 %collective-permute-start.6 = (bf16[144,896]{1,0:T(8,128)(2,1)}, bf16[144,896]{1,0:T(8,128)(2,1)S(1)}, u32[]{:S(2)}, u32[]{:S(2)}) collective-permute-start(bf16[144,896]{1,0:T(8,128)(2,1)} %get-tuple-element.45), channel_id=1, source_target_pairs={{0,4},{1,5},{2,6},{3,7},{4,8},{5,9},{6,10},{7,11},{8,12},{9,13},{1... | collective-permute-start | bytes 774152 | tf_op jit(solution)/shard_map/ppermute | solution.py:37
  91.5 3.4 %collective-permute-start.7 = (bf16[144,896]{1,0:T(8,128)(2,1)}, bf16[144,896]{1,0:T(8,128)(2,1)S(1)}, u32[]{:S(2)}, u32[]{:S(2)}) collective-permute-start(bf16[144,896]{1,0:T(8,128)(2,1)} %get-tuple-element.46), channel_id=1, source_target_pairs={{0,8},{1,9},{2,10},{3,11},{4,12},{5,13},{6,14},{7,15},{8,0},{9,1},... | collective-permute-start | bytes 774152 | tf_op jit(solution)/shard_map/ppermute | solution.py:37
  94.9 6.8 %collective-permute-done.6.refs_1_ = bf16[144,896]{1,0:T(8,128)(2,1)S(1)} collective-permute-done((bf16[144,896]{1,0:T(8,128)(2,1)}, bf16[144,896]{1,0:T(8,128)(2,1)S(1)}, u32[]{:S(2)}, u32[]{:S(2)}) %collective-permute-start.6) | collective-permute-done | bytes 258080 | tf_op jit(solution)/shard_map/ppermute | solution.py:37
  101.6 10.6 %collective-permute-done.7.refs_2_ = bf16[144,896]{1,0:T(8,128)(2,1)S(1)} collective-permute-done((bf16[144,896]{1,0:T(8,128)(2,1)}, bf16[144,896]{1,0:T(8,128)(2,1)S(1)}, u32[]{:S(2)}, u32[]{:S(2)}) %collective-permute-start.7) | collective-permute-done | bytes 258080 | tf_op jit(solution)/shard_map/ppermute | solution.py:37
  112.2 0.7 copy-done.32
  113.0 3.5 %shard_map.150.first_ref = bf16[144,3584]{1,0:T(8,128)(2,1)} custom-call(bf16[144,896]{1,0:T(8,128)(2,1)} %get-tuple-element.44.refs_0_, bf16[144,896]{1,0:T(8,128)(2,1)} %copy-done.29, bf16[144,896]{1,0:T(8,128)(2,1)} %copy-done.32, bf16[144,896]{1,0:T(8,128)(2,1)} %copy-done.33), custom_call_target="tpu_custom_call" | custom-call | flops 1056964608 | bytes 2064384 | tf_op jit(solution)/shard_map/pallas_call | solution.py:50
  118.1 23.3 %collective-permute-done.11.first_ref = bf16[144,3584]{1,0:T(8,128)(2,1)S(1)} collective-permute-done((bf16[144,3584]{1,0:T(8,128)(2,1)}, bf16[144,3584]{1,0:T(8,128)(2,1)S(1)}, u32[]{:S(2)}, u32[]{:S(2)}) %collective-permute-start.11) | collective-permute-done | bytes 1032224 | tf_op jit(solution)/shard_map/ppermute | solution.py:32
  141.9 1.0 copy-done.14
  143.0 8.9 %shard_map.159 = (bf16[144,3584]{1,0:T(8,128)(2,1)}, bf16[144,3584]{1,0:T(8,128)(2,1)}) custom-call(bf16[144,3584]{1,0:T(8,128)(2,1)} %copy-done.11, bf16[144,3584]{1,0:T(8,128)(2,1)} %collective-permute-done.29.second_ref, bf16[144,3584]{1,0:T(8,128)(2,1)} %copy-done.12, bf16[144,3584]{1,0:T(8,128)(2,1)} %copy-done.14, bf16[3584,256]{1,0:T(8,128)(2,1)} %bitcast.21, ...), custom_call_target="tpu_custom_call" | custom-call | flops 2642411520 | bytes 11698176 | tf_op jit(solution)/shard_map/pallas_call | solution.py:50
  152.0 8.9 %shard_map.158 = (bf16[144,3584]{1,0:T(8,128)(2,1)}, bf16[144,3584]{1,0:T(8,128)(2,1)}) custom-call(bf16[144,3584]{1,0:T(8,128)(2,1)} %shard_map.156.first_ref, bf16[144,3584]{1,0:T(8,128)(2,1)} %collective-permute-done.22.second_ref, bf16[144,3584]{1,0:T(8,128)(2,1)} %shard_map.157.first_grad, bf16[144,3584]{1,0:T(8,128)(2,1)} %collective-permute-done.26.second_grad, ...), custom_call_target="tpu_custom_call" | custom-call | flops 2642411520 | bytes 11698176 | tf_op jit(solution)/shard_map/pallas_call | solution.py:50
  161.4 1.0 copy-done.4
  162.3 6.4 %shard_map.152 = (bf16[144,3584]{1,0:T(8,128)(2,1)}, bf16[144,3584]{1,0:T(8,128)(2,1)}) custom-call(bf16[144,3584]{1,0:T(8,128)(2,1)} %copy-done.2, bf16[144,3584]{1,0:T(8,128)(2,1)} %copy-done.4, bf16[3584,256]{1,0:T(8,128)(2,1)} %bitcast.23, bf16[3584,256]{1,0:T(8,128)(2,1)} %bitcast.27, bf16[256,3584]{1,0:T(8,128)(2,1)} %bitcast.31), custom_call_target="tpu_custom_call" | custom-call | flops 1585446912 | bytes 9633792 | tf_op jit(solution)/shard_map/pallas_call | solution.py:50
  168.8 1.0 copy-done.3
  169.8 6.4 %shard_map.151 = (bf16[144,3584]{1,0:T(8,128)(2,1)}, bf16[144,3584]{1,0:T(8,128)(2,1)}) custom-call(bf16[144,3584]{1,0:T(8,128)(2,1)} %shard_map.150.first_ref, bf16[144,3584]{1,0:T(8,128)(2,1)} %copy-done.3, bf16[3584,256]{1,0:T(8,128)(2,1)} %bitcast.24, bf16[3584,256]{1,0:T(8,128)(2,1)} %bitcast.28, bf16[256,3584]{1,0:T(8,128)(2,1)} %bitcast.32), custom_call_target="tpu_custom_call" | custom-call | flops 1585446912 | bytes 9633792 | tf_op jit(solution)/shard_map/pallas_call | solution.py:50
  176.9 0.6 collective-permute-start.33
  177.7 1.6 collective-permute-start.14
  179.5 0.7 copy.20.gate_ref
  180.3 22.5 %collective-permute-done.33.chip_ref = bf16[144,3584]{1,0:T(8,128)(2,1)} collective-permute-done((bf16[144,3584]{1,0:T(8,128)(2,1)S(1)}, bf16[144,3584]{1,0:T(8,128)(2,1)}, u32[]{:S(2)}, u32[]{:S(2)}) %collective-permute-start.33) | collective-permute-done | bytes 1032224 | tf_op jit(solution)/shard_map/ppermute | solution.py:32
  202.7 3.9 %shard_map.160 = (bf16[144,896]{1,0:T(8,128)(2,1)}, bf16[144,896]{1,0:T(8,128)(2,1)}, bf16[144,896]{1,0:T(8,128)(2,1)}, bf16[144,896]{1,0:T(8,128)(2,1)}) custom-call(bf16[144,3584]{1,0:T(8,128)(2,1)} %get-tuple-element.76.own_ref, bf16[144,3584]{1,0:T(8,128)(2,1)} %collective-permute-done.27.core_ref, bf16[144,3584]{1,0:T(8,128)(2,1)} %collective-permute-done.33.chip_ref), custom_call_target="tpu_custom_call" | custom-call | flops 1056964608 | bytes 4128768 | tf_op jit(solution)/shard_map/pallas_call | solution.py:50
  206.6 4.6 %collective-permute-start.34 = (bf16[144,896]{1,0:T(8,128)(2,1)}, bf16[144,896]{1,0:T(8,128)(2,1)S(1)}, u32[]{:S(2)}, u32[]{:S(2)}) collective-permute-start(bf16[144,896]{1,0:T(8,128)(2,1)} %get-tuple-element.81), channel_id=1, source_target_pairs={{0,12},{1,13},{2,14},{3,15},{4,0},{5,1},{6,2},{7,3},{8,4},{9,5},{1... | collective-permute-start | bytes 774152 | tf_op jit(solution)/shard_map/ppermute | solution.py:37
  211.2 0.6 negate_select_fusion.route_ref
  211.9 2.8 collective-permute-start.35
  214.7 9.2 %collective-permute-done.14.chip_ref = bf16[144,3584]{1,0:T(8,128)(2,1)} collective-permute-done((bf16[144,3584]{1,0:T(8,128)(2,1)S(1)}, bf16[144,3584]{1,0:T(8,128)(2,1)}, u32[]{:S(2)}, u32[]{:S(2)}) %collective-permute-start.14) | collective-permute-done | bytes 1032224 | tf_op jit(solution)/shard_map/ppermute | solution.py:32
  224.0 3.9 %shard_map.153 = (bf16[144,896]{1,0:T(8,128)(2,1)}, bf16[144,896]{1,0:T(8,128)(2,1)}, bf16[144,896]{1,0:T(8,128)(2,1)}, bf16[144,896]{1,0:T(8,128)(2,1)}) custom-call(bf16[144,3584]{1,0:T(8,128)(2,1)} %get-tuple-element.48.own_ref, bf16[144,3584]{1,0:T(8,128)(2,1)} %copy-done.13, bf16[144,3584]{1,0:T(8,128)(2,1)} %collective-permute-done.14.chip_ref), custom_call_target="tpu_custom_call" | custom-call | flops 1056964608 | bytes 4128768 | tf_op jit(solution)/shard_map/pallas_call | solution.py:50
  227.8 4.6 %collective-permute-start.15 = (bf16[144,896]{1,0:T(8,128)(2,1)}, bf16[144,896]{1,0:T(8,128)(2,1)S(1)}, u32[]{:S(2)}, u32[]{:S(2)}) collective-permute-start(bf16[144,896]{1,0:T(8,128)(2,1)} %get-tuple-element.53), channel_id=1, source_target_pairs={{0,12},{1,13},{2,14},{3,15},{4,0},{5,1},{6,2},{7,3},{8,4},{9,5},{1... | collective-permute-start | bytes 774152 | tf_op jit(solution)/shard_map/ppermute | solution.py:37
  232.4 2.8 collective-permute-start.16
  235.3 0.7 negate_select_fusion.2.route_ref
  236.0 0.7 copy-done.20
  236.8 4.5 %shard_map.161 = bf16[128,3584]{1,0:T(8,128)(2,1)} custom-call(s32[128,1]{1,0:T(8,128)} %negate_select_fusion.route_ref, f32[1,3584]{1,0:T(1,128)} %gain_ref.5, bf16[128,3584]{1,0:T(8,128)(2,1)} %bitcast.44, bf16[128,3584]{1,0:T(8,128)(2,1)} %bitcast.46, bf16[144,896]{1,0:T(8,128)(2,1)} %get-tuple-element.80.refs_0_, bf16[144,896]{1,0:T(8,128)(2,1)} %copy-done.19, ...), custom_call_target="tpu_custom_call" | custom-call | flops 1056964608 | bytes 3799552 | tf_op jit(solution)/shard_map/pallas_call | solution.py:50
  241.2 1.5 collective-permute-start.37
  242.8 14.7 %collective-permute-done.16.refs_2_ = bf16[144,896]{1,0:T(8,128)(2,1)S(1)} collective-permute-done((bf16[144,896]{1,0:T(8,128)(2,1)}, bf16[144,896]{1,0:T(8,128)(2,1)S(1)}, u32[]{:S(2)}, u32[]{:S(2)}) %collective-permute-start.16) | collective-permute-done | bytes 258080 | tf_op jit(solution)/shard_map/ppermute | solution.py:37
  257.4 0.7 copy-done.23
  258.2 3.9 %shard_map.154 = bf16[128,3584]{1,0:T(8,128)(2,1)} custom-call(s32[128,1]{1,0:T(8,128)} %negate_select_fusion.2.route_ref, f32[128,1]{1,0:T(8,128)} %copy.20.gate_ref, bf16[128,3584]{1,0:T(8,128)(2,1)} %get-tuple-element.43.middle_ref, bf16[144,896]{1,0:T(8,128)(2,1)} %get-tuple-element.52.refs_0_, bf16[144,896]{1,0:T(8,128)(2,1)} %copy-done.21, ...), custom_call_target="tpu_custom_call" | custom-call | flops 1056964608 | bytes 2868224 | tf_op jit(solution)/shard_map/pallas_call | solution.py:50
  262.1 1.5 collective-permute-start.18
  263.6 19.3 %collective-permute-done.18 = bf16[128,3584]{1,0:T(8,128)(2,1)S(1)} collective-permute-done((bf16[128,3584]{1,0:T(8,128)(2,1)}, bf16[128,3584]{1,0:T(8,128)(2,1)S(1)}, u32[]{:S(2)}, u32[]{:S(2)}) %collective-permute-start.18) | collective-permute-done | bytes 917536 | tf_op jit(solution)/shard_map/ppermute | solution.py:28
  282.9 0.9 copy.27
  283.8 0.9 copy.28
  (115 shorter events, 5.6 us)
Async XLA Ops:
  1.6 17.5 %collective-permute-start = (bf16[128,448]{1,0:T(8,128)(2,1)S(1)}, bf16[128,448]{1,0:T(8,128)(2,1)S(1)}, u32[]{:S(2)}, u32[]{:S(2)}) collective-permute-start(bf16[128,448]{1,0:T(8,128)(2,1)S(1)} %bitcast.35), channel_id=1, source_target_pairs={{0,4},{1,5},{2,6},{3,7},{4,8},{5,9},{6,10},{7,11},{8,12},{9,13},{1... | collective-permute-start | bytes 344072 | tf_op jit(solution)/shard_map/ppermute | solution.py:360
  6.6 12.5 %collective-permute-start.1 = (bf16[128,448]{1,0:T(8,128)(2,1)S(1)}, bf16[128,448]{1,0:T(8,128)(2,1)S(1)}, u32[]{:S(2)}, u32[]{:S(2)}) collective-permute-start(bf16[128,448]{1,0:T(8,128)(2,1)S(1)} %bitcast.36), channel_id=1, source_target_pairs={{0,8},{1,9},{2,10},{3,11},{4,12},{5,13},{6,14},{7,15},{16,24},{17,... | collective-permute-start | bytes 344072 | tf_op jit(solution)/shard_map/ppermute | solution.py:360
  11.1 8.0 %collective-permute-start.2 = (bf16[128,448]{1,0:T(8,128)(2,1)S(1)}, bf16[128,448]{1,0:T(8,128)(2,1)S(1)}, u32[]{:S(2)}, u32[]{:S(2)}) collective-permute-start(bf16[128,448]{1,0:T(8,128)(2,1)S(1)} %bitcast.37), channel_id=1, source_target_pairs={{0,12},{1,13},{2,14},{3,15},{16,28},{17,29},{18,30},{19,31}} | collective-permute-start | bytes 344072 | tf_op jit(solution)/shard_map/ppermute | solution.py:360
  19.2 53.1 %copy-start.5 = (bf16[512,448]{1,0:T(8,128)(2,1)}, bf16[512,448]{1,0:T(8,128)(2,1)S(1)}, u32[]{:S(2)}) copy-start(bf16[512,448]{1,0:T(8,128)(2,1)S(1)} %pad_maximum_fusion.kv0) | copy-start | bytes 1376260
  19.2 25.5 %copy-start.18 = (bf16[144,896]{1,0:T(8,128)(2,1)S(1)}, bf16[144,896]{1,0:T(8,128)(2,1)}, u32[]{:S(2)}) copy-start(bf16[144,896]{1,0:T(8,128)(2,1)} %get-tuple-element.73) | copy-start | bytes 774148
  19.2 30.8 %copy-start.17 = (bf16[144,896]{1,0:T(8,128)(2,1)S(1)}, bf16[144,896]{1,0:T(8,128)(2,1)}, u32[]{:S(2)}) copy-start(bf16[144,896]{1,0:T(8,128)(2,1)} %get-tuple-element.74) | copy-start | bytes 774148
  19.2 30.8 %copy-start.16 = (bf16[144,896]{1,0:T(8,128)(2,1)S(1)}, bf16[144,896]{1,0:T(8,128)(2,1)}, u32[]{:S(2)}) copy-start(bf16[144,896]{1,0:T(8,128)(2,1)} %get-tuple-element.75) | copy-start | bytes 774148
  19.2 11.3 %collective-permute-start.19 = (bf16[144,896]{1,0:T(8,128)(2,1)}, bf16[144,896]{1,0:T(8,128)(2,1)S(1)}, u32[]{:S(2)}, u32[]{:S(2)}) collective-permute-start(bf16[144,896]{1,0:T(8,128)(2,1)} %get-tuple-element.65), channel_id=1, source_target_pairs={{0,4},{1,5},{2,6},{3,7},{4,8},{5,9},{6,10},{7,11},{8,12},{9,13},{1... | collective-permute-start | bytes 774152 | tf_op jit(solution)/shard_map/ppermute | solution.py:37
  19.5 20.4 %collective-permute-start.20 = (bf16[144,896]{1,0:T(8,128)(2,1)}, bf16[144,896]{1,0:T(8,128)(2,1)S(1)}, u32[]{:S(2)}, u32[]{:S(2)}) collective-permute-start(bf16[144,896]{1,0:T(8,128)(2,1)} %get-tuple-element.66), channel_id=1, source_target_pairs={{0,8},{1,9},{2,10},{3,11},{4,12},{5,13},{6,14},{7,15},{8,0},{9,1},... | collective-permute-start | bytes 774152 | tf_op jit(solution)/shard_map/ppermute | solution.py:37
  22.9 17.0 %collective-permute-start.21 = (bf16[144,896]{1,0:T(8,128)(2,1)}, bf16[144,896]{1,0:T(8,128)(2,1)S(1)}, u32[]{:S(2)}, u32[]{:S(2)}) collective-permute-start(bf16[144,896]{1,0:T(8,128)(2,1)} %get-tuple-element.67), channel_id=1, source_target_pairs={{0,12},{1,13},{2,14},{3,15},{4,0},{5,1},{6,2},{7,3},{8,4},{9,5},{1... | collective-permute-start | bytes 774152 | tf_op jit(solution)/shard_map/ppermute | solution.py:37
  23.1 49.2 %collective-permute-start.3 = (bf16[512,448]{1,0:T(8,128)(2,1)S(1)}, bf16[512,448]{1,0:T(8,128)(2,1)S(1)}, u32[]{:S(2)}, u32[]{:S(2)}) collective-permute-start(bf16[512,448]{1,0:T(8,128)(2,1)S(1)} %pad_maximum_fusion.kv0), channel_id=1, source_target_pairs={{0,2},{1,3},{2,0},{3,1},{4,6},{5,7},{6,4},{7,5},{8,10},{9,11},{10,... | collective-permute-start | bytes 1376264 | tf_op jit(solution)/shard_map/ppermute | solution.py:32
  30.5 9.3 %copy-start.25 = (bf16[144,896]{1,0:T(8,128)(2,1)}, bf16[144,896]{1,0:T(8,128)(2,1)S(1)}, u32[]{:S(2)}) copy-start(bf16[144,896]{1,0:T(8,128)(2,1)S(1)} %collective-permute-done.19.refs_1_) | copy-start | bytes 774148
  44.7 28.1 %copy-start.6 = (s32[1,2,2,4]{3,2,1,0:T(2,128)S(1)}, s32[1,2,2,4]{3,2,1,0:T(2,128)}, u32[]{:S(2)}) copy-start(s32[1,2,2,4]{3,2,1,0:T(2,128)} %param.17) | copy-start | bytes 196
  44.7 28.2 %copy-start.35 = (s32[1,128,1]{1,2,0:T(1,128)S(1)}, s32[1,128,1]{1,2,0:T(1,128)}, u32[]{:S(2)}) copy-start(s32[1,128,1]{1,2,0:T(1,128)} %param.18) | copy-start | bytes 1540
  44.7 11.9 %collective-permute-start.23 = (bf16[144,896]{1,0:T(8,128)(2,1)S(1)}, bf16[144,896]{1,0:T(8,128)(2,1)S(1)}, u32[]{:S(2)}, u32[]{:S(2)}) collective-permute-start(bf16[144,896]{1,0:T(8,128)(2,1)S(1)} %copy-done.18), channel_id=1, source_target_pairs={{0,4},{1,5},{2,6},{3,7},{4,8},{5,9},{6,10},{7,11},{8,12},{9,13},{1... | collective-permute-start | bytes 774152 | tf_op jit(solution)/shard_map/ppermute | solution.py:37
  50.0 15.6 %collective-permute-start.24 = (bf16[144,896]{1,0:T(8,128)(2,1)S(1)}, bf16[144,896]{1,0:T(8,128)(2,1)S(1)}, u32[]{:S(2)}, u32[]{:S(2)}) collective-permute-start(bf16[144,896]{1,0:T(8,128)(2,1)S(1)} %copy-done.17), channel_id=1, source_target_pairs={{0,8},{1,9},{2,10},{3,11},{4,12},{5,13},{6,14},{7,15},{8,0},{9,1},... | collective-permute-start | bytes 774152 | tf_op jit(solution)/shard_map/ppermute | solution.py:37
  50.0 16.7 %collective-permute-start.25 = (bf16[144,896]{1,0:T(8,128)(2,1)S(1)}, bf16[144,896]{1,0:T(8,128)(2,1)S(1)}, u32[]{:S(2)}, u32[]{:S(2)}) collective-permute-start(bf16[144,896]{1,0:T(8,128)(2,1)S(1)} %copy-done.16), channel_id=1, source_target_pairs={{0,12},{1,13},{2,14},{3,15},{4,0},{5,1},{6,2},{7,3},{8,4},{9,5},{1... | collective-permute-start | bytes 774152 | tf_op jit(solution)/shard_map/ppermute | solution.py:37
  52.4 64.6 %collective-permute-start.28 = (bf16[144,3584]{1,0:T(8,128)(2,1)}, bf16[144,3584]{1,0:T(8,128)(2,1)S(1)}, u32[]{:S(2)}, u32[]{:S(2)}) collective-permute-start(bf16[144,3584]{1,0:T(8,128)(2,1)} %shard_map.156.first_ref), channel_id=1, source_target_pairs={{0,2},{1,3},{2,0},{3,1},{4,6},{5,7},{6,4},{7,5},{8,10},{9,11},{10,... | collective-permute-start | bytes 3096584 | tf_op jit(solution)/shard_map/ppermute | solution.py:32
  56.6 10.1 %copy-start.26 = (bf16[144,896]{1,0:T(8,128)(2,1)}, bf16[144,896]{1,0:T(8,128)(2,1)S(1)}, u32[]{:S(2)}) copy-start(bf16[144,896]{1,0:T(8,128)(2,1)S(1)} %collective-permute-done.23.refs_1_) | copy-start | bytes 774148
  65.6 1.1 copy-start.28
  70.8 46.3 %collective-permute-start.30 = (bf16[144,3584]{1,0:T(8,128)(2,1)}, bf16[144,3584]{1,0:T(8,128)(2,1)S(1)}, u32[]{:S(2)}, u32[]{:S(2)}) collective-permute-start(bf16[144,3584]{1,0:T(8,128)(2,1)} %shard_map.157.first_grad), channel_id=1, source_target_pairs={{0,2},{1,3},{2,0},{3,1},{4,6},{5,7},{6,4},{7,5},{8,10},{9,11},{10,... | collective-permute-start | bytes 3096584 | tf_op jit(solution)/shard_map/ppermute | solution.py:32
  72.3 2.0 collective-permute-start.4
  72.3 2.8 copy-start.15
  72.3 2.8 collective-permute-start.5
  72.9 2.2 copy-start.7
  85.0 16.6 %collective-permute-start.6 = (bf16[144,896]{1,0:T(8,128)(2,1)}, bf16[144,896]{1,0:T(8,128)(2,1)S(1)}, u32[]{:S(2)}, u32[]{:S(2)}) collective-permute-start(bf16[144,896]{1,0:T(8,128)(2,1)} %get-tuple-element.45), channel_id=1, source_target_pairs={{0,4},{1,5},{2,6},{3,7},{4,8},{5,9},{6,10},{7,11},{8,12},{9,13},{1... | collective-permute-start | bytes 774152 | tf_op jit(solution)/shard_map/ppermute | solution.py:37
  91.5 20.7 %collective-permute-start.7 = (bf16[144,896]{1,0:T(8,128)(2,1)}, bf16[144,896]{1,0:T(8,128)(2,1)S(1)}, u32[]{:S(2)}, u32[]{:S(2)}) collective-permute-start(bf16[144,896]{1,0:T(8,128)(2,1)} %get-tuple-element.46), channel_id=1, source_target_pairs={{0,8},{1,9},{2,10},{3,11},{4,12},{5,13},{6,14},{7,15},{8,0},{9,1},... | collective-permute-start | bytes 774152 | tf_op jit(solution)/shard_map/ppermute | solution.py:37
  94.9 17.3 %collective-permute-start.8 = (bf16[144,896]{1,0:T(8,128)(2,1)}, bf16[144,896]{1,0:T(8,128)(2,1)S(1)}, u32[]{:S(2)}, u32[]{:S(2)}) collective-permute-start(bf16[144,896]{1,0:T(8,128)(2,1)} %get-tuple-element.47), channel_id=1, source_target_pairs={{0,12},{1,13},{2,14},{3,15},{4,0},{5,1},{6,2},{7,3},{8,4},{9,5},{1... | collective-permute-start | bytes 774152 | tf_op jit(solution)/shard_map/ppermute | solution.py:37
  101.6 10.6 %copy-start.29 = (bf16[144,896]{1,0:T(8,128)(2,1)}, bf16[144,896]{1,0:T(8,128)(2,1)S(1)}, u32[]{:S(2)}) copy-start(bf16[144,896]{1,0:T(8,128)(2,1)S(1)} %collective-permute-done.6.refs_1_) | copy-start | bytes 774148
  113.0 4.6 %copy-start.9 = (bf16[144,3584]{1,0:T(8,128)(2,1)S(1)}, bf16[144,3584]{1,0:T(8,128)(2,1)}, u32[]{:S(2)}) copy-start(bf16[144,3584]{1,0:T(8,128)(2,1)} %shard_map.156.first_ref) | copy-start | bytes 3096580
  113.0 4.7 %copy-start.10 = (bf16[144,3584]{1,0:T(8,128)(2,1)S(1)}, bf16[144,3584]{1,0:T(8,128)(2,1)}, u32[]{:S(2)}) copy-start(bf16[144,3584]{1,0:T(8,128)(2,1)} %shard_map.157.first_grad) | copy-start | bytes 3096580
  116.5 24.9 %collective-permute-start.11 = (bf16[144,3584]{1,0:T(8,128)(2,1)}, bf16[144,3584]{1,0:T(8,128)(2,1)S(1)}, u32[]{:S(2)}, u32[]{:S(2)}) collective-permute-start(bf16[144,3584]{1,0:T(8,128)(2,1)} %shard_map.150.first_ref), channel_id=1, source_target_pairs={{0,2},{1,3},{2,0},{3,1},{4,6},{5,7},{6,4},{7,5},{8,10},{9,11},{10,... | collective-permute-start | bytes 3096584 | tf_op jit(solution)/shard_map/ppermute | solution.py:32
  117.1 25.9 %copy-start.11 = (bf16[144,3584]{1,0:T(8,128)(2,1)}, bf16[144,3584]{1,0:T(8,128)(2,1)S(1)}, u32[]{:S(2)}) copy-start(bf16[144,3584]{1,0:T(8,128)(2,1)S(1)} %collective-permute-done.28.first_ref) | copy-start | bytes 3096580
  117.1 24.3 %collective-permute-start.29 = (bf16[144,3584]{1,0:T(8,128)(2,1)S(1)}, bf16[144,3584]{1,0:T(8,128)(2,1)}, u32[]{:S(2)}, u32[]{:S(2)}) collective-permute-start(bf16[144,3584]{1,0:T(8,128)(2,1)S(1)} %collective-permute-done.28.first_ref), channel_id=1, source_target_pairs={{0,1},{1,0},{2,3},{3,2},{4,5},{5,4},{6,7},{7,6},{8,9},{9,8},{10,11... | collective-permute-start | bytes 3096584 | tf_op jit(solution)/shard_map/ppermute | solution.py:32
  117.1 25.9 %copy-start.12 = (bf16[144,3584]{1,0:T(8,128)(2,1)}, bf16[144,3584]{1,0:T(8,128)(2,1)S(1)}, u32[]{:S(2)}) copy-start(bf16[144,3584]{1,0:T(8,128)(2,1)S(1)} %collective-permute-done.30.first_grad) | copy-start | bytes 3096580
  117.1 24.8 %collective-permute-start.31 = (bf16[144,3584]{1,0:T(8,128)(2,1)S(1)}, bf16[144,3584]{1,0:T(8,128)(2,1)S(1)}, u32[]{:S(2)}, u32[]{:S(2)}) collective-permute-start(bf16[144,3584]{1,0:T(8,128)(2,1)S(1)} %collective-permute-done.30.first_grad), channel_id=1, source_target_pairs={{0,1},{1,0},{2,3},{3,2},{4,5},{5,4},{6,7},{7,6},{8,9},{9,8},{10,11... | collective-permute-start | bytes 3096584 | tf_op jit(solution)/shard_map/ppermute | solution.py:32
  117.6 34.4 %collective-permute-start.22 = (bf16[144,3584]{1,0:T(8,128)(2,1)S(1)}, bf16[144,3584]{1,0:T(8,128)(2,1)}, u32[]{:S(2)}, u32[]{:S(2)}) collective-permute-start(bf16[144,3584]{1,0:T(8,128)(2,1)S(1)} %copy-done.9), channel_id=1, source_target_pairs={{0,1},{1,0},{2,3},{3,2},{4,5},{5,4},{6,7},{7,6},{8,9},{9,8},{10,11... | collective-permute-start | bytes 3096584 | tf_op jit(solution)/shard_map/ppermute | solution.py:32
  117.7 34.3 %collective-permute-start.26 = (bf16[144,3584]{1,0:T(8,128)(2,1)S(1)}, bf16[144,3584]{1,0:T(8,128)(2,1)}, u32[]{:S(2)}, u32[]{:S(2)}) collective-permute-start(bf16[144,3584]{1,0:T(8,128)(2,1)S(1)} %copy-done.10), channel_id=1, source_target_pairs={{0,1},{1,0},{2,3},{3,2},{4,5},{5,4},{6,7},{7,6},{8,9},{9,8},{10,11... | collective-permute-start | bytes 3096584 | tf_op jit(solution)/shard_map/ppermute | solution.py:32
  141.4 10.5 %copy-start.2 = (bf16[144,3584]{1,0:T(8,128)(2,1)}, bf16[144,3584]{1,0:T(8,128)(2,1)S(1)}, u32[]{:S(2)}) copy-start(bf16[144,3584]{1,0:T(8,128)(2,1)S(1)} %collective-permute-done.11.first_ref) | copy-start | bytes 3096580
  141.4 19.9 %collective-permute-start.12 = (bf16[144,3584]{1,0:T(8,128)(2,1)S(1)}, bf16[144,3584]{1,0:T(8,128)(2,1)S(1)}, u32[]{:S(2)}, u32[]{:S(2)}) collective-permute-start(bf16[144,3584]{1,0:T(8,128)(2,1)S(1)} %collective-permute-done.11.first_ref), channel_id=1, source_target_pairs={{0,1},{1,0},{2,3},{3,2},{4,5},{5,4},{6,7},{7,6},{8,9},{9,8},{10,11... | collective-permute-start | bytes 3096584 | tf_op jit(solution)/shard_map/ppermute | solution.py:32
  141.4 27.3 %collective-permute-start.9 = (bf16[144,3584]{1,0:T(8,128)(2,1)}, bf16[144,3584]{1,0:T(8,128)(2,1)S(1)}, u32[]{:S(2)}, u32[]{:S(2)}) collective-permute-start(bf16[144,3584]{1,0:T(8,128)(2,1)} %shard_map.150.first_ref), channel_id=1, source_target_pairs={{0,1},{1,0},{2,3},{3,2},{4,5},{5,4},{6,7},{7,6},{8,9},{9,8},{10,11... | collective-permute-start | bytes 3096584 | tf_op jit(solution)/shard_map/ppermute | solution.py:32
  141.9 1.0 copy-start.14
  151.9 24.7 %collective-permute-start.32 = (bf16[144,3584]{1,0:T(8,128)(2,1)}, bf16[144,3584]{1,0:T(8,128)(2,1)S(1)}, u32[]{:S(2)}, u32[]{:S(2)}) collective-permute-start(bf16[144,3584]{1,0:T(8,128)(2,1)} %get-tuple-element.79), channel_id=1, source_target_pairs={{0,1},{1,0},{2,3},{3,2},{4,5},{5,4},{6,7},{7,6},{8,9},{9,8},{10,11... | collective-permute-start | bytes 3096584 | tf_op jit(solution)/shard_map/ppermute | solution.py:32
  160.9 19.4 %collective-permute-start.27 = (bf16[144,3584]{1,0:T(8,128)(2,1)}, bf16[144,3584]{1,0:T(8,128)(2,1)}, u32[]{:S(2)}, u32[]{:S(2)}) collective-permute-start(bf16[144,3584]{1,0:T(8,128)(2,1)} %get-tuple-element.77), channel_id=1, source_target_pairs={{0,1},{1,0},{2,3},{3,2},{4,5},{5,4},{6,7},{7,6},{8,9},{9,8},{10,11... | collective-permute-start | bytes 3096584 | tf_op jit(solution)/shard_map/ppermute | solution.py:32
  161.4 1.0 copy-start.4
  168.7 7.9 %copy-start = (bf16[144,3584]{1,0:T(8,128)(2,1)S(1)}, bf16[144,3584]{1,0:T(8,128)(2,1)}, u32[]{:S(2)}) copy-start(bf16[144,3584]{1,0:T(8,128)(2,1)} %get-tuple-element.78) | copy-start | bytes 3096580
  168.7 8.8 %collective-permute-start.13 = (bf16[144,3584]{1,0:T(8,128)(2,1)}, bf16[144,3584]{1,0:T(8,128)(2,1)S(1)}, u32[]{:S(2)}, u32[]{:S(2)}) collective-permute-start(bf16[144,3584]{1,0:T(8,128)(2,1)} %get-tuple-element.51), channel_id=1, source_target_pairs={{0,1},{1,0},{2,3},{3,2},{4,5},{5,4},{6,7},{7,6},{8,9},{9,8},{10,11... | collective-permute-start | bytes 3096584 | tf_op jit(solution)/shard_map/ppermute | solution.py:32
  168.8 1.0 copy-start.3
  176.2 1.3 copy-start.1
  176.2 38.5 %collective-permute-start.10 = (bf16[144,3584]{1,0:T(8,128)(2,1)}, bf16[144,3584]{1,0:T(8,128)(2,1)S(1)}, u32[]{:S(2)}, u32[]{:S(2)}) collective-permute-start(bf16[144,3584]{1,0:T(8,128)(2,1)} %get-tuple-element.49), channel_id=1, source_target_pairs={{0,1},{1,0},{2,3},{3,2},{4,5},{5,4},{6,7},{7,6},{8,9},{9,8},{10,11... | collective-permute-start | bytes 3096584 | tf_op jit(solution)/shard_map/ppermute | solution.py:32
  176.9 2.4 copy-start.34
  176.9 2.7 copy-start.8
  176.9 25.8 %collective-permute-start.33 = (bf16[144,3584]{1,0:T(8,128)(2,1)S(1)}, bf16[144,3584]{1,0:T(8,128)(2,1)}, u32[]{:S(2)}, u32[]{:S(2)}) collective-permute-start(bf16[144,3584]{1,0:T(8,128)(2,1)S(1)} %add_convert_fusion), channel_id=1, source_target_pairs={{0,2},{1,3},{2,0},{3,1},{4,6},{5,7},{6,4},{7,5},{8,10},{9,11},{10,... | collective-permute-start | bytes 3096584 | tf_op jit(solution)/shard_map/ppermute | solution.py:32
  177.7 46.2 %collective-permute-start.14 = (bf16[144,3584]{1,0:T(8,128)(2,1)S(1)}, bf16[144,3584]{1,0:T(8,128)(2,1)}, u32[]{:S(2)}, u32[]{:S(2)}) collective-permute-start(bf16[144,3584]{1,0:T(8,128)(2,1)S(1)} %add_convert_fusion.1), channel_id=1, source_target_pairs={{0,2},{1,3},{2,0},{3,1},{4,6},{5,7},{6,4},{7,5},{8,10},{9,11},{10,... | collective-permute-start | bytes 3096584 | tf_op jit(solution)/shard_map/ppermute | solution.py:32
  206.6 28.7 %collective-permute-start.34 = (bf16[144,896]{1,0:T(8,128)(2,1)}, bf16[144,896]{1,0:T(8,128)(2,1)S(1)}, u32[]{:S(2)}, u32[]{:S(2)}) collective-permute-start(bf16[144,896]{1,0:T(8,128)(2,1)} %get-tuple-element.81), channel_id=1, source_target_pairs={{0,12},{1,13},{2,14},{3,15},{4,0},{5,1},{6,2},{7,3},{8,4},{9,5},{1... | collective-permute-start | bytes 774152 | tf_op jit(solution)/shard_map/ppermute | solution.py:37
  211.9 24.1 %collective-permute-start.35 = (bf16[144,896]{1,0:T(8,128)(2,1)}, bf16[144,896]{1,0:T(8,128)(2,1)S(1)}, u32[]{:S(2)}, u32[]{:S(2)}) collective-permute-start(bf16[144,896]{1,0:T(8,128)(2,1)} %get-tuple-element.82), channel_id=1, source_target_pairs={{0,8},{1,9},{2,10},{3,11},{4,12},{5,13},{6,14},{7,15},{8,0},{9,1},... | collective-permute-start | bytes 774152 | tf_op jit(solution)/shard_map/ppermute | solution.py:37
  214.7 21.3 %collective-permute-start.36 = (bf16[144,896]{1,0:T(8,128)(2,1)}, bf16[144,896]{1,0:T(8,128)(2,1)S(1)}, u32[]{:S(2)}, u32[]{:S(2)}) collective-permute-start(bf16[144,896]{1,0:T(8,128)(2,1)} %get-tuple-element.83), channel_id=1, source_target_pairs={{0,4},{1,5},{2,6},{3,7},{4,8},{5,9},{6,10},{7,11},{8,12},{9,13},{1... | collective-permute-start | bytes 774152 | tf_op jit(solution)/shard_map/ppermute | solution.py:37
  214.7 9.2 %copy-start.13 = (bf16[144,3584]{1,0:T(8,128)(2,1)}, bf16[144,3584]{1,0:T(8,128)(2,1)S(1)}, u32[]{:S(2)}) copy-start(bf16[144,3584]{1,0:T(8,128)(2,1)S(1)} %collective-permute-done.10.core_ref) | copy-start | bytes 3096580
  227.8 14.9 %collective-permute-start.15 = (bf16[144,896]{1,0:T(8,128)(2,1)}, bf16[144,896]{1,0:T(8,128)(2,1)S(1)}, u32[]{:S(2)}, u32[]{:S(2)}) collective-permute-start(bf16[144,896]{1,0:T(8,128)(2,1)} %get-tuple-element.53), channel_id=1, source_target_pairs={{0,12},{1,13},{2,14},{3,15},{4,0},{5,1},{6,2},{7,3},{8,4},{9,5},{1... | collective-permute-start | bytes 774152 | tf_op jit(solution)/shard_map/ppermute | solution.py:37
  232.4 25.0 %collective-permute-start.16 = (bf16[144,896]{1,0:T(8,128)(2,1)}, bf16[144,896]{1,0:T(8,128)(2,1)S(1)}, u32[]{:S(2)}, u32[]{:S(2)}) collective-permute-start(bf16[144,896]{1,0:T(8,128)(2,1)} %get-tuple-element.54), channel_id=1, source_target_pairs={{0,8},{1,9},{2,10},{3,11},{4,12},{5,13},{6,14},{7,15},{8,0},{9,1},... | collective-permute-start | bytes 774152 | tf_op jit(solution)/shard_map/ppermute | solution.py:37
  235.3 22.2 %collective-permute-start.17 = (bf16[144,896]{1,0:T(8,128)(2,1)}, bf16[144,896]{1,0:T(8,128)(2,1)S(1)}, u32[]{:S(2)}, u32[]{:S(2)}) collective-permute-start(bf16[144,896]{1,0:T(8,128)(2,1)} %get-tuple-element.55), channel_id=1, source_target_pairs={{0,4},{1,5},{2,6},{3,7},{4,8},{5,9},{6,10},{7,11},{8,12},{9,13},{1... | collective-permute-start | bytes 774152 | tf_op jit(solution)/shard_map/ppermute | solution.py:37
  241.2 22.4 %collective-permute-start.37 = (bf16[128,3584]{1,0:T(8,128)(2,1)}, bf16[128,3584]{1,0:T(8,128)(2,1)S(1)}, u32[]{:S(2)}, u32[]{:S(2)}) collective-permute-start(bf16[128,3584]{1,0:T(8,128)(2,1)} %shard_map.161), channel_id=1, source_target_pairs={{0,16},{16,0},{1,17},{17,1},{2,18},{18,2},{3,19},{19,3},{4,20},{20... | collective-permute-start | bytes 2752520 | tf_op jit(solution)/shard_map/ppermute | solution.py:28
  242.8 14.7 %copy-start.21 = (bf16[144,896]{1,0:T(8,128)(2,1)}, bf16[144,896]{1,0:T(8,128)(2,1)S(1)}, u32[]{:S(2)}) copy-start(bf16[144,896]{1,0:T(8,128)(2,1)S(1)} %collective-permute-done.15.refs_1_) | copy-start | bytes 774148
  262.1 20.8 %collective-permute-start.18 = (bf16[128,3584]{1,0:T(8,128)(2,1)}, bf16[128,3584]{1,0:T(8,128)(2,1)S(1)}, u32[]{:S(2)}, u32[]{:S(2)}) collective-permute-start(bf16[128,3584]{1,0:T(8,128)(2,1)} %shard_map.154), channel_id=1, source_target_pairs={{0,16},{16,0},{1,17},{17,1},{2,18},{18,2},{3,19},{19,3},{4,20},{20... | collective-permute-start | bytes 2752520 | tf_op jit(solution)/shard_map/ppermute | solution.py:28
  (10 other events, 7.3 us)

commit v3 on v2

--- a/solution.py
+++ b/solution.py
@@ -15,7 +15,7 @@
 SEL = 4
 PARTS = 4
 LANES = 128
-VMEM_BYTES = 56 * 1024 * 1024
+VMEM_BYTES = 28 * 1024 * 1024
 
 epsilon = 1e-06
 negative_large = -1e30
@@ -39,7 +39,7 @@
     )
 
 
-def call(body, outs, args, scratch=(), flops=0, smem=0):
+def call(body, outs, args, scratch=(), flops=0, smem=0, vmem=VMEM_BYTES):
     specs = [
         pl.BlockSpec(memory_space=pltpu.SMEM if i < smem else pltpu.VMEM)
         for i in range(len(args))
@@ -53,7 +53,7 @@
         in_specs=specs,
         out_specs=[pl.BlockSpec(memory_space=pltpu.VMEM) for _ in shapes],
         scratch_shapes=list(scratch),
-        compiler_params=pltpu.CompilerParams(vmem_limit_bytes=VMEM_BYTES),
+        compiler_params=pltpu.CompilerParams(vmem_limit_bytes=vmem),
         cost_estimate=pl.CostEstimate(
             flops=int(flops), bytes_accessed=int(moved_bytes), transcendentals=0
         ),
@@ -358,10 +358,6 @@
     for back in range(1, experts):
         pairs = [(i, i + back * GROUP) for i in range(length - back * GROUP)]
         column.append(lax.ppermute(keys_values[0], "expert", pairs))
-    column = jnp.concatenate(column, axis=0)
-    other_chip = swapped(column, 2)
-    kv = [column, other_chip, swapped(column, 1), swapped(other_chip, 1)]
-
     front_from = lax.rem(front_route[0] - group + experts, experts)
     back_from = lax.rem(back_route[0] - group + experts, experts)
     front_row, back_row = front_from.reshape(1, tokens), back_from.reshape(1, tokens)
@@ -373,29 +369,38 @@
         (back_row, back_gate[0], norm_gain, back_middle[0], back_grad[0]),
         flops=2 * pack_flops,
     )
+    column = after(column, [packed[0]])
+    column = jnp.concatenate(column, axis=0)
+    other_chip = swapped(column, 2)
+    kv = [column, other_chip, swapped(column, 1), swapped(other_chip, 1)]
+
     packed = after(packed, [column])
 
+    def sent(chunks):
+        return [chunks[0]] + [turned(chunks[k], k) for k in range(1, experts)]
+
     def joined(chunks):
-        chunks = [chunks[0]] + [turned(chunks[k], k) for k in range(1, experts)]
         return call(functools.partial(join_body, capacity), piece, chunks, flops=pack_flops)
 
     def pieces_of(rows):
         other = swapped(rows, 2)
         return [rows, swapped(rows, 1), other, swapped(other, 1)]
 
-    def returned(near, far):
+    def shares(near, far):
         chip = far[0].astype(f32) + swapped(far[1], 1).astype(f32)
         parts = (near[0], swapped(near[1], 1), swapped(chip.astype(bf16), 2))
-        chunks = call(
+        return parts
+
+    def split(parts):
+        return call(
             functools.partial(split_body, capacity), [chunk] * experts, parts, flops=pack_flops
         )
+
+    def sent_back(chunks):
         return [chunks[0]] + [turned(chunks[k], -k) for k in range(1, experts)]
 
-    back_rows = joined(packed[:experts])
-    grad_chunks = after(packed[experts:], [back_rows])
-    back_pieces = pieces_of(back_rows)
-    back_grads = joined(grad_chunks)
-    grad_pieces = pieces_of(back_grads)
+    row_chunks = sent(packed[:experts])
+    grad_chunks = sent(after(packed[experts:], row_chunks))
 
     per_device = tokens // BLK
     chosen = selected_blocks[0].reshape(-1)
@@ -417,10 +422,14 @@
         ],
         flops=pack_flops + 4 * tokens * HEADS * SEL * BLK * LANES,
         smem=3,
+        vmem=VMEM_BYTES + 2 * length * tokens * 4 * LANES * 2,
     )
     middle, front_chunks = result[0], result[1:]
+    front_chunks = sent(front_chunks)
+    back_pieces = pieces_of(joined(after(row_chunks, [middle])))
+    grad_pieces = pieces_of(joined(after(grad_chunks, [back_pieces[0]])))
     front_rows = joined(front_chunks)
-    front_pieces = pieces_of(front_rows)
+    front_other = swapped(front_rows, 2)
 
     work = 2 * 2 * slots * width * hidden_width
 
@@ -442,7 +451,20 @@
 
     back_far = backward(2, 4)
     back_near = backward(0, 2)
-    back_return = returned(back_near, back_far)
+    back_shares = shares(back_near, back_far)
+
+    (front_other,) = after([front_other], back_near + back_far)
+    front_pieces = [front_rows, swapped(front_rows, 1), front_other, swapped(front_other, 1)]
+    front_far = forward(2, 4)
+    front_near = forward(0, 2)
+    front_shares = shares(front_near, front_far)
+
+    back_chunks = split(after(back_shares, front_near + front_far))
+    back_return = sent_back(back_chunks)
+    front_chunks = split(after(front_shares, back_chunks))
+    front_return = sent_back(front_chunks)
+    back_return = after(back_return, front_chunks)
+
     back_result = call(
         functools.partial(back_finish_body, experts, capacity),
         whole,
@@ -450,10 +472,7 @@
         flops=pack_flops,
     )
     back_output = passed_along(back_result, "section", -1)
-
-    front_far = forward(2, 4)
-    front_near = forward(0, 2)
-    front_return = returned(front_near, front_far)
+    front_return = after(front_return, [back_result])
     front_result = call(
         functools.partial(front_finish_body, experts, capacity),
         whole,

time: 285 us -> 254 us (0.89)
  Pallas kernels: 71.1 us -> 37.2 us
  starting transfers between devices: 60.3 us -> 65.5 us
  local copies, waits for them, and re-layouts: 12.8 us -> 9.47 us
    pallas_call x13, Pallas kernels: 71.1 us -> 37.2 us  [call(): pl.pallas_call(body, out_shape=shapes, in_specs=specs, out_specs=[pl.Bloc...]
    ppermute x15, waiting for transfers between devices: 60.1 us -> 38.8 us  [turned(): lax.ppermute(array, 'expert', [(i, (i + by * GROUP) % length) for i in ra...]
    ppermute x18, waiting for transfers between devices: 56 us -> 73.9 us  [swapped(): lax.ppermute(array, 'expert', [(i, i ^ bit) for i in range(lax.axis_size(...]
    ppermute x15, starting transfers between devices: 36.4 us -> 43.9 us  [turned(): lax.ppermute(array, 'expert', [(i, (i + by * GROUP) % length) for i in ra...]
    ppermute x2, waiting for transfers between devices: 19.3 us -> 22.2 us  [passed_along(): lax.ppermute(array, axis, [(i, (i + by) % length) for i in range(length)])]
    unnamed x75 -> x58, local copies, waits for them, and re-layouts: 10.4 us -> 8.27 us
  transfers between devices with their start and end apart: 38 -> 38, of which waited for: 14 -> 15; matrix products, arithmetic and copies ran while one was open for 2% -> 2% of each run, Pallas kernels for 25% -> 14%
where the time goes in v3:
time: 254 us; the launch traced here: 251 us
  waiting for transfers between devices  135 us (53%)
  starting transfers between devices  65.5 us (26%)
  Pallas kernels  37.2 us (15%)
  local copies, waits for them, and re-layouts  9.47 us (4%)
  other arithmetic  3.17 us (1%)
    ppermute x18, waiting for transfers between devices, swapped(): lax.ppermute(array, 'expert', [(i, i ^ bit) for i in range(lax.axis_size(...  73.9 us
    ppermute x15, starting transfers between devices, turned(): lax.ppermute(array, 'expert', [(i, (i + by * GROUP) % length) for i in ra...  43.9 us
    ppermute x15, waiting for transfers between devices, turned(): lax.ppermute(array, 'expert', [(i, (i + by * GROUP) % length) for i in ra...  38.8 us
    pallas_call x13, Pallas kernels, call(): pl.pallas_call(body, out_shape=shapes, in_specs=specs, out_specs=[pl.Bloc...  37.2 us
    ppermute x2, waiting for transfers between devices, passed_along(): lax.ppermute(array, axis, [(i, (i + by) % length) for i in range(length)])  22.2 us
    ppermute x3, starting transfers between devices, shards(): column.append(lax.ppermute(keys_values[0], 'expert', pairs))  10.7 us
    unnamed x58, local copies, waits for them, and re-layouts  8.27 us
    ppermute x18, starting transfers between devices, swapped(): lax.ppermute(array, 'expert', [(i, i ^ bit) for i in range(lax.axis_size(...  7.73 us
  transfers between devices with their start and end apart: 38, of which 15 were waited for; matrix products, arithmetic and copies ran while one was open for 2% of the time, Pallas kernels for 14%

profile of v3, /device:TPU:0, one launch (start us, length us, event | category | flops | bytes accessed | tf_op | source)
XLA Modules:
  0.0 251.5 jit_solution(7987083266061231885)
XLA Ops:
  0.6 1.0 copy.19
  1.6 4.9 %collective-permute-start = (bf16[128,448]{1,0:T(8,128)(2,1)S(1)}, bf16[128,448]{1,0:T(8,128)(2,1)S(1)}, u32[]{:S(2)}, u32[]{:S(2)}) collective-permute-start(bf16[128,448]{1,0:T(8,128)(2,1)S(1)} %bitcast.41), channel_id=1, source_target_pairs={{0,4},{1,5},{2,6},{3,7},{4,8},{5,9},{6,10},{7,11},{8,12},{9,13},{1... | collective-permute-start | bytes 344072 | tf_op jit(solution)/shard_map/ppermute | solution.py:360
  6.6 4.5 %collective-permute-start.1 = (bf16[128,448]{1,0:T(8,128)(2,1)S(1)}, bf16[128,448]{1,0:T(8,128)(2,1)S(1)}, u32[]{:S(2)}, u32[]{:S(2)}) collective-permute-start(bf16[128,448]{1,0:T(8,128)(2,1)S(1)} %bitcast.42), channel_id=1, source_target_pairs={{0,8},{1,9},{2,10},{3,11},{4,12},{5,13},{6,14},{7,15},{16,24},{17,... | collective-permute-start | bytes 344072 | tf_op jit(solution)/shard_map/ppermute | solution.py:360
  11.1 1.3 collective-permute-start.2
  12.4 0.8 copy.20.gate_ref
  13.2 0.7 compare_select_fusion.route_ref
  13.8 1.2 copy-done.5
  15.0 1.2 copy-done.7
  16.2 0.7 copy-done.12
  16.9 2.4 shard_map.149
  19.3 0.7 copy-done.20
  20.1 1.6 collective-permute-start.3
  21.7 2.6 %collective-permute-start.13 = (bf16[144,896]{1,0:T(8,128)(2,1)}, bf16[144,896]{1,0:T(8,128)(2,1)}, u32[]{:S(2)}, u32[]{:S(2)}) collective-permute-start(bf16[144,896]{1,0:T(8,128)(2,1)} %get-tuple-element.91), channel_id=1, source_target_pairs={{0,8},{1,9},{2,10},{3,11},{4,12},{5,13},{6,14},{7,15},{8,0},{9,1},... | collective-permute-start | bytes 774152 | tf_op jit(solution)/shard_map/ppermute | solution.py:37
  24.3 1.2 collective-permute-start.14
  25.5 7.8 %collective-permute-done.3.kv1 = bf16[512,448]{1,0:T(8,128)(2,1)S(1)} collective-permute-done((bf16[512,448]{1,0:T(8,128)(2,1)S(1)}, bf16[512,448]{1,0:T(8,128)(2,1)S(1)}, u32[]{:S(2)}, u32[]{:S(2)}) %collective-permute-start.3) | collective-permute-done | bytes 458784 | tf_op jit(solution)/shard_map/ppermute | solution.py:32
  33.5 8.7 %collective-permute-done.13.refs_2_ = bf16[144,896]{1,0:T(8,128)(2,1)} collective-permute-done((bf16[144,896]{1,0:T(8,128)(2,1)}, bf16[144,896]{1,0:T(8,128)(2,1)}, u32[]{:S(2)}, u32[]{:S(2)}) %collective-permute-start.13) | collective-permute-done | bytes 258080 | tf_op jit(solution)/shard_map/ppermute | solution.py:37
  42.2 13.8 %collective-permute-start.16 = (bf16[144,896]{1,0:T(8,128)(2,1)}, bf16[144,896]{1,0:T(8,128)(2,1)}, u32[]{:S(2)}, u32[]{:S(2)}) collective-permute-start(bf16[144,896]{1,0:T(8,128)(2,1)} %copy-done.11), channel_id=1, source_target_pairs={{0,4},{1,5},{2,6},{3,7},{4,8},{5,9},{6,10},{7,11},{8,12},{9,13},{1... | collective-permute-start | bytes 774152 | tf_op jit(solution)/shard_map/ppermute | solution.py:37
  56.0 2.4 collective-permute-start.18
  58.5 8.1 %shard_map.150 = (bf16[128,3584]{1,0:T(8,128)(2,1)S(1)}, bf16[144,896]{1,0:T(8,128)(2,1)S(1)}, bf16[144,896]{1,0:T(8,128)(2,1)S(1)}, bf16[144,896]{1,0:T(8,128)(2,1)S(1)}, bf16[144,896]{1,0:T(8,128)(2,1)S(1)}) custom-call(s32[16]{0:T(128)S(1)} %reshape_squeeze.3.chosen_ref, s32[16]{0:T(128)S(1)} %fusion.8.index_ref, s32[1]{0:T(128)} %bitcast.2.base_ref, ...), custom_call_target="tpu_custom_call" | custom-call | flops 1593835520 | bytes 5634692 | tf_op jit(solution)/shard_map/pallas_call | solution.py:50
  66.6 2.6 %shard_map.153.first_ref = bf16[144,3584]{1,0:T(8,128)(2,1)S(1)} custom-call(bf16[144,896]{1,0:T(8,128)(2,1)S(1)} %copy-done.21, bf16[144,896]{1,0:T(8,128)(2,1)} %collective-permute-done.12.refs_1_, bf16[144,896]{1,0:T(8,128)(2,1)} %collective-permute-done.13.refs_2_, bf16[144,896]{1,0:T(8,128)(2,1)} %collective-permute-done.14.refs_3_), custom_call_target="tpu_custom_call" | custom-call | flops 1056964608 | bytes 2064384 | tf_op jit(solution)/shard_map/pallas_call | solution.py:50
  69.3 2.4 shard_map.154.first_grad
  71.7 0.6 collective-permute-start.22
  72.3 1.5 collective-permute-start.20
  73.8 6.3 %collective-permute-start.6 = (bf16[144,896]{1,0:T(8,128)(2,1)S(1)}, bf16[144,896]{1,0:T(8,128)(2,1)S(1)}, u32[]{:S(2)}, u32[]{:S(2)}) collective-permute-start(bf16[144,896]{1,0:T(8,128)(2,1)S(1)} %get-tuple-element.77), channel_id=1, source_target_pairs={{0,4},{1,5},{2,6},{3,7},{4,8},{5,9},{6,10},{7,11},{8,12},{9,13},{1... | collective-permute-start | bytes 774152 | tf_op jit(solution)/shard_map/ppermute | solution.py:37
  80.1 3.8 %collective-permute-done.6.refs_1_ = bf16[144,896]{1,0:T(8,128)(2,1)S(1)} collective-permute-done((bf16[144,896]{1,0:T(8,128)(2,1)S(1)}, bf16[144,896]{1,0:T(8,128)(2,1)S(1)}, u32[]{:S(2)}, u32[]{:S(2)}) %collective-permute-start.6) | collective-permute-done | bytes 258080 | tf_op jit(solution)/shard_map/ppermute | solution.py:37
  84.0 6.1 %collective-permute-done.7.refs_2_ = bf16[144,896]{1,0:T(8,128)(2,1)S(1)} collective-permute-done((bf16[144,896]{1,0:T(8,128)(2,1)S(1)}, bf16[144,896]{1,0:T(8,128)(2,1)S(1)}, u32[]{:S(2)}, u32[]{:S(2)}) %collective-permute-start.7) | collective-permute-done | bytes 258080 | tf_op jit(solution)/shard_map/ppermute | solution.py:37
  90.0 5.0 %collective-permute-start.8 = (bf16[144,896]{1,0:T(8,128)(2,1)S(1)}, bf16[144,896]{1,0:T(8,128)(2,1)S(1)}, u32[]{:S(2)}, u32[]{:S(2)}) collective-permute-start(bf16[144,896]{1,0:T(8,128)(2,1)S(1)} %get-tuple-element.79), channel_id=1, source_target_pairs={{0,12},{1,13},{2,14},{3,15},{4,0},{5,1},{6,2},{7,3},{8,4},{9,5},{1... | collective-permute-start | bytes 774152 | tf_op jit(solution)/shard_map/ppermute | solution.py:37
  95.1 2.2 collective-permute-done.22.first_grad
  97.3 11.1 %collective-permute-done.20.first_ref = bf16[144,3584]{1,0:T(8,128)(2,1)S(1)} collective-permute-done((bf16[144,3584]{1,0:T(8,128)(2,1)S(1)}, bf16[144,3584]{1,0:T(8,128)(2,1)S(1)}, u32[]{:S(2)}, u32[]{:S(2)}) %collective-permute-start.20) | collective-permute-done | bytes 1032224 | tf_op jit(solution)/shard_map/ppermute | solution.py:32
  108.4 1.1 shard_map.151.first_ref
  109.4 0.6 collective-permute-start.11
  110.1 0.3 copy-done.1
  110.4 3.8 %shard_map.155 = (bf16[144,3584]{1,0:T(8,128)(2,1)S(1)}, bf16[144,3584]{1,0:T(8,128)(2,1)S(1)}) custom-call(bf16[144,3584]{1,0:T(8,128)(2,1)S(1)} %shard_map.153.first_ref, bf16[144,3584]{1,0:T(8,128)(2,1)S(1)} %collective-permute-done.15.second_ref, bf16[144,3584]{1,0:T(8,128)(2,1)S(1)} %shard_map.154.first_grad, ...), custom_call_target="tpu_custom_call" | custom-call | flops 2642411520 | bytes 11698176 | tf_op jit(solution)/shard_map/pallas_call | solution.py:50
  114.2 3.8 %shard_map.156 = (bf16[144,3584]{1,0:T(8,128)(2,1)S(1)}, bf16[144,3584]{1,0:T(8,128)(2,1)S(1)}) custom-call(bf16[144,3584]{1,0:T(8,128)(2,1)S(1)} %collective-permute-done.20.first_ref, bf16[144,3584]{1,0:T(8,128)(2,1)S(1)} %collective-permute-done.21.second_ref, bf16[144,3584]{1,0:T(8,128)(2,1)S(1)} %collective-permute-done.22.first_grad, ...), custom_call_target="tpu_custom_call" | custom-call | flops 2642411520 | bytes 11698176 | tf_op jit(solution)/shard_map/pallas_call | solution.py:50
  118.1 16.6 %collective-permute-done.11.first_ref = bf16[144,3584]{1,0:T(8,128)(2,1)S(1)} collective-permute-done((bf16[144,3584]{1,0:T(8,128)(2,1)S(1)}, bf16[144,3584]{1,0:T(8,128)(2,1)S(1)}, u32[]{:S(2)}, u32[]{:S(2)}) %collective-permute-start.11) | collective-permute-done | bytes 1032224 | tf_op jit(solution)/shard_map/ppermute | solution.py:32
  134.7 0.5 collective-permute-start.9
  135.2 0.5 collective-permute-start.27
  135.7 1.6 collective-permute-done.24.second_ref
  137.4 1.9 shard_map.157
  139.4 0.9 collective-permute-done.9.second_ref
  140.3 2.9 %shard_map.152 = (bf16[144,3584]{1,0:T(8,128)(2,1)S(1)}, bf16[144,3584]{1,0:T(8,128)(2,1)}) custom-call(bf16[144,3584]{1,0:T(8,128)(2,1)S(1)} %shard_map.151.first_ref, bf16[144,3584]{1,0:T(8,128)(2,1)S(1)} %collective-permute-done.9.second_ref, bf16[3584,256]{1,0:T(8,128)(2,1)S(1)} %bitcast.24, bf16[3584,256]{1,0:T(8,128)(2,1)S(1)} %bitcast.28, ...), custom_call_target="tpu_custom_call" | custom-call | flops 1585446912 | bytes 9633792 | tf_op jit(solution)/shard_map/pallas_call | solution.py:50
  143.3 1.2 add_convert_fusion
  144.6 0.5 collective-permute-start.29
  145.1 1.2 add_convert_fusion.1
  146.3 1.5 collective-permute-start.26
  148.2 22.3 %collective-permute-done.29.chip_ref = bf16[144,3584]{1,0:T(8,128)(2,1)} collective-permute-done((bf16[144,3584]{1,0:T(8,128)(2,1)}, bf16[144,3584]{1,0:T(8,128)(2,1)}, u32[]{:S(2)}, u32[]{:S(2)}) %collective-permute-start.29) | collective-permute-done | bytes 1032224 | tf_op jit(solution)/shard_map/ppermute | solution.py:32
  170.5 1.2 copy-done.15
  171.7 2.6 %shard_map.158 = (bf16[144,896]{1,0:T(8,128)(2,1)S(1)}, bf16[144,896]{1,0:T(8,128)(2,1)S(1)}, bf16[144,896]{1,0:T(8,128)(2,1)S(1)}, bf16[144,896]{1,0:T(8,128)(2,1)S(1)}) custom-call(bf16[144,3584]{1,0:T(8,128)(2,1)S(1)} %copy-done.15, bf16[144,3584]{1,0:T(8,128)(2,1)} %collective-permute-done.27.core_ref, bf16[144,3584]{1,0:T(8,128)(2,1)} %collective-permute-done.29.chip_ref), custom_call_target="tpu_custom_call" | custom-call | flops 1056964608 | bytes 4128768 | tf_op jit(solution)/shard_map/pallas_call | solution.py:50
  174.4 2.4 collective-permute-start.33
  176.8 3.9 %collective-permute-start.34 = (bf16[144,896]{1,0:T(8,128)(2,1)S(1)}, bf16[144,896]{1,0:T(8,128)(2,1)S(1)}, u32[]{:S(2)}, u32[]{:S(2)}) collective-permute-start(bf16[144,896]{1,0:T(8,128)(2,1)S(1)} %get-tuple-element.121), channel_id=1, source_target_pairs={{0,8},{1,9},{2,10},{3,11},{4,12},{5,13},{6,14},{7,15},{8,0},{9,1},... | collective-permute-start | bytes 774152 | tf_op jit(solution)/shard_map/ppermute | solution.py:37
  180.7 11.4 %collective-permute-done.26.chip_ref = bf16[144,3584]{1,0:T(8,128)(2,1)} collective-permute-done((bf16[144,3584]{1,0:T(8,128)(2,1)}, bf16[144,3584]{1,0:T(8,128)(2,1)}, u32[]{:S(2)}, u32[]{:S(2)}) %collective-permute-start.26) | collective-permute-done | bytes 1032224 | tf_op jit(solution)/shard_map/ppermute | solution.py:32
  192.1 2.5 shard_map.159
  194.6 2.4 collective-permute-start.30
  196.9 3.9 %collective-permute-start.31 = (bf16[144,896]{1,0:T(8,128)(2,1)S(1)}, bf16[144,896]{1,0:T(8,128)(2,1)S(1)}, u32[]{:S(2)}, u32[]{:S(2)}) collective-permute-start(bf16[144,896]{1,0:T(8,128)(2,1)S(1)} %get-tuple-element.128), channel_id=1, source_target_pairs={{0,8},{1,9},{2,10},{3,11},{4,12},{5,13},{6,14},{7,15},{8,0},{9,1},... | collective-permute-start | bytes 774152 | tf_op jit(solution)/shard_map/ppermute | solution.py:37
  200.8 13.9 %collective-permute-done.34.refs_2_ = bf16[144,896]{1,0:T(8,128)(2,1)S(1)} collective-permute-done((bf16[144,896]{1,0:T(8,128)(2,1)S(1)}, bf16[144,896]{1,0:T(8,128)(2,1)S(1)}, u32[]{:S(2)}, u32[]{:S(2)}) %collective-permute-start.34) | collective-permute-done | bytes 258080 | tf_op jit(solution)/shard_map/ppermute | solution.py:37
  214.7 1.8 shard_map.160
  216.5 1.6 collective-permute-start.37
  218.1 6.3 %collective-permute-done.31.refs_2_ = bf16[144,896]{1,0:T(8,128)(2,1)S(1)} collective-permute-done((bf16[144,896]{1,0:T(8,128)(2,1)S(1)}, bf16[144,896]{1,0:T(8,128)(2,1)S(1)}, u32[]{:S(2)}, u32[]{:S(2)}) %collective-permute-start.31) | collective-permute-done | bytes 258080 | tf_op jit(solution)/shard_map/ppermute | solution.py:37
  224.5 1.3 shard_map.161
  225.8 1.6 collective-permute-start.36
  227.4 5.2 %collective-permute-done.37 = bf16[128,3584]{1,0:T(8,128)(2,1)S(1)} collective-permute-done((bf16[128,3584]{1,0:T(8,128)(2,1)S(1)}, bf16[128,3584]{1,0:T(8,128)(2,1)S(1)}, u32[]{:S(2)}, u32[]{:S(2)}) %collective-permute-start.37) | collective-permute-done | bytes 917536 | tf_op jit(solution)/shard_map/ppermute | solution.py:28
  232.6 17.0 %collective-permute-done.36 = bf16[128,3584]{1,0:T(8,128)(2,1)S(1)} collective-permute-done((bf16[128,3584]{1,0:T(8,128)(2,1)S(1)}, bf16[128,3584]{1,0:T(8,128)(2,1)S(1)}, u32[]{:S(2)}, u32[]{:S(2)}) %collective-permute-start.36) | collective-permute-done | bytes 917536 | tf_op jit(solution)/shard_map/ppermute | solution.py:28
  249.6 0.9 copy.30
  250.6 0.9 copy.31
  (98 shorter events, 1.2 us)
Async XLA Ops:
  1.6 18.4 %collective-permute-start = (bf16[128,448]{1,0:T(8,128)(2,1)S(1)}, bf16[128,448]{1,0:T(8,128)(2,1)S(1)}, u32[]{:S(2)}, u32[]{:S(2)}) collective-permute-start(bf16[128,448]{1,0:T(8,128)(2,1)S(1)} %bitcast.41), channel_id=1, source_target_pairs={{0,4},{1,5},{2,6},{3,7},{4,8},{5,9},{6,10},{7,11},{8,12},{9,13},{1... | collective-permute-start | bytes 344072 | tf_op jit(solution)/shard_map/ppermute | solution.py:360
  6.6 13.4 %collective-permute-start.1 = (bf16[128,448]{1,0:T(8,128)(2,1)S(1)}, bf16[128,448]{1,0:T(8,128)(2,1)S(1)}, u32[]{:S(2)}, u32[]{:S(2)}) collective-permute-start(bf16[128,448]{1,0:T(8,128)(2,1)S(1)} %bitcast.42), channel_id=1, source_target_pairs={{0,8},{1,9},{2,10},{3,11},{4,12},{5,13},{6,14},{7,15},{16,24},{17,... | collective-permute-start | bytes 344072 | tf_op jit(solution)/shard_map/ppermute | solution.py:360
  11.1 9.0 %collective-permute-start.2 = (bf16[128,448]{1,0:T(8,128)(2,1)S(1)}, bf16[128,448]{1,0:T(8,128)(2,1)S(1)}, u32[]{:S(2)}, u32[]{:S(2)}) collective-permute-start(bf16[128,448]{1,0:T(8,128)(2,1)S(1)} %bitcast.43), channel_id=1, source_target_pairs={{0,12},{1,13},{2,14},{3,15},{16,28},{17,29},{18,30},{19,31}} | collective-permute-start | bytes 344072 | tf_op jit(solution)/shard_map/ppermute | solution.py:360
  13.8 1.2 copy-start.5
  15.0 1.2 copy-start.7
  16.2 0.7 copy-start.12
  16.9 16.5 %copy-start.22 = (s32[1,2,2,4]{3,2,1,0:T(2,128)S(1)}, s32[1,2,2,4]{3,2,1,0:T(2,128)}, u32[]{:S(2)}) copy-start(s32[1,2,2,4]{3,2,1,0:T(2,128)} %param.17) | copy-start | bytes 196
  16.9 16.6 %copy-start.25 = (s32[1,128,1]{1,2,0:T(1,128)S(1)}, s32[1,128,1]{1,2,0:T(1,128)}, u32[]{:S(2)}) copy-start(s32[1,128,1]{1,2,0:T(1,128)} %param.18) | copy-start | bytes 1540
  16.9 41.5 %copy-start.3 = (bf16[1,128,3584]{2,1,0:T(8,128)(2,1)S(1)}, bf16[1,128,3584]{2,1,0:T(8,128)(2,1)}, u32[]{:S(2)}) copy-start(bf16[1,128,3584]{2,1,0:T(8,128)(2,1)} %param.14) | copy-start | bytes 2752516
  16.9 41.5 %copy-start.4 = (bf16[1,128,3584]{2,1,0:T(8,128)(2,1)S(1)}, bf16[1,128,3584]{2,1,0:T(8,128)(2,1)}, u32[]{:S(2)}) copy-start(bf16[1,128,3584]{2,1,0:T(8,128)(2,1)} %param.15) | copy-start | bytes 2752516
  16.9 41.5 %copy-start.13 = (f32[1,3584]{1,0:T(1,128)S(1)}, f32[1,3584]{1,0:T(1,128)}, u32[]{:S(2)}) copy-start(f32[1,3584]{1,0:T(1,128)} %gain_ref.5) | copy-start | bytes 43012
  19.3 0.7 copy-start.20
  20.0 13.3 %copy-start.9 = (bf16[144,896]{1,0:T(8,128)(2,1)}, bf16[144,896]{1,0:T(8,128)(2,1)S(1)}, u32[]{:S(2)}) copy-start(bf16[144,896]{1,0:T(8,128)(2,1)S(1)} %get-tuple-element.104) | copy-start | bytes 774148
  20.0 13.3 %copy-start.10 = (bf16[144,896]{1,0:T(8,128)(2,1)}, bf16[144,896]{1,0:T(8,128)(2,1)S(1)}, u32[]{:S(2)}) copy-start(bf16[144,896]{1,0:T(8,128)(2,1)S(1)} %get-tuple-element.103) | copy-start | bytes 774148
  20.0 13.3 %copy-start.11 = (bf16[144,896]{1,0:T(8,128)(2,1)}, bf16[144,896]{1,0:T(8,128)(2,1)S(1)}, u32[]{:S(2)}) copy-start(bf16[144,896]{1,0:T(8,128)(2,1)S(1)} %get-tuple-element.102) | copy-start | bytes 774148
  20.0 13.3 %copy-start.18 = (bf16[144,896]{1,0:T(8,128)(2,1)}, bf16[144,896]{1,0:T(8,128)(2,1)S(1)}, u32[]{:S(2)}) copy-start(bf16[144,896]{1,0:T(8,128)(2,1)S(1)} %get-tuple-element.105.refs_0_) | copy-start | bytes 774148
  20.1 13.2 %collective-permute-start.3 = (bf16[512,448]{1,0:T(8,128)(2,1)S(1)}, bf16[512,448]{1,0:T(8,128)(2,1)S(1)}, u32[]{:S(2)}, u32[]{:S(2)}) collective-permute-start(bf16[512,448]{1,0:T(8,128)(2,1)S(1)} %constant_dynamic-update-slice_fusion.kv0), channel_id=1, source_target_pairs={{0,2},{1,3},{2,0},{3,1},{4,6},{5,7},{6,4},{7,5},{8,10},{9,11},{10,... | collective-permute-start | bytes 1376264 | tf_op jit(solution)/shard_map/ppermute | solution.py:32
  21.7 11.8 %collective-permute-start.12 = (bf16[144,896]{1,0:T(8,128)(2,1)}, bf16[144,896]{1,0:T(8,128)(2,1)}, u32[]{:S(2)}, u32[]{:S(2)}) collective-permute-start(bf16[144,896]{1,0:T(8,128)(2,1)} %get-tuple-element.90), channel_id=1, source_target_pairs={{0,4},{1,5},{2,6},{3,7},{4,8},{5,9},{6,10},{7,11},{8,12},{9,13},{1... | collective-permute-start | bytes 774152 | tf_op jit(solution)/shard_map/ppermute | solution.py:37
  21.7 20.5 %collective-permute-start.13 = (bf16[144,896]{1,0:T(8,128)(2,1)}, bf16[144,896]{1,0:T(8,128)(2,1)}, u32[]{:S(2)}, u32[]{:S(2)}) collective-permute-start(bf16[144,896]{1,0:T(8,128)(2,1)} %get-tuple-element.91), channel_id=1, source_target_pairs={{0,8},{1,9},{2,10},{3,11},{4,12},{5,13},{6,14},{7,15},{8,0},{9,1},... | collective-permute-start | bytes 774152 | tf_op jit(solution)/shard_map/ppermute | solution.py:37
  24.3 17.9 %collective-permute-start.14 = (bf16[144,896]{1,0:T(8,128)(2,1)}, bf16[144,896]{1,0:T(8,128)(2,1)}, u32[]{:S(2)}, u32[]{:S(2)}) collective-permute-start(bf16[144,896]{1,0:T(8,128)(2,1)} %get-tuple-element.92), channel_id=1, source_target_pairs={{0,12},{1,13},{2,14},{3,15},{4,0},{5,1},{6,2},{7,3},{8,4},{9,5},{1... | collective-permute-start | bytes 774152 | tf_op jit(solution)/shard_map/ppermute | solution.py:37
  25.5 32.9 %collective-permute-start.4 = (bf16[512,448]{1,0:T(8,128)(2,1)S(1)}, bf16[512,448]{1,0:T(8,128)(2,1)S(1)}, u32[]{:S(2)}, u32[]{:S(2)}) collective-permute-start(bf16[512,448]{1,0:T(8,128)(2,1)S(1)} %constant_dynamic-update-slice_fusion.kv0), channel_id=1, source_target_pairs={{0,1},{1,0},{2,3},{3,2},{4,5},{5,4},{6,7},{7,6},{8,9},{9,8},{10,11... | collective-permute-start | bytes 1376264 | tf_op jit(solution)/shard_map/ppermute | solution.py:32
  33.3 25.1 %collective-permute-start.5 = (bf16[512,448]{1,0:T(8,128)(2,1)S(1)}, bf16[512,448]{1,0:T(8,128)(2,1)}, u32[]{:S(2)}, u32[]{:S(2)}) collective-permute-start(bf16[512,448]{1,0:T(8,128)(2,1)S(1)} %collective-permute-done.3.kv1), channel_id=1, source_target_pairs={{0,1},{1,0},{2,3},{3,2},{4,5},{5,4},{6,7},{7,6},{8,9},{9,8},{10,11... | collective-permute-start | bytes 1376264 | tf_op jit(solution)/shard_map/ppermute | solution.py:32
  42.2 27.1 %collective-permute-start.16 = (bf16[144,896]{1,0:T(8,128)(2,1)}, bf16[144,896]{1,0:T(8,128)(2,1)}, u32[]{:S(2)}, u32[]{:S(2)}) collective-permute-start(bf16[144,896]{1,0:T(8,128)(2,1)} %copy-done.11), channel_id=1, source_target_pairs={{0,4},{1,5},{2,6},{3,7},{4,8},{5,9},{6,10},{7,11},{8,12},{9,13},{1... | collective-permute-start | bytes 774152 | tf_op jit(solution)/shard_map/ppermute | solution.py:37
  56.0 13.3 %collective-permute-start.17 = (bf16[144,896]{1,0:T(8,128)(2,1)}, bf16[144,896]{1,0:T(8,128)(2,1)}, u32[]{:S(2)}, u32[]{:S(2)}) collective-permute-start(bf16[144,896]{1,0:T(8,128)(2,1)} %copy-done.10), channel_id=1, source_target_pairs={{0,8},{1,9},{2,10},{3,11},{4,12},{5,13},{6,14},{7,15},{8,0},{9,1},... | collective-permute-start | bytes 774152 | tf_op jit(solution)/shard_map/ppermute | solution.py:37
  56.0 13.3 %collective-permute-start.18 = (bf16[144,896]{1,0:T(8,128)(2,1)}, bf16[144,896]{1,0:T(8,128)(2,1)}, u32[]{:S(2)}, u32[]{:S(2)}) collective-permute-start(bf16[144,896]{1,0:T(8,128)(2,1)} %copy-done.9), channel_id=1, source_target_pairs={{0,12},{1,13},{2,14},{3,15},{4,0},{5,1},{6,2},{7,3},{8,4},{9,5},{1... | collective-permute-start | bytes 774152 | tf_op jit(solution)/shard_map/ppermute | solution.py:37
  58.5 8.1 %copy-start.21 = (bf16[144,896]{1,0:T(8,128)(2,1)S(1)}, bf16[144,896]{1,0:T(8,128)(2,1)}, u32[]{:S(2)}) copy-start(bf16[144,896]{1,0:T(8,128)(2,1)} %copy-done.20) | copy-start | bytes 774148
  66.6 2.7 %copy-start.16 = (bf16[128,3584]{1,0:T(8,128)(2,1)}, bf16[128,3584]{1,0:T(8,128)(2,1)S(1)}, u32[]{:S(2)}) copy-start(bf16[128,3584]{1,0:T(8,128)(2,1)S(1)} %get-tuple-element.75.middle_ref) | copy-start | bytes 2752516
  66.6 2.7 %copy-start.19 = (bf16[144,896]{1,0:T(8,128)(2,1)S(1)}, bf16[144,896]{1,0:T(8,128)(2,1)}, u32[]{:S(2)}) copy-start(bf16[144,896]{1,0:T(8,128)(2,1)} %copy-done.18) | copy-start | bytes 774148
  69.3 40.7 %copy-start.2 = (bf16[1,1,256,3584]{3,2,1,0:T(8,128)(2,1)S(1)}, bf16[1,1,256,3584]{3,2,1,0:T(8,128)(2,1)}, u32[]{:S(2)}) copy-start(bf16[1,1,256,3584]{3,2,1,0:T(8,128)(2,1)} %param.27) | copy-start | bytes 5505028
  71.7 25.5 %collective-permute-start.22 = (bf16[144,3584]{1,0:T(8,128)(2,1)S(1)}, bf16[144,3584]{1,0:T(8,128)(2,1)S(1)}, u32[]{:S(2)}, u32[]{:S(2)}) collective-permute-start(bf16[144,3584]{1,0:T(8,128)(2,1)S(1)} %shard_map.154.first_grad), channel_id=1, source_target_pairs={{0,2},{1,3},{2,0},{3,1},{4,6},{5,7},{6,4},{7,5},{8,10},{9,11},{10,... | collective-permute-start | bytes 3096584 | tf_op jit(solution)/shard_map/ppermute | solution.py:32
  72.3 36.0 %collective-permute-start.20 = (bf16[144,3584]{1,0:T(8,128)(2,1)S(1)}, bf16[144,3584]{1,0:T(8,128)(2,1)S(1)}, u32[]{:S(2)}, u32[]{:S(2)}) collective-permute-start(bf16[144,3584]{1,0:T(8,128)(2,1)S(1)} %shard_map.153.first_ref), channel_id=1, source_target_pairs={{0,2},{1,3},{2,0},{3,1},{4,6},{5,7},{6,4},{7,5},{8,10},{9,11},{10,... | collective-permute-start | bytes 3096584 | tf_op jit(solution)/shard_map/ppermute | solution.py:32
  73.8 10.1 %collective-permute-start.6 = (bf16[144,896]{1,0:T(8,128)(2,1)S(1)}, bf16[144,896]{1,0:T(8,128)(2,1)S(1)}, u32[]{:S(2)}, u32[]{:S(2)}) collective-permute-start(bf16[144,896]{1,0:T(8,128)(2,1)S(1)} %get-tuple-element.77), channel_id=1, source_target_pairs={{0,4},{1,5},{2,6},{3,7},{4,8},{5,9},{6,10},{7,11},{8,12},{9,13},{1... | collective-permute-start | bytes 774152 | tf_op jit(solution)/shard_map/ppermute | solution.py:37
  80.1 9.9 %collective-permute-start.7 = (bf16[144,896]{1,0:T(8,128)(2,1)S(1)}, bf16[144,896]{1,0:T(8,128)(2,1)S(1)}, u32[]{:S(2)}, u32[]{:S(2)}) collective-permute-start(bf16[144,896]{1,0:T(8,128)(2,1)S(1)} %get-tuple-element.78), channel_id=1, source_target_pairs={{0,8},{1,9},{2,10},{3,11},{4,12},{5,13},{6,14},{7,15},{8,0},{9,1},... | collective-permute-start | bytes 774152 | tf_op jit(solution)/shard_map/ppermute | solution.py:37
  80.1 29.9 %collective-permute-start.19 = (bf16[144,3584]{1,0:T(8,128)(2,1)S(1)}, bf16[144,3584]{1,0:T(8,128)(2,1)S(1)}, u32[]{:S(2)}, u32[]{:S(2)}) collective-permute-start(bf16[144,3584]{1,0:T(8,128)(2,1)S(1)} %shard_map.154.first_grad), channel_id=1, source_target_pairs={{0,1},{1,0},{2,3},{3,2},{4,5},{5,4},{6,7},{7,6},{8,9},{9,8},{10,11... | collective-permute-start | bytes 3096584 | tf_op jit(solution)/shard_map/ppermute | solution.py:32
  84.0 26.1 %collective-permute-start.15 = (bf16[144,3584]{1,0:T(8,128)(2,1)S(1)}, bf16[144,3584]{1,0:T(8,128)(2,1)S(1)}, u32[]{:S(2)}, u32[]{:S(2)}) collective-permute-start(bf16[144,3584]{1,0:T(8,128)(2,1)S(1)} %shard_map.153.first_ref), channel_id=1, source_target_pairs={{0,1},{1,0},{2,3},{3,2},{4,5},{5,4},{6,7},{7,6},{8,9},{9,8},{10,11... | collective-permute-start | bytes 3096584 | tf_op jit(solution)/shard_map/ppermute | solution.py:32
  90.0 18.3 %collective-permute-start.8 = (bf16[144,896]{1,0:T(8,128)(2,1)S(1)}, bf16[144,896]{1,0:T(8,128)(2,1)S(1)}, u32[]{:S(2)}, u32[]{:S(2)}) collective-permute-start(bf16[144,896]{1,0:T(8,128)(2,1)S(1)} %get-tuple-element.79), channel_id=1, source_target_pairs={{0,12},{1,13},{2,14},{3,15},{4,0},{5,1},{6,2},{7,3},{8,4},{9,5},{1... | collective-permute-start | bytes 774152 | tf_op jit(solution)/shard_map/ppermute | solution.py:37
  97.3 17.0 %collective-permute-start.23 = (bf16[144,3584]{1,0:T(8,128)(2,1)S(1)}, bf16[144,3584]{1,0:T(8,128)(2,1)S(1)}, u32[]{:S(2)}, u32[]{:S(2)}) collective-permute-start(bf16[144,3584]{1,0:T(8,128)(2,1)S(1)} %collective-permute-done.22.first_grad), channel_id=1, source_target_pairs={{0,1},{1,0},{2,3},{3,2},{4,5},{5,4},{6,7},{7,6},{8,9},{9,8},{10,11... | collective-permute-start | bytes 3096584 | tf_op jit(solution)/shard_map/ppermute | solution.py:32
  108.3 5.9 %collective-permute-start.21 = (bf16[144,3584]{1,0:T(8,128)(2,1)S(1)}, bf16[144,3584]{1,0:T(8,128)(2,1)S(1)}, u32[]{:S(2)}, u32[]{:S(2)}) collective-permute-start(bf16[144,3584]{1,0:T(8,128)(2,1)S(1)} %collective-permute-done.20.first_ref), channel_id=1, source_target_pairs={{0,1},{1,0},{2,3},{3,2},{4,5},{5,4},{6,7},{7,6},{8,9},{9,8},{10,11... | collective-permute-start | bytes 3096584 | tf_op jit(solution)/shard_map/ppermute | solution.py:32
  108.3 1.7 copy-start
  108.3 2.0 copy-start.1
  109.4 25.3 %collective-permute-start.11 = (bf16[144,3584]{1,0:T(8,128)(2,1)S(1)}, bf16[144,3584]{1,0:T(8,128)(2,1)S(1)}, u32[]{:S(2)}, u32[]{:S(2)}) collective-permute-start(bf16[144,3584]{1,0:T(8,128)(2,1)S(1)} %shard_map.151.first_ref), channel_id=1, source_target_pairs={{0,2},{1,3},{2,0},{3,1},{4,6},{5,7},{6,4},{7,5},{8,10},{9,11},{10,... | collective-permute-start | bytes 3096584 | tf_op jit(solution)/shard_map/ppermute | solution.py:32
  114.2 3.9 %copy-start.14 = (bf16[144,3584]{1,0:T(8,128)(2,1)}, bf16[144,3584]{1,0:T(8,128)(2,1)S(1)}, u32[]{:S(2)}) copy-start(bf16[144,3584]{1,0:T(8,128)(2,1)S(1)} %get-tuple-element.116.own_ref) | copy-start | bytes 3096580
  134.7 2.6 %collective-permute-start.24 = (bf16[144,3584]{1,0:T(8,128)(2,1)S(1)}, bf16[144,3584]{1,0:T(8,128)(2,1)S(1)}, u32[]{:S(2)}, u32[]{:S(2)}) collective-permute-start(bf16[144,3584]{1,0:T(8,128)(2,1)S(1)} %collective-permute-done.11.first_ref), channel_id=1, source_target_pairs={{0,1},{1,0},{2,3},{3,2},{4,5},{5,4},{6,7},{7,6},{8,9},{9,8},{10,11... | collective-permute-start | bytes 3096584 | tf_op jit(solution)/shard_map/ppermute | solution.py:32
  134.7 5.6 %collective-permute-start.9 = (bf16[144,3584]{1,0:T(8,128)(2,1)S(1)}, bf16[144,3584]{1,0:T(8,128)(2,1)S(1)}, u32[]{:S(2)}, u32[]{:S(2)}) collective-permute-start(bf16[144,3584]{1,0:T(8,128)(2,1)S(1)} %shard_map.151.first_ref), channel_id=1, source_target_pairs={{0,1},{1,0},{2,3},{3,2},{4,5},{5,4},{6,7},{7,6},{8,9},{9,8},{10,11... | collective-permute-start | bytes 3096584 | tf_op jit(solution)/shard_map/ppermute | solution.py:32
  135.2 8.1 %collective-permute-start.28 = (bf16[144,3584]{1,0:T(8,128)(2,1)S(1)}, bf16[144,3584]{1,0:T(8,128)(2,1)S(1)}, u32[]{:S(2)}, u32[]{:S(2)}) collective-permute-start(bf16[144,3584]{1,0:T(8,128)(2,1)S(1)} %get-tuple-element.112), channel_id=1, source_target_pairs={{0,1},{1,0},{2,3},{3,2},{4,5},{5,4},{6,7},{7,6},{8,9},{9,8},{10,11... | collective-permute-start | bytes 3096584 | tf_op jit(solution)/shard_map/ppermute | solution.py:32
  135.2 12.9 %collective-permute-start.27 = (bf16[144,3584]{1,0:T(8,128)(2,1)S(1)}, bf16[144,3584]{1,0:T(8,128)(2,1)}, u32[]{:S(2)}, u32[]{:S(2)}) collective-permute-start(bf16[144,3584]{1,0:T(8,128)(2,1)S(1)} %get-tuple-element.110), channel_id=1, source_target_pairs={{0,1},{1,0},{2,3},{3,2},{4,5},{5,4},{6,7},{7,6},{8,9},{9,8},{10,11... | collective-permute-start | bytes 3096584 | tf_op jit(solution)/shard_map/ppermute | solution.py:32
  139.2 5.9 %collective-permute-start.25 = (bf16[144,3584]{1,0:T(8,128)(2,1)S(1)}, bf16[144,3584]{1,0:T(8,128)(2,1)S(1)}, u32[]{:S(2)}, u32[]{:S(2)}) collective-permute-start(bf16[144,3584]{1,0:T(8,128)(2,1)S(1)} %get-tuple-element.115), channel_id=1, source_target_pairs={{0,1},{1,0},{2,3},{3,2},{4,5},{5,4},{6,7},{7,6},{8,9},{9,8},{10,11... | collective-permute-start | bytes 3096584 | tf_op jit(solution)/shard_map/ppermute | solution.py:32
  143.2 37.5 %collective-permute-start.10 = (bf16[144,3584]{1,0:T(8,128)(2,1)}, bf16[144,3584]{1,0:T(8,128)(2,1)S(1)}, u32[]{:S(2)}, u32[]{:S(2)}) collective-permute-start(bf16[144,3584]{1,0:T(8,128)(2,1)} %get-tuple-element.81), channel_id=1, source_target_pairs={{0,1},{1,0},{2,3},{3,2},{4,5},{5,4},{6,7},{7,6},{8,9},{9,8},{10,11... | collective-permute-start | bytes 3096584 | tf_op jit(solution)/shard_map/ppermute | solution.py:32
  144.6 3.3 %copy-start.24 = (s32[1,128,1]{1,2,0:T(1,128)S(1)}, s32[1,128,1]{1,2,0:T(1,128)}, u32[]{:S(2)}) copy-start(s32[1,128,1]{1,2,0:T(1,128)} %param.22) | copy-start | bytes 1540
  144.6 3.5 %copy-start.23 = (f32[1,128,1]{1,2,0:T(1,128)S(1)}, f32[1,128,1]{1,2,0:T(1,128)}, u32[]{:S(2)}) copy-start(f32[1,128,1]{1,2,0:T(1,128)} %param.19) | copy-start | bytes 1540
  144.6 26.0 %collective-permute-start.29 = (bf16[144,3584]{1,0:T(8,128)(2,1)}, bf16[144,3584]{1,0:T(8,128)(2,1)}, u32[]{:S(2)}, u32[]{:S(2)}) collective-permute-start(bf16[144,3584]{1,0:T(8,128)(2,1)} %add_convert_fusion), channel_id=1, source_target_pairs={{0,2},{1,3},{2,0},{3,1},{4,6},{5,7},{6,4},{7,5},{8,10},{9,11},{10,... | collective-permute-start | bytes 3096584 | tf_op jit(solution)/shard_map/ppermute | solution.py:32
  146.3 45.8 %collective-permute-start.26 = (bf16[144,3584]{1,0:T(8,128)(2,1)}, bf16[144,3584]{1,0:T(8,128)(2,1)}, u32[]{:S(2)}, u32[]{:S(2)}) collective-permute-start(bf16[144,3584]{1,0:T(8,128)(2,1)} %add_convert_fusion.1), channel_id=1, source_target_pairs={{0,2},{1,3},{2,0},{3,1},{4,6},{5,7},{6,4},{7,5},{8,10},{9,11},{10,... | collective-permute-start | bytes 3096584 | tf_op jit(solution)/shard_map/ppermute | solution.py:32
  170.5 1.2 copy-start.15
  174.4 26.4 %collective-permute-start.33 = (bf16[144,896]{1,0:T(8,128)(2,1)S(1)}, bf16[144,896]{1,0:T(8,128)(2,1)S(1)}, u32[]{:S(2)}, u32[]{:S(2)}) collective-permute-start(bf16[144,896]{1,0:T(8,128)(2,1)S(1)} %get-tuple-element.120), channel_id=1, source_target_pairs={{0,12},{1,13},{2,14},{3,15},{4,0},{5,1},{6,2},{7,3},{8,4},{9,5},{1... | collective-permute-start | bytes 774152 | tf_op jit(solution)/shard_map/ppermute | solution.py:37
  176.8 37.9 %collective-permute-start.34 = (bf16[144,896]{1,0:T(8,128)(2,1)S(1)}, bf16[144,896]{1,0:T(8,128)(2,1)S(1)}, u32[]{:S(2)}, u32[]{:S(2)}) collective-permute-start(bf16[144,896]{1,0:T(8,128)(2,1)S(1)} %get-tuple-element.121), channel_id=1, source_target_pairs={{0,8},{1,9},{2,10},{3,11},{4,12},{5,13},{6,14},{7,15},{8,0},{9,1},... | collective-permute-start | bytes 774152 | tf_op jit(solution)/shard_map/ppermute | solution.py:37
  180.7 34.0 %collective-permute-start.35 = (bf16[144,896]{1,0:T(8,128)(2,1)S(1)}, bf16[144,896]{1,0:T(8,128)(2,1)S(1)}, u32[]{:S(2)}, u32[]{:S(2)}) collective-permute-start(bf16[144,896]{1,0:T(8,128)(2,1)S(1)} %get-tuple-element.122), channel_id=1, source_target_pairs={{0,4},{1,5},{2,6},{3,7},{4,8},{5,9},{6,10},{7,11},{8,12},{9,13},{1... | collective-permute-start | bytes 774152 | tf_op jit(solution)/shard_map/ppermute | solution.py:37
  192.1 22.6 %copy-start.6 = (bf16[1,128,3584]{2,1,0:T(8,128)(2,1)S(1)}, bf16[1,128,3584]{2,1,0:T(8,128)(2,1)}, u32[]{:S(2)}) copy-start(bf16[1,128,3584]{2,1,0:T(8,128)(2,1)} %param.20) | copy-start | bytes 2752516
  192.1 22.6 %copy-start.8 = (bf16[1,128,3584]{2,1,0:T(8,128)(2,1)S(1)}, bf16[1,128,3584]{2,1,0:T(8,128)(2,1)}, u32[]{:S(2)}) copy-start(bf16[1,128,3584]{2,1,0:T(8,128)(2,1)} %param.21) | copy-start | bytes 2752516
  194.6 23.5 %collective-permute-start.30 = (bf16[144,896]{1,0:T(8,128)(2,1)S(1)}, bf16[144,896]{1,0:T(8,128)(2,1)S(1)}, u32[]{:S(2)}, u32[]{:S(2)}) collective-permute-start(bf16[144,896]{1,0:T(8,128)(2,1)S(1)} %get-tuple-element.127), channel_id=1, source_target_pairs={{0,12},{1,13},{2,14},{3,15},{4,0},{5,1},{6,2},{7,3},{8,4},{9,5},{1... | collective-permute-start | bytes 774152 | tf_op jit(solution)/shard_map/ppermute | solution.py:37
  196.9 27.5 %collective-permute-start.31 = (bf16[144,896]{1,0:T(8,128)(2,1)S(1)}, bf16[144,896]{1,0:T(8,128)(2,1)S(1)}, u32[]{:S(2)}, u32[]{:S(2)}) collective-permute-start(bf16[144,896]{1,0:T(8,128)(2,1)S(1)} %get-tuple-element.128), channel_id=1, source_target_pairs={{0,8},{1,9},{2,10},{3,11},{4,12},{5,13},{6,14},{7,15},{8,0},{9,1},... | collective-permute-start | bytes 774152 | tf_op jit(solution)/shard_map/ppermute | solution.py:37
  200.8 23.6 %collective-permute-start.32 = (bf16[144,896]{1,0:T(8,128)(2,1)S(1)}, bf16[144,896]{1,0:T(8,128)(2,1)S(1)}, u32[]{:S(2)}, u32[]{:S(2)}) collective-permute-start(bf16[144,896]{1,0:T(8,128)(2,1)S(1)} %get-tuple-element.129), channel_id=1, source_target_pairs={{0,4},{1,5},{2,6},{3,7},{4,8},{5,9},{6,10},{7,11},{8,12},{9,13},{1... | collective-permute-start | bytes 774152 | tf_op jit(solution)/shard_map/ppermute | solution.py:37
  214.7 9.7 %copy-start.17 = (bf16[128,3584]{1,0:T(8,128)(2,1)S(1)}, bf16[128,3584]{1,0:T(8,128)(2,1)}, u32[]{:S(2)}) copy-start(bf16[128,3584]{1,0:T(8,128)(2,1)} %copy-done.16) | copy-start | bytes 2752516
  216.5 16.1 %collective-permute-start.37 = (bf16[128,3584]{1,0:T(8,128)(2,1)S(1)}, bf16[128,3584]{1,0:T(8,128)(2,1)S(1)}, u32[]{:S(2)}, u32[]{:S(2)}) collective-permute-start(bf16[128,3584]{1,0:T(8,128)(2,1)S(1)} %shard_map.160), channel_id=1, source_target_pairs={{0,16},{16,0},{1,17},{17,1},{2,18},{18,2},{3,19},{19,3},{4,20},{20... | collective-permute-start | bytes 2752520 | tf_op jit(solution)/shard_map/ppermute | solution.py:28
  225.8 23.8 %collective-permute-start.36 = (bf16[128,3584]{1,0:T(8,128)(2,1)S(1)}, bf16[128,3584]{1,0:T(8,128)(2,1)S(1)}, u32[]{:S(2)}, u32[]{:S(2)}) collective-permute-start(bf16[128,3584]{1,0:T(8,128)(2,1)S(1)} %shard_map.161), channel_id=1, source_target_pairs={{0,16},{16,0},{1,17},{17,1},{2,18},{18,2},{3,19},{19,3},{4,20},{20... | collective-permute-start | bytes 2752520 | tf_op jit(solution)/shard_map/ppermute | solution.py:28

commit v4 on v3

--- a/solution.py
+++ b/solution.py
@@ -23,9 +23,14 @@
 f32 = jnp.float32
 
 
-def passed_along(array, axis, by):
-    length = lax.axis_size(axis)
-    return lax.ppermute(array, axis, [(i, (i + by) % length) for i in range(length)])
+def passed_along(array, by, back=0):
+    sections, length = lax.axis_size("section"), lax.axis_size("expert")
+    pairs = [
+        (s * length + i, (s + by) % sections * length + (i - back * GROUP) % length)
+        for s in range(sections)
+        for i in range(length)
+    ]
+    return lax.ppermute(array, ("section", "expert"), pairs)
 
 
 def swapped(array, bit):
@@ -140,11 +145,14 @@
         out[:, p * width : (p + 1) * width] = dot(pick, rows).astype(bf16)
 
 
-def split_body(capacity, own_ref, core_ref, chip_ref, *outs):
-    total = own_ref[...].astype(f32) + core_ref[...].astype(f32) + chip_ref[...].astype(f32)
+def split_body(capacity, count_shares, *refs):
+    shares, outs = refs[:count_shares], refs[count_shares:]
+    total = shares[0][...].astype(f32)
+    for ref in shares[1:]:
+        total = total + ref[...].astype(f32)
     rows = stacked(total.astype(bf16))
     height = PARTS * capacity
-    slots = own_ref.shape[0]
+    slots = shares[0].shape[0]
     count = height * len(outs)
     index = iota((count, 1), 0)
     group = index * 0
@@ -189,36 +197,44 @@
     out[...] = (grad_ref[...].astype(f32) + scale * amount - middle * cube * mean).astype(bf16)
 
 
-def forward_body(first_ref, second_ref, gate_ref, up_ref, down_ref, first_out, second_out):
+def hidden_body(first_ref, second_ref, gate_ref, up_ref, out_ref):
+    rows = jnp.concatenate([first_ref[...], second_ref[...]], axis=0)
+    gate_val = dot(rows, gate_ref[...])
+    up_val = dot(rows, up_ref[...])
+    out_ref[...] = (gate_val / (1.0 + jnp.exp(-gate_val)) * up_val).astype(bf16)
+
+
+def output_body(own_ref, other_ref, down_ref, top_ref, low_ref, first_out, second_out):
+    half = first_out.shape[0]
+    hidden = jnp.concatenate([own_ref[...], other_ref[...]], axis=1)
+    step = 4 * LANES
+    for n in range(0, down_ref.shape[1], step):
+        part = slice(n, n + step)
+        weight = jnp.concatenate([down_ref[:, part], top_ref[:, part], low_ref[:, part]], axis=0)
+        value = dot(hidden, weight).astype(bf16)
+        first_out[:, part] = value[:half]
+        second_out[:, part] = value[half:]
+
+
+def down_back_body(first_ref, second_ref, down_ref, top_ref, low_ref, own_out, other_out):
+    grads = jnp.concatenate([first_ref[...], second_ref[...]], axis=0)
+    own_out[...] = dot_last(grads, down_ref[...]).astype(own_out.dtype)
+    other = jnp.concatenate([top_ref[...], low_ref[...]], axis=0)
+    other_out[...] = dot_last(grads, other).astype(other_out.dtype)
+
+
+def backward_body(first_ref, second_ref, back_ref, gate_ref, up_ref, first_out, second_out):
     half = first_ref.shape[0]
     rows = jnp.concatenate([first_ref[...], second_ref[...]], axis=0)
     gate_val = dot(rows, gate_ref[...])
     up_val = dot(rows, up_ref[...])
-    hidden = (gate_val / (1.0 + jnp.exp(-gate_val)) * up_val).astype(bf16)
-    width = down_ref.shape[1]
-    step = 4 * LANES
-    for n in range(0, width, step):
-        value = dot(hidden, down_ref[:, n : n + step]).astype(bf16)
-        first_out[:, n : n + step] = value[:half]
-        second_out[:, n : n + step] = value[half:]
-
-
-def backward_body(
-    first_ref, second_ref, first_grad, second_grad, gate_ref, up_ref, down_ref, first_out, second_out
-):
-    half = first_ref.shape[0]
-    rows = jnp.concatenate([first_ref[...], second_ref[...]], axis=0)
-    gate_val = dot(rows, gate_ref[...])
-    up_val = dot(rows, up_ref[...])
-    grads = jnp.concatenate([first_grad[...], second_grad[...]], axis=0)
-    down_back = dot_last(grads, down_ref[...])
+    down_back = back_ref[...].astype(f32)
     sigmoid_val = 1.0 / (1.0 + jnp.exp(-gate_val))
     slope_val = sigmoid_val * (1.0 + gate_val * (1.0 - sigmoid_val))
     gate_grad = (down_back * up_val * slope_val).astype(bf16)
     up_grad = (down_back * gate_val * sigmoid_val).astype(bf16)
-    width = down_ref.shape[1]
     step = 4 * LANES
-    for n in range(0, width, step):
+    for n in range(0, gate_ref.shape[0], step):
         value = dot_last(gate_grad, gate_ref[n : n + step])
         value = (value + dot_last(up_grad, up_ref[n : n + step])).astype(bf16)
         first_out[:, n : n + step] = value[:half]
@@ -347,7 +363,7 @@
     capacity = average + max(1, average // 8)
     slots = experts * capacity
     hidden_width = gate_slice.shape[3]
-    weights = (gate_slice[0, 0], up_slice[0, 0], down_slice[0, 0])
+    w_gate, w_up, w_down = gate_slice[0, 0], up_slice[0, 0], down_slice[0, 0]
     me = lax.axis_index("expert")
     group = me // GROUP
     chunk = shape_of(PARTS * capacity, width // PARTS)
@@ -358,6 +374,9 @@
     for back in range(1, experts):
         pairs = [(i, i + back * GROUP) for i in range(length - back * GROUP)]
         column.append(lax.ppermute(keys_values[0], "expert", pairs))
+    early = hidden_width * 3 // 8
+    down_top = swapped(w_down[:early], 2)
+
     front_from = lax.rem(front_route[0] - group + experts, experts)
     back_from = lax.rem(back_route[0] - group + experts, experts)
     front_row, back_row = front_from.reshape(1, tokens), back_from.reshape(1, tokens)
@@ -371,10 +390,14 @@
     )
     column = after(column, [packed[0]])
     column = jnp.concatenate(column, axis=0)
-    other_chip = swapped(column, 2)
-    kv = [column, other_chip, swapped(column, 1), swapped(other_chip, 1)]
-
+    other_chip = swapped(after([column], [down_top])[0], 2)
+    kv = [column, other_chip, swapped(column, 1), None]
     packed = after(packed, [column])
+    down_low = swapped(after([w_down[early:]], [other_chip])[0], 2)
+    downs = (w_down, down_top, down_low)
+
+    front_small = jnp.concatenate([front_from.astype(f32), front_gate[0]], axis=0).reshape(1, -1)
+    back_small = jnp.concatenate([back_from.astype(f32).reshape(1, -1), norm_gain], axis=1)
 
     def sent(chunks):
         return [chunks[0]] + [turned(chunks[k], k) for k in range(1, experts)]
@@ -386,21 +409,24 @@
         other = swapped(rows, 2)
         return [rows, swapped(rows, 1), other, swapped(other, 1)]
 
-    def shares(near, far):
-        chip = far[0].astype(f32) + swapped(far[1], 1).astype(f32)
-        parts = (near[0], swapped(near[1], 1), swapped(chip.astype(bf16), 2))
-        return parts
-
     def split(parts):
         return call(
-            functools.partial(split_body, capacity), [chunk] * experts, parts, flops=pack_flops
+            functools.partial(split_body, capacity, len(parts)),
+            [chunk] * experts,
+            parts,
+            flops=pack_flops,
         )
 
-    def sent_back(chunks):
-        return [chunks[0]] + [turned(chunks[k], -k) for k in range(1, experts)]
-
-    row_chunks = sent(packed[:experts])
-    grad_chunks = sent(after(packed[experts:], row_chunks))
+    def sent_back(chunks, by):
+        return [passed_along(chunks[k], by, k) for k in range(experts)]
+
+    row_chunks = packed[:experts]
+    for k in range(1, experts, 2):
+        row_chunks[k] = turned(row_chunks[k], k)
+    arrived = row_chunks[1::2]
+    for k in range(2, experts, 2):
+        row_chunks[k] = turned(after([row_chunks[k]], arrived)[0], k)
+    kv[3] = swapped(after([other_chip], arrived)[0], 1)
 
     per_device = tokens // BLK
     chosen = selected_blocks[0].reshape(-1)
@@ -425,61 +451,74 @@
         vmem=VMEM_BYTES + 2 * length * tokens * 4 * LANES * 2,
     )
     middle, front_chunks = result[0], result[1:]
-    front_chunks = sent(front_chunks)
-    back_pieces = pieces_of(joined(after(row_chunks, [middle])))
-    grad_pieces = pieces_of(joined(after(grad_chunks, [back_pieces[0]])))
-    front_rows = joined(front_chunks)
-    front_other = swapped(front_rows, 2)
+    front_chunks = sent(after(front_chunks, row_chunks))
+    back_pieces = pieces_of(after([joined(after(row_chunks, [middle]))], [down_low])[0])
+    front_small, back_small = after([front_small, back_small], [back_pieces[0]])
+    there_small = passed_along(front_small, 1)
+    there_back_small = passed_along(back_small, -1)
+    there_front_from = there_small[0, :tokens].astype(jnp.int32).reshape(tokens, 1)
+    there_front_gate = there_small[0, tokens:].reshape(tokens, 1)
+    there_back_from = there_back_small[0, :tokens].astype(jnp.int32).reshape(tokens, 1)
+    there_gain = there_back_small[:, tokens:]
+    there_back_middle = passed_along(after([back_middle[0]], [back_pieces[0]])[0], -1)
+    front_chunks = after(front_chunks, [back_pieces[0], there_small, there_back_small])
+    grad_chunks = sent(after(packed[experts:], front_chunks))
+    there_back_grad = passed_along(after([back_grad[0]], [there_back_middle])[0], -1)
+    front_pieces = pieces_of(joined(after(front_chunks, [there_back_middle])))
+    there_middle = passed_along(after([middle], [there_back_grad])[0], 1)
+    grad_near = joined(after(grad_chunks, [front_pieces[0], there_back_grad]))
+    grad_near = [grad_near, swapped(grad_near, 1)]
 
     work = 2 * 2 * slots * width * hidden_width
-
-    def backward(first, second):
+    pair = 2 * slots
+
+    def hidden(rows):
         return call(
-            backward_body,
-            [piece, piece],
-            (*back_pieces[first:second], *grad_pieces[first:second], *weights),
-            flops=5 * work,
+            hidden_body, shape_of(pair, hidden_width), (*rows, w_gate, w_up), flops=2 * work
         )
 
-    def forward(first, second):
-        return call(
-            forward_body,
-            [piece, piece],
-            (*front_pieces[first:second], *weights),
-            flops=3 * work,
-        )
-
-    back_far = backward(2, 4)
-    back_near = backward(0, 2)
-    back_shares = shares(back_near, back_far)
-
-    (front_other,) = after([front_other], back_near + back_far)
-    front_pieces = [front_rows, swapped(front_rows, 1), front_other, swapped(front_other, 1)]
-    front_far = forward(2, 4)
-    front_near = forward(0, 2)
-    front_shares = shares(front_near, front_far)
-
-    back_chunks = split(after(back_shares, front_near + front_far))
-    back_return = sent_back(back_chunks)
-    front_chunks = split(after(front_shares, back_chunks))
-    front_return = sent_back(front_chunks)
-    back_return = after(back_return, front_chunks)
-
-    back_result = call(
+    def backward(rows, grads):
+        return call(backward_body, [piece, piece], (*rows, grads, w_gate, w_up), flops=4 * work)
+
+    hidden_near = hidden(front_pieces[:2])
+    hidden_far = hidden(front_pieces[2:])
+    down_back, other_back = call(
+        down_back_body,
+        [shape_of(pair, hidden_width, f32), shape_of(pair, hidden_width)],
+        (*grad_near, *downs),
+        flops=2 * work,
+    )
+    hidden_other = swapped(hidden_far, 2)
+    far_back = swapped(other_back, 2)
+
+    back_near = backward(back_pieces[:2], down_back)
+    back_far = backward(back_pieces[2:], far_back)
+    chip = back_far[0].astype(f32) + swapped(back_far[1], 1).astype(f32)
+    back_shares = (back_near[0], swapped(back_near[1], 1), swapped(chip.astype(bf16), 2))
+
+    front_own, front_core = call(
+        output_body, [piece, piece], (hidden_near, hidden_other, *downs), flops=2 * work
+    )
+    front_chunks = split((front_own, swapped(front_core, 1)))
+    front_return = sent_back(front_chunks, 1)
+
+    back_chunks = split(after(back_shares, front_chunks))
+    back_return = sent_back(back_chunks, -1)
+
+    front_return = after(front_return, back_chunks)
+    front_output = call(
+        functools.partial(front_finish_body, experts, capacity),
+        whole,
+        (there_front_from, there_front_gate, there_middle, *front_return),
+        flops=pack_flops,
+    )
+    back_return = after(back_return, [front_output])
+    back_output = call(
         functools.partial(back_finish_body, experts, capacity),
         whole,
-        (back_from, norm_gain, back_middle[0], back_grad[0], *back_return),
+        (there_back_from, there_gain, there_back_middle, there_back_grad, *back_return),
         flops=pack_flops,
     )
-    back_output = passed_along(back_result, "section", -1)
-    front_return = after(front_return, [back_result])
-    front_result = call(
-        functools.partial(front_finish_body, experts, capacity),
-        whole,
-        (front_from, front_gate[0], middle, *front_return),
-        flops=pack_flops,
-    )
-    front_output = passed_along(front_result, "section", 1)
     return (front_output[None], back_output[None])
 
 

time: 254 us -> 254 us (level)
  local copies, waits for them, and re-layouts: 9.47 us -> 19.7 us
  starting transfers between devices: 65.5 us -> 62.1 us
    ppermute x2 -> x13, waiting for transfers between devices: 22.2 us -> 51.2 us  [passed_along(): return lax.ppermute(array, ('section', 'expert'), pairs)]
    ppermute x15 -> x9, starting transfers between devices: 43.9 us -> 15.2 us  [turned(): lax.ppermute(array, 'expert', [(i, (i + by * GROUP) % length) for i in ra...]
    ppermute x18, waiting for transfers between devices: 73.9 us -> 46.8 us  [swapped(): lax.ppermute(array, 'expert', [(i, i ^ bit) for i in range(lax.axis_size(...]
    ppermute x2 -> x13, starting transfers between devices: 3.19 us -> 27.4 us  [passed_along(): return lax.ppermute(array, ('section', 'expert'), pairs)]
    unnamed x58 -> x86, local copies, waits for them, and re-layouts: 8.27 us -> 15.5 us
    slice x0 -> x3, local copies, waits for them, and re-layouts: none -> 3.06 us  [the longest x1 1.99 us: shards(): down_top = swapped(w_down[:early], 2)]
    ppermute x15 -> x9, waiting for transfers between devices: 38.8 us -> 36.3 us  [turned(): lax.ppermute(array, 'expert', [(i, (i + by * GROUP) % length) for i in ra...]
    pallas_call x13 -> x15, Pallas kernels: 37.2 us -> 35.5 us  [call(): pl.pallas_call(body, out_shape=shapes, in_specs=specs, out_specs=[pl.Bloc...]
  transfers between devices with their start and end apart: 38 -> 43, of which waited for: 15 -> 20; matrix products, arithmetic and copies ran while one was open for 2% -> 3% of each run, Pallas kernels for 14% -> 12%
where the time goes in v4:
time: 254 us
  waiting for transfers between devices  134 us (53%)
  starting transfers between devices  62.1 us (24%)
  Pallas kernels  35.5 us (14%)
  local copies, waits for them, and re-layouts  19.7 us (8%)
    ppermute x13, waiting for transfers between devices, passed_along(): return lax.ppermute(array, ('section', 'expert'), pairs)  51.2 us
    ppermute x18, waiting for transfers between devices, swapped(): lax.ppermute(array, 'expert', [(i, i ^ bit) for i in range(lax.axis_size(...  46.8 us
    ppermute x9, waiting for transfers between devices, turned(): lax.ppermute(array, 'expert', [(i, (i + by * GROUP) % length) for i in ra...  36.3 us
    pallas_call x15, Pallas kernels, call(): pl.pallas_call(body, out_shape=shapes, in_specs=specs, out_specs=[pl.Bloc...  35.5 us
    ppermute x13, starting transfers between devices, passed_along(): return lax.ppermute(array, ('section', 'expert'), pairs)  27.4 us
    unnamed x86, local copies, waits for them, and re-layouts  15.5 us
    ppermute x9, starting transfers between devices, turned(): lax.ppermute(array, 'expert', [(i, (i + by * GROUP) % length) for i in ra...  15.2 us
    ppermute x3, starting transfers between devices, shards(): column.append(lax.ppermute(keys_values[0], 'expert', pairs))  10.7 us
  transfers between devices with their start and end apart: 43, of which 20 were waited for; matrix products, arithmetic and copies ran while one was open for 3% of the time, Pallas kernels for 12%

profile of v4, /device:TPU:0, one launch (start us, length us, event | category | flops | bytes accessed | tf_op | source)
XLA Modules:
  0.0 253.7 jit_solution(8866904751129630734)
XLA Ops:
  0.6 1.0 copy.17
  1.6 7.0 %collective-permute-start.2 = (bf16[128,448]{1,0:T(8,128)(2,1)S(1)}, bf16[128,448]{1,0:T(8,128)(2,1)S(1)}, u32[]{:S(2)}, u32[]{:S(2)}) collective-permute-start(bf16[128,448]{1,0:T(8,128)(2,1)S(1)} %bitcast.48), channel_id=1, source_target_pairs={{0,12},{1,13},{2,14},{3,15},{16,28},{17,29},{18,30},{19,31}} | collective-permute-start | bytes 344072 | tf_op jit(solution)/shard_map/ppermute | solution.py:376
  8.6 1.3 collective-permute-start.1
  9.9 2.5 collective-permute-start
  12.4 2.0 slice_bitcast_fusion.1
  14.4 1.5 collective-permute-start.6
  18.0 1.2 copy-done.11
  19.2 1.2 copy-done.13
  20.4 1.7 shard_map.149
  25.3 5.9 %collective-permute-done.6.top_ref = bf16[96,3584]{1,0:T(8,128)(2,1)S(1)} collective-permute-done((bf16[96,3584]{1,0:T(8,128)(2,1)}, bf16[96,3584]{1,0:T(8,128)(2,1)S(1)}, u32[]{:S(2)}, u32[]{:S(2)}) %collective-permute-start.6) | collective-permute-done | bytes 688160 | tf_op jit(solution)/shard_map/ppermute | solution.py:37
  31.2 1.5 collective-permute-start.7
  32.7 1.1 slice_bitcast_fusion
  33.8 9.7 %collective-permute-done.7.kv1 = bf16[512,448]{1,0:T(8,128)(2,1)} collective-permute-done((bf16[512,448]{1,0:T(8,128)(2,1)S(1)}, bf16[512,448]{1,0:T(8,128)(2,1)}, u32[]{:S(2)}, u32[]{:S(2)}) %collective-permute-start.7) | collective-permute-done | bytes 458784 | tf_op jit(solution)/shard_map/ppermute | solution.py:37
  43.5 1.5 collective-permute-start.10
  45.6 3.2 %collective-permute-start.4 = (bf16[144,896]{1,0:T(8,128)(2,1)S(1)}, bf16[144,896]{1,0:T(8,128)(2,1)S(1)}, u32[]{:S(2)}, u32[]{:S(2)}) collective-permute-start(bf16[144,896]{1,0:T(8,128)(2,1)S(1)} %get-tuple-element.103), channel_id=1, source_target_pairs={{0,12},{1,13},{2,14},{3,15},{4,0},{5,1},{6,2},{7,3},{8,4},{9,5},{1... | collective-permute-start | bytes 774152 | tf_op jit(solution)/shard_map/ppermute | solution.py:42
  48.8 6.2 %collective-permute-done.3.refs_1_ = bf16[144,896]{1,0:T(8,128)(2,1)S(1)} collective-permute-done((bf16[144,896]{1,0:T(8,128)(2,1)S(1)}, bf16[144,896]{1,0:T(8,128)(2,1)S(1)}, u32[]{:S(2)}, u32[]{:S(2)}) %collective-permute-start.3) | collective-permute-done | bytes 258080 | tf_op jit(solution)/shard_map/ppermute | solution.py:42
  57.2 1.9 collective-permute-start.5
  59.4 1.2 copy-done.9
  60.5 1.2 copy-done.10
  61.7 9.3 %shard_map.150 = (bf16[128,3584]{1,0:T(8,128)(2,1)}, bf16[144,896]{1,0:T(8,128)(2,1)S(1)}, bf16[144,896]{1,0:T(8,128)(2,1)S(1)}, bf16[144,896]{1,0:T(8,128)(2,1)S(1)}, bf16[144,896]{1,0:T(8,128)(2,1)S(1)}) custom-call(s32[16]{0:T(128)S(1)} %reshape_squeeze.6.chosen_ref, s32[16]{0:T(128)S(1)} %fusion.10.index_ref, s32[1]{0:T(128)} %bitcast.8.base_ref, ...), custom_call_target="tpu_custom_call" | custom-call | flops 1593835520 | bytes 5634692 | tf_op jit(solution)/shard_map/pallas_call | solution.py:55
  71.0 1.3 collective-permute-done.5.refs_2_
  72.4 2.2 shard_map.151.first_ref
  74.7 1.6 collective-permute-start.12
  76.8 20.3 %collective-permute-done.12.middle_ref = bf16[128,3584]{1,0:T(8,128)(2,1)S(1)} collective-permute-done((bf16[128,3584]{1,0:T(8,128)(2,1)S(1)}, bf16[128,3584]{1,0:T(8,128)(2,1)S(1)}, u32[]{:S(2)}, u32[]{:S(2)}) %collective-permute-start.12) | collective-permute-done | bytes 917536 | tf_op jit(solution)/shard_map/ppermute | solution.py:33
  97.1 0.9 copy-done.15
  98.0 1.5 collective-permute-start.13
  99.6 2.6 %collective-permute-start.16 = (bf16[144,896]{1,0:T(8,128)(2,1)S(1)}, bf16[144,896]{1,0:T(8,128)(2,1)S(1)}, u32[]{:S(2)}, u32[]{:S(2)}) collective-permute-start(bf16[144,896]{1,0:T(8,128)(2,1)S(1)} %get-tuple-element.124), channel_id=1, source_target_pairs={{0,8},{1,9},{2,10},{3,11},{4,12},{5,13},{6,14},{7,15},{8,0},{9,1},... | collective-permute-start | bytes 774152 | tf_op jit(solution)/shard_map/ppermute | solution.py:42
  102.2 1.3 collective-permute-start.17
  103.4 7.2 %collective-permute-done.15.refs_1_ = bf16[144,896]{1,0:T(8,128)(2,1)S(1)} collective-permute-done((bf16[144,896]{1,0:T(8,128)(2,1)S(1)}, bf16[144,896]{1,0:T(8,128)(2,1)S(1)}, u32[]{:S(2)}, u32[]{:S(2)}) %collective-permute-start.15) | collective-permute-done | bytes 258080 | tf_op jit(solution)/shard_map/ppermute | solution.py:42
  111.1 8.6 %collective-permute-done.16.refs_2_ = bf16[144,896]{1,0:T(8,128)(2,1)S(1)} collective-permute-done((bf16[144,896]{1,0:T(8,128)(2,1)S(1)}, bf16[144,896]{1,0:T(8,128)(2,1)S(1)}, u32[]{:S(2)}, u32[]{:S(2)}) %collective-permute-start.16) | collective-permute-done | bytes 258080 | tf_op jit(solution)/shard_map/ppermute | solution.py:42
  120.2 3.1 %collective-permute-done.11 = f32[1,256]{1,0:T(1,128)S(1)} collective-permute-done((f32[1,256]{1,0:T(1,128)S(1)}, f32[1,256]{1,0:T(1,128)S(1)}, u32[]{:S(2)}, u32[]{:S(2)}) %collective-permute-start.11) | collective-permute-done | bytes 1056 | tf_op jit(solution)/shard_map/ppermute | solution.py:33
  123.3 2.3 collective-permute-start.29
  125.6 3.4 %collective-permute-start.30 = (bf16[144,896]{1,0:T(8,128)(2,1)S(1)}, bf16[144,896]{1,0:T(8,128)(2,1)S(1)}, u32[]{:S(2)}, u32[]{:S(2)}) collective-permute-start(bf16[144,896]{1,0:T(8,128)(2,1)S(1)} %copy-done.22), channel_id=1, source_target_pairs={{0,8},{1,9},{2,10},{3,11},{4,12},{5,13},{6,14},{7,15},{8,0},{9,1},... | collective-permute-start | bytes 774152 | tf_op jit(solution)/shard_map/ppermute | solution.py:42
  128.9 1.1 shard_map.152.first_ref
  130.1 5.5 %collective-permute-done.29.refs_1_ = bf16[144,896]{1,0:T(8,128)(2,1)S(1)} collective-permute-done((bf16[144,896]{1,0:T(8,128)(2,1)S(1)}, bf16[144,896]{1,0:T(8,128)(2,1)S(1)}, u32[]{:S(2)}, u32[]{:S(2)}) %collective-permute-start.29) | collective-permute-done | bytes 258080 | tf_op jit(solution)/shard_map/ppermute | solution.py:42
  136.1 6.8 %collective-permute-done.30.refs_2_ = bf16[144,896]{1,0:T(8,128)(2,1)S(1)} collective-permute-done((bf16[144,896]{1,0:T(8,128)(2,1)S(1)}, bf16[144,896]{1,0:T(8,128)(2,1)S(1)}, u32[]{:S(2)}, u32[]{:S(2)}) %collective-permute-start.30) | collective-permute-done | bytes 258080 | tf_op jit(solution)/shard_map/ppermute | solution.py:42
  142.9 1.1 shard_map.157.first_ref
  144.7 9.0 %collective-permute-done.20.first_ref = bf16[144,3584]{1,0:T(8,128)(2,1)S(1)} collective-permute-done((bf16[144,3584]{1,0:T(8,128)(2,1)S(1)}, bf16[144,3584]{1,0:T(8,128)(2,1)S(1)}, u32[]{:S(2)}, u32[]{:S(2)}) %collective-permute-start.20) | collective-permute-done | bytes 1032224 | tf_op jit(solution)/shard_map/ppermute | solution.py:37
  153.7 1.3 shard_map.158
  155.8 5.5 %collective-permute-done.36.back_ref = bf16[288,256]{1,0:T(8,128)(2,1)S(1)} collective-permute-done((bf16[288,256]{1,0:T(8,128)(2,1)S(1)}, bf16[288,256]{1,0:T(8,128)(2,1)S(1)}, u32[]{:S(2)}, u32[]{:S(2)}) %collective-permute-start.36) | collective-permute-done | bytes 147488 | tf_op jit(solution)/shard_map/ppermute | solution.py:37
  161.3 2.5 shard_map.160
  163.9 1.3 shard_map.153.own_ref
  165.2 1.3 shard_map.154
  167.1 2.5 shard_map.159
  169.8 2.9 %collective-permute-done.22.other_ref = bf16[288,256]{1,0:T(8,128)(2,1)S(1)} collective-permute-done((bf16[288,256]{1,0:T(8,128)(2,1)S(1)}, bf16[288,256]{1,0:T(8,128)(2,1)S(1)}, u32[]{:S(2)}, u32[]{:S(2)}) %collective-permute-start.22) | collective-permute-done | bytes 147488 | tf_op jit(solution)/shard_map/ppermute | solution.py:37
  172.7 1.2 shard_map.155
  175.4 1.2 collective-permute-done.23.refs_1_
  176.7 1.9 shard_map.156
  179.1 2.7 %collective-permute-start.25 = (bf16[144,896]{1,0:T(8,128)(2,1)}, bf16[144,896]{1,0:T(8,128)(2,1)S(1)}, u32[]{:S(2)}, u32[]{:S(2)}) collective-permute-start(bf16[144,896]{1,0:T(8,128)(2,1)} %get-tuple-element.138), channel_id=1, source_target_pairs={{0,28},{1,29},{2,30},{3,31},{4,16},{5,17},{6,18},{7,19},{8,20},{9,... | collective-permute-start | bytes 774152 | tf_op jit(solution)/shard_map/ppermute | solution.py:33
  181.8 1.0 copy-done.7
  182.8 4.4 %collective-permute-start.26 = (bf16[144,896]{1,0:T(8,128)(2,1)}, bf16[144,896]{1,0:T(8,128)(2,1)S(1)}, u32[]{:S(2)}, u32[]{:S(2)}) collective-permute-start(bf16[144,896]{1,0:T(8,128)(2,1)} %get-tuple-element.139), channel_id=1, source_target_pairs={{0,24},{1,25},{2,26},{3,27},{4,28},{5,29},{6,30},{7,31},{8,16},{9,... | collective-permute-start | bytes 774152 | tf_op jit(solution)/shard_map/ppermute | solution.py:33
  187.2 12.4 %collective-permute-done.38.refs_2_ = bf16[144,3584]{1,0:T(8,128)(2,1)S(1)} collective-permute-done((bf16[144,3584]{1,0:T(8,128)(2,1)S(1)}, bf16[144,3584]{1,0:T(8,128)(2,1)S(1)}, u32[]{:S(2)}, u32[]{:S(2)}) %collective-permute-start.38) | collective-permute-done | bytes 1032224 | tf_op jit(solution)/shard_map/ppermute | solution.py:37
  199.6 4.7 %collective-permute-start.27 = (bf16[144,896]{1,0:T(8,128)(2,1)S(1)}, bf16[144,896]{1,0:T(8,128)(2,1)S(1)}, u32[]{:S(2)}, u32[]{:S(2)}) collective-permute-start(bf16[144,896]{1,0:T(8,128)(2,1)S(1)} %get-tuple-element.140), channel_id=1, source_target_pairs={{0,20},{1,21},{2,22},{3,23},{4,24},{5,25},{6,26},{7,27},{8,28},{9,... | collective-permute-start | bytes 774152 | tf_op jit(solution)/shard_map/ppermute | solution.py:33
  204.5 1.2 copy-done.8
  205.7 1.2 copy-done.31
  206.9 2.1 shard_map.161
  209.0 10.7 %collective-permute-done.24.refs_0_ = bf16[144,896]{1,0:T(8,128)(2,1)S(1)} collective-permute-done((bf16[144,896]{1,0:T(8,128)(2,1)}, bf16[144,896]{1,0:T(8,128)(2,1)S(1)}, u32[]{:S(2)}, u32[]{:S(2)}) %collective-permute-start.24) | collective-permute-done | bytes 258080 | tf_op jit(solution)/shard_map/ppermute | solution.py:33
  220.2 2.7 %collective-permute-start.40 = (bf16[144,896]{1,0:T(8,128)(2,1)}, bf16[144,896]{1,0:T(8,128)(2,1)}, u32[]{:S(2)}, u32[]{:S(2)}) collective-permute-start(bf16[144,896]{1,0:T(8,128)(2,1)} %get-tuple-element.163), channel_id=1, source_target_pairs={{0,28},{1,29},{2,30},{3,31},{4,16},{5,17},{6,18},{7,19},{8,20},{9,... | collective-permute-start | bytes 774152 | tf_op jit(solution)/shard_map/ppermute | solution.py:33
  223.0 4.5 %collective-permute-start.41 = (bf16[144,896]{1,0:T(8,128)(2,1)}, bf16[144,896]{1,0:T(8,128)(2,1)}, u32[]{:S(2)}, u32[]{:S(2)}) collective-permute-start(bf16[144,896]{1,0:T(8,128)(2,1)} %get-tuple-element.164), channel_id=1, source_target_pairs={{0,24},{1,25},{2,26},{3,27},{4,28},{5,29},{6,30},{7,31},{8,16},{9,... | collective-permute-start | bytes 774152 | tf_op jit(solution)/shard_map/ppermute | solution.py:33
  227.5 2.9 %collective-permute-start.42 = (bf16[144,896]{1,0:T(8,128)(2,1)}, bf16[144,896]{1,0:T(8,128)(2,1)S(1)}, u32[]{:S(2)}, u32[]{:S(2)}) collective-permute-start(bf16[144,896]{1,0:T(8,128)(2,1)} %get-tuple-element.165), channel_id=1, source_target_pairs={{0,20},{1,21},{2,22},{3,23},{4,24},{5,25},{6,26},{7,27},{8,28},{9,... | collective-permute-start | bytes 774152 | tf_op jit(solution)/shard_map/ppermute | solution.py:33
  230.5 2.3 shard_map.162
  232.7 1.7 collective-permute-done.39.refs_0_
  234.4 15.4 %collective-permute-done.41.refs_2_ = bf16[144,896]{1,0:T(8,128)(2,1)} collective-permute-done((bf16[144,896]{1,0:T(8,128)(2,1)}, bf16[144,896]{1,0:T(8,128)(2,1)}, u32[]{:S(2)}, u32[]{:S(2)}) %collective-permute-start.41) | collective-permute-done | bytes 258080 | tf_op jit(solution)/shard_map/ppermute | solution.py:33
  249.8 3.9 %shard_map.163 = bf16[128,3584]{1,0:T(8,128)(2,1)} custom-call(s32[128,1]{1,0:T(8,128)S(1)} %copy.20.route_ref, f32[1,3584]{1,0:T(1,128)S(1)} %slice.35.gain_ref, bf16[128,3584]{1,0:T(8,128)(2,1)S(1)} %copy-done.16, bf16[128,3584]{1,0:T(8,128)(2,1)S(1)} %copy-done.18, bf16[144,896]{1,0:T(8,128)(2,1)} %collective-permute-done.39.refs_0_, ...), custom_call_target="tpu_custom_call" | custom-call | flops 1056964608 | bytes 3799552 | tf_op jit(solution)/shard_map/pallas_call | solution.py:55
  (141 shorter events, 15.8 us)
Async XLA Ops:
  1.6 20.5 %collective-permute-start.2 = (bf16[128,448]{1,0:T(8,128)(2,1)S(1)}, bf16[128,448]{1,0:T(8,128)(2,1)S(1)}, u32[]{:S(2)}, u32[]{:S(2)}) collective-permute-start(bf16[128,448]{1,0:T(8,128)(2,1)S(1)} %bitcast.48), channel_id=1, source_target_pairs={{0,12},{1,13},{2,14},{3,15},{16,28},{17,29},{18,30},{19,31}} | collective-permute-start | bytes 344072 | tf_op jit(solution)/shard_map/ppermute | solution.py:376
  8.6 13.6 %collective-permute-start.1 = (bf16[128,448]{1,0:T(8,128)(2,1)S(1)}, bf16[128,448]{1,0:T(8,128)(2,1)S(1)}, u32[]{:S(2)}, u32[]{:S(2)}) collective-permute-start(bf16[128,448]{1,0:T(8,128)(2,1)S(1)} %bitcast.49), channel_id=1, source_target_pairs={{0,8},{1,9},{2,10},{3,11},{4,12},{5,13},{6,14},{7,15},{16,24},{17,... | collective-permute-start | bytes 344072 | tf_op jit(solution)/shard_map/ppermute | solution.py:376
  9.9 12.3 %collective-permute-start = (bf16[128,448]{1,0:T(8,128)(2,1)S(1)}, bf16[128,448]{1,0:T(8,128)(2,1)S(1)}, u32[]{:S(2)}, u32[]{:S(2)}) collective-permute-start(bf16[128,448]{1,0:T(8,128)(2,1)S(1)} %bitcast.50), channel_id=1, source_target_pairs={{0,4},{1,5},{2,6},{3,7},{4,8},{5,9},{6,10},{7,11},{8,12},{9,13},{1... | collective-permute-start | bytes 344072 | tf_op jit(solution)/shard_map/ppermute | solution.py:376
  14.4 16.8 %collective-permute-start.6 = (bf16[96,3584]{1,0:T(8,128)(2,1)}, bf16[96,3584]{1,0:T(8,128)(2,1)S(1)}, u32[]{:S(2)}, u32[]{:S(2)}) collective-permute-start(bf16[96,3584]{1,0:T(8,128)(2,1)} %slice_bitcast_fusion.1), channel_id=1, source_target_pairs={{0,2},{1,3},{2,0},{3,1},{4,6},{5,7},{6,4},{7,5},{8,10},{9,11},{10,... | collective-permute-start | bytes 2064392 | tf_op jit(solution)/shard_map/ppermute | solution.py:37
  20.4 12.3 %copy-start = (bf16[1,1,256,3584]{3,2,1,0:T(8,128)(2,1)S(1)}, bf16[1,1,256,3584]{3,2,1,0:T(8,128)(2,1)}, u32[]{:S(2)}) copy-start(bf16[1,1,256,3584]{3,2,1,0:T(8,128)(2,1)} %param.27) | copy-start | bytes 5505028
  22.1 23.5 %copy-start.19 = (bf16[144,896]{1,0:T(8,128)(2,1)}, bf16[144,896]{1,0:T(8,128)(2,1)S(1)}, u32[]{:S(2)}) copy-start(bf16[144,896]{1,0:T(8,128)(2,1)S(1)} %get-tuple-element.148) | copy-start | bytes 774148
  22.1 26.7 %copy-start.21 = (bf16[144,896]{1,0:T(8,128)(2,1)}, bf16[144,896]{1,0:T(8,128)(2,1)S(1)}, u32[]{:S(2)}) copy-start(bf16[144,896]{1,0:T(8,128)(2,1)S(1)} %get-tuple-element.147) | copy-start | bytes 774148
  22.1 26.7 %copy-start.23 = (bf16[144,896]{1,0:T(8,128)(2,1)}, bf16[144,896]{1,0:T(8,128)(2,1)S(1)}, u32[]{:S(2)}) copy-start(bf16[144,896]{1,0:T(8,128)(2,1)S(1)} %get-tuple-element.146) | copy-start | bytes 774148
  22.1 32.9 %copy-start.25 = (bf16[144,896]{1,0:T(8,128)(2,1)}, bf16[144,896]{1,0:T(8,128)(2,1)S(1)}, u32[]{:S(2)}) copy-start(bf16[144,896]{1,0:T(8,128)(2,1)S(1)} %get-tuple-element.104) | copy-start | bytes 774148
  22.1 34.3 %copy-start.32 = (bf16[144,896]{1,0:T(8,128)(2,1)}, bf16[144,896]{1,0:T(8,128)(2,1)S(1)}, u32[]{:S(2)}) copy-start(bf16[144,896]{1,0:T(8,128)(2,1)S(1)} %get-tuple-element.149.refs_0_) | copy-start | bytes 774148
  22.1 34.3 %copy-start.34 = (bf16[144,896]{1,0:T(8,128)(2,1)}, bf16[144,896]{1,0:T(8,128)(2,1)S(1)}, u32[]{:S(2)}) copy-start(bf16[144,896]{1,0:T(8,128)(2,1)S(1)} %get-tuple-element.108.refs_0_) | copy-start | bytes 774148
  22.1 35.0 %copy-start.38 = (s32[1,2,2,4]{3,2,1,0:T(2,128)S(1)}, s32[1,2,2,4]{3,2,1,0:T(2,128)}, u32[]{:S(2)}) copy-start(s32[1,2,2,4]{3,2,1,0:T(2,128)} %param.17) | copy-start | bytes 196
  22.1 35.1 %copy-start.40 = (s32[1,128,1]{1,2,0:T(1,128)S(1)}, s32[1,128,1]{1,2,0:T(1,128)}, u32[]{:S(2)}) copy-start(s32[1,128,1]{1,2,0:T(1,128)} %param.18) | copy-start | bytes 1540
  22.1 37.2 %copy-start.6 = (f32[1,3584]{1,0:T(1,128)S(1)}, f32[1,3584]{1,0:T(1,128)}, u32[]{:S(2)}) copy-start(f32[1,3584]{1,0:T(1,128)} %gain_ref.3) | copy-start | bytes 43012
  31.2 12.3 %collective-permute-start.7 = (bf16[512,448]{1,0:T(8,128)(2,1)S(1)}, bf16[512,448]{1,0:T(8,128)(2,1)}, u32[]{:S(2)}, u32[]{:S(2)}) collective-permute-start(bf16[512,448]{1,0:T(8,128)(2,1)S(1)} %constant_dynamic-update-slice_fusion.kv0), channel_id=1, source_target_pairs={{0,2},{1,3},{2,0},{3,1},{4,6},{5,7},{6,4},{7,5},{8,10},{9,11},{10,... | collective-permute-start | bytes 1376264 | tf_op jit(solution)/shard_map/ppermute | solution.py:37
  43.5 31.1 %collective-permute-start.10 = (bf16[160,3584]{1,0:T(8,128)(2,1)}, bf16[160,3584]{1,0:T(8,128)(2,1)S(1)}, u32[]{:S(2)}, u32[]{:S(2)}) collective-permute-start(bf16[160,3584]{1,0:T(8,128)(2,1)} %slice_bitcast_fusion), channel_id=1, source_target_pairs={{0,2},{1,3},{2,0},{3,1},{4,6},{5,7},{6,4},{7,5},{8,10},{9,11},{10,... | collective-permute-start | bytes 3440648 | tf_op jit(solution)/shard_map/ppermute | solution.py:37
  45.0 10.0 %collective-permute-start.3 = (bf16[144,896]{1,0:T(8,128)(2,1)S(1)}, bf16[144,896]{1,0:T(8,128)(2,1)S(1)}, u32[]{:S(2)}, u32[]{:S(2)}) collective-permute-start(bf16[144,896]{1,0:T(8,128)(2,1)S(1)} %get-tuple-element.101), channel_id=1, source_target_pairs={{0,4},{1,5},{2,6},{3,7},{4,8},{5,9},{6,10},{7,11},{8,12},{9,13},{1... | collective-permute-start | bytes 774152 | tf_op jit(solution)/shard_map/ppermute | solution.py:42
  45.6 10.8 %collective-permute-start.4 = (bf16[144,896]{1,0:T(8,128)(2,1)S(1)}, bf16[144,896]{1,0:T(8,128)(2,1)S(1)}, u32[]{:S(2)}, u32[]{:S(2)}) collective-permute-start(bf16[144,896]{1,0:T(8,128)(2,1)S(1)} %get-tuple-element.103), channel_id=1, source_target_pairs={{0,12},{1,13},{2,14},{3,15},{4,0},{5,1},{6,2},{7,3},{8,4},{9,5},{1... | collective-permute-start | bytes 774152 | tf_op jit(solution)/shard_map/ppermute | solution.py:42
  48.8 10.3 %collective-permute-start.8 = (bf16[512,448]{1,0:T(8,128)(2,1)S(1)}, bf16[512,448]{1,0:T(8,128)(2,1)}, u32[]{:S(2)}, u32[]{:S(2)}) collective-permute-start(bf16[512,448]{1,0:T(8,128)(2,1)S(1)} %constant_dynamic-update-slice_fusion.kv0), channel_id=1, source_target_pairs={{0,1},{1,0},{2,3},{3,2},{4,5},{5,4},{6,7},{7,6},{8,9},{9,8},{10,11... | collective-permute-start | bytes 1376264 | tf_op jit(solution)/shard_map/ppermute | solution.py:37
  57.1 2.3 collective-permute-start.9
  57.2 15.2 %collective-permute-start.5 = (bf16[144,896]{1,0:T(8,128)(2,1)}, bf16[144,896]{1,0:T(8,128)(2,1)}, u32[]{:S(2)}, u32[]{:S(2)}) collective-permute-start(bf16[144,896]{1,0:T(8,128)(2,1)} %copy-done.25), channel_id=1, source_target_pairs={{0,8},{1,9},{2,10},{3,11},{4,12},{5,13},{6,14},{7,15},{8,0},{9,1},... | collective-permute-start | bytes 774152 | tf_op jit(solution)/shard_map/ppermute | solution.py:42
  61.7 10.6 %copy-start.29 = (bf16[144,896]{1,0:T(8,128)(2,1)S(1)}, bf16[144,896]{1,0:T(8,128)(2,1)}, u32[]{:S(2)}) copy-start(bf16[144,896]{1,0:T(8,128)(2,1)} %copy-done.28) | copy-start | bytes 774148
  61.7 10.6 %copy-start.35 = (bf16[144,896]{1,0:T(8,128)(2,1)S(1)}, bf16[144,896]{1,0:T(8,128)(2,1)}, u32[]{:S(2)}) copy-start(bf16[144,896]{1,0:T(8,128)(2,1)} %copy-done.34) | copy-start | bytes 774148
  72.4 25.6 %copy-start.14 = (bf16[1,128,3584]{2,1,0:T(8,128)(2,1)S(1)}, bf16[1,128,3584]{2,1,0:T(8,128)(2,1)}, u32[]{:S(2)}) copy-start(bf16[1,128,3584]{2,1,0:T(8,128)(2,1)} %param.21) | copy-start | bytes 2752516
  72.4 31.0 %copy-start.39 = (f32[1,128,1]{1,2,0:T(1,128)S(1)}, f32[1,128,1]{1,2,0:T(1,128)}, u32[]{:S(2)}) copy-start(f32[1,128,1]{1,2,0:T(1,128)} %param.19) | copy-start | bytes 1540
  72.4 50.9 %copy-start.24 = (bf16[144,896]{1,0:T(8,128)(2,1)S(1)}, bf16[144,896]{1,0:T(8,128)(2,1)}, u32[]{:S(2)}) copy-start(bf16[144,896]{1,0:T(8,128)(2,1)} %copy-done.23) | copy-start | bytes 774148
  72.4 53.1 %copy-start.22 = (bf16[144,896]{1,0:T(8,128)(2,1)S(1)}, bf16[144,896]{1,0:T(8,128)(2,1)}, u32[]{:S(2)}) copy-start(bf16[144,896]{1,0:T(8,128)(2,1)} %copy-done.21) | copy-start | bytes 774148
  72.4 56.5 %copy-start.20 = (bf16[144,896]{1,0:T(8,128)(2,1)S(1)}, bf16[144,896]{1,0:T(8,128)(2,1)}, u32[]{:S(2)}) copy-start(bf16[144,896]{1,0:T(8,128)(2,1)} %copy-done.19) | copy-start | bytes 774148
  74.7 22.4 %collective-permute-start.12 = (bf16[128,3584]{1,0:T(8,128)(2,1)S(1)}, bf16[128,3584]{1,0:T(8,128)(2,1)S(1)}, u32[]{:S(2)}, u32[]{:S(2)}) collective-permute-start(bf16[128,3584]{1,0:T(8,128)(2,1)S(1)} %bitcast.45), channel_id=1, source_target_pairs={{0,16},{1,17},{2,18},{3,19},{4,20},{5,21},{6,22},{7,23},{8,24},{9,... | collective-permute-start | bytes 2752520 | tf_op jit(solution)/shard_map/ppermute | solution.py:33
  76.2 67.9 %collective-permute-start.34 = (bf16[144,3584]{1,0:T(8,128)(2,1)S(1)}, bf16[144,3584]{1,0:T(8,128)(2,1)S(1)}, u32[]{:S(2)}, u32[]{:S(2)}) collective-permute-start(bf16[144,3584]{1,0:T(8,128)(2,1)S(1)} %shard_map.151.first_ref), channel_id=1, source_target_pairs={{0,2},{1,3},{2,0},{3,1},{4,6},{5,7},{6,4},{7,5},{8,10},{9,11},{10,... | collective-permute-start | bytes 3096584 | tf_op jit(solution)/shard_map/ppermute | solution.py:37
  98.0 44.9 %collective-permute-start.13 = (bf16[128,3584]{1,0:T(8,128)(2,1)S(1)}, bf16[128,3584]{1,0:T(8,128)(2,1)S(1)}, u32[]{:S(2)}, u32[]{:S(2)}) collective-permute-start(bf16[128,3584]{1,0:T(8,128)(2,1)S(1)} %bitcast.47), channel_id=1, source_target_pairs={{0,16},{1,17},{2,18},{3,19},{4,20},{5,21},{6,22},{7,23},{8,24},{9,... | collective-permute-start | bytes 2752520 | tf_op jit(solution)/shard_map/ppermute | solution.py:33
  99.5 11.1 %collective-permute-start.15 = (bf16[144,896]{1,0:T(8,128)(2,1)S(1)}, bf16[144,896]{1,0:T(8,128)(2,1)S(1)}, u32[]{:S(2)}, u32[]{:S(2)}) collective-permute-start(bf16[144,896]{1,0:T(8,128)(2,1)S(1)} %get-tuple-element.123), channel_id=1, source_target_pairs={{0,4},{1,5},{2,6},{3,7},{4,8},{5,9},{6,10},{7,11},{8,12},{9,13},{1... | collective-permute-start | bytes 774152 | tf_op jit(solution)/shard_map/ppermute | solution.py:42
  99.6 20.1 %collective-permute-start.16 = (bf16[144,896]{1,0:T(8,128)(2,1)S(1)}, bf16[144,896]{1,0:T(8,128)(2,1)S(1)}, u32[]{:S(2)}, u32[]{:S(2)}) collective-permute-start(bf16[144,896]{1,0:T(8,128)(2,1)S(1)} %get-tuple-element.124), channel_id=1, source_target_pairs={{0,8},{1,9},{2,10},{3,11},{4,12},{5,13},{6,14},{7,15},{8,0},{9,1},... | collective-permute-start | bytes 774152 | tf_op jit(solution)/shard_map/ppermute | solution.py:42
  102.2 18.1 %collective-permute-start.17 = (bf16[144,896]{1,0:T(8,128)(2,1)S(1)}, bf16[144,896]{1,0:T(8,128)(2,1)S(1)}, u32[]{:S(2)}, u32[]{:S(2)}) collective-permute-start(bf16[144,896]{1,0:T(8,128)(2,1)S(1)} %get-tuple-element.125), channel_id=1, source_target_pairs={{0,12},{1,13},{2,14},{3,15},{4,0},{5,1},{6,2},{7,3},{8,4},{9,5},{1... | collective-permute-start | bytes 774152 | tf_op jit(solution)/shard_map/ppermute | solution.py:42
  103.4 39.5 %copy-start.33 = (bf16[144,896]{1,0:T(8,128)(2,1)S(1)}, bf16[144,896]{1,0:T(8,128)(2,1)}, u32[]{:S(2)}) copy-start(bf16[144,896]{1,0:T(8,128)(2,1)} %copy-done.32) | copy-start | bytes 774148
  110.6 12.7 %collective-permute-start.18 = (f32[1,3712]{1,0:T(1,128)S(1)}, f32[1,3712]{1,0:T(1,128)S(1)}, u32[]{:S(2)}, u32[]{:S(2)}) collective-permute-start(f32[1,3712]{1,0:T(1,128)S(1)} %pad_maximum_fusion), channel_id=1, source_target_pairs={{0,16},{1,17},{2,18},{3,19},{4,20},{5,21},{6,22},{7,23},{8,24},{9,... | collective-permute-start | bytes 44552 | tf_op jit(solution)/shard_map/ppermute | solution.py:33
  119.7 3.6 %collective-permute-start.11 = (f32[1,256]{1,0:T(1,128)S(1)}, f32[1,256]{1,0:T(1,128)S(1)}, u32[]{:S(2)}, u32[]{:S(2)}) collective-permute-start(f32[1,256]{1,0:T(1,128)S(1)} %maximum_bitcast_fusion), channel_id=1, source_target_pairs={{0,16},{1,17},{2,18},{3,19},{4,20},{5,21},{6,22},{7,23},{8,24},{9,... | collective-permute-start | bytes 3080 | tf_op jit(solution)/shard_map/ppermute | solution.py:33
  123.3 12.3 %collective-permute-start.29 = (bf16[144,896]{1,0:T(8,128)(2,1)S(1)}, bf16[144,896]{1,0:T(8,128)(2,1)S(1)}, u32[]{:S(2)}, u32[]{:S(2)}) collective-permute-start(bf16[144,896]{1,0:T(8,128)(2,1)S(1)} %copy-done.24), channel_id=1, source_target_pairs={{0,4},{1,5},{2,6},{3,7},{4,8},{5,9},{6,10},{7,11},{8,12},{9,13},{1... | collective-permute-start | bytes 774152 | tf_op jit(solution)/shard_map/ppermute | solution.py:42
  125.6 17.3 %collective-permute-start.30 = (bf16[144,896]{1,0:T(8,128)(2,1)S(1)}, bf16[144,896]{1,0:T(8,128)(2,1)S(1)}, u32[]{:S(2)}, u32[]{:S(2)}) collective-permute-start(bf16[144,896]{1,0:T(8,128)(2,1)S(1)} %copy-done.22), channel_id=1, source_target_pairs={{0,8},{1,9},{2,10},{3,11},{4,12},{5,13},{6,14},{7,15},{8,0},{9,1},... | collective-permute-start | bytes 774152 | tf_op jit(solution)/shard_map/ppermute | solution.py:42
  128.9 14.0 %collective-permute-start.31 = (bf16[144,896]{1,0:T(8,128)(2,1)S(1)}, bf16[144,896]{1,0:T(8,128)(2,1)S(1)}, u32[]{:S(2)}, u32[]{:S(2)}) collective-permute-start(bf16[144,896]{1,0:T(8,128)(2,1)S(1)} %copy-done.20), channel_id=1, source_target_pairs={{0,12},{1,13},{2,14},{3,15},{4,0},{5,1},{6,2},{7,3},{8,4},{9,5},{1... | collective-permute-start | bytes 774152 | tf_op jit(solution)/shard_map/ppermute | solution.py:42
  130.0 23.6 %copy-start.4 = (bf16[96,3584]{1,0:T(8,128)(2,1)S(1)}, bf16[96,3584]{1,0:T(8,128)(2,1)}, u32[]{:S(2)}) copy-start(bf16[96,3584]{1,0:T(8,128)(2,1)} %copy-done.3) | copy-start | bytes 2064388
  135.6 18.1 %collective-permute-start.20 = (bf16[144,3584]{1,0:T(8,128)(2,1)S(1)}, bf16[144,3584]{1,0:T(8,128)(2,1)S(1)}, u32[]{:S(2)}, u32[]{:S(2)}) collective-permute-start(bf16[144,3584]{1,0:T(8,128)(2,1)S(1)} %shard_map.152.first_ref), channel_id=1, source_target_pairs={{0,2},{1,3},{2,0},{3,1},{4,6},{5,7},{6,4},{7,5},{8,10},{9,11},{10,... | collective-permute-start | bytes 3096584 | tf_op jit(solution)/shard_map/ppermute | solution.py:37
  144.0 9.7 %collective-permute-start.32 = (bf16[144,3584]{1,0:T(8,128)(2,1)S(1)}, bf16[144,3584]{1,0:T(8,128)(2,1)S(1)}, u32[]{:S(2)}, u32[]{:S(2)}) collective-permute-start(bf16[144,3584]{1,0:T(8,128)(2,1)S(1)} %shard_map.157.first_ref), channel_id=1, source_target_pairs={{0,1},{1,0},{2,3},{3,2},{4,5},{5,4},{6,7},{7,6},{8,9},{9,8},{10,11... | collective-permute-start | bytes 3096584 | tf_op jit(solution)/shard_map/ppermute | solution.py:37
  144.1 11.7 %collective-permute-start.35 = (bf16[144,3584]{1,0:T(8,128)(2,1)S(1)}, bf16[144,3584]{1,0:T(8,128)(2,1)S(1)}, u32[]{:S(2)}, u32[]{:S(2)}) collective-permute-start(bf16[144,3584]{1,0:T(8,128)(2,1)S(1)} %collective-permute-done.34.first_ref), channel_id=1, source_target_pairs={{0,1},{1,0},{2,3},{3,2},{4,5},{5,4},{6,7},{7,6},{8,9},{9,8},{10,11... | collective-permute-start | bytes 3096584 | tf_op jit(solution)/shard_map/ppermute | solution.py:37
  144.6 19.3 %collective-permute-start.19 = (bf16[144,3584]{1,0:T(8,128)(2,1)S(1)}, bf16[144,3584]{1,0:T(8,128)(2,1)S(1)}, u32[]{:S(2)}, u32[]{:S(2)}) collective-permute-start(bf16[144,3584]{1,0:T(8,128)(2,1)S(1)} %shard_map.152.first_ref), channel_id=1, source_target_pairs={{0,1},{1,0},{2,3},{3,2},{4,5},{5,4},{6,7},{7,6},{8,9},{9,8},{10,11... | collective-permute-start | bytes 3096584 | tf_op jit(solution)/shard_map/ppermute | solution.py:37
  153.7 11.5 %collective-permute-start.21 = (bf16[144,3584]{1,0:T(8,128)(2,1)S(1)}, bf16[144,3584]{1,0:T(8,128)(2,1)S(1)}, u32[]{:S(2)}, u32[]{:S(2)}) collective-permute-start(bf16[144,3584]{1,0:T(8,128)(2,1)S(1)} %collective-permute-done.20.first_ref), channel_id=1, source_target_pairs={{0,1},{1,0},{2,3},{3,2},{4,5},{5,4},{6,7},{7,6},{8,9},{9,8},{10,11... | collective-permute-start | bytes 3096584 | tf_op jit(solution)/shard_map/ppermute | solution.py:37
  155.0 6.3 %collective-permute-start.36 = (bf16[288,256]{1,0:T(8,128)(2,1)S(1)}, bf16[288,256]{1,0:T(8,128)(2,1)S(1)}, u32[]{:S(2)}, u32[]{:S(2)}) collective-permute-start(bf16[288,256]{1,0:T(8,128)(2,1)S(1)} %get-tuple-element.156), channel_id=1, source_target_pairs={{0,2},{1,3},{2,0},{3,1},{4,6},{5,7},{6,4},{7,5},{8,10},{9,11},{10,... | collective-permute-start | bytes 442376 | tf_op jit(solution)/shard_map/ppermute | solution.py:37
  155.6 11.4 %collective-permute-start.28 = (bf16[144,3584]{1,0:T(8,128)(2,1)S(1)}, bf16[144,3584]{1,0:T(8,128)(2,1)S(1)}, u32[]{:S(2)}, u32[]{:S(2)}) collective-permute-start(bf16[144,3584]{1,0:T(8,128)(2,1)S(1)} %shard_map.151.first_ref), channel_id=1, source_target_pairs={{0,1},{1,0},{2,3},{3,2},{4,5},{5,4},{6,7},{7,6},{8,9},{9,8},{10,11... | collective-permute-start | bytes 3096584 | tf_op jit(solution)/shard_map/ppermute | solution.py:37
  163.8 10.3 %collective-permute-start.37 = (bf16[144,3584]{1,0:T(8,128)(2,1)S(1)}, bf16[144,3584]{1,0:T(8,128)(2,1)S(1)}, u32[]{:S(2)}, u32[]{:S(2)}) collective-permute-start(bf16[144,3584]{1,0:T(8,128)(2,1)S(1)} %get-tuple-element.158), channel_id=1, source_target_pairs={{0,1},{1,0},{2,3},{3,2},{4,5},{5,4},{6,7},{7,6},{8,9},{9,8},{10,11... | collective-permute-start | bytes 3096584 | tf_op jit(solution)/shard_map/ppermute | solution.py:37
  166.4 6.3 %collective-permute-start.22 = (bf16[288,256]{1,0:T(8,128)(2,1)S(1)}, bf16[288,256]{1,0:T(8,128)(2,1)S(1)}, u32[]{:S(2)}, u32[]{:S(2)}) collective-permute-start(bf16[288,256]{1,0:T(8,128)(2,1)S(1)} %shard_map.154), channel_id=1, source_target_pairs={{0,2},{1,3},{2,0},{3,1},{4,6},{5,7},{6,4},{7,5},{8,10},{9,11},{10,... | collective-permute-start | bytes 442376 | tf_op jit(solution)/shard_map/ppermute | solution.py:37
  169.5 12.2 %collective-permute-start.33 = (bf16[144,3584]{1,0:T(8,128)(2,1)S(1)}, bf16[144,3584]{1,0:T(8,128)(2,1)S(1)}, u32[]{:S(2)}, u32[]{:S(2)}) collective-permute-start(bf16[144,3584]{1,0:T(8,128)(2,1)S(1)} %get-tuple-element.155), channel_id=1, source_target_pairs={{0,1},{1,0},{2,3},{3,2},{4,5},{5,4},{6,7},{7,6},{8,9},{9,8},{10,11... | collective-permute-start | bytes 3096584 | tf_op jit(solution)/shard_map/ppermute | solution.py:37
  174.0 2.7 %collective-permute-start.23 = (bf16[144,3584]{1,0:T(8,128)(2,1)S(1)}, bf16[144,3584]{1,0:T(8,128)(2,1)S(1)}, u32[]{:S(2)}, u32[]{:S(2)}) collective-permute-start(bf16[144,3584]{1,0:T(8,128)(2,1)S(1)} %get-tuple-element.136), channel_id=1, source_target_pairs={{0,1},{1,0},{2,3},{3,2},{4,5},{5,4},{6,7},{7,6},{8,9},{9,8},{10,11... | collective-permute-start | bytes 3096584 | tf_op jit(solution)/shard_map/ppermute | solution.py:37
  174.4 25.3 %collective-permute-start.38 = (bf16[144,3584]{1,0:T(8,128)(2,1)S(1)}, bf16[144,3584]{1,0:T(8,128)(2,1)S(1)}, u32[]{:S(2)}, u32[]{:S(2)}) collective-permute-start(bf16[144,3584]{1,0:T(8,128)(2,1)S(1)} %add_convert_fusion), channel_id=1, source_target_pairs={{0,2},{1,3},{2,0},{3,1},{4,6},{5,7},{6,4},{7,5},{8,10},{9,11},{10,... | collective-permute-start | bytes 3096584 | tf_op jit(solution)/shard_map/ppermute | solution.py:37
  175.0 55.5 %collective-permute-start.14 = (bf16[128,3584]{1,0:T(8,128)(2,1)}, bf16[128,3584]{1,0:T(8,128)(2,1)S(1)}, u32[]{:S(2)}, u32[]{:S(2)}) collective-permute-start(bf16[128,3584]{1,0:T(8,128)(2,1)} %get-tuple-element.117), channel_id=1, source_target_pairs={{0,16},{1,17},{2,18},{3,19},{4,20},{5,21},{6,22},{7,23},{8,24},{9,... | collective-permute-start | bytes 2752520 | tf_op jit(solution)/shard_map/ppermute | solution.py:33
  178.6 41.2 %collective-permute-start.24 = (bf16[144,896]{1,0:T(8,128)(2,1)}, bf16[144,896]{1,0:T(8,128)(2,1)S(1)}, u32[]{:S(2)}, u32[]{:S(2)}) collective-permute-start(bf16[144,896]{1,0:T(8,128)(2,1)} %get-tuple-element.137), channel_id=1, source_target_pairs={{0,16},{1,17},{2,18},{3,19},{4,20},{5,21},{6,22},{7,23},{8,24},{9,... | collective-permute-start | bytes 774152 | tf_op jit(solution)/shard_map/ppermute | solution.py:33
  179.1 41.1 %collective-permute-start.25 = (bf16[144,896]{1,0:T(8,128)(2,1)}, bf16[144,896]{1,0:T(8,128)(2,1)S(1)}, u32[]{:S(2)}, u32[]{:S(2)}) collective-permute-start(bf16[144,896]{1,0:T(8,128)(2,1)} %get-tuple-element.138), channel_id=1, source_target_pairs={{0,28},{1,29},{2,30},{3,31},{4,16},{5,17},{6,18},{7,19},{8,20},{9,... | collective-permute-start | bytes 774152 | tf_op jit(solution)/shard_map/ppermute | solution.py:33
  182.8 40.2 %collective-permute-start.26 = (bf16[144,896]{1,0:T(8,128)(2,1)}, bf16[144,896]{1,0:T(8,128)(2,1)S(1)}, u32[]{:S(2)}, u32[]{:S(2)}) collective-permute-start(bf16[144,896]{1,0:T(8,128)(2,1)} %get-tuple-element.139), channel_id=1, source_target_pairs={{0,24},{1,25},{2,26},{3,27},{4,28},{5,29},{6,30},{7,31},{8,16},{9,... | collective-permute-start | bytes 774152 | tf_op jit(solution)/shard_map/ppermute | solution.py:33
  199.6 27.8 %collective-permute-start.27 = (bf16[144,896]{1,0:T(8,128)(2,1)S(1)}, bf16[144,896]{1,0:T(8,128)(2,1)S(1)}, u32[]{:S(2)}, u32[]{:S(2)}) collective-permute-start(bf16[144,896]{1,0:T(8,128)(2,1)S(1)} %get-tuple-element.140), channel_id=1, source_target_pairs={{0,20},{1,21},{2,22},{3,23},{4,24},{5,25},{6,26},{7,27},{8,28},{9,... | collective-permute-start | bytes 774152 | tf_op jit(solution)/shard_map/ppermute | solution.py:33
  219.8 14.7 %collective-permute-start.39 = (bf16[144,896]{1,0:T(8,128)(2,1)}, bf16[144,896]{1,0:T(8,128)(2,1)}, u32[]{:S(2)}, u32[]{:S(2)}) collective-permute-start(bf16[144,896]{1,0:T(8,128)(2,1)} %get-tuple-element.162), channel_id=1, source_target_pairs={{0,16},{1,17},{2,18},{3,19},{4,20},{5,21},{6,22},{7,23},{8,24},{9,... | collective-permute-start | bytes 774152 | tf_op jit(solution)/shard_map/ppermute | solution.py:33
  220.2 14.2 %collective-permute-start.40 = (bf16[144,896]{1,0:T(8,128)(2,1)}, bf16[144,896]{1,0:T(8,128)(2,1)}, u32[]{:S(2)}, u32[]{:S(2)}) collective-permute-start(bf16[144,896]{1,0:T(8,128)(2,1)} %get-tuple-element.163), channel_id=1, source_target_pairs={{0,28},{1,29},{2,30},{3,31},{4,16},{5,17},{6,18},{7,19},{8,20},{9,... | collective-permute-start | bytes 774152 | tf_op jit(solution)/shard_map/ppermute | solution.py:33
  223.0 26.8 %collective-permute-start.41 = (bf16[144,896]{1,0:T(8,128)(2,1)}, bf16[144,896]{1,0:T(8,128)(2,1)}, u32[]{:S(2)}, u32[]{:S(2)}) collective-permute-start(bf16[144,896]{1,0:T(8,128)(2,1)} %get-tuple-element.164), channel_id=1, source_target_pairs={{0,24},{1,25},{2,26},{3,27},{4,28},{5,29},{6,30},{7,31},{8,16},{9,... | collective-permute-start | bytes 774152 | tf_op jit(solution)/shard_map/ppermute | solution.py:33
  227.5 22.4 %collective-permute-start.42 = (bf16[144,896]{1,0:T(8,128)(2,1)}, bf16[144,896]{1,0:T(8,128)(2,1)S(1)}, u32[]{:S(2)}, u32[]{:S(2)}) collective-permute-start(bf16[144,896]{1,0:T(8,128)(2,1)} %get-tuple-element.165), channel_id=1, source_target_pairs={{0,20},{1,21},{2,22},{3,23},{4,24},{5,25},{6,26},{7,27},{8,28},{9,... | collective-permute-start | bytes 774152 | tf_op jit(solution)/shard_map/ppermute | solution.py:33
  230.4 19.4 %copy-start.16 = (bf16[128,3584]{1,0:T(8,128)(2,1)S(1)}, bf16[128,3584]{1,0:T(8,128)(2,1)}, u32[]{:S(2)}) copy-start(bf16[128,3584]{1,0:T(8,128)(2,1)} %copy-done.15) | copy-start | bytes 2752516
  230.4 19.4 %copy-start.18 = (bf16[128,3584]{1,0:T(8,128)(2,1)S(1)}, bf16[128,3584]{1,0:T(8,128)(2,1)}, u32[]{:S(2)}) copy-start(bf16[128,3584]{1,0:T(8,128)(2,1)} %copy-done.17) | copy-start | bytes 2752516
  (20 other events, 48.7 us)

commit v5 on v4

--- a/solution.py
+++ b/solution.py
@@ -63,7 +63,7 @@
             flops=int(flops), bytes_accessed=int(moved_bytes), transcendentals=0
         ),
     )(*args)
-    return result if many else result[0]
+    return list(result) if many else result[0]
 
 
 def dot(a, b):
@@ -204,23 +204,22 @@
     out_ref[...] = (gate_val / (1.0 + jnp.exp(-gate_val)) * up_val).astype(bf16)
 
 
-def output_body(own_ref, other_ref, down_ref, top_ref, low_ref, first_out, second_out):
+def output_body(own_ref, other_ref, down_ref, far_ref, first_out, second_out):
     half = first_out.shape[0]
     hidden = jnp.concatenate([own_ref[...], other_ref[...]], axis=1)
     step = 4 * LANES
     for n in range(0, down_ref.shape[1], step):
         part = slice(n, n + step)
-        weight = jnp.concatenate([down_ref[:, part], top_ref[:, part], low_ref[:, part]], axis=0)
+        weight = jnp.concatenate([down_ref[:, part], far_ref[:, part]], axis=0)
         value = dot(hidden, weight).astype(bf16)
         first_out[:, part] = value[:half]
         second_out[:, part] = value[half:]
 
 
-def down_back_body(first_ref, second_ref, down_ref, top_ref, low_ref, own_out, other_out):
+def down_back_body(first_ref, second_ref, down_ref, far_ref, own_out, other_out):
     grads = jnp.concatenate([first_ref[...], second_ref[...]], axis=0)
     own_out[...] = dot_last(grads, down_ref[...]).astype(own_out.dtype)
-    other = jnp.concatenate([top_ref[...], low_ref[...]], axis=0)
-    other_out[...] = dot_last(grads, other).astype(other_out.dtype)
+    other_out[...] = dot_last(grads, far_ref[...]).astype(other_out.dtype)
 
 
 def backward_body(first_ref, second_ref, back_ref, gate_ref, up_ref, first_out, second_out):
@@ -254,15 +253,15 @@
     kv0,
     kv1,
     kv2,
-    kv3,
     middle_ref,
     *refs,
 ):
     outs, (kv_all, kv_now, stack, attended) = refs[:experts], refs[experts:]
     tokens, width = query_ref.shape
-    rows_each = kv0.shape[0]
-    for place, ref in enumerate((kv0, kv1, kv2, kv3)):
-        kv_all[place * rows_each : (place + 1) * rows_each, : ref.shape[1]] = ref[...]
+    lead = 0
+    for ref in (kv0, kv1, kv2):
+        kv_all[lead : lead + ref.shape[0], : ref.shape[1]] = ref[...]
+        lead += ref.shape[0]
     attended[...] = jnp.zeros_like(attended)
     heads_each = HEADS // KV_HEADS
     period = 8
@@ -374,9 +373,6 @@
     for back in range(1, experts):
         pairs = [(i, i + back * GROUP) for i in range(length - back * GROUP)]
         column.append(lax.ppermute(keys_values[0], "expert", pairs))
-    early = hidden_width * 3 // 8
-    down_top = swapped(w_down[:early], 2)
-
     front_from = lax.rem(front_route[0] - group + experts, experts)
     back_from = lax.rem(back_route[0] - group + experts, experts)
     front_row, back_row = front_from.reshape(1, tokens), back_from.reshape(1, tokens)
@@ -390,11 +386,10 @@
     )
     column = after(column, [packed[0]])
     column = jnp.concatenate(column, axis=0)
-    other_chip = swapped(after([column], [down_top])[0], 2)
-    kv = [column, other_chip, swapped(column, 1), None]
+    other_chip = swapped(column, 2)
     packed = after(packed, [column])
-    down_low = swapped(after([w_down[early:]], [other_chip])[0], 2)
-    downs = (w_down, down_top, down_low)
+    down_other = swapped(w_down, 2)
+    downs = (w_down, down_other)
 
     front_small = jnp.concatenate([front_from.astype(f32), front_gate[0]], axis=0).reshape(1, -1)
     back_small = jnp.concatenate([back_from.astype(f32).reshape(1, -1), norm_gain], axis=1)
@@ -420,13 +415,20 @@
     def sent_back(chunks, by):
         return [passed_along(chunks[k], by, k) for k in range(experts)]
 
-    row_chunks = packed[:experts]
-    for k in range(1, experts, 2):
+    row_chunks, grad_chunks = packed[:experts], packed[experts:]
+    first = 1 + 2 * (experts - 1) // 3
+    for k in range(1, first):
         row_chunks[k] = turned(row_chunks[k], k)
-    arrived = row_chunks[1::2]
-    for k in range(2, experts, 2):
+    arrived = row_chunks[1:first]
+    there_back_middle = passed_along(after([back_middle[0]], [packed[0]])[0], -1)
+    chip = jnp.concatenate([column, other_chip], axis=0)
+    kv = [column, other_chip, swapped(after([chip], arrived + [there_back_middle])[0], 1)]
+    for k in range(first, experts):
         row_chunks[k] = turned(after([row_chunks[k]], arrived)[0], k)
-    kv[3] = swapped(after([other_chip], arrived)[0], 1)
+    beside = range(1, 2)
+    for k in beside:
+        grad_chunks[k] = turned(after([grad_chunks[k]], arrived)[0], k)
+    there_back_grad = passed_along(after([back_grad[0]], [there_back_middle])[0], -1)
 
     per_device = tokens // BLK
     chosen = selected_blocks[0].reshape(-1)
@@ -451,22 +453,25 @@
         vmem=VMEM_BYTES + 2 * length * tokens * 4 * LANES * 2,
     )
     middle, front_chunks = result[0], result[1:]
-    front_chunks = sent(after(front_chunks, row_chunks))
-    back_pieces = pieces_of(after([joined(after(row_chunks, [middle]))], [down_low])[0])
-    front_small, back_small = after([front_small, back_small], [back_pieces[0]])
+    ready = row_chunks + [grad_chunks[k] for k in beside]
+    front_chunks = sent(after(front_chunks, ready))
+    back_rows = joined(after(ready, [middle, there_back_grad])[:experts])
+    back_pieces = pieces_of(after([back_rows], [down_other])[0])
+    there_middle = passed_along(after([middle], [back_rows])[0], 1)
+    for k in range(1, experts):
+        if k not in beside:
+            grad_chunks[k] = turned(after([grad_chunks[k]], front_chunks)[0], k)
+    front_near = joined(after(front_chunks, [there_middle, back_pieces[2]]))
+    front_other = swapped(front_near, 2)
+
+    front_small, back_small = after([front_small, back_small], [front_near])
     there_small = passed_along(front_small, 1)
     there_back_small = passed_along(back_small, -1)
     there_front_from = there_small[0, :tokens].astype(jnp.int32).reshape(tokens, 1)
     there_front_gate = there_small[0, tokens:].reshape(tokens, 1)
     there_back_from = there_back_small[0, :tokens].astype(jnp.int32).reshape(tokens, 1)
     there_gain = there_back_small[:, tokens:]
-    there_back_middle = passed_along(after([back_middle[0]], [back_pieces[0]])[0], -1)
-    front_chunks = after(front_chunks, [back_pieces[0], there_small, there_back_small])
-    grad_chunks = sent(after(packed[experts:], front_chunks))
-    there_back_grad = passed_along(after([back_grad[0]], [there_back_middle])[0], -1)
-    front_pieces = pieces_of(joined(after(front_chunks, [there_back_middle])))
-    there_middle = passed_along(after([middle], [there_back_grad])[0], 1)
-    grad_near = joined(after(grad_chunks, [front_pieces[0], there_back_grad]))
+    grad_near = joined(after(grad_chunks, [there_small, there_back_small]))
     grad_near = [grad_near, swapped(grad_near, 1)]
 
     work = 2 * 2 * slots * width * hidden_width
@@ -480,14 +485,16 @@
     def backward(rows, grads):
         return call(backward_body, [piece, piece], (*rows, grads, w_gate, w_up), flops=4 * work)
 
-    hidden_near = hidden(front_pieces[:2])
-    hidden_far = hidden(front_pieces[2:])
     down_back, other_back = call(
         down_back_body,
         [shape_of(pair, hidden_width, f32), shape_of(pair, hidden_width)],
         (*grad_near, *downs),
         flops=2 * work,
     )
+    (front_other,) = after([front_other], [other_back])
+    front_pieces = [front_near, swapped(front_near, 1), front_other, swapped(front_other, 1)]
+    hidden_near = hidden(front_pieces[:2])
+    hidden_far = hidden(front_pieces[2:])
     hidden_other = swapped(hidden_far, 2)
     far_back = swapped(other_back, 2)
 

time: 254 us -> 260 us (1.024)
  Pallas kernels: 35.5 us -> 40 us
    ppermute x18 -> x16, waiting for transfers between devices: 46.8 us -> 87.4 us  [swapped(): lax.ppermute(array, 'expert', [(i, i ^ bit) for i in range(lax.axis_size(...]
    ppermute x13, waiting for transfers between devices: 51.2 us -> 22.9 us  [passed_along(): return lax.ppermute(array, ('section', 'expert'), pairs)]
    ppermute x9, waiting for transfers between devices: 36.3 us -> 22.5 us  [turned(): lax.ppermute(array, 'expert', [(i, (i + by * GROUP) % length) for i in ra...]
    pallas_call x15, Pallas kernels: 35.5 us -> 40 us  [call(): pl.pallas_call(body, out_shape=shapes, in_specs=specs, out_specs=[pl.Bloc...]
    slice x2 -> x0, local copies, waits for them, and re-layouts: 3.06 us -> none  [the longest x1 1.99 us: shards(): down_top = swapped(w_down[:early], 2)]
    ppermute x9, starting transfers between devices: 15.2 us -> 18.1 us  [turned(): lax.ppermute(array, 'expert', [(i, (i + by * GROUP) % length) for i in ra...]
    ppermute x18 -> x16, starting transfers between devices: 8.68 us -> 7.02 us  [swapped(): lax.ppermute(array, 'expert', [(i, i ^ bit) for i in range(lax.axis_size(...]
    unnamed x86 -> x69, local copies, waits for them, and re-layouts: 15.5 us -> 15.2 us
  transfers between devices with their start and end apart: 43 -> 41, of which waited for: 20 -> 13; matrix products, arithmetic and copies ran while one was open for 3% -> 3% of each run, Pallas kernels for 12% -> 13%
where the time goes in v5:
time: 260 us; the launch traced here: 259 us
  waiting for transfers between devices  133 us (51%)
  starting transfers between devices  62.5 us (24%)
  Pallas kernels  40 us (15%)
  local copies, waits for them, and re-layouts  20.9 us (8%)
    ppermute x16, waiting for transfers between devices, swapped(): lax.ppermute(array, 'expert', [(i, i ^ bit) for i in range(lax.axis_size(...  87.4 us
    pallas_call x15, Pallas kernels, call(): pl.pallas_call(body, out_shape=shapes, in_specs=specs, out_specs=[pl.Bloc...  40 us
    ppermute x13, starting transfers between devices, passed_along(): return lax.ppermute(array, ('section', 'expert'), pairs)  26.6 us
    ppermute x13, waiting for transfers between devices, passed_along(): return lax.ppermute(array, ('section', 'expert'), pairs)  22.9 us
    ppermute x9, waiting for transfers between devices, turned(): lax.ppermute(array, 'expert', [(i, (i + by * GROUP) % length) for i in ra...  22.5 us
    ppermute x9, starting transfers between devices, turned(): lax.ppermute(array, 'expert', [(i, (i + by * GROUP) % length) for i in ra...  18.1 us
    unnamed x69, local copies, waits for them, and re-layouts  15.2 us
    ppermute x3, starting transfers between devices, shards(): column.append(lax.ppermute(keys_values[0], 'expert', pairs))  10.7 us
  transfers between devices with their start and end apart: 41, of which 13 were waited for; matrix products, arithmetic and copies ran while one was open for 3% of the time, Pallas kernels for 13%

profile of v5, /device:TPU:0, one launch (start us, length us, event | category | flops | bytes accessed | tf_op | source)
XLA Modules:
  0.0 259.2 jit_solution(16571070563796530416)
XLA Ops:
  0.6 1.0 copy.21
  1.6 4.9 %collective-permute-start = (bf16[128,448]{1,0:T(8,128)(2,1)S(1)}, bf16[128,448]{1,0:T(8,128)(2,1)S(1)}, u32[]{:S(2)}, u32[]{:S(2)}) collective-permute-start(bf16[128,448]{1,0:T(8,128)(2,1)S(1)} %bitcast.45), channel_id=1, source_target_pairs={{0,4},{1,5},{2,6},{3,7},{4,8},{5,9},{6,10},{7,11},{8,12},{9,13},{1... | collective-permute-start | bytes 344072 | tf_op jit(solution)/shard_map/ppermute | solution.py:375
  6.6 4.5 %collective-permute-start.1 = (bf16[128,448]{1,0:T(8,128)(2,1)S(1)}, bf16[128,448]{1,0:T(8,128)(2,1)S(1)}, u32[]{:S(2)}, u32[]{:S(2)}) collective-permute-start(bf16[128,448]{1,0:T(8,128)(2,1)S(1)} %bitcast.46), channel_id=1, source_target_pairs={{0,8},{1,9},{2,10},{3,11},{4,12},{5,13},{6,14},{7,15},{16,24},{17,... | collective-permute-start | bytes 344072 | tf_op jit(solution)/shard_map/ppermute | solution.py:375
  11.1 1.3 collective-permute-start.2
  12.4 0.8 copy.22.gate_ref
  13.8 0.7 copy-done.5
  14.6 1.2 copy-done.7
  15.7 1.2 copy-done.10
  16.9 2.3 shard_map.149
  19.3 0.8 constant_dynamic-update-slice_fusion.8
  22.1 1.5 collective-permute-start.6
  23.6 1.5 collective-permute-start.15
  25.6 3.3 %collective-permute-start.5 = (bf16[144,896]{1,0:T(8,128)(2,1)S(1)}, bf16[144,896]{1,0:T(8,128)(2,1)S(1)}, u32[]{:S(2)}, u32[]{:S(2)}) collective-permute-start(bf16[144,896]{1,0:T(8,128)(2,1)S(1)} %get-tuple-element.95), channel_id=1, source_target_pairs={{0,8},{1,9},{2,10},{3,11},{4,12},{5,13},{6,14},{7,15},{8,0},{9,1},... | collective-permute-start | bytes 774152 | tf_op jit(solution)/shard_map/ppermute | solution.py:42
  29.0 46.8 %collective-permute-done.3.kv1 = bf16[512,448]{1,0:T(8,128)(2,1)S(1)} collective-permute-done((bf16[512,448]{1,0:T(8,128)(2,1)S(1)}, bf16[512,448]{1,0:T(8,128)(2,1)S(1)}, u32[]{:S(2)}, u32[]{:S(2)}) %collective-permute-start.3) | collective-permute-done | bytes 458784 | tf_op jit(solution)/shard_map/ppermute | solution.py:37
  75.7 0.8 constant_dynamic-update-slice_fusion.4
  76.6 0.7 copy-done.19
  77.3 0.7 copy-done.21
  78.0 1.0 copy-done.11
  79.0 2.2 copy.23
  81.8 3.0 %collective-permute-start.8 = (bf16[144,896]{1,0:T(8,128)(2,1)}, bf16[144,896]{1,0:T(8,128)(2,1)}, u32[]{:S(2)}, u32[]{:S(2)}) collective-permute-start(bf16[144,896]{1,0:T(8,128)(2,1)} %get-tuple-element.104), channel_id=1, source_target_pairs={{0,12},{1,13},{2,14},{3,15},{4,0},{5,1},{6,2},{7,3},{8,4},{9,5},{1... | collective-permute-start | bytes 774152 | tf_op jit(solution)/shard_map/ppermute | solution.py:42
  84.9 1.5 copy.24.kv2
  86.4 1.0 copy-done.4
  87.4 1.2 copy-done.8
  88.6 1.2 copy-done.9
  89.8 7.5 %shard_map.150 = (bf16[128,3584]{1,0:T(8,128)(2,1)S(1)}, bf16[144,896]{1,0:T(8,128)(2,1)S(1)}, bf16[144,896]{1,0:T(8,128)(2,1)S(1)}, bf16[144,896]{1,0:T(8,128)(2,1)S(1)}, bf16[144,896]{1,0:T(8,128)(2,1)S(1)}) custom-call(s32[16]{0:T(128)S(1)} %reshape_squeeze.6.chosen_ref, s32[16]{0:T(128)S(1)} %fusion.10.index_ref, s32[1]{0:T(128)} %bitcast.4.base_ref, ...), custom_call_target="tpu_custom_call" | custom-call | flops 1593835520 | bytes 5634692 | tf_op jit(solution)/shard_map/pallas_call | solution.py:55
  97.3 7.0 %collective-permute-done.13.grad_ref = bf16[128,3584]{1,0:T(8,128)(2,1)} collective-permute-done((bf16[128,3584]{1,0:T(8,128)(2,1)}, bf16[128,3584]{1,0:T(8,128)(2,1)}, u32[]{:S(2)}, u32[]{:S(2)}) %collective-permute-start.13) | collective-permute-done | bytes 917536 | tf_op jit(solution)/shard_map/ppermute | solution.py:33
  104.4 2.1 shard_map.151.first_ref
  106.5 1.6 collective-permute-start.16
  108.5 3.5 %collective-permute-start.11 = (bf16[144,896]{1,0:T(8,128)(2,1)S(1)}, bf16[144,896]{1,0:T(8,128)(2,1)S(1)}, u32[]{:S(2)}, u32[]{:S(2)}) collective-permute-start(bf16[144,896]{1,0:T(8,128)(2,1)S(1)} %get-tuple-element.109), channel_id=1, source_target_pairs={{0,8},{1,9},{2,10},{3,11},{4,12},{5,13},{6,14},{7,15},{8,0},{9,1},... | collective-permute-start | bytes 774152 | tf_op jit(solution)/shard_map/ppermute | solution.py:42
  112.4 7.2 %collective-permute-done.10.refs_1_ = bf16[144,896]{1,0:T(8,128)(2,1)S(1)} collective-permute-done((bf16[144,896]{1,0:T(8,128)(2,1)S(1)}, bf16[144,896]{1,0:T(8,128)(2,1)S(1)}, u32[]{:S(2)}, u32[]{:S(2)}) %collective-permute-start.10) | collective-permute-done | bytes 258080 | tf_op jit(solution)/shard_map/ppermute | solution.py:42
  119.6 9.3 %collective-permute-done.11.refs_2_ = bf16[144,896]{1,0:T(8,128)(2,1)S(1)} collective-permute-done((bf16[144,896]{1,0:T(8,128)(2,1)S(1)}, bf16[144,896]{1,0:T(8,128)(2,1)S(1)}, u32[]{:S(2)}, u32[]{:S(2)}) %collective-permute-start.11) | collective-permute-done | bytes 258080 | tf_op jit(solution)/shard_map/ppermute | solution.py:42
  128.9 4.6 %collective-permute-start.20 = (bf16[144,896]{1,0:T(8,128)(2,1)S(1)}, bf16[144,896]{1,0:T(8,128)(2,1)S(1)}, u32[]{:S(2)}, u32[]{:S(2)}) collective-permute-start(bf16[144,896]{1,0:T(8,128)(2,1)S(1)} %copy-done.18), channel_id=1, source_target_pairs={{0,8},{1,9},{2,10},{3,11},{4,12},{5,13},{6,14},{7,15},{8,0},{9,1},... | collective-permute-start | bytes 774152 | tf_op jit(solution)/shard_map/ppermute | solution.py:42
  133.5 3.4 %collective-permute-start.21 = (bf16[144,896]{1,0:T(8,128)(2,1)S(1)}, bf16[144,896]{1,0:T(8,128)(2,1)S(1)}, u32[]{:S(2)}, u32[]{:S(2)}) collective-permute-start(bf16[144,896]{1,0:T(8,128)(2,1)S(1)} %copy-done.16), channel_id=1, source_target_pairs={{0,12},{1,13},{2,14},{3,15},{4,0},{5,1},{6,2},{7,3},{8,4},{9,5},{1... | collective-permute-start | bytes 774152 | tf_op jit(solution)/shard_map/ppermute | solution.py:42
  136.9 1.1 shard_map.152.first_ref
  138.0 1.6 collective-permute-start.22
  140.1 6.0 %collective-permute-done.20.refs_2_ = bf16[144,896]{1,0:T(8,128)(2,1)S(1)} collective-permute-done((bf16[144,896]{1,0:T(8,128)(2,1)S(1)}, bf16[144,896]{1,0:T(8,128)(2,1)S(1)}, u32[]{:S(2)}, u32[]{:S(2)}) %collective-permute-start.20) | collective-permute-done | bytes 258080 | tf_op jit(solution)/shard_map/ppermute | solution.py:42
  146.1 2.0 shard_map.154.first_ref
  149.4 1.5 collective-permute-done.23.second_ref
  150.9 2.8 %shard_map.155 = (f32[288,256]{1,0:T(8,128)S(1)}, bf16[288,256]{1,0:T(8,128)(2,1)S(1)}) custom-call(bf16[144,3584]{1,0:T(8,128)(2,1)S(1)} %shard_map.154.first_ref, bf16[144,3584]{1,0:T(8,128)(2,1)S(1)} %collective-permute-done.23.second_ref, bf16[256,3584]{1,0:T(8,128)(2,1)S(1)} %bitcast.37, bf16[256,3584]{1,0:T(8,128)(2,1)} %collective-permute-done.15.far_ref), custom_call_target="tpu_custom_call" | custom-call | flops 1056964608 | bytes 6176768 | tf_op jit(solution)/shard_map/pallas_call | solution.py:55
  153.7 19.8 %collective-permute-done.19.first_ref = bf16[144,3584]{1,0:T(8,128)(2,1)S(1)} collective-permute-done((bf16[144,3584]{1,0:T(8,128)(2,1)S(1)}, bf16[144,3584]{1,0:T(8,128)(2,1)S(1)}, u32[]{:S(2)}, u32[]{:S(2)}) %collective-permute-start.19) | collective-permute-done | bytes 1032224 | tf_op jit(solution)/shard_map/ppermute | solution.py:37
  174.3 5.5 %collective-permute-done.34.back_ref = bf16[288,256]{1,0:T(8,128)(2,1)S(1)} collective-permute-done((bf16[288,256]{1,0:T(8,128)(2,1)S(1)}, bf16[288,256]{1,0:T(8,128)(2,1)S(1)}, u32[]{:S(2)}, u32[]{:S(2)}) %collective-permute-start.34) | collective-permute-done | bytes 147488 | tf_op jit(solution)/shard_map/ppermute | solution.py:37
  179.8 2.5 shard_map.160
  182.3 1.3 shard_map.153.own_ref
  183.6 1.3 shard_map.156
  185.4 3.4 %shard_map.159 = (bf16[144,3584]{1,0:T(8,128)(2,1)S(1)}, bf16[144,3584]{1,0:T(8,128)(2,1)}) custom-call(bf16[144,3584]{1,0:T(8,128)(2,1)S(1)} %shard_map.151.first_ref, bf16[144,3584]{1,0:T(8,128)(2,1)S(1)} %collective-permute-done.31.second_ref, f32[288,256]{1,0:T(8,128)S(1)} %get-tuple-element.142.back_ref, bf16[3584,256]{1,0:T(8,128)(2,1)S(1)} %bitcast.31, ...), custom_call_target="tpu_custom_call" | custom-call | flops 2113929216 | bytes 8093696 | tf_op jit(solution)/shard_map/pallas_call | solution.py:55
  189.1 2.1 collective-permute-done.25.other_ref
  191.1 2.7 %shard_map.157 = (bf16[144,3584]{1,0:T(8,128)(2,1)S(1)}, bf16[144,3584]{1,0:T(8,128)(2,1)S(1)}) custom-call(bf16[288,256]{1,0:T(8,128)(2,1)S(1)} %shard_map.153.own_ref, bf16[288,256]{1,0:T(8,128)(2,1)S(1)} %collective-permute-done.25.other_ref, bf16[256,3584]{1,0:T(8,128)(2,1)S(1)} %bitcast.38, bf16[256,3584]{1,0:T(8,128)(2,1)} %collective-permute-done.15.far_ref), custom_call_target="tpu_custom_call" | custom-call | flops 1056964608 | bytes 6029312 | tf_op jit(solution)/shard_map/pallas_call | solution.py:55
  194.0 1.2 add_convert_fusion
  195.7 0.9 collective-permute-done.26.refs_1_
  196.6 1.9 shard_map.158
  198.5 1.5 collective-permute-start.27
  200.0 7.8 %collective-permute-start.28 = (bf16[144,896]{1,0:T(8,128)(2,1)}, bf16[144,896]{1,0:T(8,128)(2,1)S(1)}, u32[]{:S(2)}, u32[]{:S(2)}) collective-permute-start(bf16[144,896]{1,0:T(8,128)(2,1)} %get-tuple-element.139), channel_id=1, source_target_pairs={{0,28},{1,29},{2,30},{3,31},{4,16},{5,17},{6,18},{7,19},{8,20},{9,... | collective-permute-start | bytes 774152 | tf_op jit(solution)/shard_map/ppermute | solution.py:33
  208.0 1.8 collective-permute-start.30
  209.8 10.8 %collective-permute-done.36.refs_2_ = bf16[144,3584]{1,0:T(8,128)(2,1)S(1)} collective-permute-done((bf16[144,3584]{1,0:T(8,128)(2,1)}, bf16[144,3584]{1,0:T(8,128)(2,1)S(1)}, u32[]{:S(2)}, u32[]{:S(2)}) %collective-permute-start.36) | collective-permute-done | bytes 1032224 | tf_op jit(solution)/shard_map/ppermute | solution.py:37
  220.6 1.2 copy-done.24
  221.8 2.1 shard_map.161
  223.9 1.5 collective-permute-start.37
  225.4 7.8 %collective-permute-start.38 = (bf16[144,896]{1,0:T(8,128)(2,1)}, bf16[144,896]{1,0:T(8,128)(2,1)S(1)}, u32[]{:S(2)}, u32[]{:S(2)}) collective-permute-start(bf16[144,896]{1,0:T(8,128)(2,1)} %get-tuple-element.151), channel_id=1, source_target_pairs={{0,28},{1,29},{2,30},{3,31},{4,16},{5,17},{6,18},{7,19},{8,20},{9,... | collective-permute-start | bytes 774152 | tf_op jit(solution)/shard_map/ppermute | solution.py:33
  233.2 1.6 collective-permute-start.40
  234.9 1.2 copy-done.14
  236.2 3.2 %shard_map.162 = bf16[128,3584]{1,0:T(8,128)(2,1)} custom-call(s32[128,1]{1,0:T(8,128)S(1)} %copy.25.route_ref, f32[128,1]{1,0:T(8,128)S(1)} %copy.26.gate_ref, bf16[128,3584]{1,0:T(8,128)(2,1)S(1)} %copy-done.14, bf16[144,896]{1,0:T(8,128)(2,1)S(1)} %collective-permute-done.27.refs_0_, bf16[144,896]{1,0:T(8,128)(2,1)S(1)} %collective-permute-done.28.refs_1_, ...), custom_call_target="tpu_custom_call" | custom-call | flops 1056964608 | bytes 2868224 | tf_op jit(solution)/shard_map/pallas_call | solution.py:55
  239.4 2.9 %collective-permute-done.37.refs_0_ = bf16[144,896]{1,0:T(8,128)(2,1)S(1)} collective-permute-done((bf16[144,896]{1,0:T(8,128)(2,1)}, bf16[144,896]{1,0:T(8,128)(2,1)S(1)}, u32[]{:S(2)}, u32[]{:S(2)}) %collective-permute-start.37) | collective-permute-done | bytes 258080 | tf_op jit(solution)/shard_map/ppermute | solution.py:33
  242.3 12.9 %collective-permute-done.39.refs_2_ = bf16[144,896]{1,0:T(8,128)(2,1)S(1)} collective-permute-done((bf16[144,896]{1,0:T(8,128)(2,1)}, bf16[144,896]{1,0:T(8,128)(2,1)S(1)}, u32[]{:S(2)}, u32[]{:S(2)}) %collective-permute-start.39) | collective-permute-done | bytes 258080 | tf_op jit(solution)/shard_map/ppermute | solution.py:33
  255.3 3.9 %shard_map.163 = bf16[128,3584]{1,0:T(8,128)(2,1)} custom-call(s32[128,1]{1,0:T(8,128)S(1)} %copy.27.route_ref, f32[1,3584]{1,0:T(1,128)S(1)} %slice.19.gain_ref, bf16[128,3584]{1,0:T(8,128)(2,1)S(1)} %copy-done.12, bf16[128,3584]{1,0:T(8,128)(2,1)} %collective-permute-done.13.grad_ref, bf16[144,896]{1,0:T(8,128)(2,1)S(1)} %collective-permute-done.37.refs_0_, ...), custom_call_target="tpu_custom_call" | custom-call | flops 1056964608 | bytes 3799552 | tf_op jit(solution)/shard_map/pallas_call | solution.py:55
  (120 shorter events, 9.2 us)
Async XLA Ops:
  1.6 17.6 %collective-permute-start = (bf16[128,448]{1,0:T(8,128)(2,1)S(1)}, bf16[128,448]{1,0:T(8,128)(2,1)S(1)}, u32[]{:S(2)}, u32[]{:S(2)}) collective-permute-start(bf16[128,448]{1,0:T(8,128)(2,1)S(1)} %bitcast.45), channel_id=1, source_target_pairs={{0,4},{1,5},{2,6},{3,7},{4,8},{5,9},{6,10},{7,11},{8,12},{9,13},{1... | collective-permute-start | bytes 344072 | tf_op jit(solution)/shard_map/ppermute | solution.py:375
  6.6 12.7 %collective-permute-start.1 = (bf16[128,448]{1,0:T(8,128)(2,1)S(1)}, bf16[128,448]{1,0:T(8,128)(2,1)S(1)}, u32[]{:S(2)}, u32[]{:S(2)}) collective-permute-start(bf16[128,448]{1,0:T(8,128)(2,1)S(1)} %bitcast.46), channel_id=1, source_target_pairs={{0,8},{1,9},{2,10},{3,11},{4,12},{5,13},{6,14},{7,15},{16,24},{17,... | collective-permute-start | bytes 344072 | tf_op jit(solution)/shard_map/ppermute | solution.py:375
  11.1 8.2 %collective-permute-start.2 = (bf16[128,448]{1,0:T(8,128)(2,1)S(1)}, bf16[128,448]{1,0:T(8,128)(2,1)S(1)}, u32[]{:S(2)}, u32[]{:S(2)}) collective-permute-start(bf16[128,448]{1,0:T(8,128)(2,1)S(1)} %bitcast.47), channel_id=1, source_target_pairs={{0,12},{1,13},{2,14},{3,15},{16,28},{17,29},{18,30},{19,31}} | collective-permute-start | bytes 344072 | tf_op jit(solution)/shard_map/ppermute | solution.py:375
  16.9 6.7 %copy-start.2 = (bf16[1,1,256,3584]{3,2,1,0:T(8,128)(2,1)S(1)}, bf16[1,1,256,3584]{3,2,1,0:T(8,128)(2,1)}, u32[]{:S(2)}) copy-start(bf16[1,1,256,3584]{3,2,1,0:T(8,128)(2,1)} %param.27) | copy-start | bytes 5505028
  19.2 57.3 %copy-start.15 = (bf16[144,896]{1,0:T(8,128)(2,1)}, bf16[144,896]{1,0:T(8,128)(2,1)S(1)}, u32[]{:S(2)}) copy-start(bf16[144,896]{1,0:T(8,128)(2,1)S(1)} %get-tuple-element.128) | copy-start | bytes 774148
  19.2 58.0 %copy-start.17 = (bf16[144,896]{1,0:T(8,128)(2,1)}, bf16[144,896]{1,0:T(8,128)(2,1)S(1)}, u32[]{:S(2)}) copy-start(bf16[144,896]{1,0:T(8,128)(2,1)S(1)} %get-tuple-element.126) | copy-start | bytes 774148
  19.2 58.0 %copy-start.25 = (bf16[144,896]{1,0:T(8,128)(2,1)}, bf16[144,896]{1,0:T(8,128)(2,1)S(1)}, u32[]{:S(2)}) copy-start(bf16[144,896]{1,0:T(8,128)(2,1)S(1)} %get-tuple-element.130.refs_0_) | copy-start | bytes 774148
  19.2 58.0 %copy-start.27 = (bf16[144,896]{1,0:T(8,128)(2,1)}, bf16[144,896]{1,0:T(8,128)(2,1)S(1)}, u32[]{:S(2)}) copy-start(bf16[144,896]{1,0:T(8,128)(2,1)S(1)} %get-tuple-element.113.refs_0_) | copy-start | bytes 774148
  20.7 61.0 %copy-start.29 = (s32[1,2,2,4]{3,2,1,0:T(2,128)S(1)}, s32[1,2,2,4]{3,2,1,0:T(2,128)}, u32[]{:S(2)}) copy-start(s32[1,2,2,4]{3,2,1,0:T(2,128)} %param.17) | copy-start | bytes 196
  20.7 61.1 %copy-start.31 = (s32[1,128,1]{1,2,0:T(1,128)S(1)}, s32[1,128,1]{1,2,0:T(1,128)}, u32[]{:S(2)}) copy-start(s32[1,128,1]{1,2,0:T(1,128)} %param.18) | copy-start | bytes 1540
  22.1 62.8 %copy-start.3 = (bf16[512,448]{1,0:T(8,128)(2,1)}, bf16[512,448]{1,0:T(8,128)(2,1)S(1)}, u32[]{:S(2)}) copy-start(bf16[512,448]{1,0:T(8,128)(2,1)S(1)} %get-tuple-element.165.kv0) | copy-start | bytes 1376260
  22.1 56.0 %collective-permute-start.6 = (bf16[128,3584]{1,0:T(8,128)(2,1)S(1)}, bf16[128,3584]{1,0:T(8,128)(2,1)S(1)}, u32[]{:S(2)}, u32[]{:S(2)}) collective-permute-start(bf16[128,3584]{1,0:T(8,128)(2,1)S(1)} %bitcast.40), channel_id=1, source_target_pairs={{0,16},{1,17},{2,18},{3,19},{4,20},{5,21},{6,22},{7,23},{8,24},{9,... | collective-permute-start | bytes 2752520 | tf_op jit(solution)/shard_map/ppermute | solution.py:33
  23.6 82.9 %collective-permute-start.15 = (bf16[256,3584]{1,0:T(8,128)(2,1)S(1)}, bf16[256,3584]{1,0:T(8,128)(2,1)}, u32[]{:S(2)}, u32[]{:S(2)}) collective-permute-start(bf16[256,3584]{1,0:T(8,128)(2,1)S(1)} %bitcast.36), channel_id=1, source_target_pairs={{0,2},{1,3},{2,0},{3,1},{4,6},{5,7},{6,4},{7,5},{8,10},{9,11},{10,... | collective-permute-start | bytes 5505032 | tf_op jit(solution)/shard_map/ppermute | solution.py:37
  25.1 50.6 %collective-permute-start.3 = (bf16[512,448]{1,0:T(8,128)(2,1)S(1)}, bf16[512,448]{1,0:T(8,128)(2,1)S(1)}, u32[]{:S(2)}, u32[]{:S(2)}) collective-permute-start(bf16[512,448]{1,0:T(8,128)(2,1)S(1)} %get-tuple-element.165.kv0), channel_id=1, source_target_pairs={{0,2},{1,3},{2,0},{3,1},{4,6},{5,7},{6,4},{7,5},{8,10},{9,11},{10,... | collective-permute-start | bytes 1376264 | tf_op jit(solution)/shard_map/ppermute | solution.py:37
  25.6 51.0 %collective-permute-start.4 = (bf16[144,896]{1,0:T(8,128)(2,1)S(1)}, bf16[144,896]{1,0:T(8,128)(2,1)S(1)}, u32[]{:S(2)}, u32[]{:S(2)}) collective-permute-start(bf16[144,896]{1,0:T(8,128)(2,1)S(1)} %get-tuple-element.94), channel_id=1, source_target_pairs={{0,4},{1,5},{2,6},{3,7},{4,8},{5,9},{6,10},{7,11},{8,12},{9,13},{1... | collective-permute-start | bytes 774152 | tf_op jit(solution)/shard_map/ppermute | solution.py:42
  25.6 51.7 %collective-permute-start.5 = (bf16[144,896]{1,0:T(8,128)(2,1)S(1)}, bf16[144,896]{1,0:T(8,128)(2,1)S(1)}, u32[]{:S(2)}, u32[]{:S(2)}) collective-permute-start(bf16[144,896]{1,0:T(8,128)(2,1)S(1)} %get-tuple-element.95), channel_id=1, source_target_pairs={{0,8},{1,9},{2,10},{3,11},{4,12},{5,13},{6,14},{7,15},{8,0},{9,1},... | collective-permute-start | bytes 774152 | tf_op jit(solution)/shard_map/ppermute | solution.py:42
  76.6 9.8 %copy-start.6 = (f32[1,3584]{1,0:T(1,128)S(1)}, f32[1,3584]{1,0:T(1,128)}, u32[]{:S(2)}) copy-start(f32[1,3584]{1,0:T(1,128)} %gain_ref.3) | copy-start | bytes 43012
  81.2 3.6 %collective-permute-start.7 = (bf16[1024,448]{0,1:T(8,128)(2,1)}, bf16[1024,448]{0,1:T(8,128)(2,1)}, u32[]{:S(2)}, u32[]{:S(2)}) collective-permute-start(bf16[1024,448]{0,1:T(8,128)(2,1)} %copy.23), channel_id=1, source_target_pairs={{0,1},{1,0},{2,3},{3,2},{4,5},{5,4},{6,7},{7,6},{8,9},{9,8},{10,11... | collective-permute-start | bytes 2752520 | tf_op jit(solution)/shard_map/ppermute | solution.py:37
  81.2 23.1 %collective-permute-start.13 = (bf16[128,3584]{1,0:T(8,128)(2,1)}, bf16[128,3584]{1,0:T(8,128)(2,1)}, u32[]{:S(2)}, u32[]{:S(2)}) collective-permute-start(bf16[128,3584]{1,0:T(8,128)(2,1)} %bitcast.43), channel_id=1, source_target_pairs={{0,16},{1,17},{2,18},{3,19},{4,20},{5,21},{6,22},{7,23},{8,24},{9,... | collective-permute-start | bytes 2752520 | tf_op jit(solution)/shard_map/ppermute | solution.py:33
  81.8 15.5 %collective-permute-start.8 = (bf16[144,896]{1,0:T(8,128)(2,1)}, bf16[144,896]{1,0:T(8,128)(2,1)}, u32[]{:S(2)}, u32[]{:S(2)}) collective-permute-start(bf16[144,896]{1,0:T(8,128)(2,1)} %get-tuple-element.104), channel_id=1, source_target_pairs={{0,12},{1,13},{2,14},{3,15},{4,0},{5,1},{6,2},{7,3},{8,4},{9,5},{1... | collective-permute-start | bytes 774152 | tf_op jit(solution)/shard_map/ppermute | solution.py:42
  84.8 12.5 %collective-permute-start.9 = (bf16[144,896]{1,0:T(8,128)(2,1)}, bf16[144,896]{1,0:T(8,128)(2,1)}, u32[]{:S(2)}, u32[]{:S(2)}) collective-permute-start(bf16[144,896]{1,0:T(8,128)(2,1)} %get-tuple-element.106), channel_id=1, source_target_pairs={{0,4},{1,5},{2,6},{3,7},{4,8},{5,9},{6,10},{7,11},{8,12},{9,13},{1... | collective-permute-start | bytes 774152 | tf_op jit(solution)/shard_map/ppermute | solution.py:42
  88.6 1.2 copy-start.9
  89.8 14.5 %copy-start.20 = (bf16[144,896]{1,0:T(8,128)(2,1)S(1)}, bf16[144,896]{1,0:T(8,128)(2,1)}, u32[]{:S(2)}) copy-start(bf16[144,896]{1,0:T(8,128)(2,1)} %copy-done.19) | copy-start | bytes 774148
  89.8 14.5 %copy-start.22 = (bf16[144,896]{1,0:T(8,128)(2,1)S(1)}, bf16[144,896]{1,0:T(8,128)(2,1)}, u32[]{:S(2)}) copy-start(bf16[144,896]{1,0:T(8,128)(2,1)} %copy-done.21) | copy-start | bytes 774148
  89.8 14.5 %copy-start.28 = (bf16[144,896]{1,0:T(8,128)(2,1)S(1)}, bf16[144,896]{1,0:T(8,128)(2,1)}, u32[]{:S(2)}) copy-start(bf16[144,896]{1,0:T(8,128)(2,1)} %copy-done.27) | copy-start | bytes 774148
  104.3 24.6 %copy-start.18 = (bf16[144,896]{1,0:T(8,128)(2,1)S(1)}, bf16[144,896]{1,0:T(8,128)(2,1)}, u32[]{:S(2)}) copy-start(bf16[144,896]{1,0:T(8,128)(2,1)} %copy-done.17) | copy-start | bytes 774148
  104.3 29.1 %copy-start.16 = (bf16[144,896]{1,0:T(8,128)(2,1)S(1)}, bf16[144,896]{1,0:T(8,128)(2,1)}, u32[]{:S(2)}) copy-start(bf16[144,896]{1,0:T(8,128)(2,1)} %copy-done.15) | copy-start | bytes 774148
  104.3 32.5 %copy-start.30 = (f32[1,128,1]{1,2,0:T(1,128)S(1)}, f32[1,128,1]{1,2,0:T(1,128)}, u32[]{:S(2)}) copy-start(f32[1,128,1]{1,2,0:T(1,128)} %param.19) | copy-start | bytes 1540
  106.5 30.5 %collective-permute-start.16 = (bf16[144,3584]{1,0:T(8,128)(2,1)S(1)}, bf16[144,3584]{1,0:T(8,128)(2,1)S(1)}, u32[]{:S(2)}, u32[]{:S(2)}) collective-permute-start(bf16[144,3584]{1,0:T(8,128)(2,1)S(1)} %shard_map.151.first_ref), channel_id=1, source_target_pairs={{0,2},{1,3},{2,0},{3,1},{4,6},{5,7},{6,4},{7,5},{8,10},{9,11},{10,... | collective-permute-start | bytes 3096584 | tf_op jit(solution)/shard_map/ppermute | solution.py:37
  108.0 28.9 %collective-permute-start.14 = (bf16[128,3584]{1,0:T(8,128)(2,1)S(1)}, bf16[128,3584]{1,0:T(8,128)(2,1)S(1)}, u32[]{:S(2)}, u32[]{:S(2)}) collective-permute-start(bf16[128,3584]{1,0:T(8,128)(2,1)S(1)} %get-tuple-element.117), channel_id=1, source_target_pairs={{0,16},{1,17},{2,18},{3,19},{4,20},{5,21},{6,22},{7,23},{8,24},{9,... | collective-permute-start | bytes 2752520 | tf_op jit(solution)/shard_map/ppermute | solution.py:33
  108.5 11.1 %collective-permute-start.10 = (bf16[144,896]{1,0:T(8,128)(2,1)S(1)}, bf16[144,896]{1,0:T(8,128)(2,1)S(1)}, u32[]{:S(2)}, u32[]{:S(2)}) collective-permute-start(bf16[144,896]{1,0:T(8,128)(2,1)S(1)} %get-tuple-element.108), channel_id=1, source_target_pairs={{0,4},{1,5},{2,6},{3,7},{4,8},{5,9},{6,10},{7,11},{8,12},{9,13},{1... | collective-permute-start | bytes 774152 | tf_op jit(solution)/shard_map/ppermute | solution.py:42
  108.5 20.4 %collective-permute-start.11 = (bf16[144,896]{1,0:T(8,128)(2,1)S(1)}, bf16[144,896]{1,0:T(8,128)(2,1)S(1)}, u32[]{:S(2)}, u32[]{:S(2)}) collective-permute-start(bf16[144,896]{1,0:T(8,128)(2,1)S(1)} %get-tuple-element.109), channel_id=1, source_target_pairs={{0,8},{1,9},{2,10},{3,11},{4,12},{5,13},{6,14},{7,15},{8,0},{9,1},... | collective-permute-start | bytes 774152 | tf_op jit(solution)/shard_map/ppermute | solution.py:42
  112.0 16.9 %collective-permute-start.12 = (bf16[144,896]{1,0:T(8,128)(2,1)S(1)}, bf16[144,896]{1,0:T(8,128)(2,1)S(1)}, u32[]{:S(2)}, u32[]{:S(2)}) collective-permute-start(bf16[144,896]{1,0:T(8,128)(2,1)S(1)} %get-tuple-element.110), channel_id=1, source_target_pairs={{0,12},{1,13},{2,14},{3,15},{4,0},{5,1},{6,2},{7,3},{8,4},{9,5},{1... | collective-permute-start | bytes 774152 | tf_op jit(solution)/shard_map/ppermute | solution.py:42
  128.9 17.2 %collective-permute-start.20 = (bf16[144,896]{1,0:T(8,128)(2,1)S(1)}, bf16[144,896]{1,0:T(8,128)(2,1)S(1)}, u32[]{:S(2)}, u32[]{:S(2)}) collective-permute-start(bf16[144,896]{1,0:T(8,128)(2,1)S(1)} %copy-done.18), channel_id=1, source_target_pairs={{0,8},{1,9},{2,10},{3,11},{4,12},{5,13},{6,14},{7,15},{8,0},{9,1},... | collective-permute-start | bytes 774152 | tf_op jit(solution)/shard_map/ppermute | solution.py:42
  133.5 12.6 %collective-permute-start.21 = (bf16[144,896]{1,0:T(8,128)(2,1)S(1)}, bf16[144,896]{1,0:T(8,128)(2,1)S(1)}, u32[]{:S(2)}, u32[]{:S(2)}) collective-permute-start(bf16[144,896]{1,0:T(8,128)(2,1)S(1)} %copy-done.16), channel_id=1, source_target_pairs={{0,12},{1,13},{2,14},{3,15},{4,0},{5,1},{6,2},{7,3},{8,4},{9,5},{1... | collective-permute-start | bytes 774152 | tf_op jit(solution)/shard_map/ppermute | solution.py:42
  136.9 9.2 %copy-start.26 = (bf16[144,896]{1,0:T(8,128)(2,1)S(1)}, bf16[144,896]{1,0:T(8,128)(2,1)}, u32[]{:S(2)}) copy-start(bf16[144,896]{1,0:T(8,128)(2,1)} %copy-done.25) | copy-start | bytes 774148
  138.0 8.1 %collective-permute-start.22 = (f32[1,3712]{1,0:T(1,128)S(1)}, f32[1,3712]{1,0:T(1,128)S(1)}, u32[]{:S(2)}, u32[]{:S(2)}) collective-permute-start(f32[1,3712]{1,0:T(1,128)S(1)} %pad_maximum_fusion), channel_id=1, source_target_pairs={{0,16},{1,17},{2,18},{3,19},{4,20},{5,21},{6,22},{7,23},{8,24},{9,... | collective-permute-start | bytes 44552 | tf_op jit(solution)/shard_map/ppermute | solution.py:33
  139.6 6.5 %collective-permute-start.17 = (f32[1,256]{1,0:T(1,128)S(1)}, f32[1,256]{1,0:T(1,128)S(1)}, u32[]{:S(2)}, u32[]{:S(2)}) collective-permute-start(f32[1,256]{1,0:T(1,128)S(1)} %maximum_bitcast_fusion), channel_id=1, source_target_pairs={{0,16},{1,17},{2,18},{3,19},{4,20},{5,21},{6,22},{7,23},{8,24},{9,... | collective-permute-start | bytes 3080 | tf_op jit(solution)/shard_map/ppermute | solution.py:33
  148.2 31.6 %copy-start = (bf16[1,1,3584,256]{3,2,1,0:T(8,128)(2,1)S(1)}, bf16[1,1,3584,256]{3,2,1,0:T(8,128)(2,1)}, u32[]{:S(2)}) copy-start(bf16[1,1,3584,256]{3,2,1,0:T(8,128)(2,1)} %param.25) | copy-start | bytes 5505028
  148.2 31.6 %copy-start.1 = (bf16[1,1,3584,256]{3,2,1,0:T(8,128)(2,1)S(1)}, bf16[1,1,3584,256]{3,2,1,0:T(8,128)(2,1)}, u32[]{:S(2)}) copy-start(bf16[1,1,3584,256]{3,2,1,0:T(8,128)(2,1)} %param.26) | copy-start | bytes 5505028
  148.2 2.7 %collective-permute-start.23 = (bf16[144,3584]{1,0:T(8,128)(2,1)S(1)}, bf16[144,3584]{1,0:T(8,128)(2,1)S(1)}, u32[]{:S(2)}, u32[]{:S(2)}) collective-permute-start(bf16[144,3584]{1,0:T(8,128)(2,1)S(1)} %shard_map.154.first_ref), channel_id=1, source_target_pairs={{0,1},{1,0},{2,3},{3,2},{4,5},{5,4},{6,7},{7,6},{8,9},{9,8},{10,11... | collective-permute-start | bytes 3096584 | tf_op jit(solution)/shard_map/ppermute | solution.py:37
  148.3 25.2 %collective-permute-start.19 = (bf16[144,3584]{1,0:T(8,128)(2,1)S(1)}, bf16[144,3584]{1,0:T(8,128)(2,1)S(1)}, u32[]{:S(2)}, u32[]{:S(2)}) collective-permute-start(bf16[144,3584]{1,0:T(8,128)(2,1)S(1)} %shard_map.152.first_ref), channel_id=1, source_target_pairs={{0,2},{1,3},{2,0},{3,1},{4,6},{5,7},{6,4},{7,5},{8,10},{9,11},{10,... | collective-permute-start | bytes 3096584 | tf_op jit(solution)/shard_map/ppermute | solution.py:37
  148.9 25.4 %collective-permute-start.33 = (bf16[144,3584]{1,0:T(8,128)(2,1)S(1)}, bf16[144,3584]{1,0:T(8,128)(2,1)S(1)}, u32[]{:S(2)}, u32[]{:S(2)}) collective-permute-start(bf16[144,3584]{1,0:T(8,128)(2,1)S(1)} %collective-permute-done.16.first_ref), channel_id=1, source_target_pairs={{0,1},{1,0},{2,3},{3,2},{4,5},{5,4},{6,7},{7,6},{8,9},{9,8},{10,11... | collective-permute-start | bytes 3096584 | tf_op jit(solution)/shard_map/ppermute | solution.py:37
  149.0 33.3 %collective-permute-start.18 = (bf16[144,3584]{1,0:T(8,128)(2,1)S(1)}, bf16[144,3584]{1,0:T(8,128)(2,1)S(1)}, u32[]{:S(2)}, u32[]{:S(2)}) collective-permute-start(bf16[144,3584]{1,0:T(8,128)(2,1)S(1)} %shard_map.152.first_ref), channel_id=1, source_target_pairs={{0,1},{1,0},{2,3},{3,2},{4,5},{5,4},{6,7},{7,6},{8,9},{9,8},{10,11... | collective-permute-start | bytes 3096584 | tf_op jit(solution)/shard_map/ppermute | solution.py:37
  173.5 10.1 %collective-permute-start.24 = (bf16[144,3584]{1,0:T(8,128)(2,1)S(1)}, bf16[144,3584]{1,0:T(8,128)(2,1)S(1)}, u32[]{:S(2)}, u32[]{:S(2)}) collective-permute-start(bf16[144,3584]{1,0:T(8,128)(2,1)S(1)} %collective-permute-done.19.first_ref), channel_id=1, source_target_pairs={{0,1},{1,0},{2,3},{3,2},{4,5},{5,4},{6,7},{7,6},{8,9},{9,8},{10,11... | collective-permute-start | bytes 3096584 | tf_op jit(solution)/shard_map/ppermute | solution.py:37
  173.5 6.3 %collective-permute-start.34 = (bf16[288,256]{1,0:T(8,128)(2,1)S(1)}, bf16[288,256]{1,0:T(8,128)(2,1)S(1)}, u32[]{:S(2)}, u32[]{:S(2)}) collective-permute-start(bf16[288,256]{1,0:T(8,128)(2,1)S(1)} %get-tuple-element.134), channel_id=1, source_target_pairs={{0,2},{1,3},{2,0},{3,1},{4,6},{5,7},{6,4},{7,5},{8,10},{9,11},{10,... | collective-permute-start | bytes 442376 | tf_op jit(solution)/shard_map/ppermute | solution.py:37
  174.0 11.4 %collective-permute-start.31 = (bf16[144,3584]{1,0:T(8,128)(2,1)S(1)}, bf16[144,3584]{1,0:T(8,128)(2,1)S(1)}, u32[]{:S(2)}, u32[]{:S(2)}) collective-permute-start(bf16[144,3584]{1,0:T(8,128)(2,1)S(1)} %shard_map.151.first_ref), channel_id=1, source_target_pairs={{0,1},{1,0},{2,3},{3,2},{4,5},{5,4},{6,7},{7,6},{8,9},{9,8},{10,11... | collective-permute-start | bytes 3096584 | tf_op jit(solution)/shard_map/ppermute | solution.py:37
  182.2 11.7 %collective-permute-start.35 = (bf16[144,3584]{1,0:T(8,128)(2,1)S(1)}, bf16[144,3584]{1,0:T(8,128)(2,1)S(1)}, u32[]{:S(2)}, u32[]{:S(2)}) collective-permute-start(bf16[144,3584]{1,0:T(8,128)(2,1)S(1)} %get-tuple-element.146), channel_id=1, source_target_pairs={{0,1},{1,0},{2,3},{3,2},{4,5},{5,4},{6,7},{7,6},{8,9},{9,8},{10,11... | collective-permute-start | bytes 3096584 | tf_op jit(solution)/shard_map/ppermute | solution.py:37
  184.8 6.3 %collective-permute-start.25 = (bf16[288,256]{1,0:T(8,128)(2,1)S(1)}, bf16[288,256]{1,0:T(8,128)(2,1)S(1)}, u32[]{:S(2)}, u32[]{:S(2)}) collective-permute-start(bf16[288,256]{1,0:T(8,128)(2,1)S(1)} %shard_map.156), channel_id=1, source_target_pairs={{0,2},{1,3},{2,0},{3,1},{4,6},{5,7},{6,4},{7,5},{8,10},{9,11},{10,... | collective-permute-start | bytes 442376 | tf_op jit(solution)/shard_map/ppermute | solution.py:37
  188.9 5.0 %copy-start.23 = (bf16[144,3584]{1,0:T(8,128)(2,1)}, bf16[144,3584]{1,0:T(8,128)(2,1)S(1)}, u32[]{:S(2)}) copy-start(bf16[144,3584]{1,0:T(8,128)(2,1)S(1)} %get-tuple-element.147.refs_0_) | copy-start | bytes 3096580
  188.9 19.2 %collective-permute-start.32 = (bf16[144,3584]{1,0:T(8,128)(2,1)}, bf16[144,3584]{1,0:T(8,128)(2,1)S(1)}, u32[]{:S(2)}, u32[]{:S(2)}) collective-permute-start(bf16[144,3584]{1,0:T(8,128)(2,1)} %get-tuple-element.144), channel_id=1, source_target_pairs={{0,1},{1,0},{2,3},{3,2},{4,5},{5,4},{6,7},{7,6},{8,9},{9,8},{10,11... | collective-permute-start | bytes 3096584 | tf_op jit(solution)/shard_map/ppermute | solution.py:37
  193.9 2.7 %collective-permute-start.26 = (bf16[144,3584]{1,0:T(8,128)(2,1)S(1)}, bf16[144,3584]{1,0:T(8,128)(2,1)S(1)}, u32[]{:S(2)}, u32[]{:S(2)}) collective-permute-start(bf16[144,3584]{1,0:T(8,128)(2,1)S(1)} %get-tuple-element.137), channel_id=1, source_target_pairs={{0,1},{1,0},{2,3},{3,2},{4,5},{5,4},{6,7},{7,6},{8,9},{9,8},{10,11... | collective-permute-start | bytes 3096584 | tf_op jit(solution)/shard_map/ppermute | solution.py:37
  195.2 25.4 %collective-permute-start.36 = (bf16[144,3584]{1,0:T(8,128)(2,1)}, bf16[144,3584]{1,0:T(8,128)(2,1)S(1)}, u32[]{:S(2)}, u32[]{:S(2)}) collective-permute-start(bf16[144,3584]{1,0:T(8,128)(2,1)} %add_convert_fusion), channel_id=1, source_target_pairs={{0,2},{1,3},{2,0},{3,1},{4,6},{5,7},{6,4},{7,5},{8,10},{9,11},{10,... | collective-permute-start | bytes 3096584 | tf_op jit(solution)/shard_map/ppermute | solution.py:37
  198.5 26.9 %collective-permute-start.27 = (bf16[144,896]{1,0:T(8,128)(2,1)}, bf16[144,896]{1,0:T(8,128)(2,1)S(1)}, u32[]{:S(2)}, u32[]{:S(2)}) collective-permute-start(bf16[144,896]{1,0:T(8,128)(2,1)} %get-tuple-element.138), channel_id=1, source_target_pairs={{0,16},{1,17},{2,18},{3,19},{4,20},{5,21},{6,22},{7,23},{8,24},{9,... | collective-permute-start | bytes 774152 | tf_op jit(solution)/shard_map/ppermute | solution.py:33
  200.0 33.2 %collective-permute-start.28 = (bf16[144,896]{1,0:T(8,128)(2,1)}, bf16[144,896]{1,0:T(8,128)(2,1)S(1)}, u32[]{:S(2)}, u32[]{:S(2)}) collective-permute-start(bf16[144,896]{1,0:T(8,128)(2,1)} %get-tuple-element.139), channel_id=1, source_target_pairs={{0,28},{1,29},{2,30},{3,31},{4,16},{5,17},{6,18},{7,19},{8,20},{9,... | collective-permute-start | bytes 774152 | tf_op jit(solution)/shard_map/ppermute | solution.py:33
  207.8 25.4 %collective-permute-start.29 = (bf16[144,896]{1,0:T(8,128)(2,1)}, bf16[144,896]{1,0:T(8,128)(2,1)S(1)}, u32[]{:S(2)}, u32[]{:S(2)}) collective-permute-start(bf16[144,896]{1,0:T(8,128)(2,1)} %get-tuple-element.140), channel_id=1, source_target_pairs={{0,24},{1,25},{2,26},{3,27},{4,28},{5,29},{6,30},{7,31},{8,16},{9,... | collective-permute-start | bytes 774152 | tf_op jit(solution)/shard_map/ppermute | solution.py:33
  208.0 26.9 %collective-permute-start.30 = (bf16[144,896]{1,0:T(8,128)(2,1)S(1)}, bf16[144,896]{1,0:T(8,128)(2,1)}, u32[]{:S(2)}, u32[]{:S(2)}) collective-permute-start(bf16[144,896]{1,0:T(8,128)(2,1)S(1)} %get-tuple-element.141), channel_id=1, source_target_pairs={{0,20},{1,21},{2,22},{3,23},{4,24},{5,25},{6,26},{7,27},{8,28},{9,... | collective-permute-start | bytes 774152 | tf_op jit(solution)/shard_map/ppermute | solution.py:33
  220.6 1.2 copy-start.24
  223.9 18.4 %collective-permute-start.37 = (bf16[144,896]{1,0:T(8,128)(2,1)}, bf16[144,896]{1,0:T(8,128)(2,1)S(1)}, u32[]{:S(2)}, u32[]{:S(2)}) collective-permute-start(bf16[144,896]{1,0:T(8,128)(2,1)} %get-tuple-element.150), channel_id=1, source_target_pairs={{0,16},{1,17},{2,18},{3,19},{4,20},{5,21},{6,22},{7,23},{8,24},{9,... | collective-permute-start | bytes 774152 | tf_op jit(solution)/shard_map/ppermute | solution.py:33
  225.4 16.9 %collective-permute-start.38 = (bf16[144,896]{1,0:T(8,128)(2,1)}, bf16[144,896]{1,0:T(8,128)(2,1)S(1)}, u32[]{:S(2)}, u32[]{:S(2)}) collective-permute-start(bf16[144,896]{1,0:T(8,128)(2,1)} %get-tuple-element.151), channel_id=1, source_target_pairs={{0,28},{1,29},{2,30},{3,31},{4,16},{5,17},{6,18},{7,19},{8,20},{9,... | collective-permute-start | bytes 774152 | tf_op jit(solution)/shard_map/ppermute | solution.py:33
  233.2 22.1 %collective-permute-start.39 = (bf16[144,896]{1,0:T(8,128)(2,1)}, bf16[144,896]{1,0:T(8,128)(2,1)S(1)}, u32[]{:S(2)}, u32[]{:S(2)}) collective-permute-start(bf16[144,896]{1,0:T(8,128)(2,1)} %get-tuple-element.152), channel_id=1, source_target_pairs={{0,24},{1,25},{2,26},{3,27},{4,28},{5,29},{6,30},{7,31},{8,16},{9,... | collective-permute-start | bytes 774152 | tf_op jit(solution)/shard_map/ppermute | solution.py:33
  233.2 22.1 %collective-permute-start.40 = (bf16[144,896]{1,0:T(8,128)(2,1)}, bf16[144,896]{1,0:T(8,128)(2,1)S(1)}, u32[]{:S(2)}, u32[]{:S(2)}) collective-permute-start(bf16[144,896]{1,0:T(8,128)(2,1)} %get-tuple-element.153), channel_id=1, source_target_pairs={{0,20},{1,21},{2,22},{3,23},{4,24},{5,25},{6,26},{7,27},{8,28},{9,... | collective-permute-start | bytes 774152 | tf_op jit(solution)/shard_map/ppermute | solution.py:33
  234.9 20.4 %copy-start.12 = (bf16[128,3584]{1,0:T(8,128)(2,1)S(1)}, bf16[128,3584]{1,0:T(8,128)(2,1)}, u32[]{:S(2)}) copy-start(bf16[128,3584]{1,0:T(8,128)(2,1)} %copy-done.11) | copy-start | bytes 2752516
  234.9 1.3 copy-start.14
  (9 other events, 8.8 us)

commit v6 on v5

--- a/solution.py
+++ b/solution.py
@@ -204,22 +204,23 @@
     out_ref[...] = (gate_val / (1.0 + jnp.exp(-gate_val)) * up_val).astype(bf16)
 
 
-def output_body(own_ref, other_ref, down_ref, far_ref, first_out, second_out):
+def output_body(own_ref, other_ref, down_ref, top_ref, low_ref, first_out, second_out):
     half = first_out.shape[0]
     hidden = jnp.concatenate([own_ref[...], other_ref[...]], axis=1)
     step = 4 * LANES
     for n in range(0, down_ref.shape[1], step):
         part = slice(n, n + step)
-        weight = jnp.concatenate([down_ref[:, part], far_ref[:, part]], axis=0)
+        weight = jnp.concatenate([down_ref[:, part], top_ref[:, part], low_ref[:, part]], axis=0)
         value = dot(hidden, weight).astype(bf16)
         first_out[:, part] = value[:half]
         second_out[:, part] = value[half:]
 
 
-def down_back_body(first_ref, second_ref, down_ref, far_ref, own_out, other_out):
+def down_back_body(first_ref, second_ref, down_ref, top_ref, low_ref, own_out, other_out):
     grads = jnp.concatenate([first_ref[...], second_ref[...]], axis=0)
     own_out[...] = dot_last(grads, down_ref[...]).astype(own_out.dtype)
-    other_out[...] = dot_last(grads, far_ref[...]).astype(other_out.dtype)
+    far = jnp.concatenate([top_ref[...], low_ref[...]], axis=0)
+    other_out[...] = dot_last(grads, far).astype(other_out.dtype)
 
 
 def backward_body(first_ref, second_ref, back_ref, gate_ref, up_ref, first_out, second_out):
@@ -253,13 +254,14 @@
     kv0,
     kv1,
     kv2,
+    kv3,
     middle_ref,
     *refs,
 ):
     outs, (kv_all, kv_now, stack, attended) = refs[:experts], refs[experts:]
     tokens, width = query_ref.shape
     lead = 0
-    for ref in (kv0, kv1, kv2):
+    for ref in (kv0, kv1, kv2, kv3):
         kv_all[lead : lead + ref.shape[0], : ref.shape[1]] = ref[...]
         lead += ref.shape[0]
     attended[...] = jnp.zeros_like(attended)
@@ -388,8 +390,6 @@
     column = jnp.concatenate(column, axis=0)
     other_chip = swapped(column, 2)
     packed = after(packed, [column])
-    down_other = swapped(w_down, 2)
-    downs = (w_down, down_other)
 
     front_small = jnp.concatenate([front_from.astype(f32), front_gate[0]], axis=0).reshape(1, -1)
     back_small = jnp.concatenate([back_from.astype(f32).reshape(1, -1), norm_gain], axis=1)
@@ -420,9 +420,12 @@
     for k in range(1, first):
         row_chunks[k] = turned(row_chunks[k], k)
     arrived = row_chunks[1:first]
-    there_back_middle = passed_along(after([back_middle[0]], [packed[0]])[0], -1)
-    chip = jnp.concatenate([column, other_chip], axis=0)
-    kv = [column, other_chip, swapped(after([chip], arrived + [there_back_middle])[0], 1)]
+    cut = hidden_width * 5 // 8
+    (down_top,) = after([w_down[:cut]], arrived[:1])
+    down_top = swapped(down_top, 2)
+    there_back_middle = passed_along(after([back_middle[0]], arrived)[0], -1)
+    far = swapped(after([other_chip], arrived)[0], 1)
+    kv = [column, other_chip, swapped(column, 1), far]
     for k in range(first, experts):
         row_chunks[k] = turned(after([row_chunks[k]], arrived)[0], k)
     beside = range(1, 2)
@@ -455,14 +458,16 @@
     middle, front_chunks = result[0], result[1:]
     ready = row_chunks + [grad_chunks[k] for k in beside]
     front_chunks = sent(after(front_chunks, ready))
-    back_rows = joined(after(ready, [middle, there_back_grad])[:experts])
-    back_pieces = pieces_of(after([back_rows], [down_other])[0])
-    there_middle = passed_along(after([middle], [back_rows])[0], 1)
+    back_rows = joined(after(ready, [middle, there_back_middle])[:experts])
+    back_pieces = pieces_of(after([back_rows], [down_top])[0])
+    down_low = swapped(after([w_down[cut:]], [back_pieces[2]])[0], 2)
+    downs = (w_down, down_top, down_low)
     for k in range(1, experts):
         if k not in beside:
             grad_chunks[k] = turned(after([grad_chunks[k]], front_chunks)[0], k)
-    front_near = joined(after(front_chunks, [there_middle, back_pieces[2]]))
-    front_other = swapped(front_near, 2)
+    front_near = joined(after(front_chunks, [there_back_grad, back_pieces[2]]))
+    there_middle = passed_along(after([middle], [front_near])[0], 1)
+    front_other = swapped(after([front_near], [down_low])[0], 2)
 
     front_small, back_small = after([front_small, back_small], [front_near])
     there_small = passed_along(front_small, 1)
@@ -471,7 +476,7 @@
     there_front_gate = there_small[0, tokens:].reshape(tokens, 1)
     there_back_from = there_back_small[0, :tokens].astype(jnp.int32).reshape(tokens, 1)
     there_gain = there_back_small[:, tokens:]
-    grad_near = joined(after(grad_chunks, [there_small, there_back_small]))
+    grad_near = joined(after(grad_chunks, [there_small, there_back_small, there_middle]))
     grad_near = [grad_near, swapped(grad_near, 1)]
 
     work = 2 * 2 * slots * width * hidden_width

time: 260 us -> 224 us (0.86)
  waiting for transfers between devices: 133 us -> 110 us
  local copies, waits for them, and re-layouts: 20.9 us -> 10.3 us
  starting transfers between devices: 62.5 us -> 59.5 us
    ppermute x16 -> x18, waiting for transfers between devices: 87.4 us -> 45.4 us  [swapped(): lax.ppermute(array, 'expert', [(i, i ^ bit) for i in range(lax.axis_size(...]
    ppermute x9, waiting for transfers between devices: 22.5 us -> 39.1 us  [turned(): lax.ppermute(array, 'expert', [(i, (i + by * GROUP) % length) for i in ra...]
    unnamed x69 -> x68, local copies, waits for them, and re-layouts: 15.2 us -> 8.01 us
    ppermute x9, starting transfers between devices: 18.1 us -> 14 us  [turned(): lax.ppermute(array, 'expert', [(i, (i + by * GROUP) % length) for i in ra...]
    ppermute x13, waiting for transfers between devices: 22.9 us -> 25.7 us  [passed_along(): return lax.ppermute(array, ('section', 'expert'), pairs)]
    ppermute x16 -> x18, starting transfers between devices: 7.02 us -> 9.25 us  [swapped(): lax.ppermute(array, 'expert', [(i, i ^ bit) for i in range(lax.axis_size(...]
  transfers between devices with their start and end apart: 41 -> 43, of which waited for: 13 -> 19; matrix products, arithmetic and copies ran while one was open for 3% -> 2% of each run, Pallas kernels for 13% -> 16%
where the time goes in v6:
time: 224 us
  waiting for transfers between devices  110 us (49%)
  starting transfers between devices  59.5 us (27%)
  Pallas kernels  40.5 us (18%)
  local copies, waits for them, and re-layouts  10.3 us (5%)
    ppermute x18, waiting for transfers between devices, swapped(): lax.ppermute(array, 'expert', [(i, i ^ bit) for i in range(lax.axis_size(...  45.4 us
    pallas_call x15, Pallas kernels, call(): pl.pallas_call(body, out_shape=shapes, in_specs=specs, out_specs=[pl.Bloc...  40.5 us
    ppermute x9, waiting for transfers between devices, turned(): lax.ppermute(array, 'expert', [(i, (i + by * GROUP) % length) for i in ra...  39.1 us
    ppermute x13, waiting for transfers between devices, passed_along(): return lax.ppermute(array, ('section', 'expert'), pairs)  25.7 us
    ppermute x13, starting transfers between devices, passed_along(): return lax.ppermute(array, ('section', 'expert'), pairs)  25.5 us
    ppermute x9, starting transfers between devices, turned(): lax.ppermute(array, 'expert', [(i, (i + by * GROUP) % length) for i in ra...  14 us
    ppermute x3, starting transfers between devices, shards(): column.append(lax.ppermute(keys_values[0], 'expert', pairs))  10.7 us
    ppermute x18, starting transfers between devices, swapped(): lax.ppermute(array, 'expert', [(i, i ^ bit) for i in range(lax.axis_size(...  9.25 us
  transfers between devices with their start and end apart: 43, of which 19 were waited for; matrix products, arithmetic and copies ran while one was open for 2% of the time, Pallas kernels for 16%

profile of v6, /device:TPU:0, one launch (start us, length us, event | category | flops | bytes accessed | tf_op | source)
XLA Modules:
  0.0 223.7 jit_solution(17335808081761610335)
XLA Ops:
  0.6 1.0 copy.16
  1.6 4.9 %collective-permute-start = (bf16[128,448]{1,0:T(8,128)(2,1)S(1)}, bf16[128,448]{1,0:T(8,128)(2,1)S(1)}, u32[]{:S(2)}, u32[]{:S(2)}) collective-permute-start(bf16[128,448]{1,0:T(8,128)(2,1)S(1)} %bitcast.46), channel_id=1, source_target_pairs={{0,4},{1,5},{2,6},{3,7},{4,8},{5,9},{6,10},{7,11},{8,12},{9,13},{1... | collective-permute-start | bytes 344072 | tf_op jit(solution)/shard_map/ppermute | solution.py:377
  6.6 4.5 %collective-permute-start.1 = (bf16[128,448]{1,0:T(8,128)(2,1)S(1)}, bf16[128,448]{1,0:T(8,128)(2,1)S(1)}, u32[]{:S(2)}, u32[]{:S(2)}) collective-permute-start(bf16[128,448]{1,0:T(8,128)(2,1)S(1)} %bitcast.47), channel_id=1, source_target_pairs={{0,8},{1,9},{2,10},{3,11},{4,12},{5,13},{6,14},{7,15},{16,24},{17,... | collective-permute-start | bytes 344072 | tf_op jit(solution)/shard_map/ppermute | solution.py:377
  11.1 1.3 collective-permute-start.2
  12.4 0.8 copy.17.gate_ref
  14.6 1.2 copy-done.7
  15.7 3.0 %shard_map.149 = (bf16[144,896]{1,0:T(8,128)(2,1)S(1)}, bf16[144,896]{1,0:T(8,128)(2,1)S(1)}, bf16[144,896]{1,0:T(8,128)(2,1)S(1)}, bf16[144,896]{1,0:T(8,128)(2...) custom-call(s32[1,128]{1,0:T(1,128)S(1)} %get-tuple-element.169.rout, ...), custom_call_target="tpu_custom_call" | custom-call | flops 2113929216 | bytes 3914752 | tf_op jit(solution)/shard_map/pallas_call | solution.py:55
  19.0 1.6 collective-permute-start.3
  20.9 3.4 %collective-permute-start.6 = (bf16[144,896]{1,0:T(8,128)(2,1)S(1)}, bf16[144,896]{1,0:T(8,128)(2,1)S(1)}, u32[]{:S(2)}, u32[]{:S(2)}) collective-permute-start(bf16[144,896]{1,0:T(8,128)(2,1)S(1)} %get-tuple-element.98), channel_id=1, source_target_pairs={{0,8},{1,9},{2,10},{3,11},{4,12},{5,13},{6,14},{7,15},{8,0},{9,1},... | collective-permute-start | bytes 774152 | tf_op jit(solution)/shard_map/ppermute | solution.py:42
  24.3 1.1 slice_bitcast_fusion
  25.4 6.1 %collective-permute-done.5.refs_1_ = bf16[144,896]{1,0:T(8,128)(2,1)S(1)} collective-permute-done((bf16[144,896]{1,0:T(8,128)(2,1)S(1)}, bf16[144,896]{1,0:T(8,128)(2,1)S(1)}, u32[]{:S(2)}, u32[]{:S(2)}) %collective-permute-start.5) | collective-permute-done | bytes 258080 | tf_op jit(solution)/shard_map/ppermute | solution.py:42
  32.8 7.7 %collective-permute-done.6.refs_2_ = bf16[144,896]{1,0:T(8,128)(2,1)S(1)} collective-permute-done((bf16[144,896]{1,0:T(8,128)(2,1)S(1)}, bf16[144,896]{1,0:T(8,128)(2,1)S(1)}, u32[]{:S(2)}, u32[]{:S(2)}) %collective-permute-start.6) | collective-permute-done | bytes 258080 | tf_op jit(solution)/shard_map/ppermute | solution.py:42
  41.2 1.5 collective-permute-start.13
  43.5 1.3 collective-permute-done.4.kv2
  44.8 0.8 collective-permute-start.9
  45.7 1.2 copy-done.5
  46.9 1.2 copy-done.6
  48.1 8.4 %shard_map.150 = (bf16[128,3584]{1,0:T(8,128)(2,1)S(1)}, bf16[144,896]{1,0:T(8,128)(2,1)S(1)}, bf16[144,896]{1,0:T(8,128)(2,1)S(1)}, bf16[144,896]{1,0:T(8,128)(2,1)S(1)}, bf16[144,896]{1,0:T(8,128)(2,1)S(1)}) custom-call(s32[16]{0:T(128)S(1)} %reshape_squeeze.6.chosen_ref, s32[16]{0:T(128)S(1)} %fusion.10.index_ref, s32[1]{0:T(128)} %bitcast.4.base_ref, ...), custom_call_target="tpu_custom_call" | custom-call | flops 1593835520 | bytes 5634692 | tf_op jit(solution)/shard_map/pallas_call | solution.py:55
  56.5 1.0 collective-permute-done.8.refs_3_
  57.5 6.3 %collective-permute-done.13.middle_ref = bf16[128,3584]{1,0:T(8,128)(2,1)} collective-permute-done((bf16[128,3584]{1,0:T(8,128)(2,1)}, bf16[128,3584]{1,0:T(8,128)(2,1)}, u32[]{:S(2)}, u32[]{:S(2)}) %collective-permute-start.13) | collective-permute-done | bytes 917536 | tf_op jit(solution)/shard_map/ppermute | solution.py:33
  63.8 2.1 shard_map.151.first_ref
  66.6 1.5 collective-permute-start.14
  68.2 3.7 %collective-permute-start.12 = (bf16[144,896]{1,0:T(8,128)(2,1)S(1)}, bf16[144,896]{1,0:T(8,128)(2,1)S(1)}, u32[]{:S(2)}, u32[]{:S(2)}) collective-permute-start(bf16[144,896]{1,0:T(8,128)(2,1)S(1)} %get-tuple-element.112), channel_id=1, source_target_pairs={{0,12},{1,13},{2,14},{3,15},{4,0},{5,1},{6,2},{7,3},{8,4},{9,5},{1... | collective-permute-start | bytes 774152 | tf_op jit(solution)/shard_map/ppermute | solution.py:42
  72.0 7.2 %collective-permute-done.10.refs_1_ = bf16[144,896]{1,0:T(8,128)(2,1)S(1)} collective-permute-done((bf16[144,896]{1,0:T(8,128)(2,1)S(1)}, bf16[144,896]{1,0:T(8,128)(2,1)S(1)}, u32[]{:S(2)}, u32[]{:S(2)}) %collective-permute-start.10) | collective-permute-done | bytes 258080 | tf_op jit(solution)/shard_map/ppermute | solution.py:42
  79.2 8.7 %collective-permute-done.11.refs_2_ = bf16[144,896]{1,0:T(8,128)(2,1)S(1)} collective-permute-done((bf16[144,896]{1,0:T(8,128)(2,1)S(1)}, bf16[144,896]{1,0:T(8,128)(2,1)S(1)}, u32[]{:S(2)}, u32[]{:S(2)}) %collective-permute-start.11) | collective-permute-done | bytes 258080 | tf_op jit(solution)/shard_map/ppermute | solution.py:42
  87.9 2.0 collective-permute-done.16.first_ref
  89.9 1.1 shard_map.152.first_ref
  91.0 1.6 collective-permute-start.18
  93.3 2.1 collective-permute-start.22
  95.4 3.4 %collective-permute-start.23 = (bf16[144,896]{1,0:T(8,128)(2,1)S(1)}, bf16[144,896]{1,0:T(8,128)(2,1)S(1)}, u32[]{:S(2)}, u32[]{:S(2)}) collective-permute-start(bf16[144,896]{1,0:T(8,128)(2,1)S(1)} %copy-done.14), channel_id=1, source_target_pairs={{0,12},{1,13},{2,14},{3,15},{4,0},{5,1},{6,2},{7,3},{8,4},{9,5},{1... | collective-permute-start | bytes 774152 | tf_op jit(solution)/shard_map/ppermute | solution.py:42
  98.8 1.6 collective-permute-start.24
  100.4 8.3 %collective-permute-done.22.refs_2_ = bf16[144,896]{1,0:T(8,128)(2,1)S(1)} collective-permute-done((bf16[144,896]{1,0:T(8,128)(2,1)S(1)}, bf16[144,896]{1,0:T(8,128)(2,1)S(1)}, u32[]{:S(2)}, u32[]{:S(2)}) %collective-permute-start.22) | collective-permute-done | bytes 258080 | tf_op jit(solution)/shard_map/ppermute | solution.py:42
  108.7 1.0 collective-permute-start.17
  109.6 2.6 %collective-permute-done.17 = f32[1,256]{1,0:T(1,128)S(1)} collective-permute-done((f32[1,256]{1,0:T(1,128)S(1)}, f32[1,256]{1,0:T(1,128)S(1)}, u32[]{:S(2)}, u32[]{:S(2)}) %collective-permute-start.17) | collective-permute-done | bytes 1056 | tf_op jit(solution)/shard_map/ppermute | solution.py:33
  112.3 2.3 %shard_map.154.first_ref = bf16[144,3584]{1,0:T(8,128)(2,1)S(1)} custom-call(bf16[144,896]{1,0:T(8,128)(2,1)S(1)} %copy-done.26, bf16[144,896]{1,0:T(8,128)(2,1)} %collective-permute-done.9.refs_1_, bf16[144,896]{1,0:T(8,128)(2,1)S(1)} %collective-permute-done.22.refs_2_, bf16[144,896]{1,0:T(8,128)(2,1)S(1)} %collective-permute-done.23.refs_3_), custom_call_target="tpu_custom_call" | custom-call | flops 1056964608 | bytes 2064384 | tf_op jit(solution)/shard_map/pallas_call | solution.py:55
  114.7 1.1 collective-permute-start.21
  116.3 1.0 collective-permute-done.25.second_ref
  117.3 1.3 shard_map.155
  118.6 21.3 %collective-permute-done.21.first_ref = bf16[144,3584]{1,0:T(8,128)(2,1)S(1)} collective-permute-done((bf16[144,3584]{1,0:T(8,128)(2,1)S(1)}, bf16[144,3584]{1,0:T(8,128)(2,1)S(1)}, u32[]{:S(2)}, u32[]{:S(2)}) %collective-permute-start.21) | collective-permute-done | bytes 1032224 | tf_op jit(solution)/shard_map/ppermute | solution.py:37
  139.9 1.0 collective-permute-start.36
  141.2 5.0 %collective-permute-done.36.back_ref = bf16[288,256]{1,0:T(8,128)(2,1)S(1)} collective-permute-done((bf16[288,256]{1,0:T(8,128)(2,1)S(1)}, bf16[288,256]{1,0:T(8,128)(2,1)S(1)}, u32[]{:S(2)}, u32[]{:S(2)}) %collective-permute-start.36) | collective-permute-done | bytes 147488 | tf_op jit(solution)/shard_map/ppermute | solution.py:37
  146.2 2.5 %shard_map.160 = (bf16[144,3584]{1,0:T(8,128)(2,1)S(1)}, bf16[144,3584]{1,0:T(8,128)(2,1)S(1)}) custom-call(bf16[144,3584]{1,0:T(8,128)(2,1)S(1)} %collective-permute-done.16.first_ref, bf16[144,3584]{1,0:T(8,128)(2,1)S(1)} %collective-permute-done.35.second_ref, bf16[288,256]{1,0:T(8,128)(2,1)S(1)} %collective-permute-done.36.back_ref, ...), custom_call_target="tpu_custom_call" | custom-call | flops 2113929216 | bytes 7946240 | tf_op jit(solution)/shard_map/pallas_call | solution.py:55
  148.7 1.3 shard_map.153.own_ref
  150.0 1.3 shard_map.156
  151.3 1.1 collective-permute-start.27
  152.4 3.4 %shard_map.159 = (bf16[144,3584]{1,0:T(8,128)(2,1)S(1)}, bf16[144,3584]{1,0:T(8,128)(2,1)}) custom-call(bf16[144,3584]{1,0:T(8,128)(2,1)S(1)} %shard_map.151.first_ref, bf16[144,3584]{1,0:T(8,128)(2,1)S(1)} %collective-permute-done.33.second_ref, f32[288,256]{1,0:T(8,128)S(1)} %get-tuple-element.148.back_ref, bf16[3584,256]{1,0:T(8,128)(2,1)S(1)} %bitcast.37, ...), custom_call_target="tpu_custom_call" | custom-call | flops 2113929216 | bytes 8093696 | tf_op jit(solution)/shard_map/pallas_call | solution.py:55
  156.0 1.6 collective-permute-done.27.other_ref
  157.6 1.2 shard_map.157
  158.9 1.2 add_convert_fusion
  160.1 1.0 collective-permute-start.38
  161.5 1.9 shard_map.158
  163.4 1.2 collective-permute-start.29
  164.6 6.4 %collective-permute-start.30 = (bf16[144,896]{1,0:T(8,128)(2,1)}, bf16[144,896]{1,0:T(8,128)(2,1)S(1)}, u32[]{:S(2)}, u32[]{:S(2)}) collective-permute-start(bf16[144,896]{1,0:T(8,128)(2,1)} %get-tuple-element.145), channel_id=1, source_target_pairs={{0,28},{1,29},{2,30},{3,31},{4,16},{5,17},{6,18},{7,19},{8,20},{9,... | collective-permute-start | bytes 774152 | tf_op jit(solution)/shard_map/ppermute | solution.py:33
  171.2 1.6 collective-permute-start.32
  172.8 12.7 %collective-permute-done.38.refs_2_ = bf16[144,3584]{1,0:T(8,128)(2,1)S(1)} collective-permute-done((bf16[144,3584]{1,0:T(8,128)(2,1)}, bf16[144,3584]{1,0:T(8,128)(2,1)S(1)}, u32[]{:S(2)}, u32[]{:S(2)}) %collective-permute-start.38) | collective-permute-done | bytes 1032224 | tf_op jit(solution)/shard_map/ppermute | solution.py:37
  185.5 1.2 copy-done.24
  186.8 3.2 %shard_map.161 = (bf16[144,896]{1,0:T(8,128)(2,1)}, bf16[144,896]{1,0:T(8,128)(2,1)S(1)}, bf16[144,896]{1,0:T(8,128)(2,1)}, bf16[144,896]{1,0:T(8,128)(2,1)}) custom-call(bf16[144,3584]{1,0:T(8,128)(2,1)S(1)} %copy-done.24, bf16[144,3584]{1,0:T(8,128)(2,1)} %collective-permute-done.34.refs_1_, bf16[144,3584]{1,0:T(8,128)(2,1)S(1)} %collective-permute-done.38.refs_2_), custom_call_target="tpu_custom_call" | custom-call | flops 1056964608 | bytes 4128768 | tf_op jit(solution)/shard_map/pallas_call | solution.py:55
  190.0 1.2 collective-permute-start.39
  191.3 6.4 %collective-permute-start.40 = (bf16[144,896]{1,0:T(8,128)(2,1)S(1)}, bf16[144,896]{1,0:T(8,128)(2,1)}, u32[]{:S(2)}, u32[]{:S(2)}) collective-permute-start(bf16[144,896]{1,0:T(8,128)(2,1)S(1)} %get-tuple-element.157), channel_id=1, source_target_pairs={{0,28},{1,29},{2,30},{3,31},{4,16},{5,17},{6,18},{7,19},{8,20},{9,... | collective-permute-start | bytes 774152 | tf_op jit(solution)/shard_map/ppermute | solution.py:33
  197.6 1.6 collective-permute-start.42
  199.4 3.4 %shard_map.162 = bf16[128,3584]{1,0:T(8,128)(2,1)} custom-call(s32[128,1]{1,0:T(8,128)S(1)} %copy.18.route_ref, f32[128,1]{1,0:T(8,128)S(1)} %copy.19.gate_ref, bf16[128,3584]{1,0:T(8,128)(2,1)S(1)} %copy-done.12, bf16[144,896]{1,0:T(8,128)(2,1)S(1)} %collective-permute-done.29.refs_0_, bf16[144,896]{1,0:T(8,128)(2,1)S(1)} %collective-permute-done.30.refs_1_, ...), custom_call_target="tpu_custom_call" | custom-call | flops 1056964608 | bytes 2868224 | tf_op jit(solution)/shard_map/pallas_call | solution.py:55
  202.8 2.7 %collective-permute-done.39.refs_0_ = bf16[144,896]{1,0:T(8,128)(2,1)S(1)} collective-permute-done((bf16[144,896]{1,0:T(8,128)(2,1)}, bf16[144,896]{1,0:T(8,128)(2,1)S(1)}, u32[]{:S(2)}, u32[]{:S(2)}) %collective-permute-start.39) | collective-permute-done | bytes 258080 | tf_op jit(solution)/shard_map/ppermute | solution.py:33
  205.5 14.1 %collective-permute-done.41.refs_2_ = bf16[144,896]{1,0:T(8,128)(2,1)} collective-permute-done((bf16[144,896]{1,0:T(8,128)(2,1)}, bf16[144,896]{1,0:T(8,128)(2,1)}, u32[]{:S(2)}, u32[]{:S(2)}) %collective-permute-start.41) | collective-permute-done | bytes 258080 | tf_op jit(solution)/shard_map/ppermute | solution.py:33
  219.6 4.1 %shard_map.163 = bf16[128,3584]{1,0:T(8,128)(2,1)} custom-call(s32[128,1]{1,0:T(8,128)S(1)} %copy.20.route_ref, f32[1,3584]{1,0:T(1,128)S(1)} %slice.35.gain_ref, bf16[128,3584]{1,0:T(8,128)(2,1)} %collective-permute-done.13.middle_ref, bf16[128,3584]{1,0:T(8,128)(2,1)S(1)} %copy-done.10, bf16[144,896]{1,0:T(8,128)(2,1)S(1)} %collective-permute-done.39.refs_0_, ...), custom_call_target="tpu_custom_call" | custom-call | flops 1056964608 | bytes 3799552 | tf_op jit(solution)/shard_map/pallas_call | solution.py:55
  (123 shorter events, 8.1 us)
Async XLA Ops:
  1.6 17.2 %collective-permute-start = (bf16[128,448]{1,0:T(8,128)(2,1)S(1)}, bf16[128,448]{1,0:T(8,128)(2,1)S(1)}, u32[]{:S(2)}, u32[]{:S(2)}) collective-permute-start(bf16[128,448]{1,0:T(8,128)(2,1)S(1)} %bitcast.46), channel_id=1, source_target_pairs={{0,4},{1,5},{2,6},{3,7},{4,8},{5,9},{6,10},{7,11},{8,12},{9,13},{1... | collective-permute-start | bytes 344072 | tf_op jit(solution)/shard_map/ppermute | solution.py:377
  6.6 12.3 %collective-permute-start.1 = (bf16[128,448]{1,0:T(8,128)(2,1)S(1)}, bf16[128,448]{1,0:T(8,128)(2,1)S(1)}, u32[]{:S(2)}, u32[]{:S(2)}) collective-permute-start(bf16[128,448]{1,0:T(8,128)(2,1)S(1)} %bitcast.47), channel_id=1, source_target_pairs={{0,8},{1,9},{2,10},{3,11},{4,12},{5,13},{6,14},{7,15},{16,24},{17,... | collective-permute-start | bytes 344072 | tf_op jit(solution)/shard_map/ppermute | solution.py:377
  11.1 7.8 %collective-permute-start.2 = (bf16[128,448]{1,0:T(8,128)(2,1)S(1)}, bf16[128,448]{1,0:T(8,128)(2,1)S(1)}, u32[]{:S(2)}, u32[]{:S(2)}) collective-permute-start(bf16[128,448]{1,0:T(8,128)(2,1)S(1)} %bitcast.48), channel_id=1, source_target_pairs={{0,12},{1,13},{2,14},{3,15},{16,28},{17,29},{18,30},{19,31}} | collective-permute-start | bytes 344072 | tf_op jit(solution)/shard_map/ppermute | solution.py:377
  15.7 8.6 %copy-start = (bf16[1,1,256,3584]{3,2,1,0:T(8,128)(2,1)S(1)}, bf16[1,1,256,3584]{3,2,1,0:T(8,128)(2,1)}, u32[]{:S(2)}) copy-start(bf16[1,1,256,3584]{3,2,1,0:T(8,128)(2,1)} %param.27) | copy-start | bytes 5505028
  18.8 24.0 %copy-start.13 = (bf16[144,896]{1,0:T(8,128)(2,1)}, bf16[144,896]{1,0:T(8,128)(2,1)S(1)}, u32[]{:S(2)}) copy-start(bf16[144,896]{1,0:T(8,128)(2,1)S(1)} %get-tuple-element.134) | copy-start | bytes 774148
  18.8 24.0 %copy-start.15 = (bf16[144,896]{1,0:T(8,128)(2,1)}, bf16[144,896]{1,0:T(8,128)(2,1)S(1)}, u32[]{:S(2)}) copy-start(bf16[144,896]{1,0:T(8,128)(2,1)S(1)} %get-tuple-element.132) | copy-start | bytes 774148
  18.8 24.0 %copy-start.17 = (bf16[144,896]{1,0:T(8,128)(2,1)}, bf16[144,896]{1,0:T(8,128)(2,1)S(1)}, u32[]{:S(2)}) copy-start(bf16[144,896]{1,0:T(8,128)(2,1)S(1)} %get-tuple-element.108) | copy-start | bytes 774148
  18.8 24.0 %copy-start.18 = (bf16[144,896]{1,0:T(8,128)(2,1)}, bf16[144,896]{1,0:T(8,128)(2,1)S(1)}, u32[]{:S(2)}) copy-start(bf16[144,896]{1,0:T(8,128)(2,1)S(1)} %get-tuple-element.106) | copy-start | bytes 774148
  18.8 24.0 %copy-start.25 = (bf16[144,896]{1,0:T(8,128)(2,1)}, bf16[144,896]{1,0:T(8,128)(2,1)S(1)}, u32[]{:S(2)}) copy-start(bf16[144,896]{1,0:T(8,128)(2,1)S(1)} %get-tuple-element.136.refs_0_) | copy-start | bytes 774148
  18.8 24.0 %copy-start.27 = (bf16[144,896]{1,0:T(8,128)(2,1)}, bf16[144,896]{1,0:T(8,128)(2,1)S(1)}, u32[]{:S(2)}) copy-start(bf16[144,896]{1,0:T(8,128)(2,1)S(1)} %get-tuple-element.116.refs_0_) | copy-start | bytes 774148
  18.8 24.5 %copy-start.29 = (s32[1,2,2,4]{3,2,1,0:T(2,128)S(1)}, s32[1,2,2,4]{3,2,1,0:T(2,128)}, u32[]{:S(2)}) copy-start(s32[1,2,2,4]{3,2,1,0:T(2,128)} %param.17) | copy-start | bytes 196
  18.8 24.6 %copy-start.31 = (s32[1,128,1]{1,2,0:T(1,128)S(1)}, s32[1,128,1]{1,2,0:T(1,128)}, u32[]{:S(2)}) copy-start(s32[1,128,1]{1,2,0:T(1,128)} %param.18) | copy-start | bytes 1540
  18.8 26.9 %copy-start.4 = (f32[1,3584]{1,0:T(1,128)S(1)}, f32[1,3584]{1,0:T(1,128)}, u32[]{:S(2)}) copy-start(f32[1,3584]{1,0:T(1,128)} %gain_ref.3) | copy-start | bytes 43012
  19.0 23.8 %collective-permute-start.3 = (bf16[512,448]{1,0:T(8,128)(2,1)S(1)}, bf16[512,448]{1,0:T(8,128)(2,1)}, u32[]{:S(2)}, u32[]{:S(2)}) collective-permute-start(bf16[512,448]{1,0:T(8,128)(2,1)S(1)} %constant_dynamic-update-slice_fusion.kv0), channel_id=1, source_target_pairs={{0,2},{1,3},{2,0},{3,1},{4,6},{5,7},{6,4},{7,5},{8,10},{9,11},{10,... | collective-permute-start | bytes 1376264 | tf_op jit(solution)/shard_map/ppermute | solution.py:37
  20.5 11.0 %collective-permute-start.5 = (bf16[144,896]{1,0:T(8,128)(2,1)S(1)}, bf16[144,896]{1,0:T(8,128)(2,1)S(1)}, u32[]{:S(2)}, u32[]{:S(2)}) collective-permute-start(bf16[144,896]{1,0:T(8,128)(2,1)S(1)} %get-tuple-element.97), channel_id=1, source_target_pairs={{0,4},{1,5},{2,6},{3,7},{4,8},{5,9},{6,10},{7,11},{8,12},{9,13},{1... | collective-permute-start | bytes 774152 | tf_op jit(solution)/shard_map/ppermute | solution.py:42
  20.9 19.6 %collective-permute-start.6 = (bf16[144,896]{1,0:T(8,128)(2,1)S(1)}, bf16[144,896]{1,0:T(8,128)(2,1)S(1)}, u32[]{:S(2)}, u32[]{:S(2)}) collective-permute-start(bf16[144,896]{1,0:T(8,128)(2,1)S(1)} %get-tuple-element.98), channel_id=1, source_target_pairs={{0,8},{1,9},{2,10},{3,11},{4,12},{5,13},{6,14},{7,15},{8,0},{9,1},... | collective-permute-start | bytes 774152 | tf_op jit(solution)/shard_map/ppermute | solution.py:42
  32.2 33.7 %collective-permute-start.15 = (bf16[160,3584]{1,0:T(8,128)(2,1)}, bf16[160,3584]{1,0:T(8,128)(2,1)S(1)}, u32[]{:S(2)}, u32[]{:S(2)}) collective-permute-start(bf16[160,3584]{1,0:T(8,128)(2,1)} %slice_bitcast_fusion), channel_id=1, source_target_pairs={{0,2},{1,3},{2,0},{3,1},{4,6},{5,7},{6,4},{7,5},{8,10},{9,11},{10,... | collective-permute-start | bytes 3440648 | tf_op jit(solution)/shard_map/ppermute | solution.py:37
  41.2 22.6 %collective-permute-start.13 = (bf16[128,3584]{1,0:T(8,128)(2,1)}, bf16[128,3584]{1,0:T(8,128)(2,1)}, u32[]{:S(2)}, u32[]{:S(2)}) collective-permute-start(bf16[128,3584]{1,0:T(8,128)(2,1)} %bitcast.10.middle_ref), channel_id=1, source_target_pairs={{0,16},{1,17},{2,18},{3,19},{4,20},{5,21},{6,22},{7,23},{8,24},{9,... | collective-permute-start | bytes 2752520 | tf_op jit(solution)/shard_map/ppermute | solution.py:33
  42.7 2.0 collective-permute-start.4
  42.8 2.9 %collective-permute-start.7 = (bf16[512,448]{1,0:T(8,128)(2,1)}, bf16[512,448]{1,0:T(8,128)(2,1)}, u32[]{:S(2)}, u32[]{:S(2)}) collective-permute-start(bf16[512,448]{1,0:T(8,128)(2,1)} %collective-permute-done.3.kv1), channel_id=1, source_target_pairs={{0,1},{1,0},{2,3},{3,2},{4,5},{5,4},{6,7},{7,6},{8,9},{9,8},{10,11... | collective-permute-start | bytes 1376264 | tf_op jit(solution)/shard_map/ppermute | solution.py:37
  43.4 14.0 %collective-permute-start.8 = (bf16[144,896]{1,0:T(8,128)(2,1)}, bf16[144,896]{1,0:T(8,128)(2,1)}, u32[]{:S(2)}, u32[]{:S(2)}) collective-permute-start(bf16[144,896]{1,0:T(8,128)(2,1)} %copy-done.18), channel_id=1, source_target_pairs={{0,12},{1,13},{2,14},{3,15},{4,0},{5,1},{6,2},{7,3},{8,4},{9,5},{1... | collective-permute-start | bytes 774152 | tf_op jit(solution)/shard_map/ppermute | solution.py:42
  44.8 12.7 %collective-permute-start.9 = (bf16[144,896]{1,0:T(8,128)(2,1)}, bf16[144,896]{1,0:T(8,128)(2,1)}, u32[]{:S(2)}, u32[]{:S(2)}) collective-permute-start(bf16[144,896]{1,0:T(8,128)(2,1)} %copy-done.17), channel_id=1, source_target_pairs={{0,4},{1,5},{2,6},{3,7},{4,8},{5,9},{6,10},{7,11},{8,12},{9,13},{1... | collective-permute-start | bytes 774152 | tf_op jit(solution)/shard_map/ppermute | solution.py:42
  48.1 15.7 %copy-start.20 = (bf16[144,896]{1,0:T(8,128)(2,1)S(1)}, bf16[144,896]{1,0:T(8,128)(2,1)}, u32[]{:S(2)}) copy-start(bf16[144,896]{1,0:T(8,128)(2,1)} %copy-done.19) | copy-start | bytes 774148
  48.1 15.7 %copy-start.22 = (bf16[144,896]{1,0:T(8,128)(2,1)S(1)}, bf16[144,896]{1,0:T(8,128)(2,1)}, u32[]{:S(2)}) copy-start(bf16[144,896]{1,0:T(8,128)(2,1)} %copy-done.21) | copy-start | bytes 774148
  48.1 15.7 %copy-start.28 = (bf16[144,896]{1,0:T(8,128)(2,1)S(1)}, bf16[144,896]{1,0:T(8,128)(2,1)}, u32[]{:S(2)}) copy-start(bf16[144,896]{1,0:T(8,128)(2,1)} %copy-done.27) | copy-start | bytes 774148
  66.0 23.9 %collective-permute-start.16 = (bf16[144,3584]{1,0:T(8,128)(2,1)S(1)}, bf16[144,3584]{1,0:T(8,128)(2,1)S(1)}, u32[]{:S(2)}, u32[]{:S(2)}) collective-permute-start(bf16[144,3584]{1,0:T(8,128)(2,1)S(1)} %shard_map.151.first_ref), channel_id=1, source_target_pairs={{0,2},{1,3},{2,0},{3,1},{4,6},{5,7},{6,4},{7,5},{8,10},{9,11},{10,... | collective-permute-start | bytes 3096584 | tf_op jit(solution)/shard_map/ppermute | solution.py:37
  66.6 21.4 %collective-permute-start.14 = (bf16[128,3584]{1,0:T(8,128)(2,1)S(1)}, bf16[128,3584]{1,0:T(8,128)(2,1)S(1)}, u32[]{:S(2)}, u32[]{:S(2)}) collective-permute-start(bf16[128,3584]{1,0:T(8,128)(2,1)S(1)} %bitcast.45), channel_id=1, source_target_pairs={{0,16},{1,17},{2,18},{3,19},{4,20},{5,21},{6,22},{7,23},{8,24},{9,... | collective-permute-start | bytes 2752520 | tf_op jit(solution)/shard_map/ppermute | solution.py:33
  68.1 25.2 %copy-start.16 = (bf16[144,896]{1,0:T(8,128)(2,1)S(1)}, bf16[144,896]{1,0:T(8,128)(2,1)}, u32[]{:S(2)}) copy-start(bf16[144,896]{1,0:T(8,128)(2,1)} %copy-done.15) | copy-start | bytes 774148
  68.1 27.3 %copy-start.14 = (bf16[144,896]{1,0:T(8,128)(2,1)S(1)}, bf16[144,896]{1,0:T(8,128)(2,1)}, u32[]{:S(2)}) copy-start(bf16[144,896]{1,0:T(8,128)(2,1)} %copy-done.13) | copy-start | bytes 774148
  68.1 30.7 %copy-start.30 = (f32[1,128,1]{1,2,0:T(1,128)S(1)}, f32[1,128,1]{1,2,0:T(1,128)}, u32[]{:S(2)}) copy-start(f32[1,128,1]{1,2,0:T(1,128)} %param.19) | copy-start | bytes 1540
  68.1 44.2 %copy-start.26 = (bf16[144,896]{1,0:T(8,128)(2,1)S(1)}, bf16[144,896]{1,0:T(8,128)(2,1)}, u32[]{:S(2)}) copy-start(bf16[144,896]{1,0:T(8,128)(2,1)} %copy-done.25) | copy-start | bytes 774148
  68.1 11.1 %collective-permute-start.10 = (bf16[144,896]{1,0:T(8,128)(2,1)S(1)}, bf16[144,896]{1,0:T(8,128)(2,1)S(1)}, u32[]{:S(2)}, u32[]{:S(2)}) collective-permute-start(bf16[144,896]{1,0:T(8,128)(2,1)S(1)} %get-tuple-element.110), channel_id=1, source_target_pairs={{0,4},{1,5},{2,6},{3,7},{4,8},{5,9},{6,10},{7,11},{8,12},{9,13},{1... | collective-permute-start | bytes 774152 | tf_op jit(solution)/shard_map/ppermute | solution.py:42
  68.2 19.8 %collective-permute-start.11 = (bf16[144,896]{1,0:T(8,128)(2,1)S(1)}, bf16[144,896]{1,0:T(8,128)(2,1)S(1)}, u32[]{:S(2)}, u32[]{:S(2)}) collective-permute-start(bf16[144,896]{1,0:T(8,128)(2,1)S(1)} %get-tuple-element.111), channel_id=1, source_target_pairs={{0,8},{1,9},{2,10},{3,11},{4,12},{5,13},{6,14},{7,15},{8,0},{9,1},... | collective-permute-start | bytes 774152 | tf_op jit(solution)/shard_map/ppermute | solution.py:42
  68.2 19.7 %collective-permute-start.12 = (bf16[144,896]{1,0:T(8,128)(2,1)S(1)}, bf16[144,896]{1,0:T(8,128)(2,1)S(1)}, u32[]{:S(2)}, u32[]{:S(2)}) collective-permute-start(bf16[144,896]{1,0:T(8,128)(2,1)S(1)} %get-tuple-element.112), channel_id=1, source_target_pairs={{0,12},{1,13},{2,14},{3,15},{4,0},{5,1},{6,2},{7,3},{8,4},{9,5},{1... | collective-permute-start | bytes 774152 | tf_op jit(solution)/shard_map/ppermute | solution.py:42
  91.0 21.2 %collective-permute-start.18 = (bf16[128,3584]{1,0:T(8,128)(2,1)S(1)}, bf16[128,3584]{1,0:T(8,128)(2,1)S(1)}, u32[]{:S(2)}, u32[]{:S(2)}) collective-permute-start(bf16[128,3584]{1,0:T(8,128)(2,1)S(1)} %get-tuple-element.127), channel_id=1, source_target_pairs={{0,16},{1,17},{2,18},{3,19},{4,20},{5,21},{6,22},{7,23},{8,24},{9,... | collective-permute-start | bytes 2752520 | tf_op jit(solution)/shard_map/ppermute | solution.py:33
  92.6 22.0 %collective-permute-start.20 = (bf16[96,3584]{1,0:T(8,128)(2,1)S(1)}, bf16[96,3584]{1,0:T(8,128)(2,1)S(1)}, u32[]{:S(2)}, u32[]{:S(2)}) collective-permute-start(bf16[96,3584]{1,0:T(8,128)(2,1)S(1)} %slice_bitcast_fusion.1), channel_id=1, source_target_pairs={{0,2},{1,3},{2,0},{3,1},{4,6},{5,7},{6,4},{7,5},{8,10},{9,11},{10,... | collective-permute-start | bytes 2064392 | tf_op jit(solution)/shard_map/ppermute | solution.py:37
  93.3 15.4 %collective-permute-start.22 = (bf16[144,896]{1,0:T(8,128)(2,1)S(1)}, bf16[144,896]{1,0:T(8,128)(2,1)S(1)}, u32[]{:S(2)}, u32[]{:S(2)}) collective-permute-start(bf16[144,896]{1,0:T(8,128)(2,1)S(1)} %copy-done.16), channel_id=1, source_target_pairs={{0,8},{1,9},{2,10},{3,11},{4,12},{5,13},{6,14},{7,15},{8,0},{9,1},... | collective-permute-start | bytes 774152 | tf_op jit(solution)/shard_map/ppermute | solution.py:42
  95.4 14.2 %collective-permute-start.23 = (bf16[144,896]{1,0:T(8,128)(2,1)S(1)}, bf16[144,896]{1,0:T(8,128)(2,1)S(1)}, u32[]{:S(2)}, u32[]{:S(2)}) collective-permute-start(bf16[144,896]{1,0:T(8,128)(2,1)S(1)} %copy-done.14), channel_id=1, source_target_pairs={{0,12},{1,13},{2,14},{3,15},{4,0},{5,1},{6,2},{7,3},{8,4},{9,5},{1... | collective-permute-start | bytes 774152 | tf_op jit(solution)/shard_map/ppermute | solution.py:42
  98.8 13.4 %collective-permute-start.24 = (f32[1,3712]{1,0:T(1,128)S(1)}, f32[1,3712]{1,0:T(1,128)S(1)}, u32[]{:S(2)}, u32[]{:S(2)}) collective-permute-start(f32[1,3712]{1,0:T(1,128)S(1)} %pad_maximum_fusion), channel_id=1, source_target_pairs={{0,16},{1,17},{2,18},{3,19},{4,20},{5,21},{6,22},{7,23},{8,24},{9,... | collective-permute-start | bytes 44552 | tf_op jit(solution)/shard_map/ppermute | solution.py:33
  108.7 3.6 %collective-permute-start.17 = (f32[1,256]{1,0:T(1,128)S(1)}, f32[1,256]{1,0:T(1,128)S(1)}, u32[]{:S(2)}, u32[]{:S(2)}) collective-permute-start(f32[1,256]{1,0:T(1,128)S(1)} %maximum_bitcast_fusion), channel_id=1, source_target_pairs={{0,16},{1,17},{2,18},{3,19},{4,20},{5,21},{6,22},{7,23},{8,24},{9,... | collective-permute-start | bytes 3080 | tf_op jit(solution)/shard_map/ppermute | solution.py:33
  114.6 2.7 %collective-permute-start.25 = (bf16[144,3584]{1,0:T(8,128)(2,1)S(1)}, bf16[144,3584]{1,0:T(8,128)(2,1)S(1)}, u32[]{:S(2)}, u32[]{:S(2)}) collective-permute-start(bf16[144,3584]{1,0:T(8,128)(2,1)S(1)} %shard_map.154.first_ref), channel_id=1, source_target_pairs={{0,1},{1,0},{2,3},{3,2},{4,5},{5,4},{6,7},{7,6},{8,9},{9,8},{10,11... | collective-permute-start | bytes 3096584 | tf_op jit(solution)/shard_map/ppermute | solution.py:37
  114.7 25.2 %collective-permute-start.21 = (bf16[144,3584]{1,0:T(8,128)(2,1)S(1)}, bf16[144,3584]{1,0:T(8,128)(2,1)S(1)}, u32[]{:S(2)}, u32[]{:S(2)}) collective-permute-start(bf16[144,3584]{1,0:T(8,128)(2,1)S(1)} %shard_map.152.first_ref), channel_id=1, source_target_pairs={{0,2},{1,3},{2,0},{3,1},{4,6},{5,7},{6,4},{7,5},{8,10},{9,11},{10,... | collective-permute-start | bytes 3096584 | tf_op jit(solution)/shard_map/ppermute | solution.py:37
  115.8 25.4 %collective-permute-start.35 = (bf16[144,3584]{1,0:T(8,128)(2,1)S(1)}, bf16[144,3584]{1,0:T(8,128)(2,1)S(1)}, u32[]{:S(2)}, u32[]{:S(2)}) collective-permute-start(bf16[144,3584]{1,0:T(8,128)(2,1)S(1)} %collective-permute-done.16.first_ref), channel_id=1, source_target_pairs={{0,1},{1,0},{2,3},{3,2},{4,5},{5,4},{6,7},{7,6},{8,9},{9,8},{10,11... | collective-permute-start | bytes 3096584 | tf_op jit(solution)/shard_map/ppermute | solution.py:37
  115.9 32.8 %collective-permute-start.19 = (bf16[144,3584]{1,0:T(8,128)(2,1)S(1)}, bf16[144,3584]{1,0:T(8,128)(2,1)S(1)}, u32[]{:S(2)}, u32[]{:S(2)}) collective-permute-start(bf16[144,3584]{1,0:T(8,128)(2,1)S(1)} %shard_map.152.first_ref), channel_id=1, source_target_pairs={{0,1},{1,0},{2,3},{3,2},{4,5},{5,4},{6,7},{7,6},{8,9},{9,8},{10,11... | collective-permute-start | bytes 3096584 | tf_op jit(solution)/shard_map/ppermute | solution.py:37
  117.3 28.9 %copy-start.1 = (bf16[1,1,3584,256]{3,2,1,0:T(8,128)(2,1)S(1)}, bf16[1,1,3584,256]{3,2,1,0:T(8,128)(2,1)}, u32[]{:S(2)}) copy-start(bf16[1,1,3584,256]{3,2,1,0:T(8,128)(2,1)} %param.25) | copy-start | bytes 5505028
  117.3 28.9 %copy-start.2 = (bf16[1,1,3584,256]{3,2,1,0:T(8,128)(2,1)S(1)}, bf16[1,1,3584,256]{3,2,1,0:T(8,128)(2,1)}, u32[]{:S(2)}) copy-start(bf16[1,1,3584,256]{3,2,1,0:T(8,128)(2,1)} %param.26) | copy-start | bytes 5505028
  139.9 10.1 %collective-permute-start.26 = (bf16[144,3584]{1,0:T(8,128)(2,1)S(1)}, bf16[144,3584]{1,0:T(8,128)(2,1)S(1)}, u32[]{:S(2)}, u32[]{:S(2)}) collective-permute-start(bf16[144,3584]{1,0:T(8,128)(2,1)S(1)} %collective-permute-done.21.first_ref), channel_id=1, source_target_pairs={{0,1},{1,0},{2,3},{3,2},{4,5},{5,4},{6,7},{7,6},{8,9},{9,8},{10,11... | collective-permute-start | bytes 3096584 | tf_op jit(solution)/shard_map/ppermute | solution.py:37
  139.9 6.3 %collective-permute-start.36 = (bf16[288,256]{1,0:T(8,128)(2,1)S(1)}, bf16[288,256]{1,0:T(8,128)(2,1)S(1)}, u32[]{:S(2)}, u32[]{:S(2)}) collective-permute-start(bf16[288,256]{1,0:T(8,128)(2,1)S(1)} %get-tuple-element.140), channel_id=1, source_target_pairs={{0,2},{1,3},{2,0},{3,1},{4,6},{5,7},{6,4},{7,5},{8,10},{9,11},{10,... | collective-permute-start | bytes 442376 | tf_op jit(solution)/shard_map/ppermute | solution.py:37
  140.9 11.4 %collective-permute-start.33 = (bf16[144,3584]{1,0:T(8,128)(2,1)S(1)}, bf16[144,3584]{1,0:T(8,128)(2,1)S(1)}, u32[]{:S(2)}, u32[]{:S(2)}) collective-permute-start(bf16[144,3584]{1,0:T(8,128)(2,1)S(1)} %shard_map.151.first_ref), channel_id=1, source_target_pairs={{0,1},{1,0},{2,3},{3,2},{4,5},{5,4},{6,7},{7,6},{8,9},{9,8},{10,11... | collective-permute-start | bytes 3096584 | tf_op jit(solution)/shard_map/ppermute | solution.py:37
  148.6 10.3 %collective-permute-start.37 = (bf16[144,3584]{1,0:T(8,128)(2,1)S(1)}, bf16[144,3584]{1,0:T(8,128)(2,1)S(1)}, u32[]{:S(2)}, u32[]{:S(2)}) collective-permute-start(bf16[144,3584]{1,0:T(8,128)(2,1)S(1)} %get-tuple-element.152), channel_id=1, source_target_pairs={{0,1},{1,0},{2,3},{3,2},{4,5},{5,4},{6,7},{7,6},{8,9},{9,8},{10,11... | collective-permute-start | bytes 3096584 | tf_op jit(solution)/shard_map/ppermute | solution.py:37
  151.3 6.3 %collective-permute-start.27 = (bf16[288,256]{1,0:T(8,128)(2,1)S(1)}, bf16[288,256]{1,0:T(8,128)(2,1)S(1)}, u32[]{:S(2)}, u32[]{:S(2)}) collective-permute-start(bf16[288,256]{1,0:T(8,128)(2,1)S(1)} %shard_map.156), channel_id=1, source_target_pairs={{0,2},{1,3},{2,0},{3,1},{4,6},{5,7},{6,4},{7,5},{8,10},{9,11},{10,... | collective-permute-start | bytes 442376 | tf_op jit(solution)/shard_map/ppermute | solution.py:37
  155.8 15.4 %collective-permute-start.34 = (bf16[144,3584]{1,0:T(8,128)(2,1)}, bf16[144,3584]{1,0:T(8,128)(2,1)}, u32[]{:S(2)}, u32[]{:S(2)}) collective-permute-start(bf16[144,3584]{1,0:T(8,128)(2,1)} %get-tuple-element.150), channel_id=1, source_target_pairs={{0,1},{1,0},{2,3},{3,2},{4,5},{5,4},{6,7},{7,6},{8,9},{9,8},{10,11... | collective-permute-start | bytes 3096584 | tf_op jit(solution)/shard_map/ppermute | solution.py:37
  158.8 2.7 %collective-permute-start.28 = (bf16[144,3584]{1,0:T(8,128)(2,1)S(1)}, bf16[144,3584]{1,0:T(8,128)(2,1)S(1)}, u32[]{:S(2)}, u32[]{:S(2)}) collective-permute-start(bf16[144,3584]{1,0:T(8,128)(2,1)S(1)} %get-tuple-element.143), channel_id=1, source_target_pairs={{0,1},{1,0},{2,3},{3,2},{4,5},{5,4},{6,7},{7,6},{8,9},{9,8},{10,11... | collective-permute-start | bytes 3096584 | tf_op jit(solution)/shard_map/ppermute | solution.py:37
  160.1 25.4 %collective-permute-start.38 = (bf16[144,3584]{1,0:T(8,128)(2,1)}, bf16[144,3584]{1,0:T(8,128)(2,1)S(1)}, u32[]{:S(2)}, u32[]{:S(2)}) collective-permute-start(bf16[144,3584]{1,0:T(8,128)(2,1)} %add_convert_fusion), channel_id=1, source_target_pairs={{0,2},{1,3},{2,0},{3,1},{4,6},{5,7},{6,4},{7,5},{8,10},{9,11},{10,... | collective-permute-start | bytes 3096584 | tf_op jit(solution)/shard_map/ppermute | solution.py:37
  163.4 27.9 %collective-permute-start.29 = (bf16[144,896]{1,0:T(8,128)(2,1)}, bf16[144,896]{1,0:T(8,128)(2,1)S(1)}, u32[]{:S(2)}, u32[]{:S(2)}) collective-permute-start(bf16[144,896]{1,0:T(8,128)(2,1)} %get-tuple-element.144), channel_id=1, source_target_pairs={{0,16},{1,17},{2,18},{3,19},{4,20},{5,21},{6,22},{7,23},{8,24},{9,... | collective-permute-start | bytes 774152 | tf_op jit(solution)/shard_map/ppermute | solution.py:33
  164.6 33.0 %collective-permute-start.30 = (bf16[144,896]{1,0:T(8,128)(2,1)}, bf16[144,896]{1,0:T(8,128)(2,1)S(1)}, u32[]{:S(2)}, u32[]{:S(2)}) collective-permute-start(bf16[144,896]{1,0:T(8,128)(2,1)} %get-tuple-element.145), channel_id=1, source_target_pairs={{0,28},{1,29},{2,30},{3,31},{4,16},{5,17},{6,18},{7,19},{8,20},{9,... | collective-permute-start | bytes 774152 | tf_op jit(solution)/shard_map/ppermute | solution.py:33
  171.0 26.6 %collective-permute-start.31 = (bf16[144,896]{1,0:T(8,128)(2,1)}, bf16[144,896]{1,0:T(8,128)(2,1)}, u32[]{:S(2)}, u32[]{:S(2)}) collective-permute-start(bf16[144,896]{1,0:T(8,128)(2,1)} %get-tuple-element.146), channel_id=1, source_target_pairs={{0,24},{1,25},{2,26},{3,27},{4,28},{5,29},{6,30},{7,31},{8,16},{9,... | collective-permute-start | bytes 774152 | tf_op jit(solution)/shard_map/ppermute | solution.py:33
  171.2 28.1 %collective-permute-start.32 = (bf16[144,896]{1,0:T(8,128)(2,1)S(1)}, bf16[144,896]{1,0:T(8,128)(2,1)}, u32[]{:S(2)}, u32[]{:S(2)}) collective-permute-start(bf16[144,896]{1,0:T(8,128)(2,1)S(1)} %get-tuple-element.147), channel_id=1, source_target_pairs={{0,20},{1,21},{2,22},{3,23},{4,24},{5,25},{6,26},{7,27},{8,28},{9,... | collective-permute-start | bytes 774152 | tf_op jit(solution)/shard_map/ppermute | solution.py:33
  186.8 12.6 %copy-start.12 = (bf16[128,3584]{1,0:T(8,128)(2,1)S(1)}, bf16[128,3584]{1,0:T(8,128)(2,1)}, u32[]{:S(2)}) copy-start(bf16[128,3584]{1,0:T(8,128)(2,1)} %copy-done.11) | copy-start | bytes 2752516
  190.0 15.5 %collective-permute-start.39 = (bf16[144,896]{1,0:T(8,128)(2,1)}, bf16[144,896]{1,0:T(8,128)(2,1)S(1)}, u32[]{:S(2)}, u32[]{:S(2)}) collective-permute-start(bf16[144,896]{1,0:T(8,128)(2,1)} %get-tuple-element.156), channel_id=1, source_target_pairs={{0,16},{1,17},{2,18},{3,19},{4,20},{5,21},{6,22},{7,23},{8,24},{9,... | collective-permute-start | bytes 774152 | tf_op jit(solution)/shard_map/ppermute | solution.py:33
  191.3 14.3 %collective-permute-start.40 = (bf16[144,896]{1,0:T(8,128)(2,1)S(1)}, bf16[144,896]{1,0:T(8,128)(2,1)}, u32[]{:S(2)}, u32[]{:S(2)}) collective-permute-start(bf16[144,896]{1,0:T(8,128)(2,1)S(1)} %get-tuple-element.157), channel_id=1, source_target_pairs={{0,28},{1,29},{2,30},{3,31},{4,16},{5,17},{6,18},{7,19},{8,20},{9,... | collective-permute-start | bytes 774152 | tf_op jit(solution)/shard_map/ppermute | solution.py:33
  197.6 22.0 %collective-permute-start.41 = (bf16[144,896]{1,0:T(8,128)(2,1)}, bf16[144,896]{1,0:T(8,128)(2,1)}, u32[]{:S(2)}, u32[]{:S(2)}) collective-permute-start(bf16[144,896]{1,0:T(8,128)(2,1)} %get-tuple-element.158), channel_id=1, source_target_pairs={{0,24},{1,25},{2,26},{3,27},{4,28},{5,29},{6,30},{7,31},{8,16},{9,... | collective-permute-start | bytes 774152 | tf_op jit(solution)/shard_map/ppermute | solution.py:33
  197.6 22.0 %collective-permute-start.42 = (bf16[144,896]{1,0:T(8,128)(2,1)}, bf16[144,896]{1,0:T(8,128)(2,1)}, u32[]{:S(2)}, u32[]{:S(2)}) collective-permute-start(bf16[144,896]{1,0:T(8,128)(2,1)} %get-tuple-element.159), channel_id=1, source_target_pairs={{0,20},{1,21},{2,22},{3,23},{4,24},{5,25},{6,26},{7,27},{8,28},{9,... | collective-permute-start | bytes 774152 | tf_op jit(solution)/shard_map/ppermute | solution.py:33
  199.3 20.3 %copy-start.10 = (bf16[128,3584]{1,0:T(8,128)(2,1)S(1)}, bf16[128,3584]{1,0:T(8,128)(2,1)}, u32[]{:S(2)}) copy-start(bf16[128,3584]{1,0:T(8,128)(2,1)} %copy-done.9) | copy-start | bytes 2752516
  (11 other events, 18.0 us)

commit v7 on v5

--- a/solution.py
+++ b/solution.py
@@ -51,7 +51,6 @@
     ]
     many = isinstance(outs, list)
     shapes = outs if many else [outs]
-    moved_bytes = sum(a.size * a.dtype.itemsize for a in list(args) + shapes)
     result = pl.pallas_call(
         body,
         out_shape=shapes,
@@ -59,9 +58,7 @@
         out_specs=[pl.BlockSpec(memory_space=pltpu.VMEM) for _ in shapes],
         scratch_shapes=list(scratch),
         compiler_params=pltpu.CompilerParams(vmem_limit_bytes=vmem),
-        cost_estimate=pl.CostEstimate(
-            flops=int(flops), bytes_accessed=int(moved_bytes), transcendentals=0
-        ),
+        cost_estimate=pl.CostEstimate(flops=1, bytes_accessed=1, transcendentals=0),
     )(*args)
     return list(result) if many else result[0]
 
@@ -82,9 +79,9 @@
     return lax.broadcasted_iota(jnp.int32, shape, dim)
 
 
-def stacked(rows):
-    width = rows.shape[1] // PARTS
-    return jnp.concatenate([rows[:, p * width : (p + 1) * width] for p in range(PARTS)], axis=0)
+def stacked(rows, parts=PARTS):
+    width = rows.shape[1] // parts
+    return jnp.concatenate([rows[:, p * width : (p + 1) * width] for p in range(parts)], axis=0)
 
 
 def place_across(route_row, experts, capacity):
@@ -97,13 +94,13 @@
     return jnp.sum(place, axis=0, keepdims=True).astype(jnp.int32)
 
 
-def place_down(route_column, experts, capacity):
+def place_down(route_column, height):
     tokens = route_column.shape[0]
     names = iota((tokens, LANES), 1)
     onehot = jnp.where(names == route_column, 1.0, 0.0)
     earlier = jnp.where(iota((tokens, tokens), 1) < iota((tokens, tokens), 0), 1.0, 0.0)
     before = dot(earlier.astype(bf16), onehot.astype(bf16))
-    place = onehot * (before + (names * (PARTS * capacity)).astype(f32))
+    place = onehot * (before + (names * height).astype(f32))
     return jnp.sum(place, axis=1, keepdims=True).astype(jnp.int32)
 
 
@@ -145,13 +142,16 @@
         out[:, p * width : (p + 1) * width] = dot(pick, rows).astype(bf16)
 
 
-def split_body(capacity, count_shares, *refs):
+def split_body(capacity, count_shares, lead, *refs):
     shares, outs = refs[:count_shares], refs[count_shares:]
-    total = shares[0][...].astype(f32)
-    for ref in shares[1:]:
-        total = total + ref[...].astype(f32)
-    rows = stacked(total.astype(bf16))
-    height = PARTS * capacity
+    height, width = outs[0].shape
+    parts = height // capacity
+    total = None
+    for ref in shares:
+        at = lead if ref.shape[1] > parts * width else 0
+        share = ref[:, at : at + parts * width].astype(f32)
+        total = share if total is None else total + share
+    rows = stacked(total.astype(bf16), parts)
     slots = shares[0].shape[0]
     count = height * len(outs)
     index = iota((count, 1), 0)
@@ -161,9 +161,9 @@
         group = group + jnp.where(index >= g * capacity, 1, 0)
     for s in range(1, len(outs)):
         source = source + jnp.where(index >= s * height, 1, 0)
-    part = group - source * PARTS
+    part = group - source * parts
     place = part * slots + source * capacity + index - group * capacity
-    pick = jnp.where(iota((count, PARTS * slots), 1) == place, 1.0, 0.0).astype(bf16)
+    pick = jnp.where(iota((count, parts * slots), 1) == place, 1.0, 0.0).astype(bf16)
     packed = dot(pick, rows).astype(bf16)
     for s, ref in enumerate(outs):
         ref[...] = packed[s * height : (s + 1) * height]
@@ -171,13 +171,17 @@
 
 def unpacked(route_column, chunk_refs, experts, capacity):
     tokens = route_column.shape[0]
-    place = place_down(route_column, experts, capacity)
-    rows = jnp.concatenate([ref[...] for ref in chunk_refs], axis=0)
-    columns = iota((tokens, rows.shape[0]), 1)
+    groups = len(chunk_refs) // experts
+    each = PARTS // groups
+    place = place_down(route_column, each * capacity)
     parts = []
-    for p in range(PARTS):
-        pick = jnp.where(columns == place + p * capacity, 1.0, 0.0).astype(bf16)
-        parts.append(dot(pick, rows))
+    for g in range(groups):
+        chunks = chunk_refs[g * experts : (g + 1) * experts]
+        rows = jnp.concatenate([ref[...] for ref in chunks], axis=0)
+        columns = iota((tokens, rows.shape[0]), 1)
+        for p in range(each):
+            pick = jnp.where(columns == place + p * capacity, 1.0, 0.0).astype(bf16)
+            parts.append(dot(pick, rows))
     return jnp.concatenate(parts, axis=1)
 
 
@@ -253,13 +257,14 @@
     kv0,
     kv1,
     kv2,
+    kv3,
     middle_ref,
     *refs,
 ):
     outs, (kv_all, kv_now, stack, attended) = refs[:experts], refs[experts:]
     tokens, width = query_ref.shape
     lead = 0
-    for ref in (kv0, kv1, kv2):
+    for ref in (kv0, kv1, kv2, kv3):
         kv_all[lead : lead + ref.shape[0], : ref.shape[1]] = ref[...]
         lead += ref.shape[0]
     attended[...] = jnp.zeros_like(attended)
@@ -388,8 +393,6 @@
     column = jnp.concatenate(column, axis=0)
     other_chip = swapped(column, 2)
     packed = after(packed, [column])
-    down_other = swapped(w_down, 2)
-    downs = (w_down, down_other)
 
     front_small = jnp.concatenate([front_from.astype(f32), front_gate[0]], axis=0).reshape(1, -1)
     back_small = jnp.concatenate([back_from.astype(f32).reshape(1, -1), norm_gain], axis=1)
@@ -404,31 +407,31 @@
         other = swapped(rows, 2)
         return [rows, swapped(rows, 1), other, swapped(other, 1)]
 
-    def split(parts):
+    def split(shares, groups=1, group=0):
         return call(
-            functools.partial(split_body, capacity, len(parts)),
-            [chunk] * experts,
-            parts,
-            flops=pack_flops,
+            functools.partial(split_body, capacity, len(shares), group * (width // groups)),
+            [shape_of(PARTS // groups * capacity, width // PARTS)] * experts,
+            shares,
         )
 
     def sent_back(chunks, by):
         return [passed_along(chunks[k], by, k) for k in range(experts)]
 
     row_chunks, grad_chunks = packed[:experts], packed[experts:]
-    first = 1 + 2 * (experts - 1) // 3
-    for k in range(1, first):
-        row_chunks[k] = turned(row_chunks[k], k)
-    arrived = row_chunks[1:first]
+    row_chunks[1] = turned(row_chunks[1], 1)
+    arrived = [row_chunks[1]]
+    down_other = swapped(after([w_down], [other_chip] + arrived)[0], 2)
+    downs = (w_down, down_other)
     there_back_middle = passed_along(after([back_middle[0]], [packed[0]])[0], -1)
-    chip = jnp.concatenate([column, other_chip], axis=0)
-    kv = [column, other_chip, swapped(after([chip], arrived + [there_back_middle])[0], 1)]
-    for k in range(first, experts):
+    there_back_grad = passed_along(after([back_grad[0]], arrived + [there_back_middle])[0], -1)
+    there_small = passed_along(after([front_small], arrived)[0], 1)
+    there_back_small = passed_along(after([back_small], arrived)[0], -1)
+    kv = [column, other_chip, swapped(column, 1), swapped(other_chip, 1)]
+    for k in range(2, experts):
         row_chunks[k] = turned(after([row_chunks[k]], arrived)[0], k)
     beside = range(1, 2)
     for k in beside:
         grad_chunks[k] = turned(after([grad_chunks[k]], arrived)[0], k)
-    there_back_grad = passed_along(after([back_grad[0]], [there_back_middle])[0], -1)
 
     per_device = tokens // BLK
     chosen = selected_blocks[0].reshape(-1)
@@ -455,25 +458,17 @@
     middle, front_chunks = result[0], result[1:]
     ready = row_chunks + [grad_chunks[k] for k in beside]
     front_chunks = sent(after(front_chunks, ready))
-    back_rows = joined(after(ready, [middle, there_back_grad])[:experts])
-    back_pieces = pieces_of(after([back_rows], [down_other])[0])
-    there_middle = passed_along(after([middle], [back_rows])[0], 1)
     for k in range(1, experts):
         if k not in beside:
-            grad_chunks[k] = turned(after([grad_chunks[k]], front_chunks)[0], k)
-    front_near = joined(after(front_chunks, [there_middle, back_pieces[2]]))
-    front_other = swapped(front_near, 2)
-
-    front_small, back_small = after([front_small, back_small], [front_near])
-    there_small = passed_along(front_small, 1)
-    there_back_small = passed_along(back_small, -1)
+            grad_chunks[k] = turned(after([grad_chunks[k]], [middle])[0], k)
+    back_rows = joined(after(ready, [middle, there_back_grad, there_small, there_back_small])[:experts])
+    grad_near = joined(after(grad_chunks, [back_rows, down_other]))
+    grad_near = [grad_near, swapped(grad_near, 1)]
+    back_pieces = pieces_of(back_rows)
     there_front_from = there_small[0, :tokens].astype(jnp.int32).reshape(tokens, 1)
     there_front_gate = there_small[0, tokens:].reshape(tokens, 1)
     there_back_from = there_back_small[0, :tokens].astype(jnp.int32).reshape(tokens, 1)
     there_gain = there_back_small[:, tokens:]
-    grad_near = joined(after(grad_chunks, [there_small, there_back_small]))
-    grad_near = [grad_near, swapped(grad_near, 1)]
-
     work = 2 * 2 * slots * width * hidden_width
     pair = 2 * slots
 
@@ -488,30 +483,35 @@
     down_back, other_back = call(
         down_back_body,
         [shape_of(pair, hidden_width, f32), shape_of(pair, hidden_width)],
-        (*grad_near, *downs),
+        (*after(grad_near, front_chunks), *downs),
         flops=2 * work,
     )
-    (front_other,) = after([front_other], [other_back])
-    front_pieces = [front_near, swapped(front_near, 1), front_other, swapped(front_other, 1)]
-    hidden_near = hidden(front_pieces[:2])
-    hidden_far = hidden(front_pieces[2:])
-    hidden_other = swapped(hidden_far, 2)
     far_back = swapped(other_back, 2)
-
     back_near = backward(back_pieces[:2], down_back)
+    back_core = swapped(back_near[1], 1)
+    front_near = joined(after(front_chunks, [back_pieces[2], other_back]))
+    front_other = swapped(front_near, 2)
+    there_middle = passed_along(after([middle], [front_near])[0], 1)
+    front_core = swapped(front_near, 1)
+    hidden_near = hidden((front_near, front_core))
+    (front_other,) = after([front_other], [back_core, hidden_near, there_middle])
+    (far_back,) = after([far_back], [front_other])
     back_far = backward(back_pieces[2:], far_back)
     chip = back_far[0].astype(f32) + swapped(back_far[1], 1).astype(f32)
-    back_shares = (back_near[0], swapped(back_near[1], 1), swapped(chip.astype(bf16), 2))
+    chip = chip.astype(bf16)
+    hidden_far = hidden((front_other, swapped(front_other, 1)))
+    hidden_other = swapped(hidden_far, 2)
+    back_shares = [back_near[0], back_core, swapped(after([chip], [hidden_other])[0], 2)]
 
     front_own, front_core = call(
         output_body, [piece, piece], (hidden_near, hidden_other, *downs), flops=2 * work
     )
-    front_chunks = split((front_own, swapped(front_core, 1)))
+    front_core = swapped(front_core, 1)
+    front_chunks = split((front_own, front_core))
     front_return = sent_back(front_chunks, 1)
 
     back_chunks = split(after(back_shares, front_chunks))
     back_return = sent_back(back_chunks, -1)
-
     front_return = after(front_return, back_chunks)
     front_output = call(
         functools.partial(front_finish_body, experts, capacity),

time: 260 us -> 225 us (0.87)
  waiting for transfers between devices: 133 us -> 103 us
  local copies, waits for them, and re-layouts: 20.9 us -> 16.6 us
    ppermute x16 -> x17, waiting for transfers between devices: 87.4 us -> 22.7 us  [swapped(): lax.ppermute(array, 'expert', [(i, i ^ bit) for i in range(lax.axis_size(...]
    ppermute x13, waiting for transfers between devices: 22.9 us -> 44.1 us  [passed_along(): return lax.ppermute(array, ('section', 'expert'), pairs)]
    ppermute x9, waiting for transfers between devices: 22.5 us -> 35.8 us  [turned(): lax.ppermute(array, 'expert', [(i, (i + by * GROUP) % length) for i in ra...]
    ppermute x13, starting transfers between devices: 26.6 us -> 22 us  [passed_along(): return lax.ppermute(array, ('section', 'expert'), pairs)]
    ppermute x16 -> x17, starting transfers between devices: 7.02 us -> 9.82 us  [swapped(): lax.ppermute(array, 'expert', [(i, i ^ bit) for i in range(lax.axis_size(...]
    unnamed x69 -> x66, local copies, waits for them, and re-layouts: 15.2 us -> 13.1 us
  transfers between devices with their start and end apart: 41 -> 42, of which waited for: 13 -> 16; matrix products, arithmetic and copies ran while one was open for 3% -> 3% of each run, Pallas kernels for 13% -> 15%
where the time goes in v7:
time: 225 us; the launch traced here: 224 us
  waiting for transfers between devices  103 us (46%)
  starting transfers between devices  61.4 us (27%)
  Pallas kernels  39 us (17%)
  local copies, waits for them, and re-layouts  16.6 us (7%)
  other arithmetic  3.28 us (1%)
    ppermute x13, waiting for transfers between devices, passed_along(): return lax.ppermute(array, ('section', 'expert'), pairs)  44.1 us
    pallas_call x15, Pallas kernels, call(): pl.pallas_call(body, out_shape=shapes, in_specs=specs, out_specs=[pl.Bloc...  39 us
    ppermute x9, waiting for transfers between devices, turned(): lax.ppermute(array, 'expert', [(i, (i + by * GROUP) % length) for i in ra...  35.8 us
    ppermute x17, waiting for transfers between devices, swapped(): lax.ppermute(array, 'expert', [(i, i ^ bit) for i in range(lax.axis_size(...  22.7 us
    ppermute x13, starting transfers between devices, passed_along(): return lax.ppermute(array, ('section', 'expert'), pairs)  22 us
    ppermute x9, starting transfers between devices, turned(): lax.ppermute(array, 'expert', [(i, (i + by * GROUP) % length) for i in ra...  18.1 us
    unnamed x66, local copies, waits for them, and re-layouts  13.1 us
    ppermute x3, starting transfers between devices, shards(): column.append(lax.ppermute(keys_values[0], 'expert', pairs))  11.4 us
  transfers between devices with their start and end apart: 42, of which 16 were waited for; matrix products, arithmetic and copies ran while one was open for 3% of the time, Pallas kernels for 15%

profile of v7, /device:TPU:0, one launch (start us, length us, event | category | flops | bytes accessed | tf_op | source)
XLA Modules:
  0.0 223.9 jit_solution(4293379070950282758)
XLA Ops:
  0.6 1.1 copy.17
  1.8 4.9 %collective-permute-start = (bf16[128,448]{1,0:T(8,128)(2,1)S(1)}, bf16[128,448]{1,0:T(8,128)(2,1)S(1)}, u32[]{:S(2)}, u32[]{:S(2)}) collective-permute-start(bf16[128,448]{1,0:T(8,128)(2,1)S(1)} %bitcast.45), channel_id=1, source_target_pairs={{0,4},{1,5},{2,6},{3,7},{4,8},{5,9},{6,10},{7,11},{8,12},{9,13},{1... | collective-permute-start | bytes 344072 | tf_op jit(solution)/shard_map/ppermute | solution.py:380
  6.7 4.5 %collective-permute-start.1 = (bf16[128,448]{1,0:T(8,128)(2,1)S(1)}, bf16[128,448]{1,0:T(8,128)(2,1)S(1)}, u32[]{:S(2)}, u32[]{:S(2)}) collective-permute-start(bf16[128,448]{1,0:T(8,128)(2,1)S(1)} %bitcast.46), channel_id=1, source_target_pairs={{0,8},{1,9},{2,10},{3,11},{4,12},{5,13},{6,14},{7,15},{16,24},{17,... | collective-permute-start | bytes 344072 | tf_op jit(solution)/shard_map/ppermute | solution.py:380
  11.2 2.0 collective-permute-start.2
  14.6 1.2 copy-done.3
  16.5 3.1 %shard_map.149 = (bf16[144,896]{1,0:T(8,128)(2,1)S(1)}, bf16[144,896]{1,0:T(8,128)(2,1)S(1)}, bf16[144,896]{1,0:T(8,128)(2,1)}, bf16[144,896]{1,0:T(8,128)(2,1)}...) custom-call(s32[1,128]{1,0:T(1,128)S(1)} %get-tuple-element.171.rout, ...), custom_call_target="tpu_custom_call" | custom-call | flops 1 | bytes 1 | tf_op jit(solution)/shard_map/pallas_call | solution.py:54
  21.1 0.9 constant_dynamic-update-slice_fusion.3
  22.0 0.9 constant_dynamic-update-slice_fusion.2
  22.9 0.9 constant_dynamic-update-slice_fusion.1
  23.8 0.9 constant_dynamic-update-slice_fusion.kv0
  24.7 1.6 collective-permute-start.5
  26.3 1.5 collective-permute-start.14
  27.8 7.4 %collective-permute-done.3.refs_1_ = bf16[144,896]{1,0:T(8,128)(2,1)S(1)} collective-permute-done((bf16[144,896]{1,0:T(8,128)(2,1)S(1)}, bf16[144,896]{1,0:T(8,128)(2,1)S(1)}, u32[]{:S(2)}, u32[]{:S(2)}) %collective-permute-start.3) | collective-permute-done | bytes 258080 | tf_op jit(solution)/shard_map/ppermute | solution.py:42
  35.9 2.1 collective-permute-done.5.kv1
  38.0 1.5 collective-permute-start.20
  39.6 1.6 collective-permute-start.4
  41.4 6.2 %collective-permute-done.14.middle_ref = bf16[128,3584]{1,0:T(8,128)(2,1)S(1)} collective-permute-done((bf16[128,3584]{1,0:T(8,128)(2,1)S(1)}, bf16[128,3584]{1,0:T(8,128)(2,1)S(1)}, u32[]{:S(2)}, u32[]{:S(2)}) %collective-permute-start.14) | collective-permute-done | bytes 917536 | tf_op jit(solution)/shard_map/ppermute | solution.py:33
  47.6 0.9 copy-done.6
  48.5 1.5 collective-permute-start.15
  50.6 2.3 %collective-permute-start.8 = (bf16[144,896]{1,0:T(8,128)(2,1)}, bf16[144,896]{1,0:T(8,128)(2,1)}, u32[]{:S(2)}, u32[]{:S(2)}) collective-permute-start(bf16[144,896]{1,0:T(8,128)(2,1)} %get-tuple-element.107), channel_id=1, source_target_pairs={{0,8},{1,9},{2,10},{3,11},{4,12},{5,13},{6,14},{7,15},{8,0},{9,1},... | collective-permute-start | bytes 774152 | tf_op jit(solution)/shard_map/ppermute | solution.py:42
  53.0 0.8 copy-done.8
  53.8 1.2 collective-permute-start.9
  57.4 1.2 copy-done.5
  58.6 1.0 copy-done.9
  60.9 8.3 %shard_map.150 = (bf16[128,3584]{1,0:T(8,128)(2,1)S(1)}, bf16[144,896]{1,0:T(8,128)(2,1)S(1)}, bf16[144,896]{1,0:T(8,128)(2,1)S(1)}, bf16[144,896]{1,0:T(8,128)(2,1)S(1)}, bf16[144,896]{1,0:T(8,128)(2,1)S(1)}) custom-call(s32[16]{0:T(128)S(1)} %reshape_squeeze.7.chosen_ref, s32[16]{0:T(128)S(1)} %copy-done.16, s32[1]{0:T(128)} %bitcast.10.base_ref, ...), custom_call_target="tpu_custom_call" | custom-call | flops 1 | bytes 1 | tf_op jit(solution)/shard_map/pallas_call | solution.py:54
  70.1 3.3 %collective-permute-start.18 = (bf16[144,896]{1,0:T(8,128)(2,1)S(1)}, bf16[144,896]{1,0:T(8,128)(2,1)S(1)}, u32[]{:S(2)}, u32[]{:S(2)}) collective-permute-start(bf16[144,896]{1,0:T(8,128)(2,1)S(1)} %copy-done.21), channel_id=1, source_target_pairs={{0,8},{1,9},{2,10},{3,11},{4,12},{5,13},{6,14},{7,15},{8,0},{9,1},... | collective-permute-start | bytes 774152 | tf_op jit(solution)/shard_map/ppermute | solution.py:42
  73.4 1.3 collective-permute-start.19
  74.7 5.8 %collective-permute-done.10.refs_1_ = bf16[144,896]{1,0:T(8,128)(2,1)S(1)} collective-permute-done((bf16[144,896]{1,0:T(8,128)(2,1)S(1)}, bf16[144,896]{1,0:T(8,128)(2,1)S(1)}, u32[]{:S(2)}, u32[]{:S(2)}) %collective-permute-start.10) | collective-permute-done | bytes 258080 | tf_op jit(solution)/shard_map/ppermute | solution.py:42
  80.6 2.2 shard_map.151.first_ref
  82.7 5.2 %collective-permute-done.18.refs_2_ = bf16[144,896]{1,0:T(8,128)(2,1)S(1)} collective-permute-done((bf16[144,896]{1,0:T(8,128)(2,1)S(1)}, bf16[144,896]{1,0:T(8,128)(2,1)S(1)}, u32[]{:S(2)}, u32[]{:S(2)}) %collective-permute-start.18) | collective-permute-done | bytes 258080 | tf_op jit(solution)/shard_map/ppermute | solution.py:42
  88.0 1.1 shard_map.152.first_ref
  89.9 5.7 %collective-permute-start.11 = (bf16[144,896]{1,0:T(8,128)(2,1)S(1)}, bf16[144,896]{1,0:T(8,128)(2,1)S(1)}, u32[]{:S(2)}, u32[]{:S(2)}) collective-permute-start(bf16[144,896]{1,0:T(8,128)(2,1)S(1)} %get-tuple-element.113), channel_id=1, source_target_pairs={{0,4},{1,5},{2,6},{3,7},{4,8},{5,9},{6,10},{7,11},{8,12},{9,13},{1... | collective-permute-start | bytes 774152 | tf_op jit(solution)/shard_map/ppermute | solution.py:42
  95.6 1.5 collective-permute-start.12
  97.1 6.5 %collective-permute-done.11.refs_1_ = bf16[144,896]{1,0:T(8,128)(2,1)S(1)} collective-permute-done((bf16[144,896]{1,0:T(8,128)(2,1)S(1)}, bf16[144,896]{1,0:T(8,128)(2,1)S(1)}, u32[]{:S(2)}, u32[]{:S(2)}) %collective-permute-start.11) | collective-permute-done | bytes 258080 | tf_op jit(solution)/shard_map/ppermute | solution.py:42
  103.6 2.3 %collective-permute-start.13 = (bf16[144,896]{1,0:T(8,128)(2,1)S(1)}, bf16[144,896]{1,0:T(8,128)(2,1)S(1)}, u32[]{:S(2)}, u32[]{:S(2)}) collective-permute-start(bf16[144,896]{1,0:T(8,128)(2,1)S(1)} %get-tuple-element.115), channel_id=1, source_target_pairs={{0,12},{1,13},{2,14},{3,15},{4,0},{5,1},{6,2},{7,3},{8,4},{9,5},{1... | collective-permute-start | bytes 774152 | tf_op jit(solution)/shard_map/ppermute | solution.py:42
  105.9 8.6 %collective-permute-done.12.refs_2_ = bf16[144,896]{1,0:T(8,128)(2,1)S(1)} collective-permute-done((bf16[144,896]{1,0:T(8,128)(2,1)S(1)}, bf16[144,896]{1,0:T(8,128)(2,1)S(1)}, u32[]{:S(2)}, u32[]{:S(2)}) %collective-permute-start.12) | collective-permute-done | bytes 258080 | tf_op jit(solution)/shard_map/ppermute | solution.py:42
  114.4 2.3 %collective-permute-done.13.refs_3_ = bf16[144,896]{1,0:T(8,128)(2,1)S(1)} collective-permute-done((bf16[144,896]{1,0:T(8,128)(2,1)S(1)}, bf16[144,896]{1,0:T(8,128)(2,1)S(1)}, u32[]{:S(2)}, u32[]{:S(2)}) %collective-permute-start.13) | collective-permute-done | bytes 258080 | tf_op jit(solution)/shard_map/ppermute | solution.py:42
  116.7 2.9 %shard_map.153 = (f32[288,256]{1,0:T(8,128)S(1)}, bf16[288,256]{1,0:T(8,128)(2,1)S(1)}) custom-call(bf16[144,3584]{1,0:T(8,128)(2,1)S(1)} %shard_map.152.first_ref, bf16[144,3584]{1,0:T(8,128)(2,1)S(1)} %collective-permute-done.21.second_ref, bf16[256,3584]{1,0:T(8,128)(2,1)S(1)} %bitcast.37, bf16[256,3584]{1,0:T(8,128)(2,1)} %collective-permute-done.20.far_ref), custom_call_target="tpu_custom_call" | custom-call | flops 1 | bytes 1 | tf_op jit(solution)/shard_map/pallas_call | solution.py:54
  119.6 1.1 shard_map.154.first_ref
  120.8 1.6 collective-permute-start.24
  122.3 2.5 %shard_map.156 = (bf16[144,3584]{1,0:T(8,128)(2,1)S(1)}, bf16[144,3584]{1,0:T(8,128)(2,1)S(1)}) custom-call(bf16[144,3584]{1,0:T(8,128)(2,1)S(1)} %shard_map.151.first_ref, bf16[144,3584]{1,0:T(8,128)(2,1)S(1)} %collective-permute-done.25.second_ref, f32[288,256]{1,0:T(8,128)S(1)} %get-tuple-element.141.back_ref, bf16[3584,256]{1,0:T(8,128)(2,1)S(1)} %bitcast.28, ...), custom_call_target="tpu_custom_call" | custom-call | flops 1 | bytes 1 | tf_op jit(solution)/shard_map/pallas_call | solution.py:54
  125.0 1.5 collective-permute-start.22
  127.2 1.2 shard_map.155.own_ref
  128.4 19.2 %collective-permute-done.22.middle_ref = bf16[128,3584]{1,0:T(8,128)(2,1)S(1)} collective-permute-done((bf16[128,3584]{1,0:T(8,128)(2,1)S(1)}, bf16[128,3584]{1,0:T(8,128)(2,1)S(1)}, u32[]{:S(2)}, u32[]{:S(2)}) %collective-permute-start.22) | collective-permute-done | bytes 917536 | tf_op jit(solution)/shard_map/ppermute | solution.py:33
  147.7 1.5 collective-permute-done.35.back_ref
  149.2 2.5 %shard_map.160 = (bf16[144,3584]{1,0:T(8,128)(2,1)S(1)}, bf16[144,3584]{1,0:T(8,128)(2,1)S(1)}) custom-call(bf16[144,3584]{1,0:T(8,128)(2,1)S(1)} %collective-permute-done.17.first_ref, bf16[144,3584]{1,0:T(8,128)(2,1)S(1)} %collective-permute-done.34.second_ref, bf16[288,256]{1,0:T(8,128)(2,1)S(1)} %collective-permute-done.35.back_ref, ...), custom_call_target="tpu_custom_call" | custom-call | flops 1 | bytes 1 | tf_op jit(solution)/shard_map/pallas_call | solution.py:54
  151.7 1.3 shard_map.157
  153.0 1.6 collective-permute-start.28
  154.5 4.8 %collective-permute-done.28.other_ref = bf16[288,256]{1,0:T(8,128)(2,1)S(1)} collective-permute-done((bf16[288,256]{1,0:T(8,128)(2,1)S(1)}, bf16[288,256]{1,0:T(8,128)(2,1)S(1)}, u32[]{:S(2)}, u32[]{:S(2)}) %collective-permute-start.28) | collective-permute-done | bytes 147488 | tf_op jit(solution)/shard_map/ppermute | solution.py:37
  159.3 2.7 %shard_map.158 = (bf16[144,3584]{1,0:T(8,128)(2,1)S(1)}, bf16[144,3584]{1,0:T(8,128)(2,1)S(1)}) custom-call(bf16[288,256]{1,0:T(8,128)(2,1)S(1)} %shard_map.155.own_ref, bf16[288,256]{1,0:T(8,128)(2,1)S(1)} %collective-permute-done.28.other_ref, bf16[256,3584]{1,0:T(8,128)(2,1)S(1)} %bitcast.38, bf16[256,3584]{1,0:T(8,128)(2,1)} %collective-permute-done.20.far_ref), custom_call_target="tpu_custom_call" | custom-call | flops 1 | bytes 1 | tf_op jit(solution)/shard_map/pallas_call | solution.py:54
  162.4 1.6 collective-permute-start.37
  163.9 0.8 collective-permute-done.29.refs_1_
  164.7 1.8 shard_map.159
  166.5 1.5 collective-permute-start.30
  168.0 4.5 %collective-permute-start.31 = (bf16[144,896]{1,0:T(8,128)(2,1)S(1)}, bf16[144,896]{1,0:T(8,128)(2,1)S(1)}, u32[]{:S(2)}, u32[]{:S(2)}) collective-permute-start(bf16[144,896]{1,0:T(8,128)(2,1)S(1)} %get-tuple-element.147), channel_id=1, source_target_pairs={{0,28},{1,29},{2,30},{3,31},{4,16},{5,17},{6,18},{7,19},{8,20},{9,... | collective-permute-start | bytes 774152 | tf_op jit(solution)/shard_map/ppermute | solution.py:33
  172.6 1.6 collective-permute-start.32
  174.1 13.5 %collective-permute-done.37.refs_2_ = bf16[144,3584]{1,0:T(8,128)(2,1)S(1)} collective-permute-done((bf16[144,3584]{1,0:T(8,128)(2,1)S(1)}, bf16[144,3584]{1,0:T(8,128)(2,1)S(1)}, u32[]{:S(2)}, u32[]{:S(2)}) %collective-permute-start.37) | collective-permute-done | bytes 1032224 | tf_op jit(solution)/shard_map/ppermute | solution.py:37
  187.6 2.1 shard_map.161
  189.7 1.5 collective-permute-start.38
  191.2 5.7 %collective-permute-start.39 = (bf16[144,896]{1,0:T(8,128)(2,1)}, bf16[144,896]{1,0:T(8,128)(2,1)}, u32[]{:S(2)}, u32[]{:S(2)}) collective-permute-start(bf16[144,896]{1,0:T(8,128)(2,1)} %get-tuple-element.159), channel_id=1, source_target_pairs={{0,28},{1,29},{2,30},{3,31},{4,16},{5,17},{6,18},{7,19},{8,20},{9,... | collective-permute-start | bytes 774152 | tf_op jit(solution)/shard_map/ppermute | solution.py:33
  199.2 2.3 %shard_map.162 = bf16[128,3584]{1,0:T(8,128)(2,1)} custom-call(s32[128,1]{1,0:T(8,128)S(1)} %copy.18.route_ref, f32[128,1]{1,0:T(8,128)S(1)} %copy.19.gate_ref, bf16[128,3584]{1,0:T(8,128)(2,1)S(1)} %collective-permute-done.22.middle_ref, bf16[144,896]{1,0:T(8,128)(2,1)S(1)} %collective-permute-done.30.refs_0_, ...), custom_call_target="tpu_custom_call" | custom-call | flops 1 | bytes 1 | tf_op jit(solution)/shard_map/pallas_call | solution.py:54
  201.5 8.3 %collective-permute-done.38.refs_0_ = bf16[144,896]{1,0:T(8,128)(2,1)S(1)} collective-permute-done((bf16[144,896]{1,0:T(8,128)(2,1)}, bf16[144,896]{1,0:T(8,128)(2,1)S(1)}, u32[]{:S(2)}, u32[]{:S(2)}) %collective-permute-start.38) | collective-permute-done | bytes 258080 | tf_op jit(solution)/shard_map/ppermute | solution.py:33
  209.8 10.1 %collective-permute-done.40.refs_2_ = bf16[144,896]{1,0:T(8,128)(2,1)} collective-permute-done((bf16[144,896]{1,0:T(8,128)(2,1)}, bf16[144,896]{1,0:T(8,128)(2,1)}, u32[]{:S(2)}, u32[]{:S(2)}) %collective-permute-start.40) | collective-permute-done | bytes 258080 | tf_op jit(solution)/shard_map/ppermute | solution.py:33
  219.8 4.1 %shard_map.163 = bf16[128,3584]{1,0:T(8,128)(2,1)} custom-call(s32[128,1]{1,0:T(8,128)S(1)} %copy.20.route_ref, f32[1,3584]{1,0:T(1,128)S(1)} %slice.19.gain_ref, bf16[128,3584]{1,0:T(8,128)(2,1)S(1)} %copy-done.7, bf16[128,3584]{1,0:T(8,128)(2,1)} %collective-permute-done.15.grad_ref, bf16[144,896]{1,0:T(8,128)(2,1)S(1)} %collective-permute-done.38.refs_0_, ...), custom_call_target="tpu_custom_call" | custom-call | flops 1 | bytes 1 | tf_op jit(solution)/shard_map/pallas_call | solution.py:54
  (117 shorter events, 14.1 us)
Async XLA Ops:
  0.6 37.4 %copy-start.2 = (bf16[1,1,256,3584]{3,2,1,0:T(8,128)(2,1)S(1)}, bf16[1,1,256,3584]{3,2,1,0:T(8,128)(2,1)}, u32[]{:S(2)}) copy-start(bf16[1,1,256,3584]{3,2,1,0:T(8,128)(2,1)} %param.27) | copy-start | bytes 5505028
  1.8 18.6 %copy-start.24 = (bf16[1,128,448]{2,1,0:T(8,128)(2,1)}, bf16[1,128,448]{2,1,0:T(8,128)(2,1)S(1)}, u32[]{:S(2)}) copy-start(bf16[1,128,448]{2,1,0:T(8,128)(2,1)S(1)} %copy.17) | copy-start | bytes 344068
  1.8 18.5 %collective-permute-start = (bf16[128,448]{1,0:T(8,128)(2,1)S(1)}, bf16[128,448]{1,0:T(8,128)(2,1)S(1)}, u32[]{:S(2)}, u32[]{:S(2)}) collective-permute-start(bf16[128,448]{1,0:T(8,128)(2,1)S(1)} %bitcast.45), channel_id=1, source_target_pairs={{0,4},{1,5},{2,6},{3,7},{4,8},{5,9},{6,10},{7,11},{8,12},{9,13},{1... | collective-permute-start | bytes 344072 | tf_op jit(solution)/shard_map/ppermute | solution.py:380
  6.7 13.6 %collective-permute-start.1 = (bf16[128,448]{1,0:T(8,128)(2,1)S(1)}, bf16[128,448]{1,0:T(8,128)(2,1)S(1)}, u32[]{:S(2)}, u32[]{:S(2)}) collective-permute-start(bf16[128,448]{1,0:T(8,128)(2,1)S(1)} %bitcast.46), channel_id=1, source_target_pairs={{0,8},{1,9},{2,10},{3,11},{4,12},{5,13},{6,14},{7,15},{16,24},{17,... | collective-permute-start | bytes 344072 | tf_op jit(solution)/shard_map/ppermute | solution.py:380
  11.2 9.1 %collective-permute-start.2 = (bf16[128,448]{1,0:T(8,128)(2,1)S(1)}, bf16[128,448]{1,0:T(8,128)(2,1)}, u32[]{:S(2)}, u32[]{:S(2)}) collective-permute-start(bf16[128,448]{1,0:T(8,128)(2,1)S(1)} %bitcast.47), channel_id=1, source_target_pairs={{0,12},{1,13},{2,14},{3,15},{16,28},{17,29},{18,30},{19,31}} | collective-permute-start | bytes 344072 | tf_op jit(solution)/shard_map/ppermute | solution.py:380
  14.6 1.2 copy-start.3
  16.5 23.0 %copy-start.30 = (s32[1,128,1]{1,2,0:T(1,128)S(1)}, s32[1,128,1]{1,2,0:T(1,128)}, u32[]{:S(2)}) copy-start(s32[1,128,1]{1,2,0:T(1,128)} %param.18) | copy-start | bytes 1540
  16.5 23.1 %copy-start.29 = (f32[1,128,1]{1,2,0:T(1,128)S(1)}, f32[1,128,1]{1,2,0:T(1,128)}, u32[]{:S(2)}) copy-start(f32[1,128,1]{1,2,0:T(1,128)} %param.19) | copy-start | bytes 1540
  16.5 40.8 %copy-start.4 = (bf16[1,128,3584]{2,1,0:T(8,128)(2,1)S(1)}, bf16[1,128,3584]{2,1,0:T(8,128)(2,1)}, u32[]{:S(2)}) copy-start(bf16[1,128,3584]{2,1,0:T(8,128)(2,1)} %param.14) | copy-start | bytes 2752516
  16.5 40.8 %copy-start.15 = (f32[1,3584]{1,0:T(1,128)S(1)}, f32[1,3584]{1,0:T(1,128)}, u32[]{:S(2)}) copy-start(f32[1,3584]{1,0:T(1,128)} %gain_ref.3) | copy-start | bytes 43012
  20.3 32.6 %copy-start.10 = (bf16[144,896]{1,0:T(8,128)(2,1)}, bf16[144,896]{1,0:T(8,128)(2,1)S(1)}, u32[]{:S(2)}) copy-start(bf16[144,896]{1,0:T(8,128)(2,1)S(1)} %get-tuple-element.119.refs_0_) | copy-start | bytes 774148
  20.3 34.7 %copy-start.18 = (bf16[144,896]{1,0:T(8,128)(2,1)}, bf16[144,896]{1,0:T(8,128)(2,1)S(1)}, u32[]{:S(2)}) copy-start(bf16[144,896]{1,0:T(8,128)(2,1)S(1)} %get-tuple-element.127) | copy-start | bytes 774148
  20.3 34.7 %copy-start.22 = (bf16[144,896]{1,0:T(8,128)(2,1)}, bf16[144,896]{1,0:T(8,128)(2,1)S(1)}, u32[]{:S(2)}) copy-start(bf16[144,896]{1,0:T(8,128)(2,1)S(1)} %get-tuple-element.111) | copy-start | bytes 774148
  24.7 13.3 %collective-permute-start.5 = (bf16[512,448]{1,0:T(8,128)(2,1)S(1)}, bf16[512,448]{1,0:T(8,128)(2,1)}, u32[]{:S(2)}, u32[]{:S(2)}) collective-permute-start(bf16[512,448]{1,0:T(8,128)(2,1)S(1)} %constant_dynamic-update-slice_fusion.kv0), channel_id=1, source_target_pairs={{0,2},{1,3},{2,0},{3,1},{4,6},{5,7},{6,4},{7,5},{8,10},{9,11},{10,... | collective-permute-start | bytes 1376264 | tf_op jit(solution)/shard_map/ppermute | solution.py:37
  26.3 8.9 %collective-permute-start.3 = (bf16[144,896]{1,0:T(8,128)(2,1)S(1)}, bf16[144,896]{1,0:T(8,128)(2,1)S(1)}, u32[]{:S(2)}, u32[]{:S(2)}) collective-permute-start(bf16[144,896]{1,0:T(8,128)(2,1)S(1)} %get-tuple-element.98), channel_id=1, source_target_pairs={{0,4},{1,5},{2,6},{3,7},{4,8},{5,9},{6,10},{7,11},{8,12},{9,13},{1... | collective-permute-start | bytes 774152 | tf_op jit(solution)/shard_map/ppermute | solution.py:42
  26.3 21.3 %collective-permute-start.14 = (bf16[128,3584]{1,0:T(8,128)(2,1)S(1)}, bf16[128,3584]{1,0:T(8,128)(2,1)S(1)}, u32[]{:S(2)}, u32[]{:S(2)}) collective-permute-start(bf16[128,3584]{1,0:T(8,128)(2,1)S(1)} %bitcast.40), channel_id=1, source_target_pairs={{0,16},{1,17},{2,18},{3,19},{4,20},{5,21},{6,22},{7,23},{8,24},{9,... | collective-permute-start | bytes 2752520 | tf_op jit(solution)/shard_map/ppermute | solution.py:33
  38.0 50.0 %collective-permute-start.20 = (bf16[256,3584]{1,0:T(8,128)(2,1)S(1)}, bf16[256,3584]{1,0:T(8,128)(2,1)}, u32[]{:S(2)}, u32[]{:S(2)}) collective-permute-start(bf16[256,3584]{1,0:T(8,128)(2,1)S(1)} %bitcast.36), channel_id=1, source_target_pairs={{0,2},{1,3},{2,0},{3,1},{4,6},{5,7},{6,4},{7,5},{8,10},{9,11},{10,... | collective-permute-start | bytes 5505032 | tf_op jit(solution)/shard_map/ppermute | solution.py:37
  39.5 13.4 %collective-permute-start.6 = (bf16[512,448]{1,0:T(8,128)(2,1)S(1)}, bf16[512,448]{1,0:T(8,128)(2,1)S(1)}, u32[]{:S(2)}, u32[]{:S(2)}) collective-permute-start(bf16[512,448]{1,0:T(8,128)(2,1)S(1)} %constant_dynamic-update-slice_fusion.kv0), channel_id=1, source_target_pairs={{0,1},{1,0},{2,3},{3,2},{4,5},{5,4},{6,7},{7,6},{8,9},{9,8},{10,11... | collective-permute-start | bytes 1376264 | tf_op jit(solution)/shard_map/ppermute | solution.py:37
  39.6 11.0 %collective-permute-start.4 = (f32[1,256]{1,0:T(1,128)S(1)}, f32[1,256]{1,0:T(1,128)S(1)}, u32[]{:S(2)}, u32[]{:S(2)}) collective-permute-start(f32[1,256]{1,0:T(1,128)S(1)} %maximum_bitcast_fusion), channel_id=1, source_target_pairs={{0,16},{1,17},{2,18},{3,19},{4,20},{5,21},{6,22},{7,23},{8,24},{9,... | collective-permute-start | bytes 3080 | tf_op jit(solution)/shard_map/ppermute | solution.py:33
  41.2 15.0 %collective-permute-start.7 = (bf16[512,448]{1,0:T(8,128)(2,1)}, bf16[512,448]{1,0:T(8,128)(2,1)}, u32[]{:S(2)}, u32[]{:S(2)}) collective-permute-start(bf16[512,448]{1,0:T(8,128)(2,1)} %collective-permute-done.5.kv1), channel_id=1, source_target_pairs={{0,1},{1,0},{2,3},{3,2},{4,5},{5,4},{6,7},{7,6},{8,9},{9,8},{10,11... | collective-permute-start | bytes 1376264 | tf_op jit(solution)/shard_map/ppermute | solution.py:37
  48.5 32.1 %collective-permute-start.15 = (bf16[128,3584]{1,0:T(8,128)(2,1)}, bf16[128,3584]{1,0:T(8,128)(2,1)}, u32[]{:S(2)}, u32[]{:S(2)}) collective-permute-start(bf16[128,3584]{1,0:T(8,128)(2,1)} %bitcast.6.grad_ref), channel_id=1, source_target_pairs={{0,16},{1,17},{2,18},{3,19},{4,20},{5,21},{6,22},{7,23},{8,24},{9,... | collective-permute-start | bytes 2752520 | tf_op jit(solution)/shard_map/ppermute | solution.py:33
  50.6 4.4 %copy-start.27 = (f32[1,256]{1,0:T(1,128)}, f32[1,256]{1,0:T(1,128)S(1)}, u32[]{:S(2)}) copy-start(f32[1,256]{1,0:T(1,128)S(1)} %collective-permute-done.4) | copy-start | bytes 3076
  50.6 19.5 %collective-permute-start.8 = (bf16[144,896]{1,0:T(8,128)(2,1)}, bf16[144,896]{1,0:T(8,128)(2,1)}, u32[]{:S(2)}, u32[]{:S(2)}) collective-permute-start(bf16[144,896]{1,0:T(8,128)(2,1)} %get-tuple-element.107), channel_id=1, source_target_pairs={{0,8},{1,9},{2,10},{3,11},{4,12},{5,13},{6,14},{7,15},{8,0},{9,1},... | collective-permute-start | bytes 774152 | tf_op jit(solution)/shard_map/ppermute | solution.py:42
  53.8 19.6 %collective-permute-start.9 = (bf16[144,896]{1,0:T(8,128)(2,1)}, bf16[144,896]{1,0:T(8,128)(2,1)}, u32[]{:S(2)}, u32[]{:S(2)}) collective-permute-start(bf16[144,896]{1,0:T(8,128)(2,1)} %get-tuple-element.109), channel_id=1, source_target_pairs={{0,12},{1,13},{2,14},{3,15},{4,0},{5,1},{6,2},{7,3},{8,4},{9,5},{1... | collective-permute-start | bytes 774152 | tf_op jit(solution)/shard_map/ppermute | solution.py:42
  56.2 13.3 %collective-permute-start.16 = (f32[1,3712]{1,0:T(1,128)}, f32[1,3712]{1,0:T(1,128)}, u32[]{:S(2)}, u32[]{:S(2)}) collective-permute-start(f32[1,3712]{1,0:T(1,128)} %pad_maximum_fusion), channel_id=1, source_target_pairs={{0,16},{1,17},{2,18},{3,19},{4,20},{5,21},{6,22},{7,23},{8,24},{9,... | collective-permute-start | bytes 44552 | tf_op jit(solution)/shard_map/ppermute | solution.py:33
  57.4 1.2 copy-start.5
  58.6 1.0 copy-start.9
  60.8 8.7 %copy-start.23 = (bf16[144,896]{1,0:T(8,128)(2,1)S(1)}, bf16[144,896]{1,0:T(8,128)(2,1)}, u32[]{:S(2)}) copy-start(bf16[144,896]{1,0:T(8,128)(2,1)} %copy-done.22) | copy-start | bytes 774148
  60.8 9.2 %copy-start.21 = (bf16[144,896]{1,0:T(8,128)(2,1)S(1)}, bf16[144,896]{1,0:T(8,128)(2,1)}, u32[]{:S(2)}) copy-start(bf16[144,896]{1,0:T(8,128)(2,1)} %copy-done.20) | copy-start | bytes 774148
  60.8 12.5 %copy-start.19 = (bf16[144,896]{1,0:T(8,128)(2,1)S(1)}, bf16[144,896]{1,0:T(8,128)(2,1)}, u32[]{:S(2)}) copy-start(bf16[144,896]{1,0:T(8,128)(2,1)} %copy-done.18) | copy-start | bytes 774148
  60.8 19.7 %copy-start.11 = (bf16[144,896]{1,0:T(8,128)(2,1)S(1)}, bf16[144,896]{1,0:T(8,128)(2,1)}, u32[]{:S(2)}) copy-start(bf16[144,896]{1,0:T(8,128)(2,1)} %copy-done.10) | copy-start | bytes 774148
  60.8 19.7 %copy-start.13 = (bf16[144,896]{1,0:T(8,128)(2,1)S(1)}, bf16[144,896]{1,0:T(8,128)(2,1)}, u32[]{:S(2)}) copy-start(bf16[144,896]{1,0:T(8,128)(2,1)} %copy-done.12) | copy-start | bytes 774148
  69.5 11.0 %collective-permute-start.10 = (bf16[144,896]{1,0:T(8,128)(2,1)S(1)}, bf16[144,896]{1,0:T(8,128)(2,1)S(1)}, u32[]{:S(2)}, u32[]{:S(2)}) collective-permute-start(bf16[144,896]{1,0:T(8,128)(2,1)S(1)} %copy-done.23), channel_id=1, source_target_pairs={{0,4},{1,5},{2,6},{3,7},{4,8},{5,9},{6,10},{7,11},{8,12},{9,13},{1... | collective-permute-start | bytes 774152 | tf_op jit(solution)/shard_map/ppermute | solution.py:42
  70.1 17.9 %collective-permute-start.18 = (bf16[144,896]{1,0:T(8,128)(2,1)S(1)}, bf16[144,896]{1,0:T(8,128)(2,1)S(1)}, u32[]{:S(2)}, u32[]{:S(2)}) collective-permute-start(bf16[144,896]{1,0:T(8,128)(2,1)S(1)} %copy-done.21), channel_id=1, source_target_pairs={{0,8},{1,9},{2,10},{3,11},{4,12},{5,13},{6,14},{7,15},{8,0},{9,1},... | collective-permute-start | bytes 774152 | tf_op jit(solution)/shard_map/ppermute | solution.py:42
  73.4 14.6 %collective-permute-start.19 = (bf16[144,896]{1,0:T(8,128)(2,1)S(1)}, bf16[144,896]{1,0:T(8,128)(2,1)S(1)}, u32[]{:S(2)}, u32[]{:S(2)}) collective-permute-start(bf16[144,896]{1,0:T(8,128)(2,1)S(1)} %copy-done.19), channel_id=1, source_target_pairs={{0,12},{1,13},{2,14},{3,15},{4,0},{5,1},{6,2},{7,3},{8,4},{9,5},{1... | collective-permute-start | bytes 774152 | tf_op jit(solution)/shard_map/ppermute | solution.py:42
  89.1 27.6 %collective-permute-start.21 = (bf16[144,3584]{1,0:T(8,128)(2,1)S(1)}, bf16[144,3584]{1,0:T(8,128)(2,1)S(1)}, u32[]{:S(2)}, u32[]{:S(2)}) collective-permute-start(bf16[144,3584]{1,0:T(8,128)(2,1)S(1)} %shard_map.152.first_ref), channel_id=1, source_target_pairs={{0,1},{1,0},{2,3},{3,2},{4,5},{5,4},{6,7},{7,6},{8,9},{9,8},{10,11... | collective-permute-start | bytes 3096584 | tf_op jit(solution)/shard_map/ppermute | solution.py:37
  89.2 30.4 %collective-permute-start.17 = (bf16[144,3584]{1,0:T(8,128)(2,1)S(1)}, bf16[144,3584]{1,0:T(8,128)(2,1)S(1)}, u32[]{:S(2)}, u32[]{:S(2)}) collective-permute-start(bf16[144,3584]{1,0:T(8,128)(2,1)S(1)} %shard_map.151.first_ref), channel_id=1, source_target_pairs={{0,2},{1,3},{2,0},{3,1},{4,6},{5,7},{6,4},{7,5},{8,10},{9,11},{10,... | collective-permute-start | bytes 3096584 | tf_op jit(solution)/shard_map/ppermute | solution.py:37
  89.8 32.6 %collective-permute-start.25 = (bf16[144,3584]{1,0:T(8,128)(2,1)S(1)}, bf16[144,3584]{1,0:T(8,128)(2,1)S(1)}, u32[]{:S(2)}, u32[]{:S(2)}) collective-permute-start(bf16[144,3584]{1,0:T(8,128)(2,1)S(1)} %shard_map.151.first_ref), channel_id=1, source_target_pairs={{0,1},{1,0},{2,3},{3,2},{4,5},{5,4},{6,7},{7,6},{8,9},{9,8},{10,11... | collective-permute-start | bytes 3096584 | tf_op jit(solution)/shard_map/ppermute | solution.py:37
  89.9 13.6 %collective-permute-start.11 = (bf16[144,896]{1,0:T(8,128)(2,1)S(1)}, bf16[144,896]{1,0:T(8,128)(2,1)S(1)}, u32[]{:S(2)}, u32[]{:S(2)}) collective-permute-start(bf16[144,896]{1,0:T(8,128)(2,1)S(1)} %get-tuple-element.113), channel_id=1, source_target_pairs={{0,4},{1,5},{2,6},{3,7},{4,8},{5,9},{6,10},{7,11},{8,12},{9,13},{1... | collective-permute-start | bytes 774152 | tf_op jit(solution)/shard_map/ppermute | solution.py:42
  95.6 18.8 %collective-permute-start.12 = (bf16[144,896]{1,0:T(8,128)(2,1)S(1)}, bf16[144,896]{1,0:T(8,128)(2,1)S(1)}, u32[]{:S(2)}, u32[]{:S(2)}) collective-permute-start(bf16[144,896]{1,0:T(8,128)(2,1)S(1)} %get-tuple-element.114), channel_id=1, source_target_pairs={{0,8},{1,9},{2,10},{3,11},{4,12},{5,13},{6,14},{7,15},{8,0},{9,1},... | collective-permute-start | bytes 774152 | tf_op jit(solution)/shard_map/ppermute | solution.py:42
  103.6 13.1 %collective-permute-start.13 = (bf16[144,896]{1,0:T(8,128)(2,1)S(1)}, bf16[144,896]{1,0:T(8,128)(2,1)S(1)}, u32[]{:S(2)}, u32[]{:S(2)}) collective-permute-start(bf16[144,896]{1,0:T(8,128)(2,1)S(1)} %get-tuple-element.115), channel_id=1, source_target_pairs={{0,12},{1,13},{2,14},{3,15},{4,0},{5,1},{6,2},{7,3},{8,4},{9,5},{1... | collective-permute-start | bytes 774152 | tf_op jit(solution)/shard_map/ppermute | solution.py:42
  116.7 5.7 %copy-start.1 = (bf16[1,1,3584,256]{3,2,1,0:T(8,128)(2,1)S(1)}, bf16[1,1,3584,256]{3,2,1,0:T(8,128)(2,1)}, u32[]{:S(2)}) copy-start(bf16[1,1,3584,256]{3,2,1,0:T(8,128)(2,1)} %param.26) | copy-start | bytes 5505028
  119.6 2.8 %copy-start = (bf16[1,1,3584,256]{3,2,1,0:T(8,128)(2,1)S(1)}, bf16[1,1,3584,256]{3,2,1,0:T(8,128)(2,1)}, u32[]{:S(2)}) copy-start(bf16[1,1,3584,256]{3,2,1,0:T(8,128)(2,1)} %param.25) | copy-start | bytes 5505028
  120.7 5.9 %collective-permute-start.23 = (bf16[144,3584]{1,0:T(8,128)(2,1)S(1)}, bf16[144,3584]{1,0:T(8,128)(2,1)S(1)}, u32[]{:S(2)}, u32[]{:S(2)}) collective-permute-start(bf16[144,3584]{1,0:T(8,128)(2,1)S(1)} %shard_map.154.first_ref), channel_id=1, source_target_pairs={{0,1},{1,0},{2,3},{3,2},{4,5},{5,4},{6,7},{7,6},{8,9},{9,8},{10,11... | collective-permute-start | bytes 3096584 | tf_op jit(solution)/shard_map/ppermute | solution.py:37
  120.8 26.9 %collective-permute-start.24 = (bf16[144,3584]{1,0:T(8,128)(2,1)S(1)}, bf16[144,3584]{1,0:T(8,128)(2,1)S(1)}, u32[]{:S(2)}, u32[]{:S(2)}) collective-permute-start(bf16[144,3584]{1,0:T(8,128)(2,1)S(1)} %shard_map.154.first_ref), channel_id=1, source_target_pairs={{0,2},{1,3},{2,0},{3,1},{4,6},{5,7},{6,4},{7,5},{8,10},{9,11},{10,... | collective-permute-start | bytes 3096584 | tf_op jit(solution)/shard_map/ppermute | solution.py:37
  124.8 22.8 %collective-permute-start.26 = (bf16[144,3584]{1,0:T(8,128)(2,1)S(1)}, bf16[144,3584]{1,0:T(8,128)(2,1)S(1)}, u32[]{:S(2)}, u32[]{:S(2)}) collective-permute-start(bf16[144,3584]{1,0:T(8,128)(2,1)S(1)} %get-tuple-element.142), channel_id=1, source_target_pairs={{0,1},{1,0},{2,3},{3,2},{4,5},{5,4},{6,7},{7,6},{8,9},{9,8},{10,11... | collective-permute-start | bytes 3096584 | tf_op jit(solution)/shard_map/ppermute | solution.py:37
  125.0 22.6 %collective-permute-start.22 = (bf16[128,3584]{1,0:T(8,128)(2,1)S(1)}, bf16[128,3584]{1,0:T(8,128)(2,1)S(1)}, u32[]{:S(2)}, u32[]{:S(2)}) collective-permute-start(bf16[128,3584]{1,0:T(8,128)(2,1)S(1)} %get-tuple-element.140), channel_id=1, source_target_pairs={{0,16},{1,17},{2,18},{3,19},{4,20},{5,21},{6,22},{7,23},{8,24},{9,... | collective-permute-start | bytes 2752520 | tf_op jit(solution)/shard_map/ppermute | solution.py:33
  126.6 22.6 %collective-permute-start.34 = (bf16[144,3584]{1,0:T(8,128)(2,1)S(1)}, bf16[144,3584]{1,0:T(8,128)(2,1)S(1)}, u32[]{:S(2)}, u32[]{:S(2)}) collective-permute-start(bf16[144,3584]{1,0:T(8,128)(2,1)S(1)} %collective-permute-done.17.first_ref), channel_id=1, source_target_pairs={{0,1},{1,0},{2,3},{3,2},{4,5},{5,4},{6,7},{7,6},{8,9},{9,8},{10,11... | collective-permute-start | bytes 3096584 | tf_op jit(solution)/shard_map/ppermute | solution.py:37
  126.6 22.5 %collective-permute-start.35 = (bf16[288,256]{1,0:T(8,128)(2,1)S(1)}, bf16[288,256]{1,0:T(8,128)(2,1)S(1)}, u32[]{:S(2)}, u32[]{:S(2)}) collective-permute-start(bf16[288,256]{1,0:T(8,128)(2,1)S(1)} %get-tuple-element.135), channel_id=1, source_target_pairs={{0,2},{1,3},{2,0},{3,1},{4,6},{5,7},{6,4},{7,5},{8,10},{9,11},{10,... | collective-permute-start | bytes 442376 | tf_op jit(solution)/shard_map/ppermute | solution.py:37
  147.6 4.1 %collective-permute-start.27 = (bf16[144,3584]{1,0:T(8,128)(2,1)S(1)}, bf16[144,3584]{1,0:T(8,128)(2,1)S(1)}, u32[]{:S(2)}, u32[]{:S(2)}) collective-permute-start(bf16[144,3584]{1,0:T(8,128)(2,1)S(1)} %collective-permute-done.24.first_ref), channel_id=1, source_target_pairs={{0,1},{1,0},{2,3},{3,2},{4,5},{5,4},{6,7},{7,6},{8,9},{9,8},{10,11... | collective-permute-start | bytes 3096584 | tf_op jit(solution)/shard_map/ppermute | solution.py:37
  151.6 10.5 %collective-permute-start.36 = (bf16[144,3584]{1,0:T(8,128)(2,1)S(1)}, bf16[144,3584]{1,0:T(8,128)(2,1)S(1)}, u32[]{:S(2)}, u32[]{:S(2)}) collective-permute-start(bf16[144,3584]{1,0:T(8,128)(2,1)S(1)} %get-tuple-element.153), channel_id=1, source_target_pairs={{0,1},{1,0},{2,3},{3,2},{4,5},{5,4},{6,7},{7,6},{8,9},{9,8},{10,11... | collective-permute-start | bytes 3096584 | tf_op jit(solution)/shard_map/ppermute | solution.py:37
  153.0 6.3 %collective-permute-start.28 = (bf16[288,256]{1,0:T(8,128)(2,1)S(1)}, bf16[288,256]{1,0:T(8,128)(2,1)S(1)}, u32[]{:S(2)}, u32[]{:S(2)}) collective-permute-start(bf16[288,256]{1,0:T(8,128)(2,1)S(1)} %shard_map.157), channel_id=1, source_target_pairs={{0,2},{1,3},{2,0},{3,1},{4,6},{5,7},{6,4},{7,5},{8,10},{9,11},{10,... | collective-permute-start | bytes 442376 | tf_op jit(solution)/shard_map/ppermute | solution.py:37
  162.0 2.7 %collective-permute-start.29 = (bf16[144,3584]{1,0:T(8,128)(2,1)S(1)}, bf16[144,3584]{1,0:T(8,128)(2,1)S(1)}, u32[]{:S(2)}, u32[]{:S(2)}) collective-permute-start(bf16[144,3584]{1,0:T(8,128)(2,1)S(1)} %get-tuple-element.145), channel_id=1, source_target_pairs={{0,1},{1,0},{2,3},{3,2},{4,5},{5,4},{6,7},{7,6},{8,9},{9,8},{10,11... | collective-permute-start | bytes 3096584 | tf_op jit(solution)/shard_map/ppermute | solution.py:37
  162.4 25.3 %collective-permute-start.37 = (bf16[144,3584]{1,0:T(8,128)(2,1)S(1)}, bf16[144,3584]{1,0:T(8,128)(2,1)S(1)}, u32[]{:S(2)}, u32[]{:S(2)}) collective-permute-start(bf16[144,3584]{1,0:T(8,128)(2,1)S(1)} %add_convert_fusion), channel_id=1, source_target_pairs={{0,2},{1,3},{2,0},{3,1},{4,6},{5,7},{6,4},{7,5},{8,10},{9,11},{10,... | collective-permute-start | bytes 3096584 | tf_op jit(solution)/shard_map/ppermute | solution.py:37
  166.5 31.0 %copy-start.28 = (f32[1,256]{1,0:T(1,128)S(1)}, f32[1,256]{1,0:T(1,128)}, u32[]{:S(2)}) copy-start(f32[1,256]{1,0:T(1,128)} %copy-done.27) | copy-start | bytes 3076
  166.5 24.7 %collective-permute-start.30 = (bf16[144,896]{1,0:T(8,128)(2,1)S(1)}, bf16[144,896]{1,0:T(8,128)(2,1)S(1)}, u32[]{:S(2)}, u32[]{:S(2)}) collective-permute-start(bf16[144,896]{1,0:T(8,128)(2,1)S(1)} %get-tuple-element.146), channel_id=1, source_target_pairs={{0,16},{1,17},{2,18},{3,19},{4,20},{5,21},{6,22},{7,23},{8,24},{9,... | collective-permute-start | bytes 774152 | tf_op jit(solution)/shard_map/ppermute | solution.py:33
  168.0 28.9 %collective-permute-start.31 = (bf16[144,896]{1,0:T(8,128)(2,1)S(1)}, bf16[144,896]{1,0:T(8,128)(2,1)S(1)}, u32[]{:S(2)}, u32[]{:S(2)}) collective-permute-start(bf16[144,896]{1,0:T(8,128)(2,1)S(1)} %get-tuple-element.147), channel_id=1, source_target_pairs={{0,28},{1,29},{2,30},{3,31},{4,16},{5,17},{6,18},{7,19},{8,20},{9,... | collective-permute-start | bytes 774152 | tf_op jit(solution)/shard_map/ppermute | solution.py:33
  172.6 24.9 %collective-permute-start.32 = (bf16[144,896]{1,0:T(8,128)(2,1)S(1)}, bf16[144,896]{1,0:T(8,128)(2,1)S(1)}, u32[]{:S(2)}, u32[]{:S(2)}) collective-permute-start(bf16[144,896]{1,0:T(8,128)(2,1)S(1)} %get-tuple-element.148), channel_id=1, source_target_pairs={{0,24},{1,25},{2,26},{3,27},{4,28},{5,29},{6,30},{7,31},{8,16},{9,... | collective-permute-start | bytes 774152 | tf_op jit(solution)/shard_map/ppermute | solution.py:33
  174.1 25.1 %collective-permute-start.33 = (bf16[144,896]{1,0:T(8,128)(2,1)}, bf16[144,896]{1,0:T(8,128)(2,1)S(1)}, u32[]{:S(2)}, u32[]{:S(2)}) collective-permute-start(bf16[144,896]{1,0:T(8,128)(2,1)} %get-tuple-element.149), channel_id=1, source_target_pairs={{0,20},{1,21},{2,22},{3,23},{4,24},{5,25},{6,26},{7,27},{8,28},{9,... | collective-permute-start | bytes 774152 | tf_op jit(solution)/shard_map/ppermute | solution.py:33
  189.7 30.1 %copy-start.7 = (bf16[128,3584]{1,0:T(8,128)(2,1)S(1)}, bf16[128,3584]{1,0:T(8,128)(2,1)}, u32[]{:S(2)}) copy-start(bf16[128,3584]{1,0:T(8,128)(2,1)} %copy-done.6) | copy-start | bytes 2752516
  189.7 20.0 %collective-permute-start.38 = (bf16[144,896]{1,0:T(8,128)(2,1)}, bf16[144,896]{1,0:T(8,128)(2,1)S(1)}, u32[]{:S(2)}, u32[]{:S(2)}) collective-permute-start(bf16[144,896]{1,0:T(8,128)(2,1)} %get-tuple-element.158), channel_id=1, source_target_pairs={{0,16},{1,17},{2,18},{3,19},{4,20},{5,21},{6,22},{7,23},{8,24},{9,... | collective-permute-start | bytes 774152 | tf_op jit(solution)/shard_map/ppermute | solution.py:33
  191.2 18.5 %collective-permute-start.39 = (bf16[144,896]{1,0:T(8,128)(2,1)}, bf16[144,896]{1,0:T(8,128)(2,1)}, u32[]{:S(2)}, u32[]{:S(2)}) collective-permute-start(bf16[144,896]{1,0:T(8,128)(2,1)} %get-tuple-element.159), channel_id=1, source_target_pairs={{0,28},{1,29},{2,30},{3,31},{4,16},{5,17},{6,18},{7,19},{8,20},{9,... | collective-permute-start | bytes 774152 | tf_op jit(solution)/shard_map/ppermute | solution.py:33
  196.9 22.9 %collective-permute-start.40 = (bf16[144,896]{1,0:T(8,128)(2,1)}, bf16[144,896]{1,0:T(8,128)(2,1)}, u32[]{:S(2)}, u32[]{:S(2)}) collective-permute-start(bf16[144,896]{1,0:T(8,128)(2,1)} %get-tuple-element.160), channel_id=1, source_target_pairs={{0,24},{1,25},{2,26},{3,27},{4,28},{5,29},{6,30},{7,31},{8,16},{9,... | collective-permute-start | bytes 774152 | tf_op jit(solution)/shard_map/ppermute | solution.py:33
  197.5 22.4 %collective-permute-start.41 = (bf16[144,896]{1,0:T(8,128)(2,1)}, bf16[144,896]{1,0:T(8,128)(2,1)}, u32[]{:S(2)}, u32[]{:S(2)}) collective-permute-start(bf16[144,896]{1,0:T(8,128)(2,1)} %get-tuple-element.161), channel_id=1, source_target_pairs={{0,20},{1,21},{2,22},{3,23},{4,24},{5,25},{6,26},{7,27},{8,28},{9,... | collective-permute-start | bytes 774152 | tf_op jit(solution)/shard_map/ppermute | solution.py:33
  (9 other events, 6.5 us)

commit v8 on v7

--- a/solution.py
+++ b/solution.py
@@ -51,6 +51,7 @@
     ]
     many = isinstance(outs, list)
     shapes = outs if many else [outs]
+    moved_bytes = sum(a.size * a.dtype.itemsize for a in list(args) + shapes)
     result = pl.pallas_call(
         body,
         out_shape=shapes,
@@ -58,7 +59,9 @@
         out_specs=[pl.BlockSpec(memory_space=pltpu.VMEM) for _ in shapes],
         scratch_shapes=list(scratch),
         compiler_params=pltpu.CompilerParams(vmem_limit_bytes=vmem),
-        cost_estimate=pl.CostEstimate(flops=1, bytes_accessed=1, transcendentals=0),
+        cost_estimate=pl.CostEstimate(
+            flops=int(flops), bytes_accessed=int(moved_bytes), transcendentals=0
+        ),
     )(*args)
     return list(result) if many else result[0]
 
@@ -418,17 +421,17 @@
         return [passed_along(chunks[k], by, k) for k in range(experts)]
 
     row_chunks, grad_chunks = packed[:experts], packed[experts:]
-    row_chunks[1] = turned(row_chunks[1], 1)
-    arrived = [row_chunks[1]]
-    down_other = swapped(after([w_down], [other_chip] + arrived)[0], 2)
+    first = 1 + 2 * (experts - 1) // 3
+    for k in range(1, first):
+        row_chunks[k] = turned(row_chunks[k], k)
+    arrived = row_chunks[1:first]
+    down_other = swapped(after([w_down], [other_chip, arrived[0]])[0], 2)
     downs = (w_down, down_other)
-    there_back_middle = passed_along(after([back_middle[0]], [packed[0]])[0], -1)
-    there_back_grad = passed_along(after([back_grad[0]], arrived + [there_back_middle])[0], -1)
-    there_small = passed_along(after([front_small], arrived)[0], 1)
-    there_back_small = passed_along(after([back_small], arrived)[0], -1)
-    kv = [column, other_chip, swapped(column, 1), swapped(other_chip, 1)]
-    for k in range(2, experts):
+    far = swapped(after([other_chip], arrived)[0], 1)
+    kv = [column, other_chip, swapped(column, 1), far]
+    for k in range(first, experts):
         row_chunks[k] = turned(after([row_chunks[k]], arrived)[0], k)
+    there_back_middle = passed_along(after([back_middle[0]], arrived)[0], -1)
     beside = range(1, 2)
     for k in beside:
         grad_chunks[k] = turned(after([grad_chunks[k]], arrived)[0], k)
@@ -461,14 +464,12 @@
     for k in range(1, experts):
         if k not in beside:
             grad_chunks[k] = turned(after([grad_chunks[k]], [middle])[0], k)
-    back_rows = joined(after(ready, [middle, there_back_grad, there_small, there_back_small])[:experts])
-    grad_near = joined(after(grad_chunks, [back_rows, down_other]))
+    back_rows = joined(after(ready, [middle])[:experts])
+    grad_near = joined(after(grad_chunks, [back_rows, down_other, there_back_middle]))
     grad_near = [grad_near, swapped(grad_near, 1)]
-    back_pieces = pieces_of(back_rows)
-    there_front_from = there_small[0, :tokens].astype(jnp.int32).reshape(tokens, 1)
-    there_front_gate = there_small[0, tokens:].reshape(tokens, 1)
-    there_back_from = there_back_small[0, :tokens].astype(jnp.int32).reshape(tokens, 1)
-    there_gain = there_back_small[:, tokens:]
+    there_back_grad = passed_along(after([back_grad[0]], [grad_near[0]])[0], -1)
+    back_other = swapped(back_rows, 2)
+
     work = 2 * 2 * slots * width * hidden_width
     pair = 2 * slots
 
@@ -487,16 +488,23 @@
         flops=2 * work,
     )
     far_back = swapped(other_back, 2)
-    back_near = backward(back_pieces[:2], down_back)
+    front_near = joined(after(front_chunks, [back_other, other_back, there_back_grad]))
+    front_other = swapped(front_near, 2)
+    front_small, back_small, late = after([front_small, back_small, middle], [front_near])
+    there_middle = passed_along(late, 1)
+    there_small = passed_along(front_small, 1)
+    there_back_small = passed_along(back_small, -1)
+    there_front_from = there_small[0, :tokens].astype(jnp.int32).reshape(tokens, 1)
+    there_front_gate = there_small[0, tokens:].reshape(tokens, 1)
+    there_back_from = there_back_small[0, :tokens].astype(jnp.int32).reshape(tokens, 1)
+    there_gain = there_back_small[:, tokens:]
+    back_near = backward((back_rows, swapped(after([back_rows], [front_near])[0], 1)), down_back)
     back_core = swapped(back_near[1], 1)
-    front_near = joined(after(front_chunks, [back_pieces[2], other_back]))
-    front_other = swapped(front_near, 2)
-    there_middle = passed_along(after([middle], [front_near])[0], 1)
     front_core = swapped(front_near, 1)
     hidden_near = hidden((front_near, front_core))
-    (front_other,) = after([front_other], [back_core, hidden_near, there_middle])
+    (front_other,) = after([front_other], [back_core, hidden_near, there_middle, there_small, there_back_small])
     (far_back,) = after([far_back], [front_other])
-    back_far = backward(back_pieces[2:], far_back)
+    back_far = backward((back_other, swapped(back_other, 1)), far_back)
     chip = back_far[0].astype(f32) + swapped(back_far[1], 1).astype(f32)
     chip = chip.astype(bf16)
     hidden_far = hidden((front_other, swapped(front_other, 1)))

time: 225 us -> 231 us (1.027)
  waiting for transfers between devices: 103 us -> 108 us
  Pallas kernels: 39 us -> 41.9 us
    ppermute x9, waiting for transfers between devices: 35.8 us -> 46.2 us  [turned(): lax.ppermute(array, 'expert', [(i, (i + by * GROUP) % length) for i in ra...]
    ppermute x13, waiting for transfers between devices: 44.1 us -> 39.1 us  [passed_along(): return lax.ppermute(array, ('section', 'expert'), pairs)]
    pallas_call x15, Pallas kernels: 39 us -> 41.9 us  [call(): pl.pallas_call(body, out_shape=shapes, in_specs=specs, out_specs=[pl.Bloc...]
    unnamed x66 -> x68, local copies, waits for them, and re-layouts: 13.1 us -> 12 us
  transfers between devices with their start and end apart: 42 -> 42, of which waited for: 16 -> 15; matrix products, arithmetic and copies ran while one was open for 3% -> 2% of each run, Pallas kernels for 15% -> 16%
where the time goes in v8:
time: 231 us; the launch traced here: 230 us
  waiting for transfers between devices  108 us (47%)
  starting transfers between devices  60.7 us (26%)
  Pallas kernels  41.9 us (18%)
  local copies, waits for them, and re-layouts  14.8 us (6%)
  other arithmetic  3.2 us (1%)
    ppermute x9, waiting for transfers between devices, turned(): lax.ppermute(array, 'expert', [(i, (i + by * GROUP) % length) for i in ra...  46.2 us
    pallas_call x15, Pallas kernels, call(): pl.pallas_call(body, out_shape=shapes, in_specs=specs, out_specs=[pl.Bloc...  41.9 us
    ppermute x13, waiting for transfers between devices, passed_along(): return lax.ppermute(array, ('section', 'expert'), pairs)  39.1 us
    ppermute x17, waiting for transfers between devices, swapped(): lax.ppermute(array, 'expert', [(i, i ^ bit) for i in range(lax.axis_size(...  22.9 us
    ppermute x13, starting transfers between devices, passed_along(): return lax.ppermute(array, ('section', 'expert'), pairs)  22 us
    ppermute x9, starting transfers between devices, turned(): lax.ppermute(array, 'expert', [(i, (i + by * GROUP) % length) for i in ra...  16.1 us
    unnamed x68, local copies, waits for them, and re-layouts  12 us
    ppermute x3, starting transfers between devices, shards(): column.append(lax.ppermute(keys_values[0], 'expert', pairs))  11.4 us
  transfers between devices with their start and end apart: 42, of which 15 were waited for; matrix products, arithmetic and copies ran while one was open for 2% of the time, Pallas kernels for 16%

profile of v8, /device:TPU:0, one launch (start us, length us, event | category | flops | bytes accessed | tf_op | source)
XLA Modules:
  0.0 229.9 jit_solution(18063522297784335631)
XLA Ops:
  0.6 1.0 copy.16
  1.6 4.9 %collective-permute-start = (bf16[128,448]{1,0:T(8,128)(2,1)S(1)}, bf16[128,448]{1,0:T(8,128)(2,1)S(1)}, u32[]{:S(2)}, u32[]{:S(2)}) collective-permute-start(bf16[128,448]{1,0:T(8,128)(2,1)S(1)} %bitcast.43), channel_id=1, source_target_pairs={{0,4},{1,5},{2,6},{3,7},{4,8},{5,9},{6,10},{7,11},{8,12},{9,13},{1... | collective-permute-start | bytes 344072 | tf_op jit(solution)/shard_map/ppermute | solution.py:383
  6.6 4.5 %collective-permute-start.1 = (bf16[128,448]{1,0:T(8,128)(2,1)S(1)}, bf16[128,448]{1,0:T(8,128)(2,1)S(1)}, u32[]{:S(2)}, u32[]{:S(2)}) collective-permute-start(bf16[128,448]{1,0:T(8,128)(2,1)S(1)} %bitcast.44), channel_id=1, source_target_pairs={{0,8},{1,9},{2,10},{3,11},{4,12},{5,13},{6,14},{7,15},{16,24},{17,... | collective-permute-start | bytes 344072 | tf_op jit(solution)/shard_map/ppermute | solution.py:383
  11.1 2.0 collective-permute-start.2
  13.8 1.2 fusion.11
  15.8 1.2 copy-done.9
  17.0 3.6 %shard_map.149 = (bf16[144,896]{1,0:T(8,128)(2,1)S(1)}, bf16[144,896]{1,0:T(8,128)(2,1)S(1)}, bf16[144,896]{1,0:T(8,128)(2,1)S(1)}, bf16[144,896]{1,0:T(8,128)(2...) custom-call(s32[1,128]{1,0:T(1,128)S(1)} %get-tuple-element.173.rout, ...), custom_call_target="tpu_custom_call" | custom-call | flops 2113929216 | bytes 3914752 | tf_op jit(solution)/shard_map/pallas_call | solution.py:55
  22.1 0.9 constant_dynamic-update-slice_fusion.1
  23.0 0.9 constant_dynamic-update-slice_fusion.kv0
  23.9 1.6 collective-permute-start.3
  25.5 8.9 %collective-permute-done.5.refs_1_ = bf16[144,896]{1,0:T(8,128)(2,1)S(1)} collective-permute-done((bf16[144,896]{1,0:T(8,128)(2,1)S(1)}, bf16[144,896]{1,0:T(8,128)(2,1)S(1)}, u32[]{:S(2)}, u32[]{:S(2)}) %collective-permute-start.5) | collective-permute-done | bytes 258080 | tf_op jit(solution)/shard_map/ppermute | solution.py:42
  35.1 2.1 collective-permute-done.3.kv1
  37.2 1.5 collective-permute-start.16
  38.7 11.4 %collective-permute-done.6.refs_2_ = bf16[144,896]{1,0:T(8,128)(2,1)S(1)} collective-permute-done((bf16[144,896]{1,0:T(8,128)(2,1)S(1)}, bf16[144,896]{1,0:T(8,128)(2,1)S(1)}, u32[]{:S(2)}, u32[]{:S(2)}) %collective-permute-start.6) | collective-permute-done | bytes 258080 | tf_op jit(solution)/shard_map/ppermute | solution.py:42
  50.8 1.5 collective-permute-start.17
  52.8 0.8 reshape_squeeze.6.chosen_ref
  54.2 2.3 %collective-permute-start.8 = (bf16[144,896]{1,0:T(8,128)(2,1)}, bf16[144,896]{1,0:T(8,128)(2,1)}, u32[]{:S(2)}, u32[]{:S(2)}) collective-permute-start(bf16[144,896]{1,0:T(8,128)(2,1)} %get-tuple-element.109), channel_id=1, source_target_pairs={{0,12},{1,13},{2,14},{3,15},{4,0},{5,1},{6,2},{7,3},{8,4},{9,5},{1... | collective-permute-start | bytes 774152 | tf_op jit(solution)/shard_map/ppermute | solution.py:42
  56.7 1.2 copy-done.8
  57.9 8.5 %shard_map.150 = (bf16[128,3584]{1,0:T(8,128)(2,1)S(1)}, bf16[144,896]{1,0:T(8,128)(2,1)S(1)}, bf16[144,896]{1,0:T(8,128)(2,1)S(1)}, bf16[144,896]{1,0:T(8,128)(2,1)S(1)}, bf16[144,896]{1,0:T(8,128)(2,1)S(1)}) custom-call(s32[16]{0:T(128)S(1)} %reshape_squeeze.6.chosen_ref, s32[16]{0:T(128)S(1)} %fusion.10.index_ref, s32[1]{0:T(128)} %bitcast.4.base_ref, ...), custom_call_target="tpu_custom_call" | custom-call | flops 1593835520 | bytes 5634692 | tf_op jit(solution)/shard_map/pallas_call | solution.py:55
  67.0 3.3 %collective-permute-start.15 = (bf16[144,896]{1,0:T(8,128)(2,1)S(1)}, bf16[144,896]{1,0:T(8,128)(2,1)S(1)}, u32[]{:S(2)}, u32[]{:S(2)}) collective-permute-start(bf16[144,896]{1,0:T(8,128)(2,1)S(1)} %copy-done.16), channel_id=1, source_target_pairs={{0,12},{1,13},{2,14},{3,15},{4,0},{5,1},{6,2},{7,3},{8,4},{9,5},{1... | collective-permute-start | bytes 774152 | tf_op jit(solution)/shard_map/ppermute | solution.py:42
  70.4 2.0 shard_map.151.first_ref
  72.4 9.4 %collective-permute-done.14.refs_2_ = bf16[144,896]{1,0:T(8,128)(2,1)S(1)} collective-permute-done((bf16[144,896]{1,0:T(8,128)(2,1)S(1)}, bf16[144,896]{1,0:T(8,128)(2,1)S(1)}, u32[]{:S(2)}, u32[]{:S(2)}) %collective-permute-start.14) | collective-permute-done | bytes 258080 | tf_op jit(solution)/shard_map/ppermute | solution.py:42
  81.9 1.1 shard_map.152.first_ref
  84.2 5.1 %collective-permute-start.10 = (bf16[144,896]{1,0:T(8,128)(2,1)S(1)}, bf16[144,896]{1,0:T(8,128)(2,1)S(1)}, u32[]{:S(2)}, u32[]{:S(2)}) collective-permute-start(bf16[144,896]{1,0:T(8,128)(2,1)S(1)} %get-tuple-element.113), channel_id=1, source_target_pairs={{0,4},{1,5},{2,6},{3,7},{4,8},{5,9},{6,10},{7,11},{8,12},{9,13},{1... | collective-permute-start | bytes 774152 | tf_op jit(solution)/shard_map/ppermute | solution.py:42
  89.3 2.6 %collective-permute-start.11 = (bf16[144,896]{1,0:T(8,128)(2,1)S(1)}, bf16[144,896]{1,0:T(8,128)(2,1)S(1)}, u32[]{:S(2)}, u32[]{:S(2)}) collective-permute-start(bf16[144,896]{1,0:T(8,128)(2,1)S(1)} %get-tuple-element.114), channel_id=1, source_target_pairs={{0,8},{1,9},{2,10},{3,11},{4,12},{5,13},{6,14},{7,15},{8,0},{9,1},... | collective-permute-start | bytes 774152 | tf_op jit(solution)/shard_map/ppermute | solution.py:42
  91.8 6.6 %collective-permute-done.10.refs_1_ = bf16[144,896]{1,0:T(8,128)(2,1)S(1)} collective-permute-done((bf16[144,896]{1,0:T(8,128)(2,1)S(1)}, bf16[144,896]{1,0:T(8,128)(2,1)S(1)}, u32[]{:S(2)}, u32[]{:S(2)}) %collective-permute-start.10) | collective-permute-done | bytes 258080 | tf_op jit(solution)/shard_map/ppermute | solution.py:42
  98.4 2.2 collective-permute-start.12
  100.6 8.2 %collective-permute-done.11.refs_2_ = bf16[144,896]{1,0:T(8,128)(2,1)S(1)} collective-permute-done((bf16[144,896]{1,0:T(8,128)(2,1)S(1)}, bf16[144,896]{1,0:T(8,128)(2,1)S(1)}, u32[]{:S(2)}, u32[]{:S(2)}) %collective-permute-start.11) | collective-permute-done | bytes 258080 | tf_op jit(solution)/shard_map/ppermute | solution.py:42
  108.7 1.7 collective-permute-done.12.refs_3_
  110.5 2.8 %shard_map.153 = (f32[288,256]{1,0:T(8,128)S(1)}, bf16[288,256]{1,0:T(8,128)(2,1)S(1)}) custom-call(bf16[144,3584]{1,0:T(8,128)(2,1)S(1)} %shard_map.152.first_ref, bf16[144,3584]{1,0:T(8,128)(2,1)S(1)} %collective-permute-done.18.second_ref, bf16[256,3584]{1,0:T(8,128)(2,1)S(1)} %bitcast.37, bf16[256,3584]{1,0:T(8,128)(2,1)} %collective-permute-done.16.far_ref), custom_call_target="tpu_custom_call" | custom-call | flops 1056964608 | bytes 6176768 | tf_op jit(solution)/shard_map/pallas_call | solution.py:55
  113.3 0.9 copy-done.11
  114.2 1.1 shard_map.154.first_ref
  116.0 1.5 collective-permute-start.23
  118.0 2.5 %shard_map.156 = (bf16[144,3584]{1,0:T(8,128)(2,1)S(1)}, bf16[144,3584]{1,0:T(8,128)(2,1)S(1)}) custom-call(bf16[144,3584]{1,0:T(8,128)(2,1)S(1)} %shard_map.151.first_ref, bf16[144,3584]{1,0:T(8,128)(2,1)S(1)} %collective-permute-done.24.second_ref, f32[288,256]{1,0:T(8,128)S(1)} %get-tuple-element.142.back_ref, bf16[3584,256]{1,0:T(8,128)(2,1)S(1)} %bitcast.28, ...), custom_call_target="tpu_custom_call" | custom-call | flops 2113929216 | bytes 8093696 | tf_op jit(solution)/shard_map/pallas_call | solution.py:55
  120.7 1.6 collective-permute-start.21
  122.8 20.6 %collective-permute-done.20 = f32[1,256]{1,0:T(1,128)S(1)} collective-permute-done((f32[1,256]{1,0:T(1,128)S(1)}, f32[1,256]{1,0:T(1,128)S(1)}, u32[]{:S(2)}, u32[]{:S(2)}) %collective-permute-start.20) | collective-permute-done | bytes 1056 | tf_op jit(solution)/shard_map/ppermute | solution.py:33
  143.5 1.5 collective-permute-start.26
  145.0 1.3 shard_map.155.own_ref
  146.3 0.9 collective-permute-done.26
  147.2 1.5 collective-permute-start.35
  148.7 0.9 copy-done.13
  149.6 1.0 copy-done.3
  150.7 1.7 collective-permute-done.35.back_ref
  152.4 2.5 %shard_map.160 = (bf16[144,3584]{1,0:T(8,128)(2,1)S(1)}, bf16[144,3584]{1,0:T(8,128)(2,1)S(1)}) custom-call(bf16[144,3584]{1,0:T(8,128)(2,1)S(1)} %collective-permute-done.13.first_ref, bf16[144,3584]{1,0:T(8,128)(2,1)S(1)} %collective-permute-done.34.second_ref, bf16[288,256]{1,0:T(8,128)(2,1)S(1)} %collective-permute-done.35.back_ref, ...), custom_call_target="tpu_custom_call" | custom-call | flops 2113929216 | bytes 7946240 | tf_op jit(solution)/shard_map/pallas_call | solution.py:55
  154.9 1.3 shard_map.157
  156.2 1.6 collective-permute-start.28
  157.8 4.7 %collective-permute-done.28.other_ref = bf16[288,256]{1,0:T(8,128)(2,1)S(1)} collective-permute-done((bf16[288,256]{1,0:T(8,128)(2,1)S(1)}, bf16[288,256]{1,0:T(8,128)(2,1)S(1)}, u32[]{:S(2)}, u32[]{:S(2)}) %collective-permute-start.28) | collective-permute-done | bytes 147488 | tf_op jit(solution)/shard_map/ppermute | solution.py:37
  162.5 2.7 %shard_map.158 = (bf16[144,3584]{1,0:T(8,128)(2,1)S(1)}, bf16[144,3584]{1,0:T(8,128)(2,1)S(1)}) custom-call(bf16[288,256]{1,0:T(8,128)(2,1)S(1)} %shard_map.155.own_ref, bf16[288,256]{1,0:T(8,128)(2,1)S(1)} %collective-permute-done.28.other_ref, bf16[256,3584]{1,0:T(8,128)(2,1)S(1)} %bitcast.38, bf16[256,3584]{1,0:T(8,128)(2,1)} %collective-permute-done.16.far_ref), custom_call_target="tpu_custom_call" | custom-call | flops 1056964608 | bytes 6029312 | tf_op jit(solution)/shard_map/pallas_call | solution.py:55
  165.3 1.2 add_convert_fusion
  166.6 1.5 collective-permute-start.37
  168.1 1.9 shard_map.159
  170.0 1.5 collective-permute-start.30
  171.5 4.0 %collective-permute-start.31 = (bf16[144,896]{1,0:T(8,128)(2,1)}, bf16[144,896]{1,0:T(8,128)(2,1)}, u32[]{:S(2)}, u32[]{:S(2)}) collective-permute-start(bf16[144,896]{1,0:T(8,128)(2,1)} %get-tuple-element.149), channel_id=1, source_target_pairs={{0,28},{1,29},{2,30},{3,31},{4,16},{5,17},{6,18},{7,19},{8,20},{9,... | collective-permute-start | bytes 774152 | tf_op jit(solution)/shard_map/ppermute | solution.py:33
  175.4 2.7 %collective-permute-start.32 = (bf16[144,896]{1,0:T(8,128)(2,1)}, bf16[144,896]{1,0:T(8,128)(2,1)}, u32[]{:S(2)}, u32[]{:S(2)}) collective-permute-start(bf16[144,896]{1,0:T(8,128)(2,1)} %get-tuple-element.150), channel_id=1, source_target_pairs={{0,24},{1,25},{2,26},{3,27},{4,28},{5,29},{6,30},{7,31},{8,16},{9,... | collective-permute-start | bytes 774152 | tf_op jit(solution)/shard_map/ppermute | solution.py:33
  178.3 13.7 %collective-permute-done.37.refs_2_ = bf16[144,3584]{1,0:T(8,128)(2,1)} collective-permute-done((bf16[144,3584]{1,0:T(8,128)(2,1)}, bf16[144,3584]{1,0:T(8,128)(2,1)}, u32[]{:S(2)}, u32[]{:S(2)}) %collective-permute-start.37) | collective-permute-done | bytes 1032224 | tf_op jit(solution)/shard_map/ppermute | solution.py:37
  192.1 3.3 %shard_map.161 = (bf16[144,896]{1,0:T(8,128)(2,1)}, bf16[144,896]{1,0:T(8,128)(2,1)}, bf16[144,896]{1,0:T(8,128)(2,1)}, bf16[144,896]{1,0:T(8,128)(2,1)}) custom-call(bf16[144,3584]{1,0:T(8,128)(2,1)S(1)} %get-tuple-element.157.refs_0_, bf16[144,3584]{1,0:T(8,128)(2,1)S(1)} %copy-done.4, bf16[144,3584]{1,0:T(8,128)(2,1)} %collective-permute-done.37.refs_2_), custom_call_target="tpu_custom_call" | custom-call | bytes 4128768 | tf_op jit(solution)/shard_map/pallas_call | solution.py:55
  195.4 1.5 collective-permute-start.38
  196.9 4.0 %collective-permute-start.39 = (bf16[144,896]{1,0:T(8,128)(2,1)}, bf16[144,896]{1,0:T(8,128)(2,1)S(1)}, u32[]{:S(2)}, u32[]{:S(2)}) collective-permute-start(bf16[144,896]{1,0:T(8,128)(2,1)} %get-tuple-element.161), channel_id=1, source_target_pairs={{0,28},{1,29},{2,30},{3,31},{4,16},{5,17},{6,18},{7,19},{8,20},{9,... | collective-permute-start | bytes 774152 | tf_op jit(solution)/shard_map/ppermute | solution.py:33
  200.9 2.7 %collective-permute-start.40 = (bf16[144,896]{1,0:T(8,128)(2,1)}, bf16[144,896]{1,0:T(8,128)(2,1)S(1)}, u32[]{:S(2)}, u32[]{:S(2)}) collective-permute-start(bf16[144,896]{1,0:T(8,128)(2,1)} %get-tuple-element.162), channel_id=1, source_target_pairs={{0,24},{1,25},{2,26},{3,27},{4,28},{5,29},{6,30},{7,31},{8,16},{9,... | collective-permute-start | bytes 774152 | tf_op jit(solution)/shard_map/ppermute | solution.py:33
  203.8 1.2 copy-done.14
  205.0 3.4 %shard_map.162 = bf16[128,3584]{1,0:T(8,128)(2,1)} custom-call(s32[128,1]{1,0:T(8,128)S(1)} %copy.18.route_ref, f32[128,1]{1,0:T(8,128)S(1)} %copy.19.gate_ref, bf16[128,3584]{1,0:T(8,128)(2,1)S(1)} %copy-done.14, bf16[144,896]{1,0:T(8,128)(2,1)S(1)} %collective-permute-done.30.refs_0_, bf16[144,896]{1,0:T(8,128)(2,1)} %collective-permute-done.31.refs_1_, ...), custom_call_target="tpu_custom_call" | custom-call | flops 1056964608 | bytes 2868224 | tf_op jit(solution)/shard_map/pallas_call | solution.py:55
  208.4 3.9 %collective-permute-done.38.refs_0_ = bf16[144,896]{1,0:T(8,128)(2,1)S(1)} collective-permute-done((bf16[144,896]{1,0:T(8,128)(2,1)}, bf16[144,896]{1,0:T(8,128)(2,1)S(1)}, u32[]{:S(2)}, u32[]{:S(2)}) %collective-permute-start.38) | collective-permute-done | bytes 258080 | tf_op jit(solution)/shard_map/ppermute | solution.py:33
  212.4 13.6 %collective-permute-done.40.refs_2_ = bf16[144,896]{1,0:T(8,128)(2,1)S(1)} collective-permute-done((bf16[144,896]{1,0:T(8,128)(2,1)}, bf16[144,896]{1,0:T(8,128)(2,1)S(1)}, u32[]{:S(2)}, u32[]{:S(2)}) %collective-permute-start.40) | collective-permute-done | bytes 258080 | tf_op jit(solution)/shard_map/ppermute | solution.py:33
  226.0 3.9 %shard_map.163 = bf16[128,3584]{1,0:T(8,128)(2,1)} custom-call(s32[128,1]{1,0:T(8,128)S(1)} %copy.20.route_ref, f32[1,3584]{1,0:T(1,128)S(1)} %slice.19.gain_ref, bf16[128,3584]{1,0:T(8,128)(2,1)} %collective-permute-done.17.middle_ref, bf16[128,3584]{1,0:T(8,128)(2,1)S(1)} %copy-done.12, bf16[144,896]{1,0:T(8,128)(2,1)S(1)} %collective-permute-done.38.refs_0_, ...), custom_call_target="tpu_custom_call" | custom-call | flops 1056964608 | bytes 3799552 | tf_op jit(solution)/shard_map/pallas_call | solution.py:55
  (119 shorter events, 9.9 us)
Async XLA Ops:
  1.6 19.7 %collective-permute-start = (bf16[128,448]{1,0:T(8,128)(2,1)S(1)}, bf16[128,448]{1,0:T(8,128)(2,1)S(1)}, u32[]{:S(2)}, u32[]{:S(2)}) collective-permute-start(bf16[128,448]{1,0:T(8,128)(2,1)S(1)} %bitcast.43), channel_id=1, source_target_pairs={{0,4},{1,5},{2,6},{3,7},{4,8},{5,9},{6,10},{7,11},{8,12},{9,13},{1... | collective-permute-start | bytes 344072 | tf_op jit(solution)/shard_map/ppermute | solution.py:383
  6.6 14.7 %collective-permute-start.1 = (bf16[128,448]{1,0:T(8,128)(2,1)S(1)}, bf16[128,448]{1,0:T(8,128)(2,1)S(1)}, u32[]{:S(2)}, u32[]{:S(2)}) collective-permute-start(bf16[128,448]{1,0:T(8,128)(2,1)S(1)} %bitcast.44), channel_id=1, source_target_pairs={{0,8},{1,9},{2,10},{3,11},{4,12},{5,13},{6,14},{7,15},{16,24},{17,... | collective-permute-start | bytes 344072 | tf_op jit(solution)/shard_map/ppermute | solution.py:383
  11.1 10.3 %collective-permute-start.2 = (bf16[128,448]{1,0:T(8,128)(2,1)S(1)}, bf16[128,448]{1,0:T(8,128)(2,1)}, u32[]{:S(2)}, u32[]{:S(2)}) collective-permute-start(bf16[128,448]{1,0:T(8,128)(2,1)S(1)} %bitcast.45), channel_id=1, source_target_pairs={{0,12},{1,13},{2,14},{3,15},{16,28},{17,29},{18,30},{19,31}} | collective-permute-start | bytes 344072 | tf_op jit(solution)/shard_map/ppermute | solution.py:383
  16.9 20.2 %copy-start.2 = (bf16[1,1,256,3584]{3,2,1,0:T(8,128)(2,1)S(1)}, bf16[1,1,256,3584]{3,2,1,0:T(8,128)(2,1)}, u32[]{:S(2)}) copy-start(bf16[1,1,256,3584]{3,2,1,0:T(8,128)(2,1)} %param.27) | copy-start | bytes 5505028
  16.9 39.8 %copy-start.6 = (f32[1,3584]{1,0:T(1,128)S(1)}, f32[1,3584]{1,0:T(1,128)}, u32[]{:S(2)}) copy-start(f32[1,3584]{1,0:T(1,128)} %gain_ref.3) | copy-start | bytes 43012
  16.9 39.8 %copy-start.7 = (bf16[1,128,3584]{2,1,0:T(8,128)(2,1)S(1)}, bf16[1,128,3584]{2,1,0:T(8,128)(2,1)}, u32[]{:S(2)}) copy-start(bf16[1,128,3584]{2,1,0:T(8,128)(2,1)} %param.14) | copy-start | bytes 2752516
  21.3 28.8 %copy-start.17 = (bf16[144,896]{1,0:T(8,128)(2,1)}, bf16[144,896]{1,0:T(8,128)(2,1)S(1)}, u32[]{:S(2)}) copy-start(bf16[144,896]{1,0:T(8,128)(2,1)S(1)} %get-tuple-element.122) | copy-start | bytes 774148
  21.3 31.0 %copy-start.19 = (bf16[144,896]{1,0:T(8,128)(2,1)}, bf16[144,896]{1,0:T(8,128)(2,1)S(1)}, u32[]{:S(2)}) copy-start(bf16[144,896]{1,0:T(8,128)(2,1)S(1)} %get-tuple-element.111) | copy-start | bytes 774148
  21.3 31.0 %copy-start.24 = (bf16[144,896]{1,0:T(8,128)(2,1)}, bf16[144,896]{1,0:T(8,128)(2,1)S(1)}, u32[]{:S(2)}) copy-start(bf16[144,896]{1,0:T(8,128)(2,1)S(1)} %get-tuple-element.127.refs_0_) | copy-start | bytes 774148
  21.3 31.0 %copy-start.26 = (bf16[144,896]{1,0:T(8,128)(2,1)}, bf16[144,896]{1,0:T(8,128)(2,1)S(1)}, u32[]{:S(2)}) copy-start(bf16[144,896]{1,0:T(8,128)(2,1)S(1)} %get-tuple-element.116.refs_0_) | copy-start | bytes 774148
  23.9 13.3 %collective-permute-start.3 = (bf16[512,448]{1,0:T(8,128)(2,1)S(1)}, bf16[512,448]{1,0:T(8,128)(2,1)}, u32[]{:S(2)}, u32[]{:S(2)}) collective-permute-start(bf16[512,448]{1,0:T(8,128)(2,1)S(1)} %constant_dynamic-update-slice_fusion.kv0), channel_id=1, source_target_pairs={{0,2},{1,3},{2,0},{3,1},{4,6},{5,7},{6,4},{7,5},{8,10},{9,11},{10,... | collective-permute-start | bytes 1376264 | tf_op jit(solution)/shard_map/ppermute | solution.py:37
  25.5 8.9 %collective-permute-start.5 = (bf16[144,896]{1,0:T(8,128)(2,1)S(1)}, bf16[144,896]{1,0:T(8,128)(2,1)S(1)}, u32[]{:S(2)}, u32[]{:S(2)}) collective-permute-start(bf16[144,896]{1,0:T(8,128)(2,1)S(1)} %get-tuple-element.99), channel_id=1, source_target_pairs={{0,4},{1,5},{2,6},{3,7},{4,8},{5,9},{6,10},{7,11},{8,12},{9,13},{1... | collective-permute-start | bytes 774152 | tf_op jit(solution)/shard_map/ppermute | solution.py:42
  37.2 44.7 %collective-permute-start.16 = (bf16[256,3584]{1,0:T(8,128)(2,1)S(1)}, bf16[256,3584]{1,0:T(8,128)(2,1)}, u32[]{:S(2)}, u32[]{:S(2)}) collective-permute-start(bf16[256,3584]{1,0:T(8,128)(2,1)S(1)} %bitcast.36), channel_id=1, source_target_pairs={{0,2},{1,3},{2,0},{3,1},{4,6},{5,7},{6,4},{7,5},{8,10},{9,11},{10,... | collective-permute-start | bytes 5505032 | tf_op jit(solution)/shard_map/ppermute | solution.py:37
  38.7 11.4 %collective-permute-start.6 = (bf16[144,896]{1,0:T(8,128)(2,1)S(1)}, bf16[144,896]{1,0:T(8,128)(2,1)S(1)}, u32[]{:S(2)}, u32[]{:S(2)}) collective-permute-start(bf16[144,896]{1,0:T(8,128)(2,1)S(1)} %get-tuple-element.100), channel_id=1, source_target_pairs={{0,8},{1,9},{2,10},{3,11},{4,12},{5,13},{6,14},{7,15},{8,0},{9,1},... | collective-permute-start | bytes 774152 | tf_op jit(solution)/shard_map/ppermute | solution.py:42
  50.8 31.1 %collective-permute-start.17 = (bf16[128,3584]{1,0:T(8,128)(2,1)}, bf16[128,3584]{1,0:T(8,128)(2,1)}, u32[]{:S(2)}, u32[]{:S(2)}) collective-permute-start(bf16[128,3584]{1,0:T(8,128)(2,1)} %bitcast.10.middle_ref), channel_id=1, source_target_pairs={{0,16},{1,17},{2,18},{3,19},{4,20},{5,21},{6,22},{7,23},{8,24},{9,... | collective-permute-start | bytes 2752520 | tf_op jit(solution)/shard_map/ppermute | solution.py:33
  52.3 4.3 %collective-permute-start.4 = (bf16[512,448]{1,0:T(8,128)(2,1)S(1)}, bf16[512,448]{1,0:T(8,128)(2,1)}, u32[]{:S(2)}, u32[]{:S(2)}) collective-permute-start(bf16[512,448]{1,0:T(8,128)(2,1)S(1)} %constant_dynamic-update-slice_fusion.kv0), channel_id=1, source_target_pairs={{0,1},{1,0},{2,3},{3,2},{4,5},{5,4},{6,7},{7,6},{8,9},{9,8},{10,11... | collective-permute-start | bytes 1376264 | tf_op jit(solution)/shard_map/ppermute | solution.py:37
  52.3 4.4 %collective-permute-start.7 = (bf16[512,448]{1,0:T(8,128)(2,1)}, bf16[512,448]{1,0:T(8,128)(2,1)}, u32[]{:S(2)}, u32[]{:S(2)}) collective-permute-start(bf16[512,448]{1,0:T(8,128)(2,1)} %collective-permute-done.3.kv1), channel_id=1, source_target_pairs={{0,1},{1,0},{2,3},{3,2},{4,5},{5,4},{6,7},{7,6},{8,9},{9,8},{10,11... | collective-permute-start | bytes 1376264 | tf_op jit(solution)/shard_map/ppermute | solution.py:37
  54.2 12.8 %collective-permute-start.8 = (bf16[144,896]{1,0:T(8,128)(2,1)}, bf16[144,896]{1,0:T(8,128)(2,1)}, u32[]{:S(2)}, u32[]{:S(2)}) collective-permute-start(bf16[144,896]{1,0:T(8,128)(2,1)} %get-tuple-element.109), channel_id=1, source_target_pairs={{0,12},{1,13},{2,14},{3,15},{4,0},{5,1},{6,2},{7,3},{8,4},{9,5},{1... | collective-permute-start | bytes 774152 | tf_op jit(solution)/shard_map/ppermute | solution.py:42
  56.6 13.7 %collective-permute-start.9 = (bf16[144,896]{1,0:T(8,128)(2,1)}, bf16[144,896]{1,0:T(8,128)(2,1)S(1)}, u32[]{:S(2)}, u32[]{:S(2)}) collective-permute-start(bf16[144,896]{1,0:T(8,128)(2,1)} %copy-done.19), channel_id=1, source_target_pairs={{0,4},{1,5},{2,6},{3,7},{4,8},{5,9},{6,10},{7,11},{8,12},{9,13},{1... | collective-permute-start | bytes 774152 | tf_op jit(solution)/shard_map/ppermute | solution.py:42
  57.9 8.5 %copy-start.18 = (bf16[144,896]{1,0:T(8,128)(2,1)S(1)}, bf16[144,896]{1,0:T(8,128)(2,1)}, u32[]{:S(2)}) copy-start(bf16[144,896]{1,0:T(8,128)(2,1)} %copy-done.17) | copy-start | bytes 774148
  57.9 9.1 %copy-start.16 = (bf16[144,896]{1,0:T(8,128)(2,1)S(1)}, bf16[144,896]{1,0:T(8,128)(2,1)}, u32[]{:S(2)}) copy-start(bf16[144,896]{1,0:T(8,128)(2,1)} %copy-done.15) | copy-start | bytes 774148
  57.9 12.4 %copy-start.21 = (bf16[144,896]{1,0:T(8,128)(2,1)S(1)}, bf16[144,896]{1,0:T(8,128)(2,1)}, u32[]{:S(2)}) copy-start(bf16[144,896]{1,0:T(8,128)(2,1)} %copy-done.20) | copy-start | bytes 774148
  57.9 12.4 %copy-start.23 = (bf16[144,896]{1,0:T(8,128)(2,1)S(1)}, bf16[144,896]{1,0:T(8,128)(2,1)}, u32[]{:S(2)}) copy-start(bf16[144,896]{1,0:T(8,128)(2,1)} %copy-done.22) | copy-start | bytes 774148
  57.9 12.5 %copy-start.27 = (bf16[144,896]{1,0:T(8,128)(2,1)S(1)}, bf16[144,896]{1,0:T(8,128)(2,1)}, u32[]{:S(2)}) copy-start(bf16[144,896]{1,0:T(8,128)(2,1)} %copy-done.26) | copy-start | bytes 774148
  66.4 15.5 %copy-start.25 = (bf16[144,896]{1,0:T(8,128)(2,1)S(1)}, bf16[144,896]{1,0:T(8,128)(2,1)}, u32[]{:S(2)}) copy-start(bf16[144,896]{1,0:T(8,128)(2,1)} %copy-done.24) | copy-start | bytes 774148
  66.4 15.5 %collective-permute-start.14 = (bf16[144,896]{1,0:T(8,128)(2,1)S(1)}, bf16[144,896]{1,0:T(8,128)(2,1)S(1)}, u32[]{:S(2)}, u32[]{:S(2)}) collective-permute-start(bf16[144,896]{1,0:T(8,128)(2,1)S(1)} %copy-done.18), channel_id=1, source_target_pairs={{0,8},{1,9},{2,10},{3,11},{4,12},{5,13},{6,14},{7,15},{8,0},{9,1},... | collective-permute-start | bytes 774152 | tf_op jit(solution)/shard_map/ppermute | solution.py:42
  67.0 14.9 %collective-permute-start.15 = (bf16[144,896]{1,0:T(8,128)(2,1)S(1)}, bf16[144,896]{1,0:T(8,128)(2,1)S(1)}, u32[]{:S(2)}, u32[]{:S(2)}) collective-permute-start(bf16[144,896]{1,0:T(8,128)(2,1)S(1)} %copy-done.16), channel_id=1, source_target_pairs={{0,12},{1,13},{2,14},{3,15},{4,0},{5,1},{6,2},{7,3},{8,4},{9,5},{1... | collective-permute-start | bytes 774152 | tf_op jit(solution)/shard_map/ppermute | solution.py:42
  72.4 11.2 %copy-start.10 = (bf16[1,128,3584]{2,1,0:T(8,128)(2,1)S(1)}, bf16[1,128,3584]{2,1,0:T(8,128)(2,1)}, u32[]{:S(2)}) copy-start(bf16[1,128,3584]{2,1,0:T(8,128)(2,1)} %param.21) | copy-start | bytes 2752516
  83.0 27.5 %collective-permute-start.18 = (bf16[144,3584]{1,0:T(8,128)(2,1)S(1)}, bf16[144,3584]{1,0:T(8,128)(2,1)S(1)}, u32[]{:S(2)}, u32[]{:S(2)}) collective-permute-start(bf16[144,3584]{1,0:T(8,128)(2,1)S(1)} %shard_map.152.first_ref), channel_id=1, source_target_pairs={{0,1},{1,0},{2,3},{3,2},{4,5},{5,4},{6,7},{7,6},{8,9},{9,8},{10,11... | collective-permute-start | bytes 3096584 | tf_op jit(solution)/shard_map/ppermute | solution.py:37
  83.1 30.2 %collective-permute-start.13 = (bf16[144,3584]{1,0:T(8,128)(2,1)S(1)}, bf16[144,3584]{1,0:T(8,128)(2,1)S(1)}, u32[]{:S(2)}, u32[]{:S(2)}) collective-permute-start(bf16[144,3584]{1,0:T(8,128)(2,1)S(1)} %shard_map.151.first_ref), channel_id=1, source_target_pairs={{0,2},{1,3},{2,0},{3,1},{4,6},{5,7},{6,4},{7,5},{8,10},{9,11},{10,... | collective-permute-start | bytes 3096584 | tf_op jit(solution)/shard_map/ppermute | solution.py:37
  83.7 29.6 %collective-permute-start.19 = (bf16[128,3584]{1,0:T(8,128)(2,1)S(1)}, bf16[128,3584]{1,0:T(8,128)(2,1)S(1)}, u32[]{:S(2)}, u32[]{:S(2)}) collective-permute-start(bf16[128,3584]{1,0:T(8,128)(2,1)S(1)} %bitcast.42), channel_id=1, source_target_pairs={{0,16},{1,17},{2,18},{3,19},{4,20},{5,21},{6,22},{7,23},{8,24},{9,... | collective-permute-start | bytes 2752520 | tf_op jit(solution)/shard_map/ppermute | solution.py:33
  84.2 14.2 %collective-permute-start.10 = (bf16[144,896]{1,0:T(8,128)(2,1)S(1)}, bf16[144,896]{1,0:T(8,128)(2,1)S(1)}, u32[]{:S(2)}, u32[]{:S(2)}) collective-permute-start(bf16[144,896]{1,0:T(8,128)(2,1)S(1)} %get-tuple-element.113), channel_id=1, source_target_pairs={{0,4},{1,5},{2,6},{3,7},{4,8},{5,9},{6,10},{7,11},{8,12},{9,13},{1... | collective-permute-start | bytes 774152 | tf_op jit(solution)/shard_map/ppermute | solution.py:42
  89.3 19.5 %collective-permute-start.11 = (bf16[144,896]{1,0:T(8,128)(2,1)S(1)}, bf16[144,896]{1,0:T(8,128)(2,1)S(1)}, u32[]{:S(2)}, u32[]{:S(2)}) collective-permute-start(bf16[144,896]{1,0:T(8,128)(2,1)S(1)} %get-tuple-element.114), channel_id=1, source_target_pairs={{0,8},{1,9},{2,10},{3,11},{4,12},{5,13},{6,14},{7,15},{8,0},{9,1},... | collective-permute-start | bytes 774152 | tf_op jit(solution)/shard_map/ppermute | solution.py:42
  98.4 12.1 %collective-permute-start.12 = (bf16[144,896]{1,0:T(8,128)(2,1)S(1)}, bf16[144,896]{1,0:T(8,128)(2,1)S(1)}, u32[]{:S(2)}, u32[]{:S(2)}) collective-permute-start(bf16[144,896]{1,0:T(8,128)(2,1)S(1)} %get-tuple-element.115), channel_id=1, source_target_pairs={{0,12},{1,13},{2,14},{3,15},{4,0},{5,1},{6,2},{7,3},{8,4},{9,5},{1... | collective-permute-start | bytes 774152 | tf_op jit(solution)/shard_map/ppermute | solution.py:42
  114.2 1.2 copy-start.29
  114.2 3.8 %copy-start = (bf16[1,1,3584,256]{3,2,1,0:T(8,128)(2,1)S(1)}, bf16[1,1,3584,256]{3,2,1,0:T(8,128)(2,1)}, u32[]{:S(2)}) copy-start(bf16[1,1,3584,256]{3,2,1,0:T(8,128)(2,1)} %param.25) | copy-start | bytes 5505028
  114.2 3.8 %copy-start.1 = (bf16[1,1,3584,256]{3,2,1,0:T(8,128)(2,1)S(1)}, bf16[1,1,3584,256]{3,2,1,0:T(8,128)(2,1)}, u32[]{:S(2)}) copy-start(bf16[1,1,3584,256]{3,2,1,0:T(8,128)(2,1)} %param.26) | copy-start | bytes 5505028
  115.3 2.7 %collective-permute-start.24 = (bf16[144,3584]{1,0:T(8,128)(2,1)S(1)}, bf16[144,3584]{1,0:T(8,128)(2,1)S(1)}, u32[]{:S(2)}, u32[]{:S(2)}) collective-permute-start(bf16[144,3584]{1,0:T(8,128)(2,1)S(1)} %shard_map.151.first_ref), channel_id=1, source_target_pairs={{0,1},{1,0},{2,3},{3,2},{4,5},{5,4},{6,7},{7,6},{8,9},{9,8},{10,11... | collective-permute-start | bytes 3096584 | tf_op jit(solution)/shard_map/ppermute | solution.py:37
  115.4 28.1 %collective-permute-start.22 = (bf16[144,3584]{1,0:T(8,128)(2,1)S(1)}, bf16[144,3584]{1,0:T(8,128)(2,1)S(1)}, u32[]{:S(2)}, u32[]{:S(2)}) collective-permute-start(bf16[144,3584]{1,0:T(8,128)(2,1)S(1)} %shard_map.154.first_ref), channel_id=1, source_target_pairs={{0,1},{1,0},{2,3},{3,2},{4,5},{5,4},{6,7},{7,6},{8,9},{9,8},{10,11... | collective-permute-start | bytes 3096584 | tf_op jit(solution)/shard_map/ppermute | solution.py:37
  116.0 33.7 %collective-permute-start.23 = (bf16[144,3584]{1,0:T(8,128)(2,1)S(1)}, bf16[144,3584]{1,0:T(8,128)(2,1)S(1)}, u32[]{:S(2)}, u32[]{:S(2)}) collective-permute-start(bf16[144,3584]{1,0:T(8,128)(2,1)S(1)} %shard_map.154.first_ref), channel_id=1, source_target_pairs={{0,2},{1,3},{2,0},{3,1},{4,6},{5,7},{6,4},{7,5},{8,10},{9,11},{10,... | collective-permute-start | bytes 3096584 | tf_op jit(solution)/shard_map/ppermute | solution.py:37
  118.0 2.7 %copy-start.31 = (s32[1,128,1]{1,2,0:T(1,128)S(1)}, s32[1,128,1]{1,2,0:T(1,128)}, u32[]{:S(2)}) copy-start(s32[1,128,1]{1,2,0:T(1,128)} %param.18) | copy-start | bytes 1540
  118.0 2.7 %copy-start.30 = (f32[1,128,1]{1,2,0:T(1,128)S(1)}, f32[1,128,1]{1,2,0:T(1,128)}, u32[]{:S(2)}) copy-start(f32[1,128,1]{1,2,0:T(1,128)} %param.19) | copy-start | bytes 1540
  120.5 29.2 %collective-permute-start.25 = (bf16[144,3584]{1,0:T(8,128)(2,1)S(1)}, bf16[144,3584]{1,0:T(8,128)(2,1)S(1)}, u32[]{:S(2)}, u32[]{:S(2)}) collective-permute-start(bf16[144,3584]{1,0:T(8,128)(2,1)S(1)} %get-tuple-element.143), channel_id=1, source_target_pairs={{0,1},{1,0},{2,3},{3,2},{4,5},{5,4},{6,7},{7,6},{8,9},{9,8},{10,11... | collective-permute-start | bytes 3096584 | tf_op jit(solution)/shard_map/ppermute | solution.py:37
  120.7 28.0 %collective-permute-start.21 = (bf16[128,3584]{1,0:T(8,128)(2,1)S(1)}, bf16[128,3584]{1,0:T(8,128)(2,1)S(1)}, u32[]{:S(2)}, u32[]{:S(2)}) collective-permute-start(bf16[128,3584]{1,0:T(8,128)(2,1)S(1)} %get-tuple-element.140), channel_id=1, source_target_pairs={{0,16},{1,17},{2,18},{3,19},{4,20},{5,21},{6,22},{7,23},{8,24},{9,... | collective-permute-start | bytes 2752520 | tf_op jit(solution)/shard_map/ppermute | solution.py:33
  122.3 21.2 %collective-permute-start.20 = (f32[1,256]{1,0:T(1,128)S(1)}, f32[1,256]{1,0:T(1,128)S(1)}, u32[]{:S(2)}, u32[]{:S(2)}) collective-permute-start(f32[1,256]{1,0:T(1,128)S(1)} %maximum_bitcast_fusion), channel_id=1, source_target_pairs={{0,16},{1,17},{2,18},{3,19},{4,20},{5,21},{6,22},{7,23},{8,24},{9,... | collective-permute-start | bytes 3080 | tf_op jit(solution)/shard_map/ppermute | solution.py:33
  143.5 8.9 %collective-permute-start.34 = (bf16[144,3584]{1,0:T(8,128)(2,1)S(1)}, bf16[144,3584]{1,0:T(8,128)(2,1)S(1)}, u32[]{:S(2)}, u32[]{:S(2)}) collective-permute-start(bf16[144,3584]{1,0:T(8,128)(2,1)S(1)} %collective-permute-done.13.first_ref), channel_id=1, source_target_pairs={{0,1},{1,0},{2,3},{3,2},{4,5},{5,4},{6,7},{7,6},{8,9},{9,8},{10,11... | collective-permute-start | bytes 3096584 | tf_op jit(solution)/shard_map/ppermute | solution.py:37
  143.5 3.7 %collective-permute-start.26 = (f32[1,3712]{1,0:T(1,128)S(1)}, f32[1,3712]{1,0:T(1,128)S(1)}, u32[]{:S(2)}, u32[]{:S(2)}) collective-permute-start(f32[1,3712]{1,0:T(1,128)S(1)} %pad_maximum_fusion), channel_id=1, source_target_pairs={{0,16},{1,17},{2,18},{3,19},{4,20},{5,21},{6,22},{7,23},{8,24},{9,... | collective-permute-start | bytes 44552 | tf_op jit(solution)/shard_map/ppermute | solution.py:33
  147.2 5.1 %collective-permute-start.35 = (bf16[288,256]{1,0:T(8,128)(2,1)S(1)}, bf16[288,256]{1,0:T(8,128)(2,1)S(1)}, u32[]{:S(2)}, u32[]{:S(2)}) collective-permute-start(bf16[288,256]{1,0:T(8,128)(2,1)S(1)} %get-tuple-element.133), channel_id=1, source_target_pairs={{0,2},{1,3},{2,0},{3,1},{4,6},{5,7},{6,4},{7,5},{8,10},{9,11},{10,... | collective-permute-start | bytes 442376 | tf_op jit(solution)/shard_map/ppermute | solution.py:37
  150.7 4.3 %collective-permute-start.27 = (bf16[144,3584]{1,0:T(8,128)(2,1)S(1)}, bf16[144,3584]{1,0:T(8,128)(2,1)S(1)}, u32[]{:S(2)}, u32[]{:S(2)}) collective-permute-start(bf16[144,3584]{1,0:T(8,128)(2,1)S(1)} %collective-permute-done.23.first_ref), channel_id=1, source_target_pairs={{0,1},{1,0},{2,3},{3,2},{4,5},{5,4},{6,7},{7,6},{8,9},{9,8},{10,11... | collective-permute-start | bytes 3096584 | tf_op jit(solution)/shard_map/ppermute | solution.py:37
  154.8 10.5 %collective-permute-start.36 = (bf16[144,3584]{1,0:T(8,128)(2,1)S(1)}, bf16[144,3584]{1,0:T(8,128)(2,1)S(1)}, u32[]{:S(2)}, u32[]{:S(2)}) collective-permute-start(bf16[144,3584]{1,0:T(8,128)(2,1)S(1)} %get-tuple-element.155), channel_id=1, source_target_pairs={{0,1},{1,0},{2,3},{3,2},{4,5},{5,4},{6,7},{7,6},{8,9},{9,8},{10,11... | collective-permute-start | bytes 3096584 | tf_op jit(solution)/shard_map/ppermute | solution.py:37
  156.2 6.3 %collective-permute-start.28 = (bf16[288,256]{1,0:T(8,128)(2,1)S(1)}, bf16[288,256]{1,0:T(8,128)(2,1)S(1)}, u32[]{:S(2)}, u32[]{:S(2)}) collective-permute-start(bf16[288,256]{1,0:T(8,128)(2,1)S(1)} %shard_map.157), channel_id=1, source_target_pairs={{0,2},{1,3},{2,0},{3,1},{4,6},{5,7},{6,4},{7,5},{8,10},{9,11},{10,... | collective-permute-start | bytes 442376 | tf_op jit(solution)/shard_map/ppermute | solution.py:37
  165.3 2.8 %collective-permute-start.29 = (bf16[144,3584]{1,0:T(8,128)(2,1)S(1)}, bf16[144,3584]{1,0:T(8,128)(2,1)S(1)}, u32[]{:S(2)}, u32[]{:S(2)}) collective-permute-start(bf16[144,3584]{1,0:T(8,128)(2,1)S(1)} %get-tuple-element.147), channel_id=1, source_target_pairs={{0,1},{1,0},{2,3},{3,2},{4,5},{5,4},{6,7},{7,6},{8,9},{9,8},{10,11... | collective-permute-start | bytes 3096584 | tf_op jit(solution)/shard_map/ppermute | solution.py:37
  166.6 25.5 %copy-start.4 = (bf16[144,3584]{1,0:T(8,128)(2,1)S(1)}, bf16[144,3584]{1,0:T(8,128)(2,1)}, u32[]{:S(2)}) copy-start(bf16[144,3584]{1,0:T(8,128)(2,1)} %copy-done.3) | copy-start | bytes 3096580
  166.6 25.5 %collective-permute-start.37 = (bf16[144,3584]{1,0:T(8,128)(2,1)}, bf16[144,3584]{1,0:T(8,128)(2,1)}, u32[]{:S(2)}, u32[]{:S(2)}) collective-permute-start(bf16[144,3584]{1,0:T(8,128)(2,1)} %add_convert_fusion), channel_id=1, source_target_pairs={{0,2},{1,3},{2,0},{3,1},{4,6},{5,7},{6,4},{7,5},{8,10},{9,11},{10,... | collective-permute-start | bytes 3096584 | tf_op jit(solution)/shard_map/ppermute | solution.py:37
  170.0 27.0 %collective-permute-start.30 = (bf16[144,896]{1,0:T(8,128)(2,1)}, bf16[144,896]{1,0:T(8,128)(2,1)S(1)}, u32[]{:S(2)}, u32[]{:S(2)}) collective-permute-start(bf16[144,896]{1,0:T(8,128)(2,1)} %get-tuple-element.148), channel_id=1, source_target_pairs={{0,16},{1,17},{2,18},{3,19},{4,20},{5,21},{6,22},{7,23},{8,24},{9,... | collective-permute-start | bytes 774152 | tf_op jit(solution)/shard_map/ppermute | solution.py:33
  171.5 29.4 %collective-permute-start.31 = (bf16[144,896]{1,0:T(8,128)(2,1)}, bf16[144,896]{1,0:T(8,128)(2,1)}, u32[]{:S(2)}, u32[]{:S(2)}) collective-permute-start(bf16[144,896]{1,0:T(8,128)(2,1)} %get-tuple-element.149), channel_id=1, source_target_pairs={{0,28},{1,29},{2,30},{3,31},{4,16},{5,17},{6,18},{7,19},{8,20},{9,... | collective-permute-start | bytes 774152 | tf_op jit(solution)/shard_map/ppermute | solution.py:33
  175.4 28.1 %collective-permute-start.32 = (bf16[144,896]{1,0:T(8,128)(2,1)}, bf16[144,896]{1,0:T(8,128)(2,1)}, u32[]{:S(2)}, u32[]{:S(2)}) collective-permute-start(bf16[144,896]{1,0:T(8,128)(2,1)} %get-tuple-element.150), channel_id=1, source_target_pairs={{0,24},{1,25},{2,26},{3,27},{4,28},{5,29},{6,30},{7,31},{8,16},{9,... | collective-permute-start | bytes 774152 | tf_op jit(solution)/shard_map/ppermute | solution.py:33
  178.1 25.6 %collective-permute-start.33 = (bf16[144,896]{1,0:T(8,128)(2,1)S(1)}, bf16[144,896]{1,0:T(8,128)(2,1)}, u32[]{:S(2)}, u32[]{:S(2)}) collective-permute-start(bf16[144,896]{1,0:T(8,128)(2,1)S(1)} %get-tuple-element.151), channel_id=1, source_target_pairs={{0,20},{1,21},{2,22},{3,23},{4,24},{5,25},{6,26},{7,27},{8,28},{9,... | collective-permute-start | bytes 774152 | tf_op jit(solution)/shard_map/ppermute | solution.py:33
  195.4 16.9 %collective-permute-start.38 = (bf16[144,896]{1,0:T(8,128)(2,1)}, bf16[144,896]{1,0:T(8,128)(2,1)S(1)}, u32[]{:S(2)}, u32[]{:S(2)}) collective-permute-start(bf16[144,896]{1,0:T(8,128)(2,1)} %get-tuple-element.160), channel_id=1, source_target_pairs={{0,16},{1,17},{2,18},{3,19},{4,20},{5,21},{6,22},{7,23},{8,24},{9,... | collective-permute-start | bytes 774152 | tf_op jit(solution)/shard_map/ppermute | solution.py:33
  196.9 15.4 %collective-permute-start.39 = (bf16[144,896]{1,0:T(8,128)(2,1)}, bf16[144,896]{1,0:T(8,128)(2,1)S(1)}, u32[]{:S(2)}, u32[]{:S(2)}) collective-permute-start(bf16[144,896]{1,0:T(8,128)(2,1)} %get-tuple-element.161), channel_id=1, source_target_pairs={{0,28},{1,29},{2,30},{3,31},{4,16},{5,17},{6,18},{7,19},{8,20},{9,... | collective-permute-start | bytes 774152 | tf_op jit(solution)/shard_map/ppermute | solution.py:33
  200.9 25.0 %collective-permute-start.40 = (bf16[144,896]{1,0:T(8,128)(2,1)}, bf16[144,896]{1,0:T(8,128)(2,1)S(1)}, u32[]{:S(2)}, u32[]{:S(2)}) collective-permute-start(bf16[144,896]{1,0:T(8,128)(2,1)} %get-tuple-element.162), channel_id=1, source_target_pairs={{0,24},{1,25},{2,26},{3,27},{4,28},{5,29},{6,30},{7,31},{8,16},{9,... | collective-permute-start | bytes 774152 | tf_op jit(solution)/shard_map/ppermute | solution.py:33
  203.6 22.4 %collective-permute-start.41 = (bf16[144,896]{1,0:T(8,128)(2,1)}, bf16[144,896]{1,0:T(8,128)(2,1)S(1)}, u32[]{:S(2)}, u32[]{:S(2)}) collective-permute-start(bf16[144,896]{1,0:T(8,128)(2,1)} %get-tuple-element.163), channel_id=1, source_target_pairs={{0,20},{1,21},{2,22},{3,23},{4,24},{5,25},{6,26},{7,27},{8,28},{9,... | collective-permute-start | bytes 774152 | tf_op jit(solution)/shard_map/ppermute | solution.py:33
  203.7 22.2 %copy-start.12 = (bf16[128,3584]{1,0:T(8,128)(2,1)S(1)}, bf16[128,3584]{1,0:T(8,128)(2,1)}, u32[]{:S(2)}) copy-start(bf16[128,3584]{1,0:T(8,128)(2,1)} %copy-done.11) | copy-start | bytes 2752516
  203.7 1.3 copy-start.14
  (10 other events, 8.8 us)

commit v9 on v5

--- a/solution.py
+++ b/solution.py
@@ -253,13 +253,14 @@
     kv0,
     kv1,
     kv2,
+    kv3,
     middle_ref,
     *refs,
 ):
     outs, (kv_all, kv_now, stack, attended) = refs[:experts], refs[experts:]
     tokens, width = query_ref.shape
     lead = 0
-    for ref in (kv0, kv1, kv2):
+    for ref in (kv0, kv1, kv2, kv3):
         kv_all[lead : lead + ref.shape[0], : ref.shape[1]] = ref[...]
         lead += ref.shape[0]
     attended[...] = jnp.zeros_like(attended)
@@ -388,8 +389,6 @@
     column = jnp.concatenate(column, axis=0)
     other_chip = swapped(column, 2)
     packed = after(packed, [column])
-    down_other = swapped(w_down, 2)
-    downs = (w_down, down_other)
 
     front_small = jnp.concatenate([front_from.astype(f32), front_gate[0]], axis=0).reshape(1, -1)
     back_small = jnp.concatenate([back_from.astype(f32).reshape(1, -1), norm_gain], axis=1)
@@ -416,19 +415,14 @@
         return [passed_along(chunks[k], by, k) for k in range(experts)]
 
     row_chunks, grad_chunks = packed[:experts], packed[experts:]
-    first = 1 + 2 * (experts - 1) // 3
-    for k in range(1, first):
-        row_chunks[k] = turned(row_chunks[k], k)
-    arrived = row_chunks[1:first]
-    there_back_middle = passed_along(after([back_middle[0]], [packed[0]])[0], -1)
-    chip = jnp.concatenate([column, other_chip], axis=0)
-    kv = [column, other_chip, swapped(after([chip], arrived + [there_back_middle])[0], 1)]
-    for k in range(first, experts):
+    row_chunks[1] = turned(row_chunks[1], 1)
+    arrived = [row_chunks[1]]
+    down_other = swapped(after([w_down], [other_chip] + arrived)[0], 2)
+    downs = (w_down, down_other)
+    kv = [column, other_chip, swapped(column, 1), swapped(other_chip, 1)]
+    for k in range(2, experts):
         row_chunks[k] = turned(after([row_chunks[k]], arrived)[0], k)
-    beside = range(1, 2)
-    for k in beside:
-        grad_chunks[k] = turned(after([grad_chunks[k]], arrived)[0], k)
-    there_back_grad = passed_along(after([back_grad[0]], [there_back_middle])[0], -1)
+    there_back_middle = passed_along(after([back_middle[0]], [other_chip] + arrived)[0], -1)
 
     per_device = tokens // BLK
     chosen = selected_blocks[0].reshape(-1)
@@ -453,16 +447,14 @@
         vmem=VMEM_BYTES + 2 * length * tokens * 4 * LANES * 2,
     )
     middle, front_chunks = result[0], result[1:]
-    ready = row_chunks + [grad_chunks[k] for k in beside]
-    front_chunks = sent(after(front_chunks, ready))
-    back_rows = joined(after(ready, [middle, there_back_grad])[:experts])
-    back_pieces = pieces_of(after([back_rows], [down_other])[0])
-    there_middle = passed_along(after([middle], [back_rows])[0], 1)
+    front_chunks = sent(after(front_chunks, row_chunks))
+    back_rows = joined(after(row_chunks, [middle, there_back_middle]))
+    back_pieces = pieces_of(back_rows)
     for k in range(1, experts):
-        if k not in beside:
-            grad_chunks[k] = turned(after([grad_chunks[k]], front_chunks)[0], k)
-    front_near = joined(after(front_chunks, [there_middle, back_pieces[2]]))
-    front_other = swapped(front_near, 2)
+        grad_chunks[k] = turned(after([grad_chunks[k]], front_chunks)[0], k)
+    front_near = joined(after(front_chunks, [back_pieces[2], down_other]))
+    there_back_grad = passed_along(after([back_grad[0]], [front_near])[0], -1)
+    front_other = after([swapped(front_near, 2)], [there_back_grad])[0]
 
     front_small, back_small = after([front_small, back_small], [front_near])
     there_small = passed_along(front_small, 1)
@@ -471,7 +463,7 @@
     there_front_gate = there_small[0, tokens:].reshape(tokens, 1)
     there_back_from = there_back_small[0, :tokens].astype(jnp.int32).reshape(tokens, 1)
     there_gain = there_back_small[:, tokens:]
-    grad_near = joined(after(grad_chunks, [there_small, there_back_small]))
+    grad_near = joined(after(grad_chunks, [front_other]))
     grad_near = [grad_near, swapped(grad_near, 1)]
 
     work = 2 * 2 * slots * width * hidden_width
@@ -485,31 +477,34 @@
     def backward(rows, grads):
         return call(backward_body, [piece, piece], (*rows, grads, w_gate, w_up), flops=4 * work)
 
-    down_back, other_back = call(
-        down_back_body,
-        [shape_of(pair, hidden_width, f32), shape_of(pair, hidden_width)],
-        (*grad_near, *downs),
-        flops=2 * work,
-    )
-    (front_other,) = after([front_other], [other_back])
+    there_middle = passed_along(after([middle], [front_other])[0], 1)
     front_pieces = [front_near, swapped(front_near, 1), front_other, swapped(front_other, 1)]
     hidden_near = hidden(front_pieces[:2])
     hidden_far = hidden(front_pieces[2:])
     hidden_other = swapped(hidden_far, 2)
+    down_back, other_back = call(
+        down_back_body,
+        [shape_of(pair, hidden_width, f32), shape_of(pair, hidden_width)],
+        (*after(grad_near, [there_small, there_back_small, hidden_far]), *downs),
+        flops=2 * work,
+    )
     far_back = swapped(other_back, 2)
 
+    front_own, front_core = call(
+        output_body, [piece, piece], (hidden_near, hidden_other, *downs), flops=2 * work
+    )
+    (far_back,) = after([far_back], [front_own])
     back_near = backward(back_pieces[:2], down_back)
     back_far = backward(back_pieces[2:], far_back)
     chip = back_far[0].astype(f32) + swapped(back_far[1], 1).astype(f32)
-    back_shares = (back_near[0], swapped(back_near[1], 1), swapped(chip.astype(bf16), 2))
-
-    front_own, front_core = call(
-        output_body, [piece, piece], (hidden_near, hidden_other, *downs), flops=2 * work
-    )
-    front_chunks = split((front_own, swapped(front_core, 1)))
+    (chip,) = after([chip.astype(bf16)], [hidden_other])
+    back_shares = (back_near[0], swapped(back_near[1], 1), swapped(chip, 2))
+
+    front_shares = (front_own, swapped(front_core, 1))
+    front_chunks = split(front_shares)
     front_return = sent_back(front_chunks, 1)
 
-    back_chunks = split(after(back_shares, front_chunks))
+    back_chunks = split(after(back_shares, front_chunks + [there_middle]))
     back_return = sent_back(back_chunks, -1)
 
     front_return = after(front_return, back_chunks)

time: 260 us -> 225 us (0.87)
  waiting for transfers between devices: 133 us -> 116 us
  starting transfers between devices: 62.5 us -> 51 us
  local copies, waits for them, and re-layouts: 20.9 us -> 13.1 us
    ppermute x16 -> x17, waiting for transfers between devices: 87.4 us -> 24.6 us  [swapped(): lax.ppermute(array, 'expert', [(i, i ^ bit) for i in range(lax.axis_size(...]
    ppermute x13, waiting for transfers between devices: 22.9 us -> 58.6 us  [passed_along(): return lax.ppermute(array, ('section', 'expert'), pairs)]
    ppermute x9, starting transfers between devices: 18.1 us -> 8.04 us  [turned(): lax.ppermute(array, 'expert', [(i, (i + by * GROUP) % length) for i in ra...]
    ppermute x9, waiting for transfers between devices: 22.5 us -> 32.5 us  [turned(): lax.ppermute(array, 'expert', [(i, (i + by * GROUP) % length) for i in ra...]
    ppermute x13, starting transfers between devices: 26.6 us -> 21.7 us  [passed_along(): return lax.ppermute(array, ('section', 'expert'), pairs)]
    unnamed x69 -> x66, local copies, waits for them, and re-layouts: 15.2 us -> 10.3 us
    ppermute x16 -> x17, starting transfers between devices: 7.02 us -> 9.92 us  [swapped(): lax.ppermute(array, 'expert', [(i, i ^ bit) for i in range(lax.axis_size(...]
  transfers between devices with their start and end apart: 41 -> 42, of which waited for: 13 -> 15; matrix products, arithmetic and copies ran while one was open for 3% -> 2% of each run, Pallas kernels for 13% -> 16%
where the time goes in v9:
time: 225 us
  waiting for transfers between devices  116 us (52%)
  starting transfers between devices  51 us (23%)
  Pallas kernels  40.6 us (18%)
  local copies, waits for them, and re-layouts  13.1 us (6%)
  other arithmetic  3.21 us (1%)
    ppermute x13, waiting for transfers between devices, passed_along(): return lax.ppermute(array, ('section', 'expert'), pairs)  58.6 us
    pallas_call x15, Pallas kernels, call(): pl.pallas_call(body, out_shape=shapes, in_specs=specs, out_specs=[pl.Bloc...  40.6 us
    ppermute x9, waiting for transfers between devices, turned(): lax.ppermute(array, 'expert', [(i, (i + by * GROUP) % length) for i in ra...  32.5 us
    ppermute x17, waiting for transfers between devices, swapped(): lax.ppermute(array, 'expert', [(i, i ^ bit) for i in range(lax.axis_size(...  24.6 us
    ppermute x13, starting transfers between devices, passed_along(): return lax.ppermute(array, ('section', 'expert'), pairs)  21.7 us
    ppermute x3, starting transfers between devices, shards(): column.append(lax.ppermute(keys_values[0], 'expert', pairs))  11.4 us
    unnamed x66, local copies, waits for them, and re-layouts  10.3 us
    ppermute x17, starting transfers between devices, swapped(): lax.ppermute(array, 'expert', [(i, i ^ bit) for i in range(lax.axis_size(...  9.92 us
  transfers between devices with their start and end apart: 42, of which 15 were waited for; matrix products, arithmetic and copies ran while one was open for 2% of the time, Pallas kernels for 16%

profile of v9, /device:TPU:0, one launch (start us, length us, event | category | flops | bytes accessed | tf_op | source)
XLA Modules:
  0.0 224.6 jit_solution(1322818378288023464)
XLA Ops:
  0.6 1.0 copy.16
  1.6 4.9 %collective-permute-start = (bf16[128,448]{1,0:T(8,128)(2,1)S(1)}, bf16[128,448]{1,0:T(8,128)(2,1)S(1)}, u32[]{:S(2)}, u32[]{:S(2)}) collective-permute-start(bf16[128,448]{1,0:T(8,128)(2,1)S(1)} %bitcast.43), channel_id=1, source_target_pairs={{0,4},{1,5},{2,6},{3,7},{4,8},{5,9},{6,10},{7,11},{8,12},{9,13},{1... | collective-permute-start | bytes 344072 | tf_op jit(solution)/shard_map/ppermute | solution.py:376
  6.6 4.5 %collective-permute-start.1 = (bf16[128,448]{1,0:T(8,128)(2,1)S(1)}, bf16[128,448]{1,0:T(8,128)(2,1)S(1)}, u32[]{:S(2)}, u32[]{:S(2)}) collective-permute-start(bf16[128,448]{1,0:T(8,128)(2,1)S(1)} %bitcast.44), channel_id=1, source_target_pairs={{0,8},{1,9},{2,10},{3,11},{4,12},{5,13},{6,14},{7,15},{16,24},{17,... | collective-permute-start | bytes 344072 | tf_op jit(solution)/shard_map/ppermute | solution.py:376
  11.1 2.0 collective-permute-start.2
  13.0 0.8 copy.17.gate_ref
  13.8 1.2 fusion.11
  15.1 0.7 copy-done.3
  15.8 1.2 copy-done.7
  16.9 3.3 %shard_map.149 = (bf16[144,896]{1,0:T(8,128)(2,1)S(1)}, bf16[144,896]{1,0:T(8,128)(2,1)S(1)}, bf16[144,896]{1,0:T(8,128)(2,1)}, bf16[144,896]{1,0:T(8,128)(2,1)}...) custom-call(s32[1,128]{1,0:T(1,128)S(1)} %get-tuple-element.171.rout, ...), custom_call_target="tpu_custom_call" | custom-call | flops 2113929216 | bytes 3914752 | tf_op jit(solution)/shard_map/pallas_call | solution.py:55
  20.3 0.7 copy-done.17
  21.0 0.7 copy-done.27
  21.8 0.9 constant_dynamic-update-slice_fusion.1
  22.7 0.9 constant_dynamic-update-slice_fusion.kv0
  23.6 1.6 collective-permute-start.3
  25.2 8.9 %collective-permute-done.6.refs_1_ = bf16[144,896]{1,0:T(8,128)(2,1)S(1)} collective-permute-done((bf16[144,896]{1,0:T(8,128)(2,1)S(1)}, bf16[144,896]{1,0:T(8,128)(2,1)S(1)}, u32[]{:S(2)}, u32[]{:S(2)}) %collective-permute-start.6) | collective-permute-done | bytes 258080 | tf_op jit(solution)/shard_map/ppermute | solution.py:42
  34.1 0.7 copy-done.19
  34.8 2.1 collective-permute-done.3.kv1
  36.9 1.5 collective-permute-start.12
  38.4 1.6 collective-permute-start.14
  40.2 0.8 reshape_squeeze.6.chosen_ref
  41.6 1.3 collective-permute-start.8
  43.0 1.2 copy-done.6
  44.1 8.4 %shard_map.150 = (bf16[128,3584]{1,0:T(8,128)(2,1)S(1)}, bf16[144,896]{1,0:T(8,128)(2,1)S(1)}, bf16[144,896]{1,0:T(8,128)(2,1)S(1)}, bf16[144,896]{1,0:T(8,128)(2,1)S(1)}, bf16[144,896]{1,0:T(8,128)(2,1)S(1)}) custom-call(s32[16]{0:T(128)S(1)} %reshape_squeeze.6.chosen_ref, s32[16]{0:T(128)S(1)} %fusion.10.index_ref, s32[1]{0:T(128)} %bitcast.4.base_ref, ...), custom_call_target="tpu_custom_call" | custom-call | flops 1593835520 | bytes 5634692 | tf_op jit(solution)/shard_map/pallas_call | solution.py:55
  52.6 7.3 %collective-permute-done.7.refs_2_ = bf16[144,896]{1,0:T(8,128)(2,1)} collective-permute-done((bf16[144,896]{1,0:T(8,128)(2,1)}, bf16[144,896]{1,0:T(8,128)(2,1)}, u32[]{:S(2)}, u32[]{:S(2)}) %collective-permute-start.7) | collective-permute-done | bytes 258080 | tf_op jit(solution)/shard_map/ppermute | solution.py:42
  59.9 2.2 shard_map.151.first_ref
  62.8 4.0 %collective-permute-start.11 = (bf16[144,896]{1,0:T(8,128)(2,1)S(1)}, bf16[144,896]{1,0:T(8,128)(2,1)S(1)}, u32[]{:S(2)}, u32[]{:S(2)}) collective-permute-start(bf16[144,896]{1,0:T(8,128)(2,1)S(1)} %get-tuple-element.111), channel_id=1, source_target_pairs={{0,12},{1,13},{2,14},{3,15},{4,0},{5,1},{6,2},{7,3},{8,4},{9,5},{1... | collective-permute-start | bytes 774152 | tf_op jit(solution)/shard_map/ppermute | solution.py:42
  67.2 16.3 %collective-permute-done.10.refs_2_ = bf16[144,896]{1,0:T(8,128)(2,1)S(1)} collective-permute-done((bf16[144,896]{1,0:T(8,128)(2,1)S(1)}, bf16[144,896]{1,0:T(8,128)(2,1)S(1)}, u32[]{:S(2)}, u32[]{:S(2)}) %collective-permute-start.10) | collective-permute-done | bytes 258080 | tf_op jit(solution)/shard_map/ppermute | solution.py:42
  83.5 19.5 %collective-permute-done.13.first_ref = bf16[144,3584]{1,0:T(8,128)(2,1)S(1)} collective-permute-done((bf16[144,3584]{1,0:T(8,128)(2,1)S(1)}, bf16[144,3584]{1,0:T(8,128)(2,1)S(1)}, u32[]{:S(2)}, u32[]{:S(2)}) %collective-permute-start.13) | collective-permute-done | bytes 1032224 | tf_op jit(solution)/shard_map/ppermute | solution.py:37
  103.0 1.1 shard_map.152.first_ref
  104.2 1.6 collective-permute-start.16
  106.2 1.3 collective-permute-start.30
  107.5 1.0 collective-permute-start.28
  108.5 18.9 %collective-permute-done.17.grad_ref = bf16[128,3584]{1,0:T(8,128)(2,1)S(1)} collective-permute-done((bf16[128,3584]{1,0:T(8,128)(2,1)S(1)}, bf16[128,3584]{1,0:T(8,128)(2,1)S(1)}, u32[]{:S(2)}, u32[]{:S(2)}) %collective-permute-start.17) | collective-permute-done | bytes 917536 | tf_op jit(solution)/shard_map/ppermute | solution.py:33
  127.4 1.0 copy-done.9
  128.7 1.1 shard_map.157.first_ref
  130.9 1.0 collective-permute-start.32
  132.0 1.0 collective-permute-start.15
  133.0 1.2 shard_map.154
  134.3 1.3 collective-permute-done.15
  135.6 1.0 collective-permute-start.21
  136.6 2.8 %shard_map.158 = (f32[288,256]{1,0:T(8,128)S(1)}, bf16[288,256]{1,0:T(8,128)(2,1)S(1)}) custom-call(bf16[144,3584]{1,0:T(8,128)(2,1)S(1)} %shard_map.157.first_ref, bf16[144,3584]{1,0:T(8,128)(2,1)S(1)} %collective-permute-done.31.second_ref, bf16[256,3584]{1,0:T(8,128)(2,1)S(1)} %bitcast.29, bf16[256,3584]{1,0:T(8,128)(2,1)} %collective-permute-done.14.far_ref), custom_call_target="tpu_custom_call" | custom-call | flops 1056964608 | bytes 6176768 | tf_op jit(solution)/shard_map/pallas_call | solution.py:55
  139.3 1.1 collective-permute-start.35
  140.4 1.2 shard_map.153.own_ref
  141.8 2.7 %shard_map.155 = (bf16[144,3584]{1,0:T(8,128)(2,1)S(1)}, bf16[144,3584]{1,0:T(8,128)(2,1)S(1)}) custom-call(bf16[288,256]{1,0:T(8,128)(2,1)S(1)} %shard_map.153.own_ref, bf16[288,256]{1,0:T(8,128)(2,1)S(1)} %collective-permute-done.21.other_ref, bf16[256,3584]{1,0:T(8,128)(2,1)S(1)} %bitcast.30, bf16[256,3584]{1,0:T(8,128)(2,1)} %collective-permute-done.14.far_ref), custom_call_target="tpu_custom_call" | custom-call | flops 1056964608 | bytes 6029312 | tf_op jit(solution)/shard_map/pallas_call | solution.py:55
  144.6 0.8 collective-permute-done.35.back_ref
  145.4 2.5 %shard_map.160 = (bf16[144,3584]{1,0:T(8,128)(2,1)S(1)}, bf16[144,3584]{1,0:T(8,128)(2,1)S(1)}) custom-call(bf16[144,3584]{1,0:T(8,128)(2,1)S(1)} %collective-permute-done.13.first_ref, bf16[144,3584]{1,0:T(8,128)(2,1)S(1)} %collective-permute-done.34.second_ref, bf16[288,256]{1,0:T(8,128)(2,1)S(1)} %collective-permute-done.35.back_ref, ...), custom_call_target="tpu_custom_call" | custom-call | flops 2113929216 | bytes 7946240 | tf_op jit(solution)/shard_map/pallas_call | solution.py:55
  147.9 1.6 collective-permute-start.18
  149.5 2.4 %shard_map.159 = (bf16[144,3584]{1,0:T(8,128)(2,1)S(1)}, bf16[144,3584]{1,0:T(8,128)(2,1)S(1)}) custom-call(bf16[144,3584]{1,0:T(8,128)(2,1)S(1)} %shard_map.151.first_ref, bf16[144,3584]{1,0:T(8,128)(2,1)S(1)} %collective-permute-done.27.second_ref, f32[288,256]{1,0:T(8,128)S(1)} %get-tuple-element.147.back_ref, bf16[3584,256]{1,0:T(8,128)(2,1)S(1)} %bitcast.34, ...), custom_call_target="tpu_custom_call" | custom-call | flops 2113929216 | bytes 8093696 | tf_op jit(solution)/shard_map/pallas_call | solution.py:55
  152.5 1.2 add_convert_fusion
  154.4 1.8 collective-permute-done.22.refs_1_
  156.1 1.9 shard_map.156
  158.6 2.2 collective-permute-start.24
  160.8 15.9 %collective-permute-done.18.middle_ref = bf16[128,3584]{1,0:T(8,128)(2,1)S(1)} collective-permute-done((bf16[128,3584]{1,0:T(8,128)(2,1)S(1)}, bf16[128,3584]{1,0:T(8,128)(2,1)S(1)}, u32[]{:S(2)}, u32[]{:S(2)}) %collective-permute-start.18) | collective-permute-done | bytes 917536 | tf_op jit(solution)/shard_map/ppermute | solution.py:33
  176.7 0.9 copy-done.11
  177.6 2.6 %collective-permute-start.25 = (bf16[144,896]{1,0:T(8,128)(2,1)}, bf16[144,896]{1,0:T(8,128)(2,1)}, u32[]{:S(2)}, u32[]{:S(2)}) collective-permute-start(bf16[144,896]{1,0:T(8,128)(2,1)} %get-tuple-element.131), channel_id=1, source_target_pairs={{0,24},{1,25},{2,26},{3,27},{4,28},{5,29},{6,30},{7,31},{8,16},{9,... | collective-permute-start | bytes 774152 | tf_op jit(solution)/shard_map/ppermute | solution.py:33
  180.6 1.2 copy-done.22
  181.8 2.1 shard_map.161
  184.0 1.5 collective-permute-start.38
  185.5 9.0 %collective-permute-start.39 = (bf16[144,896]{1,0:T(8,128)(2,1)}, bf16[144,896]{1,0:T(8,128)(2,1)S(1)}, u32[]{:S(2)}, u32[]{:S(2)}) collective-permute-start(bf16[144,896]{1,0:T(8,128)(2,1)} %get-tuple-element.159), channel_id=1, source_target_pairs={{0,28},{1,29},{2,30},{3,31},{4,16},{5,17},{6,18},{7,19},{8,20},{9,... | collective-permute-start | bytes 774152 | tf_op jit(solution)/shard_map/ppermute | solution.py:33
  194.4 6.7 %collective-permute-done.25.refs_2_ = bf16[144,896]{1,0:T(8,128)(2,1)} collective-permute-done((bf16[144,896]{1,0:T(8,128)(2,1)}, bf16[144,896]{1,0:T(8,128)(2,1)}, u32[]{:S(2)}, u32[]{:S(2)}) %collective-permute-start.25) | collective-permute-done | bytes 258080 | tf_op jit(solution)/shard_map/ppermute | solution.py:33
  201.3 3.7 %shard_map.162 = bf16[128,3584]{1,0:T(8,128)(2,1)} custom-call(s32[128,1]{1,0:T(8,128)S(1)} %copy.18.route_ref, f32[128,1]{1,0:T(8,128)S(1)} %copy.19.gate_ref, bf16[128,3584]{1,0:T(8,128)(2,1)S(1)} %copy-done.12, bf16[144,896]{1,0:T(8,128)(2,1)} %collective-permute-done.23.refs_0_, bf16[144,896]{1,0:T(8,128)(2,1)} %collective-permute-done.24.refs_1_, ...), custom_call_target="tpu_custom_call" | custom-call | flops 1056964608 | bytes 2868224 | tf_op jit(solution)/shard_map/pallas_call | solution.py:55
  205.0 7.9 %collective-permute-done.38.refs_0_ = bf16[144,896]{1,0:T(8,128)(2,1)S(1)} collective-permute-done((bf16[144,896]{1,0:T(8,128)(2,1)}, bf16[144,896]{1,0:T(8,128)(2,1)S(1)}, u32[]{:S(2)}, u32[]{:S(2)}) %collective-permute-start.38) | collective-permute-done | bytes 258080 | tf_op jit(solution)/shard_map/ppermute | solution.py:33
  212.9 7.8 %collective-permute-done.40.refs_2_ = bf16[144,896]{1,0:T(8,128)(2,1)S(1)} collective-permute-done((bf16[144,896]{1,0:T(8,128)(2,1)}, bf16[144,896]{1,0:T(8,128)(2,1)S(1)}, u32[]{:S(2)}, u32[]{:S(2)}) %collective-permute-start.40) | collective-permute-done | bytes 258080 | tf_op jit(solution)/shard_map/ppermute | solution.py:33
  220.7 3.9 %shard_map.163 = bf16[128,3584]{1,0:T(8,128)(2,1)} custom-call(s32[128,1]{1,0:T(8,128)S(1)} %copy.20.route_ref, f32[1,3584]{1,0:T(1,128)S(1)} %slice.19.gain_ref, bf16[128,3584]{1,0:T(8,128)(2,1)} %collective-permute-done.12.middle_ref, bf16[128,3584]{1,0:T(8,128)(2,1)S(1)} %copy-done.10, bf16[144,896]{1,0:T(8,128)(2,1)S(1)} %collective-permute-done.38.refs_0_, ...), custom_call_target="tpu_custom_call" | custom-call | flops 1056964608 | bytes 3799552 | tf_op jit(solution)/shard_map/pallas_call | solution.py:55
  (117 shorter events, 6.7 us)
Async XLA Ops:
  1.6 19.3 %collective-permute-start = (bf16[128,448]{1,0:T(8,128)(2,1)S(1)}, bf16[128,448]{1,0:T(8,128)(2,1)S(1)}, u32[]{:S(2)}, u32[]{:S(2)}) collective-permute-start(bf16[128,448]{1,0:T(8,128)(2,1)S(1)} %bitcast.43), channel_id=1, source_target_pairs={{0,4},{1,5},{2,6},{3,7},{4,8},{5,9},{6,10},{7,11},{8,12},{9,13},{1... | collective-permute-start | bytes 344072 | tf_op jit(solution)/shard_map/ppermute | solution.py:376
  6.6 14.4 %collective-permute-start.1 = (bf16[128,448]{1,0:T(8,128)(2,1)S(1)}, bf16[128,448]{1,0:T(8,128)(2,1)S(1)}, u32[]{:S(2)}, u32[]{:S(2)}) collective-permute-start(bf16[128,448]{1,0:T(8,128)(2,1)S(1)} %bitcast.44), channel_id=1, source_target_pairs={{0,8},{1,9},{2,10},{3,11},{4,12},{5,13},{6,14},{7,15},{16,24},{17,... | collective-permute-start | bytes 344072 | tf_op jit(solution)/shard_map/ppermute | solution.py:376
  11.1 9.9 %collective-permute-start.2 = (bf16[128,448]{1,0:T(8,128)(2,1)S(1)}, bf16[128,448]{1,0:T(8,128)(2,1)}, u32[]{:S(2)}, u32[]{:S(2)}) collective-permute-start(bf16[128,448]{1,0:T(8,128)(2,1)S(1)} %bitcast.45), channel_id=1, source_target_pairs={{0,12},{1,13},{2,14},{3,15},{16,28},{17,29},{18,30},{19,31}} | collective-permute-start | bytes 344072 | tf_op jit(solution)/shard_map/ppermute | solution.py:376
  16.9 21.5 %copy-start = (bf16[1,1,256,3584]{3,2,1,0:T(8,128)(2,1)S(1)}, bf16[1,1,256,3584]{3,2,1,0:T(8,128)(2,1)}, u32[]{:S(2)}) copy-start(bf16[1,1,256,3584]{3,2,1,0:T(8,128)(2,1)} %param.27) | copy-start | bytes 5505028
  16.9 26.0 %copy-start.4 = (f32[1,3584]{1,0:T(1,128)S(1)}, f32[1,3584]{1,0:T(1,128)}, u32[]{:S(2)}) copy-start(f32[1,3584]{1,0:T(1,128)} %gain_ref.3) | copy-start | bytes 43012
  16.9 26.0 %copy-start.5 = (bf16[1,128,3584]{2,1,0:T(8,128)(2,1)S(1)}, bf16[1,128,3584]{2,1,0:T(8,128)(2,1)}, u32[]{:S(2)}) copy-start(bf16[1,128,3584]{2,1,0:T(8,128)(2,1)} %param.14) | copy-start | bytes 2752516
  21.0 17.4 %copy-start.13 = (bf16[144,896]{1,0:T(8,128)(2,1)}, bf16[144,896]{1,0:T(8,128)(2,1)S(1)}, u32[]{:S(2)}) copy-start(bf16[144,896]{1,0:T(8,128)(2,1)S(1)} %get-tuple-element.135) | copy-start | bytes 774148
  21.0 17.4 %copy-start.15 = (bf16[144,896]{1,0:T(8,128)(2,1)}, bf16[144,896]{1,0:T(8,128)(2,1)S(1)}, u32[]{:S(2)}) copy-start(bf16[144,896]{1,0:T(8,128)(2,1)S(1)} %get-tuple-element.137) | copy-start | bytes 774148
  21.0 19.0 %copy-start.23 = (bf16[144,896]{1,0:T(8,128)(2,1)}, bf16[144,896]{1,0:T(8,128)(2,1)S(1)}, u32[]{:S(2)}) copy-start(bf16[144,896]{1,0:T(8,128)(2,1)S(1)} %get-tuple-element.140.refs_0_) | copy-start | bytes 774148
  21.0 19.0 %copy-start.25 = (bf16[144,896]{1,0:T(8,128)(2,1)}, bf16[144,896]{1,0:T(8,128)(2,1)S(1)}, u32[]{:S(2)}) copy-start(bf16[144,896]{1,0:T(8,128)(2,1)S(1)} %get-tuple-element.114.refs_0_) | copy-start | bytes 774148
  23.6 13.3 %collective-permute-start.3 = (bf16[512,448]{1,0:T(8,128)(2,1)S(1)}, bf16[512,448]{1,0:T(8,128)(2,1)}, u32[]{:S(2)}, u32[]{:S(2)}) collective-permute-start(bf16[512,448]{1,0:T(8,128)(2,1)S(1)} %constant_dynamic-update-slice_fusion.kv0), channel_id=1, source_target_pairs={{0,2},{1,3},{2,0},{3,1},{4,6},{5,7},{6,4},{7,5},{8,10},{9,11},{10,... | collective-permute-start | bytes 1376264 | tf_op jit(solution)/shard_map/ppermute | solution.py:37
  25.1 8.9 %collective-permute-start.6 = (bf16[144,896]{1,0:T(8,128)(2,1)S(1)}, bf16[144,896]{1,0:T(8,128)(2,1)S(1)}, u32[]{:S(2)}, u32[]{:S(2)}) collective-permute-start(bf16[144,896]{1,0:T(8,128)(2,1)S(1)} %get-tuple-element.103), channel_id=1, source_target_pairs={{0,4},{1,5},{2,6},{3,7},{4,8},{5,9},{6,10},{7,11},{8,12},{9,13},{1... | collective-permute-start | bytes 774152 | tf_op jit(solution)/shard_map/ppermute | solution.py:42
  36.9 23.0 %collective-permute-start.12 = (bf16[128,3584]{1,0:T(8,128)(2,1)}, bf16[128,3584]{1,0:T(8,128)(2,1)}, u32[]{:S(2)}, u32[]{:S(2)}) collective-permute-start(bf16[128,3584]{1,0:T(8,128)(2,1)} %bitcast.10.middle_ref), channel_id=1, source_target_pairs={{0,16},{1,17},{2,18},{3,19},{4,20},{5,21},{6,22},{7,23},{8,24},{9,... | collective-permute-start | bytes 2752520 | tf_op jit(solution)/shard_map/ppermute | solution.py:33
  38.4 4.5 %collective-permute-start.4 = (bf16[512,448]{1,0:T(8,128)(2,1)S(1)}, bf16[512,448]{1,0:T(8,128)(2,1)}, u32[]{:S(2)}, u32[]{:S(2)}) collective-permute-start(bf16[512,448]{1,0:T(8,128)(2,1)S(1)} %constant_dynamic-update-slice_fusion.kv0), channel_id=1, source_target_pairs={{0,1},{1,0},{2,3},{3,2},{4,5},{5,4},{6,7},{7,6},{8,9},{9,8},{10,11... | collective-permute-start | bytes 1376264 | tf_op jit(solution)/shard_map/ppermute | solution.py:37
  38.4 45.1 %collective-permute-start.14 = (bf16[256,3584]{1,0:T(8,128)(2,1)S(1)}, bf16[256,3584]{1,0:T(8,128)(2,1)}, u32[]{:S(2)}, u32[]{:S(2)}) collective-permute-start(bf16[256,3584]{1,0:T(8,128)(2,1)S(1)} %bitcast.28), channel_id=1, source_target_pairs={{0,2},{1,3},{2,0},{3,1},{4,6},{5,7},{6,4},{7,5},{8,10},{9,11},{10,... | collective-permute-start | bytes 5505032 | tf_op jit(solution)/shard_map/ppermute | solution.py:37
  40.0 2.9 %collective-permute-start.5 = (bf16[512,448]{1,0:T(8,128)(2,1)}, bf16[512,448]{1,0:T(8,128)(2,1)}, u32[]{:S(2)}, u32[]{:S(2)}) collective-permute-start(bf16[512,448]{1,0:T(8,128)(2,1)} %collective-permute-done.3.kv1), channel_id=1, source_target_pairs={{0,1},{1,0},{2,3},{3,2},{4,5},{5,4},{6,7},{7,6},{8,9},{9,8},{10,11... | collective-permute-start | bytes 1376264 | tf_op jit(solution)/shard_map/ppermute | solution.py:37
  41.6 10.9 %collective-permute-start.8 = (bf16[144,896]{1,0:T(8,128)(2,1)}, bf16[144,896]{1,0:T(8,128)(2,1)}, u32[]{:S(2)}, u32[]{:S(2)}) collective-permute-start(bf16[144,896]{1,0:T(8,128)(2,1)} %get-tuple-element.107), channel_id=1, source_target_pairs={{0,12},{1,13},{2,14},{3,15},{4,0},{5,1},{6,2},{7,3},{8,4},{9,5},{1... | collective-permute-start | bytes 774152 | tf_op jit(solution)/shard_map/ppermute | solution.py:42
  42.9 17.0 %collective-permute-start.7 = (bf16[144,896]{1,0:T(8,128)(2,1)}, bf16[144,896]{1,0:T(8,128)(2,1)}, u32[]{:S(2)}, u32[]{:S(2)}) collective-permute-start(bf16[144,896]{1,0:T(8,128)(2,1)} %get-tuple-element.105), channel_id=1, source_target_pairs={{0,8},{1,9},{2,10},{3,11},{4,12},{5,13},{6,14},{7,15},{8,0},{9,1},... | collective-permute-start | bytes 774152 | tf_op jit(solution)/shard_map/ppermute | solution.py:42
  44.1 15.8 %copy-start.20 = (bf16[144,896]{1,0:T(8,128)(2,1)S(1)}, bf16[144,896]{1,0:T(8,128)(2,1)}, u32[]{:S(2)}) copy-start(bf16[144,896]{1,0:T(8,128)(2,1)} %copy-done.19) | copy-start | bytes 774148
  44.1 15.8 %copy-start.26 = (bf16[144,896]{1,0:T(8,128)(2,1)S(1)}, bf16[144,896]{1,0:T(8,128)(2,1)}, u32[]{:S(2)}) copy-start(bf16[144,896]{1,0:T(8,128)(2,1)} %copy-done.25) | copy-start | bytes 774148
  62.1 40.9 %collective-permute-start.13 = (bf16[144,3584]{1,0:T(8,128)(2,1)S(1)}, bf16[144,3584]{1,0:T(8,128)(2,1)S(1)}, u32[]{:S(2)}, u32[]{:S(2)}) collective-permute-start(bf16[144,3584]{1,0:T(8,128)(2,1)S(1)} %shard_map.151.first_ref), channel_id=1, source_target_pairs={{0,2},{1,3},{2,0},{3,1},{4,6},{5,7},{6,4},{7,5},{8,10},{9,11},{10,... | collective-permute-start | bytes 3096584 | tf_op jit(solution)/shard_map/ppermute | solution.py:37
  62.7 43.1 %copy-start.8 = (bf16[1,128,3584]{2,1,0:T(8,128)(2,1)S(1)}, bf16[1,128,3584]{2,1,0:T(8,128)(2,1)}, u32[]{:S(2)}) copy-start(bf16[1,128,3584]{2,1,0:T(8,128)(2,1)} %param.21) | copy-start | bytes 2752516
  62.7 43.6 %copy-start.18 = (bf16[144,896]{1,0:T(8,128)(2,1)S(1)}, bf16[144,896]{1,0:T(8,128)(2,1)}, u32[]{:S(2)}) copy-start(bf16[144,896]{1,0:T(8,128)(2,1)} %copy-done.17) | copy-start | bytes 774148
  62.7 44.8 %copy-start.16 = (bf16[144,896]{1,0:T(8,128)(2,1)S(1)}, bf16[144,896]{1,0:T(8,128)(2,1)}, u32[]{:S(2)}) copy-start(bf16[144,896]{1,0:T(8,128)(2,1)} %copy-done.15) | copy-start | bytes 774148
  62.7 44.8 %copy-start.14 = (bf16[144,896]{1,0:T(8,128)(2,1)S(1)}, bf16[144,896]{1,0:T(8,128)(2,1)}, u32[]{:S(2)}) copy-start(bf16[144,896]{1,0:T(8,128)(2,1)} %copy-done.13) | copy-start | bytes 774148
  62.7 66.0 %copy-start.24 = (bf16[144,896]{1,0:T(8,128)(2,1)S(1)}, bf16[144,896]{1,0:T(8,128)(2,1)}, u32[]{:S(2)}) copy-start(bf16[144,896]{1,0:T(8,128)(2,1)} %copy-done.23) | copy-start | bytes 774148
  62.7 20.8 %collective-permute-start.10 = (bf16[144,896]{1,0:T(8,128)(2,1)S(1)}, bf16[144,896]{1,0:T(8,128)(2,1)S(1)}, u32[]{:S(2)}, u32[]{:S(2)}) collective-permute-start(bf16[144,896]{1,0:T(8,128)(2,1)S(1)} %get-tuple-element.110), channel_id=1, source_target_pairs={{0,8},{1,9},{2,10},{3,11},{4,12},{5,13},{6,14},{7,15},{8,0},{9,1},... | collective-permute-start | bytes 774152 | tf_op jit(solution)/shard_map/ppermute | solution.py:42
  62.8 20.7 %collective-permute-start.11 = (bf16[144,896]{1,0:T(8,128)(2,1)S(1)}, bf16[144,896]{1,0:T(8,128)(2,1)S(1)}, u32[]{:S(2)}, u32[]{:S(2)}) collective-permute-start(bf16[144,896]{1,0:T(8,128)(2,1)S(1)} %get-tuple-element.111), channel_id=1, source_target_pairs={{0,12},{1,13},{2,14},{3,15},{4,0},{5,1},{6,2},{7,3},{8,4},{9,5},{1... | collective-permute-start | bytes 774152 | tf_op jit(solution)/shard_map/ppermute | solution.py:42
  66.7 16.8 %collective-permute-start.9 = (bf16[144,896]{1,0:T(8,128)(2,1)S(1)}, bf16[144,896]{1,0:T(8,128)(2,1)S(1)}, u32[]{:S(2)}, u32[]{:S(2)}) collective-permute-start(bf16[144,896]{1,0:T(8,128)(2,1)S(1)} %get-tuple-element.109), channel_id=1, source_target_pairs={{0,4},{1,5},{2,6},{3,7},{4,8},{5,9},{6,10},{7,11},{8,12},{9,13},{1... | collective-permute-start | bytes 774152 | tf_op jit(solution)/shard_map/ppermute | solution.py:42
  104.1 26.8 %copy-start.30 = (s32[1,128,1]{1,2,0:T(1,128)S(1)}, s32[1,128,1]{1,2,0:T(1,128)}, u32[]{:S(2)}) copy-start(s32[1,128,1]{1,2,0:T(1,128)} %param.18) | copy-start | bytes 1540
  104.1 26.8 %copy-start.29 = (f32[1,128,1]{1,2,0:T(1,128)S(1)}, f32[1,128,1]{1,2,0:T(1,128)}, u32[]{:S(2)}) copy-start(f32[1,128,1]{1,2,0:T(1,128)} %param.19) | copy-start | bytes 1540
  104.1 26.8 %copy-start.28 = (f32[1,128]{1,0:T(1,128)S(1)}, f32[1,128]{1,0:T(1,128)}, u32[]{:S(2)}) copy-start(f32[1,128]{1,0:T(1,128)} %get-tuple-element.170) | copy-start | bytes 1540
  104.1 28.9 %copy-start.1 = (bf16[1,1,3584,256]{3,2,1,0:T(8,128)(2,1)S(1)}, bf16[1,1,3584,256]{3,2,1,0:T(8,128)(2,1)}, u32[]{:S(2)}) copy-start(bf16[1,1,3584,256]{3,2,1,0:T(8,128)(2,1)} %param.25) | copy-start | bytes 5505028
  104.1 28.9 %copy-start.2 = (bf16[1,1,3584,256]{3,2,1,0:T(8,128)(2,1)S(1)}, bf16[1,1,3584,256]{3,2,1,0:T(8,128)(2,1)}, u32[]{:S(2)}) copy-start(bf16[1,1,3584,256]{3,2,1,0:T(8,128)(2,1)} %param.26) | copy-start | bytes 5505028
  104.2 24.5 %collective-permute-start.16 = (bf16[144,3584]{1,0:T(8,128)(2,1)S(1)}, bf16[144,3584]{1,0:T(8,128)(2,1)S(1)}, u32[]{:S(2)}, u32[]{:S(2)}) collective-permute-start(bf16[144,3584]{1,0:T(8,128)(2,1)S(1)} %shard_map.152.first_ref), channel_id=1, source_target_pairs={{0,2},{1,3},{2,0},{3,1},{4,6},{5,7},{6,4},{7,5},{8,10},{9,11},{10,... | collective-permute-start | bytes 3096584 | tf_op jit(solution)/shard_map/ppermute | solution.py:37
  105.7 21.7 %collective-permute-start.17 = (bf16[128,3584]{1,0:T(8,128)(2,1)S(1)}, bf16[128,3584]{1,0:T(8,128)(2,1)S(1)}, u32[]{:S(2)}, u32[]{:S(2)}) collective-permute-start(bf16[128,3584]{1,0:T(8,128)(2,1)S(1)} %bitcast.42), channel_id=1, source_target_pairs={{0,16},{1,17},{2,18},{3,19},{4,20},{5,21},{6,22},{7,23},{8,24},{9,... | collective-permute-start | bytes 2752520 | tf_op jit(solution)/shard_map/ppermute | solution.py:33
  106.2 22.4 %collective-permute-start.30 = (bf16[144,896]{1,0:T(8,128)(2,1)S(1)}, bf16[144,896]{1,0:T(8,128)(2,1)S(1)}, u32[]{:S(2)}, u32[]{:S(2)}) collective-permute-start(bf16[144,896]{1,0:T(8,128)(2,1)S(1)} %copy-done.18), channel_id=1, source_target_pairs={{0,12},{1,13},{2,14},{3,15},{4,0},{5,1},{6,2},{7,3},{8,4},{9,5},{1... | collective-permute-start | bytes 774152 | tf_op jit(solution)/shard_map/ppermute | solution.py:42
  107.5 21.2 %collective-permute-start.29 = (bf16[144,896]{1,0:T(8,128)(2,1)S(1)}, bf16[144,896]{1,0:T(8,128)(2,1)S(1)}, u32[]{:S(2)}, u32[]{:S(2)}) collective-permute-start(bf16[144,896]{1,0:T(8,128)(2,1)S(1)} %copy-done.16), channel_id=1, source_target_pairs={{0,8},{1,9},{2,10},{3,11},{4,12},{5,13},{6,14},{7,15},{8,0},{9,1},... | collective-permute-start | bytes 774152 | tf_op jit(solution)/shard_map/ppermute | solution.py:42
  107.5 21.2 %collective-permute-start.28 = (bf16[144,896]{1,0:T(8,128)(2,1)S(1)}, bf16[144,896]{1,0:T(8,128)(2,1)S(1)}, u32[]{:S(2)}, u32[]{:S(2)}) collective-permute-start(bf16[144,896]{1,0:T(8,128)(2,1)S(1)} %copy-done.14), channel_id=1, source_target_pairs={{0,4},{1,5},{2,6},{3,7},{4,8},{5,9},{6,10},{7,11},{8,12},{9,13},{1... | collective-permute-start | bytes 774152 | tf_op jit(solution)/shard_map/ppermute | solution.py:42
  128.6 3.3 %collective-permute-start.20 = (bf16[144,3584]{1,0:T(8,128)(2,1)S(1)}, bf16[144,3584]{1,0:T(8,128)(2,1)S(1)}, u32[]{:S(2)}, u32[]{:S(2)}) collective-permute-start(bf16[144,3584]{1,0:T(8,128)(2,1)S(1)} %collective-permute-done.16.first_ref), channel_id=1, source_target_pairs={{0,1},{1,0},{2,3},{3,2},{4,5},{5,4},{6,7},{7,6},{8,9},{9,8},{10,11... | collective-permute-start | bytes 3096584 | tf_op jit(solution)/shard_map/ppermute | solution.py:37
  129.8 6.8 %collective-permute-start.31 = (bf16[144,3584]{1,0:T(8,128)(2,1)S(1)}, bf16[144,3584]{1,0:T(8,128)(2,1)S(1)}, u32[]{:S(2)}, u32[]{:S(2)}) collective-permute-start(bf16[144,3584]{1,0:T(8,128)(2,1)S(1)} %shard_map.157.first_ref), channel_id=1, source_target_pairs={{0,1},{1,0},{2,3},{3,2},{4,5},{5,4},{6,7},{7,6},{8,9},{9,8},{10,11... | collective-permute-start | bytes 3096584 | tf_op jit(solution)/shard_map/ppermute | solution.py:37
  130.3 10.1 %collective-permute-start.19 = (bf16[144,3584]{1,0:T(8,128)(2,1)S(1)}, bf16[144,3584]{1,0:T(8,128)(2,1)S(1)}, u32[]{:S(2)}, u32[]{:S(2)}) collective-permute-start(bf16[144,3584]{1,0:T(8,128)(2,1)S(1)} %shard_map.152.first_ref), channel_id=1, source_target_pairs={{0,1},{1,0},{2,3},{3,2},{4,5},{5,4},{6,7},{7,6},{8,9},{9,8},{10,11... | collective-permute-start | bytes 3096584 | tf_op jit(solution)/shard_map/ppermute | solution.py:37
  130.4 15.0 %collective-permute-start.34 = (bf16[144,3584]{1,0:T(8,128)(2,1)S(1)}, bf16[144,3584]{1,0:T(8,128)(2,1)S(1)}, u32[]{:S(2)}, u32[]{:S(2)}) collective-permute-start(bf16[144,3584]{1,0:T(8,128)(2,1)S(1)} %collective-permute-done.13.first_ref), channel_id=1, source_target_pairs={{0,1},{1,0},{2,3},{3,2},{4,5},{5,4},{6,7},{7,6},{8,9},{9,8},{10,11... | collective-permute-start | bytes 3096584 | tf_op jit(solution)/shard_map/ppermute | solution.py:37
  130.9 4.6 %collective-permute-start.32 = (f32[1,3712]{1,0:T(1,128)S(1)}, f32[1,3712]{1,0:T(1,128)S(1)}, u32[]{:S(2)}, u32[]{:S(2)}) collective-permute-start(f32[1,3712]{1,0:T(1,128)S(1)} %pad_maximum_fusion), channel_id=1, source_target_pairs={{0,16},{1,17},{2,18},{3,19},{4,20},{5,21},{6,22},{7,23},{8,24},{9,... | collective-permute-start | bytes 44552 | tf_op jit(solution)/shard_map/ppermute | solution.py:33
  132.0 3.6 %collective-permute-start.15 = (f32[1,256]{1,0:T(1,128)S(1)}, f32[1,256]{1,0:T(1,128)S(1)}, u32[]{:S(2)}, u32[]{:S(2)}) collective-permute-start(f32[1,256]{1,0:T(1,128)S(1)} %maximum_bitcast_fusion), channel_id=1, source_target_pairs={{0,16},{1,17},{2,18},{3,19},{4,20},{5,21},{6,22},{7,23},{8,24},{9,... | collective-permute-start | bytes 3080 | tf_op jit(solution)/shard_map/ppermute | solution.py:33
  135.5 14.0 %collective-permute-start.27 = (bf16[144,3584]{1,0:T(8,128)(2,1)S(1)}, bf16[144,3584]{1,0:T(8,128)(2,1)S(1)}, u32[]{:S(2)}, u32[]{:S(2)}) collective-permute-start(bf16[144,3584]{1,0:T(8,128)(2,1)S(1)} %shard_map.151.first_ref), channel_id=1, source_target_pairs={{0,1},{1,0},{2,3},{3,2},{4,5},{5,4},{6,7},{7,6},{8,9},{9,8},{10,11... | collective-permute-start | bytes 3096584 | tf_op jit(solution)/shard_map/ppermute | solution.py:37
  135.6 6.3 %collective-permute-start.21 = (bf16[288,256]{1,0:T(8,128)(2,1)S(1)}, bf16[288,256]{1,0:T(8,128)(2,1)S(1)}, u32[]{:S(2)}, u32[]{:S(2)}) collective-permute-start(bf16[288,256]{1,0:T(8,128)(2,1)S(1)} %shard_map.154), channel_id=1, source_target_pairs={{0,2},{1,3},{2,0},{3,1},{4,6},{5,7},{6,4},{7,5},{8,10},{9,11},{10,... | collective-permute-start | bytes 442376 | tf_op jit(solution)/shard_map/ppermute | solution.py:37
  139.3 6.0 %collective-permute-start.35 = (bf16[288,256]{1,0:T(8,128)(2,1)S(1)}, bf16[288,256]{1,0:T(8,128)(2,1)S(1)}, u32[]{:S(2)}, u32[]{:S(2)}) collective-permute-start(bf16[288,256]{1,0:T(8,128)(2,1)S(1)} %get-tuple-element.150), channel_id=1, source_target_pairs={{0,2},{1,3},{2,0},{3,1},{4,6},{5,7},{6,4},{7,5},{8,10},{9,11},{10,... | collective-permute-start | bytes 442376 | tf_op jit(solution)/shard_map/ppermute | solution.py:37
  147.8 4.7 %collective-permute-start.36 = (bf16[144,3584]{1,0:T(8,128)(2,1)S(1)}, bf16[144,3584]{1,0:T(8,128)(2,1)S(1)}, u32[]{:S(2)}, u32[]{:S(2)}) collective-permute-start(bf16[144,3584]{1,0:T(8,128)(2,1)S(1)} %get-tuple-element.153), channel_id=1, source_target_pairs={{0,1},{1,0},{2,3},{3,2},{4,5},{5,4},{6,7},{7,6},{8,9},{9,8},{10,11... | collective-permute-start | bytes 3096584 | tf_op jit(solution)/shard_map/ppermute | solution.py:37
  147.9 28.7 %collective-permute-start.18 = (bf16[128,3584]{1,0:T(8,128)(2,1)S(1)}, bf16[128,3584]{1,0:T(8,128)(2,1)S(1)}, u32[]{:S(2)}, u32[]{:S(2)}) collective-permute-start(bf16[128,3584]{1,0:T(8,128)(2,1)S(1)} %get-tuple-element.126), channel_id=1, source_target_pairs={{0,16},{1,17},{2,18},{3,19},{4,20},{5,21},{6,22},{7,23},{8,24},{9,... | collective-permute-start | bytes 2752520 | tf_op jit(solution)/shard_map/ppermute | solution.py:33
  152.0 6.1 %copy-start.21 = (bf16[144,3584]{1,0:T(8,128)(2,1)}, bf16[144,3584]{1,0:T(8,128)(2,1)S(1)}, u32[]{:S(2)}) copy-start(bf16[144,3584]{1,0:T(8,128)(2,1)S(1)} %get-tuple-element.155.refs_0_) | copy-start | bytes 3096580
  152.0 28.4 %collective-permute-start.33 = (bf16[144,3584]{1,0:T(8,128)(2,1)S(1)}, bf16[144,3584]{1,0:T(8,128)(2,1)S(1)}, u32[]{:S(2)}, u32[]{:S(2)}) collective-permute-start(bf16[144,3584]{1,0:T(8,128)(2,1)S(1)} %get-tuple-element.149), channel_id=1, source_target_pairs={{0,1},{1,0},{2,3},{3,2},{4,5},{5,4},{6,7},{7,6},{8,9},{9,8},{10,11... | collective-permute-start | bytes 3096584 | tf_op jit(solution)/shard_map/ppermute | solution.py:37
  152.2 3.9 %collective-permute-start.22 = (bf16[144,3584]{1,0:T(8,128)(2,1)S(1)}, bf16[144,3584]{1,0:T(8,128)(2,1)S(1)}, u32[]{:S(2)}, u32[]{:S(2)}) collective-permute-start(bf16[144,3584]{1,0:T(8,128)(2,1)S(1)} %get-tuple-element.128), channel_id=1, source_target_pairs={{0,1},{1,0},{2,3},{3,2},{4,5},{5,4},{6,7},{7,6},{8,9},{9,8},{10,11... | collective-permute-start | bytes 3096584 | tf_op jit(solution)/shard_map/ppermute | solution.py:37
  153.8 26.8 %collective-permute-start.37 = (bf16[144,3584]{1,0:T(8,128)(2,1)}, bf16[144,3584]{1,0:T(8,128)(2,1)S(1)}, u32[]{:S(2)}, u32[]{:S(2)}) collective-permute-start(bf16[144,3584]{1,0:T(8,128)(2,1)} %add_convert_fusion), channel_id=1, source_target_pairs={{0,2},{1,3},{2,0},{3,1},{4,6},{5,7},{6,4},{7,5},{8,10},{9,11},{10,... | collective-permute-start | bytes 3096584 | tf_op jit(solution)/shard_map/ppermute | solution.py:37
  158.0 27.4 %collective-permute-start.23 = (bf16[144,896]{1,0:T(8,128)(2,1)}, bf16[144,896]{1,0:T(8,128)(2,1)}, u32[]{:S(2)}, u32[]{:S(2)}) collective-permute-start(bf16[144,896]{1,0:T(8,128)(2,1)} %get-tuple-element.129), channel_id=1, source_target_pairs={{0,16},{1,17},{2,18},{3,19},{4,20},{5,21},{6,22},{7,23},{8,24},{9,... | collective-permute-start | bytes 774152 | tf_op jit(solution)/shard_map/ppermute | solution.py:33
  158.6 35.9 %collective-permute-start.24 = (bf16[144,896]{1,0:T(8,128)(2,1)}, bf16[144,896]{1,0:T(8,128)(2,1)}, u32[]{:S(2)}, u32[]{:S(2)}) collective-permute-start(bf16[144,896]{1,0:T(8,128)(2,1)} %get-tuple-element.130), channel_id=1, source_target_pairs={{0,28},{1,29},{2,30},{3,31},{4,16},{5,17},{6,18},{7,19},{8,20},{9,... | collective-permute-start | bytes 774152 | tf_op jit(solution)/shard_map/ppermute | solution.py:33
  177.6 23.6 %collective-permute-start.25 = (bf16[144,896]{1,0:T(8,128)(2,1)}, bf16[144,896]{1,0:T(8,128)(2,1)}, u32[]{:S(2)}, u32[]{:S(2)}) collective-permute-start(bf16[144,896]{1,0:T(8,128)(2,1)} %get-tuple-element.131), channel_id=1, source_target_pairs={{0,24},{1,25},{2,26},{3,27},{4,28},{5,29},{6,30},{7,31},{8,16},{9,... | collective-permute-start | bytes 774152 | tf_op jit(solution)/shard_map/ppermute | solution.py:33
  180.4 20.9 %collective-permute-start.26 = (bf16[144,896]{1,0:T(8,128)(2,1)S(1)}, bf16[144,896]{1,0:T(8,128)(2,1)}, u32[]{:S(2)}, u32[]{:S(2)}) collective-permute-start(bf16[144,896]{1,0:T(8,128)(2,1)S(1)} %get-tuple-element.132), channel_id=1, source_target_pairs={{0,20},{1,21},{2,22},{3,23},{4,24},{5,25},{6,26},{7,27},{8,28},{9,... | collective-permute-start | bytes 774152 | tf_op jit(solution)/shard_map/ppermute | solution.py:33
  181.8 19.5 %copy-start.12 = (bf16[128,3584]{1,0:T(8,128)(2,1)S(1)}, bf16[128,3584]{1,0:T(8,128)(2,1)}, u32[]{:S(2)}) copy-start(bf16[128,3584]{1,0:T(8,128)(2,1)} %copy-done.11) | copy-start | bytes 2752516
  184.0 28.9 %collective-permute-start.38 = (bf16[144,896]{1,0:T(8,128)(2,1)}, bf16[144,896]{1,0:T(8,128)(2,1)S(1)}, u32[]{:S(2)}, u32[]{:S(2)}) collective-permute-start(bf16[144,896]{1,0:T(8,128)(2,1)} %get-tuple-element.158), channel_id=1, source_target_pairs={{0,16},{1,17},{2,18},{3,19},{4,20},{5,21},{6,22},{7,23},{8,24},{9,... | collective-permute-start | bytes 774152 | tf_op jit(solution)/shard_map/ppermute | solution.py:33
  185.5 27.4 %collective-permute-start.39 = (bf16[144,896]{1,0:T(8,128)(2,1)}, bf16[144,896]{1,0:T(8,128)(2,1)S(1)}, u32[]{:S(2)}, u32[]{:S(2)}) collective-permute-start(bf16[144,896]{1,0:T(8,128)(2,1)} %get-tuple-element.159), channel_id=1, source_target_pairs={{0,28},{1,29},{2,30},{3,31},{4,16},{5,17},{6,18},{7,19},{8,20},{9,... | collective-permute-start | bytes 774152 | tf_op jit(solution)/shard_map/ppermute | solution.py:33
  194.4 26.3 %collective-permute-start.40 = (bf16[144,896]{1,0:T(8,128)(2,1)}, bf16[144,896]{1,0:T(8,128)(2,1)S(1)}, u32[]{:S(2)}, u32[]{:S(2)}) collective-permute-start(bf16[144,896]{1,0:T(8,128)(2,1)} %get-tuple-element.160), channel_id=1, source_target_pairs={{0,24},{1,25},{2,26},{3,27},{4,28},{5,29},{6,30},{7,31},{8,16},{9,... | collective-permute-start | bytes 774152 | tf_op jit(solution)/shard_map/ppermute | solution.py:33
  201.2 19.6 %collective-permute-start.41 = (bf16[144,896]{1,0:T(8,128)(2,1)}, bf16[144,896]{1,0:T(8,128)(2,1)S(1)}, u32[]{:S(2)}, u32[]{:S(2)}) collective-permute-start(bf16[144,896]{1,0:T(8,128)(2,1)} %get-tuple-element.161), channel_id=1, source_target_pairs={{0,20},{1,21},{2,22},{3,23},{4,24},{5,25},{6,26},{7,27},{8,28},{9,... | collective-permute-start | bytes 774152 | tf_op jit(solution)/shard_map/ppermute | solution.py:33
  201.3 19.4 %copy-start.10 = (bf16[128,3584]{1,0:T(8,128)(2,1)S(1)}, bf16[128,3584]{1,0:T(8,128)(2,1)}, u32[]{:S(2)}) copy-start(bf16[128,3584]{1,0:T(8,128)(2,1)} %copy-done.9) | copy-start | bytes 2752516
  (9 other events, 8.3 us)

commit v10 on v9

--- a/solution.py
+++ b/solution.py
@@ -447,14 +447,37 @@
         vmem=VMEM_BYTES + 2 * length * tokens * 4 * LANES * 2,
     )
     middle, front_chunks = result[0], result[1:]
-    front_chunks = sent(after(front_chunks, row_chunks))
+    work = 2 * 2 * slots * width * hidden_width
+    pair = 2 * slots
+
+    def hidden(rows):
+        return call(
+            hidden_body, shape_of(pair, hidden_width), (*rows, w_gate, w_up), flops=2 * work
+        )
+
+    def backward(rows, grads):
+        return call(backward_body, [piece, piece], (*rows, grads, w_gate, w_up), flops=4 * work)
+
+    for k in range(1, experts):
+        grad_chunks[k] = turned(after([grad_chunks[k]], [middle])[0], k)
+    front_chunks = sent(after(front_chunks, row_chunks + grad_chunks[1:2]))
     back_rows = joined(after(row_chunks, [middle, there_back_middle]))
     back_pieces = pieces_of(back_rows)
-    for k in range(1, experts):
-        grad_chunks[k] = turned(after([grad_chunks[k]], front_chunks)[0], k)
-    front_near = joined(after(front_chunks, [back_pieces[2], down_other]))
-    there_back_grad = passed_along(after([back_grad[0]], [front_near])[0], -1)
-    front_other = after([swapped(front_near, 2)], [there_back_grad])[0]
+    grad_near = joined(after(grad_chunks, [back_rows, down_other]))
+    there_back_grad = passed_along(after([back_grad[0]], [grad_near])[0], -1)
+    grad_near = [grad_near, swapped(grad_near, 1)]
+    down_back, other_back = call(
+        down_back_body,
+        [shape_of(pair, hidden_width, f32), shape_of(pair, hidden_width)],
+        (*grad_near, *downs),
+        flops=2 * work,
+    )
+    far_back = swapped(other_back, 2)
+    back_near = backward(back_pieces[:2], down_back)
+    back_core = swapped(back_near[1], 1)
+    front_near = joined(after(front_chunks, [back_pieces[2], there_back_grad, far_back, back_near[0]]))
+    there_middle = passed_along(after([middle], [front_near])[0], 1)
+    front_other = after([swapped(front_near, 2)], [there_middle])[0]
 
     front_small, back_small = after([front_small, back_small], [front_near])
     there_small = passed_along(front_small, 1)
@@ -463,48 +486,25 @@
     there_front_gate = there_small[0, tokens:].reshape(tokens, 1)
     there_back_from = there_back_small[0, :tokens].astype(jnp.int32).reshape(tokens, 1)
     there_gain = there_back_small[:, tokens:]
-    grad_near = joined(after(grad_chunks, [front_other]))
-    grad_near = [grad_near, swapped(grad_near, 1)]
-
-    work = 2 * 2 * slots * width * hidden_width
-    pair = 2 * slots
-
-    def hidden(rows):
-        return call(
-            hidden_body, shape_of(pair, hidden_width), (*rows, w_gate, w_up), flops=2 * work
-        )
-
-    def backward(rows, grads):
-        return call(backward_body, [piece, piece], (*rows, grads, w_gate, w_up), flops=4 * work)
-
-    there_middle = passed_along(after([middle], [front_other])[0], 1)
     front_pieces = [front_near, swapped(front_near, 1), front_other, swapped(front_other, 1)]
     hidden_near = hidden(front_pieces[:2])
     hidden_far = hidden(front_pieces[2:])
     hidden_other = swapped(hidden_far, 2)
-    down_back, other_back = call(
-        down_back_body,
-        [shape_of(pair, hidden_width, f32), shape_of(pair, hidden_width)],
-        (*after(grad_near, [there_small, there_back_small, hidden_far]), *downs),
-        flops=2 * work,
-    )
-    far_back = swapped(other_back, 2)
-
+    (hidden_other,) = after([hidden_other], [there_small, there_back_small])
     front_own, front_core = call(
         output_body, [piece, piece], (hidden_near, hidden_other, *downs), flops=2 * work
     )
-    (far_back,) = after([far_back], [front_own])
-    back_near = backward(back_pieces[:2], down_back)
+    (far_back,) = after([far_back], [front_other])
     back_far = backward(back_pieces[2:], far_back)
     chip = back_far[0].astype(f32) + swapped(back_far[1], 1).astype(f32)
     (chip,) = after([chip.astype(bf16)], [hidden_other])
-    back_shares = (back_near[0], swapped(back_near[1], 1), swapped(chip, 2))
+    back_shares = (back_near[0], back_core, swapped(chip, 2))
 
     front_shares = (front_own, swapped(front_core, 1))
     front_chunks = split(front_shares)
     front_return = sent_back(front_chunks, 1)
 
-    back_chunks = split(after(back_shares, front_chunks + [there_middle]))
+    back_chunks = split(after(back_shares, front_chunks))
     back_return = sent_back(back_chunks, -1)
 
     front_return = after(front_return, back_chunks)

time: 225 us -> 214 us (0.951)
  waiting for transfers between devices: 116 us -> 106 us
  starting transfers between devices: 51 us -> 48.6 us
    ppermute x13, waiting for transfers between devices: 58.6 us -> 39.4 us  [passed_along(): return lax.ppermute(array, ('section', 'expert'), pairs)]
    ppermute x9, waiting for transfers between devices: 32.5 us -> 40.2 us  [turned(): lax.ppermute(array, 'expert', [(i, (i + by * GROUP) % length) for i in ra...]
    ppermute x13, starting transfers between devices: 21.7 us -> 15.7 us  [passed_along(): return lax.ppermute(array, ('section', 'expert'), pairs)]
    ppermute x9, starting transfers between devices: 8.04 us -> 13 us  [turned(): lax.ppermute(array, 'expert', [(i, (i + by * GROUP) % length) for i in ra...]
    ppermute x17, waiting for transfers between devices: 24.6 us -> 26.9 us  [swapped(): lax.ppermute(array, 'expert', [(i, i ^ bit) for i in range(lax.axis_size(...]
  transfers between devices with their start and end apart: 42 -> 42, of which waited for: 15 -> 19; matrix products, arithmetic and copies ran while one was open for 2% -> 2% of each run, Pallas kernels for 16% -> 17%
where the time goes in v10:
time: 214 us; the launch traced here: 213 us
  waiting for transfers between devices  106 us (50%)
  starting transfers between devices  48.6 us (23%)
  Pallas kernels  41.9 us (20%)
  local copies, waits for them, and re-layouts  12.1 us (6%)
  other arithmetic  3.23 us (2%)
    pallas_call x15, Pallas kernels, call(): pl.pallas_call(body, out_shape=shapes, in_specs=specs, out_specs=[pl.Bloc...  41.9 us
    ppermute x9, waiting for transfers between devices, turned(): lax.ppermute(array, 'expert', [(i, (i + by * GROUP) % length) for i in ra...  40.2 us
    ppermute x13, waiting for transfers between devices, passed_along(): return lax.ppermute(array, ('section', 'expert'), pairs)  39.4 us
    ppermute x17, waiting for transfers between devices, swapped(): lax.ppermute(array, 'expert', [(i, i ^ bit) for i in range(lax.axis_size(...  26.9 us
    ppermute x13, starting transfers between devices, passed_along(): return lax.ppermute(array, ('section', 'expert'), pairs)  15.7 us
    ppermute x9, starting transfers between devices, turned(): lax.ppermute(array, 'expert', [(i, (i + by * GROUP) % length) for i in ra...  13 us
    ppermute x3, starting transfers between devices, shards(): column.append(lax.ppermute(keys_values[0], 'expert', pairs))  11.4 us
    unnamed x66, local copies, waits for them, and re-layouts  9.36 us
  transfers between devices with their start and end apart: 42, of which 19 were waited for; matrix products, arithmetic and copies ran while one was open for 2% of the time, Pallas kernels for 17%

profile of v10, /device:TPU:0, one launch (start us, length us, event | category | flops | bytes accessed | tf_op | source)
XLA Modules:
  0.0 213.4 jit_solution(6595458863065636070)
XLA Ops:
  0.6 1.0 copy.16
  1.6 4.9 %collective-permute-start = (bf16[128,448]{1,0:T(8,128)(2,1)S(1)}, bf16[128,448]{1,0:T(8,128)(2,1)S(1)}, u32[]{:S(2)}, u32[]{:S(2)}) collective-permute-start(bf16[128,448]{1,0:T(8,128)(2,1)S(1)} %bitcast.43), channel_id=1, source_target_pairs={{0,4},{1,5},{2,6},{3,7},{4,8},{5,9},{6,10},{7,11},{8,12},{9,13},{1... | collective-permute-start | bytes 344072 | tf_op jit(solution)/shard_map/ppermute | solution.py:376
  6.6 4.5 %collective-permute-start.1 = (bf16[128,448]{1,0:T(8,128)(2,1)S(1)}, bf16[128,448]{1,0:T(8,128)(2,1)S(1)}, u32[]{:S(2)}, u32[]{:S(2)}) collective-permute-start(bf16[128,448]{1,0:T(8,128)(2,1)S(1)} %bitcast.44), channel_id=1, source_target_pairs={{0,8},{1,9},{2,10},{3,11},{4,12},{5,13},{6,14},{7,15},{16,24},{17,... | collective-permute-start | bytes 344072 | tf_op jit(solution)/shard_map/ppermute | solution.py:376
  11.1 2.0 collective-permute-start.2
  13.0 0.8 copy.17.gate_ref
  13.8 1.3 fusion.11
  15.1 0.7 copy-done.3
  15.8 1.2 copy-done.7
  17.0 3.3 %shard_map.149 = (bf16[144,896]{1,0:T(8,128)(2,1)S(1)}, bf16[144,896]{1,0:T(8,128)(2,1)S(1)}, bf16[144,896]{1,0:T(8,128)(2,1)}, bf16[144,896]{1,0:T(8,128)(2,1)}...) custom-call(s32[1,128]{1,0:T(1,128)S(1)} %get-tuple-element.169.rout, ...), custom_call_target="tpu_custom_call" | custom-call | flops 2113929216 | bytes 3914752 | tf_op jit(solution)/shard_map/pallas_call | solution.py:55
  20.3 0.7 copy-done.13
  21.0 0.7 copy-done.27
  21.8 0.9 constant_dynamic-update-slice_fusion.1
  22.7 0.9 constant_dynamic-update-slice_fusion.kv0
  23.6 1.6 collective-permute-start.3
  25.2 8.9 %collective-permute-done.6.refs_1_ = bf16[144,896]{1,0:T(8,128)(2,1)S(1)} collective-permute-done((bf16[144,896]{1,0:T(8,128)(2,1)S(1)}, bf16[144,896]{1,0:T(8,128)(2,1)S(1)}, u32[]{:S(2)}, u32[]{:S(2)}) %collective-permute-start.6) | collective-permute-done | bytes 258080 | tf_op jit(solution)/shard_map/ppermute | solution.py:42
  34.1 0.7 copy-done.19
  34.8 2.1 collective-permute-done.3.kv1
  36.9 1.5 collective-permute-start.17
  38.4 1.6 collective-permute-start.13
  40.2 0.8 reshape_squeeze.6.chosen_ref
  41.6 1.4 collective-permute-start.8
  43.1 1.2 copy-done.6
  44.3 8.5 %shard_map.150 = (bf16[128,3584]{1,0:T(8,128)(2,1)S(1)}, bf16[144,896]{1,0:T(8,128)(2,1)S(1)}, bf16[144,896]{1,0:T(8,128)(2,1)S(1)}, bf16[144,896]{1,0:T(8,128)(2,1)S(1)}, bf16[144,896]{1,0:T(8,128)(2,1)S(1)}) custom-call(s32[16]{0:T(128)S(1)} %reshape_squeeze.6.chosen_ref, s32[16]{0:T(128)S(1)} %fusion.10.index_ref, s32[1]{0:T(128)} %bitcast.4.base_ref, ...), custom_call_target="tpu_custom_call" | custom-call | flops 1593835520 | bytes 5634692 | tf_op jit(solution)/shard_map/pallas_call | solution.py:55
  52.8 0.7 collective-permute-start.9
  53.5 2.0 collective-permute-done.7.refs_2_
  55.5 0.9 collective-permute-start.15
  56.4 8.2 %collective-permute-start.16 = (bf16[144,896]{1,0:T(8,128)(2,1)S(1)}, bf16[144,896]{1,0:T(8,128)(2,1)S(1)}, u32[]{:S(2)}, u32[]{:S(2)}) collective-permute-start(bf16[144,896]{1,0:T(8,128)(2,1)S(1)} %copy-done.14), channel_id=1, source_target_pairs={{0,12},{1,13},{2,14},{3,15},{4,0},{5,1},{6,2},{7,3},{8,4},{9,5},{1... | collective-permute-start | bytes 774152 | tf_op jit(solution)/shard_map/ppermute | solution.py:42
  64.6 2.2 %shard_map.151.first_ref = bf16[144,3584]{1,0:T(8,128)(2,1)S(1)} custom-call(bf16[144,896]{1,0:T(8,128)(2,1)S(1)} %copy-done.26, bf16[144,896]{1,0:T(8,128)(2,1)S(1)} %copy-done.20, bf16[144,896]{1,0:T(8,128)(2,1)} %collective-permute-done.7.refs_2_, bf16[144,896]{1,0:T(8,128)(2,1)} %collective-permute-done.8.refs_3_), custom_call_target="tpu_custom_call" | custom-call | flops 1056964608 | bytes 2064384 | tf_op jit(solution)/shard_map/pallas_call | solution.py:55
  66.8 10.7 %collective-permute-done.15.refs_2_ = bf16[144,896]{1,0:T(8,128)(2,1)S(1)} collective-permute-done((bf16[144,896]{1,0:T(8,128)(2,1)S(1)}, bf16[144,896]{1,0:T(8,128)(2,1)S(1)}, u32[]{:S(2)}, u32[]{:S(2)}) %collective-permute-start.15) | collective-permute-done | bytes 258080 | tf_op jit(solution)/shard_map/ppermute | solution.py:42
  77.5 5.4 %collective-permute-done.16.refs_3_ = bf16[144,896]{1,0:T(8,128)(2,1)S(1)} collective-permute-done((bf16[144,896]{1,0:T(8,128)(2,1)S(1)}, bf16[144,896]{1,0:T(8,128)(2,1)S(1)}, u32[]{:S(2)}, u32[]{:S(2)}) %collective-permute-start.16) | collective-permute-done | bytes 258080 | tf_op jit(solution)/shard_map/ppermute | solution.py:42
  83.0 1.1 shard_map.152.first_ref
  86.3 8.8 %collective-permute-done.10.refs_1_ = bf16[144,896]{1,0:T(8,128)(2,1)S(1)} collective-permute-done((bf16[144,896]{1,0:T(8,128)(2,1)S(1)}, bf16[144,896]{1,0:T(8,128)(2,1)S(1)}, u32[]{:S(2)}, u32[]{:S(2)}) %collective-permute-start.10) | collective-permute-done | bytes 258080 | tf_op jit(solution)/shard_map/ppermute | solution.py:42
  95.1 1.2 collective-permute-start.12
  96.3 2.8 %shard_map.153 = (f32[288,256]{1,0:T(8,128)S(1)}, bf16[288,256]{1,0:T(8,128)(2,1)S(1)}) custom-call(bf16[144,3584]{1,0:T(8,128)(2,1)S(1)} %shard_map.152.first_ref, bf16[144,3584]{1,0:T(8,128)(2,1)S(1)} %collective-permute-done.19.second_ref, bf16[256,3584]{1,0:T(8,128)(2,1)S(1)} %bitcast.37, bf16[256,3584]{1,0:T(8,128)(2,1)} %collective-permute-done.17.far_ref), custom_call_target="tpu_custom_call" | custom-call | flops 1056964608 | bytes 6176768 | tf_op jit(solution)/shard_map/pallas_call | solution.py:55
  99.1 1.6 collective-permute-start.20
  100.6 2.4 %shard_map.154 = (bf16[144,3584]{1,0:T(8,128)(2,1)S(1)}, bf16[144,3584]{1,0:T(8,128)(2,1)S(1)}) custom-call(bf16[144,3584]{1,0:T(8,128)(2,1)S(1)} %shard_map.151.first_ref, bf16[144,3584]{1,0:T(8,128)(2,1)S(1)} %collective-permute-done.21.second_ref, f32[288,256]{1,0:T(8,128)S(1)} %get-tuple-element.131.back_ref, bf16[3584,256]{1,0:T(8,128)(2,1)S(1)} %bitcast.28, ...), custom_call_target="tpu_custom_call" | custom-call | flops 2113929216 | bytes 8093696 | tf_op jit(solution)/shard_map/pallas_call | solution.py:55
  103.1 4.0 %collective-permute-done.11.refs_2_ = bf16[144,896]{1,0:T(8,128)(2,1)S(1)} collective-permute-done((bf16[144,896]{1,0:T(8,128)(2,1)S(1)}, bf16[144,896]{1,0:T(8,128)(2,1)S(1)}, u32[]{:S(2)}, u32[]{:S(2)}) %collective-permute-start.11) | collective-permute-done | bytes 258080 | tf_op jit(solution)/shard_map/ppermute | solution.py:42
  107.4 2.9 %collective-permute-done.14.first_ref = bf16[144,3584]{1,0:T(8,128)(2,1)S(1)} collective-permute-done((bf16[144,3584]{1,0:T(8,128)(2,1)S(1)}, bf16[144,3584]{1,0:T(8,128)(2,1)S(1)}, u32[]{:S(2)}, u32[]{:S(2)}) %collective-permute-start.14) | collective-permute-done | bytes 1032224 | tf_op jit(solution)/shard_map/ppermute | solution.py:37
  110.3 2.3 %collective-permute-done.20.back_ref = bf16[288,256]{1,0:T(8,128)(2,1)S(1)} collective-permute-done((bf16[288,256]{1,0:T(8,128)(2,1)S(1)}, bf16[288,256]{1,0:T(8,128)(2,1)S(1)}, u32[]{:S(2)}, u32[]{:S(2)}) %collective-permute-start.20) | collective-permute-done | bytes 147488 | tf_op jit(solution)/shard_map/ppermute | solution.py:37
  112.6 1.1 shard_map.155.first_ref
  114.8 20.7 %collective-permute-done.23.middle_ref = bf16[128,3584]{1,0:T(8,128)(2,1)S(1)} collective-permute-done((bf16[128,3584]{1,0:T(8,128)(2,1)S(1)}, bf16[128,3584]{1,0:T(8,128)(2,1)S(1)}, u32[]{:S(2)}, u32[]{:S(2)}) %collective-permute-start.23) | collective-permute-done | bytes 917536 | tf_op jit(solution)/shard_map/ppermute | solution.py:33
  135.5 0.9 copy-done.11
  136.5 1.3 collective-permute-done.25.first_ref
  138.3 2.5 %shard_map.160 = (bf16[144,3584]{1,0:T(8,128)(2,1)S(1)}, bf16[144,3584]{1,0:T(8,128)(2,1)S(1)}) custom-call(bf16[144,3584]{1,0:T(8,128)(2,1)S(1)} %collective-permute-done.14.first_ref, bf16[144,3584]{1,0:T(8,128)(2,1)S(1)} %collective-permute-done.35.second_ref, bf16[288,256]{1,0:T(8,128)(2,1)S(1)} %collective-permute-done.20.back_ref, ...), custom_call_target="tpu_custom_call" | custom-call | flops 2113929216 | bytes 7946240 | tf_op jit(solution)/shard_map/pallas_call | solution.py:55
  140.9 1.3 shard_map.157
  143.5 1.5 collective-permute-start.28
  145.0 1.2 shard_map.156.own_ref
  146.5 0.7 collective-permute-done.28
  147.2 1.3 collective-permute-done.27.other_ref
  148.4 2.7 %shard_map.158 = (bf16[144,3584]{1,0:T(8,128)(2,1)S(1)}, bf16[144,3584]{1,0:T(8,128)(2,1)S(1)}) custom-call(bf16[288,256]{1,0:T(8,128)(2,1)S(1)} %shard_map.156.own_ref, bf16[288,256]{1,0:T(8,128)(2,1)S(1)} %collective-permute-done.27.other_ref, bf16[256,3584]{1,0:T(8,128)(2,1)S(1)} %bitcast.38, bf16[256,3584]{1,0:T(8,128)(2,1)} %collective-permute-done.17.far_ref), custom_call_target="tpu_custom_call" | custom-call | flops 1056964608 | bytes 6029312 | tf_op jit(solution)/shard_map/pallas_call | solution.py:55
  151.3 1.2 add_convert_fusion
  153.0 0.8 collective-permute-done.29.refs_1_
  153.9 1.9 shard_map.159
  156.3 4.1 %collective-permute-start.31 = (bf16[144,896]{1,0:T(8,128)(2,1)}, bf16[144,896]{1,0:T(8,128)(2,1)}, u32[]{:S(2)}, u32[]{:S(2)}) collective-permute-start(bf16[144,896]{1,0:T(8,128)(2,1)} %get-tuple-element.145), channel_id=1, source_target_pairs={{0,28},{1,29},{2,30},{3,31},{4,16},{5,17},{6,18},{7,19},{8,20},{9,... | collective-permute-start | bytes 774152 | tf_op jit(solution)/shard_map/ppermute | solution.py:33
  160.7 1.0 collective-permute-start.33
  161.7 16.3 %collective-permute-done.37.refs_2_ = bf16[144,3584]{1,0:T(8,128)(2,1)S(1)} collective-permute-done((bf16[144,3584]{1,0:T(8,128)(2,1)}, bf16[144,3584]{1,0:T(8,128)(2,1)S(1)}, u32[]{:S(2)}, u32[]{:S(2)}) %collective-permute-start.37) | collective-permute-done | bytes 1032224 | tf_op jit(solution)/shard_map/ppermute | solution.py:37
  177.9 1.2 copy-done.22
  179.1 3.3 %shard_map.161 = (bf16[144,896]{1,0:T(8,128)(2,1)}, bf16[144,896]{1,0:T(8,128)(2,1)}, bf16[144,896]{1,0:T(8,128)(2,1)}, bf16[144,896]{1,0:T(8,128)(2,1)}) custom-call(bf16[144,3584]{1,0:T(8,128)(2,1)S(1)} %copy-done.22, bf16[144,3584]{1,0:T(8,128)(2,1)} %collective-permute-done.34.refs_1_, bf16[144,3584]{1,0:T(8,128)(2,1)S(1)} %collective-permute-done.37.refs_2_), custom_call_target="tpu_custom_call" | custom-call | flops 1056964608 | bytes 4128768 | tf_op jit(solution)/shard_map/pallas_call | solution.py:55
  182.9 4.1 %collective-permute-start.39 = (bf16[144,896]{1,0:T(8,128)(2,1)}, bf16[144,896]{1,0:T(8,128)(2,1)}, u32[]{:S(2)}, u32[]{:S(2)}) collective-permute-start(bf16[144,896]{1,0:T(8,128)(2,1)} %get-tuple-element.157), channel_id=1, source_target_pairs={{0,28},{1,29},{2,30},{3,31},{4,16},{5,17},{6,18},{7,19},{8,20},{9,... | collective-permute-start | bytes 774152 | tf_op jit(solution)/shard_map/ppermute | solution.py:33
  187.1 0.9 collective-permute-start.41
  188.1 3.5 %shard_map.162 = bf16[128,3584]{1,0:T(8,128)(2,1)} custom-call(s32[128,1]{1,0:T(8,128)S(1)} %copy.18.route_ref, f32[128,1]{1,0:T(8,128)S(1)} %copy.19.gate_ref, bf16[128,3584]{1,0:T(8,128)(2,1)S(1)} %copy-done.12, bf16[144,896]{1,0:T(8,128)(2,1)S(1)} %collective-permute-done.30.refs_0_, bf16[144,896]{1,0:T(8,128)(2,1)} %collective-permute-done.31.refs_1_, ...), custom_call_target="tpu_custom_call" | custom-call | flops 1056964608 | bytes 2868224 | tf_op jit(solution)/shard_map/pallas_call | solution.py:55
  191.6 5.6 %collective-permute-done.38.refs_0_ = bf16[144,896]{1,0:T(8,128)(2,1)S(1)} collective-permute-done((bf16[144,896]{1,0:T(8,128)(2,1)}, bf16[144,896]{1,0:T(8,128)(2,1)S(1)}, u32[]{:S(2)}, u32[]{:S(2)}) %collective-permute-start.38) | collective-permute-done | bytes 258080 | tf_op jit(solution)/shard_map/ppermute | solution.py:33
  197.2 12.1 %collective-permute-done.40.refs_2_ = bf16[144,896]{1,0:T(8,128)(2,1)} collective-permute-done((bf16[144,896]{1,0:T(8,128)(2,1)}, bf16[144,896]{1,0:T(8,128)(2,1)}, u32[]{:S(2)}, u32[]{:S(2)}) %collective-permute-start.40) | collective-permute-done | bytes 258080 | tf_op jit(solution)/shard_map/ppermute | solution.py:33
  209.3 4.1 %shard_map.163 = bf16[128,3584]{1,0:T(8,128)(2,1)} custom-call(s32[128,1]{1,0:T(8,128)S(1)} %copy.20.route_ref, f32[1,3584]{1,0:T(1,128)S(1)} %slice.19.gain_ref, bf16[128,3584]{1,0:T(8,128)(2,1)} %collective-permute-done.13.middle_ref, bf16[128,3584]{1,0:T(8,128)(2,1)S(1)} %copy-done.10, bf16[144,896]{1,0:T(8,128)(2,1)S(1)} %collective-permute-done.38.refs_0_, ...), custom_call_target="tpu_custom_call" | custom-call | flops 1056964608 | bytes 3799552 | tf_op jit(solution)/shard_map/pallas_call | solution.py:55
  (117 shorter events, 8.8 us)
Async XLA Ops:
  1.6 19.4 %collective-permute-start = (bf16[128,448]{1,0:T(8,128)(2,1)S(1)}, bf16[128,448]{1,0:T(8,128)(2,1)S(1)}, u32[]{:S(2)}, u32[]{:S(2)}) collective-permute-start(bf16[128,448]{1,0:T(8,128)(2,1)S(1)} %bitcast.43), channel_id=1, source_target_pairs={{0,4},{1,5},{2,6},{3,7},{4,8},{5,9},{6,10},{7,11},{8,12},{9,13},{1... | collective-permute-start | bytes 344072 | tf_op jit(solution)/shard_map/ppermute | solution.py:376
  6.6 14.4 %collective-permute-start.1 = (bf16[128,448]{1,0:T(8,128)(2,1)S(1)}, bf16[128,448]{1,0:T(8,128)(2,1)S(1)}, u32[]{:S(2)}, u32[]{:S(2)}) collective-permute-start(bf16[128,448]{1,0:T(8,128)(2,1)S(1)} %bitcast.44), channel_id=1, source_target_pairs={{0,8},{1,9},{2,10},{3,11},{4,12},{5,13},{6,14},{7,15},{16,24},{17,... | collective-permute-start | bytes 344072 | tf_op jit(solution)/shard_map/ppermute | solution.py:376
  11.1 10.0 %collective-permute-start.2 = (bf16[128,448]{1,0:T(8,128)(2,1)S(1)}, bf16[128,448]{1,0:T(8,128)(2,1)}, u32[]{:S(2)}, u32[]{:S(2)}) collective-permute-start(bf16[128,448]{1,0:T(8,128)(2,1)S(1)} %bitcast.45), channel_id=1, source_target_pairs={{0,12},{1,13},{2,14},{3,15},{16,28},{17,29},{18,30},{19,31}} | collective-permute-start | bytes 344072 | tf_op jit(solution)/shard_map/ppermute | solution.py:376
  17.0 19.9 %copy-start.2 = (bf16[1,1,256,3584]{3,2,1,0:T(8,128)(2,1)S(1)}, bf16[1,1,256,3584]{3,2,1,0:T(8,128)(2,1)}, u32[]{:S(2)}) copy-start(bf16[1,1,256,3584]{3,2,1,0:T(8,128)(2,1)} %param.27) | copy-start | bytes 5505028
  17.0 26.1 %copy-start.4 = (f32[1,3584]{1,0:T(1,128)S(1)}, f32[1,3584]{1,0:T(1,128)}, u32[]{:S(2)}) copy-start(f32[1,3584]{1,0:T(1,128)} %gain_ref.3) | copy-start | bytes 43012
  17.0 26.1 %copy-start.5 = (bf16[1,128,3584]{2,1,0:T(8,128)(2,1)S(1)}, bf16[1,128,3584]{2,1,0:T(8,128)(2,1)}, u32[]{:S(2)}) copy-start(bf16[1,128,3584]{2,1,0:T(8,128)(2,1)} %param.14) | copy-start | bytes 2752516
  21.0 15.9 %copy-start.15 = (bf16[144,896]{1,0:T(8,128)(2,1)}, bf16[144,896]{1,0:T(8,128)(2,1)S(1)}, u32[]{:S(2)}) copy-start(bf16[144,896]{1,0:T(8,128)(2,1)S(1)} %get-tuple-element.121) | copy-start | bytes 774148
  21.0 17.4 %copy-start.17 = (bf16[144,896]{1,0:T(8,128)(2,1)}, bf16[144,896]{1,0:T(8,128)(2,1)S(1)}, u32[]{:S(2)}) copy-start(bf16[144,896]{1,0:T(8,128)(2,1)S(1)} %get-tuple-element.109) | copy-start | bytes 774148
  21.0 17.4 %copy-start.23 = (bf16[144,896]{1,0:T(8,128)(2,1)}, bf16[144,896]{1,0:T(8,128)(2,1)S(1)}, u32[]{:S(2)}) copy-start(bf16[144,896]{1,0:T(8,128)(2,1)S(1)} %get-tuple-element.125.refs_0_) | copy-start | bytes 774148
  21.0 19.0 %copy-start.25 = (bf16[144,896]{1,0:T(8,128)(2,1)}, bf16[144,896]{1,0:T(8,128)(2,1)S(1)}, u32[]{:S(2)}) copy-start(bf16[144,896]{1,0:T(8,128)(2,1)S(1)} %get-tuple-element.115.refs_0_) | copy-start | bytes 774148
  23.6 13.3 %collective-permute-start.3 = (bf16[512,448]{1,0:T(8,128)(2,1)S(1)}, bf16[512,448]{1,0:T(8,128)(2,1)}, u32[]{:S(2)}, u32[]{:S(2)}) collective-permute-start(bf16[512,448]{1,0:T(8,128)(2,1)S(1)} %constant_dynamic-update-slice_fusion.kv0), channel_id=1, source_target_pairs={{0,2},{1,3},{2,0},{3,1},{4,6},{5,7},{6,4},{7,5},{8,10},{9,11},{10,... | collective-permute-start | bytes 1376264 | tf_op jit(solution)/shard_map/ppermute | solution.py:37
  25.2 8.9 %collective-permute-start.6 = (bf16[144,896]{1,0:T(8,128)(2,1)S(1)}, bf16[144,896]{1,0:T(8,128)(2,1)S(1)}, u32[]{:S(2)}, u32[]{:S(2)}) collective-permute-start(bf16[144,896]{1,0:T(8,128)(2,1)S(1)} %get-tuple-element.102), channel_id=1, source_target_pairs={{0,4},{1,5},{2,6},{3,7},{4,8},{5,9},{6,10},{7,11},{8,12},{9,13},{1... | collective-permute-start | bytes 774152 | tf_op jit(solution)/shard_map/ppermute | solution.py:42
  36.9 46.1 %collective-permute-start.17 = (bf16[256,3584]{1,0:T(8,128)(2,1)S(1)}, bf16[256,3584]{1,0:T(8,128)(2,1)}, u32[]{:S(2)}, u32[]{:S(2)}) collective-permute-start(bf16[256,3584]{1,0:T(8,128)(2,1)S(1)} %bitcast.36), channel_id=1, source_target_pairs={{0,2},{1,3},{2,0},{3,1},{4,6},{5,7},{6,4},{7,5},{8,10},{9,11},{10,... | collective-permute-start | bytes 5505032 | tf_op jit(solution)/shard_map/ppermute | solution.py:37
  38.4 3.2 %collective-permute-start.4 = (bf16[512,448]{1,0:T(8,128)(2,1)S(1)}, bf16[512,448]{1,0:T(8,128)(2,1)}, u32[]{:S(2)}, u32[]{:S(2)}) collective-permute-start(bf16[512,448]{1,0:T(8,128)(2,1)S(1)} %constant_dynamic-update-slice_fusion.kv0), channel_id=1, source_target_pairs={{0,1},{1,0},{2,3},{3,2},{4,5},{5,4},{6,7},{7,6},{8,9},{9,8},{10,11... | collective-permute-start | bytes 1376264 | tf_op jit(solution)/shard_map/ppermute | solution.py:37
  38.4 26.2 %collective-permute-start.13 = (bf16[128,3584]{1,0:T(8,128)(2,1)}, bf16[128,3584]{1,0:T(8,128)(2,1)}, u32[]{:S(2)}, u32[]{:S(2)}) collective-permute-start(bf16[128,3584]{1,0:T(8,128)(2,1)} %bitcast.10.middle_ref), channel_id=1, source_target_pairs={{0,16},{1,17},{2,18},{3,19},{4,20},{5,21},{6,22},{7,23},{8,24},{9,... | collective-permute-start | bytes 2752520 | tf_op jit(solution)/shard_map/ppermute | solution.py:33
  40.0 3.0 %collective-permute-start.5 = (bf16[512,448]{1,0:T(8,128)(2,1)}, bf16[512,448]{1,0:T(8,128)(2,1)}, u32[]{:S(2)}, u32[]{:S(2)}) collective-permute-start(bf16[512,448]{1,0:T(8,128)(2,1)} %collective-permute-done.3.kv1), channel_id=1, source_target_pairs={{0,1},{1,0},{2,3},{3,2},{4,5},{5,4},{6,7},{7,6},{8,9},{9,8},{10,11... | collective-permute-start | bytes 1376264 | tf_op jit(solution)/shard_map/ppermute | solution.py:37
  41.6 13.9 %collective-permute-start.7 = (bf16[144,896]{1,0:T(8,128)(2,1)}, bf16[144,896]{1,0:T(8,128)(2,1)}, u32[]{:S(2)}, u32[]{:S(2)}) collective-permute-start(bf16[144,896]{1,0:T(8,128)(2,1)} %get-tuple-element.104), channel_id=1, source_target_pairs={{0,8},{1,9},{2,10},{3,11},{4,12},{5,13},{6,14},{7,15},{8,0},{9,1},... | collective-permute-start | bytes 774152 | tf_op jit(solution)/shard_map/ppermute | solution.py:42
  41.6 14.8 %collective-permute-start.8 = (bf16[144,896]{1,0:T(8,128)(2,1)}, bf16[144,896]{1,0:T(8,128)(2,1)}, u32[]{:S(2)}, u32[]{:S(2)}) collective-permute-start(bf16[144,896]{1,0:T(8,128)(2,1)} %get-tuple-element.106), channel_id=1, source_target_pairs={{0,12},{1,13},{2,14},{3,15},{4,0},{5,1},{6,2},{7,3},{8,4},{9,5},{1... | collective-permute-start | bytes 774152 | tf_op jit(solution)/shard_map/ppermute | solution.py:42
  44.2 8.5 %copy-start.18 = (bf16[144,896]{1,0:T(8,128)(2,1)S(1)}, bf16[144,896]{1,0:T(8,128)(2,1)}, u32[]{:S(2)}) copy-start(bf16[144,896]{1,0:T(8,128)(2,1)} %copy-done.17) | copy-start | bytes 774148
  44.2 11.2 %copy-start.16 = (bf16[144,896]{1,0:T(8,128)(2,1)S(1)}, bf16[144,896]{1,0:T(8,128)(2,1)}, u32[]{:S(2)}) copy-start(bf16[144,896]{1,0:T(8,128)(2,1)} %copy-done.15) | copy-start | bytes 774148
  44.2 12.1 %copy-start.14 = (bf16[144,896]{1,0:T(8,128)(2,1)S(1)}, bf16[144,896]{1,0:T(8,128)(2,1)}, u32[]{:S(2)}) copy-start(bf16[144,896]{1,0:T(8,128)(2,1)} %copy-done.13) | copy-start | bytes 774148
  44.3 20.3 %copy-start.20 = (bf16[144,896]{1,0:T(8,128)(2,1)S(1)}, bf16[144,896]{1,0:T(8,128)(2,1)}, u32[]{:S(2)}) copy-start(bf16[144,896]{1,0:T(8,128)(2,1)} %copy-done.19) | copy-start | bytes 774148
  44.3 20.3 %copy-start.26 = (bf16[144,896]{1,0:T(8,128)(2,1)S(1)}, bf16[144,896]{1,0:T(8,128)(2,1)}, u32[]{:S(2)}) copy-start(bf16[144,896]{1,0:T(8,128)(2,1)} %copy-done.25) | copy-start | bytes 774148
  52.7 30.2 %copy-start.24 = (bf16[144,896]{1,0:T(8,128)(2,1)S(1)}, bf16[144,896]{1,0:T(8,128)(2,1)}, u32[]{:S(2)}) copy-start(bf16[144,896]{1,0:T(8,128)(2,1)} %copy-done.23) | copy-start | bytes 774148
  52.8 14.0 %collective-permute-start.9 = (bf16[144,896]{1,0:T(8,128)(2,1)S(1)}, bf16[144,896]{1,0:T(8,128)(2,1)S(1)}, u32[]{:S(2)}, u32[]{:S(2)}) collective-permute-start(bf16[144,896]{1,0:T(8,128)(2,1)S(1)} %copy-done.18), channel_id=1, source_target_pairs={{0,4},{1,5},{2,6},{3,7},{4,8},{5,9},{6,10},{7,11},{8,12},{9,13},{1... | collective-permute-start | bytes 774152 | tf_op jit(solution)/shard_map/ppermute | solution.py:42
  55.5 22.1 %collective-permute-start.15 = (bf16[144,896]{1,0:T(8,128)(2,1)S(1)}, bf16[144,896]{1,0:T(8,128)(2,1)S(1)}, u32[]{:S(2)}, u32[]{:S(2)}) collective-permute-start(bf16[144,896]{1,0:T(8,128)(2,1)S(1)} %copy-done.16), channel_id=1, source_target_pairs={{0,8},{1,9},{2,10},{3,11},{4,12},{5,13},{6,14},{7,15},{8,0},{9,1},... | collective-permute-start | bytes 774152 | tf_op jit(solution)/shard_map/ppermute | solution.py:42
  56.4 26.6 %collective-permute-start.16 = (bf16[144,896]{1,0:T(8,128)(2,1)S(1)}, bf16[144,896]{1,0:T(8,128)(2,1)S(1)}, u32[]{:S(2)}, u32[]{:S(2)}) collective-permute-start(bf16[144,896]{1,0:T(8,128)(2,1)S(1)} %copy-done.14), channel_id=1, source_target_pairs={{0,12},{1,13},{2,14},{3,15},{4,0},{5,1},{6,2},{7,3},{8,4},{9,5},{1... | collective-permute-start | bytes 774152 | tf_op jit(solution)/shard_map/ppermute | solution.py:42
  66.8 18.4 %copy-start.8 = (bf16[1,128,3584]{2,1,0:T(8,128)(2,1)S(1)}, bf16[1,128,3584]{2,1,0:T(8,128)(2,1)}, u32[]{:S(2)}) copy-start(bf16[1,128,3584]{2,1,0:T(8,128)(2,1)} %param.21) | copy-start | bytes 2752516
  84.1 11.1 %collective-permute-start.19 = (bf16[144,3584]{1,0:T(8,128)(2,1)S(1)}, bf16[144,3584]{1,0:T(8,128)(2,1)S(1)}, u32[]{:S(2)}, u32[]{:S(2)}) collective-permute-start(bf16[144,3584]{1,0:T(8,128)(2,1)S(1)} %shard_map.152.first_ref), channel_id=1, source_target_pairs={{0,1},{1,0},{2,3},{3,2},{4,5},{5,4},{6,7},{7,6},{8,9},{9,8},{10,11... | collective-permute-start | bytes 3096584 | tf_op jit(solution)/shard_map/ppermute | solution.py:37
  84.2 14.9 %collective-permute-start.21 = (bf16[144,3584]{1,0:T(8,128)(2,1)S(1)}, bf16[144,3584]{1,0:T(8,128)(2,1)S(1)}, u32[]{:S(2)}, u32[]{:S(2)}) collective-permute-start(bf16[144,3584]{1,0:T(8,128)(2,1)S(1)} %shard_map.151.first_ref), channel_id=1, source_target_pairs={{0,1},{1,0},{2,3},{3,2},{4,5},{5,4},{6,7},{7,6},{8,9},{9,8},{10,11... | collective-permute-start | bytes 3096584 | tf_op jit(solution)/shard_map/ppermute | solution.py:37
  84.6 25.7 %collective-permute-start.14 = (bf16[144,3584]{1,0:T(8,128)(2,1)S(1)}, bf16[144,3584]{1,0:T(8,128)(2,1)S(1)}, u32[]{:S(2)}, u32[]{:S(2)}) collective-permute-start(bf16[144,3584]{1,0:T(8,128)(2,1)S(1)} %shard_map.151.first_ref), channel_id=1, source_target_pairs={{0,2},{1,3},{2,0},{3,1},{4,6},{5,7},{6,4},{7,5},{8,10},{9,11},{10,... | collective-permute-start | bytes 3096584 | tf_op jit(solution)/shard_map/ppermute | solution.py:37
  85.2 25.1 %collective-permute-start.18 = (bf16[128,3584]{1,0:T(8,128)(2,1)S(1)}, bf16[128,3584]{1,0:T(8,128)(2,1)S(1)}, u32[]{:S(2)}, u32[]{:S(2)}) collective-permute-start(bf16[128,3584]{1,0:T(8,128)(2,1)S(1)} %bitcast.42), channel_id=1, source_target_pairs={{0,16},{1,17},{2,18},{3,19},{4,20},{5,21},{6,22},{7,23},{8,24},{9,... | collective-permute-start | bytes 2752520 | tf_op jit(solution)/shard_map/ppermute | solution.py:33
  85.7 15.0 %copy-start = (bf16[1,1,3584,256]{3,2,1,0:T(8,128)(2,1)S(1)}, bf16[1,1,3584,256]{3,2,1,0:T(8,128)(2,1)}, u32[]{:S(2)}) copy-start(bf16[1,1,3584,256]{3,2,1,0:T(8,128)(2,1)} %param.25) | copy-start | bytes 5505028
  85.7 15.0 %copy-start.1 = (bf16[1,1,3584,256]{3,2,1,0:T(8,128)(2,1)S(1)}, bf16[1,1,3584,256]{3,2,1,0:T(8,128)(2,1)}, u32[]{:S(2)}) copy-start(bf16[1,1,3584,256]{3,2,1,0:T(8,128)(2,1)} %param.26) | copy-start | bytes 5505028
  85.7 9.4 %collective-permute-start.10 = (bf16[144,896]{1,0:T(8,128)(2,1)S(1)}, bf16[144,896]{1,0:T(8,128)(2,1)S(1)}, u32[]{:S(2)}, u32[]{:S(2)}) collective-permute-start(bf16[144,896]{1,0:T(8,128)(2,1)S(1)} %get-tuple-element.111), channel_id=1, source_target_pairs={{0,4},{1,5},{2,6},{3,7},{4,8},{5,9},{6,10},{7,11},{8,12},{9,13},{1... | collective-permute-start | bytes 774152 | tf_op jit(solution)/shard_map/ppermute | solution.py:42
  95.1 12.0 %collective-permute-start.11 = (bf16[144,896]{1,0:T(8,128)(2,1)S(1)}, bf16[144,896]{1,0:T(8,128)(2,1)S(1)}, u32[]{:S(2)}, u32[]{:S(2)}) collective-permute-start(bf16[144,896]{1,0:T(8,128)(2,1)S(1)} %get-tuple-element.112), channel_id=1, source_target_pairs={{0,8},{1,9},{2,10},{3,11},{4,12},{5,13},{6,14},{7,15},{8,0},{9,1},... | collective-permute-start | bytes 774152 | tf_op jit(solution)/shard_map/ppermute | solution.py:42
  95.1 12.3 %collective-permute-start.12 = (bf16[144,896]{1,0:T(8,128)(2,1)S(1)}, bf16[144,896]{1,0:T(8,128)(2,1)S(1)}, u32[]{:S(2)}, u32[]{:S(2)}) collective-permute-start(bf16[144,896]{1,0:T(8,128)(2,1)S(1)} %get-tuple-element.113), channel_id=1, source_target_pairs={{0,12},{1,13},{2,14},{3,15},{4,0},{5,1},{6,2},{7,3},{8,4},{9,5},{1... | collective-permute-start | bytes 774152 | tf_op jit(solution)/shard_map/ppermute | solution.py:42
  99.1 13.5 %collective-permute-start.20 = (bf16[288,256]{1,0:T(8,128)(2,1)S(1)}, bf16[288,256]{1,0:T(8,128)(2,1)S(1)}, u32[]{:S(2)}, u32[]{:S(2)}) collective-permute-start(bf16[288,256]{1,0:T(8,128)(2,1)S(1)} %get-tuple-element.130), channel_id=1, source_target_pairs={{0,2},{1,3},{2,0},{3,1},{4,6},{5,7},{6,4},{7,5},{8,10},{9,11},{10,... | collective-permute-start | bytes 442376 | tf_op jit(solution)/shard_map/ppermute | solution.py:37
  103.1 10.6 %copy-start.21 = (bf16[144,3584]{1,0:T(8,128)(2,1)}, bf16[144,3584]{1,0:T(8,128)(2,1)S(1)}, u32[]{:S(2)}) copy-start(bf16[144,3584]{1,0:T(8,128)(2,1)S(1)} %get-tuple-element.153.refs_0_) | copy-start | bytes 3096580
  110.3 3.4 %copy-start.9 = (bf16[128,3584]{1,0:T(8,128)(2,1)}, bf16[128,3584]{1,0:T(8,128)(2,1)S(1)}, u32[]{:S(2)}) copy-start(bf16[128,3584]{1,0:T(8,128)(2,1)S(1)} %collective-permute-done.18.grad_ref) | copy-start | bytes 2752516
  113.7 27.1 %copy-start.30 = (s32[1,128,1]{1,2,0:T(1,128)S(1)}, s32[1,128,1]{1,2,0:T(1,128)}, u32[]{:S(2)}) copy-start(s32[1,128,1]{1,2,0:T(1,128)} %param.18) | copy-start | bytes 1540
  113.7 27.1 %copy-start.28 = (f32[1,128]{1,0:T(1,128)S(1)}, f32[1,128]{1,0:T(1,128)}, u32[]{:S(2)}) copy-start(f32[1,128]{1,0:T(1,128)} %get-tuple-element.168) | copy-start | bytes 1540
  113.7 24.0 %collective-permute-start.25 = (bf16[144,3584]{1,0:T(8,128)(2,1)S(1)}, bf16[144,3584]{1,0:T(8,128)(2,1)S(1)}, u32[]{:S(2)}, u32[]{:S(2)}) collective-permute-start(bf16[144,3584]{1,0:T(8,128)(2,1)S(1)} %shard_map.155.first_ref), channel_id=1, source_target_pairs={{0,2},{1,3},{2,0},{3,1},{4,6},{5,7},{6,4},{7,5},{8,10},{9,11},{10,... | collective-permute-start | bytes 3096584 | tf_op jit(solution)/shard_map/ppermute | solution.py:37
  114.3 21.2 %collective-permute-start.23 = (bf16[128,3584]{1,0:T(8,128)(2,1)S(1)}, bf16[128,3584]{1,0:T(8,128)(2,1)S(1)}, u32[]{:S(2)}, u32[]{:S(2)}) collective-permute-start(bf16[128,3584]{1,0:T(8,128)(2,1)S(1)} %get-tuple-element.138), channel_id=1, source_target_pairs={{0,16},{1,17},{2,18},{3,19},{4,20},{5,21},{6,22},{7,23},{8,24},{9,... | collective-permute-start | bytes 2752520 | tf_op jit(solution)/shard_map/ppermute | solution.py:33
  114.8 23.4 %collective-permute-start.35 = (bf16[144,3584]{1,0:T(8,128)(2,1)S(1)}, bf16[144,3584]{1,0:T(8,128)(2,1)S(1)}, u32[]{:S(2)}, u32[]{:S(2)}) collective-permute-start(bf16[144,3584]{1,0:T(8,128)(2,1)S(1)} %collective-permute-done.14.first_ref), channel_id=1, source_target_pairs={{0,1},{1,0},{2,3},{3,2},{4,5},{5,4},{6,7},{7,6},{8,9},{9,8},{10,11... | collective-permute-start | bytes 3096584 | tf_op jit(solution)/shard_map/ppermute | solution.py:37
  137.7 3.1 %collective-permute-start.26 = (bf16[144,3584]{1,0:T(8,128)(2,1)S(1)}, bf16[144,3584]{1,0:T(8,128)(2,1)S(1)}, u32[]{:S(2)}, u32[]{:S(2)}) collective-permute-start(bf16[144,3584]{1,0:T(8,128)(2,1)S(1)} %collective-permute-done.25.first_ref), channel_id=1, source_target_pairs={{0,1},{1,0},{2,3},{3,2},{4,5},{5,4},{6,7},{7,6},{8,9},{9,8},{10,11... | collective-permute-start | bytes 3096584 | tf_op jit(solution)/shard_map/ppermute | solution.py:37
  137.7 5.7 %collective-permute-start.24 = (bf16[144,3584]{1,0:T(8,128)(2,1)S(1)}, bf16[144,3584]{1,0:T(8,128)(2,1)S(1)}, u32[]{:S(2)}, u32[]{:S(2)}) collective-permute-start(bf16[144,3584]{1,0:T(8,128)(2,1)S(1)} %shard_map.155.first_ref), channel_id=1, source_target_pairs={{0,1},{1,0},{2,3},{3,2},{4,5},{5,4},{6,7},{7,6},{8,9},{9,8},{10,11... | collective-permute-start | bytes 3096584 | tf_op jit(solution)/shard_map/ppermute | solution.py:37
  140.7 10.5 %collective-permute-start.36 = (bf16[144,3584]{1,0:T(8,128)(2,1)S(1)}, bf16[144,3584]{1,0:T(8,128)(2,1)S(1)}, u32[]{:S(2)}, u32[]{:S(2)}) collective-permute-start(bf16[144,3584]{1,0:T(8,128)(2,1)S(1)} %get-tuple-element.151), channel_id=1, source_target_pairs={{0,1},{1,0},{2,3},{3,2},{4,5},{5,4},{6,7},{7,6},{8,9},{9,8},{10,11... | collective-permute-start | bytes 3096584 | tf_op jit(solution)/shard_map/ppermute | solution.py:37
  142.1 6.3 %collective-permute-start.27 = (bf16[288,256]{1,0:T(8,128)(2,1)S(1)}, bf16[288,256]{1,0:T(8,128)(2,1)S(1)}, u32[]{:S(2)}, u32[]{:S(2)}) collective-permute-start(bf16[288,256]{1,0:T(8,128)(2,1)S(1)} %shard_map.157), channel_id=1, source_target_pairs={{0,2},{1,3},{2,0},{3,1},{4,6},{5,7},{6,4},{7,5},{8,10},{9,11},{10,... | collective-permute-start | bytes 442376 | tf_op jit(solution)/shard_map/ppermute | solution.py:37
  142.7 17.9 %collective-permute-start.34 = (bf16[144,3584]{1,0:T(8,128)(2,1)S(1)}, bf16[144,3584]{1,0:T(8,128)(2,1)}, u32[]{:S(2)}, u32[]{:S(2)}) collective-permute-start(bf16[144,3584]{1,0:T(8,128)(2,1)S(1)} %get-tuple-element.148), channel_id=1, source_target_pairs={{0,1},{1,0},{2,3},{3,2},{4,5},{5,4},{6,7},{7,6},{8,9},{9,8},{10,11... | collective-permute-start | bytes 3096584 | tf_op jit(solution)/shard_map/ppermute | solution.py:37
  143.0 3.6 %collective-permute-start.22 = (f32[1,256]{1,0:T(1,128)S(1)}, f32[1,256]{1,0:T(1,128)S(1)}, u32[]{:S(2)}, u32[]{:S(2)}) collective-permute-start(f32[1,256]{1,0:T(1,128)S(1)} %maximum_bitcast_fusion), channel_id=1, source_target_pairs={{0,16},{1,17},{2,18},{3,19},{4,20},{5,21},{6,22},{7,23},{8,24},{9,... | collective-permute-start | bytes 3080 | tf_op jit(solution)/shard_map/ppermute | solution.py:33
  143.5 3.7 %collective-permute-start.28 = (f32[1,3712]{1,0:T(1,128)S(1)}, f32[1,3712]{1,0:T(1,128)S(1)}, u32[]{:S(2)}, u32[]{:S(2)}) collective-permute-start(f32[1,3712]{1,0:T(1,128)S(1)} %pad_maximum_fusion), channel_id=1, source_target_pairs={{0,16},{1,17},{2,18},{3,19},{4,20},{5,21},{6,22},{7,23},{8,24},{9,... | collective-permute-start | bytes 44552 | tf_op jit(solution)/shard_map/ppermute | solution.py:33
  151.2 2.7 %collective-permute-start.29 = (bf16[144,3584]{1,0:T(8,128)(2,1)S(1)}, bf16[144,3584]{1,0:T(8,128)(2,1)S(1)}, u32[]{:S(2)}, u32[]{:S(2)}) collective-permute-start(bf16[144,3584]{1,0:T(8,128)(2,1)S(1)} %get-tuple-element.143), channel_id=1, source_target_pairs={{0,1},{1,0},{2,3},{3,2},{4,5},{5,4},{6,7},{7,6},{8,9},{9,8},{10,11... | collective-permute-start | bytes 3096584 | tf_op jit(solution)/shard_map/ppermute | solution.py:37
  152.5 25.4 %collective-permute-start.37 = (bf16[144,3584]{1,0:T(8,128)(2,1)}, bf16[144,3584]{1,0:T(8,128)(2,1)S(1)}, u32[]{:S(2)}, u32[]{:S(2)}) collective-permute-start(bf16[144,3584]{1,0:T(8,128)(2,1)} %add_convert_fusion), channel_id=1, source_target_pairs={{0,2},{1,3},{2,0},{3,1},{4,6},{5,7},{6,4},{7,5},{8,10},{9,11},{10,... | collective-permute-start | bytes 3096584 | tf_op jit(solution)/shard_map/ppermute | solution.py:37
  155.8 27.1 %collective-permute-start.30 = (bf16[144,896]{1,0:T(8,128)(2,1)}, bf16[144,896]{1,0:T(8,128)(2,1)S(1)}, u32[]{:S(2)}, u32[]{:S(2)}) collective-permute-start(bf16[144,896]{1,0:T(8,128)(2,1)} %get-tuple-element.144), channel_id=1, source_target_pairs={{0,16},{1,17},{2,18},{3,19},{4,20},{5,21},{6,22},{7,23},{8,24},{9,... | collective-permute-start | bytes 774152 | tf_op jit(solution)/shard_map/ppermute | solution.py:33
  156.3 30.8 %collective-permute-start.31 = (bf16[144,896]{1,0:T(8,128)(2,1)}, bf16[144,896]{1,0:T(8,128)(2,1)}, u32[]{:S(2)}, u32[]{:S(2)}) collective-permute-start(bf16[144,896]{1,0:T(8,128)(2,1)} %get-tuple-element.145), channel_id=1, source_target_pairs={{0,28},{1,29},{2,30},{3,31},{4,16},{5,17},{6,18},{7,19},{8,20},{9,... | collective-permute-start | bytes 774152 | tf_op jit(solution)/shard_map/ppermute | solution.py:33
  160.4 26.6 %collective-permute-start.32 = (bf16[144,896]{1,0:T(8,128)(2,1)}, bf16[144,896]{1,0:T(8,128)(2,1)}, u32[]{:S(2)}, u32[]{:S(2)}) collective-permute-start(bf16[144,896]{1,0:T(8,128)(2,1)} %get-tuple-element.146), channel_id=1, source_target_pairs={{0,24},{1,25},{2,26},{3,27},{4,28},{5,29},{6,30},{7,31},{8,16},{9,... | collective-permute-start | bytes 774152 | tf_op jit(solution)/shard_map/ppermute | solution.py:33
  160.7 27.4 %copy-start.12 = (bf16[128,3584]{1,0:T(8,128)(2,1)S(1)}, bf16[128,3584]{1,0:T(8,128)(2,1)}, u32[]{:S(2)}) copy-start(bf16[128,3584]{1,0:T(8,128)(2,1)} %copy-done.11) | copy-start | bytes 2752516
  160.7 27.4 %collective-permute-start.33 = (bf16[144,896]{1,0:T(8,128)(2,1)S(1)}, bf16[144,896]{1,0:T(8,128)(2,1)}, u32[]{:S(2)}, u32[]{:S(2)}) collective-permute-start(bf16[144,896]{1,0:T(8,128)(2,1)S(1)} %get-tuple-element.147), channel_id=1, source_target_pairs={{0,20},{1,21},{2,22},{3,23},{4,24},{5,25},{6,26},{7,27},{8,28},{9,... | collective-permute-start | bytes 774152 | tf_op jit(solution)/shard_map/ppermute | solution.py:33
  182.4 14.8 %collective-permute-start.38 = (bf16[144,896]{1,0:T(8,128)(2,1)}, bf16[144,896]{1,0:T(8,128)(2,1)S(1)}, u32[]{:S(2)}, u32[]{:S(2)}) collective-permute-start(bf16[144,896]{1,0:T(8,128)(2,1)} %get-tuple-element.156), channel_id=1, source_target_pairs={{0,16},{1,17},{2,18},{3,19},{4,20},{5,21},{6,22},{7,23},{8,24},{9,... | collective-permute-start | bytes 774152 | tf_op jit(solution)/shard_map/ppermute | solution.py:33
  182.9 14.3 %collective-permute-start.39 = (bf16[144,896]{1,0:T(8,128)(2,1)}, bf16[144,896]{1,0:T(8,128)(2,1)}, u32[]{:S(2)}, u32[]{:S(2)}) collective-permute-start(bf16[144,896]{1,0:T(8,128)(2,1)} %get-tuple-element.157), channel_id=1, source_target_pairs={{0,28},{1,29},{2,30},{3,31},{4,16},{5,17},{6,18},{7,19},{8,20},{9,... | collective-permute-start | bytes 774152 | tf_op jit(solution)/shard_map/ppermute | solution.py:33
  187.1 22.2 %collective-permute-start.40 = (bf16[144,896]{1,0:T(8,128)(2,1)}, bf16[144,896]{1,0:T(8,128)(2,1)}, u32[]{:S(2)}, u32[]{:S(2)}) collective-permute-start(bf16[144,896]{1,0:T(8,128)(2,1)} %get-tuple-element.158), channel_id=1, source_target_pairs={{0,24},{1,25},{2,26},{3,27},{4,28},{5,29},{6,30},{7,31},{8,16},{9,... | collective-permute-start | bytes 774152 | tf_op jit(solution)/shard_map/ppermute | solution.py:33
  187.1 22.2 %collective-permute-start.41 = (bf16[144,896]{1,0:T(8,128)(2,1)}, bf16[144,896]{1,0:T(8,128)(2,1)}, u32[]{:S(2)}, u32[]{:S(2)}) collective-permute-start(bf16[144,896]{1,0:T(8,128)(2,1)} %get-tuple-element.159), channel_id=1, source_target_pairs={{0,20},{1,21},{2,22},{3,23},{4,24},{5,25},{6,26},{7,27},{8,28},{9,... | collective-permute-start | bytes 774152 | tf_op jit(solution)/shard_map/ppermute | solution.py:33
  188.1 21.2 %copy-start.10 = (bf16[128,3584]{1,0:T(8,128)(2,1)S(1)}, bf16[128,3584]{1,0:T(8,128)(2,1)}, u32[]{:S(2)}) copy-start(bf16[128,3584]{1,0:T(8,128)(2,1)} %copy-done.9) | copy-start | bytes 2752516
  (9 other events, 9.2 us)

commit v11 on v10

--- a/solution.py
+++ b/solution.py
@@ -44,7 +44,7 @@
     )
 
 
-def call(body, outs, args, scratch=(), flops=0, smem=0, vmem=VMEM_BYTES):
+def call(body, outs, args, scratch=(), flops=0, smem=0, vmem=VMEM_BYTES, cheap=False):
     specs = [
         pl.BlockSpec(memory_space=pltpu.SMEM if i < smem else pltpu.VMEM)
         for i in range(len(args))
@@ -60,7 +60,9 @@
         scratch_shapes=list(scratch),
         compiler_params=pltpu.CompilerParams(vmem_limit_bytes=vmem),
         cost_estimate=pl.CostEstimate(
-            flops=int(flops), bytes_accessed=int(moved_bytes), transcendentals=0
+            flops=1 if cheap else int(flops),
+            bytes_accessed=1 if cheap else int(moved_bytes),
+            transcendentals=0,
         ),
     )(*args)
     return list(result) if many else result[0]
@@ -408,7 +410,7 @@
             functools.partial(split_body, capacity, len(parts)),
             [chunk] * experts,
             parts,
-            flops=pack_flops,
+            cheap=True,
         )
 
     def sent_back(chunks, by):
@@ -462,7 +464,7 @@
         grad_chunks[k] = turned(after([grad_chunks[k]], [middle])[0], k)
     front_chunks = sent(after(front_chunks, row_chunks + grad_chunks[1:2]))
     back_rows = joined(after(row_chunks, [middle, there_back_middle]))
-    back_pieces = pieces_of(back_rows)
+    back_other = swapped(back_rows, 2)
     grad_near = joined(after(grad_chunks, [back_rows, down_other]))
     there_back_grad = passed_along(after([back_grad[0]], [grad_near])[0], -1)
     grad_near = [grad_near, swapped(grad_near, 1)]
@@ -473,11 +475,15 @@
         flops=2 * work,
     )
     far_back = swapped(other_back, 2)
-    back_near = backward(back_pieces[:2], down_back)
+    back_near = backward((back_rows, swapped(back_rows, 1)), down_back)
     back_core = swapped(back_near[1], 1)
-    front_near = joined(after(front_chunks, [back_pieces[2], there_back_grad, far_back, back_near[0]]))
+    ready = [back_other, there_back_grad, far_back, back_near[0]]
+    front_near = joined(after(front_chunks, ready))
     there_middle = passed_along(after([middle], [front_near])[0], 1)
-    front_other = after([swapped(front_near, 2)], [there_middle])[0]
+    (far_back,) = after([far_back], [there_middle])
+    back_far = backward((back_other, swapped(after([back_other], [front_near])[0], 1)), far_back)
+    chip = (back_far[0].astype(f32) + swapped(back_far[1], 1).astype(f32)).astype(bf16)
+    front_other = after([swapped(front_near, 2)], back_far[:1])[0]
 
     front_small, back_small = after([front_small, back_small], [front_near])
     there_small = passed_along(front_small, 1)
@@ -490,14 +496,11 @@
     hidden_near = hidden(front_pieces[:2])
     hidden_far = hidden(front_pieces[2:])
     hidden_other = swapped(hidden_far, 2)
-    (hidden_other,) = after([hidden_other], [there_small, there_back_small])
+    (hidden_other,) = after([hidden_other], [there_small, there_back_small, chip])
     front_own, front_core = call(
-        output_body, [piece, piece], (hidden_near, hidden_other, *downs), flops=2 * work
-    )
-    (far_back,) = after([far_back], [front_other])
-    back_far = backward(back_pieces[2:], far_back)
-    chip = back_far[0].astype(f32) + swapped(back_far[1], 1).astype(f32)
-    (chip,) = after([chip.astype(bf16)], [hidden_other])
+        output_body, [piece, piece], (hidden_near, hidden_other, *downs), cheap=True
+    )
+    (chip,) = after([chip], [hidden_far])
     back_shares = (back_near[0], back_core, swapped(chip, 2))
 
     front_shares = (front_own, swapped(front_core, 1))

time: 214 us -> 209 us (0.977)
  waiting for transfers between devices: 106 us -> 91.5 us
  starting transfers between devices: 48.6 us -> 62.6 us
    ppermute x9, starting transfers between devices: 13 us -> 22 us  [turned(): lax.ppermute(array, 'expert', [(i, (i + by * GROUP) % length) for i in ra...]
    ppermute x9, waiting for transfers between devices: 40.2 us -> 31.8 us  [turned(): lax.ppermute(array, 'expert', [(i, (i + by * GROUP) % length) for i in ra...]
    ppermute x13, starting transfers between devices: 15.7 us -> 21 us  [passed_along(): return lax.ppermute(array, ('section', 'expert'), pairs)]
    ppermute x17, waiting for transfers between devices: 26.9 us -> 23.2 us  [swapped(): lax.ppermute(array, 'expert', [(i, i ^ bit) for i in range(lax.axis_size(...]
    ppermute x13, waiting for transfers between devices: 39.4 us -> 36.5 us  [passed_along(): return lax.ppermute(array, ('section', 'expert'), pairs)]
    unnamed x66 -> x58, local copies, waits for them, and re-layouts: 9.36 us -> 8.93 us
  transfers between devices with their start and end apart: 42 -> 42, of which waited for: 19 -> 15; matrix products, arithmetic and copies ran while one was open for 2% -> 2% of each run, Pallas kernels for 17% -> 15%
where the time goes in v11:
time: 209 us; the launch traced here: 208 us
  waiting for transfers between devices  91.5 us (44%)
  starting transfers between devices  62.6 us (30%)
  Pallas kernels  41 us (20%)
  local copies, waits for them, and re-layouts  10.1 us (5%)
    pallas_call x15, Pallas kernels, call(): pl.pallas_call(body, out_shape=shapes, in_specs=specs, out_specs=[pl.Bloc...  41 us
    ppermute x13, waiting for transfers between devices, passed_along(): return lax.ppermute(array, ('section', 'expert'), pairs)  36.5 us
    ppermute x9, waiting for transfers between devices, turned(): lax.ppermute(array, 'expert', [(i, (i + by * GROUP) % length) for i in ra...  31.8 us
    ppermute x17, waiting for transfers between devices, swapped(): lax.ppermute(array, 'expert', [(i, i ^ bit) for i in range(lax.axis_size(...  23.2 us
    ppermute x9, starting transfers between devices, turned(): lax.ppermute(array, 'expert', [(i, (i + by * GROUP) % length) for i in ra...  22 us
    ppermute x13, starting transfers between devices, passed_along(): return lax.ppermute(array, ('section', 'expert'), pairs)  21 us
    ppermute x3, starting transfers between devices, shards(): column.append(lax.ppermute(keys_values[0], 'expert', pairs))  10.7 us
    unnamed x58, local copies, waits for them, and re-layouts  8.93 us
  transfers between devices with their start and end apart: 42, of which 15 were waited for; matrix products, arithmetic and copies ran while one was open for 2% of the time, Pallas kernels for 15%

profile of v11, /device:TPU:0, one launch (start us, length us, event | category | flops | bytes accessed | tf_op | source)
XLA Modules:
  0.0 208.3 jit_solution(16100847639014954007)
XLA Ops:
  0.6 1.0 copy.16
  1.6 4.9 %collective-permute-start = (bf16[128,448]{1,0:T(8,128)(2,1)S(1)}, bf16[128,448]{1,0:T(8,128)(2,1)S(1)}, u32[]{:S(2)}, u32[]{:S(2)}) collective-permute-start(bf16[128,448]{1,0:T(8,128)(2,1)S(1)} %bitcast.43), channel_id=1, source_target_pairs={{0,4},{1,5},{2,6},{3,7},{4,8},{5,9},{6,10},{7,11},{8,12},{9,13},{1... | collective-permute-start | bytes 344072 | tf_op jit(solution)/shard_map/ppermute | solution.py:378
  6.6 4.5 %collective-permute-start.1 = (bf16[128,448]{1,0:T(8,128)(2,1)S(1)}, bf16[128,448]{1,0:T(8,128)(2,1)S(1)}, u32[]{:S(2)}, u32[]{:S(2)}) collective-permute-start(bf16[128,448]{1,0:T(8,128)(2,1)S(1)} %bitcast.44), channel_id=1, source_target_pairs={{0,8},{1,9},{2,10},{3,11},{4,12},{5,13},{6,14},{7,15},{16,24},{17,... | collective-permute-start | bytes 344072 | tf_op jit(solution)/shard_map/ppermute | solution.py:378
  11.1 1.3 collective-permute-start.2
  12.4 0.8 copy.17.gate_ref
  13.8 0.7 copy-done.3
  14.6 1.2 copy-done.7
  15.7 3.0 %shard_map.149 = (bf16[144,896]{1,0:T(8,128)(2,1)S(1)}, bf16[144,896]{1,0:T(8,128)(2,1)S(1)}, bf16[144,896]{1,0:T(8,128)(2,1)S(1)}, bf16[144,896]{1,0:T(8,128)(2...) custom-call(s32[1,128]{1,0:T(1,128)S(1)} %get-tuple-element.171.rout, ...), custom_call_target="tpu_custom_call" | custom-call | flops 2113929216 | bytes 3914752 | tf_op jit(solution)/shard_map/pallas_call | solution.py:55
  18.8 0.7 copy-done.13
  19.6 1.6 collective-permute-start.3
  21.2 8.9 %collective-permute-done.6.refs_1_ = bf16[144,896]{1,0:T(8,128)(2,1)S(1)} collective-permute-done((bf16[144,896]{1,0:T(8,128)(2,1)S(1)}, bf16[144,896]{1,0:T(8,128)(2,1)S(1)}, u32[]{:S(2)}, u32[]{:S(2)}) %collective-permute-start.6) | collective-permute-done | bytes 258080 | tf_op jit(solution)/shard_map/ppermute | solution.py:42
  30.1 0.7 copy-done.18
  30.8 2.0 collective-permute-done.3.kv1
  32.8 1.5 collective-permute-start.17
  34.3 1.5 collective-permute-start.13
  36.2 2.8 %collective-permute-start.8 = (bf16[144,896]{1,0:T(8,128)(2,1)}, bf16[144,896]{1,0:T(8,128)(2,1)}, u32[]{:S(2)}, u32[]{:S(2)}) collective-permute-start(bf16[144,896]{1,0:T(8,128)(2,1)} %copy-done.17), channel_id=1, source_target_pairs={{0,12},{1,13},{2,14},{3,15},{4,0},{5,1},{6,2},{7,3},{8,4},{9,5},{1... | collective-permute-start | bytes 774152 | tf_op jit(solution)/shard_map/ppermute | solution.py:42
  39.1 1.2 copy-done.5
  40.3 1.2 copy-done.6
  41.5 8.3 %shard_map.150 = (bf16[128,3584]{1,0:T(8,128)(2,1)S(1)}, bf16[144,896]{1,0:T(8,128)(2,1)S(1)}, bf16[144,896]{1,0:T(8,128)(2,1)S(1)}, bf16[144,896]{1,0:T(8,128)(2,1)S(1)}, bf16[144,896]{1,0:T(8,128)(2,1)S(1)}) custom-call(s32[16]{0:T(128)S(1)} %reshape_squeeze.6.chosen_ref, s32[16]{0:T(128)S(1)} %fusion.10.index_ref, s32[1]{0:T(128)} %bitcast.4.base_ref, ...), custom_call_target="tpu_custom_call" | custom-call | flops 1593835520 | bytes 5634692 | tf_op jit(solution)/shard_map/pallas_call | solution.py:55
  49.8 1.7 collective-permute-start.16
  51.5 1.4 collective-permute-start.15
  52.9 3.1 %collective-permute-done.7.refs_2_ = bf16[144,896]{1,0:T(8,128)(2,1)} collective-permute-done((bf16[144,896]{1,0:T(8,128)(2,1)S(1)}, bf16[144,896]{1,0:T(8,128)(2,1)}, u32[]{:S(2)}, u32[]{:S(2)}) %collective-permute-start.7) | collective-permute-done | bytes 258080 | tf_op jit(solution)/shard_map/ppermute | solution.py:42
  56.0 12.4 %collective-permute-start.9 = (bf16[144,896]{1,0:T(8,128)(2,1)S(1)}, bf16[144,896]{1,0:T(8,128)(2,1)S(1)}, u32[]{:S(2)}, u32[]{:S(2)}) collective-permute-start(bf16[144,896]{1,0:T(8,128)(2,1)S(1)} %get-tuple-element.110), channel_id=1, source_target_pairs={{0,4},{1,5},{2,6},{3,7},{4,8},{5,9},{6,10},{7,11},{8,12},{9,13},{1... | collective-permute-start | bytes 774152 | tf_op jit(solution)/shard_map/ppermute | solution.py:42
  68.4 2.2 %shard_map.151.first_ref = bf16[144,3584]{1,0:T(8,128)(2,1)S(1)} custom-call(bf16[144,896]{1,0:T(8,128)(2,1)S(1)} %copy-done.23, bf16[144,896]{1,0:T(8,128)(2,1)S(1)} %copy-done.19, bf16[144,896]{1,0:T(8,128)(2,1)} %collective-permute-done.7.refs_2_, bf16[144,896]{1,0:T(8,128)(2,1)} %collective-permute-done.8.refs_3_), custom_call_target="tpu_custom_call" | custom-call | flops 1056964608 | bytes 2064384 | tf_op jit(solution)/shard_map/pallas_call | solution.py:55
  70.6 6.8 %collective-permute-done.15.refs_2_ = bf16[144,896]{1,0:T(8,128)(2,1)S(1)} collective-permute-done((bf16[144,896]{1,0:T(8,128)(2,1)S(1)}, bf16[144,896]{1,0:T(8,128)(2,1)S(1)}, u32[]{:S(2)}, u32[]{:S(2)}) %collective-permute-start.15) | collective-permute-done | bytes 258080 | tf_op jit(solution)/shard_map/ppermute | solution.py:42
  77.3 1.1 shard_map.152.first_ref
  79.6 0.9 collective-permute-start.18
  80.5 2.0 collective-permute-start.10
  82.4 8.7 %collective-permute-done.10.refs_1_ = bf16[144,896]{1,0:T(8,128)(2,1)S(1)} collective-permute-done((bf16[144,896]{1,0:T(8,128)(2,1)S(1)}, bf16[144,896]{1,0:T(8,128)(2,1)S(1)}, u32[]{:S(2)}, u32[]{:S(2)}) %collective-permute-start.10) | collective-permute-done | bytes 258080 | tf_op jit(solution)/shard_map/ppermute | solution.py:42
  91.1 0.9 collective-permute-start.11
  92.0 0.9 collective-permute-start.12
  92.8 2.8 %shard_map.153 = (f32[288,256]{1,0:T(8,128)S(1)}, bf16[288,256]{1,0:T(8,128)(2,1)S(1)}) custom-call(bf16[144,3584]{1,0:T(8,128)(2,1)S(1)} %shard_map.152.first_ref, bf16[144,3584]{1,0:T(8,128)(2,1)S(1)} %collective-permute-done.19.second_ref, bf16[256,3584]{1,0:T(8,128)(2,1)S(1)} %bitcast.37, bf16[256,3584]{1,0:T(8,128)(2,1)} %collective-permute-done.17.far_ref), custom_call_target="tpu_custom_call" | custom-call | flops 1056964608 | bytes 6176768 | tf_op jit(solution)/shard_map/pallas_call | solution.py:55
  95.6 1.6 collective-permute-start.20
  97.2 2.4 %shard_map.154 = (bf16[144,3584]{1,0:T(8,128)(2,1)S(1)}, bf16[144,3584]{1,0:T(8,128)(2,1)S(1)}) custom-call(bf16[144,3584]{1,0:T(8,128)(2,1)S(1)} %shard_map.151.first_ref, bf16[144,3584]{1,0:T(8,128)(2,1)S(1)} %collective-permute-done.21.second_ref, f32[288,256]{1,0:T(8,128)S(1)} %get-tuple-element.132.back_ref, bf16[3584,256]{1,0:T(8,128)(2,1)S(1)} %bitcast.28, ...), custom_call_target="tpu_custom_call" | custom-call | flops 2113929216 | bytes 8093696 | tf_op jit(solution)/shard_map/pallas_call | solution.py:55
  99.6 3.9 %collective-permute-done.11.refs_2_ = bf16[144,896]{1,0:T(8,128)(2,1)S(1)} collective-permute-done((bf16[144,896]{1,0:T(8,128)(2,1)S(1)}, bf16[144,896]{1,0:T(8,128)(2,1)S(1)}, u32[]{:S(2)}, u32[]{:S(2)}) %collective-permute-start.11) | collective-permute-done | bytes 258080 | tf_op jit(solution)/shard_map/ppermute | solution.py:42
  103.9 0.7 collective-permute-done.14.first_ref
  104.7 2.3 %collective-permute-done.20.back_ref = bf16[288,256]{1,0:T(8,128)(2,1)S(1)} collective-permute-done((bf16[288,256]{1,0:T(8,128)(2,1)S(1)}, bf16[288,256]{1,0:T(8,128)(2,1)S(1)}, u32[]{:S(2)}, u32[]{:S(2)}) %collective-permute-start.20) | collective-permute-done | bytes 147488 | tf_op jit(solution)/shard_map/ppermute | solution.py:37
  107.0 1.1 shard_map.155.first_ref
  108.2 0.9 collective-permute-start.23
  109.7 21.3 %collective-permute-done.23.middle_ref = bf16[128,3584]{1,0:T(8,128)(2,1)S(1)} collective-permute-done((bf16[128,3584]{1,0:T(8,128)(2,1)S(1)}, bf16[128,3584]{1,0:T(8,128)(2,1)S(1)}, u32[]{:S(2)}, u32[]{:S(2)}) %collective-permute-start.23) | collective-permute-done | bytes 917536 | tf_op jit(solution)/shard_map/ppermute | solution.py:33
  130.9 0.9 copy-done.11
  131.9 2.5 %shard_map.157 = (bf16[144,3584]{1,0:T(8,128)(2,1)S(1)}, bf16[144,3584]{1,0:T(8,128)(2,1)S(1)}) custom-call(bf16[144,3584]{1,0:T(8,128)(2,1)S(1)} %collective-permute-done.14.first_ref, bf16[144,3584]{1,0:T(8,128)(2,1)S(1)} %collective-permute-done.26.second_ref, bf16[288,256]{1,0:T(8,128)(2,1)S(1)} %collective-permute-done.20.back_ref, ...), custom_call_target="tpu_custom_call" | custom-call | flops 2113929216 | bytes 7946240 | tf_op jit(solution)/shard_map/pallas_call | solution.py:55
  135.0 0.9 collective-permute-start.29
  135.9 1.1 collective-permute-start.22
  137.1 1.2 shard_map.156.own_ref
  138.3 1.3 shard_map.158
  140.2 1.2 add_convert_fusion
  141.4 3.5 %collective-permute-done.28.other_ref = bf16[288,256]{1,0:T(8,128)(2,1)S(1)} collective-permute-done((bf16[288,256]{1,0:T(8,128)(2,1)S(1)}, bf16[288,256]{1,0:T(8,128)(2,1)S(1)}, u32[]{:S(2)}, u32[]{:S(2)}) %collective-permute-start.28) | collective-permute-done | bytes 147488 | tf_op jit(solution)/shard_map/ppermute | solution.py:37
  144.9 2.7 %shard_map.159 = (bf16[144,3584]{1,0:T(8,128)(2,1)S(1)}, bf16[144,3584]{1,0:T(8,128)(2,1)S(1)}) custom-call(bf16[288,256]{1,0:T(8,128)(2,1)S(1)} %shard_map.156.own_ref, bf16[288,256]{1,0:T(8,128)(2,1)S(1)} %collective-permute-done.28.other_ref, bf16[256,3584]{1,0:T(8,128)(2,1)S(1)} %bitcast.38, bf16[256,3584]{1,0:T(8,128)(2,1)} %collective-permute-done.17.far_ref), custom_call_target="tpu_custom_call" | custom-call | flops 1 | bytes 1 | tf_op jit(solution)/shard_map/pallas_call | solution.py:55
  148.8 1.6 collective-permute-done.31.refs_1_
  150.4 1.9 shard_map.160
  152.3 0.9 collective-permute-start.32
  153.1 5.1 %collective-permute-start.33 = (bf16[144,896]{1,0:T(8,128)(2,1)}, bf16[144,896]{1,0:T(8,128)(2,1)}, u32[]{:S(2)}, u32[]{:S(2)}) collective-permute-start(bf16[144,896]{1,0:T(8,128)(2,1)} %get-tuple-element.150), channel_id=1, source_target_pairs={{0,28},{1,29},{2,30},{3,31},{4,16},{5,17},{6,18},{7,19},{8,20},{9,... | collective-permute-start | bytes 774152 | tf_op jit(solution)/shard_map/ppermute | solution.py:33
  158.3 1.8 collective-permute-start.35
  160.3 13.1 %collective-permute-done.37.refs_2_ = bf16[144,3584]{1,0:T(8,128)(2,1)} collective-permute-done((bf16[144,3584]{1,0:T(8,128)(2,1)}, bf16[144,3584]{1,0:T(8,128)(2,1)}, u32[]{:S(2)}, u32[]{:S(2)}) %collective-permute-start.37) | collective-permute-done | bytes 1032224 | tf_op jit(solution)/shard_map/ppermute | solution.py:37
  173.3 3.3 %shard_map.161 = (bf16[144,896]{1,0:T(8,128)(2,1)}, bf16[144,896]{1,0:T(8,128)(2,1)}, bf16[144,896]{1,0:T(8,128)(2,1)}, bf16[144,896]{1,0:T(8,128)(2,1)}) custom-call(bf16[144,3584]{1,0:T(8,128)(2,1)S(1)} %get-tuple-element.155.refs_0_, bf16[144,3584]{1,0:T(8,128)(2,1)S(1)} %collective-permute-done.36.refs_1_, bf16[144,3584]{1,0:T(8,128)(2,1)} %collective-permute-done.37.refs_2_), custom_call_target="tpu_custom_call" | custom-call | flops 1 | bytes 1 | tf_op jit(solution)/shard_map/pallas_call | solution.py:55
  176.6 0.9 collective-permute-start.38
  177.5 5.1 %collective-permute-start.39 = (bf16[144,896]{1,0:T(8,128)(2,1)}, bf16[144,896]{1,0:T(8,128)(2,1)S(1)}, u32[]{:S(2)}, u32[]{:S(2)}) collective-permute-start(bf16[144,896]{1,0:T(8,128)(2,1)} %get-tuple-element.159), channel_id=1, source_target_pairs={{0,28},{1,29},{2,30},{3,31},{4,16},{5,17},{6,18},{7,19},{8,20},{9,... | collective-permute-start | bytes 774152 | tf_op jit(solution)/shard_map/ppermute | solution.py:33
  182.7 1.8 collective-permute-start.41
  184.6 1.2 copy-done.12
  185.8 3.4 %shard_map.162 = bf16[128,3584]{1,0:T(8,128)(2,1)} custom-call(s32[128,1]{1,0:T(8,128)S(1)} %copy.18.route_ref, f32[128,1]{1,0:T(8,128)S(1)} %copy.19.gate_ref, bf16[128,3584]{1,0:T(8,128)(2,1)S(1)} %copy-done.12, bf16[144,896]{1,0:T(8,128)(2,1)S(1)} %collective-permute-done.32.refs_0_, bf16[144,896]{1,0:T(8,128)(2,1)} %collective-permute-done.33.refs_1_, ...), custom_call_target="tpu_custom_call" | custom-call | flops 1056964608 | bytes 2868224 | tf_op jit(solution)/shard_map/pallas_call | solution.py:55
  189.3 4.4 %collective-permute-done.38.refs_0_ = bf16[144,896]{1,0:T(8,128)(2,1)S(1)} collective-permute-done((bf16[144,896]{1,0:T(8,128)(2,1)}, bf16[144,896]{1,0:T(8,128)(2,1)S(1)}, u32[]{:S(2)}, u32[]{:S(2)}) %collective-permute-start.38) | collective-permute-done | bytes 258080 | tf_op jit(solution)/shard_map/ppermute | solution.py:33
  193.6 10.8 %collective-permute-done.40.refs_2_ = bf16[144,896]{1,0:T(8,128)(2,1)S(1)} collective-permute-done((bf16[144,896]{1,0:T(8,128)(2,1)}, bf16[144,896]{1,0:T(8,128)(2,1)S(1)}, u32[]{:S(2)}, u32[]{:S(2)}) %collective-permute-start.40) | collective-permute-done | bytes 258080 | tf_op jit(solution)/shard_map/ppermute | solution.py:33
  204.4 3.9 %shard_map.163 = bf16[128,3584]{1,0:T(8,128)(2,1)} custom-call(s32[128,1]{1,0:T(8,128)S(1)} %copy.20.route_ref, f32[1,3584]{1,0:T(1,128)S(1)} %slice.19.gain_ref, bf16[128,3584]{1,0:T(8,128)(2,1)} %collective-permute-done.13.middle_ref, bf16[128,3584]{1,0:T(8,128)(2,1)S(1)} %copy-done.10, bf16[144,896]{1,0:T(8,128)(2,1)S(1)} %collective-permute-done.38.refs_0_, ...), custom_call_target="tpu_custom_call" | custom-call | flops 1056964608 | bytes 3799552 | tf_op jit(solution)/shard_map/pallas_call | solution.py:55
  (109 shorter events, 6.1 us)
Async XLA Ops:
  1.6 17.9 %collective-permute-start = (bf16[128,448]{1,0:T(8,128)(2,1)S(1)}, bf16[128,448]{1,0:T(8,128)(2,1)S(1)}, u32[]{:S(2)}, u32[]{:S(2)}) collective-permute-start(bf16[128,448]{1,0:T(8,128)(2,1)S(1)} %bitcast.43), channel_id=1, source_target_pairs={{0,4},{1,5},{2,6},{3,7},{4,8},{5,9},{6,10},{7,11},{8,12},{9,13},{1... | collective-permute-start | bytes 344072 | tf_op jit(solution)/shard_map/ppermute | solution.py:378
  6.6 12.9 %collective-permute-start.1 = (bf16[128,448]{1,0:T(8,128)(2,1)S(1)}, bf16[128,448]{1,0:T(8,128)(2,1)S(1)}, u32[]{:S(2)}, u32[]{:S(2)}) collective-permute-start(bf16[128,448]{1,0:T(8,128)(2,1)S(1)} %bitcast.44), channel_id=1, source_target_pairs={{0,8},{1,9},{2,10},{3,11},{4,12},{5,13},{6,14},{7,15},{16,24},{17,... | collective-permute-start | bytes 344072 | tf_op jit(solution)/shard_map/ppermute | solution.py:378
  11.1 8.4 %collective-permute-start.2 = (bf16[128,448]{1,0:T(8,128)(2,1)S(1)}, bf16[128,448]{1,0:T(8,128)(2,1)S(1)}, u32[]{:S(2)}, u32[]{:S(2)}) collective-permute-start(bf16[128,448]{1,0:T(8,128)(2,1)S(1)} %bitcast.45), channel_id=1, source_target_pairs={{0,12},{1,13},{2,14},{3,15},{16,28},{17,29},{18,30},{19,31}} | collective-permute-start | bytes 344072 | tf_op jit(solution)/shard_map/ppermute | solution.py:378
  14.6 1.2 copy-start.7
  15.7 17.0 %copy-start.2 = (bf16[1,1,256,3584]{3,2,1,0:T(8,128)(2,1)S(1)}, bf16[1,1,256,3584]{3,2,1,0:T(8,128)(2,1)}, u32[]{:S(2)}) copy-start(bf16[1,1,256,3584]{3,2,1,0:T(8,128)(2,1)} %param.27) | copy-start | bytes 5505028
  15.7 20.3 %copy-start.24 = (s32[1,2,2,4]{3,2,1,0:T(2,128)S(1)}, s32[1,2,2,4]{3,2,1,0:T(2,128)}, u32[]{:S(2)}) copy-start(s32[1,2,2,4]{3,2,1,0:T(2,128)} %param.17) | copy-start | bytes 196
  15.7 20.4 %copy-start.26 = (s32[1,128,1]{1,2,0:T(1,128)S(1)}, s32[1,128,1]{1,2,0:T(1,128)}, u32[]{:S(2)}) copy-start(s32[1,128,1]{1,2,0:T(1,128)} %param.18) | copy-start | bytes 1540
  15.7 23.3 %copy-start.4 = (f32[1,3584]{1,0:T(1,128)S(1)}, f32[1,3584]{1,0:T(1,128)}, u32[]{:S(2)}) copy-start(f32[1,3584]{1,0:T(1,128)} %gain_ref.3) | copy-start | bytes 43012
  19.5 14.8 %copy-start.15 = (bf16[144,896]{1,0:T(8,128)(2,1)}, bf16[144,896]{1,0:T(8,128)(2,1)S(1)}, u32[]{:S(2)}) copy-start(bf16[144,896]{1,0:T(8,128)(2,1)S(1)} %get-tuple-element.124) | copy-start | bytes 774148
  19.5 16.3 %copy-start.17 = (bf16[144,896]{1,0:T(8,128)(2,1)}, bf16[144,896]{1,0:T(8,128)(2,1)S(1)}, u32[]{:S(2)}) copy-start(bf16[144,896]{1,0:T(8,128)(2,1)S(1)} %get-tuple-element.107) | copy-start | bytes 774148
  19.5 16.3 %copy-start.20 = (bf16[144,896]{1,0:T(8,128)(2,1)}, bf16[144,896]{1,0:T(8,128)(2,1)S(1)}, u32[]{:S(2)}) copy-start(bf16[144,896]{1,0:T(8,128)(2,1)S(1)} %get-tuple-element.126.refs_0_) | copy-start | bytes 774148
  19.5 16.3 %copy-start.22 = (bf16[144,896]{1,0:T(8,128)(2,1)}, bf16[144,896]{1,0:T(8,128)(2,1)S(1)}, u32[]{:S(2)}) copy-start(bf16[144,896]{1,0:T(8,128)(2,1)S(1)} %get-tuple-element.116.refs_0_) | copy-start | bytes 774148
  19.6 13.2 %collective-permute-start.3 = (bf16[512,448]{1,0:T(8,128)(2,1)S(1)}, bf16[512,448]{1,0:T(8,128)(2,1)S(1)}, u32[]{:S(2)}, u32[]{:S(2)}) collective-permute-start(bf16[512,448]{1,0:T(8,128)(2,1)S(1)} %constant_dynamic-update-slice_fusion.kv0), channel_id=1, source_target_pairs={{0,2},{1,3},{2,0},{3,1},{4,6},{5,7},{6,4},{7,5},{8,10},{9,11},{10,... | collective-permute-start | bytes 1376264 | tf_op jit(solution)/shard_map/ppermute | solution.py:37
  21.2 8.9 %collective-permute-start.6 = (bf16[144,896]{1,0:T(8,128)(2,1)S(1)}, bf16[144,896]{1,0:T(8,128)(2,1)S(1)}, u32[]{:S(2)}, u32[]{:S(2)}) collective-permute-start(bf16[144,896]{1,0:T(8,128)(2,1)S(1)} %get-tuple-element.103), channel_id=1, source_target_pairs={{0,4},{1,5},{2,6},{3,7},{4,8},{5,9},{6,10},{7,11},{8,12},{9,13},{1... | collective-permute-start | bytes 774152 | tf_op jit(solution)/shard_map/ppermute | solution.py:42
  32.8 44.6 %collective-permute-start.17 = (bf16[256,3584]{1,0:T(8,128)(2,1)S(1)}, bf16[256,3584]{1,0:T(8,128)(2,1)}, u32[]{:S(2)}, u32[]{:S(2)}) collective-permute-start(bf16[256,3584]{1,0:T(8,128)(2,1)S(1)} %bitcast.36), channel_id=1, source_target_pairs={{0,2},{1,3},{2,0},{3,1},{4,6},{5,7},{6,4},{7,5},{8,10},{9,11},{10,... | collective-permute-start | bytes 5505032 | tf_op jit(solution)/shard_map/ppermute | solution.py:37
  34.3 4.8 %collective-permute-start.4 = (bf16[512,448]{1,0:T(8,128)(2,1)S(1)}, bf16[512,448]{1,0:T(8,128)(2,1)}, u32[]{:S(2)}, u32[]{:S(2)}) collective-permute-start(bf16[512,448]{1,0:T(8,128)(2,1)S(1)} %constant_dynamic-update-slice_fusion.kv0), channel_id=1, source_target_pairs={{0,1},{1,0},{2,3},{3,2},{4,5},{5,4},{6,7},{7,6},{8,9},{9,8},{10,11... | collective-permute-start | bytes 1376264 | tf_op jit(solution)/shard_map/ppermute | solution.py:37
  34.3 34.1 %collective-permute-start.13 = (bf16[128,3584]{1,0:T(8,128)(2,1)}, bf16[128,3584]{1,0:T(8,128)(2,1)}, u32[]{:S(2)}, u32[]{:S(2)}) collective-permute-start(bf16[128,3584]{1,0:T(8,128)(2,1)} %bitcast.10.middle_ref), channel_id=1, source_target_pairs={{0,16},{1,17},{2,18},{3,19},{4,20},{5,21},{6,22},{7,23},{8,24},{9,... | collective-permute-start | bytes 2752520 | tf_op jit(solution)/shard_map/ppermute | solution.py:33
  35.8 3.3 %collective-permute-start.5 = (bf16[512,448]{1,0:T(8,128)(2,1)S(1)}, bf16[512,448]{1,0:T(8,128)(2,1)}, u32[]{:S(2)}, u32[]{:S(2)}) collective-permute-start(bf16[512,448]{1,0:T(8,128)(2,1)S(1)} %collective-permute-done.3.kv1), channel_id=1, source_target_pairs={{0,1},{1,0},{2,3},{3,2},{4,5},{5,4},{6,7},{7,6},{8,9},{9,8},{10,11... | collective-permute-start | bytes 1376264 | tf_op jit(solution)/shard_map/ppermute | solution.py:37
  36.2 15.3 %collective-permute-start.8 = (bf16[144,896]{1,0:T(8,128)(2,1)}, bf16[144,896]{1,0:T(8,128)(2,1)}, u32[]{:S(2)}, u32[]{:S(2)}) collective-permute-start(bf16[144,896]{1,0:T(8,128)(2,1)} %copy-done.17), channel_id=1, source_target_pairs={{0,12},{1,13},{2,14},{3,15},{4,0},{5,1},{6,2},{7,3},{8,4},{9,5},{1... | collective-permute-start | bytes 774152 | tf_op jit(solution)/shard_map/ppermute | solution.py:42
  39.0 16.9 %collective-permute-start.7 = (bf16[144,896]{1,0:T(8,128)(2,1)S(1)}, bf16[144,896]{1,0:T(8,128)(2,1)}, u32[]{:S(2)}, u32[]{:S(2)}) collective-permute-start(bf16[144,896]{1,0:T(8,128)(2,1)S(1)} %get-tuple-element.105), channel_id=1, source_target_pairs={{0,8},{1,9},{2,10},{3,11},{4,12},{5,13},{6,14},{7,15},{8,0},{9,1},... | collective-permute-start | bytes 774152 | tf_op jit(solution)/shard_map/ppermute | solution.py:42
  39.1 1.2 copy-start.5
  41.4 8.3 %copy-start.16 = (bf16[144,896]{1,0:T(8,128)(2,1)S(1)}, bf16[144,896]{1,0:T(8,128)(2,1)}, u32[]{:S(2)}) copy-start(bf16[144,896]{1,0:T(8,128)(2,1)} %copy-done.15) | copy-start | bytes 774148
  41.5 10.0 %copy-start.14 = (bf16[144,896]{1,0:T(8,128)(2,1)S(1)}, bf16[144,896]{1,0:T(8,128)(2,1)}, u32[]{:S(2)}) copy-start(bf16[144,896]{1,0:T(8,128)(2,1)} %copy-done.13) | copy-start | bytes 774148
  41.5 26.9 %copy-start.19 = (bf16[144,896]{1,0:T(8,128)(2,1)S(1)}, bf16[144,896]{1,0:T(8,128)(2,1)}, u32[]{:S(2)}) copy-start(bf16[144,896]{1,0:T(8,128)(2,1)} %copy-done.18) | copy-start | bytes 774148
  41.5 26.9 %copy-start.23 = (bf16[144,896]{1,0:T(8,128)(2,1)S(1)}, bf16[144,896]{1,0:T(8,128)(2,1)}, u32[]{:S(2)}) copy-start(bf16[144,896]{1,0:T(8,128)(2,1)} %copy-done.22) | copy-start | bytes 774148
  49.8 27.6 %copy-start.21 = (bf16[144,896]{1,0:T(8,128)(2,1)S(1)}, bf16[144,896]{1,0:T(8,128)(2,1)}, u32[]{:S(2)}) copy-start(bf16[144,896]{1,0:T(8,128)(2,1)} %copy-done.20) | copy-start | bytes 774148
  49.8 20.8 %collective-permute-start.16 = (bf16[144,896]{1,0:T(8,128)(2,1)S(1)}, bf16[144,896]{1,0:T(8,128)(2,1)S(1)}, u32[]{:S(2)}, u32[]{:S(2)}) collective-permute-start(bf16[144,896]{1,0:T(8,128)(2,1)S(1)} %copy-done.16), channel_id=1, source_target_pairs={{0,12},{1,13},{2,14},{3,15},{4,0},{5,1},{6,2},{7,3},{8,4},{9,5},{1... | collective-permute-start | bytes 774152 | tf_op jit(solution)/shard_map/ppermute | solution.py:42
  51.5 25.9 %collective-permute-start.15 = (bf16[144,896]{1,0:T(8,128)(2,1)S(1)}, bf16[144,896]{1,0:T(8,128)(2,1)S(1)}, u32[]{:S(2)}, u32[]{:S(2)}) collective-permute-start(bf16[144,896]{1,0:T(8,128)(2,1)S(1)} %copy-done.14), channel_id=1, source_target_pairs={{0,8},{1,9},{2,10},{3,11},{4,12},{5,13},{6,14},{7,15},{8,0},{9,1},... | collective-permute-start | bytes 774152 | tf_op jit(solution)/shard_map/ppermute | solution.py:42
  56.0 21.4 %collective-permute-start.9 = (bf16[144,896]{1,0:T(8,128)(2,1)S(1)}, bf16[144,896]{1,0:T(8,128)(2,1)S(1)}, u32[]{:S(2)}, u32[]{:S(2)}) collective-permute-start(bf16[144,896]{1,0:T(8,128)(2,1)S(1)} %get-tuple-element.110), channel_id=1, source_target_pairs={{0,4},{1,5},{2,6},{3,7},{4,8},{5,9},{6,10},{7,11},{8,12},{9,13},{1... | collective-permute-start | bytes 774152 | tf_op jit(solution)/shard_map/ppermute | solution.py:42
  70.5 9.0 %copy-start.8 = (bf16[1,128,3584]{2,1,0:T(8,128)(2,1)S(1)}, bf16[1,128,3584]{2,1,0:T(8,128)(2,1)}, u32[]{:S(2)}) copy-start(bf16[1,128,3584]{2,1,0:T(8,128)(2,1)} %param.21) | copy-start | bytes 2752516
  78.4 13.5 %collective-permute-start.19 = (bf16[144,3584]{1,0:T(8,128)(2,1)S(1)}, bf16[144,3584]{1,0:T(8,128)(2,1)S(1)}, u32[]{:S(2)}, u32[]{:S(2)}) collective-permute-start(bf16[144,3584]{1,0:T(8,128)(2,1)S(1)} %shard_map.152.first_ref), channel_id=1, source_target_pairs={{0,1},{1,0},{2,3},{3,2},{4,5},{5,4},{6,7},{7,6},{8,9},{9,8},{10,11... | collective-permute-start | bytes 3096584 | tf_op jit(solution)/shard_map/ppermute | solution.py:37
  78.5 17.1 %collective-permute-start.21 = (bf16[144,3584]{1,0:T(8,128)(2,1)S(1)}, bf16[144,3584]{1,0:T(8,128)(2,1)S(1)}, u32[]{:S(2)}, u32[]{:S(2)}) collective-permute-start(bf16[144,3584]{1,0:T(8,128)(2,1)S(1)} %shard_map.151.first_ref), channel_id=1, source_target_pairs={{0,1},{1,0},{2,3},{3,2},{4,5},{5,4},{6,7},{7,6},{8,9},{9,8},{10,11... | collective-permute-start | bytes 3096584 | tf_op jit(solution)/shard_map/ppermute | solution.py:37
  79.0 25.7 %collective-permute-start.14 = (bf16[144,3584]{1,0:T(8,128)(2,1)S(1)}, bf16[144,3584]{1,0:T(8,128)(2,1)S(1)}, u32[]{:S(2)}, u32[]{:S(2)}) collective-permute-start(bf16[144,3584]{1,0:T(8,128)(2,1)S(1)} %shard_map.151.first_ref), channel_id=1, source_target_pairs={{0,2},{1,3},{2,0},{3,1},{4,6},{5,7},{6,4},{7,5},{8,10},{9,11},{10,... | collective-permute-start | bytes 3096584 | tf_op jit(solution)/shard_map/ppermute | solution.py:37
  79.6 25.1 %collective-permute-start.18 = (bf16[128,3584]{1,0:T(8,128)(2,1)S(1)}, bf16[128,3584]{1,0:T(8,128)(2,1)S(1)}, u32[]{:S(2)}, u32[]{:S(2)}) collective-permute-start(bf16[128,3584]{1,0:T(8,128)(2,1)S(1)} %bitcast.42), channel_id=1, source_target_pairs={{0,16},{1,17},{2,18},{3,19},{4,20},{5,21},{6,22},{7,23},{8,24},{9,... | collective-permute-start | bytes 2752520 | tf_op jit(solution)/shard_map/ppermute | solution.py:33
  80.4 16.7 %copy-start = (bf16[1,1,3584,256]{3,2,1,0:T(8,128)(2,1)S(1)}, bf16[1,1,3584,256]{3,2,1,0:T(8,128)(2,1)}, u32[]{:S(2)}) copy-start(bf16[1,1,3584,256]{3,2,1,0:T(8,128)(2,1)} %param.25) | copy-start | bytes 5505028
  80.4 16.7 %copy-start.1 = (bf16[1,1,3584,256]{3,2,1,0:T(8,128)(2,1)S(1)}, bf16[1,1,3584,256]{3,2,1,0:T(8,128)(2,1)}, u32[]{:S(2)}) copy-start(bf16[1,1,3584,256]{3,2,1,0:T(8,128)(2,1)} %param.26) | copy-start | bytes 5505028
  80.5 10.6 %collective-permute-start.10 = (bf16[144,896]{1,0:T(8,128)(2,1)S(1)}, bf16[144,896]{1,0:T(8,128)(2,1)S(1)}, u32[]{:S(2)}, u32[]{:S(2)}) collective-permute-start(bf16[144,896]{1,0:T(8,128)(2,1)S(1)} %get-tuple-element.112), channel_id=1, source_target_pairs={{0,4},{1,5},{2,6},{3,7},{4,8},{5,9},{6,10},{7,11},{8,12},{9,13},{1... | collective-permute-start | bytes 774152 | tf_op jit(solution)/shard_map/ppermute | solution.py:42
  91.1 12.4 %collective-permute-start.11 = (bf16[144,896]{1,0:T(8,128)(2,1)S(1)}, bf16[144,896]{1,0:T(8,128)(2,1)S(1)}, u32[]{:S(2)}, u32[]{:S(2)}) collective-permute-start(bf16[144,896]{1,0:T(8,128)(2,1)S(1)} %get-tuple-element.113), channel_id=1, source_target_pairs={{0,8},{1,9},{2,10},{3,11},{4,12},{5,13},{6,14},{7,15},{8,0},{9,1},... | collective-permute-start | bytes 774152 | tf_op jit(solution)/shard_map/ppermute | solution.py:42
  92.0 12.0 %collective-permute-start.12 = (bf16[144,896]{1,0:T(8,128)(2,1)S(1)}, bf16[144,896]{1,0:T(8,128)(2,1)S(1)}, u32[]{:S(2)}, u32[]{:S(2)}) collective-permute-start(bf16[144,896]{1,0:T(8,128)(2,1)S(1)} %get-tuple-element.114), channel_id=1, source_target_pairs={{0,12},{1,13},{2,14},{3,15},{4,0},{5,1},{6,2},{7,3},{8,4},{9,5},{1... | collective-permute-start | bytes 774152 | tf_op jit(solution)/shard_map/ppermute | solution.py:42
  95.6 11.4 %collective-permute-start.20 = (bf16[288,256]{1,0:T(8,128)(2,1)S(1)}, bf16[288,256]{1,0:T(8,128)(2,1)S(1)}, u32[]{:S(2)}, u32[]{:S(2)}) collective-permute-start(bf16[288,256]{1,0:T(8,128)(2,1)S(1)} %get-tuple-element.131), channel_id=1, source_target_pairs={{0,2},{1,3},{2,0},{3,1},{4,6},{5,7},{6,4},{7,5},{8,10},{9,11},{10,... | collective-permute-start | bytes 442376 | tf_op jit(solution)/shard_map/ppermute | solution.py:37
  104.7 3.4 %copy-start.9 = (bf16[128,3584]{1,0:T(8,128)(2,1)}, bf16[128,3584]{1,0:T(8,128)(2,1)S(1)}, u32[]{:S(2)}) copy-start(bf16[128,3584]{1,0:T(8,128)(2,1)S(1)} %collective-permute-done.18.grad_ref) | copy-start | bytes 2752516
  108.1 26.9 %copy-start.25 = (f32[1,128,1]{1,2,0:T(1,128)S(1)}, f32[1,128,1]{1,2,0:T(1,128)}, u32[]{:S(2)}) copy-start(f32[1,128,1]{1,2,0:T(1,128)} %param.19) | copy-start | bytes 1540
  108.1 23.8 %collective-permute-start.26 = (bf16[144,3584]{1,0:T(8,128)(2,1)S(1)}, bf16[144,3584]{1,0:T(8,128)(2,1)S(1)}, u32[]{:S(2)}, u32[]{:S(2)}) collective-permute-start(bf16[144,3584]{1,0:T(8,128)(2,1)S(1)} %collective-permute-done.14.first_ref), channel_id=1, source_target_pairs={{0,1},{1,0},{2,3},{3,2},{4,5},{5,4},{6,7},{7,6},{8,9},{9,8},{10,11... | collective-permute-start | bytes 3096584 | tf_op jit(solution)/shard_map/ppermute | solution.py:37
  108.2 22.8 %collective-permute-start.23 = (bf16[128,3584]{1,0:T(8,128)(2,1)S(1)}, bf16[128,3584]{1,0:T(8,128)(2,1)S(1)}, u32[]{:S(2)}, u32[]{:S(2)}) collective-permute-start(bf16[128,3584]{1,0:T(8,128)(2,1)S(1)} %get-tuple-element.139), channel_id=1, source_target_pairs={{0,16},{1,17},{2,18},{3,19},{4,20},{5,21},{6,22},{7,23},{8,24},{9,... | collective-permute-start | bytes 2752520 | tf_op jit(solution)/shard_map/ppermute | solution.py:33
  109.1 25.2 %collective-permute-start.25 = (bf16[144,3584]{1,0:T(8,128)(2,1)S(1)}, bf16[144,3584]{1,0:T(8,128)(2,1)S(1)}, u32[]{:S(2)}, u32[]{:S(2)}) collective-permute-start(bf16[144,3584]{1,0:T(8,128)(2,1)S(1)} %shard_map.155.first_ref), channel_id=1, source_target_pairs={{0,2},{1,3},{2,0},{3,1},{4,6},{5,7},{6,4},{7,5},{8,10},{9,11},{10,... | collective-permute-start | bytes 3096584 | tf_op jit(solution)/shard_map/ppermute | solution.py:37
  109.7 27.4 %collective-permute-start.24 = (bf16[144,3584]{1,0:T(8,128)(2,1)S(1)}, bf16[144,3584]{1,0:T(8,128)(2,1)S(1)}, u32[]{:S(2)}, u32[]{:S(2)}) collective-permute-start(bf16[144,3584]{1,0:T(8,128)(2,1)S(1)} %shard_map.155.first_ref), channel_id=1, source_target_pairs={{0,1},{1,0},{2,3},{3,2},{4,5},{5,4},{6,7},{7,6},{8,9},{9,8},{10,11... | collective-permute-start | bytes 3096584 | tf_op jit(solution)/shard_map/ppermute | solution.py:37
  134.3 4.0 %collective-permute-start.27 = (bf16[144,3584]{1,0:T(8,128)(2,1)S(1)}, bf16[144,3584]{1,0:T(8,128)(2,1)S(1)}, u32[]{:S(2)}, u32[]{:S(2)}) collective-permute-start(bf16[144,3584]{1,0:T(8,128)(2,1)S(1)} %collective-permute-done.25.first_ref), channel_id=1, source_target_pairs={{0,1},{1,0},{2,3},{3,2},{4,5},{5,4},{6,7},{7,6},{8,9},{9,8},{10,11... | collective-permute-start | bytes 3096584 | tf_op jit(solution)/shard_map/ppermute | solution.py:37
  134.4 5.8 %collective-permute-start.30 = (bf16[144,3584]{1,0:T(8,128)(2,1)S(1)}, bf16[144,3584]{1,0:T(8,128)(2,1)S(1)}, u32[]{:S(2)}, u32[]{:S(2)}) collective-permute-start(bf16[144,3584]{1,0:T(8,128)(2,1)S(1)} %get-tuple-element.145), channel_id=1, source_target_pairs={{0,1},{1,0},{2,3},{3,2},{4,5},{5,4},{6,7},{7,6},{8,9},{9,8},{10,11... | collective-permute-start | bytes 3096584 | tf_op jit(solution)/shard_map/ppermute | solution.py:37
  135.0 6.4 %collective-permute-start.29 = (f32[1,3712]{1,0:T(1,128)S(1)}, f32[1,3712]{1,0:T(1,128)S(1)}, u32[]{:S(2)}, u32[]{:S(2)}) collective-permute-start(f32[1,3712]{1,0:T(1,128)S(1)} %pad_maximum_fusion), channel_id=1, source_target_pairs={{0,16},{1,17},{2,18},{3,19},{4,20},{5,21},{6,22},{7,23},{8,24},{9,... | collective-permute-start | bytes 44552 | tf_op jit(solution)/shard_map/ppermute | solution.py:33
  135.9 5.5 %collective-permute-start.22 = (f32[1,256]{1,0:T(1,128)S(1)}, f32[1,256]{1,0:T(1,128)S(1)}, u32[]{:S(2)}, u32[]{:S(2)}) collective-permute-start(f32[1,256]{1,0:T(1,128)S(1)} %maximum_bitcast_fusion), channel_id=1, source_target_pairs={{0,16},{1,17},{2,18},{3,19},{4,20},{5,21},{6,22},{7,23},{8,24},{9,... | collective-permute-start | bytes 3080 | tf_op jit(solution)/shard_map/ppermute | solution.py:33
  139.6 5.3 %collective-permute-start.28 = (bf16[288,256]{1,0:T(8,128)(2,1)S(1)}, bf16[288,256]{1,0:T(8,128)(2,1)S(1)}, u32[]{:S(2)}, u32[]{:S(2)}) collective-permute-start(bf16[288,256]{1,0:T(8,128)(2,1)S(1)} %shard_map.158), channel_id=1, source_target_pairs={{0,2},{1,3},{2,0},{3,1},{4,6},{5,7},{6,4},{7,5},{8,10},{9,11},{10,... | collective-permute-start | bytes 442376 | tf_op jit(solution)/shard_map/ppermute | solution.py:37
  147.7 2.7 %collective-permute-start.31 = (bf16[144,3584]{1,0:T(8,128)(2,1)S(1)}, bf16[144,3584]{1,0:T(8,128)(2,1)S(1)}, u32[]{:S(2)}, u32[]{:S(2)}) collective-permute-start(bf16[144,3584]{1,0:T(8,128)(2,1)S(1)} %get-tuple-element.148), channel_id=1, source_target_pairs={{0,1},{1,0},{2,3},{3,2},{4,5},{5,4},{6,7},{7,6},{8,9},{9,8},{10,11... | collective-permute-start | bytes 3096584 | tf_op jit(solution)/shard_map/ppermute | solution.py:37
  147.7 10.5 %collective-permute-start.36 = (bf16[144,3584]{1,0:T(8,128)(2,1)S(1)}, bf16[144,3584]{1,0:T(8,128)(2,1)S(1)}, u32[]{:S(2)}, u32[]{:S(2)}) collective-permute-start(bf16[144,3584]{1,0:T(8,128)(2,1)S(1)} %get-tuple-element.153), channel_id=1, source_target_pairs={{0,1},{1,0},{2,3},{3,2},{4,5},{5,4},{6,7},{7,6},{8,9},{9,8},{10,11... | collective-permute-start | bytes 3096584 | tf_op jit(solution)/shard_map/ppermute | solution.py:37
  148.2 25.1 %collective-permute-start.37 = (bf16[144,3584]{1,0:T(8,128)(2,1)}, bf16[144,3584]{1,0:T(8,128)(2,1)}, u32[]{:S(2)}, u32[]{:S(2)}) collective-permute-start(bf16[144,3584]{1,0:T(8,128)(2,1)} %add_convert_fusion), channel_id=1, source_target_pairs={{0,2},{1,3},{2,0},{3,1},{4,6},{5,7},{6,4},{7,5},{8,10},{9,11},{10,... | collective-permute-start | bytes 3096584 | tf_op jit(solution)/shard_map/ppermute | solution.py:37
  152.3 25.3 %collective-permute-start.32 = (bf16[144,896]{1,0:T(8,128)(2,1)}, bf16[144,896]{1,0:T(8,128)(2,1)S(1)}, u32[]{:S(2)}, u32[]{:S(2)}) collective-permute-start(bf16[144,896]{1,0:T(8,128)(2,1)} %get-tuple-element.149), channel_id=1, source_target_pairs={{0,16},{1,17},{2,18},{3,19},{4,20},{5,21},{6,22},{7,23},{8,24},{9,... | collective-permute-start | bytes 774152 | tf_op jit(solution)/shard_map/ppermute | solution.py:33
  153.1 29.5 %collective-permute-start.33 = (bf16[144,896]{1,0:T(8,128)(2,1)}, bf16[144,896]{1,0:T(8,128)(2,1)}, u32[]{:S(2)}, u32[]{:S(2)}) collective-permute-start(bf16[144,896]{1,0:T(8,128)(2,1)} %get-tuple-element.150), channel_id=1, source_target_pairs={{0,28},{1,29},{2,30},{3,31},{4,16},{5,17},{6,18},{7,19},{8,20},{9,... | collective-permute-start | bytes 774152 | tf_op jit(solution)/shard_map/ppermute | solution.py:33
  158.3 24.4 %collective-permute-start.34 = (bf16[144,896]{1,0:T(8,128)(2,1)}, bf16[144,896]{1,0:T(8,128)(2,1)}, u32[]{:S(2)}, u32[]{:S(2)}) collective-permute-start(bf16[144,896]{1,0:T(8,128)(2,1)} %get-tuple-element.151), channel_id=1, source_target_pairs={{0,24},{1,25},{2,26},{3,27},{4,28},{5,29},{6,30},{7,31},{8,16},{9,... | collective-permute-start | bytes 774152 | tf_op jit(solution)/shard_map/ppermute | solution.py:33
  158.3 26.3 %collective-permute-start.35 = (bf16[144,896]{1,0:T(8,128)(2,1)S(1)}, bf16[144,896]{1,0:T(8,128)(2,1)}, u32[]{:S(2)}, u32[]{:S(2)}) collective-permute-start(bf16[144,896]{1,0:T(8,128)(2,1)S(1)} %get-tuple-element.152), channel_id=1, source_target_pairs={{0,20},{1,21},{2,22},{3,23},{4,24},{5,25},{6,26},{7,27},{8,28},{9,... | collective-permute-start | bytes 774152 | tf_op jit(solution)/shard_map/ppermute | solution.py:33
  176.6 17.0 %collective-permute-start.38 = (bf16[144,896]{1,0:T(8,128)(2,1)}, bf16[144,896]{1,0:T(8,128)(2,1)S(1)}, u32[]{:S(2)}, u32[]{:S(2)}) collective-permute-start(bf16[144,896]{1,0:T(8,128)(2,1)} %get-tuple-element.158), channel_id=1, source_target_pairs={{0,16},{1,17},{2,18},{3,19},{4,20},{5,21},{6,22},{7,23},{8,24},{9,... | collective-permute-start | bytes 774152 | tf_op jit(solution)/shard_map/ppermute | solution.py:33
  177.5 16.1 %collective-permute-start.39 = (bf16[144,896]{1,0:T(8,128)(2,1)}, bf16[144,896]{1,0:T(8,128)(2,1)S(1)}, u32[]{:S(2)}, u32[]{:S(2)}) collective-permute-start(bf16[144,896]{1,0:T(8,128)(2,1)} %get-tuple-element.159), channel_id=1, source_target_pairs={{0,28},{1,29},{2,30},{3,31},{4,16},{5,17},{6,18},{7,19},{8,20},{9,... | collective-permute-start | bytes 774152 | tf_op jit(solution)/shard_map/ppermute | solution.py:33
  182.7 21.8 %collective-permute-start.40 = (bf16[144,896]{1,0:T(8,128)(2,1)}, bf16[144,896]{1,0:T(8,128)(2,1)S(1)}, u32[]{:S(2)}, u32[]{:S(2)}) collective-permute-start(bf16[144,896]{1,0:T(8,128)(2,1)} %get-tuple-element.160), channel_id=1, source_target_pairs={{0,24},{1,25},{2,26},{3,27},{4,28},{5,29},{6,30},{7,31},{8,16},{9,... | collective-permute-start | bytes 774152 | tf_op jit(solution)/shard_map/ppermute | solution.py:33
  182.7 21.8 %collective-permute-start.41 = (bf16[144,896]{1,0:T(8,128)(2,1)}, bf16[144,896]{1,0:T(8,128)(2,1)S(1)}, u32[]{:S(2)}, u32[]{:S(2)}) collective-permute-start(bf16[144,896]{1,0:T(8,128)(2,1)} %get-tuple-element.161), channel_id=1, source_target_pairs={{0,20},{1,21},{2,22},{3,23},{4,24},{5,25},{6,26},{7,27},{8,28},{9,... | collective-permute-start | bytes 774152 | tf_op jit(solution)/shard_map/ppermute | solution.py:33
  184.5 19.9 %copy-start.10 = (bf16[128,3584]{1,0:T(8,128)(2,1)S(1)}, bf16[128,3584]{1,0:T(8,128)(2,1)}, u32[]{:S(2)}) copy-start(bf16[128,3584]{1,0:T(8,128)(2,1)} %copy-done.9) | copy-start | bytes 2752516
  184.6 1.3 copy-start.12
  (5 other events, 4.2 us)

commit v12 on v11

--- a/solution.py
+++ b/solution.py
@@ -206,22 +206,23 @@
     out_ref[...] = (gate_val / (1.0 + jnp.exp(-gate_val)) * up_val).astype(bf16)
 
 
-def output_body(own_ref, other_ref, down_ref, far_ref, first_out, second_out):
+def output_body(own_ref, other_ref, down_ref, top_ref, low_ref, first_out, second_out):
     half = first_out.shape[0]
     hidden = jnp.concatenate([own_ref[...], other_ref[...]], axis=1)
     step = 4 * LANES
     for n in range(0, down_ref.shape[1], step):
         part = slice(n, n + step)
-        weight = jnp.concatenate([down_ref[:, part], far_ref[:, part]], axis=0)
+        weight = jnp.concatenate([down_ref[:, part], top_ref[:, part], low_ref[:, part]], axis=0)
         value = dot(hidden, weight).astype(bf16)
         first_out[:, part] = value[:half]
         second_out[:, part] = value[half:]
 
 
-def down_back_body(first_ref, second_ref, down_ref, far_ref, own_out, other_out):
+def down_back_body(first_ref, second_ref, down_ref, top_ref, low_ref, own_out, other_out):
     grads = jnp.concatenate([first_ref[...], second_ref[...]], axis=0)
     own_out[...] = dot_last(grads, down_ref[...]).astype(own_out.dtype)
-    other_out[...] = dot_last(grads, far_ref[...]).astype(other_out.dtype)
+    far = jnp.concatenate([top_ref[...], low_ref[...]], axis=0)
+    other_out[...] = dot_last(grads, far).astype(other_out.dtype)
 
 
 def backward_body(first_ref, second_ref, back_ref, gate_ref, up_ref, first_out, second_out):
@@ -417,14 +418,18 @@
         return [passed_along(chunks[k], by, k) for k in range(experts)]
 
     row_chunks, grad_chunks = packed[:experts], packed[experts:]
-    row_chunks[1] = turned(row_chunks[1], 1)
-    arrived = [row_chunks[1]]
-    down_other = swapped(after([w_down], [other_chip] + arrived)[0], 2)
-    downs = (w_down, down_other)
-    kv = [column, other_chip, swapped(column, 1), swapped(other_chip, 1)]
-    for k in range(2, experts):
+    first = 1 + 2 * (experts - 1) // 3
+    for k in range(1, first):
+        row_chunks[k] = turned(row_chunks[k], k)
+    arrived = row_chunks[1:first]
+    cut = hidden_width * 5 // 8
+    (down_top,) = after([w_down[:cut]], arrived[:1])
+    down_top = swapped(down_top, 2)
+    there_back_middle = passed_along(after([back_middle[0]], arrived)[0], -1)
+    far = swapped(after([other_chip], arrived)[0], 1)
+    kv = [column, other_chip, swapped(column, 1), far]
+    for k in range(first, experts):
         row_chunks[k] = turned(after([row_chunks[k]], arrived)[0], k)
-    there_back_middle = passed_along(after([back_middle[0]], [other_chip] + arrived)[0], -1)
 
     per_device = tokens // BLK
     chosen = selected_blocks[0].reshape(-1)
@@ -463,11 +468,16 @@
     for k in range(1, experts):
         grad_chunks[k] = turned(after([grad_chunks[k]], [middle])[0], k)
     front_chunks = sent(after(front_chunks, row_chunks + grad_chunks[1:2]))
-    back_rows = joined(after(row_chunks, [middle, there_back_middle]))
+    back_rows = joined(after(row_chunks, [middle]))
     back_other = swapped(back_rows, 2)
-    grad_near = joined(after(grad_chunks, [back_rows, down_other]))
+    down_low = swapped(after([w_down[cut:]], [back_rows])[0], 2)
+    downs = (w_down, down_top, down_low)
+    grad_near = joined(after(grad_chunks, [back_rows, down_top, there_back_middle]))
     there_back_grad = passed_along(after([back_grad[0]], [grad_near])[0], -1)
-    grad_near = [grad_near, swapped(grad_near, 1)]
+    ready = [back_other, there_back_grad, down_low]
+    front_near = joined(after(front_chunks, ready))
+    there_middle = passed_along(after([middle], [front_near])[0], 1)
+    grad_near = [grad_near, swapped(after([grad_near], [front_near])[0], 1)]
     down_back, other_back = call(
         down_back_body,
         [shape_of(pair, hidden_width, f32), shape_of(pair, hidden_width)],
@@ -475,15 +485,13 @@
         flops=2 * work,
     )
     far_back = swapped(other_back, 2)
-    back_near = backward((back_rows, swapped(back_rows, 1)), down_back)
+    late = after([back_rows], [front_near])[0]
+    back_near = backward((back_rows, swapped(late, 1)), down_back)
     back_core = swapped(back_near[1], 1)
-    ready = [back_other, there_back_grad, far_back, back_near[0]]
-    front_near = joined(after(front_chunks, ready))
-    there_middle = passed_along(after([middle], [front_near])[0], 1)
     (far_back,) = after([far_back], [there_middle])
     back_far = backward((back_other, swapped(after([back_other], [front_near])[0], 1)), far_back)
     chip = (back_far[0].astype(f32) + swapped(back_far[1], 1).astype(f32)).astype(bf16)
-    front_other = after([swapped(front_near, 2)], back_far[:1])[0]
+    front_other = after([swapped(front_near, 2)], [back_near[0], there_middle])[0]
 
     front_small, back_small = after([front_small, back_small], [front_near])
     there_small = passed_along(front_small, 1)

time: 209 us -> 213 us (1.019)
  waiting for transfers between devices: 91.5 us -> 109 us
  starting transfers between devices: 62.6 us -> 51.1 us
  Pallas kernels: 41 us -> 37 us
    ppermute x9, waiting for transfers between devices: 31.8 us -> 53.3 us  [turned(): lax.ppermute(array, 'expert', [(i, (i + by * GROUP) % length) for i in ra...]
    ppermute x9, starting transfers between devices: 22 us -> 7.65 us  [turned(): lax.ppermute(array, 'expert', [(i, (i + by * GROUP) % length) for i in ra...]
    pallas_call x15, Pallas kernels: 41 us -> 37 us  [call(): pl.pallas_call(body, out_shape=shapes, in_specs=specs, out_specs=[pl.Bloc...]
    ppermute x13, waiting for transfers between devices: 36.5 us -> 33.7 us  [passed_along(): return lax.ppermute(array, ('section', 'expert'), pairs)]
    ppermute x17 -> x18, starting transfers between devices: 8.86 us -> 10.4 us  [swapped(): lax.ppermute(array, 'expert', [(i, i ^ bit) for i in range(lax.axis_size(...]
    ppermute x17 -> x18, waiting for transfers between devices: 23.2 us -> 21.9 us  [swapped(): lax.ppermute(array, 'expert', [(i, i ^ bit) for i in range(lax.axis_size(...]
    unnamed x58 -> x70, local copies, waits for them, and re-layouts: 8.93 us -> 9.91 us
  transfers between devices with their start and end apart: 42 -> 43, of which waited for: 15 -> 18; matrix products, arithmetic and copies ran while one was open for 2% -> 2% of each run, Pallas kernels for 15% -> 15%
where the time goes in v12:
time: 213 us; the launch traced here: 212 us
  waiting for transfers between devices  109 us (51%)
  starting transfers between devices  51.1 us (24%)
  Pallas kernels  37 us (17%)
  local copies, waits for them, and re-layouts  12.2 us (6%)
    ppermute x9, waiting for transfers between devices, turned(): lax.ppermute(array, 'expert', [(i, (i + by * GROUP) % length) for i in ra...  53.3 us
    pallas_call x15, Pallas kernels, call(): pl.pallas_call(body, out_shape=shapes, in_specs=specs, out_specs=[pl.Bloc...  37 us
    ppermute x13, waiting for transfers between devices, passed_along(): return lax.ppermute(array, ('section', 'expert'), pairs)  33.7 us
    ppermute x13, starting transfers between devices, passed_along(): return lax.ppermute(array, ('section', 'expert'), pairs)  22.4 us
    ppermute x18, waiting for transfers between devices, swapped(): lax.ppermute(array, 'expert', [(i, i ^ bit) for i in range(lax.axis_size(...  21.9 us
    ppermute x3, starting transfers between devices, shards(): column.append(lax.ppermute(keys_values[0], 'expert', pairs))  10.7 us
    ppermute x18, starting transfers between devices, swapped(): lax.ppermute(array, 'expert', [(i, i ^ bit) for i in range(lax.axis_size(...  10.4 us
    unnamed x70, local copies, waits for them, and re-layouts  9.91 us
  transfers between devices with their start and end apart: 43, of which 18 were waited for; matrix products, arithmetic and copies ran while one was open for 2% of the time, Pallas kernels for 15%

profile of v12, /device:TPU:0, one launch (start us, length us, event | category | flops | bytes accessed | tf_op | source)
XLA Modules:
  0.0 212.5 jit_solution(14447607714928152879)
XLA Ops:
  0.6 1.0 copy.16
  1.6 4.9 %collective-permute-start = (bf16[128,448]{1,0:T(8,128)(2,1)S(1)}, bf16[128,448]{1,0:T(8,128)(2,1)S(1)}, u32[]{:S(2)}, u32[]{:S(2)}) collective-permute-start(bf16[128,448]{1,0:T(8,128)(2,1)S(1)} %bitcast.46), channel_id=1, source_target_pairs={{0,4},{1,5},{2,6},{3,7},{4,8},{5,9},{6,10},{7,11},{8,12},{9,13},{1... | collective-permute-start | bytes 344072 | tf_op jit(solution)/shard_map/ppermute | solution.py:379
  6.6 4.5 %collective-permute-start.1 = (bf16[128,448]{1,0:T(8,128)(2,1)S(1)}, bf16[128,448]{1,0:T(8,128)(2,1)S(1)}, u32[]{:S(2)}, u32[]{:S(2)}) collective-permute-start(bf16[128,448]{1,0:T(8,128)(2,1)S(1)} %bitcast.47), channel_id=1, source_target_pairs={{0,8},{1,9},{2,10},{3,11},{4,12},{5,13},{6,14},{7,15},{16,24},{17,... | collective-permute-start | bytes 344072 | tf_op jit(solution)/shard_map/ppermute | solution.py:379
  11.1 1.3 collective-permute-start.2
  12.4 0.8 copy.17.gate_ref
  13.8 0.7 copy-done.5
  14.6 1.2 copy-done.9
  15.7 3.0 %shard_map.149 = (bf16[144,896]{1,0:T(8,128)(2,1)S(1)}, bf16[144,896]{1,0:T(8,128)(2,1)S(1)}, bf16[144,896]{1,0:T(8,128)(2,1)S(1)}, bf16[144,896]{1,0:T(8,128)(2...) custom-call(s32[1,128]{1,0:T(1,128)S(1)} %get-tuple-element.177.rout, ...), custom_call_target="tpu_custom_call" | custom-call | flops 2113929216 | bytes 3914752 | tf_op jit(solution)/shard_map/pallas_call | solution.py:55
  19.6 1.6 collective-permute-start.3
  21.2 3.1 %collective-permute-start.6 = (bf16[144,896]{1,0:T(8,128)(2,1)S(1)}, bf16[144,896]{1,0:T(8,128)(2,1)S(1)}, u32[]{:S(2)}, u32[]{:S(2)}) collective-permute-start(bf16[144,896]{1,0:T(8,128)(2,1)S(1)} %get-tuple-element.102), channel_id=1, source_target_pairs={{0,8},{1,9},{2,10},{3,11},{4,12},{5,13},{6,14},{7,15},{8,0},{9,1},... | collective-permute-start | bytes 774152 | tf_op jit(solution)/shard_map/ppermute | solution.py:42
  24.3 1.1 slice_bitcast_fusion
  25.4 6.8 %collective-permute-done.5.refs_1_ = bf16[144,896]{1,0:T(8,128)(2,1)S(1)} collective-permute-done((bf16[144,896]{1,0:T(8,128)(2,1)S(1)}, bf16[144,896]{1,0:T(8,128)(2,1)S(1)}, u32[]{:S(2)}, u32[]{:S(2)}) %collective-permute-start.5) | collective-permute-done | bytes 258080 | tf_op jit(solution)/shard_map/ppermute | solution.py:42
  33.4 7.2 %collective-permute-done.6.refs_2_ = bf16[144,896]{1,0:T(8,128)(2,1)S(1)} collective-permute-done((bf16[144,896]{1,0:T(8,128)(2,1)S(1)}, bf16[144,896]{1,0:T(8,128)(2,1)S(1)}, u32[]{:S(2)}, u32[]{:S(2)}) %collective-permute-start.6) | collective-permute-done | bytes 258080 | tf_op jit(solution)/shard_map/ppermute | solution.py:42
  41.4 1.5 collective-permute-start.17
  43.7 1.2 collective-permute-done.4.kv2
  44.9 1.0 collective-permute-done.7.kv3
  45.9 1.2 copy-done.7
  47.1 1.2 copy-done.8
  48.3 8.5 %shard_map.150 = (bf16[128,3584]{1,0:T(8,128)(2,1)S(1)}, bf16[144,896]{1,0:T(8,128)(2,1)S(1)}, bf16[144,896]{1,0:T(8,128)(2,1)S(1)}, bf16[144,896]{1,0:T(8,128)(2,1)S(1)}, bf16[144,896]{1,0:T(8,128)(2,1)S(1)}) custom-call(s32[16]{0:T(128)S(1)} %reshape_squeeze.6.chosen_ref, s32[16]{0:T(128)S(1)} %fusion.10.index_ref, s32[1]{0:T(128)} %bitcast.4.base_ref, ...), custom_call_target="tpu_custom_call" | custom-call | flops 1593835520 | bytes 5634692 | tf_op jit(solution)/shard_map/pallas_call | solution.py:55
  56.9 1.3 collective-permute-start.14
  58.2 0.8 collective-permute-start.9
  58.9 2.0 shard_map.151.first_ref
  61.0 2.4 %collective-permute-done.17.middle_ref = bf16[128,3584]{1,0:T(8,128)(2,1)} collective-permute-done((bf16[128,3584]{1,0:T(8,128)(2,1)}, bf16[128,3584]{1,0:T(8,128)(2,1)}, u32[]{:S(2)}, u32[]{:S(2)}) %collective-permute-start.17) | collective-permute-done | bytes 917536 | tf_op jit(solution)/shard_map/ppermute | solution.py:33
  63.9 1.9 collective-permute-done.15.refs_3_
  65.8 14.8 %collective-permute-done.14.refs_2_ = bf16[144,896]{1,0:T(8,128)(2,1)S(1)} collective-permute-done((bf16[144,896]{1,0:T(8,128)(2,1)S(1)}, bf16[144,896]{1,0:T(8,128)(2,1)S(1)}, u32[]{:S(2)}, u32[]{:S(2)}) %collective-permute-start.14) | collective-permute-done | bytes 258080 | tf_op jit(solution)/shard_map/ppermute | solution.py:42
  80.6 1.1 shard_map.152.first_ref
  83.3 1.9 collective-permute-start.11
  85.2 8.7 %collective-permute-done.10.refs_1_ = bf16[144,896]{1,0:T(8,128)(2,1)S(1)} collective-permute-done((bf16[144,896]{1,0:T(8,128)(2,1)S(1)}, bf16[144,896]{1,0:T(8,128)(2,1)S(1)}, u32[]{:S(2)}, u32[]{:S(2)}) %collective-permute-start.10) | collective-permute-done | bytes 258080 | tf_op jit(solution)/shard_map/ppermute | solution.py:42
  94.0 8.4 %collective-permute-done.11.refs_2_ = bf16[144,896]{1,0:T(8,128)(2,1)S(1)} collective-permute-done((bf16[144,896]{1,0:T(8,128)(2,1)S(1)}, bf16[144,896]{1,0:T(8,128)(2,1)S(1)}, u32[]{:S(2)}, u32[]{:S(2)}) %collective-permute-start.11) | collective-permute-done | bytes 258080 | tf_op jit(solution)/shard_map/ppermute | solution.py:42
  102.3 5.5 %collective-permute-done.12.refs_3_ = bf16[144,896]{1,0:T(8,128)(2,1)S(1)} collective-permute-done((bf16[144,896]{1,0:T(8,128)(2,1)S(1)}, bf16[144,896]{1,0:T(8,128)(2,1)S(1)}, u32[]{:S(2)}, u32[]{:S(2)}) %collective-permute-start.12) | collective-permute-done | bytes 258080 | tf_op jit(solution)/shard_map/ppermute | solution.py:42
  107.9 1.1 shard_map.153.first_ref
  109.6 1.5 collective-permute-start.23
  111.1 1.5 collective-permute-start.21
  112.8 1.3 shard_map.155
  114.9 2.4 %shard_map.156 = (bf16[144,3584]{1,0:T(8,128)(2,1)S(1)}, bf16[144,3584]{1,0:T(8,128)(2,1)S(1)}) custom-call(bf16[144,3584]{1,0:T(8,128)(2,1)S(1)} %shard_map.151.first_ref, bf16[144,3584]{1,0:T(8,128)(2,1)S(1)} %collective-permute-done.24.second_ref, f32[288,256]{1,0:T(8,128)S(1)} %get-tuple-element.143.back_ref, bf16[3584,256]{1,0:T(8,128)(2,1)S(1)} %bitcast.34, ...), custom_call_target="tpu_custom_call" | custom-call | flops 2113929216 | bytes 8093696 | tf_op jit(solution)/shard_map/pallas_call | solution.py:55
  117.3 1.0 copy-done.3
  118.3 15.5 %collective-permute-done.21.middle_ref = bf16[128,3584]{1,0:T(8,128)(2,1)S(1)} collective-permute-done((bf16[128,3584]{1,0:T(8,128)(2,1)S(1)}, bf16[128,3584]{1,0:T(8,128)(2,1)S(1)}, u32[]{:S(2)}, u32[]{:S(2)}) %collective-permute-start.21) | collective-permute-done | bytes 917536 | tf_op jit(solution)/shard_map/ppermute | solution.py:33
  133.8 1.4 collective-permute-done.23.first_ref
  135.2 2.3 %collective-permute-done.30.back_ref = bf16[288,256]{1,0:T(8,128)(2,1)S(1)} collective-permute-done((bf16[288,256]{1,0:T(8,128)(2,1)S(1)}, bf16[288,256]{1,0:T(8,128)(2,1)S(1)}, u32[]{:S(2)}, u32[]{:S(2)}) %collective-permute-start.30) | collective-permute-done | bytes 147488 | tf_op jit(solution)/shard_map/ppermute | solution.py:37
  137.5 2.5 %shard_map.158 = (bf16[144,3584]{1,0:T(8,128)(2,1)S(1)}, bf16[144,3584]{1,0:T(8,128)(2,1)S(1)}) custom-call(bf16[144,3584]{1,0:T(8,128)(2,1)S(1)} %collective-permute-done.13.first_ref, bf16[144,3584]{1,0:T(8,128)(2,1)S(1)} %collective-permute-done.29.second_ref, bf16[288,256]{1,0:T(8,128)(2,1)S(1)} %collective-permute-done.30.back_ref, ...), custom_call_target="tpu_custom_call" | custom-call | flops 2113929216 | bytes 7946240 | tf_op jit(solution)/shard_map/pallas_call | solution.py:55
  140.1 1.6 collective-permute-start.28
  142.2 1.2 shard_map.154.own_ref
  143.5 1.3 shard_map.157
  144.7 1.6 collective-permute-start.27
  146.3 1.2 add_convert_fusion
  147.5 3.0 %collective-permute-done.27.other_ref = bf16[288,256]{1,0:T(8,128)(2,1)S(1)} collective-permute-done((bf16[288,256]{1,0:T(8,128)(2,1)S(1)}, bf16[288,256]{1,0:T(8,128)(2,1)S(1)}, u32[]{:S(2)}, u32[]{:S(2)}) %collective-permute-start.27) | collective-permute-done | bytes 147488 | tf_op jit(solution)/shard_map/ppermute | solution.py:37
  150.5 1.2 shard_map.159
  152.3 1.5 collective-permute-start.38
  154.4 1.9 shard_map.160
  156.3 1.5 collective-permute-start.33
  157.8 2.9 %collective-permute-start.34 = (bf16[144,896]{1,0:T(8,128)(2,1)}, bf16[144,896]{1,0:T(8,128)(2,1)}, u32[]{:S(2)}, u32[]{:S(2)}) collective-permute-start(bf16[144,896]{1,0:T(8,128)(2,1)} %get-tuple-element.156), channel_id=1, source_target_pairs={{0,28},{1,29},{2,30},{3,31},{4,16},{5,17},{6,18},{7,19},{8,20},{9,... | collective-permute-start | bytes 774152 | tf_op jit(solution)/shard_map/ppermute | solution.py:33
  160.7 2.0 collective-permute-start.35
  162.7 2.0 collective-permute-start.36
  164.9 12.4 %collective-permute-done.38.refs_2_ = bf16[144,3584]{1,0:T(8,128)(2,1)S(1)} collective-permute-done((bf16[144,3584]{1,0:T(8,128)(2,1)}, bf16[144,3584]{1,0:T(8,128)(2,1)S(1)}, u32[]{:S(2)}, u32[]{:S(2)}) %collective-permute-start.38) | collective-permute-done | bytes 1032224 | tf_op jit(solution)/shard_map/ppermute | solution.py:37
  177.3 2.1 shard_map.161
  179.4 1.5 collective-permute-start.39
  180.9 4.4 %collective-permute-start.40 = (bf16[144,896]{1,0:T(8,128)(2,1)}, bf16[144,896]{1,0:T(8,128)(2,1)S(1)}, u32[]{:S(2)}, u32[]{:S(2)}) collective-permute-start(bf16[144,896]{1,0:T(8,128)(2,1)} %get-tuple-element.165), channel_id=1, source_target_pairs={{0,28},{1,29},{2,30},{3,31},{4,16},{5,17},{6,18},{7,19},{8,20},{9,... | collective-permute-start | bytes 774152 | tf_op jit(solution)/shard_map/ppermute | solution.py:33
  185.4 1.0 collective-permute-start.41
  186.3 1.4 collective-permute-start.42
  187.9 1.2 copy-done.14
  189.2 3.6 %shard_map.162 = bf16[128,3584]{1,0:T(8,128)(2,1)} custom-call(s32[128,1]{1,0:T(8,128)S(1)} %copy.18.route_ref, f32[128,1]{1,0:T(8,128)S(1)} %copy.19.gate_ref, bf16[128,3584]{1,0:T(8,128)(2,1)S(1)} %copy-done.14, bf16[144,896]{1,0:T(8,128)(2,1)} %collective-permute-done.33.refs_0_, bf16[144,896]{1,0:T(8,128)(2,1)} %collective-permute-done.34.refs_1_, ...), custom_call_target="tpu_custom_call" | custom-call | flops 1056964608 | bytes 2868224 | tf_op jit(solution)/shard_map/pallas_call | solution.py:55
  192.7 6.6 %collective-permute-done.39.refs_0_ = bf16[144,896]{1,0:T(8,128)(2,1)S(1)} collective-permute-done((bf16[144,896]{1,0:T(8,128)(2,1)}, bf16[144,896]{1,0:T(8,128)(2,1)S(1)}, u32[]{:S(2)}, u32[]{:S(2)}) %collective-permute-start.39) | collective-permute-done | bytes 258080 | tf_op jit(solution)/shard_map/ppermute | solution.py:33
  199.3 9.3 %collective-permute-done.41.refs_2_ = bf16[144,896]{1,0:T(8,128)(2,1)S(1)} collective-permute-done((bf16[144,896]{1,0:T(8,128)(2,1)}, bf16[144,896]{1,0:T(8,128)(2,1)S(1)}, u32[]{:S(2)}, u32[]{:S(2)}) %collective-permute-start.41) | collective-permute-done | bytes 258080 | tf_op jit(solution)/shard_map/ppermute | solution.py:33
  208.6 3.9 %shard_map.163 = bf16[128,3584]{1,0:T(8,128)(2,1)} custom-call(s32[128,1]{1,0:T(8,128)S(1)} %copy.20.route_ref, f32[1,3584]{1,0:T(1,128)S(1)} %slice.35.gain_ref, bf16[128,3584]{1,0:T(8,128)(2,1)} %collective-permute-done.17.middle_ref, bf16[128,3584]{1,0:T(8,128)(2,1)S(1)} %copy-done.12, bf16[144,896]{1,0:T(8,128)(2,1)S(1)} %collective-permute-done.39.refs_0_, ...), custom_call_target="tpu_custom_call" | custom-call | flops 1056964608 | bytes 3799552 | tf_op jit(solution)/shard_map/pallas_call | solution.py:55
  (125 shorter events, 10.2 us)
Async XLA Ops:
  1.6 17.9 %collective-permute-start = (bf16[128,448]{1,0:T(8,128)(2,1)S(1)}, bf16[128,448]{1,0:T(8,128)(2,1)S(1)}, u32[]{:S(2)}, u32[]{:S(2)}) collective-permute-start(bf16[128,448]{1,0:T(8,128)(2,1)S(1)} %bitcast.46), channel_id=1, source_target_pairs={{0,4},{1,5},{2,6},{3,7},{4,8},{5,9},{6,10},{7,11},{8,12},{9,13},{1... | collective-permute-start | bytes 344072 | tf_op jit(solution)/shard_map/ppermute | solution.py:379
  6.6 12.9 %collective-permute-start.1 = (bf16[128,448]{1,0:T(8,128)(2,1)S(1)}, bf16[128,448]{1,0:T(8,128)(2,1)S(1)}, u32[]{:S(2)}, u32[]{:S(2)}) collective-permute-start(bf16[128,448]{1,0:T(8,128)(2,1)S(1)} %bitcast.47), channel_id=1, source_target_pairs={{0,8},{1,9},{2,10},{3,11},{4,12},{5,13},{6,14},{7,15},{16,24},{17,... | collective-permute-start | bytes 344072 | tf_op jit(solution)/shard_map/ppermute | solution.py:379
  11.1 8.5 %collective-permute-start.2 = (bf16[128,448]{1,0:T(8,128)(2,1)S(1)}, bf16[128,448]{1,0:T(8,128)(2,1)S(1)}, u32[]{:S(2)}, u32[]{:S(2)}) collective-permute-start(bf16[128,448]{1,0:T(8,128)(2,1)S(1)} %bitcast.48), channel_id=1, source_target_pairs={{0,12},{1,13},{2,14},{3,15},{16,28},{17,29},{18,30},{19,31}} | collective-permute-start | bytes 344072 | tf_op jit(solution)/shard_map/ppermute | solution.py:379
  15.7 8.6 %copy-start = (bf16[1,1,256,3584]{3,2,1,0:T(8,128)(2,1)S(1)}, bf16[1,1,256,3584]{3,2,1,0:T(8,128)(2,1)}, u32[]{:S(2)}) copy-start(bf16[1,1,256,3584]{3,2,1,0:T(8,128)(2,1)} %param.27) | copy-start | bytes 5505028
  19.5 23.4 %copy-start.15 = (bf16[144,896]{1,0:T(8,128)(2,1)}, bf16[144,896]{1,0:T(8,128)(2,1)S(1)}, u32[]{:S(2)}) copy-start(bf16[144,896]{1,0:T(8,128)(2,1)S(1)} %get-tuple-element.113) | copy-start | bytes 774148
  19.5 23.4 %copy-start.17 = (bf16[144,896]{1,0:T(8,128)(2,1)}, bf16[144,896]{1,0:T(8,128)(2,1)S(1)}, u32[]{:S(2)}) copy-start(bf16[144,896]{1,0:T(8,128)(2,1)S(1)} %get-tuple-element.124) | copy-start | bytes 774148
  19.5 23.4 %copy-start.19 = (bf16[144,896]{1,0:T(8,128)(2,1)}, bf16[144,896]{1,0:T(8,128)(2,1)S(1)}, u32[]{:S(2)}) copy-start(bf16[144,896]{1,0:T(8,128)(2,1)S(1)} %get-tuple-element.126) | copy-start | bytes 774148
  19.5 23.5 %copy-start.21 = (bf16[144,896]{1,0:T(8,128)(2,1)}, bf16[144,896]{1,0:T(8,128)(2,1)S(1)}, u32[]{:S(2)}) copy-start(bf16[144,896]{1,0:T(8,128)(2,1)S(1)} %get-tuple-element.110) | copy-start | bytes 774148
  19.5 23.5 %copy-start.28 = (bf16[144,896]{1,0:T(8,128)(2,1)}, bf16[144,896]{1,0:T(8,128)(2,1)S(1)}, u32[]{:S(2)}) copy-start(bf16[144,896]{1,0:T(8,128)(2,1)S(1)} %get-tuple-element.118.refs_0_) | copy-start | bytes 774148
  19.5 24.0 %copy-start.30 = (s32[1,2,2,4]{3,2,1,0:T(2,128)S(1)}, s32[1,2,2,4]{3,2,1,0:T(2,128)}, u32[]{:S(2)}) copy-start(s32[1,2,2,4]{3,2,1,0:T(2,128)} %param.17) | copy-start | bytes 196
  19.5 24.1 %copy-start.32 = (s32[1,128,1]{1,2,0:T(1,128)S(1)}, s32[1,128,1]{1,2,0:T(1,128)}, u32[]{:S(2)}) copy-start(s32[1,128,1]{1,2,0:T(1,128)} %param.18) | copy-start | bytes 1540
  19.5 26.4 %copy-start.6 = (f32[1,3584]{1,0:T(1,128)S(1)}, f32[1,3584]{1,0:T(1,128)}, u32[]{:S(2)}) copy-start(f32[1,3584]{1,0:T(1,128)} %gain_ref.3) | copy-start | bytes 43012
  19.6 23.3 %collective-permute-start.3 = (bf16[512,448]{1,0:T(8,128)(2,1)S(1)}, bf16[512,448]{1,0:T(8,128)(2,1)}, u32[]{:S(2)}, u32[]{:S(2)}) collective-permute-start(bf16[512,448]{1,0:T(8,128)(2,1)S(1)} %constant_dynamic-update-slice_fusion.kv0), channel_id=1, source_target_pairs={{0,2},{1,3},{2,0},{3,1},{4,6},{5,7},{6,4},{7,5},{8,10},{9,11},{10,... | collective-permute-start | bytes 1376264 | tf_op jit(solution)/shard_map/ppermute | solution.py:37
  21.2 11.0 %collective-permute-start.5 = (bf16[144,896]{1,0:T(8,128)(2,1)S(1)}, bf16[144,896]{1,0:T(8,128)(2,1)S(1)}, u32[]{:S(2)}, u32[]{:S(2)}) collective-permute-start(bf16[144,896]{1,0:T(8,128)(2,1)S(1)} %get-tuple-element.101), channel_id=1, source_target_pairs={{0,4},{1,5},{2,6},{3,7},{4,8},{5,9},{6,10},{7,11},{8,12},{9,13},{1... | collective-permute-start | bytes 774152 | tf_op jit(solution)/shard_map/ppermute | solution.py:42
  21.2 19.5 %collective-permute-start.6 = (bf16[144,896]{1,0:T(8,128)(2,1)S(1)}, bf16[144,896]{1,0:T(8,128)(2,1)S(1)}, u32[]{:S(2)}, u32[]{:S(2)}) collective-permute-start(bf16[144,896]{1,0:T(8,128)(2,1)S(1)} %get-tuple-element.102), channel_id=1, source_target_pairs={{0,8},{1,9},{2,10},{3,11},{4,12},{5,13},{6,14},{7,15},{8,0},{9,1},... | collective-permute-start | bytes 774152 | tf_op jit(solution)/shard_map/ppermute | solution.py:42
  32.9 47.7 %collective-permute-start.16 = (bf16[160,3584]{1,0:T(8,128)(2,1)}, bf16[160,3584]{1,0:T(8,128)(2,1)S(1)}, u32[]{:S(2)}, u32[]{:S(2)}) collective-permute-start(bf16[160,3584]{1,0:T(8,128)(2,1)} %slice_bitcast_fusion), channel_id=1, source_target_pairs={{0,2},{1,3},{2,0},{3,1},{4,6},{5,7},{6,4},{7,5},{8,10},{9,11},{10,... | collective-permute-start | bytes 3440648 | tf_op jit(solution)/shard_map/ppermute | solution.py:37
  41.4 22.0 %collective-permute-start.17 = (bf16[128,3584]{1,0:T(8,128)(2,1)}, bf16[128,3584]{1,0:T(8,128)(2,1)}, u32[]{:S(2)}, u32[]{:S(2)}) collective-permute-start(bf16[128,3584]{1,0:T(8,128)(2,1)} %bitcast.10.middle_ref), channel_id=1, source_target_pairs={{0,16},{1,17},{2,18},{3,19},{4,20},{5,21},{6,22},{7,23},{8,24},{9,... | collective-permute-start | bytes 2752520 | tf_op jit(solution)/shard_map/ppermute | solution.py:33
  42.9 2.0 collective-permute-start.4
  42.9 3.0 %collective-permute-start.7 = (bf16[512,448]{1,0:T(8,128)(2,1)}, bf16[512,448]{1,0:T(8,128)(2,1)}, u32[]{:S(2)}, u32[]{:S(2)}) collective-permute-start(bf16[512,448]{1,0:T(8,128)(2,1)} %collective-permute-done.3.kv1), channel_id=1, source_target_pairs={{0,1},{1,0},{2,3},{3,2},{4,5},{5,4},{6,7},{7,6},{8,9},{9,8},{10,11... | collective-permute-start | bytes 1376264 | tf_op jit(solution)/shard_map/ppermute | solution.py:37
  43.6 14.6 %collective-permute-start.8 = (bf16[144,896]{1,0:T(8,128)(2,1)}, bf16[144,896]{1,0:T(8,128)(2,1)}, u32[]{:S(2)}, u32[]{:S(2)}) collective-permute-start(bf16[144,896]{1,0:T(8,128)(2,1)} %copy-done.21), channel_id=1, source_target_pairs={{0,12},{1,13},{2,14},{3,15},{4,0},{5,1},{6,2},{7,3},{8,4},{9,5},{1... | collective-permute-start | bytes 774152 | tf_op jit(solution)/shard_map/ppermute | solution.py:42
  48.2 8.5 %copy-start.20 = (bf16[144,896]{1,0:T(8,128)(2,1)S(1)}, bf16[144,896]{1,0:T(8,128)(2,1)}, u32[]{:S(2)}) copy-start(bf16[144,896]{1,0:T(8,128)(2,1)} %copy-done.19) | copy-start | bytes 774148
  48.3 8.6 %copy-start.18 = (bf16[144,896]{1,0:T(8,128)(2,1)S(1)}, bf16[144,896]{1,0:T(8,128)(2,1)}, u32[]{:S(2)}) copy-start(bf16[144,896]{1,0:T(8,128)(2,1)} %copy-done.17) | copy-start | bytes 774148
  48.3 9.9 %copy-start.16 = (bf16[144,896]{1,0:T(8,128)(2,1)S(1)}, bf16[144,896]{1,0:T(8,128)(2,1)}, u32[]{:S(2)}) copy-start(bf16[144,896]{1,0:T(8,128)(2,1)} %copy-done.15) | copy-start | bytes 774148
  48.3 10.7 %copy-start.23 = (bf16[144,896]{1,0:T(8,128)(2,1)S(1)}, bf16[144,896]{1,0:T(8,128)(2,1)}, u32[]{:S(2)}) copy-start(bf16[144,896]{1,0:T(8,128)(2,1)} %copy-done.22) | copy-start | bytes 774148
  48.3 10.7 %copy-start.25 = (bf16[144,896]{1,0:T(8,128)(2,1)S(1)}, bf16[144,896]{1,0:T(8,128)(2,1)}, u32[]{:S(2)}) copy-start(bf16[144,896]{1,0:T(8,128)(2,1)} %copy-done.24) | copy-start | bytes 774148
  48.3 10.7 %copy-start.29 = (bf16[144,896]{1,0:T(8,128)(2,1)S(1)}, bf16[144,896]{1,0:T(8,128)(2,1)}, u32[]{:S(2)}) copy-start(bf16[144,896]{1,0:T(8,128)(2,1)} %copy-done.28) | copy-start | bytes 774148
  56.8 23.8 %copy-start.27 = (bf16[144,896]{1,0:T(8,128)(2,1)S(1)}, bf16[144,896]{1,0:T(8,128)(2,1)}, u32[]{:S(2)}) copy-start(bf16[144,896]{1,0:T(8,128)(2,1)} %copy-done.26) | copy-start | bytes 774148
  56.8 9.0 %collective-permute-start.15 = (bf16[144,896]{1,0:T(8,128)(2,1)S(1)}, bf16[144,896]{1,0:T(8,128)(2,1)S(1)}, u32[]{:S(2)}, u32[]{:S(2)}) collective-permute-start(bf16[144,896]{1,0:T(8,128)(2,1)S(1)} %copy-done.20), channel_id=1, source_target_pairs={{0,12},{1,13},{2,14},{3,15},{4,0},{5,1},{6,2},{7,3},{8,4},{9,5},{1... | collective-permute-start | bytes 774152 | tf_op jit(solution)/shard_map/ppermute | solution.py:42
  56.9 23.7 %collective-permute-start.14 = (bf16[144,896]{1,0:T(8,128)(2,1)S(1)}, bf16[144,896]{1,0:T(8,128)(2,1)S(1)}, u32[]{:S(2)}, u32[]{:S(2)}) collective-permute-start(bf16[144,896]{1,0:T(8,128)(2,1)S(1)} %copy-done.18), channel_id=1, source_target_pairs={{0,8},{1,9},{2,10},{3,11},{4,12},{5,13},{6,14},{7,15},{8,0},{9,1},... | collective-permute-start | bytes 774152 | tf_op jit(solution)/shard_map/ppermute | solution.py:42
  58.2 22.4 %collective-permute-start.9 = (bf16[144,896]{1,0:T(8,128)(2,1)S(1)}, bf16[144,896]{1,0:T(8,128)(2,1)S(1)}, u32[]{:S(2)}, u32[]{:S(2)}) collective-permute-start(bf16[144,896]{1,0:T(8,128)(2,1)S(1)} %copy-done.16), channel_id=1, source_target_pairs={{0,4},{1,5},{2,6},{3,7},{4,8},{5,9},{6,10},{7,11},{8,12},{9,13},{1... | collective-permute-start | bytes 774152 | tf_op jit(solution)/shard_map/ppermute | solution.py:42
  61.0 20.7 %copy-start.10 = (bf16[1,128,3584]{2,1,0:T(8,128)(2,1)S(1)}, bf16[1,128,3584]{2,1,0:T(8,128)(2,1)}, u32[]{:S(2)}) copy-start(bf16[1,128,3584]{2,1,0:T(8,128)(2,1)} %param.21) | copy-start | bytes 2752516
  63.4 44.5 %collective-permute-start.13 = (bf16[144,3584]{1,0:T(8,128)(2,1)S(1)}, bf16[144,3584]{1,0:T(8,128)(2,1)S(1)}, u32[]{:S(2)}, u32[]{:S(2)}) collective-permute-start(bf16[144,3584]{1,0:T(8,128)(2,1)S(1)} %shard_map.151.first_ref), channel_id=1, source_target_pairs={{0,2},{1,3},{2,0},{3,1},{4,6},{5,7},{6,4},{7,5},{8,10},{9,11},{10,... | collective-permute-start | bytes 3096584 | tf_op jit(solution)/shard_map/ppermute | solution.py:37
  81.7 26.2 %collective-permute-start.18 = (bf16[128,3584]{1,0:T(8,128)(2,1)S(1)}, bf16[128,3584]{1,0:T(8,128)(2,1)S(1)}, u32[]{:S(2)}, u32[]{:S(2)}) collective-permute-start(bf16[128,3584]{1,0:T(8,128)(2,1)S(1)} %bitcast.45), channel_id=1, source_target_pairs={{0,16},{1,17},{2,18},{3,19},{4,20},{5,21},{6,22},{7,23},{8,24},{9,... | collective-permute-start | bytes 2752520 | tf_op jit(solution)/shard_map/ppermute | solution.py:33
  82.3 25.5 %collective-permute-start.19 = (bf16[96,3584]{1,0:T(8,128)(2,1)S(1)}, bf16[96,3584]{1,0:T(8,128)(2,1)S(1)}, u32[]{:S(2)}, u32[]{:S(2)}) collective-permute-start(bf16[96,3584]{1,0:T(8,128)(2,1)S(1)} %slice_bitcast_fusion.1), channel_id=1, source_target_pairs={{0,2},{1,3},{2,0},{3,1},{4,6},{5,7},{6,4},{7,5},{8,10},{9,11},{10,... | collective-permute-start | bytes 2064392 | tf_op jit(solution)/shard_map/ppermute | solution.py:37
  82.9 11.0 %collective-permute-start.10 = (bf16[144,896]{1,0:T(8,128)(2,1)S(1)}, bf16[144,896]{1,0:T(8,128)(2,1)S(1)}, u32[]{:S(2)}, u32[]{:S(2)}) collective-permute-start(bf16[144,896]{1,0:T(8,128)(2,1)S(1)} %get-tuple-element.115), channel_id=1, source_target_pairs={{0,4},{1,5},{2,6},{3,7},{4,8},{5,9},{6,10},{7,11},{8,12},{9,13},{1... | collective-permute-start | bytes 774152 | tf_op jit(solution)/shard_map/ppermute | solution.py:42
  83.3 19.0 %collective-permute-start.11 = (bf16[144,896]{1,0:T(8,128)(2,1)S(1)}, bf16[144,896]{1,0:T(8,128)(2,1)S(1)}, u32[]{:S(2)}, u32[]{:S(2)}) collective-permute-start(bf16[144,896]{1,0:T(8,128)(2,1)S(1)} %get-tuple-element.116), channel_id=1, source_target_pairs={{0,8},{1,9},{2,10},{3,11},{4,12},{5,13},{6,14},{7,15},{8,0},{9,1},... | collective-permute-start | bytes 774152 | tf_op jit(solution)/shard_map/ppermute | solution.py:42
  93.9 13.9 %collective-permute-start.12 = (bf16[144,896]{1,0:T(8,128)(2,1)S(1)}, bf16[144,896]{1,0:T(8,128)(2,1)S(1)}, u32[]{:S(2)}, u32[]{:S(2)}) collective-permute-start(bf16[144,896]{1,0:T(8,128)(2,1)S(1)} %get-tuple-element.117), channel_id=1, source_target_pairs={{0,12},{1,13},{2,14},{3,15},{4,0},{5,1},{6,2},{7,3},{8,4},{9,5},{1... | collective-permute-start | bytes 774152 | tf_op jit(solution)/shard_map/ppermute | solution.py:42
  109.0 3.6 %collective-permute-start.25 = (bf16[144,3584]{1,0:T(8,128)(2,1)S(1)}, bf16[144,3584]{1,0:T(8,128)(2,1)S(1)}, u32[]{:S(2)}, u32[]{:S(2)}) collective-permute-start(bf16[144,3584]{1,0:T(8,128)(2,1)S(1)} %shard_map.152.first_ref), channel_id=1, source_target_pairs={{0,1},{1,0},{2,3},{3,2},{4,5},{5,4},{6,7},{7,6},{8,9},{9,8},{10,11... | collective-permute-start | bytes 3096584 | tf_op jit(solution)/shard_map/ppermute | solution.py:37
  109.1 5.0 %collective-permute-start.24 = (bf16[144,3584]{1,0:T(8,128)(2,1)S(1)}, bf16[144,3584]{1,0:T(8,128)(2,1)S(1)}, u32[]{:S(2)}, u32[]{:S(2)}) collective-permute-start(bf16[144,3584]{1,0:T(8,128)(2,1)S(1)} %shard_map.151.first_ref), channel_id=1, source_target_pairs={{0,1},{1,0},{2,3},{3,2},{4,5},{5,4},{6,7},{7,6},{8,9},{9,8},{10,11... | collective-permute-start | bytes 3096584 | tf_op jit(solution)/shard_map/ppermute | solution.py:37
  109.6 25.7 %collective-permute-start.23 = (bf16[144,3584]{1,0:T(8,128)(2,1)S(1)}, bf16[144,3584]{1,0:T(8,128)(2,1)S(1)}, u32[]{:S(2)}, u32[]{:S(2)}) collective-permute-start(bf16[144,3584]{1,0:T(8,128)(2,1)S(1)} %shard_map.153.first_ref), channel_id=1, source_target_pairs={{0,2},{1,3},{2,0},{3,1},{4,6},{5,7},{6,4},{7,5},{8,10},{9,11},{10,... | collective-permute-start | bytes 3096584 | tf_op jit(solution)/shard_map/ppermute | solution.py:37
  111.0 26.5 %collective-permute-start.29 = (bf16[144,3584]{1,0:T(8,128)(2,1)S(1)}, bf16[144,3584]{1,0:T(8,128)(2,1)S(1)}, u32[]{:S(2)}, u32[]{:S(2)}) collective-permute-start(bf16[144,3584]{1,0:T(8,128)(2,1)S(1)} %collective-permute-done.13.first_ref), channel_id=1, source_target_pairs={{0,1},{1,0},{2,3},{3,2},{4,5},{5,4},{6,7},{7,6},{8,9},{9,8},{10,11... | collective-permute-start | bytes 3096584 | tf_op jit(solution)/shard_map/ppermute | solution.py:37
  111.1 22.8 %collective-permute-start.21 = (bf16[128,3584]{1,0:T(8,128)(2,1)S(1)}, bf16[128,3584]{1,0:T(8,128)(2,1)S(1)}, u32[]{:S(2)}, u32[]{:S(2)}) collective-permute-start(bf16[128,3584]{1,0:T(8,128)(2,1)S(1)} %get-tuple-element.140), channel_id=1, source_target_pairs={{0,16},{1,17},{2,18},{3,19},{4,20},{5,21},{6,22},{7,23},{8,24},{9,... | collective-permute-start | bytes 2752520 | tf_op jit(solution)/shard_map/ppermute | solution.py:33
  112.6 29.7 %collective-permute-start.22 = (bf16[144,3584]{1,0:T(8,128)(2,1)S(1)}, bf16[144,3584]{1,0:T(8,128)(2,1)S(1)}, u32[]{:S(2)}, u32[]{:S(2)}) collective-permute-start(bf16[144,3584]{1,0:T(8,128)(2,1)S(1)} %shard_map.153.first_ref), channel_id=1, source_target_pairs={{0,1},{1,0},{2,3},{3,2},{4,5},{5,4},{6,7},{7,6},{8,9},{9,8},{10,11... | collective-permute-start | bytes 3096584 | tf_op jit(solution)/shard_map/ppermute | solution.py:37
  114.1 23.4 %collective-permute-start.30 = (bf16[288,256]{1,0:T(8,128)(2,1)S(1)}, bf16[288,256]{1,0:T(8,128)(2,1)S(1)}, u32[]{:S(2)}, u32[]{:S(2)}) collective-permute-start(bf16[288,256]{1,0:T(8,128)(2,1)S(1)} %get-tuple-element.148), channel_id=1, source_target_pairs={{0,2},{1,3},{2,0},{3,1},{4,6},{5,7},{6,4},{7,5},{8,10},{9,11},{10,... | collective-permute-start | bytes 442376 | tf_op jit(solution)/shard_map/ppermute | solution.py:37
  133.8 6.2 %copy-start.13 = (bf16[128,3584]{1,0:T(8,128)(2,1)}, bf16[128,3584]{1,0:T(8,128)(2,1)S(1)}, u32[]{:S(2)}) copy-start(bf16[128,3584]{1,0:T(8,128)(2,1)S(1)} %collective-permute-done.21.middle_ref) | copy-start | bytes 2752516
  135.2 4.9 %copy-start.31 = (f32[1,128,1]{1,2,0:T(1,128)S(1)}, f32[1,128,1]{1,2,0:T(1,128)}, u32[]{:S(2)}) copy-start(f32[1,128,1]{1,2,0:T(1,128)} %param.19) | copy-start | bytes 1540
  135.2 8.3 %collective-permute-start.26 = (bf16[144,3584]{1,0:T(8,128)(2,1)S(1)}, bf16[144,3584]{1,0:T(8,128)(2,1)S(1)}, u32[]{:S(2)}, u32[]{:S(2)}) collective-permute-start(bf16[144,3584]{1,0:T(8,128)(2,1)S(1)} %collective-permute-done.23.first_ref), channel_id=1, source_target_pairs={{0,1},{1,0},{2,3},{3,2},{4,5},{5,4},{6,7},{7,6},{8,9},{9,8},{10,11... | collective-permute-start | bytes 3096584 | tf_op jit(solution)/shard_map/ppermute | solution.py:37
  140.0 6.3 %collective-permute-start.31 = (bf16[144,3584]{1,0:T(8,128)(2,1)S(1)}, bf16[144,3584]{1,0:T(8,128)(2,1)S(1)}, u32[]{:S(2)}, u32[]{:S(2)}) collective-permute-start(bf16[144,3584]{1,0:T(8,128)(2,1)S(1)} %get-tuple-element.151), channel_id=1, source_target_pairs={{0,1},{1,0},{2,3},{3,2},{4,5},{5,4},{6,7},{7,6},{8,9},{9,8},{10,11... | collective-permute-start | bytes 3096584 | tf_op jit(solution)/shard_map/ppermute | solution.py:37
  140.1 7.4 %collective-permute-start.28 = (f32[1,3712]{1,0:T(1,128)S(1)}, f32[1,3712]{1,0:T(1,128)S(1)}, u32[]{:S(2)}, u32[]{:S(2)}) collective-permute-start(f32[1,3712]{1,0:T(1,128)S(1)} %pad_maximum_fusion), channel_id=1, source_target_pairs={{0,16},{1,17},{2,18},{3,19},{4,20},{5,21},{6,22},{7,23},{8,24},{9,... | collective-permute-start | bytes 44552 | tf_op jit(solution)/shard_map/ppermute | solution.py:33
  141.7 5.8 %collective-permute-start.20 = (f32[1,256]{1,0:T(1,128)S(1)}, f32[1,256]{1,0:T(1,128)S(1)}, u32[]{:S(2)}, u32[]{:S(2)}) collective-permute-start(f32[1,256]{1,0:T(1,128)S(1)} %maximum_bitcast_fusion), channel_id=1, source_target_pairs={{0,16},{1,17},{2,18},{3,19},{4,20},{5,21},{6,22},{7,23},{8,24},{9,... | collective-permute-start | bytes 3080 | tf_op jit(solution)/shard_map/ppermute | solution.py:33
  144.7 5.7 %collective-permute-start.27 = (bf16[288,256]{1,0:T(8,128)(2,1)S(1)}, bf16[288,256]{1,0:T(8,128)(2,1)S(1)}, u32[]{:S(2)}, u32[]{:S(2)}) collective-permute-start(bf16[288,256]{1,0:T(8,128)(2,1)S(1)} %shard_map.157), channel_id=1, source_target_pairs={{0,2},{1,3},{2,0},{3,1},{4,6},{5,7},{6,4},{7,5},{8,10},{9,11},{10,... | collective-permute-start | bytes 442376 | tf_op jit(solution)/shard_map/ppermute | solution.py:37
  151.7 25.6 %copy-start.4 = (bf16[144,3584]{1,0:T(8,128)(2,1)S(1)}, bf16[144,3584]{1,0:T(8,128)(2,1)}, u32[]{:S(2)}) copy-start(bf16[144,3584]{1,0:T(8,128)(2,1)} %copy-done.3) | copy-start | bytes 3096580
  151.7 2.7 %collective-permute-start.32 = (bf16[144,3584]{1,0:T(8,128)(2,1)S(1)}, bf16[144,3584]{1,0:T(8,128)(2,1)S(1)}, u32[]{:S(2)}, u32[]{:S(2)}) collective-permute-start(bf16[144,3584]{1,0:T(8,128)(2,1)S(1)} %get-tuple-element.154), channel_id=1, source_target_pairs={{0,1},{1,0},{2,3},{3,2},{4,5},{5,4},{6,7},{7,6},{8,9},{9,8},{10,11... | collective-permute-start | bytes 3096584 | tf_op jit(solution)/shard_map/ppermute | solution.py:37
  151.8 10.9 %collective-permute-start.37 = (bf16[144,3584]{1,0:T(8,128)(2,1)S(1)}, bf16[144,3584]{1,0:T(8,128)(2,1)S(1)}, u32[]{:S(2)}, u32[]{:S(2)}) collective-permute-start(bf16[144,3584]{1,0:T(8,128)(2,1)S(1)} %get-tuple-element.159), channel_id=1, source_target_pairs={{0,1},{1,0},{2,3},{3,2},{4,5},{5,4},{6,7},{7,6},{8,9},{9,8},{10,11... | collective-permute-start | bytes 3096584 | tf_op jit(solution)/shard_map/ppermute | solution.py:37
  152.3 25.0 %collective-permute-start.38 = (bf16[144,3584]{1,0:T(8,128)(2,1)}, bf16[144,3584]{1,0:T(8,128)(2,1)S(1)}, u32[]{:S(2)}, u32[]{:S(2)}) collective-permute-start(bf16[144,3584]{1,0:T(8,128)(2,1)} %add_convert_fusion), channel_id=1, source_target_pairs={{0,2},{1,3},{2,0},{3,1},{4,6},{5,7},{6,4},{7,5},{8,10},{9,11},{10,... | collective-permute-start | bytes 3096584 | tf_op jit(solution)/shard_map/ppermute | solution.py:37
  156.3 24.6 %collective-permute-start.33 = (bf16[144,896]{1,0:T(8,128)(2,1)}, bf16[144,896]{1,0:T(8,128)(2,1)}, u32[]{:S(2)}, u32[]{:S(2)}) collective-permute-start(bf16[144,896]{1,0:T(8,128)(2,1)} %get-tuple-element.155), channel_id=1, source_target_pairs={{0,16},{1,17},{2,18},{3,19},{4,20},{5,21},{6,22},{7,23},{8,24},{9,... | collective-permute-start | bytes 774152 | tf_op jit(solution)/shard_map/ppermute | solution.py:33
  157.8 27.5 %collective-permute-start.34 = (bf16[144,896]{1,0:T(8,128)(2,1)}, bf16[144,896]{1,0:T(8,128)(2,1)}, u32[]{:S(2)}, u32[]{:S(2)}) collective-permute-start(bf16[144,896]{1,0:T(8,128)(2,1)} %get-tuple-element.156), channel_id=1, source_target_pairs={{0,28},{1,29},{2,30},{3,31},{4,16},{5,17},{6,18},{7,19},{8,20},{9,... | collective-permute-start | bytes 774152 | tf_op jit(solution)/shard_map/ppermute | solution.py:33
  160.7 25.6 %collective-permute-start.35 = (bf16[144,896]{1,0:T(8,128)(2,1)}, bf16[144,896]{1,0:T(8,128)(2,1)}, u32[]{:S(2)}, u32[]{:S(2)}) collective-permute-start(bf16[144,896]{1,0:T(8,128)(2,1)} %get-tuple-element.157), channel_id=1, source_target_pairs={{0,24},{1,25},{2,26},{3,27},{4,28},{5,29},{6,30},{7,31},{8,16},{9,... | collective-permute-start | bytes 774152 | tf_op jit(solution)/shard_map/ppermute | solution.py:33
  162.7 25.2 %collective-permute-start.36 = (bf16[144,896]{1,0:T(8,128)(2,1)S(1)}, bf16[144,896]{1,0:T(8,128)(2,1)}, u32[]{:S(2)}, u32[]{:S(2)}) collective-permute-start(bf16[144,896]{1,0:T(8,128)(2,1)S(1)} %get-tuple-element.158), channel_id=1, source_target_pairs={{0,20},{1,21},{2,22},{3,23},{4,24},{5,25},{6,26},{7,27},{8,28},{9,... | collective-permute-start | bytes 774152 | tf_op jit(solution)/shard_map/ppermute | solution.py:33
  179.4 19.9 %collective-permute-start.39 = (bf16[144,896]{1,0:T(8,128)(2,1)}, bf16[144,896]{1,0:T(8,128)(2,1)S(1)}, u32[]{:S(2)}, u32[]{:S(2)}) collective-permute-start(bf16[144,896]{1,0:T(8,128)(2,1)} %get-tuple-element.164), channel_id=1, source_target_pairs={{0,16},{1,17},{2,18},{3,19},{4,20},{5,21},{6,22},{7,23},{8,24},{9,... | collective-permute-start | bytes 774152 | tf_op jit(solution)/shard_map/ppermute | solution.py:33
  180.9 18.4 %collective-permute-start.40 = (bf16[144,896]{1,0:T(8,128)(2,1)}, bf16[144,896]{1,0:T(8,128)(2,1)S(1)}, u32[]{:S(2)}, u32[]{:S(2)}) collective-permute-start(bf16[144,896]{1,0:T(8,128)(2,1)} %get-tuple-element.165), channel_id=1, source_target_pairs={{0,28},{1,29},{2,30},{3,31},{4,16},{5,17},{6,18},{7,19},{8,20},{9,... | collective-permute-start | bytes 774152 | tf_op jit(solution)/shard_map/ppermute | solution.py:33
  185.4 23.2 %collective-permute-start.41 = (bf16[144,896]{1,0:T(8,128)(2,1)}, bf16[144,896]{1,0:T(8,128)(2,1)S(1)}, u32[]{:S(2)}, u32[]{:S(2)}) collective-permute-start(bf16[144,896]{1,0:T(8,128)(2,1)} %get-tuple-element.166), channel_id=1, source_target_pairs={{0,24},{1,25},{2,26},{3,27},{4,28},{5,29},{6,30},{7,31},{8,16},{9,... | collective-permute-start | bytes 774152 | tf_op jit(solution)/shard_map/ppermute | solution.py:33
  186.3 22.2 %collective-permute-start.42 = (bf16[144,896]{1,0:T(8,128)(2,1)}, bf16[144,896]{1,0:T(8,128)(2,1)S(1)}, u32[]{:S(2)}, u32[]{:S(2)}) collective-permute-start(bf16[144,896]{1,0:T(8,128)(2,1)} %get-tuple-element.167), channel_id=1, source_target_pairs={{0,20},{1,21},{2,22},{3,23},{4,24},{5,25},{6,26},{7,27},{8,28},{9,... | collective-permute-start | bytes 774152 | tf_op jit(solution)/shard_map/ppermute | solution.py:33
  187.9 20.7 %copy-start.12 = (bf16[128,3584]{1,0:T(8,128)(2,1)S(1)}, bf16[128,3584]{1,0:T(8,128)(2,1)}, u32[]{:S(2)}) copy-start(bf16[128,3584]{1,0:T(8,128)(2,1)} %copy-done.11) | copy-start | bytes 2752516
  (12 other events, 13.7 us)

commit v13 on v12

--- a/solution.py
+++ b/solution.py
@@ -430,6 +430,7 @@
     kv = [column, other_chip, swapped(column, 1), far]
     for k in range(first, experts):
         row_chunks[k] = turned(after([row_chunks[k]], arrived)[0], k)
+    grad_chunks[1] = turned(after([grad_chunks[1]], arrived)[0], 1)
 
     per_device = tokens // BLK
     chosen = selected_blocks[0].reshape(-1)
@@ -465,10 +466,10 @@
     def backward(rows, grads):
         return call(backward_body, [piece, piece], (*rows, grads, w_gate, w_up), flops=4 * work)
 
-    for k in range(1, experts):
+    for k in range(2, experts):
         grad_chunks[k] = turned(after([grad_chunks[k]], [middle])[0], k)
     front_chunks = sent(after(front_chunks, row_chunks + grad_chunks[1:2]))
-    back_rows = joined(after(row_chunks, [middle]))
+    back_rows = joined(after(row_chunks, [middle, grad_chunks[1]]))
     back_other = swapped(back_rows, 2)
     down_low = swapped(after([w_down[cut:]], [back_rows])[0], 2)
     downs = (w_down, down_top, down_low)

time: 213 us -> 208 us (0.977)
  waiting for transfers between devices: 109 us -> 100 us
  starting transfers between devices: 51.1 us -> 54.9 us
    ppermute x9, waiting for transfers between devices: 53.3 us -> 44.4 us  [turned(): lax.ppermute(array, 'expert', [(i, (i + by * GROUP) % length) for i in ra...]
    ppermute x9, starting transfers between devices: 7.65 us -> 11 us  [turned(): lax.ppermute(array, 'expert', [(i, (i + by * GROUP) % length) for i in ra...]
    unnamed x70 -> x68, local copies, waits for them, and re-layouts: 9.91 us -> 9.9 us
  transfers between devices with their start and end apart: 43 -> 43, of which waited for: 18 -> 17; matrix products, arithmetic and copies ran while one was open for 2% -> 2% of each run, Pallas kernels for 15% -> 15%
where the time goes in v13:
time: 208 us
  waiting for transfers between devices  100 us (48%)
  starting transfers between devices  54.9 us (26%)
  Pallas kernels  37 us (18%)
  local copies, waits for them, and re-layouts  12.2 us (6%)
    ppermute x9, waiting for transfers between devices, turned(): lax.ppermute(array, 'expert', [(i, (i + by * GROUP) % length) for i in ra...  44.4 us
    pallas_call x15, Pallas kernels, call(): pl.pallas_call(body, out_shape=shapes, in_specs=specs, out_specs=[pl.Bloc...  37 us
    ppermute x13, waiting for transfers between devices, passed_along(): return lax.ppermute(array, ('section', 'expert'), pairs)  35.1 us
    ppermute x13, starting transfers between devices, passed_along(): return lax.ppermute(array, ('section', 'expert'), pairs)  22.7 us
    ppermute x18, waiting for transfers between devices, swapped(): lax.ppermute(array, 'expert', [(i, i ^ bit) for i in range(lax.axis_size(...  21 us
    ppermute x9, starting transfers between devices, turned(): lax.ppermute(array, 'expert', [(i, (i + by * GROUP) % length) for i in ra...  11 us
    ppermute x3, starting transfers between devices, shards(): column.append(lax.ppermute(keys_values[0], 'expert', pairs))  10.7 us
    ppermute x18, starting transfers between devices, swapped(): lax.ppermute(array, 'expert', [(i, i ^ bit) for i in range(lax.axis_size(...  10.5 us
  transfers between devices with their start and end apart: 43, of which 17 were waited for; matrix products, arithmetic and copies ran while one was open for 2% of the time, Pallas kernels for 15%

profile of v13, /device:TPU:0, one launch (start us, length us, event | category | flops | bytes accessed | tf_op | source)
XLA Modules:
  0.0 207.7 jit_solution(4352759293500494020)
XLA Ops:
  0.6 1.0 copy.16
  1.6 4.9 %collective-permute-start = (bf16[128,448]{1,0:T(8,128)(2,1)S(1)}, bf16[128,448]{1,0:T(8,128)(2,1)S(1)}, u32[]{:S(2)}, u32[]{:S(2)}) collective-permute-start(bf16[128,448]{1,0:T(8,128)(2,1)S(1)} %bitcast.46), channel_id=1, source_target_pairs={{0,4},{1,5},{2,6},{3,7},{4,8},{5,9},{6,10},{7,11},{8,12},{9,13},{1... | collective-permute-start | bytes 344072 | tf_op jit(solution)/shard_map/ppermute | solution.py:379
  6.6 4.5 %collective-permute-start.1 = (bf16[128,448]{1,0:T(8,128)(2,1)S(1)}, bf16[128,448]{1,0:T(8,128)(2,1)S(1)}, u32[]{:S(2)}, u32[]{:S(2)}) collective-permute-start(bf16[128,448]{1,0:T(8,128)(2,1)S(1)} %bitcast.47), channel_id=1, source_target_pairs={{0,8},{1,9},{2,10},{3,11},{4,12},{5,13},{6,14},{7,15},{16,24},{17,... | collective-permute-start | bytes 344072 | tf_op jit(solution)/shard_map/ppermute | solution.py:379
  11.1 1.3 collective-permute-start.2
  12.4 0.8 copy.17.gate_ref
  13.8 0.7 copy-done.5
  14.6 1.2 copy-done.9
  15.7 3.0 %shard_map.149 = (bf16[144,896]{1,0:T(8,128)(2,1)S(1)}, bf16[144,896]{1,0:T(8,128)(2,1)S(1)}, bf16[144,896]{1,0:T(8,128)(2,1)S(1)}, bf16[144,896]{1,0:T(8,128)(2...) custom-call(s32[1,128]{1,0:T(1,128)S(1)} %get-tuple-element.177.rout, ...), custom_call_target="tpu_custom_call" | custom-call | flops 2113929216 | bytes 3914752 | tf_op jit(solution)/shard_map/pallas_call | solution.py:55
  19.6 1.6 collective-permute-start.3
  21.2 3.2 %collective-permute-start.6 = (bf16[144,896]{1,0:T(8,128)(2,1)S(1)}, bf16[144,896]{1,0:T(8,128)(2,1)S(1)}, u32[]{:S(2)}, u32[]{:S(2)}) collective-permute-start(bf16[144,896]{1,0:T(8,128)(2,1)S(1)} %get-tuple-element.102), channel_id=1, source_target_pairs={{0,8},{1,9},{2,10},{3,11},{4,12},{5,13},{6,14},{7,15},{8,0},{9,1},... | collective-permute-start | bytes 774152 | tf_op jit(solution)/shard_map/ppermute | solution.py:42
  24.3 1.1 slice_bitcast_fusion
  25.4 6.8 %collective-permute-done.5.refs_1_ = bf16[144,896]{1,0:T(8,128)(2,1)S(1)} collective-permute-done((bf16[144,896]{1,0:T(8,128)(2,1)S(1)}, bf16[144,896]{1,0:T(8,128)(2,1)S(1)}, u32[]{:S(2)}, u32[]{:S(2)}) %collective-permute-start.5) | collective-permute-done | bytes 258080 | tf_op jit(solution)/shard_map/ppermute | solution.py:42
  32.2 0.7 copy-done.21
  33.4 7.2 %collective-permute-done.6.refs_2_ = bf16[144,896]{1,0:T(8,128)(2,1)S(1)} collective-permute-done((bf16[144,896]{1,0:T(8,128)(2,1)S(1)}, bf16[144,896]{1,0:T(8,128)(2,1)S(1)}, u32[]{:S(2)}, u32[]{:S(2)}) %collective-permute-start.6) | collective-permute-done | bytes 258080 | tf_op jit(solution)/shard_map/ppermute | solution.py:42
  40.7 0.7 copy-done.23
  41.4 1.5 collective-permute-start.17
  43.7 1.2 collective-permute-done.4.kv2
  44.9 2.6 %collective-permute-start.8 = (bf16[144,896]{1,0:T(8,128)(2,1)}, bf16[144,896]{1,0:T(8,128)(2,1)S(1)}, u32[]{:S(2)}, u32[]{:S(2)}) collective-permute-start(bf16[144,896]{1,0:T(8,128)(2,1)} %copy-done.19), channel_id=1, source_target_pairs={{0,12},{1,13},{2,14},{3,15},{4,0},{5,1},{6,2},{7,3},{8,4},{9,5},{1... | collective-permute-start | bytes 774152 | tf_op jit(solution)/shard_map/ppermute | solution.py:42
  47.6 1.2 copy-done.7
  48.8 1.2 copy-done.8
  50.0 8.5 %shard_map.150 = (bf16[128,3584]{1,0:T(8,128)(2,1)S(1)}, bf16[144,896]{1,0:T(8,128)(2,1)S(1)}, bf16[144,896]{1,0:T(8,128)(2,1)S(1)}, bf16[144,896]{1,0:T(8,128)(2,1)S(1)}, bf16[144,896]{1,0:T(8,128)(2,1)S(1)}) custom-call(s32[16]{0:T(128)S(1)} %reshape_squeeze.6.chosen_ref, s32[16]{0:T(128)S(1)} %fusion.10.index_ref, s32[1]{0:T(128)} %bitcast.4.base_ref, ...), custom_call_target="tpu_custom_call" | custom-call | flops 1593835520 | bytes 5634692 | tf_op jit(solution)/shard_map/pallas_call | solution.py:55
  58.5 0.8 collective-permute-start.14
  59.4 1.1 shard_map.151.first_ref
  61.1 2.3 %collective-permute-done.17.middle_ref = bf16[128,3584]{1,0:T(8,128)(2,1)} collective-permute-done((bf16[128,3584]{1,0:T(8,128)(2,1)}, bf16[128,3584]{1,0:T(8,128)(2,1)}, u32[]{:S(2)}, u32[]{:S(2)}) %collective-permute-start.17) | collective-permute-done | bytes 917536 | tf_op jit(solution)/shard_map/ppermute | solution.py:33
  63.4 3.1 %collective-permute-done.15.refs_3_ = bf16[144,896]{1,0:T(8,128)(2,1)S(1)} collective-permute-done((bf16[144,896]{1,0:T(8,128)(2,1)S(1)}, bf16[144,896]{1,0:T(8,128)(2,1)S(1)}, u32[]{:S(2)}, u32[]{:S(2)}) %collective-permute-start.15) | collective-permute-done | bytes 258080 | tf_op jit(solution)/shard_map/ppermute | solution.py:42
  66.5 9.8 %collective-permute-done.14.refs_2_ = bf16[144,896]{1,0:T(8,128)(2,1)S(1)} collective-permute-done((bf16[144,896]{1,0:T(8,128)(2,1)S(1)}, bf16[144,896]{1,0:T(8,128)(2,1)S(1)}, u32[]{:S(2)}, u32[]{:S(2)}) %collective-permute-start.14) | collective-permute-done | bytes 258080 | tf_op jit(solution)/shard_map/ppermute | solution.py:42
  76.4 2.0 shard_map.152.first_ref
  79.7 3.4 %collective-permute-start.11 = (bf16[144,896]{1,0:T(8,128)(2,1)S(1)}, bf16[144,896]{1,0:T(8,128)(2,1)S(1)}, u32[]{:S(2)}, u32[]{:S(2)}) collective-permute-start(bf16[144,896]{1,0:T(8,128)(2,1)S(1)} %get-tuple-element.115), channel_id=1, source_target_pairs={{0,8},{1,9},{2,10},{3,11},{4,12},{5,13},{6,14},{7,15},{8,0},{9,1},... | collective-permute-start | bytes 774152 | tf_op jit(solution)/shard_map/ppermute | solution.py:42
  83.1 7.6 %collective-permute-done.10.refs_1_ = bf16[144,896]{1,0:T(8,128)(2,1)S(1)} collective-permute-done((bf16[144,896]{1,0:T(8,128)(2,1)S(1)}, bf16[144,896]{1,0:T(8,128)(2,1)S(1)}, u32[]{:S(2)}, u32[]{:S(2)}) %collective-permute-start.10) | collective-permute-done | bytes 258080 | tf_op jit(solution)/shard_map/ppermute | solution.py:42
  90.7 0.7 collective-permute-start.12
  91.4 8.2 %collective-permute-done.11.refs_2_ = bf16[144,896]{1,0:T(8,128)(2,1)S(1)} collective-permute-done((bf16[144,896]{1,0:T(8,128)(2,1)S(1)}, bf16[144,896]{1,0:T(8,128)(2,1)S(1)}, u32[]{:S(2)}, u32[]{:S(2)}) %collective-permute-start.11) | collective-permute-done | bytes 258080 | tf_op jit(solution)/shard_map/ppermute | solution.py:42
  99.6 1.7 collective-permute-done.12.refs_3_
  101.3 1.1 shard_map.153.first_ref
  103.0 1.5 collective-permute-start.23
  104.5 1.5 collective-permute-start.21
  106.2 1.3 shard_map.155
  108.3 2.4 %shard_map.156 = (bf16[144,3584]{1,0:T(8,128)(2,1)S(1)}, bf16[144,3584]{1,0:T(8,128)(2,1)S(1)}) custom-call(bf16[144,3584]{1,0:T(8,128)(2,1)S(1)} %shard_map.151.first_ref, bf16[144,3584]{1,0:T(8,128)(2,1)S(1)} %collective-permute-done.24.second_ref, f32[288,256]{1,0:T(8,128)S(1)} %get-tuple-element.143.back_ref, bf16[3584,256]{1,0:T(8,128)(2,1)S(1)} %bitcast.34, ...), custom_call_target="tpu_custom_call" | custom-call | flops 2113929216 | bytes 8093696 | tf_op jit(solution)/shard_map/pallas_call | solution.py:55
  110.7 1.0 copy-done.3
  111.7 15.5 %collective-permute-done.21.middle_ref = bf16[128,3584]{1,0:T(8,128)(2,1)S(1)} collective-permute-done((bf16[128,3584]{1,0:T(8,128)(2,1)S(1)}, bf16[128,3584]{1,0:T(8,128)(2,1)S(1)}, u32[]{:S(2)}, u32[]{:S(2)}) %collective-permute-start.21) | collective-permute-done | bytes 917536 | tf_op jit(solution)/shard_map/ppermute | solution.py:33
  127.2 1.4 collective-permute-done.23.first_ref
  128.6 2.3 %collective-permute-done.30.back_ref = bf16[288,256]{1,0:T(8,128)(2,1)S(1)} collective-permute-done((bf16[288,256]{1,0:T(8,128)(2,1)S(1)}, bf16[288,256]{1,0:T(8,128)(2,1)S(1)}, u32[]{:S(2)}, u32[]{:S(2)}) %collective-permute-start.30) | collective-permute-done | bytes 147488 | tf_op jit(solution)/shard_map/ppermute | solution.py:37
  130.9 2.5 %shard_map.158 = (bf16[144,3584]{1,0:T(8,128)(2,1)S(1)}, bf16[144,3584]{1,0:T(8,128)(2,1)S(1)}) custom-call(bf16[144,3584]{1,0:T(8,128)(2,1)S(1)} %collective-permute-done.13.first_ref, bf16[144,3584]{1,0:T(8,128)(2,1)S(1)} %collective-permute-done.29.second_ref, bf16[288,256]{1,0:T(8,128)(2,1)S(1)} %collective-permute-done.30.back_ref, ...), custom_call_target="tpu_custom_call" | custom-call | flops 2113929216 | bytes 7946240 | tf_op jit(solution)/shard_map/pallas_call | solution.py:55
  133.5 1.6 collective-permute-start.28
  135.6 1.2 shard_map.154.own_ref
  136.9 1.3 shard_map.157
  138.1 1.6 collective-permute-start.27
  139.7 1.2 add_convert_fusion
  140.9 2.9 %collective-permute-done.27.other_ref = bf16[288,256]{1,0:T(8,128)(2,1)S(1)} collective-permute-done((bf16[288,256]{1,0:T(8,128)(2,1)S(1)}, bf16[288,256]{1,0:T(8,128)(2,1)S(1)}, u32[]{:S(2)}, u32[]{:S(2)}) %collective-permute-start.27) | collective-permute-done | bytes 147488 | tf_op jit(solution)/shard_map/ppermute | solution.py:37
  143.9 1.2 shard_map.159
  145.7 1.5 collective-permute-start.38
  147.8 1.9 shard_map.160
  149.7 1.5 collective-permute-start.33
  151.3 3.2 %collective-permute-start.34 = (bf16[144,896]{1,0:T(8,128)(2,1)}, bf16[144,896]{1,0:T(8,128)(2,1)}, u32[]{:S(2)}, u32[]{:S(2)}) collective-permute-start(bf16[144,896]{1,0:T(8,128)(2,1)} %get-tuple-element.156), channel_id=1, source_target_pairs={{0,28},{1,29},{2,30},{3,31},{4,16},{5,17},{6,18},{7,19},{8,20},{9,... | collective-permute-start | bytes 774152 | tf_op jit(solution)/shard_map/ppermute | solution.py:33
  154.5 3.5 %collective-permute-start.35 = (bf16[144,896]{1,0:T(8,128)(2,1)}, bf16[144,896]{1,0:T(8,128)(2,1)}, u32[]{:S(2)}, u32[]{:S(2)}) collective-permute-start(bf16[144,896]{1,0:T(8,128)(2,1)} %get-tuple-element.157), channel_id=1, source_target_pairs={{0,24},{1,25},{2,26},{3,27},{4,28},{5,29},{6,30},{7,31},{8,16},{9,... | collective-permute-start | bytes 774152 | tf_op jit(solution)/shard_map/ppermute | solution.py:33
  158.2 12.5 %collective-permute-done.38.refs_2_ = bf16[144,3584]{1,0:T(8,128)(2,1)S(1)} collective-permute-done((bf16[144,3584]{1,0:T(8,128)(2,1)}, bf16[144,3584]{1,0:T(8,128)(2,1)S(1)}, u32[]{:S(2)}, u32[]{:S(2)}) %collective-permute-start.38) | collective-permute-done | bytes 1032224 | tf_op jit(solution)/shard_map/ppermute | solution.py:37
  170.7 2.1 %shard_map.161 = (bf16[144,896]{1,0:T(8,128)(2,1)}, bf16[144,896]{1,0:T(8,128)(2,1)}, bf16[144,896]{1,0:T(8,128)(2,1)}, bf16[144,896]{1,0:T(8,128)(2,1)}) custom-call(bf16[144,3584]{1,0:T(8,128)(2,1)S(1)} %copy-done.4, bf16[144,3584]{1,0:T(8,128)(2,1)S(1)} %collective-permute-done.37.refs_1_, bf16[144,3584]{1,0:T(8,128)(2,1)S(1)} %collective-permute-done.38.refs_2_), custom_call_target="tpu_custom_call" | custom-call | flops 1 | bytes 1 | tf_op jit(solution)/shard_map/pallas_call | solution.py:55
  172.8 1.5 collective-permute-start.39
  174.3 4.8 %collective-permute-start.40 = (bf16[144,896]{1,0:T(8,128)(2,1)}, bf16[144,896]{1,0:T(8,128)(2,1)S(1)}, u32[]{:S(2)}, u32[]{:S(2)}) collective-permute-start(bf16[144,896]{1,0:T(8,128)(2,1)} %get-tuple-element.165), channel_id=1, source_target_pairs={{0,28},{1,29},{2,30},{3,31},{4,16},{5,17},{6,18},{7,19},{8,20},{9,... | collective-permute-start | bytes 774152 | tf_op jit(solution)/shard_map/ppermute | solution.py:33
  179.1 2.5 %collective-permute-start.41 = (bf16[144,896]{1,0:T(8,128)(2,1)}, bf16[144,896]{1,0:T(8,128)(2,1)S(1)}, u32[]{:S(2)}, u32[]{:S(2)}) collective-permute-start(bf16[144,896]{1,0:T(8,128)(2,1)} %get-tuple-element.166), channel_id=1, source_target_pairs={{0,24},{1,25},{2,26},{3,27},{4,28},{5,29},{6,30},{7,31},{8,16},{9,... | collective-permute-start | bytes 774152 | tf_op jit(solution)/shard_map/ppermute | solution.py:33
  181.8 1.2 copy-done.14
  183.0 3.6 %shard_map.162 = bf16[128,3584]{1,0:T(8,128)(2,1)} custom-call(s32[128,1]{1,0:T(8,128)S(1)} %copy.18.route_ref, f32[128,1]{1,0:T(8,128)S(1)} %copy.19.gate_ref, bf16[128,3584]{1,0:T(8,128)(2,1)S(1)} %copy-done.14, bf16[144,896]{1,0:T(8,128)(2,1)} %collective-permute-done.33.refs_0_, bf16[144,896]{1,0:T(8,128)(2,1)} %collective-permute-done.34.refs_1_, ...), custom_call_target="tpu_custom_call" | custom-call | flops 1056964608 | bytes 2868224 | tf_op jit(solution)/shard_map/pallas_call | solution.py:55
  186.6 6.1 %collective-permute-done.39.refs_0_ = bf16[144,896]{1,0:T(8,128)(2,1)S(1)} collective-permute-done((bf16[144,896]{1,0:T(8,128)(2,1)}, bf16[144,896]{1,0:T(8,128)(2,1)S(1)}, u32[]{:S(2)}, u32[]{:S(2)}) %collective-permute-start.39) | collective-permute-done | bytes 258080 | tf_op jit(solution)/shard_map/ppermute | solution.py:33
  192.7 11.1 %collective-permute-done.41.refs_2_ = bf16[144,896]{1,0:T(8,128)(2,1)S(1)} collective-permute-done((bf16[144,896]{1,0:T(8,128)(2,1)}, bf16[144,896]{1,0:T(8,128)(2,1)S(1)}, u32[]{:S(2)}, u32[]{:S(2)}) %collective-permute-start.41) | collective-permute-done | bytes 258080 | tf_op jit(solution)/shard_map/ppermute | solution.py:33
  203.8 3.9 %shard_map.163 = bf16[128,3584]{1,0:T(8,128)(2,1)} custom-call(s32[128,1]{1,0:T(8,128)S(1)} %copy.20.route_ref, f32[1,3584]{1,0:T(1,128)S(1)} %slice.35.gain_ref, bf16[128,3584]{1,0:T(8,128)(2,1)} %collective-permute-done.17.middle_ref, bf16[128,3584]{1,0:T(8,128)(2,1)S(1)} %copy-done.12, bf16[144,896]{1,0:T(8,128)(2,1)S(1)} %collective-permute-done.39.refs_0_, ...), custom_call_target="tpu_custom_call" | custom-call | flops 1056964608 | bytes 3799552 | tf_op jit(solution)/shard_map/pallas_call | solution.py:55
  (123 shorter events, 8.6 us)
Async XLA Ops:
  1.6 17.9 %collective-permute-start = (bf16[128,448]{1,0:T(8,128)(2,1)S(1)}, bf16[128,448]{1,0:T(8,128)(2,1)S(1)}, u32[]{:S(2)}, u32[]{:S(2)}) collective-permute-start(bf16[128,448]{1,0:T(8,128)(2,1)S(1)} %bitcast.46), channel_id=1, source_target_pairs={{0,4},{1,5},{2,6},{3,7},{4,8},{5,9},{6,10},{7,11},{8,12},{9,13},{1... | collective-permute-start | bytes 344072 | tf_op jit(solution)/shard_map/ppermute | solution.py:379
  6.6 12.9 %collective-permute-start.1 = (bf16[128,448]{1,0:T(8,128)(2,1)S(1)}, bf16[128,448]{1,0:T(8,128)(2,1)S(1)}, u32[]{:S(2)}, u32[]{:S(2)}) collective-permute-start(bf16[128,448]{1,0:T(8,128)(2,1)S(1)} %bitcast.47), channel_id=1, source_target_pairs={{0,8},{1,9},{2,10},{3,11},{4,12},{5,13},{6,14},{7,15},{16,24},{17,... | collective-permute-start | bytes 344072 | tf_op jit(solution)/shard_map/ppermute | solution.py:379
  11.1 8.4 %collective-permute-start.2 = (bf16[128,448]{1,0:T(8,128)(2,1)S(1)}, bf16[128,448]{1,0:T(8,128)(2,1)S(1)}, u32[]{:S(2)}, u32[]{:S(2)}) collective-permute-start(bf16[128,448]{1,0:T(8,128)(2,1)S(1)} %bitcast.48), channel_id=1, source_target_pairs={{0,12},{1,13},{2,14},{3,15},{16,28},{17,29},{18,30},{19,31}} | collective-permute-start | bytes 344072 | tf_op jit(solution)/shard_map/ppermute | solution.py:379
  15.7 8.6 %copy-start = (bf16[1,1,256,3584]{3,2,1,0:T(8,128)(2,1)S(1)}, bf16[1,1,256,3584]{3,2,1,0:T(8,128)(2,1)}, u32[]{:S(2)}) copy-start(bf16[1,1,256,3584]{3,2,1,0:T(8,128)(2,1)} %param.27) | copy-start | bytes 5505028
  19.4 23.4 %copy-start.15 = (bf16[144,896]{1,0:T(8,128)(2,1)}, bf16[144,896]{1,0:T(8,128)(2,1)S(1)}, u32[]{:S(2)}) copy-start(bf16[144,896]{1,0:T(8,128)(2,1)S(1)} %get-tuple-element.124) | copy-start | bytes 774148
  19.4 23.4 %copy-start.17 = (bf16[144,896]{1,0:T(8,128)(2,1)}, bf16[144,896]{1,0:T(8,128)(2,1)S(1)}, u32[]{:S(2)}) copy-start(bf16[144,896]{1,0:T(8,128)(2,1)S(1)} %get-tuple-element.126) | copy-start | bytes 774148
  19.5 23.5 %copy-start.19 = (bf16[144,896]{1,0:T(8,128)(2,1)}, bf16[144,896]{1,0:T(8,128)(2,1)S(1)}, u32[]{:S(2)}) copy-start(bf16[144,896]{1,0:T(8,128)(2,1)S(1)} %get-tuple-element.110) | copy-start | bytes 774148
  19.5 23.5 %copy-start.20 = (bf16[144,896]{1,0:T(8,128)(2,1)}, bf16[144,896]{1,0:T(8,128)(2,1)S(1)}, u32[]{:S(2)}) copy-start(bf16[144,896]{1,0:T(8,128)(2,1)S(1)} %get-tuple-element.112) | copy-start | bytes 774148
  19.5 23.5 %copy-start.27 = (bf16[144,896]{1,0:T(8,128)(2,1)}, bf16[144,896]{1,0:T(8,128)(2,1)S(1)}, u32[]{:S(2)}) copy-start(bf16[144,896]{1,0:T(8,128)(2,1)S(1)} %get-tuple-element.118.refs_0_) | copy-start | bytes 774148
  19.5 24.0 %copy-start.29 = (s32[1,2,2,4]{3,2,1,0:T(2,128)S(1)}, s32[1,2,2,4]{3,2,1,0:T(2,128)}, u32[]{:S(2)}) copy-start(s32[1,2,2,4]{3,2,1,0:T(2,128)} %param.17) | copy-start | bytes 196
  19.5 24.1 %copy-start.31 = (s32[1,128,1]{1,2,0:T(1,128)S(1)}, s32[1,128,1]{1,2,0:T(1,128)}, u32[]{:S(2)}) copy-start(s32[1,128,1]{1,2,0:T(1,128)} %param.18) | copy-start | bytes 1540
  19.5 28.1 %copy-start.6 = (f32[1,3584]{1,0:T(1,128)S(1)}, f32[1,3584]{1,0:T(1,128)}, u32[]{:S(2)}) copy-start(f32[1,3584]{1,0:T(1,128)} %gain_ref.3) | copy-start | bytes 43012
  19.6 23.3 %collective-permute-start.3 = (bf16[512,448]{1,0:T(8,128)(2,1)S(1)}, bf16[512,448]{1,0:T(8,128)(2,1)}, u32[]{:S(2)}, u32[]{:S(2)}) collective-permute-start(bf16[512,448]{1,0:T(8,128)(2,1)S(1)} %constant_dynamic-update-slice_fusion.kv0), channel_id=1, source_target_pairs={{0,2},{1,3},{2,0},{3,1},{4,6},{5,7},{6,4},{7,5},{8,10},{9,11},{10,... | collective-permute-start | bytes 1376264 | tf_op jit(solution)/shard_map/ppermute | solution.py:37
  21.2 11.0 %collective-permute-start.5 = (bf16[144,896]{1,0:T(8,128)(2,1)S(1)}, bf16[144,896]{1,0:T(8,128)(2,1)S(1)}, u32[]{:S(2)}, u32[]{:S(2)}) collective-permute-start(bf16[144,896]{1,0:T(8,128)(2,1)S(1)} %get-tuple-element.101), channel_id=1, source_target_pairs={{0,4},{1,5},{2,6},{3,7},{4,8},{5,9},{6,10},{7,11},{8,12},{9,13},{1... | collective-permute-start | bytes 774152 | tf_op jit(solution)/shard_map/ppermute | solution.py:42
  21.2 19.5 %collective-permute-start.6 = (bf16[144,896]{1,0:T(8,128)(2,1)S(1)}, bf16[144,896]{1,0:T(8,128)(2,1)S(1)}, u32[]{:S(2)}, u32[]{:S(2)}) collective-permute-start(bf16[144,896]{1,0:T(8,128)(2,1)S(1)} %get-tuple-element.102), channel_id=1, source_target_pairs={{0,8},{1,9},{2,10},{3,11},{4,12},{5,13},{6,14},{7,15},{8,0},{9,1},... | collective-permute-start | bytes 774152 | tf_op jit(solution)/shard_map/ppermute | solution.py:42
  32.9 43.5 %collective-permute-start.16 = (bf16[160,3584]{1,0:T(8,128)(2,1)}, bf16[160,3584]{1,0:T(8,128)(2,1)S(1)}, u32[]{:S(2)}, u32[]{:S(2)}) collective-permute-start(bf16[160,3584]{1,0:T(8,128)(2,1)} %slice_bitcast_fusion), channel_id=1, source_target_pairs={{0,2},{1,3},{2,0},{3,1},{4,6},{5,7},{6,4},{7,5},{8,10},{9,11},{10,... | collective-permute-start | bytes 3440648 | tf_op jit(solution)/shard_map/ppermute | solution.py:37
  41.4 22.0 %collective-permute-start.17 = (bf16[128,3584]{1,0:T(8,128)(2,1)}, bf16[128,3584]{1,0:T(8,128)(2,1)}, u32[]{:S(2)}, u32[]{:S(2)}) collective-permute-start(bf16[128,3584]{1,0:T(8,128)(2,1)} %bitcast.10.middle_ref), channel_id=1, source_target_pairs={{0,16},{1,17},{2,18},{3,19},{4,20},{5,21},{6,22},{7,23},{8,24},{9,... | collective-permute-start | bytes 2752520 | tf_op jit(solution)/shard_map/ppermute | solution.py:33
  42.9 2.0 collective-permute-start.4
  42.9 4.6 %collective-permute-start.7 = (bf16[512,448]{1,0:T(8,128)(2,1)}, bf16[512,448]{1,0:T(8,128)(2,1)}, u32[]{:S(2)}, u32[]{:S(2)}) collective-permute-start(bf16[512,448]{1,0:T(8,128)(2,1)} %collective-permute-done.3.kv1), channel_id=1, source_target_pairs={{0,1},{1,0},{2,3},{3,2},{4,5},{5,4},{6,7},{7,6},{8,9},{9,8},{10,11... | collective-permute-start | bytes 1376264 | tf_op jit(solution)/shard_map/ppermute | solution.py:37
  43.6 14.9 %collective-permute-start.9 = (bf16[144,896]{1,0:T(8,128)(2,1)}, bf16[144,896]{1,0:T(8,128)(2,1)}, u32[]{:S(2)}, u32[]{:S(2)}) collective-permute-start(bf16[144,896]{1,0:T(8,128)(2,1)} %copy-done.20), channel_id=1, source_target_pairs={{0,4},{1,5},{2,6},{3,7},{4,8},{5,9},{6,10},{7,11},{8,12},{9,13},{1... | collective-permute-start | bytes 774152 | tf_op jit(solution)/shard_map/ppermute | solution.py:42
  44.9 14.4 %collective-permute-start.8 = (bf16[144,896]{1,0:T(8,128)(2,1)}, bf16[144,896]{1,0:T(8,128)(2,1)S(1)}, u32[]{:S(2)}, u32[]{:S(2)}) collective-permute-start(bf16[144,896]{1,0:T(8,128)(2,1)} %copy-done.19), channel_id=1, source_target_pairs={{0,12},{1,13},{2,14},{3,15},{4,0},{5,1},{6,2},{7,3},{8,4},{9,5},{1... | collective-permute-start | bytes 774152 | tf_op jit(solution)/shard_map/ppermute | solution.py:42
  49.9 8.5 %copy-start.18 = (bf16[144,896]{1,0:T(8,128)(2,1)S(1)}, bf16[144,896]{1,0:T(8,128)(2,1)}, u32[]{:S(2)}) copy-start(bf16[144,896]{1,0:T(8,128)(2,1)} %copy-done.17) | copy-start | bytes 774148
  49.9 8.6 %copy-start.16 = (bf16[144,896]{1,0:T(8,128)(2,1)S(1)}, bf16[144,896]{1,0:T(8,128)(2,1)}, u32[]{:S(2)}) copy-start(bf16[144,896]{1,0:T(8,128)(2,1)} %copy-done.15) | copy-start | bytes 774148
  49.9 9.4 %copy-start.22 = (bf16[144,896]{1,0:T(8,128)(2,1)S(1)}, bf16[144,896]{1,0:T(8,128)(2,1)}, u32[]{:S(2)}) copy-start(bf16[144,896]{1,0:T(8,128)(2,1)} %copy-done.21) | copy-start | bytes 774148
  49.9 9.4 %copy-start.24 = (bf16[144,896]{1,0:T(8,128)(2,1)S(1)}, bf16[144,896]{1,0:T(8,128)(2,1)}, u32[]{:S(2)}) copy-start(bf16[144,896]{1,0:T(8,128)(2,1)} %copy-done.23) | copy-start | bytes 774148
  50.0 9.4 %copy-start.28 = (bf16[144,896]{1,0:T(8,128)(2,1)S(1)}, bf16[144,896]{1,0:T(8,128)(2,1)}, u32[]{:S(2)}) copy-start(bf16[144,896]{1,0:T(8,128)(2,1)} %copy-done.27) | copy-start | bytes 774148
  58.4 17.9 %copy-start.26 = (bf16[144,896]{1,0:T(8,128)(2,1)S(1)}, bf16[144,896]{1,0:T(8,128)(2,1)}, u32[]{:S(2)}) copy-start(bf16[144,896]{1,0:T(8,128)(2,1)} %copy-done.25) | copy-start | bytes 774148
  58.4 8.1 %collective-permute-start.15 = (bf16[144,896]{1,0:T(8,128)(2,1)S(1)}, bf16[144,896]{1,0:T(8,128)(2,1)S(1)}, u32[]{:S(2)}, u32[]{:S(2)}) collective-permute-start(bf16[144,896]{1,0:T(8,128)(2,1)S(1)} %copy-done.18), channel_id=1, source_target_pairs={{0,12},{1,13},{2,14},{3,15},{4,0},{5,1},{6,2},{7,3},{8,4},{9,5},{1... | collective-permute-start | bytes 774152 | tf_op jit(solution)/shard_map/ppermute | solution.py:42
  58.5 17.8 %collective-permute-start.14 = (bf16[144,896]{1,0:T(8,128)(2,1)S(1)}, bf16[144,896]{1,0:T(8,128)(2,1)S(1)}, u32[]{:S(2)}, u32[]{:S(2)}) collective-permute-start(bf16[144,896]{1,0:T(8,128)(2,1)S(1)} %copy-done.16), channel_id=1, source_target_pairs={{0,8},{1,9},{2,10},{3,11},{4,12},{5,13},{6,14},{7,15},{8,0},{9,1},... | collective-permute-start | bytes 774152 | tf_op jit(solution)/shard_map/ppermute | solution.py:42
  60.5 17.9 %copy-start.10 = (bf16[1,128,3584]{2,1,0:T(8,128)(2,1)S(1)}, bf16[1,128,3584]{2,1,0:T(8,128)(2,1)}, u32[]{:S(2)}) copy-start(bf16[1,128,3584]{2,1,0:T(8,128)(2,1)} %param.21) | copy-start | bytes 2752516
  60.5 40.8 %collective-permute-start.13 = (bf16[144,3584]{1,0:T(8,128)(2,1)S(1)}, bf16[144,3584]{1,0:T(8,128)(2,1)S(1)}, u32[]{:S(2)}, u32[]{:S(2)}) collective-permute-start(bf16[144,3584]{1,0:T(8,128)(2,1)S(1)} %shard_map.151.first_ref), channel_id=1, source_target_pairs={{0,2},{1,3},{2,0},{3,1},{4,6},{5,7},{6,4},{7,5},{8,10},{9,11},{10,... | collective-permute-start | bytes 3096584 | tf_op jit(solution)/shard_map/ppermute | solution.py:37
  78.4 22.8 %collective-permute-start.18 = (bf16[128,3584]{1,0:T(8,128)(2,1)S(1)}, bf16[128,3584]{1,0:T(8,128)(2,1)S(1)}, u32[]{:S(2)}, u32[]{:S(2)}) collective-permute-start(bf16[128,3584]{1,0:T(8,128)(2,1)S(1)} %bitcast.45), channel_id=1, source_target_pairs={{0,16},{1,17},{2,18},{3,19},{4,20},{5,21},{6,22},{7,23},{8,24},{9,... | collective-permute-start | bytes 2752520 | tf_op jit(solution)/shard_map/ppermute | solution.py:33
  79.0 22.2 %collective-permute-start.19 = (bf16[96,3584]{1,0:T(8,128)(2,1)S(1)}, bf16[96,3584]{1,0:T(8,128)(2,1)S(1)}, u32[]{:S(2)}, u32[]{:S(2)}) collective-permute-start(bf16[96,3584]{1,0:T(8,128)(2,1)S(1)} %slice_bitcast_fusion.1), channel_id=1, source_target_pairs={{0,2},{1,3},{2,0},{3,1},{4,6},{5,7},{6,4},{7,5},{8,10},{9,11},{10,... | collective-permute-start | bytes 2064392 | tf_op jit(solution)/shard_map/ppermute | solution.py:37
  79.6 11.0 %collective-permute-start.10 = (bf16[144,896]{1,0:T(8,128)(2,1)S(1)}, bf16[144,896]{1,0:T(8,128)(2,1)S(1)}, u32[]{:S(2)}, u32[]{:S(2)}) collective-permute-start(bf16[144,896]{1,0:T(8,128)(2,1)S(1)} %get-tuple-element.114), channel_id=1, source_target_pairs={{0,4},{1,5},{2,6},{3,7},{4,8},{5,9},{6,10},{7,11},{8,12},{9,13},{1... | collective-permute-start | bytes 774152 | tf_op jit(solution)/shard_map/ppermute | solution.py:42
  79.7 19.8 %collective-permute-start.11 = (bf16[144,896]{1,0:T(8,128)(2,1)S(1)}, bf16[144,896]{1,0:T(8,128)(2,1)S(1)}, u32[]{:S(2)}, u32[]{:S(2)}) collective-permute-start(bf16[144,896]{1,0:T(8,128)(2,1)S(1)} %get-tuple-element.115), channel_id=1, source_target_pairs={{0,8},{1,9},{2,10},{3,11},{4,12},{5,13},{6,14},{7,15},{8,0},{9,1},... | collective-permute-start | bytes 774152 | tf_op jit(solution)/shard_map/ppermute | solution.py:42
  90.7 10.6 %collective-permute-start.12 = (bf16[144,896]{1,0:T(8,128)(2,1)S(1)}, bf16[144,896]{1,0:T(8,128)(2,1)S(1)}, u32[]{:S(2)}, u32[]{:S(2)}) collective-permute-start(bf16[144,896]{1,0:T(8,128)(2,1)S(1)} %get-tuple-element.116), channel_id=1, source_target_pairs={{0,12},{1,13},{2,14},{3,15},{4,0},{5,1},{6,2},{7,3},{8,4},{9,5},{1... | collective-permute-start | bytes 774152 | tf_op jit(solution)/shard_map/ppermute | solution.py:42
  102.4 3.6 %collective-permute-start.25 = (bf16[144,3584]{1,0:T(8,128)(2,1)S(1)}, bf16[144,3584]{1,0:T(8,128)(2,1)S(1)}, u32[]{:S(2)}, u32[]{:S(2)}) collective-permute-start(bf16[144,3584]{1,0:T(8,128)(2,1)S(1)} %shard_map.152.first_ref), channel_id=1, source_target_pairs={{0,1},{1,0},{2,3},{3,2},{4,5},{5,4},{6,7},{7,6},{8,9},{9,8},{10,11... | collective-permute-start | bytes 3096584 | tf_op jit(solution)/shard_map/ppermute | solution.py:37
  102.5 5.0 %collective-permute-start.24 = (bf16[144,3584]{1,0:T(8,128)(2,1)S(1)}, bf16[144,3584]{1,0:T(8,128)(2,1)S(1)}, u32[]{:S(2)}, u32[]{:S(2)}) collective-permute-start(bf16[144,3584]{1,0:T(8,128)(2,1)S(1)} %shard_map.151.first_ref), channel_id=1, source_target_pairs={{0,1},{1,0},{2,3},{3,2},{4,5},{5,4},{6,7},{7,6},{8,9},{9,8},{10,11... | collective-permute-start | bytes 3096584 | tf_op jit(solution)/shard_map/ppermute | solution.py:37
  103.0 25.7 %collective-permute-start.23 = (bf16[144,3584]{1,0:T(8,128)(2,1)S(1)}, bf16[144,3584]{1,0:T(8,128)(2,1)S(1)}, u32[]{:S(2)}, u32[]{:S(2)}) collective-permute-start(bf16[144,3584]{1,0:T(8,128)(2,1)S(1)} %shard_map.153.first_ref), channel_id=1, source_target_pairs={{0,2},{1,3},{2,0},{3,1},{4,6},{5,7},{6,4},{7,5},{8,10},{9,11},{10,... | collective-permute-start | bytes 3096584 | tf_op jit(solution)/shard_map/ppermute | solution.py:37
  104.5 26.5 %collective-permute-start.29 = (bf16[144,3584]{1,0:T(8,128)(2,1)S(1)}, bf16[144,3584]{1,0:T(8,128)(2,1)S(1)}, u32[]{:S(2)}, u32[]{:S(2)}) collective-permute-start(bf16[144,3584]{1,0:T(8,128)(2,1)S(1)} %collective-permute-done.13.first_ref), channel_id=1, source_target_pairs={{0,1},{1,0},{2,3},{3,2},{4,5},{5,4},{6,7},{7,6},{8,9},{9,8},{10,11... | collective-permute-start | bytes 3096584 | tf_op jit(solution)/shard_map/ppermute | solution.py:37
  104.5 22.8 %collective-permute-start.21 = (bf16[128,3584]{1,0:T(8,128)(2,1)S(1)}, bf16[128,3584]{1,0:T(8,128)(2,1)S(1)}, u32[]{:S(2)}, u32[]{:S(2)}) collective-permute-start(bf16[128,3584]{1,0:T(8,128)(2,1)S(1)} %get-tuple-element.140), channel_id=1, source_target_pairs={{0,16},{1,17},{2,18},{3,19},{4,20},{5,21},{6,22},{7,23},{8,24},{9,... | collective-permute-start | bytes 2752520 | tf_op jit(solution)/shard_map/ppermute | solution.py:33
  106.0 29.6 %collective-permute-start.22 = (bf16[144,3584]{1,0:T(8,128)(2,1)S(1)}, bf16[144,3584]{1,0:T(8,128)(2,1)S(1)}, u32[]{:S(2)}, u32[]{:S(2)}) collective-permute-start(bf16[144,3584]{1,0:T(8,128)(2,1)S(1)} %shard_map.153.first_ref), channel_id=1, source_target_pairs={{0,1},{1,0},{2,3},{3,2},{4,5},{5,4},{6,7},{7,6},{8,9},{9,8},{10,11... | collective-permute-start | bytes 3096584 | tf_op jit(solution)/shard_map/ppermute | solution.py:37
  106.2 2.0 copy-start.2
  107.5 23.4 %collective-permute-start.30 = (bf16[288,256]{1,0:T(8,128)(2,1)S(1)}, bf16[288,256]{1,0:T(8,128)(2,1)S(1)}, u32[]{:S(2)}, u32[]{:S(2)}) collective-permute-start(bf16[288,256]{1,0:T(8,128)(2,1)S(1)} %get-tuple-element.148), channel_id=1, source_target_pairs={{0,2},{1,3},{2,0},{3,1},{4,6},{5,7},{6,4},{7,5},{8,10},{9,11},{10,... | collective-permute-start | bytes 442376 | tf_op jit(solution)/shard_map/ppermute | solution.py:37
  127.2 6.2 %copy-start.13 = (bf16[128,3584]{1,0:T(8,128)(2,1)}, bf16[128,3584]{1,0:T(8,128)(2,1)S(1)}, u32[]{:S(2)}) copy-start(bf16[128,3584]{1,0:T(8,128)(2,1)S(1)} %collective-permute-done.21.middle_ref) | copy-start | bytes 2752516
  128.6 4.9 %copy-start.30 = (f32[1,128,1]{1,2,0:T(1,128)S(1)}, f32[1,128,1]{1,2,0:T(1,128)}, u32[]{:S(2)}) copy-start(f32[1,128,1]{1,2,0:T(1,128)} %param.19) | copy-start | bytes 1540
  128.6 8.3 %collective-permute-start.26 = (bf16[144,3584]{1,0:T(8,128)(2,1)S(1)}, bf16[144,3584]{1,0:T(8,128)(2,1)S(1)}, u32[]{:S(2)}, u32[]{:S(2)}) collective-permute-start(bf16[144,3584]{1,0:T(8,128)(2,1)S(1)} %collective-permute-done.23.first_ref), channel_id=1, source_target_pairs={{0,1},{1,0},{2,3},{3,2},{4,5},{5,4},{6,7},{7,6},{8,9},{9,8},{10,11... | collective-permute-start | bytes 3096584 | tf_op jit(solution)/shard_map/ppermute | solution.py:37
  133.4 6.3 %collective-permute-start.31 = (bf16[144,3584]{1,0:T(8,128)(2,1)S(1)}, bf16[144,3584]{1,0:T(8,128)(2,1)S(1)}, u32[]{:S(2)}, u32[]{:S(2)}) collective-permute-start(bf16[144,3584]{1,0:T(8,128)(2,1)S(1)} %get-tuple-element.151), channel_id=1, source_target_pairs={{0,1},{1,0},{2,3},{3,2},{4,5},{5,4},{6,7},{7,6},{8,9},{9,8},{10,11... | collective-permute-start | bytes 3096584 | tf_op jit(solution)/shard_map/ppermute | solution.py:37
  133.5 7.4 %collective-permute-start.28 = (f32[1,3712]{1,0:T(1,128)S(1)}, f32[1,3712]{1,0:T(1,128)S(1)}, u32[]{:S(2)}, u32[]{:S(2)}) collective-permute-start(f32[1,3712]{1,0:T(1,128)S(1)} %pad_maximum_fusion), channel_id=1, source_target_pairs={{0,16},{1,17},{2,18},{3,19},{4,20},{5,21},{6,22},{7,23},{8,24},{9,... | collective-permute-start | bytes 44552 | tf_op jit(solution)/shard_map/ppermute | solution.py:33
  135.1 5.8 %collective-permute-start.20 = (f32[1,256]{1,0:T(1,128)S(1)}, f32[1,256]{1,0:T(1,128)S(1)}, u32[]{:S(2)}, u32[]{:S(2)}) collective-permute-start(f32[1,256]{1,0:T(1,128)S(1)} %maximum_bitcast_fusion), channel_id=1, source_target_pairs={{0,16},{1,17},{2,18},{3,19},{4,20},{5,21},{6,22},{7,23},{8,24},{9,... | collective-permute-start | bytes 3080 | tf_op jit(solution)/shard_map/ppermute | solution.py:33
  138.1 5.7 %collective-permute-start.27 = (bf16[288,256]{1,0:T(8,128)(2,1)S(1)}, bf16[288,256]{1,0:T(8,128)(2,1)S(1)}, u32[]{:S(2)}, u32[]{:S(2)}) collective-permute-start(bf16[288,256]{1,0:T(8,128)(2,1)S(1)} %shard_map.157), channel_id=1, source_target_pairs={{0,2},{1,3},{2,0},{3,1},{4,6},{5,7},{6,4},{7,5},{8,10},{9,11},{10,... | collective-permute-start | bytes 442376 | tf_op jit(solution)/shard_map/ppermute | solution.py:37
  145.1 25.6 %copy-start.4 = (bf16[144,3584]{1,0:T(8,128)(2,1)S(1)}, bf16[144,3584]{1,0:T(8,128)(2,1)}, u32[]{:S(2)}) copy-start(bf16[144,3584]{1,0:T(8,128)(2,1)} %copy-done.3) | copy-start | bytes 3096580
  145.1 2.7 %collective-permute-start.32 = (bf16[144,3584]{1,0:T(8,128)(2,1)S(1)}, bf16[144,3584]{1,0:T(8,128)(2,1)S(1)}, u32[]{:S(2)}, u32[]{:S(2)}) collective-permute-start(bf16[144,3584]{1,0:T(8,128)(2,1)S(1)} %get-tuple-element.154), channel_id=1, source_target_pairs={{0,1},{1,0},{2,3},{3,2},{4,5},{5,4},{6,7},{7,6},{8,9},{9,8},{10,11... | collective-permute-start | bytes 3096584 | tf_op jit(solution)/shard_map/ppermute | solution.py:37
  145.2 12.7 %collective-permute-start.37 = (bf16[144,3584]{1,0:T(8,128)(2,1)S(1)}, bf16[144,3584]{1,0:T(8,128)(2,1)S(1)}, u32[]{:S(2)}, u32[]{:S(2)}) collective-permute-start(bf16[144,3584]{1,0:T(8,128)(2,1)S(1)} %get-tuple-element.159), channel_id=1, source_target_pairs={{0,1},{1,0},{2,3},{3,2},{4,5},{5,4},{6,7},{7,6},{8,9},{9,8},{10,11... | collective-permute-start | bytes 3096584 | tf_op jit(solution)/shard_map/ppermute | solution.py:37
  145.7 25.0 %collective-permute-start.38 = (bf16[144,3584]{1,0:T(8,128)(2,1)}, bf16[144,3584]{1,0:T(8,128)(2,1)S(1)}, u32[]{:S(2)}, u32[]{:S(2)}) collective-permute-start(bf16[144,3584]{1,0:T(8,128)(2,1)} %add_convert_fusion), channel_id=1, source_target_pairs={{0,2},{1,3},{2,0},{3,1},{4,6},{5,7},{6,4},{7,5},{8,10},{9,11},{10,... | collective-permute-start | bytes 3096584 | tf_op jit(solution)/shard_map/ppermute | solution.py:37
  149.7 24.6 %collective-permute-start.33 = (bf16[144,896]{1,0:T(8,128)(2,1)}, bf16[144,896]{1,0:T(8,128)(2,1)}, u32[]{:S(2)}, u32[]{:S(2)}) collective-permute-start(bf16[144,896]{1,0:T(8,128)(2,1)} %get-tuple-element.155), channel_id=1, source_target_pairs={{0,16},{1,17},{2,18},{3,19},{4,20},{5,21},{6,22},{7,23},{8,24},{9,... | collective-permute-start | bytes 774152 | tf_op jit(solution)/shard_map/ppermute | solution.py:33
  151.3 27.9 %collective-permute-start.34 = (bf16[144,896]{1,0:T(8,128)(2,1)}, bf16[144,896]{1,0:T(8,128)(2,1)}, u32[]{:S(2)}, u32[]{:S(2)}) collective-permute-start(bf16[144,896]{1,0:T(8,128)(2,1)} %get-tuple-element.156), channel_id=1, source_target_pairs={{0,28},{1,29},{2,30},{3,31},{4,16},{5,17},{6,18},{7,19},{8,20},{9,... | collective-permute-start | bytes 774152 | tf_op jit(solution)/shard_map/ppermute | solution.py:33
  154.5 27.1 %collective-permute-start.35 = (bf16[144,896]{1,0:T(8,128)(2,1)}, bf16[144,896]{1,0:T(8,128)(2,1)}, u32[]{:S(2)}, u32[]{:S(2)}) collective-permute-start(bf16[144,896]{1,0:T(8,128)(2,1)} %get-tuple-element.157), channel_id=1, source_target_pairs={{0,24},{1,25},{2,26},{3,27},{4,28},{5,29},{6,30},{7,31},{8,16},{9,... | collective-permute-start | bytes 774152 | tf_op jit(solution)/shard_map/ppermute | solution.py:33
  158.0 23.8 %collective-permute-start.36 = (bf16[144,896]{1,0:T(8,128)(2,1)S(1)}, bf16[144,896]{1,0:T(8,128)(2,1)}, u32[]{:S(2)}, u32[]{:S(2)}) collective-permute-start(bf16[144,896]{1,0:T(8,128)(2,1)S(1)} %get-tuple-element.158), channel_id=1, source_target_pairs={{0,20},{1,21},{2,22},{3,23},{4,24},{5,25},{6,26},{7,27},{8,28},{9,... | collective-permute-start | bytes 774152 | tf_op jit(solution)/shard_map/ppermute | solution.py:33
  172.8 19.9 %collective-permute-start.39 = (bf16[144,896]{1,0:T(8,128)(2,1)}, bf16[144,896]{1,0:T(8,128)(2,1)S(1)}, u32[]{:S(2)}, u32[]{:S(2)}) collective-permute-start(bf16[144,896]{1,0:T(8,128)(2,1)} %get-tuple-element.164), channel_id=1, source_target_pairs={{0,16},{1,17},{2,18},{3,19},{4,20},{5,21},{6,22},{7,23},{8,24},{9,... | collective-permute-start | bytes 774152 | tf_op jit(solution)/shard_map/ppermute | solution.py:33
  174.3 18.4 %collective-permute-start.40 = (bf16[144,896]{1,0:T(8,128)(2,1)}, bf16[144,896]{1,0:T(8,128)(2,1)S(1)}, u32[]{:S(2)}, u32[]{:S(2)}) collective-permute-start(bf16[144,896]{1,0:T(8,128)(2,1)} %get-tuple-element.165), channel_id=1, source_target_pairs={{0,28},{1,29},{2,30},{3,31},{4,16},{5,17},{6,18},{7,19},{8,20},{9,... | collective-permute-start | bytes 774152 | tf_op jit(solution)/shard_map/ppermute | solution.py:33
  179.1 24.7 %collective-permute-start.41 = (bf16[144,896]{1,0:T(8,128)(2,1)}, bf16[144,896]{1,0:T(8,128)(2,1)S(1)}, u32[]{:S(2)}, u32[]{:S(2)}) collective-permute-start(bf16[144,896]{1,0:T(8,128)(2,1)} %get-tuple-element.166), channel_id=1, source_target_pairs={{0,24},{1,25},{2,26},{3,27},{4,28},{5,29},{6,30},{7,31},{8,16},{9,... | collective-permute-start | bytes 774152 | tf_op jit(solution)/shard_map/ppermute | solution.py:33
  181.6 22.2 %collective-permute-start.42 = (bf16[144,896]{1,0:T(8,128)(2,1)}, bf16[144,896]{1,0:T(8,128)(2,1)S(1)}, u32[]{:S(2)}, u32[]{:S(2)}) collective-permute-start(bf16[144,896]{1,0:T(8,128)(2,1)} %get-tuple-element.167), channel_id=1, source_target_pairs={{0,20},{1,21},{2,22},{3,23},{4,24},{5,25},{6,26},{7,27},{8,28},{9,... | collective-permute-start | bytes 774152 | tf_op jit(solution)/shard_map/ppermute | solution.py:33
  181.7 22.1 %copy-start.12 = (bf16[128,3584]{1,0:T(8,128)(2,1)S(1)}, bf16[128,3584]{1,0:T(8,128)(2,1)}, u32[]{:S(2)}) copy-start(bf16[128,3584]{1,0:T(8,128)(2,1)} %copy-done.11) | copy-start | bytes 2752516
  (11 other events, 11.6 us)

commit v14 on v13

--- a/solution.py
+++ b/solution.py
@@ -471,28 +471,15 @@
     front_chunks = sent(after(front_chunks, row_chunks + grad_chunks[1:2]))
     back_rows = joined(after(row_chunks, [middle, grad_chunks[1]]))
     back_other = swapped(back_rows, 2)
-    down_low = swapped(after([w_down[cut:]], [back_rows])[0], 2)
-    downs = (w_down, down_top, down_low)
     grad_near = joined(after(grad_chunks, [back_rows, down_top, there_back_middle]))
     there_back_grad = passed_along(after([back_grad[0]], [grad_near])[0], -1)
-    ready = [back_other, there_back_grad, down_low]
+    ready = [back_other, there_back_grad]
     front_near = joined(after(front_chunks, ready))
     there_middle = passed_along(after([middle], [front_near])[0], 1)
+    down_low = swapped(after([w_down[cut:]], [front_near])[0], 2)
+    downs = (w_down, down_top, down_low)
     grad_near = [grad_near, swapped(after([grad_near], [front_near])[0], 1)]
-    down_back, other_back = call(
-        down_back_body,
-        [shape_of(pair, hidden_width, f32), shape_of(pair, hidden_width)],
-        (*grad_near, *downs),
-        flops=2 * work,
-    )
-    far_back = swapped(other_back, 2)
-    late = after([back_rows], [front_near])[0]
-    back_near = backward((back_rows, swapped(late, 1)), down_back)
-    back_core = swapped(back_near[1], 1)
-    (far_back,) = after([far_back], [there_middle])
-    back_far = backward((back_other, swapped(after([back_other], [front_near])[0], 1)), far_back)
-    chip = (back_far[0].astype(f32) + swapped(back_far[1], 1).astype(f32)).astype(bf16)
-    front_other = after([swapped(front_near, 2)], [back_near[0], there_middle])[0]
+    front_other = after([swapped(front_near, 2)], [there_middle])[0]
 
     front_small, back_small = after([front_small, back_small], [front_near])
     there_small = passed_along(front_small, 1)
@@ -505,7 +492,20 @@
     hidden_near = hidden(front_pieces[:2])
     hidden_far = hidden(front_pieces[2:])
     hidden_other = swapped(hidden_far, 2)
-    (hidden_other,) = after([hidden_other], [there_small, there_back_small, chip])
+    down_back, other_back = call(
+        down_back_body,
+        [shape_of(pair, hidden_width, f32), shape_of(pair, hidden_width)],
+        (*after(grad_near, [hidden_other, hidden_near]), *downs),
+        flops=2 * work,
+    )
+    far_back = swapped(other_back, 2)
+    late = after([back_rows], [front_near])[0]
+    back_near = backward((back_rows, swapped(late, 1)), down_back)
+    back_core = swapped(back_near[1], 1)
+    (far_back,) = after([far_back], [there_middle])
+    back_far = backward((back_other, swapped(after([back_other], [front_near])[0], 1)), far_back)
+    chip = (back_far[0].astype(f32) + swapped(back_far[1], 1).astype(f32)).astype(bf16)
+    (hidden_other,) = after([hidden_other], [there_small, there_back_small])
     front_own, front_core = call(
         output_body, [piece, piece], (hidden_near, hidden_other, *downs), cheap=True
     )

time: 208 us -> 229 us (1.10)
  waiting for transfers between devices: 100 us -> 122 us
    ppermute x18, waiting for transfers between devices: 21 us -> 36.9 us  [swapped(): lax.ppermute(array, 'expert', [(i, i ^ bit) for i in range(lax.axis_size(...]
    ppermute x13, waiting for transfers between devices: 35.1 us -> 42 us  [passed_along(): return lax.ppermute(array, ('section', 'expert'), pairs)]
    ppermute x18, starting transfers between devices: 10.5 us -> 6.93 us  [swapped(): lax.ppermute(array, 'expert', [(i, i ^ bit) for i in range(lax.axis_size(...]
    unnamed x68 -> x72, local copies, waits for them, and re-layouts: 9.9 us -> 10.9 us
  transfers between devices with their start and end apart: 43 -> 43, of which waited for: 17 -> 19; matrix products, arithmetic and copies ran while one was open for 2% -> 2% of each run, Pallas kernels for 15% -> 14%
where the time goes in v14:
time: 229 us
  waiting for transfers between devices  122 us (53%)
  starting transfers between devices  53.2 us (23%)
  Pallas kernels  37.4 us (16%)
  local copies, waits for them, and re-layouts  13.2 us (6%)
    ppermute x9, waiting for transfers between devices, turned(): lax.ppermute(array, 'expert', [(i, (i + by * GROUP) % length) for i in ra...  42.7 us
    ppermute x13, waiting for transfers between devices, passed_along(): return lax.ppermute(array, ('section', 'expert'), pairs)  42 us
    pallas_call x15, Pallas kernels, call(): pl.pallas_call(body, out_shape=shapes, in_specs=specs, out_specs=[pl.Bloc...  37.4 us
    ppermute x18, waiting for transfers between devices, swapped(): lax.ppermute(array, 'expert', [(i, i ^ bit) for i in range(lax.axis_size(...  36.9 us
    ppermute x13, starting transfers between devices, passed_along(): return lax.ppermute(array, ('section', 'expert'), pairs)  24.3 us
    ppermute x9, starting transfers between devices, turned(): lax.ppermute(array, 'expert', [(i, (i + by * GROUP) % length) for i in ra...  11.2 us
    unnamed x72, local copies, waits for them, and re-layouts  10.9 us
    ppermute x3, starting transfers between devices, shards(): column.append(lax.ppermute(keys_values[0], 'expert', pairs))  10.7 us
  transfers between devices with their start and end apart: 43, of which 19 were waited for; matrix products, arithmetic and copies ran while one was open for 2% of the time, Pallas kernels for 14%

profile of v14, /device:TPU:0, one launch (start us, length us, event | category | flops | bytes accessed | tf_op | source)
XLA Modules:
  0.0 228.6 jit_solution(14752382389552915396)
XLA Ops:
  0.6 1.0 copy.16
  1.6 4.9 %collective-permute-start = (bf16[128,448]{1,0:T(8,128)(2,1)S(1)}, bf16[128,448]{1,0:T(8,128)(2,1)S(1)}, u32[]{:S(2)}, u32[]{:S(2)}) collective-permute-start(bf16[128,448]{1,0:T(8,128)(2,1)S(1)} %bitcast.46), channel_id=1, source_target_pairs={{0,4},{1,5},{2,6},{3,7},{4,8},{5,9},{6,10},{7,11},{8,12},{9,13},{1... | collective-permute-start | bytes 344072 | tf_op jit(solution)/shard_map/ppermute | solution.py:379
  6.6 4.5 %collective-permute-start.1 = (bf16[128,448]{1,0:T(8,128)(2,1)S(1)}, bf16[128,448]{1,0:T(8,128)(2,1)S(1)}, u32[]{:S(2)}, u32[]{:S(2)}) collective-permute-start(bf16[128,448]{1,0:T(8,128)(2,1)S(1)} %bitcast.47), channel_id=1, source_target_pairs={{0,8},{1,9},{2,10},{3,11},{4,12},{5,13},{6,14},{7,15},{16,24},{17,... | collective-permute-start | bytes 344072 | tf_op jit(solution)/shard_map/ppermute | solution.py:379
  11.1 1.3 collective-permute-start.2
  12.4 0.8 copy.17.gate_ref
  13.2 0.7 fusion.11
  13.8 0.7 copy-done.7
  14.6 1.2 copy-done.11
  15.7 3.0 %shard_map.149 = (bf16[144,896]{1,0:T(8,128)(2,1)S(1)}, bf16[144,896]{1,0:T(8,128)(2,1)S(1)}, bf16[144,896]{1,0:T(8,128)(2,1)S(1)}, bf16[144,896]{1,0:T(8,128)(2...) custom-call(s32[1,128]{1,0:T(1,128)S(1)} %get-tuple-element.181.rout, ...), custom_call_target="tpu_custom_call" | custom-call | flops 2113929216 | bytes 3914752 | tf_op jit(solution)/shard_map/pallas_call | solution.py:55
  19.0 1.6 collective-permute-start.3
  20.9 3.4 %collective-permute-start.6 = (bf16[144,896]{1,0:T(8,128)(2,1)S(1)}, bf16[144,896]{1,0:T(8,128)(2,1)S(1)}, u32[]{:S(2)}, u32[]{:S(2)}) collective-permute-start(bf16[144,896]{1,0:T(8,128)(2,1)S(1)} %get-tuple-element.104), channel_id=1, source_target_pairs={{0,8},{1,9},{2,10},{3,11},{4,12},{5,13},{6,14},{7,15},{8,0},{9,1},... | collective-permute-start | bytes 774152 | tf_op jit(solution)/shard_map/ppermute | solution.py:42
  24.3 1.1 slice_bitcast_fusion
  25.4 6.1 %collective-permute-done.5.refs_1_ = bf16[144,896]{1,0:T(8,128)(2,1)S(1)} collective-permute-done((bf16[144,896]{1,0:T(8,128)(2,1)S(1)}, bf16[144,896]{1,0:T(8,128)(2,1)S(1)}, u32[]{:S(2)}, u32[]{:S(2)}) %collective-permute-start.5) | collective-permute-done | bytes 258080 | tf_op jit(solution)/shard_map/ppermute | solution.py:42
  31.6 0.7 copy-done.23
  32.8 7.7 %collective-permute-done.6.refs_2_ = bf16[144,896]{1,0:T(8,128)(2,1)S(1)} collective-permute-done((bf16[144,896]{1,0:T(8,128)(2,1)S(1)}, bf16[144,896]{1,0:T(8,128)(2,1)S(1)}, u32[]{:S(2)}, u32[]{:S(2)}) %collective-permute-start.6) | collective-permute-done | bytes 258080 | tf_op jit(solution)/shard_map/ppermute | solution.py:42
  40.5 0.7 copy-done.25
  41.2 1.5 collective-permute-start.17
  43.5 1.2 collective-permute-done.4.kv2
  44.8 2.7 %collective-permute-start.8 = (bf16[144,896]{1,0:T(8,128)(2,1)}, bf16[144,896]{1,0:T(8,128)(2,1)S(1)}, u32[]{:S(2)}, u32[]{:S(2)}) collective-permute-start(bf16[144,896]{1,0:T(8,128)(2,1)} %copy-done.21), channel_id=1, source_target_pairs={{0,12},{1,13},{2,14},{3,15},{4,0},{5,1},{6,2},{7,3},{8,4},{9,5},{1... | collective-permute-start | bytes 774152 | tf_op jit(solution)/shard_map/ppermute | solution.py:42
  47.4 1.2 copy-done.9
  48.6 1.2 copy-done.10
  49.8 8.5 %shard_map.150 = (bf16[128,3584]{1,0:T(8,128)(2,1)S(1)}, bf16[144,896]{1,0:T(8,128)(2,1)S(1)}, bf16[144,896]{1,0:T(8,128)(2,1)S(1)}, bf16[144,896]{1,0:T(8,128)(2,1)S(1)}, bf16[144,896]{1,0:T(8,128)(2,1)S(1)}) custom-call(s32[16]{0:T(128)S(1)} %reshape_squeeze.6.chosen_ref, s32[16]{0:T(128)S(1)} %fusion.10.index_ref, s32[1]{0:T(128)} %bitcast.4.base_ref, ...), custom_call_target="tpu_custom_call" | custom-call | flops 1593835520 | bytes 5634692 | tf_op jit(solution)/shard_map/pallas_call | solution.py:55
  58.4 0.8 collective-permute-start.14
  59.2 1.1 shard_map.151.first_ref
  60.9 2.8 %collective-permute-done.17.middle_ref = bf16[128,3584]{1,0:T(8,128)(2,1)} collective-permute-done((bf16[128,3584]{1,0:T(8,128)(2,1)}, bf16[128,3584]{1,0:T(8,128)(2,1)}, u32[]{:S(2)}, u32[]{:S(2)}) %collective-permute-start.17) | collective-permute-done | bytes 917536 | tf_op jit(solution)/shard_map/ppermute | solution.py:33
  63.8 2.6 %collective-permute-done.15.refs_3_ = bf16[144,896]{1,0:T(8,128)(2,1)S(1)} collective-permute-done((bf16[144,896]{1,0:T(8,128)(2,1)S(1)}, bf16[144,896]{1,0:T(8,128)(2,1)S(1)}, u32[]{:S(2)}, u32[]{:S(2)}) %collective-permute-start.15) | collective-permute-done | bytes 258080 | tf_op jit(solution)/shard_map/ppermute | solution.py:42
  66.4 9.8 %collective-permute-done.14.refs_2_ = bf16[144,896]{1,0:T(8,128)(2,1)S(1)} collective-permute-done((bf16[144,896]{1,0:T(8,128)(2,1)S(1)}, bf16[144,896]{1,0:T(8,128)(2,1)S(1)}, u32[]{:S(2)}, u32[]{:S(2)}) %collective-permute-start.14) | collective-permute-done | bytes 258080 | tf_op jit(solution)/shard_map/ppermute | solution.py:42
  76.2 2.0 shard_map.152.first_ref
  78.9 3.4 %collective-permute-start.11 = (bf16[144,896]{1,0:T(8,128)(2,1)S(1)}, bf16[144,896]{1,0:T(8,128)(2,1)S(1)}, u32[]{:S(2)}, u32[]{:S(2)}) collective-permute-start(bf16[144,896]{1,0:T(8,128)(2,1)S(1)} %get-tuple-element.117), channel_id=1, source_target_pairs={{0,8},{1,9},{2,10},{3,11},{4,12},{5,13},{6,14},{7,15},{8,0},{9,1},... | collective-permute-start | bytes 774152 | tf_op jit(solution)/shard_map/ppermute | solution.py:42
  82.7 7.3 %collective-permute-done.10.refs_1_ = bf16[144,896]{1,0:T(8,128)(2,1)S(1)} collective-permute-done((bf16[144,896]{1,0:T(8,128)(2,1)S(1)}, bf16[144,896]{1,0:T(8,128)(2,1)S(1)}, u32[]{:S(2)}, u32[]{:S(2)}) %collective-permute-start.10) | collective-permute-done | bytes 258080 | tf_op jit(solution)/shard_map/ppermute | solution.py:42
  89.9 9.1 %collective-permute-done.11.refs_2_ = bf16[144,896]{1,0:T(8,128)(2,1)S(1)} collective-permute-done((bf16[144,896]{1,0:T(8,128)(2,1)S(1)}, bf16[144,896]{1,0:T(8,128)(2,1)S(1)}, u32[]{:S(2)}, u32[]{:S(2)}) %collective-permute-start.11) | collective-permute-done | bytes 258080 | tf_op jit(solution)/shard_map/ppermute | solution.py:42
  99.6 1.0 copy-done.13
  100.5 1.1 shard_map.153.first_ref
  102.2 1.0 collective-permute-start.20
  103.8 19.9 %collective-permute-done.20.middle_ref = bf16[128,3584]{1,0:T(8,128)(2,1)S(1)} collective-permute-done((bf16[128,3584]{1,0:T(8,128)(2,1)S(1)}, bf16[128,3584]{1,0:T(8,128)(2,1)S(1)}, u32[]{:S(2)}, u32[]{:S(2)}) %collective-permute-start.20) | collective-permute-done | bytes 917536 | tf_op jit(solution)/shard_map/ppermute | solution.py:33
  123.7 0.9 copy-done.15
  124.6 1.3 collective-permute-done.22.first_ref
  126.5 2.0 collective-permute-done.23.second_ref
  128.5 1.3 shard_map.155
  130.4 1.2 shard_map.154.own_ref
  131.6 15.4 %collective-permute-done.24.other_ref = bf16[288,256]{1,0:T(8,128)(2,1)S(1)} collective-permute-done((bf16[288,256]{1,0:T(8,128)(2,1)S(1)}, bf16[288,256]{1,0:T(8,128)(2,1)S(1)}, u32[]{:S(2)}, u32[]{:S(2)}) %collective-permute-start.24) | collective-permute-done | bytes 147488 | tf_op jit(solution)/shard_map/ppermute | solution.py:37
  147.0 1.3 shard_map.158
  148.9 4.9 %collective-permute-done.36.back_ref = bf16[288,256]{1,0:T(8,128)(2,1)S(1)} collective-permute-done((bf16[288,256]{1,0:T(8,128)(2,1)S(1)}, bf16[288,256]{1,0:T(8,128)(2,1)S(1)}, u32[]{:S(2)}, u32[]{:S(2)}) %collective-permute-start.36) | collective-permute-done | bytes 147488 | tf_op jit(solution)/shard_map/ppermute | solution.py:37
  153.8 2.5 %shard_map.160 = (bf16[144,3584]{1,0:T(8,128)(2,1)S(1)}, bf16[144,3584]{1,0:T(8,128)(2,1)S(1)}) custom-call(bf16[144,3584]{1,0:T(8,128)(2,1)S(1)} %collective-permute-done.13.first_ref, bf16[144,3584]{1,0:T(8,128)(2,1)S(1)} %collective-permute-done.35.second_ref, bf16[288,256]{1,0:T(8,128)(2,1)S(1)} %collective-permute-done.36.back_ref, ...), custom_call_target="tpu_custom_call" | custom-call | flops 2113929216 | bytes 7946240 | tf_op jit(solution)/shard_map/pallas_call | solution.py:55
  156.4 1.6 collective-permute-start.25
  158.5 2.4 %shard_map.159 = (bf16[144,3584]{1,0:T(8,128)(2,1)S(1)}, bf16[144,3584]{1,0:T(8,128)(2,1)S(1)}) custom-call(bf16[144,3584]{1,0:T(8,128)(2,1)S(1)} %shard_map.151.first_ref, bf16[144,3584]{1,0:T(8,128)(2,1)S(1)} %collective-permute-done.32.second_ref, f32[288,256]{1,0:T(8,128)S(1)} %get-tuple-element.156.back_ref, bf16[3584,256]{1,0:T(8,128)(2,1)S(1)} %bitcast.37, ...), custom_call_target="tpu_custom_call" | custom-call | flops 2113929216 | bytes 8093696 | tf_op jit(solution)/shard_map/pallas_call | solution.py:55
  161.6 1.2 shard_map.156
  162.9 1.2 add_convert_fusion
  164.7 0.9 collective-permute-done.27.refs_1_
  165.5 1.9 shard_map.157
  167.4 1.2 collective-permute-start.28
  168.6 4.5 %collective-permute-start.29 = (bf16[144,896]{1,0:T(8,128)(2,1)}, bf16[144,896]{1,0:T(8,128)(2,1)}, u32[]{:S(2)}, u32[]{:S(2)}) collective-permute-start(bf16[144,896]{1,0:T(8,128)(2,1)} %get-tuple-element.149), channel_id=1, source_target_pairs={{0,28},{1,29},{2,30},{3,31},{4,16},{5,17},{6,18},{7,19},{8,20},{9,... | collective-permute-start | bytes 774152 | tf_op jit(solution)/shard_map/ppermute | solution.py:33
  173.1 4.0 %collective-permute-start.30 = (bf16[144,896]{1,0:T(8,128)(2,1)}, bf16[144,896]{1,0:T(8,128)(2,1)}, u32[]{:S(2)}, u32[]{:S(2)}) collective-permute-start(bf16[144,896]{1,0:T(8,128)(2,1)} %get-tuple-element.150), channel_id=1, source_target_pairs={{0,24},{1,25},{2,26},{3,27},{4,28},{5,29},{6,30},{7,31},{8,16},{9,... | collective-permute-start | bytes 774152 | tf_op jit(solution)/shard_map/ppermute | solution.py:33
  177.0 1.0 copy-done.5
  178.3 11.3 %collective-permute-done.38.refs_2_ = bf16[144,3584]{1,0:T(8,128)(2,1)S(1)} collective-permute-done((bf16[144,3584]{1,0:T(8,128)(2,1)}, bf16[144,3584]{1,0:T(8,128)(2,1)S(1)}, u32[]{:S(2)}, u32[]{:S(2)}) %collective-permute-start.38) | collective-permute-done | bytes 1032224 | tf_op jit(solution)/shard_map/ppermute | solution.py:37
  189.5 1.2 copy-done.6
  190.8 2.1 shard_map.161
  192.8 1.0 collective-permute-start.39
  193.8 4.6 %collective-permute-start.40 = (bf16[144,896]{1,0:T(8,128)(2,1)}, bf16[144,896]{1,0:T(8,128)(2,1)}, u32[]{:S(2)}, u32[]{:S(2)}) collective-permute-start(bf16[144,896]{1,0:T(8,128)(2,1)} %get-tuple-element.169), channel_id=1, source_target_pairs={{0,28},{1,29},{2,30},{3,31},{4,16},{5,17},{6,18},{7,19},{8,20},{9,... | collective-permute-start | bytes 774152 | tf_op jit(solution)/shard_map/ppermute | solution.py:33
  198.5 3.8 %collective-permute-start.41 = (bf16[144,896]{1,0:T(8,128)(2,1)}, bf16[144,896]{1,0:T(8,128)(2,1)}, u32[]{:S(2)}, u32[]{:S(2)}) collective-permute-start(bf16[144,896]{1,0:T(8,128)(2,1)} %get-tuple-element.170), channel_id=1, source_target_pairs={{0,24},{1,25},{2,26},{3,27},{4,28},{5,29},{6,30},{7,31},{8,16},{9,... | collective-permute-start | bytes 774152 | tf_op jit(solution)/shard_map/ppermute | solution.py:33
  202.5 3.6 %shard_map.162 = bf16[128,3584]{1,0:T(8,128)(2,1)} custom-call(s32[128,1]{1,0:T(8,128)S(1)} %copy.18.route_ref, f32[128,1]{1,0:T(8,128)S(1)} %copy.19.gate_ref, bf16[128,3584]{1,0:T(8,128)(2,1)S(1)} %copy-done.16, bf16[144,896]{1,0:T(8,128)(2,1)} %collective-permute-done.28.refs_0_, bf16[144,896]{1,0:T(8,128)(2,1)} %collective-permute-done.29.refs_1_, ...), custom_call_target="tpu_custom_call" | custom-call | flops 1056964608 | bytes 2868224 | tf_op jit(solution)/shard_map/pallas_call | solution.py:55
  206.1 7.1 %collective-permute-done.39.refs_0_ = bf16[144,896]{1,0:T(8,128)(2,1)} collective-permute-done((bf16[144,896]{1,0:T(8,128)(2,1)}, bf16[144,896]{1,0:T(8,128)(2,1)}, u32[]{:S(2)}, u32[]{:S(2)}) %collective-permute-start.39) | collective-permute-done | bytes 258080 | tf_op jit(solution)/shard_map/ppermute | solution.py:33
  213.2 11.2 %collective-permute-done.41.refs_2_ = bf16[144,896]{1,0:T(8,128)(2,1)} collective-permute-done((bf16[144,896]{1,0:T(8,128)(2,1)}, bf16[144,896]{1,0:T(8,128)(2,1)}, u32[]{:S(2)}, u32[]{:S(2)}) %collective-permute-start.41) | collective-permute-done | bytes 258080 | tf_op jit(solution)/shard_map/ppermute | solution.py:33
  224.3 4.2 %shard_map.163 = bf16[128,3584]{1,0:T(8,128)(2,1)} custom-call(s32[128,1]{1,0:T(8,128)S(1)} %copy.20.route_ref, f32[1,3584]{1,0:T(1,128)S(1)} %slice.35.gain_ref, bf16[128,3584]{1,0:T(8,128)(2,1)} %collective-permute-done.17.middle_ref, bf16[128,3584]{1,0:T(8,128)(2,1)S(1)} %copy-done.14, bf16[144,896]{1,0:T(8,128)(2,1)} %collective-permute-done.39.refs_0_, ...), custom_call_target="tpu_custom_call" | custom-call | flops 1056964608 | bytes 3799552 | tf_op jit(solution)/shard_map/pallas_call | solution.py:55
  (127 shorter events, 9.3 us)
Async XLA Ops:
  1.6 17.2 %collective-permute-start = (bf16[128,448]{1,0:T(8,128)(2,1)S(1)}, bf16[128,448]{1,0:T(8,128)(2,1)S(1)}, u32[]{:S(2)}, u32[]{:S(2)}) collective-permute-start(bf16[128,448]{1,0:T(8,128)(2,1)S(1)} %bitcast.46), channel_id=1, source_target_pairs={{0,4},{1,5},{2,6},{3,7},{4,8},{5,9},{6,10},{7,11},{8,12},{9,13},{1... | collective-permute-start | bytes 344072 | tf_op jit(solution)/shard_map/ppermute | solution.py:379
  6.6 12.3 %collective-permute-start.1 = (bf16[128,448]{1,0:T(8,128)(2,1)S(1)}, bf16[128,448]{1,0:T(8,128)(2,1)S(1)}, u32[]{:S(2)}, u32[]{:S(2)}) collective-permute-start(bf16[128,448]{1,0:T(8,128)(2,1)S(1)} %bitcast.47), channel_id=1, source_target_pairs={{0,8},{1,9},{2,10},{3,11},{4,12},{5,13},{6,14},{7,15},{16,24},{17,... | collective-permute-start | bytes 344072 | tf_op jit(solution)/shard_map/ppermute | solution.py:379
  11.1 7.8 %collective-permute-start.2 = (bf16[128,448]{1,0:T(8,128)(2,1)S(1)}, bf16[128,448]{1,0:T(8,128)(2,1)S(1)}, u32[]{:S(2)}, u32[]{:S(2)}) collective-permute-start(bf16[128,448]{1,0:T(8,128)(2,1)S(1)} %bitcast.48), channel_id=1, source_target_pairs={{0,12},{1,13},{2,14},{3,15},{16,28},{17,29},{18,30},{19,31}} | collective-permute-start | bytes 344072 | tf_op jit(solution)/shard_map/ppermute | solution.py:379
  15.7 8.6 %copy-start = (bf16[1,1,256,3584]{3,2,1,0:T(8,128)(2,1)S(1)}, bf16[1,1,256,3584]{3,2,1,0:T(8,128)(2,1)}, u32[]{:S(2)}) copy-start(bf16[1,1,256,3584]{3,2,1,0:T(8,128)(2,1)} %param.27) | copy-start | bytes 5505028
  18.8 24.0 %copy-start.17 = (bf16[144,896]{1,0:T(8,128)(2,1)}, bf16[144,896]{1,0:T(8,128)(2,1)S(1)}, u32[]{:S(2)}) copy-start(bf16[144,896]{1,0:T(8,128)(2,1)S(1)} %get-tuple-element.126) | copy-start | bytes 774148
  18.8 24.0 %copy-start.19 = (bf16[144,896]{1,0:T(8,128)(2,1)}, bf16[144,896]{1,0:T(8,128)(2,1)S(1)}, u32[]{:S(2)}) copy-start(bf16[144,896]{1,0:T(8,128)(2,1)S(1)} %get-tuple-element.128) | copy-start | bytes 774148
  18.8 24.0 %copy-start.21 = (bf16[144,896]{1,0:T(8,128)(2,1)}, bf16[144,896]{1,0:T(8,128)(2,1)S(1)}, u32[]{:S(2)}) copy-start(bf16[144,896]{1,0:T(8,128)(2,1)S(1)} %get-tuple-element.112) | copy-start | bytes 774148
  18.8 24.0 %copy-start.22 = (bf16[144,896]{1,0:T(8,128)(2,1)}, bf16[144,896]{1,0:T(8,128)(2,1)S(1)}, u32[]{:S(2)}) copy-start(bf16[144,896]{1,0:T(8,128)(2,1)S(1)} %get-tuple-element.114) | copy-start | bytes 774148
  18.8 24.0 %copy-start.27 = (bf16[144,896]{1,0:T(8,128)(2,1)}, bf16[144,896]{1,0:T(8,128)(2,1)S(1)}, u32[]{:S(2)}) copy-start(bf16[144,896]{1,0:T(8,128)(2,1)S(1)} %get-tuple-element.131.refs_0_) | copy-start | bytes 774148
  18.8 24.0 %copy-start.29 = (bf16[144,896]{1,0:T(8,128)(2,1)}, bf16[144,896]{1,0:T(8,128)(2,1)S(1)}, u32[]{:S(2)}) copy-start(bf16[144,896]{1,0:T(8,128)(2,1)S(1)} %get-tuple-element.120.refs_0_) | copy-start | bytes 774148
  18.8 24.5 %copy-start.31 = (s32[1,2,2,4]{3,2,1,0:T(2,128)S(1)}, s32[1,2,2,4]{3,2,1,0:T(2,128)}, u32[]{:S(2)}) copy-start(s32[1,2,2,4]{3,2,1,0:T(2,128)} %param.17) | copy-start | bytes 196
  18.8 24.6 %copy-start.33 = (s32[1,128,1]{1,2,0:T(1,128)S(1)}, s32[1,128,1]{1,2,0:T(1,128)}, u32[]{:S(2)}) copy-start(s32[1,128,1]{1,2,0:T(1,128)} %param.18) | copy-start | bytes 1540
  18.8 28.6 %copy-start.8 = (f32[1,3584]{1,0:T(1,128)S(1)}, f32[1,3584]{1,0:T(1,128)}, u32[]{:S(2)}) copy-start(f32[1,3584]{1,0:T(1,128)} %gain_ref.3) | copy-start | bytes 43012
  19.0 23.8 %collective-permute-start.3 = (bf16[512,448]{1,0:T(8,128)(2,1)S(1)}, bf16[512,448]{1,0:T(8,128)(2,1)}, u32[]{:S(2)}, u32[]{:S(2)}) collective-permute-start(bf16[512,448]{1,0:T(8,128)(2,1)S(1)} %constant_dynamic-update-slice_fusion.kv0), channel_id=1, source_target_pairs={{0,2},{1,3},{2,0},{3,1},{4,6},{5,7},{6,4},{7,5},{8,10},{9,11},{10,... | collective-permute-start | bytes 1376264 | tf_op jit(solution)/shard_map/ppermute | solution.py:37
  20.5 11.0 %collective-permute-start.5 = (bf16[144,896]{1,0:T(8,128)(2,1)S(1)}, bf16[144,896]{1,0:T(8,128)(2,1)S(1)}, u32[]{:S(2)}, u32[]{:S(2)}) collective-permute-start(bf16[144,896]{1,0:T(8,128)(2,1)S(1)} %get-tuple-element.103), channel_id=1, source_target_pairs={{0,4},{1,5},{2,6},{3,7},{4,8},{5,9},{6,10},{7,11},{8,12},{9,13},{1... | collective-permute-start | bytes 774152 | tf_op jit(solution)/shard_map/ppermute | solution.py:42
  20.9 19.6 %collective-permute-start.6 = (bf16[144,896]{1,0:T(8,128)(2,1)S(1)}, bf16[144,896]{1,0:T(8,128)(2,1)S(1)}, u32[]{:S(2)}, u32[]{:S(2)}) collective-permute-start(bf16[144,896]{1,0:T(8,128)(2,1)S(1)} %get-tuple-element.104), channel_id=1, source_target_pairs={{0,8},{1,9},{2,10},{3,11},{4,12},{5,13},{6,14},{7,15},{8,0},{9,1},... | collective-permute-start | bytes 774152 | tf_op jit(solution)/shard_map/ppermute | solution.py:42
  32.2 44.0 %collective-permute-start.16 = (bf16[160,3584]{1,0:T(8,128)(2,1)}, bf16[160,3584]{1,0:T(8,128)(2,1)S(1)}, u32[]{:S(2)}, u32[]{:S(2)}) collective-permute-start(bf16[160,3584]{1,0:T(8,128)(2,1)} %slice_bitcast_fusion), channel_id=1, source_target_pairs={{0,2},{1,3},{2,0},{3,1},{4,6},{5,7},{6,4},{7,5},{8,10},{9,11},{10,... | collective-permute-start | bytes 3440648 | tf_op jit(solution)/shard_map/ppermute | solution.py:37
  41.2 22.6 %collective-permute-start.17 = (bf16[128,3584]{1,0:T(8,128)(2,1)}, bf16[128,3584]{1,0:T(8,128)(2,1)}, u32[]{:S(2)}, u32[]{:S(2)}) collective-permute-start(bf16[128,3584]{1,0:T(8,128)(2,1)} %bitcast.10.middle_ref), channel_id=1, source_target_pairs={{0,16},{1,17},{2,18},{3,19},{4,20},{5,21},{6,22},{7,23},{8,24},{9,... | collective-permute-start | bytes 2752520 | tf_op jit(solution)/shard_map/ppermute | solution.py:33
  42.7 2.0 collective-permute-start.4
  42.8 4.6 %collective-permute-start.7 = (bf16[512,448]{1,0:T(8,128)(2,1)}, bf16[512,448]{1,0:T(8,128)(2,1)}, u32[]{:S(2)}, u32[]{:S(2)}) collective-permute-start(bf16[512,448]{1,0:T(8,128)(2,1)} %collective-permute-done.3.kv1), channel_id=1, source_target_pairs={{0,1},{1,0},{2,3},{3,2},{4,5},{5,4},{6,7},{7,6},{8,9},{9,8},{10,11... | collective-permute-start | bytes 1376264 | tf_op jit(solution)/shard_map/ppermute | solution.py:37
  43.4 15.0 %collective-permute-start.9 = (bf16[144,896]{1,0:T(8,128)(2,1)}, bf16[144,896]{1,0:T(8,128)(2,1)}, u32[]{:S(2)}, u32[]{:S(2)}) collective-permute-start(bf16[144,896]{1,0:T(8,128)(2,1)} %copy-done.22), channel_id=1, source_target_pairs={{0,4},{1,5},{2,6},{3,7},{4,8},{5,9},{6,10},{7,11},{8,12},{9,13},{1... | collective-permute-start | bytes 774152 | tf_op jit(solution)/shard_map/ppermute | solution.py:42
  44.8 14.4 %collective-permute-start.8 = (bf16[144,896]{1,0:T(8,128)(2,1)}, bf16[144,896]{1,0:T(8,128)(2,1)S(1)}, u32[]{:S(2)}, u32[]{:S(2)}) collective-permute-start(bf16[144,896]{1,0:T(8,128)(2,1)} %copy-done.21), channel_id=1, source_target_pairs={{0,12},{1,13},{2,14},{3,15},{4,0},{5,1},{6,2},{7,3},{8,4},{9,5},{1... | collective-permute-start | bytes 774152 | tf_op jit(solution)/shard_map/ppermute | solution.py:42
  49.8 8.6 %copy-start.18 = (bf16[144,896]{1,0:T(8,128)(2,1)S(1)}, bf16[144,896]{1,0:T(8,128)(2,1)}, u32[]{:S(2)}) copy-start(bf16[144,896]{1,0:T(8,128)(2,1)} %copy-done.17) | copy-start | bytes 774148
  49.8 9.4 %copy-start.24 = (bf16[144,896]{1,0:T(8,128)(2,1)S(1)}, bf16[144,896]{1,0:T(8,128)(2,1)}, u32[]{:S(2)}) copy-start(bf16[144,896]{1,0:T(8,128)(2,1)} %copy-done.23) | copy-start | bytes 774148
  49.8 9.4 %copy-start.26 = (bf16[144,896]{1,0:T(8,128)(2,1)S(1)}, bf16[144,896]{1,0:T(8,128)(2,1)}, u32[]{:S(2)}) copy-start(bf16[144,896]{1,0:T(8,128)(2,1)} %copy-done.25) | copy-start | bytes 774148
  49.8 9.4 %copy-start.30 = (bf16[144,896]{1,0:T(8,128)(2,1)S(1)}, bf16[144,896]{1,0:T(8,128)(2,1)}, u32[]{:S(2)}) copy-start(bf16[144,896]{1,0:T(8,128)(2,1)} %copy-done.29) | copy-start | bytes 774148
  58.3 17.9 %copy-start.28 = (bf16[144,896]{1,0:T(8,128)(2,1)S(1)}, bf16[144,896]{1,0:T(8,128)(2,1)}, u32[]{:S(2)}) copy-start(bf16[144,896]{1,0:T(8,128)(2,1)} %copy-done.27) | copy-start | bytes 774148
  58.3 8.1 %collective-permute-start.15 = (bf16[144,896]{1,0:T(8,128)(2,1)S(1)}, bf16[144,896]{1,0:T(8,128)(2,1)S(1)}, u32[]{:S(2)}, u32[]{:S(2)}) collective-permute-start(bf16[144,896]{1,0:T(8,128)(2,1)S(1)} %copy-done.20), channel_id=1, source_target_pairs={{0,12},{1,13},{2,14},{3,15},{4,0},{5,1},{6,2},{7,3},{8,4},{9,5},{1... | collective-permute-start | bytes 774152 | tf_op jit(solution)/shard_map/ppermute | solution.py:42
  58.4 17.8 %collective-permute-start.14 = (bf16[144,896]{1,0:T(8,128)(2,1)S(1)}, bf16[144,896]{1,0:T(8,128)(2,1)S(1)}, u32[]{:S(2)}, u32[]{:S(2)}) collective-permute-start(bf16[144,896]{1,0:T(8,128)(2,1)S(1)} %copy-done.18), channel_id=1, source_target_pairs={{0,8},{1,9},{2,10},{3,11},{4,12},{5,13},{6,14},{7,15},{8,0},{9,1},... | collective-permute-start | bytes 774152 | tf_op jit(solution)/shard_map/ppermute | solution.py:42
  60.3 17.9 %copy-start.12 = (bf16[1,128,3584]{2,1,0:T(8,128)(2,1)S(1)}, bf16[1,128,3584]{2,1,0:T(8,128)(2,1)}, u32[]{:S(2)}) copy-start(bf16[1,128,3584]{2,1,0:T(8,128)(2,1)} %param.21) | copy-start | bytes 2752516
  60.3 38.7 %collective-permute-start.13 = (bf16[144,3584]{1,0:T(8,128)(2,1)S(1)}, bf16[144,3584]{1,0:T(8,128)(2,1)S(1)}, u32[]{:S(2)}, u32[]{:S(2)}) collective-permute-start(bf16[144,3584]{1,0:T(8,128)(2,1)S(1)} %shard_map.151.first_ref), channel_id=1, source_target_pairs={{0,2},{1,3},{2,0},{3,1},{4,6},{5,7},{6,4},{7,5},{8,10},{9,11},{10,... | collective-permute-start | bytes 3096584 | tf_op jit(solution)/shard_map/ppermute | solution.py:37
  78.3 21.3 %collective-permute-start.18 = (bf16[128,3584]{1,0:T(8,128)(2,1)S(1)}, bf16[128,3584]{1,0:T(8,128)(2,1)S(1)}, u32[]{:S(2)}, u32[]{:S(2)}) collective-permute-start(bf16[128,3584]{1,0:T(8,128)(2,1)S(1)} %bitcast.45), channel_id=1, source_target_pairs={{0,16},{1,17},{2,18},{3,19},{4,20},{5,21},{6,22},{7,23},{8,24},{9,... | collective-permute-start | bytes 2752520 | tf_op jit(solution)/shard_map/ppermute | solution.py:33
  78.8 49.6 %copy-start.1 = (bf16[1,1,3584,256]{3,2,1,0:T(8,128)(2,1)S(1)}, bf16[1,1,3584,256]{3,2,1,0:T(8,128)(2,1)}, u32[]{:S(2)}) copy-start(bf16[1,1,3584,256]{3,2,1,0:T(8,128)(2,1)} %param.25) | copy-start | bytes 5505028
  78.8 49.6 %copy-start.2 = (bf16[1,1,3584,256]{3,2,1,0:T(8,128)(2,1)S(1)}, bf16[1,1,3584,256]{3,2,1,0:T(8,128)(2,1)}, u32[]{:S(2)}) copy-start(bf16[1,1,3584,256]{3,2,1,0:T(8,128)(2,1)} %param.26) | copy-start | bytes 5505028
  78.8 11.1 %collective-permute-start.10 = (bf16[144,896]{1,0:T(8,128)(2,1)S(1)}, bf16[144,896]{1,0:T(8,128)(2,1)S(1)}, u32[]{:S(2)}, u32[]{:S(2)}) collective-permute-start(bf16[144,896]{1,0:T(8,128)(2,1)S(1)} %get-tuple-element.116), channel_id=1, source_target_pairs={{0,4},{1,5},{2,6},{3,7},{4,8},{5,9},{6,10},{7,11},{8,12},{9,13},{1... | collective-permute-start | bytes 774152 | tf_op jit(solution)/shard_map/ppermute | solution.py:42
  78.9 20.1 %collective-permute-start.11 = (bf16[144,896]{1,0:T(8,128)(2,1)S(1)}, bf16[144,896]{1,0:T(8,128)(2,1)S(1)}, u32[]{:S(2)}, u32[]{:S(2)}) collective-permute-start(bf16[144,896]{1,0:T(8,128)(2,1)S(1)} %get-tuple-element.117), channel_id=1, source_target_pairs={{0,8},{1,9},{2,10},{3,11},{4,12},{5,13},{6,14},{7,15},{8,0},{9,1},... | collective-permute-start | bytes 774152 | tf_op jit(solution)/shard_map/ppermute | solution.py:42
  82.3 16.8 %collective-permute-start.12 = (bf16[144,896]{1,0:T(8,128)(2,1)S(1)}, bf16[144,896]{1,0:T(8,128)(2,1)S(1)}, u32[]{:S(2)}, u32[]{:S(2)}) collective-permute-start(bf16[144,896]{1,0:T(8,128)(2,1)S(1)} %get-tuple-element.118), channel_id=1, source_target_pairs={{0,12},{1,13},{2,14},{3,15},{4,0},{5,1},{6,2},{7,3},{8,4},{9,5},{1... | collective-permute-start | bytes 774152 | tf_op jit(solution)/shard_map/ppermute | solution.py:42
  101.6 24.2 %collective-permute-start.22 = (bf16[144,3584]{1,0:T(8,128)(2,1)S(1)}, bf16[144,3584]{1,0:T(8,128)(2,1)S(1)}, u32[]{:S(2)}, u32[]{:S(2)}) collective-permute-start(bf16[144,3584]{1,0:T(8,128)(2,1)S(1)} %shard_map.153.first_ref), channel_id=1, source_target_pairs={{0,2},{1,3},{2,0},{3,1},{4,6},{5,7},{6,4},{7,5},{8,10},{9,11},{10,... | collective-permute-start | bytes 3096584 | tf_op jit(solution)/shard_map/ppermute | solution.py:37
  102.2 21.4 %collective-permute-start.20 = (bf16[128,3584]{1,0:T(8,128)(2,1)S(1)}, bf16[128,3584]{1,0:T(8,128)(2,1)S(1)}, u32[]{:S(2)}, u32[]{:S(2)}) collective-permute-start(bf16[128,3584]{1,0:T(8,128)(2,1)S(1)} %get-tuple-element.141), channel_id=1, source_target_pairs={{0,16},{1,17},{2,18},{3,19},{4,20},{5,21},{6,22},{7,23},{8,24},{9,... | collective-permute-start | bytes 2752520 | tf_op jit(solution)/shard_map/ppermute | solution.py:33
  103.3 27.1 %collective-permute-start.21 = (bf16[144,3584]{1,0:T(8,128)(2,1)S(1)}, bf16[144,3584]{1,0:T(8,128)(2,1)S(1)}, u32[]{:S(2)}, u32[]{:S(2)}) collective-permute-start(bf16[144,3584]{1,0:T(8,128)(2,1)S(1)} %shard_map.153.first_ref), channel_id=1, source_target_pairs={{0,1},{1,0},{2,3},{3,2},{4,5},{5,4},{6,7},{7,6},{8,9},{9,8},{10,11... | collective-permute-start | bytes 3096584 | tf_op jit(solution)/shard_map/ppermute | solution.py:37
  103.3 28.3 %collective-permute-start.33 = (bf16[144,3584]{1,0:T(8,128)(2,1)S(1)}, bf16[144,3584]{1,0:T(8,128)(2,1)S(1)}, u32[]{:S(2)}, u32[]{:S(2)}) collective-permute-start(bf16[144,3584]{1,0:T(8,128)(2,1)S(1)} %shard_map.152.first_ref), channel_id=1, source_target_pairs={{0,1},{1,0},{2,3},{3,2},{4,5},{5,4},{6,7},{7,6},{8,9},{9,8},{10,11... | collective-permute-start | bytes 3096584 | tf_op jit(solution)/shard_map/ppermute | solution.py:37
  103.8 50.0 %collective-permute-start.35 = (bf16[144,3584]{1,0:T(8,128)(2,1)S(1)}, bf16[144,3584]{1,0:T(8,128)(2,1)S(1)}, u32[]{:S(2)}, u32[]{:S(2)}) collective-permute-start(bf16[144,3584]{1,0:T(8,128)(2,1)S(1)} %collective-permute-done.13.first_ref), channel_id=1, source_target_pairs={{0,1},{1,0},{2,3},{3,2},{4,5},{5,4},{6,7},{7,6},{8,9},{9,8},{10,11... | collective-permute-start | bytes 3096584 | tf_op jit(solution)/shard_map/ppermute | solution.py:37
  125.8 2.6 %collective-permute-start.23 = (bf16[144,3584]{1,0:T(8,128)(2,1)S(1)}, bf16[144,3584]{1,0:T(8,128)(2,1)S(1)}, u32[]{:S(2)}, u32[]{:S(2)}) collective-permute-start(bf16[144,3584]{1,0:T(8,128)(2,1)S(1)} %collective-permute-done.22.first_ref), channel_id=1, source_target_pairs={{0,1},{1,0},{2,3},{3,2},{4,5},{5,4},{6,7},{7,6},{8,9},{9,8},{10,11... | collective-permute-start | bytes 3096584 | tf_op jit(solution)/shard_map/ppermute | solution.py:37
  125.9 21.1 %collective-permute-start.26 = (bf16[96,3584]{1,0:T(8,128)(2,1)S(1)}, bf16[96,3584]{1,0:T(8,128)(2,1)S(1)}, u32[]{:S(2)}, u32[]{:S(2)}) collective-permute-start(bf16[96,3584]{1,0:T(8,128)(2,1)S(1)} %slice_bitcast_fusion.1), channel_id=1, source_target_pairs={{0,2},{1,3},{2,0},{3,1},{4,6},{5,7},{6,4},{7,5},{8,10},{9,11},{10,... | collective-permute-start | bytes 2064392 | tf_op jit(solution)/shard_map/ppermute | solution.py:37
  129.7 17.2 %collective-permute-start.24 = (bf16[288,256]{1,0:T(8,128)(2,1)S(1)}, bf16[288,256]{1,0:T(8,128)(2,1)S(1)}, u32[]{:S(2)}, u32[]{:S(2)}) collective-permute-start(bf16[288,256]{1,0:T(8,128)(2,1)S(1)} %shard_map.155), channel_id=1, source_target_pairs={{0,2},{1,3},{2,0},{3,1},{4,6},{5,7},{6,4},{7,5},{8,10},{9,11},{10,... | collective-permute-start | bytes 442376 | tf_op jit(solution)/shard_map/ppermute | solution.py:37
  148.3 5.5 %collective-permute-start.36 = (bf16[288,256]{1,0:T(8,128)(2,1)S(1)}, bf16[288,256]{1,0:T(8,128)(2,1)S(1)}, u32[]{:S(2)}, u32[]{:S(2)}) collective-permute-start(bf16[288,256]{1,0:T(8,128)(2,1)S(1)} %get-tuple-element.160), channel_id=1, source_target_pairs={{0,2},{1,3},{2,0},{3,1},{4,6},{5,7},{6,4},{7,5},{8,10},{9,11},{10,... | collective-permute-start | bytes 442376 | tf_op jit(solution)/shard_map/ppermute | solution.py:37
  148.9 9.6 %collective-permute-start.32 = (bf16[144,3584]{1,0:T(8,128)(2,1)S(1)}, bf16[144,3584]{1,0:T(8,128)(2,1)S(1)}, u32[]{:S(2)}, u32[]{:S(2)}) collective-permute-start(bf16[144,3584]{1,0:T(8,128)(2,1)S(1)} %shard_map.151.first_ref), channel_id=1, source_target_pairs={{0,1},{1,0},{2,3},{3,2},{4,5},{5,4},{6,7},{7,6},{8,9},{9,8},{10,11... | collective-permute-start | bytes 3096584 | tf_op jit(solution)/shard_map/ppermute | solution.py:37
  156.3 6.6 %collective-permute-start.37 = (bf16[144,3584]{1,0:T(8,128)(2,1)S(1)}, bf16[144,3584]{1,0:T(8,128)(2,1)S(1)}, u32[]{:S(2)}, u32[]{:S(2)}) collective-permute-start(bf16[144,3584]{1,0:T(8,128)(2,1)S(1)} %get-tuple-element.163), channel_id=1, source_target_pairs={{0,1},{1,0},{2,3},{3,2},{4,5},{5,4},{6,7},{7,6},{8,9},{9,8},{10,11... | collective-permute-start | bytes 3096584 | tf_op jit(solution)/shard_map/ppermute | solution.py:37
  156.4 5.2 %collective-permute-start.25 = (f32[1,3712]{1,0:T(1,128)S(1)}, f32[1,3712]{1,0:T(1,128)S(1)}, u32[]{:S(2)}, u32[]{:S(2)}) collective-permute-start(f32[1,3712]{1,0:T(1,128)S(1)} %pad_maximum_fusion), channel_id=1, source_target_pairs={{0,16},{1,17},{2,18},{3,19},{4,20},{5,21},{6,22},{7,23},{8,24},{9,... | collective-permute-start | bytes 44552 | tf_op jit(solution)/shard_map/ppermute | solution.py:33
  158.0 3.6 %collective-permute-start.19 = (f32[1,256]{1,0:T(1,128)S(1)}, f32[1,256]{1,0:T(1,128)S(1)}, u32[]{:S(2)}, u32[]{:S(2)}) collective-permute-start(f32[1,256]{1,0:T(1,128)S(1)} %maximum_bitcast_fusion), channel_id=1, source_target_pairs={{0,16},{1,17},{2,18},{3,19},{4,20},{5,21},{6,22},{7,23},{8,24},{9,... | collective-permute-start | bytes 3080 | tf_op jit(solution)/shard_map/ppermute | solution.py:33
  161.0 16.1 %collective-permute-start.34 = (bf16[144,3584]{1,0:T(8,128)(2,1)S(1)}, bf16[144,3584]{1,0:T(8,128)(2,1)S(1)}, u32[]{:S(2)}, u32[]{:S(2)}) collective-permute-start(bf16[144,3584]{1,0:T(8,128)(2,1)S(1)} %get-tuple-element.158), channel_id=1, source_target_pairs={{0,1},{1,0},{2,3},{3,2},{4,5},{5,4},{6,7},{7,6},{8,9},{9,8},{10,11... | collective-permute-start | bytes 3096584 | tf_op jit(solution)/shard_map/ppermute | solution.py:37
  162.8 2.7 %collective-permute-start.27 = (bf16[144,3584]{1,0:T(8,128)(2,1)S(1)}, bf16[144,3584]{1,0:T(8,128)(2,1)S(1)}, u32[]{:S(2)}, u32[]{:S(2)}) collective-permute-start(bf16[144,3584]{1,0:T(8,128)(2,1)S(1)} %get-tuple-element.147), channel_id=1, source_target_pairs={{0,1},{1,0},{2,3},{3,2},{4,5},{5,4},{6,7},{7,6},{8,9},{9,8},{10,11... | collective-permute-start | bytes 3096584 | tf_op jit(solution)/shard_map/ppermute | solution.py:37
  164.1 25.4 %copy-start.4 = (bf16[144,3584]{1,0:T(8,128)(2,1)S(1)}, bf16[144,3584]{1,0:T(8,128)(2,1)}, u32[]{:S(2)}) copy-start(bf16[144,3584]{1,0:T(8,128)(2,1)} %copy-done.3) | copy-start | bytes 3096580
  164.1 25.4 %collective-permute-start.38 = (bf16[144,3584]{1,0:T(8,128)(2,1)}, bf16[144,3584]{1,0:T(8,128)(2,1)S(1)}, u32[]{:S(2)}, u32[]{:S(2)}) collective-permute-start(bf16[144,3584]{1,0:T(8,128)(2,1)} %add_convert_fusion), channel_id=1, source_target_pairs={{0,2},{1,3},{2,0},{3,1},{4,6},{5,7},{6,4},{7,5},{8,10},{9,11},{10,... | collective-permute-start | bytes 3096584 | tf_op jit(solution)/shard_map/ppermute | solution.py:37
  165.5 36.9 %copy-start.16 = (bf16[128,3584]{1,0:T(8,128)(2,1)S(1)}, bf16[128,3584]{1,0:T(8,128)(2,1)}, u32[]{:S(2)}) copy-start(bf16[128,3584]{1,0:T(8,128)(2,1)} %copy-done.15) | copy-start | bytes 2752516
  167.4 26.4 %collective-permute-start.28 = (bf16[144,896]{1,0:T(8,128)(2,1)}, bf16[144,896]{1,0:T(8,128)(2,1)}, u32[]{:S(2)}, u32[]{:S(2)}) collective-permute-start(bf16[144,896]{1,0:T(8,128)(2,1)} %get-tuple-element.148), channel_id=1, source_target_pairs={{0,16},{1,17},{2,18},{3,19},{4,20},{5,21},{6,22},{7,23},{8,24},{9,... | collective-permute-start | bytes 774152 | tf_op jit(solution)/shard_map/ppermute | solution.py:33
  168.6 29.9 %collective-permute-start.29 = (bf16[144,896]{1,0:T(8,128)(2,1)}, bf16[144,896]{1,0:T(8,128)(2,1)}, u32[]{:S(2)}, u32[]{:S(2)}) collective-permute-start(bf16[144,896]{1,0:T(8,128)(2,1)} %get-tuple-element.149), channel_id=1, source_target_pairs={{0,28},{1,29},{2,30},{3,31},{4,16},{5,17},{6,18},{7,19},{8,20},{9,... | collective-permute-start | bytes 774152 | tf_op jit(solution)/shard_map/ppermute | solution.py:33
  173.1 29.2 %collective-permute-start.30 = (bf16[144,896]{1,0:T(8,128)(2,1)}, bf16[144,896]{1,0:T(8,128)(2,1)}, u32[]{:S(2)}, u32[]{:S(2)}) collective-permute-start(bf16[144,896]{1,0:T(8,128)(2,1)} %get-tuple-element.150), channel_id=1, source_target_pairs={{0,24},{1,25},{2,26},{3,27},{4,28},{5,29},{6,30},{7,31},{8,16},{9,... | collective-permute-start | bytes 774152 | tf_op jit(solution)/shard_map/ppermute | solution.py:33
  178.0 24.4 %collective-permute-start.31 = (bf16[144,896]{1,0:T(8,128)(2,1)S(1)}, bf16[144,896]{1,0:T(8,128)(2,1)}, u32[]{:S(2)}, u32[]{:S(2)}) collective-permute-start(bf16[144,896]{1,0:T(8,128)(2,1)S(1)} %get-tuple-element.151), channel_id=1, source_target_pairs={{0,20},{1,21},{2,22},{3,23},{4,24},{5,25},{6,26},{7,27},{8,28},{9,... | collective-permute-start | bytes 774152 | tf_op jit(solution)/shard_map/ppermute | solution.py:33
  192.8 20.4 %collective-permute-start.39 = (bf16[144,896]{1,0:T(8,128)(2,1)}, bf16[144,896]{1,0:T(8,128)(2,1)}, u32[]{:S(2)}, u32[]{:S(2)}) collective-permute-start(bf16[144,896]{1,0:T(8,128)(2,1)} %get-tuple-element.168), channel_id=1, source_target_pairs={{0,16},{1,17},{2,18},{3,19},{4,20},{5,21},{6,22},{7,23},{8,24},{9,... | collective-permute-start | bytes 774152 | tf_op jit(solution)/shard_map/ppermute | solution.py:33
  193.8 19.4 %collective-permute-start.40 = (bf16[144,896]{1,0:T(8,128)(2,1)}, bf16[144,896]{1,0:T(8,128)(2,1)}, u32[]{:S(2)}, u32[]{:S(2)}) collective-permute-start(bf16[144,896]{1,0:T(8,128)(2,1)} %get-tuple-element.169), channel_id=1, source_target_pairs={{0,28},{1,29},{2,30},{3,31},{4,16},{5,17},{6,18},{7,19},{8,20},{9,... | collective-permute-start | bytes 774152 | tf_op jit(solution)/shard_map/ppermute | solution.py:33
  198.5 25.9 %collective-permute-start.41 = (bf16[144,896]{1,0:T(8,128)(2,1)}, bf16[144,896]{1,0:T(8,128)(2,1)}, u32[]{:S(2)}, u32[]{:S(2)}) collective-permute-start(bf16[144,896]{1,0:T(8,128)(2,1)} %get-tuple-element.170), channel_id=1, source_target_pairs={{0,24},{1,25},{2,26},{3,27},{4,28},{5,29},{6,30},{7,31},{8,16},{9,... | collective-permute-start | bytes 774152 | tf_op jit(solution)/shard_map/ppermute | solution.py:33
  202.3 22.1 %collective-permute-start.42 = (bf16[144,896]{1,0:T(8,128)(2,1)}, bf16[144,896]{1,0:T(8,128)(2,1)}, u32[]{:S(2)}, u32[]{:S(2)}) collective-permute-start(bf16[144,896]{1,0:T(8,128)(2,1)} %get-tuple-element.171), channel_id=1, source_target_pairs={{0,20},{1,21},{2,22},{3,23},{4,24},{5,25},{6,26},{7,27},{8,28},{9,... | collective-permute-start | bytes 774152 | tf_op jit(solution)/shard_map/ppermute | solution.py:33
  202.4 21.9 %copy-start.14 = (bf16[128,3584]{1,0:T(8,128)(2,1)S(1)}, bf16[128,3584]{1,0:T(8,128)(2,1)}, u32[]{:S(2)}) copy-start(bf16[128,3584]{1,0:T(8,128)(2,1)} %copy-done.13) | copy-start | bytes 2752516
  (13 other events, 28.2 us)
